TPU v7x, 32 devices: a whole 2x2x4 slice. The times are simulated.
32 devices in a mesh: tok: 2 (over core), blk: 16 (over z, y, x).
Axes of the slice: x: 2, y: 2, z: 4, core: 2. Of those that a mesh axis runs over, the one named last changes fastest.
Arguments:
- q_proj: bfloat16 [2048, 2048], P('blk', 'tok'), may hold values from -6 to 6
- k_proj: bfloat16 [2048, 2048], P('blk', 'tok'), may hold values from -6 to 6
- v_proj: bfloat16 [2048, 2048], P('blk', 'tok'), may hold values from -6 to 6
- residual: bfloat16 [2048, 2048], P('blk', 'tok'), may hold values from -6 to 6
- prompt_lengths: int32 [8], replicated, may hold values from 1 to 512, 2048 in all
- expert_ids: int32 [2048, 6], P('blk'), may hold values from 0 to 15, all different within a row; in each aligned block of 128 rows (0 to 127, 128 to 255, ...) at most 96 rows name the same one
- gate_weights: float32 [2048, 6], P('blk'), may hold values from 0.02 to 0.6
- page_table: int32 [128], P('blk'), may hold values from 0 to 127, as said below
- out_weight: bfloat16 [2048, 2048], P('tok'), may hold values from -0.125 to 0.125
- norm_gain: float32 [2048], replicated, may hold values from 0.1 to 1.9
- w_gate: bfloat16 [16, 2048, 1408], P('blk', None, 'tok'), may hold values from -0.125 to 0.125
- w_up: bfloat16 [16, 2048, 1408], P('blk', None, 'tok'), may hold values from -0.125 to 0.125
- w_down: bfloat16 [16, 1408, 2048], P('blk', 'tok'), may hold values from -0.15625 to 0.15625
Outputs:
- layer_out: bfloat16 [2048, 2048], P('blk', 'tok')
- kv_cache: bfloat16 [128, 16, 2, 2048], P('blk', None, None, 'tok')
Inputs may be any that keep to these rules, and one draw needn't show every extreme that they name: `prompt_lengths`: the prompts fill the pack of 2048 tokens; the longest has exactly 512 tokens. `expert_ids`: each token names 6 different experts. Among the 128 tokens of one index of blk (aligned blocks) no expert is named by more than 96 tokens, a bound that some block reaches. `page_table`: each aligned block of 8 entries is a permutation of the same block's page numbers.
All inputs are finite; a program needn't handle non-finite values.
Results may differ from a plain program's by a relative error of at most 0.012.
Values may be sent and summed in bfloat16 or wider, within the bound.
No kernel may reach another device: no remote copies, remote signals or barrier semaphores. Data moves between devices by JAX's collectives and lax.ppermute only.
A program may use at most 64 MiB of HBM per device.

v0:
```python
import jax
import jax.numpy as jnp
from jax import lax
from jax.sharding import PartitionSpec as P

HEAD_DIM = 128
TOPK = 6
REACH = 4
PAGE = 16


EPSILON = 1e-06


def shifted(block, axis, distance):
    devices = range(lax.axis_size(axis))
    route = [(i - distance, i) for i in devices if i - distance in devices]
    return lax.ppermute(block, axis, route)


def positions_of(token_ids, prompt_lengths):
    seg_ends = jnp.cumsum(prompt_lengths)
    before = token_ids[:, None] >= seg_ends[None, :]
    segment = jnp.sum(before.astype(jnp.int32), axis=1)
    seg_start = jnp.max(jnp.where(before, seg_ends[None, :], 0), axis=1)
    return (segment, token_ids - seg_start)


def rotate(block_rows, position):
    row_count = block_rows.shape[0]
    half_dim = HEAD_DIM // 2
    head_view = block_rows.reshape(row_count, -1, HEAD_DIM).astype(jnp.float32)
    inv_freq = 10000.0 ** (-jnp.arange(half_dim, dtype=jnp.float32) / half_dim)
    angles = position.astype(jnp.float32)[:, None] * inv_freq[None, :]
    cosine = jnp.cos(angles)[:, None, :]
    sine_part = jnp.sin(angles)[:, None, :]
    lower_half = head_view[..., :half_dim]
    upper_half = head_view[..., half_dim:]
    turned = jnp.concatenate(
        [
            lower_half * cosine - upper_half * sine_part,
            upper_half * cosine + lower_half * sine_part,
        ],
        axis=-1,
    )
    return turned.reshape(row_count, -1).astype(jnp.bfloat16)


def attend(rot_query, key_rows, value_rows, q_seg, q_index, k_seg, k_index):
    q_count = rot_query.shape[0]
    k_count = key_rows.shape[0]
    q_heads = rot_query.reshape(q_count, -1, HEAD_DIM)
    k_heads = key_rows.reshape(k_count, -1, HEAD_DIM)
    v_heads = value_rows.reshape(k_count, -1, HEAD_DIM)
    scores = jnp.einsum(
        "qhd,khd->hqk", q_heads, k_heads, preferred_element_type=jnp.float32
    ) * HEAD_DIM ** (-0.5)
    allowed = (
        (k_seg[None, :] == q_seg[:, None])
        & (k_index[None, :] <= q_index[:, None])
        & (k_index[None, :] >= 0)
    )
    scores = jnp.where(allowed[None], scores, -1e30)
    top_score = jnp.max(scores, axis=2, keepdims=True)
    exp_terms = jnp.where(allowed[None], jnp.exp(scores - top_score), 0.0)
    soft_weights = (exp_terms / jnp.sum(exp_terms, axis=2, keepdims=True)).astype(jnp.bfloat16)
    mixed_heads = jnp.einsum(
        "hqk,khd->qhd", soft_weights, v_heads, preferred_element_type=jnp.float32
    )
    return mixed_heads.reshape(q_count, -1).astype(jnp.bfloat16)


def on_device(
    q_proj,
    k_proj,
    v_proj,
    residual,
    prompt_lengths,
    expert_ids,
    gate_weights,
    page_table,
    out_weight,
    norm_gain,
    w_gate,
    w_up,
    w_down,
):
    tok_rows = q_proj.shape[0]
    col_width = residual.shape[1]
    model_width = norm_gain.shape[0]
    blk_index = lax.axis_index("blk")
    tok_index = lax.axis_index("tok")
    token_ids = blk_index * tok_rows + jnp.arange(tok_rows, dtype=jnp.int32)
    segment, position = positions_of(token_ids, prompt_lengths)
    rot_query = rotate(q_proj, position)
    rot_keys = rotate(k_proj, position)
    own_pair = jnp.stack([rot_keys, v_proj])
    pair_list = [own_pair]
    id_list = [token_ids]
    carried = own_pair
    for distance in range(1, REACH + 1):
        carried = shifted(carried, "blk", 1)
        pair_list.append(carried)
        id_list.append(token_ids - distance * tok_rows)
    all_pairs = jnp.concatenate(pair_list, axis=1)
    key_ids = jnp.concatenate(id_list)
    key_seg, unused = positions_of(key_ids, prompt_lengths)
    attention = attend(rot_query, all_pairs[0], all_pairs[1], segment, token_ids, key_seg, key_ids)
    partial_value = jnp.dot(attention, out_weight, preferred_element_type=jnp.float32)
    attn_sum = lax.psum(partial_value, "tok")
    full_res = lax.all_gather(residual, "tok", axis=1, tiled=True)
    stream = (full_res.astype(jnp.float32) + attn_sum).astype(jnp.bfloat16)
    wide_rows = stream.astype(jnp.float32)
    inv_scale = lax.rsqrt(jnp.mean(wide_rows * wide_rows, axis=1, keepdims=True) + EPSILON)
    normed = (wide_rows * inv_scale * norm_gain[None, :]).astype(jnp.bfloat16)
    own_share = lax.dynamic_slice_in_dim(stream, tok_index * col_width, col_width, 1)
    experts = lax.axis_size("blk")
    capacity = max(2, min(tok_rows, 2 * TOPK * tok_rows // experts))
    flat_ids = expert_ids.reshape(-1)
    hit_table = (flat_ids[:, None] == jnp.arange(experts, dtype=jnp.int32)[None, :]).astype(
        jnp.int32
    )
    rank_table = jnp.cumsum(hit_table, axis=0) - hit_table
    slot_ids = flat_ids * capacity + jnp.sum(rank_table * hit_table, axis=1)
    picked = (
        slot_ids[:, None] == jnp.arange(experts * capacity, dtype=jnp.int32)[None, :]
    ).reshape(tok_rows, TOPK, experts * capacity)
    placing = jnp.sum(picked.astype(jnp.bfloat16), axis=1)
    mixing = jnp.sum(jnp.where(picked, gate_weights[:, :, None], 0.0), axis=1)
    send_rows = jnp.einsum("te,td->ed", placing, normed, preferred_element_type=jnp.float32).astype(
        jnp.bfloat16
    )
    send_rows = send_rows.reshape(experts, capacity, model_width)
    arrived = lax.all_to_all(send_rows, "blk", split_axis=0, concat_axis=0, tiled=True)
    sources, slot_count, feat_width = arrived.shape
    flat_rows = arrived.reshape(sources * slot_count, feat_width)
    gate_act = jnp.dot(flat_rows, w_gate[0], preferred_element_type=jnp.float32)
    up_act = jnp.dot(flat_rows, w_up[0], preferred_element_type=jnp.float32)
    hidden = (jax.nn.silu(gate_act) * up_act).astype(jnp.bfloat16)
    partial_out = jnp.dot(hidden, w_down[0], preferred_element_type=jnp.float32).reshape(
        sources, slot_count, feat_width
    )
    summed = lax.psum_scatter(
        partial_out.astype(jnp.bfloat16), "tok", scatter_dimension=2, tiled=True
    )
    returned = lax.all_to_all(summed, "blk", split_axis=0, concat_axis=0, tiled=True)
    moe = jnp.dot(
        mixing,
        returned.reshape(experts * capacity, col_width).astype(jnp.float32),
        precision=lax.Precision.HIGHEST,
    )
    layer_out = (own_share.astype(jnp.float32) + moe).astype(jnp.bfloat16)
    page_count = tok_rows // PAGE
    local_page = page_table - blk_index * page_count
    kv_rows = jnp.stack([rot_keys, v_proj], axis=1).reshape(page_count, PAGE, 2, -1)
    kv_pages = jnp.zeros_like(kv_rows).at[local_page].set(kv_rows)
    return (layer_out, kv_pages)


def solution(mesh):
    placed = (
        P("blk", "tok"),
        P("blk", "tok"),
        P("blk", "tok"),
        P("blk", "tok"),
        P(),
        P("blk", None),
        P("blk", None),
        P("blk"),
        P("tok", None),
        P(),
        P("blk", None, "tok"),
        P("blk", None, "tok"),
        P("blk", "tok", None),
    )
    return jax.shard_map(
        on_device,
        mesh=mesh,
        in_specs=placed,
        out_specs=(P("blk", "tok"), P("blk", None, None, "tok")),
        check_vma=False,
    )
```

profile of v0, /device:TPU:14, one launch (start us, length us, event | category | flops | bytes accessed | tf_op | source)
XLA Modules:
  0.0 394.2 jit_solution(7418667251106261116)
XLA Ops:
  10.6 2.0 copy.78
  15.2 1.8 copy.63
  17.0 2.1 pad_maximum_fusion
  19.1 3.4 collective-permute-start
  23.6 11.3 %collective-permute-done = bf16[2,128,1024]{1,2,0:T(8,128)(2,1)} collective-permute-done((bf16[2,128,1024]{1,2,0:T(8,128)(2,1)}, bf16[2,128,1024]{1,2,0:T(8,128)(2,1)}, u32[]{:S(2)}, u32[]{:S(2)}) %collective-permute-start) | collective-permute-done | bytes 524320 | tf_op jit(solution)/shard_map/ppermute | solution.py:18
  34.9 5.2 %collective-permute-start.1 = (bf16[2,128,1024]{1,2,0:T(8,128)(2,1)}, bf16[2,128,1024]{1,2,0:T(8,128)(2,1)}, u32[]{:S(2)}, u32[]{:S(2)}) collective-permute-start(bf16[2,128,1024]{1,2,0:T(8,128)(2,1)} %collective-permute-done), channel_id=1, source_target_pairs={{0,1},{1,2},{2,3},{3,4},{4,5},{5,6},{6,7},{7,8},{8,9},{9,10},{10,1... | collective-permute-start | bytes 1572872 | tf_op jit(solution)/shard_map/ppermute | solution.py:18
  41.0 9.7 %collective-permute-done.1 = bf16[2,128,1024]{1,2,0:T(8,128)(2,1)} collective-permute-done((bf16[2,128,1024]{1,2,0:T(8,128)(2,1)}, bf16[2,128,1024]{1,2,0:T(8,128)(2,1)}, u32[]{:S(2)}, u32[]{:S(2)}) %collective-permute-start.1) | collective-permute-done | bytes 524320 | tf_op jit(solution)/shard_map/ppermute | solution.py:18
  50.7 6.2 %collective-permute-start.2 = (bf16[2,128,1024]{1,2,0:T(8,128)(2,1)}, bf16[2,128,1024]{1,2,0:T(8,128)(2,1)}, u32[]{:S(2)}, u32[]{:S(2)}) collective-permute-start(bf16[2,128,1024]{1,2,0:T(8,128)(2,1)} %collective-permute-done.1), channel_id=1, source_target_pairs={{0,1},{1,2},{2,3},{3,4},{4,5},{5,6},{6,7},{7,8},{8,9},{9,10},{10,1... | collective-permute-start | bytes 1572872 | tf_op jit(solution)/shard_map/ppermute | solution.py:18
  57.6 2.0 copy.79
  59.6 1.9 copy.80
  61.5 2.1 subtract_convert_fusion
  63.6 3.0 collective-permute-done.2
  66.6 6.2 %collective-permute-start.3 = (bf16[2,128,1024]{1,2,0:T(8,128)(2,1)}, bf16[2,128,1024]{1,2,0:T(8,128)(2,1)S(1)}, u32[]{:S(2)}, u32[]{:S(2)}) collective-permute-start(bf16[2,128,1024]{1,2,0:T(8,128)(2,1)} %collective-permute-done.2), channel_id=1, source_target_pairs={{0,1},{1,2},{2,3},{3,4},{4,5},{5,6},{6,7},{7,8},{8,9},{9,10},{10,1... | collective-permute-start | bytes 1572872 | tf_op jit(solution)/shard_map/ppermute | solution.py:18
  72.9 1.9 constant_dynamic-update-slice_fusion.3
  74.9 1.9 constant_dynamic-update-slice_fusion.2
  76.8 1.9 constant_dynamic-update-slice_fusion.1
  78.7 2.8 collective-permute-done.3
  82.4 3.5 fusion.41
  85.9 4.2 %fusion.44 = (f32[8,128]{1,0:T(8,128)S(1)}, f32[8,128,640]{2,1,0:T(8,128)}) fusion(pred[128,640]{1,0:T(8,128)(4,1)S(1)} %and_and_fusion, bf16[640,8,128]{0,2,1:T(8,128)(2,1)} %bitcast.65, bf16[128,8,64]{2,0,1:T(8,128)(2,1)} %get-tuple-element.17, bf16[128,8,64]{2,0,1:T(8,128)(2,1)S(1)} %get-tuple-element.16), kind=kOutput, calls=%fused_computation.84 | convolution fusion | flops 171573888 | bytes 4280320 | tf_op jit(solution)/shard_map/sub | solution.py:65
  90.1 3.0 fusion.13
  98.0 2.3 all_gather.3
  101.1 16.1 %all-reduce.2.cloned.1.call-done = f32[128,2048]{1,0:T(8,128)} async-done(((f32[128,2048]{1,0:T(8,128)}), f32[128,2048]{1,0:T(8,128)}) %all-reduce.2.cloned.1.call-update) | async-done | bytes 1048592 | tf_op jit(solution)/shard_map/psum | solution.py:110
  118.8 1.9 convolution_convert_fusion
  120.7 144.1 %all_to_all.10 = bf16[16,96,2048]{2,1,0:T(8,128)(2,1)S(1)} all-to-all(bf16[16,96,2048]{2,1,0:T(8,128)(2,1)S(1)} %bitcast.58), channel_id=1, replica_groups=mesh['tok'=2,'blk'=16] {'blk'}, dimensions={0} | all-to-all | bytes 12582912 | tf_op jit(solution)/shard_map/all_to_all | solution.py:134
  264.8 4.7 %fusion.4 = f32[1536,704]{0,1:T(8,128)S(1)} fusion(bf16[1536,2048]{1,0:T(8,128)(2,1)S(1)} %bitcast.59, bf16[1,2048,704]{1,2,0:T(8,128)(2,1)S(1)} %copy-done.12), kind=kOutput, calls=%fused_computation.10 | convolution fusion | flops 4429185024 | bytes 13500416 | tf_op jit(solution)/shard_map/dot_general | solution.py:137
  269.5 6.3 %multiply_convert_fusion = bf16[1536,704]{0,1:T(8,128)(2,1)} fusion(f32[1536,704]{0,1:T(8,128)S(1)} %fusion.4, bf16[1536,2048]{1,0:T(8,128)(2,1)S(1)} %bitcast.60, bf16[1,2048,704]{1,2,0:T(8,128)(2,1)S(1)} %copy-done.13), kind=kOutput, calls=%fused_computation.7 | convolution fusion | flops 4435673088 | bytes 15663104 | tf_op jit(solution)/shard_map/dot_general | solution.py:138
  275.8 4.2 %copy.72 = bf16[1536,704]{1,0:T(8,128)(2,1)} copy(bf16[1536,704]{0,1:T(8,128)(2,1)} %multiply_convert_fusion) | data formatting | bytes 4325376 | tf_op jit(solution)/shard_map/convert_element_type | solution.py:139
  280.0 8.7 %convolution_convert_fusion.1 = bf16[16,96,2048]{2,1,0:T(8,128)(2,1)} fusion(bf16[16,96,704]{2,1,0:T(8,128)(2,1)} %bitcast.61, bf16[1,704,2048]{2,1,0:T(8,128)(2,1)S(1)} %copy-done), kind=kOutput, calls=%fused_computation.6 | convolution fusion | flops 4432330752 | bytes 11337728 | tf_op jit(solution)/shard_map/dot_general | solution.py:140
  288.7 14.8 %reduce-scatter.2.cloned.1.call-done = bf16[16,96,1024]{2,1,0:T(8,128)(2,1)} async-done(((bf16[16,96,2048]{2,1,0:T(8,128)(2,1)}), bf16[16,96,1024]{2,1,0:T(8,128)(2,1)}) %reduce-scatter.2.cloned.1.call-update) | async-done | bytes 3145744 | tf_op jit(solution)/shard_map/reduce_scatter | solution.py:143
  303.6 7.0 %all-to-all-start.1 = ((bf16[16,96,1024]{2,1,0:T(8,128)(2,1)}), bf16[16,96,1024]{2,1,0:T(8,128)(2,1)}, u32[]{:S(2)}, u32[]{:S(2)}) async-start(bf16[16,96,1024]{2,1,0:T(8,128)(2,1)} %reduce-scatter.2.cloned.1.call-done), calls=%async_computation.2 | async-start | bytes 6291456 | tf_op jit(solution)/shard_map/all_to_all | solution.py:146
  317.4 65.7 %all-to-all-done.1 = bf16[16,96,1024]{2,1,0:T(8,128)(2,1)} async-done(((bf16[16,96,1024]{2,1,0:T(8,128)(2,1)}), bf16[16,96,1024]{2,1,0:T(8,128)(2,1)}, u32[]{:S(2)}, u32[]{:S(2)}) %all-to-all-start.1) | async-done | bytes 3145760 | tf_op jit(solution)/shard_map/all_to_all | solution.py:146
  383.1 4.3 %fusion.12 = bf16[128,1024]{1,0:T(8,128)(2,1)} fusion(f32[128,1536]{1,0:T(8,128)} %select_reduce_fusion, bf16[1536,1024]{1,0:T(8,128)(2,1)} %bitcast.20, bf16[128,2048]{1,0:T(8,128)(2,1)} %copy-done.2, s32[]{:T(128)S(6)} %select_n.24), kind=kOutput, calls=%fused_computation.24 | convolution fusion | flops 2416312320 | bytes 4456452 | tf_op jit(solution)/shard_map/dot_general | solution.py:147
  (83 shorter events, 23.7 us)
Async XLA Ops:
  7.2 272.9 %copy-start = (bf16[1,704,2048]{2,1,0:T(8,128)(2,1)S(1)}, bf16[1,704,2048]{2,1,0:T(8,128)(2,1)}, u32[]{:S(2)}) copy-start(bf16[1,704,2048]{2,1,0:T(8,128)(2,1)} %param.25) | copy-start | bytes 8650756
  7.2 5.3 %copy-start.14 = (s32[8]{0:T(128)S(1)}, s32[8]{0:T(128)}, u32[]{:S(2)}) copy-start(s32[8]{0:T(128)} %param.17) | copy-start | bytes 100
  7.2 110.0 %all-reduce.2.cloned.1.call-start = ((), (), s32[]{:S(2)}) async-start(), calls=%async_computation.3 | async-start | bytes 2097152 | tf_op jit(solution)/shard_map/psum | solution.py:110
  12.7 0.5 copy-start.11
  13.5 1.3 copy-start.3
  13.5 1.3 copy-start.5
  15.1 46.4 %copy-start.4 = (f32[128,64]{1,0:T(8,128)S(1)}, f32[128,64]{1,0:T(8,128)}, u32[]{:S(2)}) copy-start(f32[128,64]{1,0:T(8,128)} %copy-done.3) | copy-start | bytes 98308
  15.2 46.4 %copy-start.6 = (f32[128,64]{1,0:T(8,128)S(1)}, f32[128,64]{1,0:T(8,128)}, u32[]{:S(2)}) copy-start(f32[128,64]{1,0:T(8,128)} %copy-done.5) | copy-start | bytes 98308
  19.1 15.9 %collective-permute-start = (bf16[2,128,1024]{1,2,0:T(8,128)(2,1)}, bf16[2,128,1024]{1,2,0:T(8,128)(2,1)}, u32[]{:S(2)}, u32[]{:S(2)}) collective-permute-start(bf16[2,128,1024]{1,2,0:T(8,128)(2,1)} %get-tuple-element.20), channel_id=1, source_target_pairs={{0,1},{1,2},{2,3},{3,4},{4,5},{5,6},{6,7},{7,8},{8,9},{9,10},{10,1... | collective-permute-start | bytes 1572872 | tf_op jit(solution)/shard_map/ppermute | solution.py:18
  34.9 15.8 %collective-permute-start.1 = (bf16[2,128,1024]{1,2,0:T(8,128)(2,1)}, bf16[2,128,1024]{1,2,0:T(8,128)(2,1)}, u32[]{:S(2)}, u32[]{:S(2)}) collective-permute-start(bf16[2,128,1024]{1,2,0:T(8,128)(2,1)} %collective-permute-done), channel_id=1, source_target_pairs={{0,1},{1,2},{2,3},{3,4},{4,5},{5,6},{6,7},{7,8},{8,9},{9,10},{10,1... | collective-permute-start | bytes 1572872 | tf_op jit(solution)/shard_map/ppermute | solution.py:18
  50.7 15.9 %collective-permute-start.2 = (bf16[2,128,1024]{1,2,0:T(8,128)(2,1)}, bf16[2,128,1024]{1,2,0:T(8,128)(2,1)}, u32[]{:S(2)}, u32[]{:S(2)}) collective-permute-start(bf16[2,128,1024]{1,2,0:T(8,128)(2,1)} %collective-permute-done.1), channel_id=1, source_target_pairs={{0,1},{1,2},{2,3},{3,4},{4,5},{5,6},{6,7},{7,8},{8,9},{9,10},{10,1... | collective-permute-start | bytes 1572872 | tf_op jit(solution)/shard_map/ppermute | solution.py:18
  66.6 14.9 %collective-permute-start.3 = (bf16[2,128,1024]{1,2,0:T(8,128)(2,1)}, bf16[2,128,1024]{1,2,0:T(8,128)(2,1)S(1)}, u32[]{:S(2)}, u32[]{:S(2)}) collective-permute-start(bf16[2,128,1024]{1,2,0:T(8,128)(2,1)} %collective-permute-done.2), channel_id=1, source_target_pairs={{0,1},{1,2},{2,3},{3,4},{4,5},{5,6},{6,7},{7,8},{8,9},{9,10},{10,1... | collective-permute-start | bytes 1572872 | tf_op jit(solution)/shard_map/ppermute | solution.py:18
  90.1 3.4 copy-start.1
  93.5 1.9 copy-start.8
  93.5 4.6 %copy-start.7 = (bf16[128,1024]{1,0:T(8,128)(2,1)S(1)}, bf16[128,1024]{1,0:T(8,128)(2,1)}, u32[]{:S(2)}) copy-start(bf16[128,1024]{1,0:T(8,128)(2,1)} %param.16) | copy-start | bytes 786436
  95.2 23.6 %copy-start.9 = (f32[2048]{0:T(1024)S(1)}, f32[2048]{0:T(1024)}, u32[]{:S(2)}) copy-start(f32[2048]{0:T(1024)} %param.22) | copy-start | bytes 24580
  95.3 208.3 %reduce-scatter.2.cloned.1.call-start = ((), (), s32[]{:S(2)}) async-start(), calls=%async_computation.4 | async-start | bytes 9437184 | tf_op jit(solution)/shard_map/reduce_scatter | solution.py:143
  118.8 1.9 copy-start.2
  120.7 144.1 %copy-start.12 = (bf16[1,2048,704]{1,2,0:T(8,128)(2,1)S(1)}, bf16[1,2048,704]{1,2,0:T(8,128)(2,1)}, u32[]{:S(2)}) copy-start(bf16[1,2048,704]{1,2,0:T(8,128)(2,1)} %param.23) | copy-start | bytes 8650756
  264.8 4.7 %copy-start.13 = (bf16[1,2048,704]{1,2,0:T(8,128)(2,1)S(1)}, bf16[1,2048,704]{1,2,0:T(8,128)(2,1)}, u32[]{:S(2)}) copy-start(bf16[1,2048,704]{1,2,0:T(8,128)(2,1)} %param.24) | copy-start | bytes 8650756
  303.6 79.5 %all-to-all-start.1 = ((bf16[16,96,1024]{2,1,0:T(8,128)(2,1)}), bf16[16,96,1024]{2,1,0:T(8,128)(2,1)}, u32[]{:S(2)}, u32[]{:S(2)}) async-start(bf16[16,96,1024]{2,1,0:T(8,128)(2,1)} %reduce-scatter.2.cloned.1.call-done), calls=%async_computation.2 | async-start | bytes 6291456 | tf_op jit(solution)/shard_map/all_to_all | solution.py:146
  310.5 2.2 copy-start.15
  310.9 5.0 %copy-start.10 = (f32[128,6]{0,1:T(8,128)S(1)}, f32[128,6]{0,1:T(8,128)}, u32[]{:S(2)}) copy-start(f32[128,6]{0,1:T(8,128)} %param.19) | copy-start | bytes 9220
Sparse Core Ops, SparseCore 0:
  95.4 21.7 all-reduce.1
  288.9 14.6 reduce-scatter.1
where the time goes:
time: 395 us; the launch traced here: 394 us
  blocking collectives  146 us (37%)
  waiting for transfers between devices  124 us (31%)
  matrix products  34.8 us (9%)
  local copies, waits for them, and re-layouts  33.4 us (8%)
  starting transfers between devices  28 us (7%)
  between operations  14.4 us (4%)
  other arithmetic  13.7 us (3%)
    all_to_all x1, blocking collectives, on_device(): lax.all_to_all(send_rows, 'blk', split_axis=0, concat_axis=0, tiled=True)  144 us
    all_to_all x1, waiting for transfers between devices, on_device(): lax.all_to_all(summed, 'blk', split_axis=0, concat_axis=0, tiled=True)  65.7 us
    ppermute x4, waiting for transfers between devices, shifted(): return lax.ppermute(block, axis, route)  26.9 us
    ppermute x4, starting transfers between devices, shifted(): return lax.ppermute(block, axis, route)  20.9 us
    unnamed x44, local copies, waits for them, and re-layouts  19.3 us
    psum x1, waiting for transfers between devices, on_device(): attn_sum = lax.psum(partial_value, 'tok')  16.1 us
    reduce_scatter x1, waiting for transfers between devices, on_device(): lax.psum_scatter(partial_out.astype(jnp.bfloat16), 'tok', scatter_dimensi...  14.8 us
    dot_general x1, matrix products, on_device(): jnp.dot(hidden, w_down[0], preferred_element_type=jnp.float32)  8.66 us
  transfers between devices with their start and end apart: 7, of which 7 were waited for; matrix products, arithmetic and copies ran while one was open for 6% of the time, Pallas kernels for 0%

commit v1 on v0

--- a/solution.py
+++ b/solution.py
@@ -1,14 +1,16 @@
+import functools
+
 import jax
 import jax.numpy as jnp
 from jax import lax
+from jax.experimental import pallas as pl
+from jax.experimental.pallas import tpu as pltpu
 from jax.sharding import PartitionSpec as P
 
 HEAD_DIM = 128
-TOPK = 6
 REACH = 4
 PAGE = 16
-
-
+PLANE = 4
 EPSILON = 1e-06
 
 
@@ -16,6 +18,35 @@
     devices = range(lax.axis_size(axis))
     route = [(i - distance, i) for i in devices if i - distance in devices]
     return lax.ppermute(block, axis, route)
+
+
+def flipped(block, mask):
+    return lax.ppermute(block, "blk", [(i, i ^ mask) for i in range(lax.axis_size("blk"))])
+
+
+def from_plane(block, ahead):
+    count = lax.axis_size("blk")
+    return lax.ppermute(
+        block, "blk", [((i + PLANE * ahead) % count, i) for i in range(count)]
+    )
+
+
+def to_plane(block, ahead):
+    count = lax.axis_size("blk")
+    return lax.ppermute(
+        block, "blk", [(i, (i + PLANE * ahead) % count) for i in range(count)]
+    )
+
+
+def from_core(block, ahead):
+    count = lax.axis_size("tok")
+    return lax.ppermute(block, "tok", [((i + ahead) % count, i) for i in range(count)])
+
+
+def core_sum(block):
+    if lax.axis_size("tok") == 2:
+        return block + from_core(block, 1)
+    return lax.psum(block, "tok")
 
 
 def positions_of(token_ids, prompt_lengths):
@@ -68,6 +99,99 @@
         "hqk,khd->qhd", soft_weights, v_heads, preferred_element_type=jnp.float32
     )
     return mixed_heads.reshape(q_count, -1).astype(jnp.bfloat16)
+
+
+def gate_lanes(expert_ids, gate_weights, experts):
+    hits = expert_ids[:, :, None] == jnp.arange(experts, dtype=jnp.int32)[None, None, :]
+    gates = jnp.sum(jnp.where(hits, gate_weights[:, :, None], 0.0), axis=1)
+    pieces = []
+    for _ in range(3):
+        piece = lax.reduce_precision(gates, 8, 7)
+        pieces.append(piece.astype(jnp.bfloat16))
+        gates = gates - piece
+    lanes = jnp.concatenate(pieces, axis=1)
+    return jnp.pad(lanes, ((0, 0), (0, -lanes.shape[1] % 128)))
+
+
+def expert_kernel(experts, place_ref, rows_ref, gate_ref, up_ref, down_ref, out_ref):
+    width = gate_ref.shape[1]
+    parts, _, part_width = out_ref.shape
+    rows = rows_ref[:, :width]
+    lanes = rows_ref[:, width:].astype(jnp.float32)
+    lane_ids = lax.broadcasted_iota(jnp.int32, lanes.shape, 1)
+    named = (lane_ids < 3 * experts) & (lane_ids % experts == place_ref[0])
+    weight = jnp.sum(jnp.where(named, lanes, 0.0), axis=1, keepdims=True)
+    turned = (((1,), (1,)), ((), ()))
+    gate_act = lax.dot_general(rows, gate_ref[...], turned, preferred_element_type=jnp.float32)
+    up_act = lax.dot_general(rows, up_ref[...], turned, preferred_element_type=jnp.float32)
+    hidden = (gate_act / (1.0 + jnp.exp(-gate_act)) * up_act).astype(jnp.bfloat16)
+    for part in range(parts):
+        columns = slice(part * part_width, (part + 1) * part_width)
+        product = jnp.dot(hidden, down_ref[:, columns], preferred_element_type=jnp.float32)
+        slot = lax.rem(part - place_ref[1] + parts, parts)
+        out_ref[pl.ds(slot, 1)] = (weight * product).astype(jnp.bfloat16)[None]
+
+
+def run_expert(place, rows, w_gate, w_up, w_down, experts, parts, tile):
+    count, full_width = rows.shape
+    units, width = w_gate.shape
+    whole = functools.partial(pl.BlockSpec, memory_space=pltpu.VMEM)
+    return pl.pallas_call(
+        functools.partial(expert_kernel, experts),
+        grid_spec=pltpu.PrefetchScalarGridSpec(
+            num_scalar_prefetch=1,
+            grid=(count // tile,),
+            in_specs=[
+                pl.BlockSpec((tile, full_width), lambda i, place: (i, 0)),
+                whole(),
+                whole(),
+                whole(),
+            ],
+            out_specs=pl.BlockSpec((parts, tile, width // parts), lambda i, place: (0, i, 0)),
+        ),
+        out_shape=jax.ShapeDtypeStruct((parts, count, width // parts), jnp.bfloat16),
+        cost_estimate=pl.CostEstimate(
+            flops=6 * count * width * units,
+            bytes_accessed=2 * (3 * width * units + 2 * count * width),
+            transcendentals=count * units,
+        ),
+        compiler_params=pltpu.CompilerParams(vmem_limit_bytes=48 << 20),
+    )(place, rows, w_gate, w_up, w_down)
+
+
+def plane_gather(blocks):
+    half = blocks.shape[1] // 2
+    first, second = blocks[:, :half], blocks[:, half:]
+    first_pair = jnp.stack([first, flipped(first, 1)])
+    second_pair = jnp.stack([second, flipped(second, 2)])
+    first_other = flipped(first_pair, 2)
+    second_other = flipped(second_pair, 1)
+    firsts = [first_pair[0], first_pair[1], first_other[0], first_other[1]]
+    seconds = [second_pair[0], second_other[0], second_pair[1], second_other[1]]
+    return jnp.stack(
+        [jnp.concatenate([a, b], axis=1) for a, b in zip(firsts, seconds, strict=True)]
+    )
+
+
+def wide(block):
+    return block.astype(jnp.float32)
+
+
+def narrow(block):
+    return block.astype(jnp.bfloat16)
+
+
+def plane_scatter(kept, came):
+    half = kept.shape[-1] // 2
+    total = wide(kept) + wide(came)
+    first, second = total[..., :half], total[..., half:]
+    got = flipped(narrow(first[2:4]), 2)
+    first = first[0:2] + wide(got)
+    got = flipped(narrow(jnp.stack([second[1], second[3]])), 1)
+    second = jnp.stack([second[0], second[2]]) + wide(got)
+    got_first = flipped(narrow(first[1]), 1)
+    got_second = flipped(narrow(second[1]), 2)
+    return jnp.concatenate([first[0] + wide(got_first), second[0] + wide(got_second)], axis=-1)
 
 
 def on_device(
@@ -90,6 +214,9 @@
     model_width = norm_gain.shape[0]
     blk_index = lax.axis_index("blk")
     tok_index = lax.axis_index("tok")
+    cores = lax.axis_size("tok")
+    experts = lax.axis_size("blk")
+    planes = experts // PLANE
     token_ids = blk_index * tok_rows + jnp.arange(tok_rows, dtype=jnp.int32)
     segment, position = positions_of(token_ids, prompt_lengths)
     rot_query = rotate(q_proj, position)
@@ -107,48 +234,59 @@
     key_seg, unused = positions_of(key_ids, prompt_lengths)
     attention = attend(rot_query, all_pairs[0], all_pairs[1], segment, token_ids, key_seg, key_ids)
     partial_value = jnp.dot(attention, out_weight, preferred_element_type=jnp.float32)
-    attn_sum = lax.psum(partial_value, "tok")
-    full_res = lax.all_gather(residual, "tok", axis=1, tiled=True)
-    stream = (full_res.astype(jnp.float32) + attn_sum).astype(jnp.bfloat16)
+    placed_residual = lax.dynamic_update_slice_in_dim(
+        jnp.zeros((tok_rows, model_width), jnp.bfloat16), residual, tok_index * col_width, 1
+    )
+    stream = core_sum(partial_value + wide(placed_residual)).astype(jnp.bfloat16)
     wide_rows = stream.astype(jnp.float32)
     inv_scale = lax.rsqrt(jnp.mean(wide_rows * wide_rows, axis=1, keepdims=True) + EPSILON)
     normed = (wide_rows * inv_scale * norm_gain[None, :]).astype(jnp.bfloat16)
     own_share = lax.dynamic_slice_in_dim(stream, tok_index * col_width, col_width, 1)
-    experts = lax.axis_size("blk")
-    capacity = max(2, min(tok_rows, 2 * TOPK * tok_rows // experts))
-    flat_ids = expert_ids.reshape(-1)
-    hit_table = (flat_ids[:, None] == jnp.arange(experts, dtype=jnp.int32)[None, :]).astype(
-        jnp.int32
-    )
-    rank_table = jnp.cumsum(hit_table, axis=0) - hit_table
-    slot_ids = flat_ids * capacity + jnp.sum(rank_table * hit_table, axis=1)
-    picked = (
-        slot_ids[:, None] == jnp.arange(experts * capacity, dtype=jnp.int32)[None, :]
-    ).reshape(tok_rows, TOPK, experts * capacity)
-    placing = jnp.sum(picked.astype(jnp.bfloat16), axis=1)
-    mixing = jnp.sum(jnp.where(picked, gate_weights[:, :, None], 0.0), axis=1)
-    send_rows = jnp.einsum("te,td->ed", placing, normed, preferred_element_type=jnp.float32).astype(
-        jnp.bfloat16
-    )
-    send_rows = send_rows.reshape(experts, capacity, model_width)
-    arrived = lax.all_to_all(send_rows, "blk", split_axis=0, concat_axis=0, tiled=True)
-    sources, slot_count, feat_width = arrived.shape
-    flat_rows = arrived.reshape(sources * slot_count, feat_width)
-    gate_act = jnp.dot(flat_rows, w_gate[0], preferred_element_type=jnp.float32)
-    up_act = jnp.dot(flat_rows, w_up[0], preferred_element_type=jnp.float32)
-    hidden = (jax.nn.silu(gate_act) * up_act).astype(jnp.bfloat16)
-    partial_out = jnp.dot(hidden, w_down[0], preferred_element_type=jnp.float32).reshape(
-        sources, slot_count, feat_width
-    )
-    summed = lax.psum_scatter(
-        partial_out.astype(jnp.bfloat16), "tok", scatter_dimension=2, tiled=True
-    )
-    returned = lax.all_to_all(summed, "blk", split_axis=0, concat_axis=0, tiled=True)
-    moe = jnp.dot(
-        mixing,
-        returned.reshape(experts * capacity, col_width).astype(jnp.float32),
-        precision=lax.Precision.HIGHEST,
-    )
+
+    part_rows = tok_rows // cores
+    lanes = gate_lanes(expert_ids, gate_weights, experts)
+    payload = lax.dynamic_slice_in_dim(
+        jnp.concatenate([normed, lanes], axis=1), tok_index * part_rows, part_rows, 0
+    )[None]
+    place = jnp.stack([blk_index, tok_index]).astype(jnp.int32)
+    groups = [[0]] + [sorted({ahead, planes - ahead}) for ahead in range(1, planes // 2 + 1)]
+    came = {0: payload}
+    for ahead in range(1, planes):
+        came[ahead] = from_plane(payload, ahead)
+    gate_turned, up_turned = w_gate[0].T, w_up[0].T
+    results = {}
+    for group in groups:
+        column = jnp.concatenate([came[ahead] for ahead in group])
+        if planes > 4 and results:
+            column, results = lax.optimization_barrier((column, results))
+        held = plane_gather(column)
+        count = len(group)
+        own_rows = held.reshape(PLANE * count * part_rows, held.shape[-1])
+        outs = []
+        for ahead in range(cores):
+            rows = own_rows if ahead == 0 else from_core(own_rows, ahead)
+            outs.append(
+                run_expert(
+                    place, rows, gate_turned, up_turned, w_down[0], experts, cores, PLANE * part_rows
+                )
+            )
+        full = (PLANE, count, part_rows, col_width)
+        kept = jnp.stack([outs[j][0].reshape(full) for j in range(cores)], axis=2)
+        arrived = 0.0
+        for ahead in range(1, cores):
+            sent = jnp.stack([outs[(ahead + j) % cores][ahead] for j in range(cores)])
+            got = from_core(sent, cores - ahead)
+            arrived = arrived + wide(got)
+        arrived = jnp.stack([arrived[j].reshape(full) for j in range(cores)], axis=2)
+        merged = (PLANE, count, cores * part_rows, col_width)
+        summed = plane_scatter(kept.reshape(merged), arrived.reshape(merged))
+        for place_in, ahead in enumerate(group):
+            results[ahead] = summed[place_in]
+    moe = results[0]
+    for ahead in range(1, planes):
+        moe = moe + wide(to_plane(narrow(results[ahead]), ahead))
+    moe = jnp.roll(moe.reshape(cores, part_rows, col_width), tok_index, axis=0)
+    moe = moe.reshape(tok_rows, col_width)
     layer_out = (own_share.astype(jnp.float32) + moe).astype(jnp.bfloat16)
     page_count = tok_rows // PAGE
     local_page = page_table - blk_index * page_count

time: 395 us -> 248 us (0.63)
  the two profiles are of different devices: /device:TPU:14 before, /device:TPU:0 now
where the time goes in v1:
time: 248 us; the launch traced here: 247 us
  waiting for transfers between devices  95.6 us (39%)
  starting transfers between devices  60.5 us (24%)
  Pallas kernels  43.2 us (17%)
  local copies, waits for them, and re-layouts  26.3 us (11%)
  other arithmetic  12.4 us (5%)
  matrix products  7.66 us (3%)
    pallas_call x6, Pallas kernels, run_expert(): pl.pallas_call(functools.partial(expert_kernel, experts), grid_spec=pltpu...  43.2 us
    ppermute x24, waiting for transfers between devices, flipped(): lax.ppermute(block, 'blk', [(i, i ^ mask) for i in range(lax.axis_size('b...  40.9 us
    ppermute x24, starting transfers between devices, flipped(): lax.ppermute(block, 'blk', [(i, i ^ mask) for i in range(lax.axis_size('b...  27.8 us
    ppermute x4, waiting for transfers between devices, shifted(): return lax.ppermute(block, axis, route)  24.9 us
    ppermute x4, starting transfers between devices, shifted(): return lax.ppermute(block, axis, route)  22 us
    unnamed x42, local copies, waits for them, and re-layouts  15.4 us
    ppermute x3, waiting for transfers between devices, to_plane(): lax.ppermute(block, 'blk', [(i, (i + PLANE * ahead) % count) for i in ran...  14.6 us
    ppermute x3, waiting for transfers between devices, from_plane(): lax.ppermute(block, 'blk', [((i + PLANE * ahead) % count, i) for i in ran...  13.1 us
  transfers between devices with their start and end apart: 41, of which 21 were waited for; matrix products, arithmetic and copies ran while one was open for 11% of the time, Pallas kernels for 17%

profile of v1, /device:TPU:0, one launch (start us, length us, event | category | flops | bytes accessed | tf_op | source)
XLA Modules:
  0.0 247.4 jit_solution(12645147188004650371)
XLA Ops:
  5.9 5.6 %collective-permute-start = (bf16[2,128,1024]{1,2,0:T(8,128)(2,1)}, bf16[2,128,1024]{1,2,0:T(8,128)(2,1)}, u32[]{:S(2)}, u32[]{:S(2)}) collective-permute-start(bf16[2,128,1024]{1,2,0:T(8,128)(2,1)} %get-tuple-element.62), channel_id=1, source_target_pairs={{0,1},{1,2},{2,3},{3,4},{4,5},{5,6},{6,7},{7,8},{8,9},{9,10},{10,1... | collective-permute-start | bytes 1572872 | tf_op jit(solution)/shard_map/ppermute | solution.py:20
  12.7 9.5 %collective-permute-done = bf16[2,128,1024]{1,2,0:T(8,128)(2,1)} collective-permute-done((bf16[2,128,1024]{1,2,0:T(8,128)(2,1)}, bf16[2,128,1024]{1,2,0:T(8,128)(2,1)}, u32[]{:S(2)}, u32[]{:S(2)}) %collective-permute-start) | collective-permute-done | bytes 524320 | tf_op jit(solution)/shard_map/ppermute | solution.py:20
  22.2 5.2 %collective-permute-start.1 = (bf16[2,128,1024]{1,2,0:T(8,128)(2,1)}, bf16[2,128,1024]{1,2,0:T(8,128)(2,1)}, u32[]{:S(2)}, u32[]{:S(2)}) collective-permute-start(bf16[2,128,1024]{1,2,0:T(8,128)(2,1)} %collective-permute-done), channel_id=1, source_target_pairs={{0,1},{1,2},{2,3},{3,4},{4,5},{5,6},{6,7},{7,8},{8,9},{9,10},{10,1... | collective-permute-start | bytes 1572872 | tf_op jit(solution)/shard_map/ppermute | solution.py:20
  28.2 9.0 %collective-permute-done.1 = bf16[2,128,1024]{1,2,0:T(8,128)(2,1)} collective-permute-done((bf16[2,128,1024]{1,2,0:T(8,128)(2,1)}, bf16[2,128,1024]{1,2,0:T(8,128)(2,1)}, u32[]{:S(2)}, u32[]{:S(2)}) %collective-permute-start.1) | collective-permute-done | bytes 524320 | tf_op jit(solution)/shard_map/ppermute | solution.py:20
  37.2 5.2 %collective-permute-start.2 = (bf16[2,128,1024]{1,2,0:T(8,128)(2,1)}, bf16[2,128,1024]{1,2,0:T(8,128)(2,1)}, u32[]{:S(2)}, u32[]{:S(2)}) collective-permute-start(bf16[2,128,1024]{1,2,0:T(8,128)(2,1)} %collective-permute-done.1), channel_id=1, source_target_pairs={{0,1},{1,2},{2,3},{3,4},{4,5},{5,6},{6,7},{7,8},{8,9},{9,10},{10,1... | collective-permute-start | bytes 1572872 | tf_op jit(solution)/shard_map/ppermute | solution.py:20
  48.2 3.1 %collective-permute-done.2 = bf16[2,128,1024]{1,2,0:T(8,128)(2,1)} collective-permute-done((bf16[2,128,1024]{1,2,0:T(8,128)(2,1)}, bf16[2,128,1024]{1,2,0:T(8,128)(2,1)}, u32[]{:S(2)}, u32[]{:S(2)}) %collective-permute-start.2) | collective-permute-done | bytes 524320 | tf_op jit(solution)/shard_map/ppermute | solution.py:20
  51.3 6.0 %collective-permute-start.3 = (bf16[2,128,1024]{1,2,0:T(8,128)(2,1)}, bf16[2,128,1024]{1,2,0:T(8,128)(2,1)}, u32[]{:S(2)}, u32[]{:S(2)}) collective-permute-start(bf16[2,128,1024]{1,2,0:T(8,128)(2,1)} %collective-permute-done.2), channel_id=1, source_target_pairs={{0,1},{1,2},{2,3},{3,4},{4,5},{5,6},{6,7},{7,8},{8,9},{9,10},{10,1... | collective-permute-start | bytes 1572872 | tf_op jit(solution)/shard_map/ppermute | solution.py:20
  62.0 3.3 %collective-permute-done.3 = bf16[2,128,1024]{1,2,0:T(8,128)(2,1)} collective-permute-done((bf16[2,128,1024]{1,2,0:T(8,128)(2,1)}, bf16[2,128,1024]{1,2,0:T(8,128)(2,1)}, u32[]{:S(2)}, u32[]{:S(2)}) %collective-permute-start.3) | collective-permute-done | bytes 524320 | tf_op jit(solution)/shard_map/ppermute | solution.py:20
  68.1 4.3 %fusion.70 = (f32[8,128]{1,0:T(8,128)S(1)}, f32[8,128,640]{2,1,0:T(8,128)}) fusion(pred[128,640]{1,0:T(8,128)(4,1)S(1)} %and_and_fusion, bf16[640,8,128]{0,2,1:T(8,128)(2,1)} %bitcast.265, bf16[128,8,64]{2,0,1:T(8,128)(2,1)} %get-tuple-element.31, bf16[128,8,64]{2,0,1:T(8,128)(2,1)} %get-tuple-element.30), kind=kOutput, calls=%fused_computation.186 | convolution fusion | flops 171573888 | bytes 4280320 | tf_op jit(solution)/shard_map/sub | solution.py:96
  72.5 2.6 %fusion.6 = bf16[8,128,128]{2,1,0:T(8,128)(2,1)S(1)} fusion(bf16[640,8,128]{0,2,1:T(8,128)(2,1)S(1)} %bitcast.264, f32[8,128,640]{2,1,0:T(8,128)} %get-tuple-element.90, f32[8,128]{1,0:T(8,128)S(1)} %get-tuple-element.89), kind=kOutput, calls=%fused_computation.18 | convolution fusion | flops 169213952 | bytes 4198400 | tf_op jit(solution)/shard_map/hqk,khd->qhd/dot_general | solution.py:98
  76.8 2.1 collective-permute-done.4
  79.5 5.4 %collective-permute-start.6 = (bf16[1,32,2176]{2,1,0:T(8,128)(2,1)S(1)}, bf16[1,32,2176]{2,1,0:T(8,128)(2,1)S(1)}, u32[]{:S(2)}, u32[]{:S(2)}) collective-permute-start(bf16[1,32,2176]{2,1,0:T(8,128)(2,1)S(1)} %get-tuple-element.78), channel_id=1, source_target_pairs={{0,2},{1,3},{2,0},{3,1},{4,6},{5,7},{6,4},{7,5},{8,10},{9,11},{10,... | collective-permute-start | bytes 417800 | tf_op jit(solution)/shard_map/ppermute | solution.py:24
  87.2 6.2 %collective-permute-start.15 = (bf16[1,64,2176]{2,1,0:T(8,128)(2,1)S(1)}, bf16[1,64,2176]{2,1,0:T(8,128)(2,1)S(1)}, u32[]{:S(2)}, u32[]{:S(2)}) collective-permute-start(bf16[1,64,2176]{2,1,0:T(8,128)(2,1)S(1)} %get-tuple-element.59), channel_id=1, source_target_pairs={{4,0},{5,1},{6,2},{7,3},{8,4},{9,5},{10,6},{11,7},{12,8},{13,9},{1... | collective-permute-start | bytes 835592 | tf_op jit(solution)/shard_map/ppermute | solution.py:29
  94.5 2.1 collective-permute-start.7
  96.6 4.5 %collective-permute-done.5 = bf16[1,32,2176]{2,1,0:T(8,128)(2,1)S(1)} collective-permute-done((bf16[1,32,2176]{2,1,0:T(8,128)(2,1)S(1)}, bf16[1,32,2176]{2,1,0:T(8,128)(2,1)S(1)}, u32[]{:S(2)}, u32[]{:S(2)}) %collective-permute-start.5) | collective-permute-done | bytes 139296 | tf_op jit(solution)/shard_map/ppermute | solution.py:24
  102.7 4.8 %collective-permute-done.16 = bf16[1,64,2176]{2,1,0:T(8,128)(2,1)S(1)} collective-permute-done((bf16[1,64,2176]{2,1,0:T(8,128)(2,1)S(1)}, bf16[1,64,2176]{2,1,0:T(8,128)(2,1)S(1)}, u32[]{:S(2)}, u32[]{:S(2)}) %collective-permute-start.16) | collective-permute-done | bytes 278560 | tf_op jit(solution)/shard_map/ppermute | solution.py:29
  109.1 8.3 %collective-permute-done.28 = bf16[1,64,2176]{2,1,0:T(8,128)(2,1)S(1)} collective-permute-done((bf16[1,64,2176]{2,1,0:T(8,128)(2,1)S(1)}, bf16[1,64,2176]{2,1,0:T(8,128)(2,1)S(1)}, u32[]{:S(2)}, u32[]{:S(2)}) %collective-permute-start.28) | collective-permute-done | bytes 278560 | tf_op jit(solution)/shard_map/ppermute | solution.py:29
  119.2 3.4 %collective-permute-done.30 = bf16[1,32,2176]{2,1,0:T(8,128)(2,1)S(1)} collective-permute-done((bf16[1,32,2176]{2,1,0:T(8,128)(2,1)S(1)}, bf16[1,32,2176]{2,1,0:T(8,128)(2,1)S(1)}, u32[]{:S(2)}, u32[]{:S(2)}) %collective-permute-start.30) | collective-permute-done | bytes 139296 | tf_op jit(solution)/shard_map/ppermute | solution.py:24
  125.0 5.9 %shard_map.140 = bf16[2,256,1024]{2,1,0:T(8,128)(2,1)S(1)} custom-call(s32[2]{0:T(128)S(1)} %pad_add_fusion.place_ref, bf16[256,2176]{1,0:T(8,128)(2,1)S(1)} %bitcast.223, bf16[704,2048]{1,0:T(8,128)(2,1)S(1)} %bitcast.218, bf16[704,2048]{1,0:T(8,128)(2,1)} %bitcast.228, bf16[704,2048]{1,0:T(8,128)(2,1)} %bitcast.234), custom_call_target="tpu_custom_call" | custom-call | flops 2214592512 | bytes 10747904 | tf_op jit(solution)/shard_map/pallas_call | solution.py:139
  133.5 5.9 %shard_map.144 = bf16[2,256,1024]{2,1,0:T(8,128)(2,1)S(1)} custom-call(s32[2]{0:T(128)S(1)} %pad_add_fusion.place_ref, bf16[256,2176]{1,0:T(8,128)(2,1)S(1)} %bitcast.225, bf16[704,2048]{1,0:T(8,128)(2,1)S(1)} %bitcast.219, bf16[704,2048]{1,0:T(8,128)(2,1)} %bitcast.229, bf16[704,2048]{1,0:T(8,128)(2,1)} %bitcast.235), custom_call_target="tpu_custom_call" | custom-call | flops 2214592512 | bytes 10747904 | tf_op jit(solution)/shard_map/pallas_call | solution.py:139
  140.5 2.8 %collective-permute-done.19 = bf16[2,2,32,2176]{3,2,1,0:T(8,128)(2,1)S(1)} collective-permute-done((bf16[2,2,32,2176]{3,2,1,0:T(8,128)(2,1)S(1)}, bf16[2,2,32,2176]{3,2,1,0:T(8,128)(2,1)S(1)}, u32[]{:S(2)}, u32[]{:S(2)}) %collective-permute-start.19) | collective-permute-done | bytes 557088 | tf_op jit(solution)/shard_map/ppermute | solution.py:24
  144.4 5.9 %shard_map.141 = bf16[2,256,1024]{2,1,0:T(8,128)(2,1)S(1)} custom-call(s32[2]{0:T(128)S(1)} %pad_add_fusion.place_ref, bf16[256,2176]{1,0:T(8,128)(2,1)S(1)} %collective-permute-done.9.rows_ref, bf16[704,2048]{1,0:T(8,128)(2,1)S(1)} %bitcast.220, bf16[704,2048]{1,0:T(8,128)(2,1)} %bitcast.230, bf16[704,2048]{1,0:T(8,128)(2,1)} %bitcast.236), custom_call_target="tpu_custom_call" | custom-call | flops 2214592512 | bytes 10747904 | tf_op jit(solution)/shard_map/pallas_call | solution.py:139
  152.0 9.8 %shard_map.142 = bf16[2,512,1024]{2,1,0:T(8,128)(2,1)S(1)} custom-call(s32[2]{0:T(128)S(1)} %pad_add_fusion.place_ref, bf16[512,2176]{1,0:T(8,128)(2,1)S(1)} %bitcast.227, bf16[704,2048]{1,0:T(8,128)(2,1)} %bitcast.216, bf16[704,2048]{1,0:T(8,128)(2,1)} %bitcast.231, bf16[704,2048]{1,0:T(8,128)(2,1)} %bitcast.237), custom_call_target="tpu_custom_call" | custom-call | flops 4429185024 | bytes 12845056 | tf_op jit(solution)/shard_map/pallas_call | solution.py:139
  164.4 5.9 %shard_map.145 = bf16[2,256,1024]{2,1,0:T(8,128)(2,1)S(1)} custom-call(s32[2]{0:T(128)S(1)} %pad_add_fusion.place_ref, bf16[256,2176]{1,0:T(8,128)(2,1)S(1)} %collective-permute-done.33.rows_ref, bf16[704,2048]{1,0:T(8,128)(2,1)S(1)} %bitcast.221, bf16[704,2048]{1,0:T(8,128)(2,1)} %bitcast.232, bf16[704,2048]{1,0:T(8,128)(2,1)} %bitcast.238), custom_call_target="tpu_custom_call" | custom-call | flops 2214592512 | bytes 10747904 | tf_op jit(solution)/shard_map/pallas_call | solution.py:139
  173.8 5.7 %collective-permute-done.13 = bf16[2,1,128,512]{3,2,1,0:T(8,128)(2,1)S(1)} collective-permute-done((bf16[2,1,128,512]{3,2,1,0:T(8,128)(2,1)S(1)}, bf16[2,1,128,512]{3,2,1,0:T(8,128)(2,1)S(1)}, u32[]{:S(2)}, u32[]{:S(2)}) %collective-permute-start.13) | collective-permute-done | bytes 262176 | tf_op jit(solution)/shard_map/ppermute | solution.py:24
  182.5 9.8 %shard_map.143 = bf16[2,512,1024]{2,1,0:T(8,128)(2,1)S(1)} custom-call(s32[2]{0:T(128)S(1)} %pad_add_fusion.place_ref, bf16[512,2176]{1,0:T(8,128)(2,1)S(1)} %collective-permute-done.21.rows_ref, bf16[704,2048]{1,0:T(8,128)(2,1)} %bitcast.217, bf16[704,2048]{1,0:T(8,128)(2,1)} %bitcast.233, bf16[704,2048]{1,0:T(8,128)(2,1)} %bitcast.239), custom_call_target="tpu_custom_call" | custom-call | flops 4429185024 | bytes 12845056 | tf_op jit(solution)/shard_map/pallas_call | solution.py:139
  197.8 5.6 %collective-permute-done.37 = bf16[2,1,128,512]{3,2,1,0:T(8,128)(2,1)S(1)} collective-permute-done((bf16[2,1,128,512]{3,2,1,0:T(8,128)(2,1)S(1)}, bf16[2,1,128,512]{3,2,1,0:T(8,128)(2,1)S(1)}, u32[]{:S(2)}, u32[]{:S(2)}) %collective-permute-start.37) | collective-permute-done | bytes 262176 | tf_op jit(solution)/shard_map/ppermute | solution.py:24
  211.7 9.4 %collective-permute-done.25 = bf16[2,2,128,512]{3,2,1,0:T(8,128)(2,1)S(1)} collective-permute-done((bf16[2,2,128,512]{3,2,1,0:T(8,128)(2,1)S(1)}, bf16[2,2,128,512]{3,2,1,0:T(8,128)(2,1)S(1)}, u32[]{:S(2)}, u32[]{:S(2)}) %collective-permute-start.25) | collective-permute-done | bytes 524320 | tf_op jit(solution)/shard_map/ppermute | solution.py:24
  224.1 3.9 %collective-permute-done.26 = bf16[2,128,512]{2,1,0:T(8,128)(2,1)S(1)} collective-permute-done((bf16[2,128,512]{2,1,0:T(8,128)(2,1)S(1)}, bf16[2,128,512]{2,1,0:T(8,128)(2,1)S(1)}, u32[]{:S(2)}, u32[]{:S(2)}) %collective-permute-start.26) | collective-permute-done | bytes 262176 | tf_op jit(solution)/shard_map/ppermute | solution.py:24
  229.2 2.5 %collective-permute-start.40 = (bf16[128,1024]{1,0:T(8,128)(2,1)S(1)}, bf16[128,1024]{1,0:T(8,128)(2,1)S(1)}, u32[]{:S(2)}, u32[]{:S(2)}) collective-permute-start(bf16[128,1024]{1,0:T(8,128)(2,1)S(1)} %get-tuple-element.61), channel_id=1, source_target_pairs={{0,12},{1,13},{2,14},{3,15},{4,0},{5,1},{6,2},{7,3},{8,4},{9,5},{1... | collective-permute-start | bytes 786440 | tf_op jit(solution)/shard_map/ppermute | solution.py:36
  231.8 7.4 %collective-permute-done.39 = bf16[128,1024]{1,0:T(8,128)(2,1)S(1)} collective-permute-done((bf16[128,1024]{1,0:T(8,128)(2,1)S(1)}, bf16[128,1024]{1,0:T(8,128)(2,1)S(1)}, u32[]{:S(2)}, u32[]{:S(2)}) %collective-permute-start.39) | collective-permute-done | bytes 262176 | tf_op jit(solution)/shard_map/ppermute | solution.py:36
  239.2 7.1 %collective-permute-done.40 = bf16[128,1024]{1,0:T(8,128)(2,1)S(1)} collective-permute-done((bf16[128,1024]{1,0:T(8,128)(2,1)S(1)}, bf16[128,1024]{1,0:T(8,128)(2,1)S(1)}, u32[]{:S(2)}, u32[]{:S(2)}) %collective-permute-start.40) | collective-permute-done | bytes 262176 | tf_op jit(solution)/shard_map/ppermute | solution.py:36
  (225 shorter events, 67.4 us)
Async XLA Ops:
  5.9 16.3 %collective-permute-start = (bf16[2,128,1024]{1,2,0:T(8,128)(2,1)}, bf16[2,128,1024]{1,2,0:T(8,128)(2,1)}, u32[]{:S(2)}, u32[]{:S(2)}) collective-permute-start(bf16[2,128,1024]{1,2,0:T(8,128)(2,1)} %get-tuple-element.62), channel_id=1, source_target_pairs={{0,1},{1,2},{2,3},{3,4},{4,5},{5,6},{6,7},{7,8},{8,9},{9,10},{10,1... | collective-permute-start | bytes 1572872 | tf_op jit(solution)/shard_map/ppermute | solution.py:20
  22.2 15.0 %collective-permute-start.1 = (bf16[2,128,1024]{1,2,0:T(8,128)(2,1)}, bf16[2,128,1024]{1,2,0:T(8,128)(2,1)}, u32[]{:S(2)}, u32[]{:S(2)}) collective-permute-start(bf16[2,128,1024]{1,2,0:T(8,128)(2,1)} %collective-permute-done), channel_id=1, source_target_pairs={{0,1},{1,2},{2,3},{3,4},{4,5},{5,6},{6,7},{7,8},{8,9},{9,10},{10,1... | collective-permute-start | bytes 1572872 | tf_op jit(solution)/shard_map/ppermute | solution.py:20
  37.2 14.1 %collective-permute-start.2 = (bf16[2,128,1024]{1,2,0:T(8,128)(2,1)}, bf16[2,128,1024]{1,2,0:T(8,128)(2,1)}, u32[]{:S(2)}, u32[]{:S(2)}) collective-permute-start(bf16[2,128,1024]{1,2,0:T(8,128)(2,1)} %collective-permute-done.1), channel_id=1, source_target_pairs={{0,1},{1,2},{2,3},{3,4},{4,5},{5,6},{6,7},{7,8},{8,9},{9,10},{10,1... | collective-permute-start | bytes 1572872 | tf_op jit(solution)/shard_map/ppermute | solution.py:20
  51.3 14.0 %collective-permute-start.3 = (bf16[2,128,1024]{1,2,0:T(8,128)(2,1)}, bf16[2,128,1024]{1,2,0:T(8,128)(2,1)}, u32[]{:S(2)}, u32[]{:S(2)}) collective-permute-start(bf16[2,128,1024]{1,2,0:T(8,128)(2,1)} %collective-permute-done.2), channel_id=1, source_target_pairs={{0,1},{1,2},{2,3},{3,4},{4,5},{5,6},{6,7},{7,8},{8,9},{9,10},{10,1... | collective-permute-start | bytes 1572872 | tf_op jit(solution)/shard_map/ppermute | solution.py:20
  79.5 15.0 %collective-permute-start.6 = (bf16[1,32,2176]{2,1,0:T(8,128)(2,1)S(1)}, bf16[1,32,2176]{2,1,0:T(8,128)(2,1)S(1)}, u32[]{:S(2)}, u32[]{:S(2)}) collective-permute-start(bf16[1,32,2176]{2,1,0:T(8,128)(2,1)S(1)} %get-tuple-element.78), channel_id=1, source_target_pairs={{0,2},{1,3},{2,0},{3,1},{4,6},{5,7},{6,4},{7,5},{8,10},{9,11},{10,... | collective-permute-start | bytes 417800 | tf_op jit(solution)/shard_map/ppermute | solution.py:24
  87.2 15.4 %collective-permute-start.15 = (bf16[1,64,2176]{2,1,0:T(8,128)(2,1)S(1)}, bf16[1,64,2176]{2,1,0:T(8,128)(2,1)S(1)}, u32[]{:S(2)}, u32[]{:S(2)}) collective-permute-start(bf16[1,64,2176]{2,1,0:T(8,128)(2,1)S(1)} %get-tuple-element.59), channel_id=1, source_target_pairs={{4,0},{5,1},{6,2},{7,3},{8,4},{9,5},{10,6},{11,7},{12,8},{13,9},{1... | collective-permute-start | bytes 835592 | tf_op jit(solution)/shard_map/ppermute | solution.py:29
  93.4 14.0 %collective-permute-start.16 = (bf16[1,64,2176]{2,1,0:T(8,128)(2,1)S(1)}, bf16[1,64,2176]{2,1,0:T(8,128)(2,1)S(1)}, u32[]{:S(2)}, u32[]{:S(2)}) collective-permute-start(bf16[1,64,2176]{2,1,0:T(8,128)(2,1)S(1)} %get-tuple-element.59), channel_id=1, source_target_pairs={{12,0},{13,1},{14,2},{15,3},{0,4},{1,5},{2,6},{3,7},{4,8},{5,9},{6... | collective-permute-start | bytes 835592 | tf_op jit(solution)/shard_map/ppermute | solution.py:29
  93.4 24.0 %collective-permute-start.28 = (bf16[1,64,2176]{2,1,0:T(8,128)(2,1)S(1)}, bf16[1,64,2176]{2,1,0:T(8,128)(2,1)S(1)}, u32[]{:S(2)}, u32[]{:S(2)}) collective-permute-start(bf16[1,64,2176]{2,1,0:T(8,128)(2,1)S(1)} %get-tuple-element.59), channel_id=1, source_target_pairs={{8,0},{9,1},{10,2},{11,3},{12,4},{13,5},{14,6},{15,7},{0,8},{1,9},... | collective-permute-start | bytes 835592 | tf_op jit(solution)/shard_map/ppermute | solution.py:29
  94.5 24.3 %collective-permute-start.7 = (bf16[2,1,32,2176]{3,2,1,0:T(8,128)(2,1)S(1)}, bf16[2,1,32,2176]{3,2,1,0:T(8,128)(2,1)S(1)}, u32[]{:S(2)}, u32[]{:S(2)}) collective-permute-start(bf16[2,1,32,2176]{3,2,1,0:T(8,128)(2,1)S(1)} %pad_maximum_fusion.11), channel_id=1, source_target_pairs={{0,1},{1,0},{2,3},{3,2},{4,5},{5,4},{6,7},{7,6},{8,9},{9,8},{10,11... | collective-permute-start | bytes 835592 | tf_op jit(solution)/shard_map/ppermute | solution.py:24
  101.1 17.7 %collective-permute-start.8 = (bf16[2,1,32,2176]{3,2,1,0:T(8,128)(2,1)S(1)}, bf16[2,1,32,2176]{3,2,1,0:T(8,128)(2,1)S(1)}, u32[]{:S(2)}, u32[]{:S(2)}) collective-permute-start(bf16[2,1,32,2176]{3,2,1,0:T(8,128)(2,1)S(1)} %pad_maximum_fusion.12), channel_id=1, source_target_pairs={{0,2},{1,3},{2,0},{3,1},{4,6},{5,7},{6,4},{7,5},{8,10},{9,11},{10,... | collective-permute-start | bytes 835592 | tf_op jit(solution)/shard_map/ppermute | solution.py:24
  107.5 23.4 %collective-permute-start.18 = (bf16[2,32,2176]{2,1,0:T(8,128)(2,1)S(1)}, bf16[2,32,2176]{2,1,0:T(8,128)(2,1)S(1)}, u32[]{:S(2)}, u32[]{:S(2)}) collective-permute-start(bf16[2,32,2176]{2,1,0:T(8,128)(2,1)S(1)} %get-tuple-element.56), channel_id=1, source_target_pairs={{0,2},{1,3},{2,0},{3,1},{4,6},{5,7},{6,4},{7,5},{8,10},{9,11},{10,... | collective-permute-start | bytes 835592 | tf_op jit(solution)/shard_map/ppermute | solution.py:24
  109.1 23.0 %collective-permute-start.17 = (bf16[2,32,2176]{2,1,0:T(8,128)(2,1)S(1)}, bf16[2,32,2176]{2,1,0:T(8,128)(2,1)S(1)}, u32[]{:S(2)}, u32[]{:S(2)}) collective-permute-start(bf16[2,32,2176]{2,1,0:T(8,128)(2,1)S(1)} %get-tuple-element.57), channel_id=1, source_target_pairs={{0,1},{1,0},{2,3},{3,2},{4,5},{5,4},{6,7},{7,6},{8,9},{9,8},{10,11... | collective-permute-start | bytes 835592 | tf_op jit(solution)/shard_map/ppermute | solution.py:24
  119.1 25.3 %collective-permute-start.9 = (bf16[256,2176]{1,0:T(8,128)(2,1)S(1)}, bf16[256,2176]{1,0:T(8,128)(2,1)S(1)}, u32[]{:S(2)}, u32[]{:S(2)}) collective-permute-start(bf16[256,2176]{1,0:T(8,128)(2,1)S(1)} %bitcast.222), channel_id=1, source_target_pairs={{16,0},{0,16},{17,1},{1,17},{18,2},{2,18},{19,3},{3,19},{20,4},{4,... | collective-permute-start | bytes 3342344 | tf_op jit(solution)/shard_map/ppermute | solution.py:43
  122.6 10.5 %collective-permute-start.31 = (bf16[2,1,32,2176]{3,2,1,0:T(8,128)(2,1)S(1)}, bf16[2,1,32,2176]{3,2,1,0:T(8,128)(2,1)S(1)}, u32[]{:S(2)}, u32[]{:S(2)}) collective-permute-start(bf16[2,1,32,2176]{3,2,1,0:T(8,128)(2,1)S(1)} %pad_maximum_fusion.13), channel_id=1, source_target_pairs={{0,1},{1,0},{2,3},{3,2},{4,5},{5,4},{6,7},{7,6},{8,9},{9,8},{10,11... | collective-permute-start | bytes 835592 | tf_op jit(solution)/shard_map/ppermute | solution.py:24
  124.2 9.0 %collective-permute-start.32 = (bf16[2,1,32,2176]{3,2,1,0:T(8,128)(2,1)S(1)}, bf16[2,1,32,2176]{3,2,1,0:T(8,128)(2,1)S(1)}, u32[]{:S(2)}, u32[]{:S(2)}) collective-permute-start(bf16[2,1,32,2176]{3,2,1,0:T(8,128)(2,1)S(1)} %pad_maximum_fusion.14), channel_id=1, source_target_pairs={{0,2},{1,3},{2,0},{3,1},{4,6},{5,7},{6,4},{7,5},{8,10},{9,11},{10,... | collective-permute-start | bytes 835592 | tf_op jit(solution)/shard_map/ppermute | solution.py:24
  131.1 12.2 %collective-permute-start.19 = (bf16[2,2,32,2176]{3,2,1,0:T(8,128)(2,1)S(1)}, bf16[2,2,32,2176]{3,2,1,0:T(8,128)(2,1)S(1)}, u32[]{:S(2)}, u32[]{:S(2)}) collective-permute-start(bf16[2,2,32,2176]{3,2,1,0:T(8,128)(2,1)S(1)} %pad_maximum_fusion.6), channel_id=1, source_target_pairs={{0,1},{1,0},{2,3},{3,2},{4,5},{5,4},{6,7},{7,6},{8,9},{9,8},{10,11... | collective-permute-start | bytes 1671176 | tf_op jit(solution)/shard_map/ppermute | solution.py:24
  132.2 11.6 %collective-permute-start.20 = (bf16[2,2,32,2176]{3,2,1,0:T(8,128)(2,1)S(1)}, bf16[2,2,32,2176]{3,2,1,0:T(8,128)(2,1)S(1)}, u32[]{:S(2)}, u32[]{:S(2)}) collective-permute-start(bf16[2,2,32,2176]{3,2,1,0:T(8,128)(2,1)S(1)} %pad_maximum_fusion.7), channel_id=1, source_target_pairs={{0,2},{1,3},{2,0},{3,1},{4,6},{5,7},{6,4},{7,5},{8,10},{9,11},{10,... | collective-permute-start | bytes 1671176 | tf_op jit(solution)/shard_map/ppermute | solution.py:24
  133.5 29.8 %collective-permute-start.33 = (bf16[256,2176]{1,0:T(8,128)(2,1)S(1)}, bf16[256,2176]{1,0:T(8,128)(2,1)S(1)}, u32[]{:S(2)}, u32[]{:S(2)}) collective-permute-start(bf16[256,2176]{1,0:T(8,128)(2,1)S(1)} %bitcast.224), channel_id=1, source_target_pairs={{16,0},{0,16},{17,1},{1,17},{18,2},{2,18},{19,3},{3,19},{20,4},{4,... | collective-permute-start | bytes 3342344 | tf_op jit(solution)/shard_map/ppermute | solution.py:43
  144.4 38.1 %collective-permute-start.21 = (bf16[512,2176]{1,0:T(8,128)(2,1)S(1)}, bf16[512,2176]{1,0:T(8,128)(2,1)S(1)}, u32[]{:S(2)}, u32[]{:S(2)}) collective-permute-start(bf16[512,2176]{1,0:T(8,128)(2,1)S(1)} %bitcast.226), channel_id=1, source_target_pairs={{16,0},{0,16},{17,1},{1,17},{18,2},{2,18},{19,3},{3,19},{20,4},{4,... | collective-permute-start | bytes 6684680 | tf_op jit(solution)/shard_map/ppermute | solution.py:43
  151.5 18.8 %collective-permute-start.10 = (bf16[2,256,1024]{2,1,0:T(8,128)(2,1)}, bf16[2,256,1024]{2,1,0:T(8,128)(2,1)S(1)}, u32[]{:S(2)}, u32[]{:S(2)}) collective-permute-start(bf16[2,256,1024]{2,1,0:T(8,128)(2,1)} %pad_maximum_fusion.4), channel_id=1, source_target_pairs={{16,0},{0,16},{17,1},{1,17},{18,2},{2,18},{19,3},{3,19},{20,4},{4,... | collective-permute-start | bytes 3145736 | tf_op jit(solution)/shard_map/ppermute | solution.py:43
  171.2 8.3 %collective-permute-start.13 = (bf16[2,1,128,512]{3,2,1,0:T(8,128)(2,1)S(1)}, bf16[2,1,128,512]{3,2,1,0:T(8,128)(2,1)S(1)}, u32[]{:S(2)}, u32[]{:S(2)}) collective-permute-start(bf16[2,1,128,512]{3,2,1,0:T(8,128)(2,1)S(1)} %pad_maximum_fusion.15), channel_id=1, source_target_pairs={{0,1},{1,0},{2,3},{3,2},{4,5},{5,4},{6,7},{7,6},{8,9},{9,8},{10,11... | collective-permute-start | bytes 786440 | tf_op jit(solution)/shard_map/ppermute | solution.py:24
  172.7 21.2 %collective-permute-start.34 = (bf16[2,256,1024]{2,1,0:T(8,128)(2,1)S(1)}, bf16[2,256,1024]{2,1,0:T(8,128)(2,1)S(1)}, u32[]{:S(2)}, u32[]{:S(2)}) collective-permute-start(bf16[2,256,1024]{2,1,0:T(8,128)(2,1)S(1)} %pad_maximum_fusion.5), channel_id=1, source_target_pairs={{16,0},{0,16},{17,1},{1,17},{18,2},{2,18},{19,3},{3,19},{20,4},{4,... | collective-permute-start | bytes 3145736 | tf_op jit(solution)/shard_map/ppermute | solution.py:43
  172.8 8.8 %collective-permute-start.11 = (bf16[2,1,128,512]{3,2,1,0:T(8,128)(2,1)S(1)}, bf16[2,1,128,512]{3,2,1,0:T(8,128)(2,1)S(1)}, u32[]{:S(2)}, u32[]{:S(2)}) collective-permute-start(bf16[2,1,128,512]{3,2,1,0:T(8,128)(2,1)S(1)} %slice.359), channel_id=1, source_target_pairs={{0,2},{1,3},{2,0},{3,1},{4,6},{5,7},{6,4},{7,5},{8,10},{9,11},{10,... | collective-permute-start | bytes 786440 | tf_op jit(solution)/shard_map/ppermute | solution.py:24
  179.6 52.2 %collective-permute-start.14 = (bf16[1,128,512]{2,1,0:T(8,128)(2,1)S(1)}, bf16[1,128,512]{2,1,0:T(8,128)(2,1)S(1)}, u32[]{:S(2)}, u32[]{:S(2)}) collective-permute-start(bf16[1,128,512]{2,1,0:T(8,128)(2,1)S(1)} %fusion.36), channel_id=1, source_target_pairs={{0,2},{1,3},{2,0},{3,1},{4,6},{5,7},{6,4},{7,5},{8,10},{9,11},{10,... | collective-permute-start | bytes 393224 | tf_op jit(solution)/shard_map/ppermute | solution.py:24
  181.7 50.0 %collective-permute-start.12 = (bf16[1,128,512]{2,1,0:T(8,128)(2,1)S(1)}, bf16[1,128,512]{2,1,0:T(8,128)(2,1)S(1)}, u32[]{:S(2)}, u32[]{:S(2)}) collective-permute-start(bf16[1,128,512]{2,1,0:T(8,128)(2,1)S(1)} %fusion.35), channel_id=1, source_target_pairs={{0,1},{1,0},{2,3},{3,2},{4,5},{5,4},{6,7},{7,6},{8,9},{9,8},{10,11... | collective-permute-start | bytes 393224 | tf_op jit(solution)/shard_map/ppermute | solution.py:24
  193.7 12.2 %collective-permute-start.22 = (bf16[2,512,1024]{2,1,0:T(8,128)(2,1)S(1)}, bf16[2,512,1024]{2,1,0:T(8,128)(2,1)S(1)}, u32[]{:S(2)}, u32[]{:S(2)}) collective-permute-start(bf16[2,512,1024]{2,1,0:T(8,128)(2,1)S(1)} %pad_maximum_fusion.1), channel_id=1, source_target_pairs={{16,0},{0,16},{17,1},{1,17},{18,2},{2,18},{19,3},{3,19},{20,4},{4,... | collective-permute-start | bytes 6291464 | tf_op jit(solution)/shard_map/ppermute | solution.py:43
  195.3 8.1 %collective-permute-start.37 = (bf16[2,1,128,512]{3,2,1,0:T(8,128)(2,1)S(1)}, bf16[2,1,128,512]{3,2,1,0:T(8,128)(2,1)S(1)}, u32[]{:S(2)}, u32[]{:S(2)}) collective-permute-start(bf16[2,1,128,512]{3,2,1,0:T(8,128)(2,1)S(1)} %pad_maximum_fusion.16), channel_id=1, source_target_pairs={{0,1},{1,0},{2,3},{3,2},{4,5},{5,4},{6,7},{7,6},{8,9},{9,8},{10,11... | collective-permute-start | bytes 786440 | tf_op jit(solution)/shard_map/ppermute | solution.py:24
  207.9 13.2 %collective-permute-start.25 = (bf16[2,2,128,512]{3,2,1,0:T(8,128)(2,1)S(1)}, bf16[2,2,128,512]{3,2,1,0:T(8,128)(2,1)S(1)}, u32[]{:S(2)}, u32[]{:S(2)}) collective-permute-start(bf16[2,2,128,512]{3,2,1,0:T(8,128)(2,1)S(1)} %pad_maximum_fusion.9), channel_id=1, source_target_pairs={{0,1},{1,0},{2,3},{3,2},{4,5},{5,4},{6,7},{7,6},{8,9},{9,8},{10,11... | collective-permute-start | bytes 1572872 | tf_op jit(solution)/shard_map/ppermute | solution.py:24
  210.9 11.4 %collective-permute-start.23 = (bf16[2,2,128,512]{3,2,1,0:T(8,128)(2,1)S(1)}, bf16[2,2,128,512]{3,2,1,0:T(8,128)(2,1)S(1)}, u32[]{:S(2)}, u32[]{:S(2)}) collective-permute-start(bf16[2,2,128,512]{3,2,1,0:T(8,128)(2,1)S(1)} %slice.381), channel_id=1, source_target_pairs={{0,2},{1,3},{2,0},{3,1},{4,6},{5,7},{6,4},{7,5},{8,10},{9,11},{10,... | collective-permute-start | bytes 1572872 | tf_op jit(solution)/shard_map/ppermute | solution.py:24
  224.0 15.2 %collective-permute-start.39 = (bf16[128,1024]{1,0:T(8,128)(2,1)S(1)}, bf16[128,1024]{1,0:T(8,128)(2,1)S(1)}, u32[]{:S(2)}, u32[]{:S(2)}) collective-permute-start(bf16[128,1024]{1,0:T(8,128)(2,1)S(1)} %maximum_bitcast_fusion.10), channel_id=1, source_target_pairs={{0,8},{1,9},{2,10},{3,11},{4,12},{5,13},{6,14},{7,15},{8,0},{9,1},... | collective-permute-start | bytes 786440 | tf_op jit(solution)/shard_map/ppermute | solution.py:36
  229.2 17.1 %collective-permute-start.40 = (bf16[128,1024]{1,0:T(8,128)(2,1)S(1)}, bf16[128,1024]{1,0:T(8,128)(2,1)S(1)}, u32[]{:S(2)}, u32[]{:S(2)}) collective-permute-start(bf16[128,1024]{1,0:T(8,128)(2,1)S(1)} %get-tuple-element.61), channel_id=1, source_target_pairs={{0,12},{1,13},{2,14},{3,15},{4,0},{5,1},{6,2},{7,3},{8,4},{9,5},{1... | collective-permute-start | bytes 786440 | tf_op jit(solution)/shard_map/ppermute | solution.py:36
  231.7 14.7 %collective-permute-start.27 = (bf16[128,1024]{1,0:T(8,128)(2,1)S(1)}, bf16[128,1024]{1,0:T(8,128)(2,1)S(1)}, u32[]{:S(2)}, u32[]{:S(2)}) collective-permute-start(bf16[128,1024]{1,0:T(8,128)(2,1)S(1)} %get-tuple-element.60), channel_id=1, source_target_pairs={{0,4},{1,5},{2,6},{3,7},{4,8},{5,9},{6,10},{7,11},{8,12},{9,13},{1... | collective-permute-start | bytes 786440 | tf_op jit(solution)/shard_map/ppermute | solution.py:36
  (24 other events, 89.1 us)

commit v2 on v1

--- a/solution.py
+++ b/solution.py
@@ -18,10 +18,6 @@
     devices = range(lax.axis_size(axis))
     route = [(i - distance, i) for i in devices if i - distance in devices]
     return lax.ppermute(block, axis, route)
-
-
-def flipped(block, mask):
-    return lax.ppermute(block, "blk", [(i, i ^ mask) for i in range(lax.axis_size("blk"))])
 
 
 def from_plane(block, ahead):
@@ -113,11 +109,22 @@
     return jnp.pad(lanes, ((0, 0), (0, -lanes.shape[1] % 128)))
 
 
-def expert_kernel(experts, place_ref, rows_ref, gate_ref, up_ref, down_ref, out_ref):
+def crossed(block, first):
+    cores, count = lax.axis_size("tok"), lax.axis_size("blk")
+    route = []
+    for core in range(cores):
+        mask = 1 if (core % 2 == 0) == first else 2
+        route += [(core * count + i, core * count + (i ^ mask)) for i in range(count)]
+    return lax.ppermute(block, ("tok", "blk"), route)
+
+
+def expert_kernel(experts, ahead, place_ref, near_ref, far_ref, gate_ref, up_ref, down_ref, *outs):
     width = gate_ref.shape[1]
-    parts, _, part_width = out_ref.shape
-    rows = rows_ref[:, :width]
-    lanes = rows_ref[:, width:].astype(jnp.float32)
+    parts = len(outs)
+    blocks, part_rows, part_width = outs[0].shape
+    held = jnp.concatenate([near_ref[...], far_ref[...]], axis=0)
+    rows = held[:, :width]
+    lanes = held[:, width:].astype(jnp.float32)
     lane_ids = lax.broadcasted_iota(jnp.int32, lanes.shape, 1)
     named = (lane_ids < 3 * experts) & (lane_ids % experts == place_ref[0])
     weight = jnp.sum(jnp.where(named, lanes, 0.0), axis=1, keepdims=True)
@@ -126,51 +133,32 @@
     up_act = lax.dot_general(rows, up_ref[...], turned, preferred_element_type=jnp.float32)
     hidden = (gate_act / (1.0 + jnp.exp(-gate_act)) * up_act).astype(jnp.bfloat16)
     for part in range(parts):
-        columns = slice(part * part_width, (part + 1) * part_width)
+        start = lax.rem(place_ref[1] + part, parts) * part_width
+        columns = pl.ds(pl.multiple_of(start, 128), part_width)
         product = jnp.dot(hidden, down_ref[:, columns], preferred_element_type=jnp.float32)
-        slot = lax.rem(part - place_ref[1] + parts, parts)
-        out_ref[pl.ds(slot, 1)] = (weight * product).astype(jnp.bfloat16)[None]
-
-
-def run_expert(place, rows, w_gate, w_up, w_down, experts, parts, tile):
-    count, full_width = rows.shape
+        product = (weight * product).astype(jnp.bfloat16)
+        order = (0, 2, 1, 3) if (part - ahead) % 2 else (0, 1, 2, 3)
+        for block in range(blocks):
+            outs[part][order[block]] = product[block * part_rows : (block + 1) * part_rows]
+
+
+def run_expert(place, near, far, w_gate, w_up, w_down, experts, parts, ahead):
+    count = 2 * near.shape[0]
     units, width = w_gate.shape
-    whole = functools.partial(pl.BlockSpec, memory_space=pltpu.VMEM)
+    whole = pl.BlockSpec(memory_space=pltpu.VMEM)
+    out_shape = jax.ShapeDtypeStruct((PLANE, count // PLANE, width // parts), jnp.bfloat16)
     return pl.pallas_call(
-        functools.partial(expert_kernel, experts),
-        grid_spec=pltpu.PrefetchScalarGridSpec(
-            num_scalar_prefetch=1,
-            grid=(count // tile,),
-            in_specs=[
-                pl.BlockSpec((tile, full_width), lambda i, place: (i, 0)),
-                whole(),
-                whole(),
-                whole(),
-            ],
-            out_specs=pl.BlockSpec((parts, tile, width // parts), lambda i, place: (0, i, 0)),
-        ),
-        out_shape=jax.ShapeDtypeStruct((parts, count, width // parts), jnp.bfloat16),
+        functools.partial(expert_kernel, experts, ahead),
+        in_specs=[pl.BlockSpec(memory_space=pltpu.SMEM)] + [whole] * 5,
+        out_specs=[whole] * parts,
+        out_shape=[out_shape] * parts,
         cost_estimate=pl.CostEstimate(
             flops=6 * count * width * units,
             bytes_accessed=2 * (3 * width * units + 2 * count * width),
             transcendentals=count * units,
         ),
-        compiler_params=pltpu.CompilerParams(vmem_limit_bytes=48 << 20),
-    )(place, rows, w_gate, w_up, w_down)
-
-
-def plane_gather(blocks):
-    half = blocks.shape[1] // 2
-    first, second = blocks[:, :half], blocks[:, half:]
-    first_pair = jnp.stack([first, flipped(first, 1)])
-    second_pair = jnp.stack([second, flipped(second, 2)])
-    first_other = flipped(first_pair, 2)
-    second_other = flipped(second_pair, 1)
-    firsts = [first_pair[0], first_pair[1], first_other[0], first_other[1]]
-    seconds = [second_pair[0], second_other[0], second_pair[1], second_other[1]]
-    return jnp.stack(
-        [jnp.concatenate([a, b], axis=1) for a, b in zip(firsts, seconds, strict=True)]
-    )
+        compiler_params=pltpu.CompilerParams(vmem_limit_bytes=24 << 20),
+    )(place, near, far, w_gate, w_up, w_down)
 
 
 def wide(block):
@@ -181,17 +169,13 @@
     return block.astype(jnp.bfloat16)
 
 
-def plane_scatter(kept, came):
-    half = kept.shape[-1] // 2
-    total = wide(kept) + wide(came)
-    first, second = total[..., :half], total[..., half:]
-    got = flipped(narrow(first[2:4]), 2)
-    first = first[0:2] + wide(got)
-    got = flipped(narrow(jnp.stack([second[1], second[3]])), 1)
-    second = jnp.stack([second[0], second[2]]) + wide(got)
-    got_first = flipped(narrow(first[1]), 1)
-    got_second = flipped(narrow(second[1]), 2)
-    return jnp.concatenate([first[0] + wide(got_first), second[0] + wide(got_second)], axis=-1)
+def plane_scatter(totals):
+    sent = narrow(jnp.stack([total[2:4] for total in totals]))
+    got = crossed(sent, False)
+    totals = [total[0:2] + wide(got[i]) for i, total in enumerate(totals)]
+    sent = narrow(jnp.stack([total[1] for total in totals]))
+    got = crossed(sent, True)
+    return [total[0] + wide(got[i]) for i, total in enumerate(totals)]
 
 
 def on_device(
@@ -247,41 +231,52 @@
     lanes = gate_lanes(expert_ids, gate_weights, experts)
     payload = lax.dynamic_slice_in_dim(
         jnp.concatenate([normed, lanes], axis=1), tok_index * part_rows, part_rows, 0
-    )[None]
+    )
     place = jnp.stack([blk_index, tok_index]).astype(jnp.int32)
-    groups = [[0]] + [sorted({ahead, planes - ahead}) for ahead in range(1, planes // 2 + 1)]
+    gate_turned, up_turned = w_gate[0].T, w_up[0].T
     came = {0: payload}
     for ahead in range(1, planes):
         came[ahead] = from_plane(payload, ahead)
-    gate_turned, up_turned = w_gate[0].T, w_up[0].T
+    if planes <= 4:
+        groups = [[0]] + [sorted({i, planes - i}) for i in range(1, planes // 2 + 1)]
+    else:
+        groups = [[0]] + [list(range(i, min(i + 8, planes))) for i in range(1, planes, 8)]
     results = {}
     for group in groups:
         column = jnp.concatenate([came[ahead] for ahead in group])
         if planes > 4 and results:
             column, results = lax.optimization_barrier((column, results))
-        held = plane_gather(column)
-        count = len(group)
-        own_rows = held.reshape(PLANE * count * part_rows, held.shape[-1])
+        near = jnp.concatenate([column, crossed(column, True)])
+        far = crossed(near, False)
         outs = []
         for ahead in range(cores):
-            rows = own_rows if ahead == 0 else from_core(own_rows, ahead)
+            near_rows = from_core(near, ahead) if ahead else near
+            far_rows = from_core(far, ahead) if ahead else far
             outs.append(
                 run_expert(
-                    place, rows, gate_turned, up_turned, w_down[0], experts, cores, PLANE * part_rows
+                    place,
+                    near_rows,
+                    far_rows,
+                    gate_turned,
+                    up_turned,
+                    w_down[0],
+                    experts,
+                    cores,
+                    ahead,
                 )
             )
-        full = (PLANE, count, part_rows, col_width)
-        kept = jnp.stack([outs[j][0].reshape(full) for j in range(cores)], axis=2)
-        arrived = 0.0
-        for ahead in range(1, cores):
-            sent = jnp.stack([outs[(ahead + j) % cores][ahead] for j in range(cores)])
-            got = from_core(sent, cores - ahead)
-            arrived = arrived + wide(got)
-        arrived = jnp.stack([arrived[j].reshape(full) for j in range(cores)], axis=2)
-        merged = (PLANE, count, cores * part_rows, col_width)
-        summed = plane_scatter(kept.reshape(merged), arrived.reshape(merged))
-        for place_in, ahead in enumerate(group):
-            results[ahead] = summed[place_in]
+        totals = []
+        for rows_of in range(cores):
+            total = wide(outs[rows_of][0])
+            for ahead in range(1, cores):
+                sent = outs[(rows_of + ahead) % cores][ahead]
+                total = total + wide(from_core(sent, cores - ahead))
+            totals.append(total)
+        summed = plane_scatter(totals)
+        for i, ahead in enumerate(group):
+            results[ahead] = jnp.concatenate(
+                [total[i * part_rows : (i + 1) * part_rows] for total in summed]
+            )
     moe = results[0]
     for ahead in range(1, planes):
         moe = moe + wide(to_plane(narrow(results[ahead]), ahead))

time: 248 us -> 227 us (0.915)
  Pallas kernels: 43.2 us -> 28.2 us
  starting transfers between devices: 60.5 us -> 49.9 us
  local copies, waits for them, and re-layouts: 26.3 us -> 31.1 us
  waiting for transfers between devices: 95.6 us -> 92.9 us
    ppermute x24 -> x12, starting transfers between devices: 27.8 us -> 10.4 us  [crossed(): return lax.ppermute(block, ('tok', 'blk'), route)]
    pallas_call x6, Pallas kernels: 43.2 us -> 28.2 us  [run_expert(): pl.pallas_call(functools.partial(expert_kernel, experts, ahead), in_specs...]
    ppermute x24 -> x12, waiting for transfers between devices: 40.9 us -> 31.3 us  [crossed(): return lax.ppermute(block, ('tok', 'blk'), route)]
    unnamed x42 -> x66, local copies, waits for them, and re-layouts: 15.4 us -> 21.5 us
    ppermute x3, waiting for transfers between devices: 13.1 us -> 18.9 us  [from_plane(): lax.ppermute(block, 'blk', [((i + PLANE * ahead) % count, i) for i in ran...]
    slice x18 -> x8, local copies, waits for them, and re-layouts: 4.16 us -> 0.16 us  [the longest x6 0.13 us: plane_scatter(): sent = narrow(jnp.stack([total[1] for total in totals]))]
    concatenate x0 -> x6, other arithmetic: none -> 3.98 us  [the longest x3 2.18 us: on_device(): jnp.concatenate([total[i * part_rows:(i + 1) * part_rows] for total in su...]
    ppermute x3, waiting for transfers between devices: 14.6 us -> 11.3 us  [to_plane(): lax.ppermute(block, 'blk', [(i, (i + PLANE * ahead) % count) for i in ran...]
  transfers between devices with their start and end apart: 41 -> 35, of which waited for: 21 -> 15; matrix products, arithmetic and copies ran while one was open for 11% -> 12% of each run, Pallas kernels for 17% -> 13%
where the time goes in v2:
time: 227 us; the launch traced here: 225 us
  waiting for transfers between devices  92.9 us (41%)
  starting transfers between devices  49.9 us (22%)
  local copies, waits for them, and re-layouts  31.1 us (14%)
  Pallas kernels  28.2 us (12%)
  other arithmetic  14.1 us (6%)
  matrix products  7.59 us (3%)
    ppermute x12, waiting for transfers between devices, crossed(): return lax.ppermute(block, ('tok', 'blk'), route)  31.3 us
    pallas_call x6, Pallas kernels, run_expert(): pl.pallas_call(functools.partial(expert_kernel, experts, ahead), in_specs...  28.2 us
    ppermute x4, waiting for transfers between devices, shifted(): return lax.ppermute(block, axis, route)  27.7 us
    ppermute x4, starting transfers between devices, shifted(): return lax.ppermute(block, axis, route)  22 us
    unnamed x66, local copies, waits for them, and re-layouts  21.5 us
    ppermute x3, waiting for transfers between devices, from_plane(): lax.ppermute(block, 'blk', [((i + PLANE * ahead) % count, i) for i in ran...  18.9 us
    ppermute x3, waiting for transfers between devices, to_plane(): lax.ppermute(block, 'blk', [(i, (i + PLANE * ahead) % count) for i in ran...  11.3 us
    ppermute x12, starting transfers between devices, crossed(): return lax.ppermute(block, ('tok', 'blk'), route)  10.4 us
  transfers between devices with their start and end apart: 35, of which 15 were waited for; matrix products, arithmetic and copies ran while one was open for 12% of the time, Pallas kernels for 13%

profile of v2, /device:TPU:0, one launch (start us, length us, event | category | flops | bytes accessed | tf_op | source)
XLA Modules:
  0.0 225.2 jit_solution(900478027813778497)
XLA Ops:
  5.3 5.7 %collective-permute-start = (bf16[2,128,1024]{1,2,0:T(8,128)(2,1)}, bf16[2,128,1024]{1,2,0:T(8,128)(2,1)}, u32[]{:S(2)}, u32[]{:S(2)}) collective-permute-start(bf16[2,128,1024]{1,2,0:T(8,128)(2,1)} %get-tuple-element.52), channel_id=1, source_target_pairs={{0,1},{1,2},{2,3},{3,4},{4,5},{5,6},{6,7},{7,8},{8,9},{9,10},{10,1... | collective-permute-start | bytes 1572872 | tf_op jit(solution)/shard_map/ppermute | solution.py:20
  11.2 10.5 %collective-permute-done = bf16[2,128,1024]{1,2,0:T(8,128)(2,1)} collective-permute-done((bf16[2,128,1024]{1,2,0:T(8,128)(2,1)}, bf16[2,128,1024]{1,2,0:T(8,128)(2,1)}, u32[]{:S(2)}, u32[]{:S(2)}) %collective-permute-start) | collective-permute-done | bytes 524320 | tf_op jit(solution)/shard_map/ppermute | solution.py:20
  21.6 5.2 %collective-permute-start.1 = (bf16[2,128,1024]{1,2,0:T(8,128)(2,1)}, bf16[2,128,1024]{1,2,0:T(8,128)(2,1)}, u32[]{:S(2)}, u32[]{:S(2)}) collective-permute-start(bf16[2,128,1024]{1,2,0:T(8,128)(2,1)} %collective-permute-done), channel_id=1, source_target_pairs={{0,1},{1,2},{2,3},{3,4},{4,5},{5,6},{6,7},{7,8},{8,9},{9,10},{10,1... | collective-permute-start | bytes 1572872 | tf_op jit(solution)/shard_map/ppermute | solution.py:20
  27.6 9.0 %collective-permute-done.1 = bf16[2,128,1024]{1,2,0:T(8,128)(2,1)} collective-permute-done((bf16[2,128,1024]{1,2,0:T(8,128)(2,1)}, bf16[2,128,1024]{1,2,0:T(8,128)(2,1)}, u32[]{:S(2)}, u32[]{:S(2)}) %collective-permute-start.1) | collective-permute-done | bytes 524320 | tf_op jit(solution)/shard_map/ppermute | solution.py:20
  36.6 5.2 %collective-permute-start.2 = (bf16[2,128,1024]{1,2,0:T(8,128)(2,1)}, bf16[2,128,1024]{1,2,0:T(8,128)(2,1)}, u32[]{:S(2)}, u32[]{:S(2)}) collective-permute-start(bf16[2,128,1024]{1,2,0:T(8,128)(2,1)} %collective-permute-done.1), channel_id=1, source_target_pairs={{0,1},{1,2},{2,3},{3,4},{4,5},{5,6},{6,7},{7,8},{8,9},{9,10},{10,1... | collective-permute-start | bytes 1572872 | tf_op jit(solution)/shard_map/ppermute | solution.py:20
  44.7 2.0 subtract_convert_fusion
  46.7 4.0 %collective-permute-done.2 = bf16[2,128,1024]{1,2,0:T(8,128)(2,1)} collective-permute-done((bf16[2,128,1024]{1,2,0:T(8,128)(2,1)}, bf16[2,128,1024]{1,2,0:T(8,128)(2,1)}, u32[]{:S(2)}, u32[]{:S(2)}) %collective-permute-start.2) | collective-permute-done | bytes 524320 | tf_op jit(solution)/shard_map/ppermute | solution.py:20
  50.7 6.0 %collective-permute-start.3 = (bf16[2,128,1024]{1,2,0:T(8,128)(2,1)}, bf16[2,128,1024]{1,2,0:T(8,128)(2,1)}, u32[]{:S(2)}, u32[]{:S(2)}) collective-permute-start(bf16[2,128,1024]{1,2,0:T(8,128)(2,1)} %collective-permute-done.2), channel_id=1, source_target_pairs={{0,1},{1,2},{2,3},{3,4},{4,5},{5,6},{6,7},{7,8},{8,9},{9,10},{10,1... | collective-permute-start | bytes 1572872 | tf_op jit(solution)/shard_map/ppermute | solution.py:20
  60.5 4.2 %collective-permute-done.3 = bf16[2,128,1024]{1,2,0:T(8,128)(2,1)} collective-permute-done((bf16[2,128,1024]{1,2,0:T(8,128)(2,1)}, bf16[2,128,1024]{1,2,0:T(8,128)(2,1)}, u32[]{:S(2)}, u32[]{:S(2)}) %collective-permute-start.3) | collective-permute-done | bytes 524320 | tf_op jit(solution)/shard_map/ppermute | solution.py:20
  67.6 4.3 %fusion.52 = (f32[8,128]{1,0:T(8,128)S(1)}, f32[8,128,640]{2,1,0:T(8,128)}) fusion(pred[128,640]{1,0:T(8,128)(4,1)S(1)} %and_and_fusion, bf16[640,8,128]{0,2,1:T(8,128)(2,1)} %bitcast.112, bf16[128,8,64]{2,0,1:T(8,128)(2,1)} %get-tuple-element.41, bf16[128,8,64]{2,0,1:T(8,128)(2,1)S(1)} %copy-done.19), kind=kOutput, calls=%fused_computation.154 | convolution fusion | flops 171573888 | bytes 4280320 | tf_op jit(solution)/shard_map/sub | solution.py:92
  71.8 2.6 %fusion.6 = bf16[8,128,128]{2,1,0:T(8,128)(2,1)S(1)} fusion(bf16[640,8,128]{0,2,1:T(8,128)(2,1)S(1)} %bitcast.111, f32[8,128,640]{2,1,0:T(8,128)} %get-tuple-element.72, f32[8,128]{1,0:T(8,128)S(1)} %get-tuple-element.71), kind=kOutput, calls=%fused_computation.15 | convolution fusion | flops 169213952 | bytes 4198400 | tf_op jit(solution)/shard_map/hqk,khd->qhd/dot_general | solution.py:94
  75.8 2.5 %collective-permute-done.4 = f32[128,2048]{1,0:T(8,128)S(1)} collective-permute-done((f32[128,2048]{1,0:T(8,128)S(1)}, f32[128,2048]{1,0:T(8,128)S(1)}, u32[]{:S(2)}, u32[]{:S(2)}) %collective-permute-start.4) | collective-permute-done | bytes 1048608 | tf_op jit(solution)/shard_map/ppermute | solution.py:39
  80.3 3.4 %collective-permute-start.5 = (bf16[64,2176]{1,0:T(8,128)(2,1)}, bf16[64,2176]{1,0:T(8,128)(2,1)S(1)}, u32[]{:S(2)}, u32[]{:S(2)}) collective-permute-start(bf16[64,2176]{1,0:T(8,128)(2,1)} %fusion.19), channel_id=1, source_target_pairs={{0,1},{1,0},{2,3},{3,2},{4,5},{5,4},{6,7},{7,6},{8,9},{9,8},{10,11... | collective-permute-start | bytes 835592 | tf_op jit(solution)/shard_map/ppermute | solution.py:118
  83.7 7.6 %collective-permute-start.13 = (bf16[64,2176]{1,0:T(8,128)(2,1)}, bf16[64,2176]{1,0:T(8,128)(2,1)S(1)}, u32[]{:S(2)}, u32[]{:S(2)}) collective-permute-start(bf16[64,2176]{1,0:T(8,128)(2,1)} %fusion.19), channel_id=1, source_target_pairs={{4,0},{5,1},{6,2},{7,3},{8,4},{9,5},{10,6},{11,7},{12,8},{13,9},{1... | collective-permute-start | bytes 835592 | tf_op jit(solution)/shard_map/ppermute | solution.py:25
  93.7 5.0 %collective-permute-done.13 = bf16[64,2176]{1,0:T(8,128)(2,1)S(1)} collective-permute-done((bf16[64,2176]{1,0:T(8,128)(2,1)}, bf16[64,2176]{1,0:T(8,128)(2,1)S(1)}, u32[]{:S(2)}, u32[]{:S(2)}) %collective-permute-start.13) | collective-permute-done | bytes 278560 | tf_op jit(solution)/shard_map/ppermute | solution.py:25
  98.7 6.8 %collective-permute-done.14 = bf16[64,2176]{1,0:T(8,128)(2,1)S(1)} collective-permute-done((bf16[64,2176]{1,0:T(8,128)(2,1)}, bf16[64,2176]{1,0:T(8,128)(2,1)S(1)}, u32[]{:S(2)}, u32[]{:S(2)}) %collective-permute-start.14) | collective-permute-done | bytes 278560 | tf_op jit(solution)/shard_map/ppermute | solution.py:25
  105.6 2.2 collective-permute-start.15
  108.5 7.0 %collective-permute-done.24 = bf16[64,2176]{1,0:T(8,128)(2,1)S(1)} collective-permute-done((bf16[64,2176]{1,0:T(8,128)(2,1)}, bf16[64,2176]{1,0:T(8,128)(2,1)S(1)}, u32[]{:S(2)}, u32[]{:S(2)}) %collective-permute-start.24) | collective-permute-done | bytes 278560 | tf_op jit(solution)/shard_map/ppermute | solution.py:25
  117.0 5.8 %collective-permute-done.25 = bf16[64,2176]{1,0:T(8,128)(2,1)S(1)} collective-permute-done((bf16[64,2176]{1,0:T(8,128)(2,1)S(1)}, bf16[64,2176]{1,0:T(8,128)(2,1)S(1)}, u32[]{:S(2)}, u32[]{:S(2)}) %collective-permute-start.25) | collective-permute-done | bytes 278560 | tf_op jit(solution)/shard_map/ppermute | solution.py:118
  128.3 1.8 copy-done.4
  130.1 4.5 %shard_map.140 = (bf16[4,64,1024]{2,1,0:T(8,128)(2,1)S(1)}, bf16[4,64,1024]{2,1,0:T(8,128)(2,1)}) custom-call(s32[2]{0:T(128)S(1)} %pad_add_fusion.place_ref, bf16[128,2176]{1,0:T(8,128)(2,1)S(1)} %pad_maximum_fusion.1.near_ref, bf16[128,2176]{1,0:T(8,128)(2,1)} %collective-permute-done.6.far_ref, bf16[704,2048]{1,0:T(8,128)(2,1)S(1)} %bitcast.90, ...), custom_call_target="tpu_custom_call" | custom-call | flops 2214592512 | bytes 10747904 | tf_op jit(solution)/shard_map/pallas_call | solution.py:150
  142.2 4.0 %shard_map.144 = (bf16[4,64,1024]{2,1,0:T(8,128)(2,1)S(1)}, bf16[4,64,1024]{2,1,0:T(8,128)(2,1)S(1)}) custom-call(s32[2]{0:T(128)S(1)} %pad_add_fusion.place_ref, bf16[128,2176]{1,0:T(8,128)(2,1)} %constant_dynamic-update-slice_fusion.9.near_ref, bf16[128,2176]{1,0:T(8,128)(2,1)} %collective-permute-done.26.far_ref, bf16[704,2048]{1,0:T(8,128)(2,1)S(1)} %bitcast.91, ...), custom_call_target="tpu_custom_call" | custom-call | flops 2214592512 | bytes 10747904 | tf_op jit(solution)/shard_map/pallas_call | solution.py:150
  146.9 3.9 %shard_map.141 = (bf16[4,64,1024]{2,1,0:T(8,128)(2,1)S(1)}, bf16[4,64,1024]{2,1,0:T(8,128)(2,1)S(1)}) custom-call(s32[2]{0:T(128)S(1)} %pad_add_fusion.place_ref, bf16[128,2176]{1,0:T(8,128)(2,1)} %collective-permute-done.7.near_ref, bf16[128,2176]{1,0:T(8,128)(2,1)} %collective-permute-done.8.far_ref, bf16[704,2048]{1,0:T(8,128)(2,1)S(1)} %bitcast.92, ...), custom_call_target="tpu_custom_call" | custom-call | flops 2214592512 | bytes 10747904 | tf_op jit(solution)/shard_map/pallas_call | solution.py:150
  153.2 3.2 %shard_map.145 = (bf16[4,64,1024]{2,1,0:T(8,128)(2,1)S(1)}, bf16[4,64,1024]{2,1,0:T(8,128)(2,1)S(1)}) custom-call(s32[2]{0:T(128)S(1)} %pad_add_fusion.place_ref, bf16[128,2176]{1,0:T(8,128)(2,1)S(1)} %collective-permute-done.27.near_ref, bf16[128,2176]{1,0:T(8,128)(2,1)S(1)} %collective-permute-done.28.far_ref, bf16[704,2048]{1,0:T(8,128)(2,1)S(1)} %bitcast.93, ...), custom_call_target="tpu_custom_call" | custom-call | flops 2214592512 | bytes 10747904 | tf_op jit(solution)/shard_map/pallas_call | solution.py:150
  156.8 6.9 %shard_map.142 = (bf16[4,128,1024]{2,1,0:T(8,128)(2,1)S(1)}, bf16[4,128,1024]{2,1,0:T(8,128)(2,1)S(1)}) custom-call(s32[2]{0:T(128)S(1)} %pad_add_fusion.place_ref, bf16[256,2176]{1,0:T(8,128)(2,1)} %constant_dynamic-update-slice_fusion.6.near_ref, bf16[256,2176]{1,0:T(8,128)(2,1)} %collective-permute-done.16.far_ref, bf16[704,2048]{1,0:T(8,128)(2,1)S(1)} %bitcast.94, ...), custom_call_target="tpu_custom_call" | custom-call | flops 4429185024 | bytes 12845056 | tf_op jit(solution)/shard_map/pallas_call | solution.py:150
  164.2 5.6 %shard_map.143 = (bf16[4,128,1024]{2,1,0:T(8,128)(2,1)S(1)}, bf16[4,128,1024]{2,1,0:T(8,128)(2,1)S(1)}) custom-call(s32[2]{0:T(128)S(1)} %pad_add_fusion.place_ref, bf16[256,2176]{1,0:T(8,128)(2,1)S(1)} %collective-permute-done.17.near_ref, bf16[256,2176]{1,0:T(8,128)(2,1)S(1)} %collective-permute-done.18.far_ref, bf16[704,2048]{1,0:T(8,128)(2,1)S(1)} %bitcast.95, ...), custom_call_target="tpu_custom_call" | custom-call | flops 4429185024 | bytes 12845056 | tf_op jit(solution)/shard_map/pallas_call | solution.py:150
  175.6 3.9 %collective-permute-done.31 = bf16[2,2,64,1024]{3,2,1,0:T(8,128)(2,1)S(1)} collective-permute-done((bf16[2,2,64,1024]{3,2,1,0:T(8,128)(2,1)S(1)}, bf16[2,2,64,1024]{3,2,1,0:T(8,128)(2,1)S(1)}, u32[]{:S(2)}, u32[]{:S(2)}) %collective-permute-start.31) | collective-permute-done | bytes 524320 | tf_op jit(solution)/shard_map/ppermute | solution.py:118
  179.8 13.7 %collective-permute-done.21 = bf16[2,2,128,1024]{3,2,1,0:T(8,128)(2,1)S(1)} collective-permute-done((bf16[2,2,128,1024]{3,2,1,0:T(8,128)(2,1)S(1)}, bf16[2,2,128,1024]{3,2,1,0:T(8,128)(2,1)S(1)}, u32[]{:S(2)}, u32[]{:S(2)}) %collective-permute-start.21) | collective-permute-done | bytes 1048608 | tf_op jit(solution)/shard_map/ppermute | solution.py:118
  194.1 7.8 %collective-permute-done.11 = bf16[2,2,64,1024]{3,2,1,0:T(8,128)(2,1)S(1)} collective-permute-done((bf16[2,2,64,1024]{3,2,1,0:T(8,128)(2,1)S(1)}, bf16[2,2,64,1024]{3,2,1,0:T(8,128)(2,1)S(1)}, u32[]{:S(2)}, u32[]{:S(2)}) %collective-permute-start.11) | collective-permute-done | bytes 524320 | tf_op jit(solution)/shard_map/ppermute | solution.py:118
  203.0 1.9 collective-permute-start.33
  208.0 2.5 %collective-permute-start.34 = (bf16[128,1024]{1,0:T(8,128)(2,1)}, bf16[128,1024]{1,0:T(8,128)(2,1)S(1)}, u32[]{:S(2)}, u32[]{:S(2)}) collective-permute-start(bf16[128,1024]{1,0:T(8,128)(2,1)} %pad_maximum_fusion.12), channel_id=1, source_target_pairs={{0,12},{1,13},{2,14},{3,15},{4,0},{5,1},{6,2},{7,3},{8,4},{9,5},{1... | collective-permute-start | bytes 786440 | tf_op jit(solution)/shard_map/ppermute | solution.py:32
  212.8 9.7 %collective-permute-done.33 = bf16[128,1024]{1,0:T(8,128)(2,1)S(1)} collective-permute-done((bf16[128,1024]{1,0:T(8,128)(2,1)}, bf16[128,1024]{1,0:T(8,128)(2,1)S(1)}, u32[]{:S(2)}, u32[]{:S(2)}) %collective-permute-start.33) | collective-permute-done | bytes 262176 | tf_op jit(solution)/shard_map/ppermute | solution.py:32
  (196 shorter events, 55.5 us)
Async XLA Ops:
  5.3 16.3 %collective-permute-start = (bf16[2,128,1024]{1,2,0:T(8,128)(2,1)}, bf16[2,128,1024]{1,2,0:T(8,128)(2,1)}, u32[]{:S(2)}, u32[]{:S(2)}) collective-permute-start(bf16[2,128,1024]{1,2,0:T(8,128)(2,1)} %get-tuple-element.52), channel_id=1, source_target_pairs={{0,1},{1,2},{2,3},{3,4},{4,5},{5,6},{6,7},{7,8},{8,9},{9,10},{10,1... | collective-permute-start | bytes 1572872 | tf_op jit(solution)/shard_map/ppermute | solution.py:20
  21.6 15.0 %collective-permute-start.1 = (bf16[2,128,1024]{1,2,0:T(8,128)(2,1)}, bf16[2,128,1024]{1,2,0:T(8,128)(2,1)}, u32[]{:S(2)}, u32[]{:S(2)}) collective-permute-start(bf16[2,128,1024]{1,2,0:T(8,128)(2,1)} %collective-permute-done), channel_id=1, source_target_pairs={{0,1},{1,2},{2,3},{3,4},{4,5},{5,6},{6,7},{7,8},{8,9},{9,10},{10,1... | collective-permute-start | bytes 1572872 | tf_op jit(solution)/shard_map/ppermute | solution.py:20
  36.6 14.1 %collective-permute-start.2 = (bf16[2,128,1024]{1,2,0:T(8,128)(2,1)}, bf16[2,128,1024]{1,2,0:T(8,128)(2,1)}, u32[]{:S(2)}, u32[]{:S(2)}) collective-permute-start(bf16[2,128,1024]{1,2,0:T(8,128)(2,1)} %collective-permute-done.1), channel_id=1, source_target_pairs={{0,1},{1,2},{2,3},{3,4},{4,5},{5,6},{6,7},{7,8},{8,9},{9,10},{10,1... | collective-permute-start | bytes 1572872 | tf_op jit(solution)/shard_map/ppermute | solution.py:20
  50.7 14.0 %collective-permute-start.3 = (bf16[2,128,1024]{1,2,0:T(8,128)(2,1)}, bf16[2,128,1024]{1,2,0:T(8,128)(2,1)}, u32[]{:S(2)}, u32[]{:S(2)}) collective-permute-start(bf16[2,128,1024]{1,2,0:T(8,128)(2,1)} %collective-permute-done.2), channel_id=1, source_target_pairs={{0,1},{1,2},{2,3},{3,4},{4,5},{5,6},{6,7},{7,8},{8,9},{9,10},{10,1... | collective-permute-start | bytes 1572872 | tf_op jit(solution)/shard_map/ppermute | solution.py:20
  80.3 12.1 %collective-permute-start.5 = (bf16[64,2176]{1,0:T(8,128)(2,1)}, bf16[64,2176]{1,0:T(8,128)(2,1)S(1)}, u32[]{:S(2)}, u32[]{:S(2)}) collective-permute-start(bf16[64,2176]{1,0:T(8,128)(2,1)} %fusion.19), channel_id=1, source_target_pairs={{0,1},{1,0},{2,3},{3,2},{4,5},{5,4},{6,7},{7,6},{8,9},{9,8},{10,11... | collective-permute-start | bytes 835592 | tf_op jit(solution)/shard_map/ppermute | solution.py:118
  83.7 15.0 %collective-permute-start.13 = (bf16[64,2176]{1,0:T(8,128)(2,1)}, bf16[64,2176]{1,0:T(8,128)(2,1)S(1)}, u32[]{:S(2)}, u32[]{:S(2)}) collective-permute-start(bf16[64,2176]{1,0:T(8,128)(2,1)} %fusion.19), channel_id=1, source_target_pairs={{4,0},{5,1},{6,2},{7,3},{8,4},{9,5},{10,6},{11,7},{12,8},{13,9},{1... | collective-permute-start | bytes 835592 | tf_op jit(solution)/shard_map/ppermute | solution.py:25
  91.3 14.2 %collective-permute-start.14 = (bf16[64,2176]{1,0:T(8,128)(2,1)}, bf16[64,2176]{1,0:T(8,128)(2,1)S(1)}, u32[]{:S(2)}, u32[]{:S(2)}) collective-permute-start(bf16[64,2176]{1,0:T(8,128)(2,1)} %fusion.19), channel_id=1, source_target_pairs={{12,0},{13,1},{14,2},{15,3},{0,4},{1,5},{2,6},{3,7},{4,8},{5,9},{6... | collective-permute-start | bytes 835592 | tf_op jit(solution)/shard_map/ppermute | solution.py:25
  91.3 24.2 %collective-permute-start.24 = (bf16[64,2176]{1,0:T(8,128)(2,1)}, bf16[64,2176]{1,0:T(8,128)(2,1)S(1)}, u32[]{:S(2)}, u32[]{:S(2)}) collective-permute-start(bf16[64,2176]{1,0:T(8,128)(2,1)} %fusion.19), channel_id=1, source_target_pairs={{8,0},{9,1},{10,2},{11,3},{12,4},{13,5},{14,6},{15,7},{0,8},{1,9},... | collective-permute-start | bytes 835592 | tf_op jit(solution)/shard_map/ppermute | solution.py:25
  93.4 33.1 %collective-permute-start.6 = (bf16[128,2176]{1,0:T(8,128)(2,1)S(1)}, bf16[128,2176]{1,0:T(8,128)(2,1)}, u32[]{:S(2)}, u32[]{:S(2)}) collective-permute-start(bf16[128,2176]{1,0:T(8,128)(2,1)S(1)} %pad_maximum_fusion.1.near_ref), channel_id=1, source_target_pairs={{0,2},{1,3},{2,0},{3,1},{4,6},{5,7},{6,4},{7,5},{8,10},{9,11},{10,... | collective-permute-start | bytes 1671176 | tf_op jit(solution)/shard_map/ppermute | solution.py:118
  93.7 52.6 %collective-permute-start.7 = (bf16[128,2176]{1,0:T(8,128)(2,1)S(1)}, bf16[128,2176]{1,0:T(8,128)(2,1)}, u32[]{:S(2)}, u32[]{:S(2)}) collective-permute-start(bf16[128,2176]{1,0:T(8,128)(2,1)S(1)} %pad_maximum_fusion.1.near_ref), channel_id=1, source_target_pairs={{16,0},{0,16},{17,1},{1,17},{18,2},{2,18},{19,3},{3,19},{20,4},{4,... | collective-permute-start | bytes 1671176 | tf_op jit(solution)/shard_map/ppermute | solution.py:39
  105.6 18.4 %collective-permute-start.15 = (bf16[128,2176]{1,0:T(8,128)(2,1)S(1)}, bf16[128,2176]{1,0:T(8,128)(2,1)S(1)}, u32[]{:S(2)}, u32[]{:S(2)}) collective-permute-start(bf16[128,2176]{1,0:T(8,128)(2,1)S(1)} %pad_maximum_fusion.2), channel_id=1, source_target_pairs={{0,1},{1,0},{2,3},{3,2},{4,5},{5,4},{6,7},{7,6},{8,9},{9,8},{10,11... | collective-permute-start | bytes 1671176 | tf_op jit(solution)/shard_map/ppermute | solution.py:118
  116.3 6.5 %collective-permute-start.25 = (bf16[64,2176]{1,0:T(8,128)(2,1)S(1)}, bf16[64,2176]{1,0:T(8,128)(2,1)S(1)}, u32[]{:S(2)}, u32[]{:S(2)}) collective-permute-start(bf16[64,2176]{1,0:T(8,128)(2,1)S(1)} %collective-permute-done.24), channel_id=1, source_target_pairs={{0,1},{1,0},{2,3},{3,2},{4,5},{5,4},{6,7},{7,6},{8,9},{9,8},{10,11... | collective-permute-start | bytes 835592 | tf_op jit(solution)/shard_map/ppermute | solution.py:118
  123.6 15.0 %collective-permute-start.26 = (bf16[128,2176]{1,0:T(8,128)(2,1)}, bf16[128,2176]{1,0:T(8,128)(2,1)}, u32[]{:S(2)}, u32[]{:S(2)}) collective-permute-start(bf16[128,2176]{1,0:T(8,128)(2,1)} %constant_dynamic-update-slice_fusion.9.near_ref), channel_id=1, source_target_pairs={{0,2},{1,3},{2,0},{3,1},{4,6},{5,7},{6,4},{7,5},{8,10},{9,11},{10,... | collective-permute-start | bytes 1671176 | tf_op jit(solution)/shard_map/ppermute | solution.py:118
  124.8 27.9 %collective-permute-start.16 = (bf16[256,2176]{1,0:T(8,128)(2,1)}, bf16[256,2176]{1,0:T(8,128)(2,1)}, u32[]{:S(2)}, u32[]{:S(2)}) collective-permute-start(bf16[256,2176]{1,0:T(8,128)(2,1)} %constant_dynamic-update-slice_fusion.6.near_ref), channel_id=1, source_target_pairs={{0,2},{1,3},{2,0},{3,1},{4,6},{5,7},{6,4},{7,5},{8,10},{9,11},{10,... | collective-permute-start | bytes 3342344 | tf_op jit(solution)/shard_map/ppermute | solution.py:118
  126.5 20.4 %collective-permute-start.8 = (bf16[128,2176]{1,0:T(8,128)(2,1)}, bf16[128,2176]{1,0:T(8,128)(2,1)}, u32[]{:S(2)}, u32[]{:S(2)}) collective-permute-start(bf16[128,2176]{1,0:T(8,128)(2,1)} %collective-permute-done.6.far_ref), channel_id=1, source_target_pairs={{16,0},{0,16},{17,1},{1,17},{18,2},{2,18},{19,3},{3,19},{20,4},{4,... | collective-permute-start | bytes 1671176 | tf_op jit(solution)/shard_map/ppermute | solution.py:39
  135.5 15.4 %collective-permute-start.10 = (bf16[4,64,1024]{2,1,0:T(8,128)(2,1)}, bf16[4,64,1024]{2,1,0:T(8,128)(2,1)}, u32[]{:S(2)}, u32[]{:S(2)}) collective-permute-start(bf16[4,64,1024]{2,1,0:T(8,128)(2,1)} %get-tuple-element.17), channel_id=1, source_target_pairs={{16,0},{0,16},{17,1},{1,17},{18,2},{2,18},{19,3},{3,19},{20,4},{4,... | collective-permute-start | bytes 1572872 | tf_op jit(solution)/shard_map/ppermute | solution.py:39
  138.6 14.0 %collective-permute-start.27 = (bf16[128,2176]{1,0:T(8,128)(2,1)}, bf16[128,2176]{1,0:T(8,128)(2,1)S(1)}, u32[]{:S(2)}, u32[]{:S(2)}) collective-permute-start(bf16[128,2176]{1,0:T(8,128)(2,1)} %constant_dynamic-update-slice_fusion.9.near_ref), channel_id=1, source_target_pairs={{16,0},{0,16},{17,1},{1,17},{18,2},{2,18},{19,3},{3,19},{20,4},{4,... | collective-permute-start | bytes 1671176 | tf_op jit(solution)/shard_map/ppermute | solution.py:39
  146.3 17.9 %collective-permute-start.17 = (bf16[256,2176]{1,0:T(8,128)(2,1)}, bf16[256,2176]{1,0:T(8,128)(2,1)S(1)}, u32[]{:S(2)}, u32[]{:S(2)}) collective-permute-start(bf16[256,2176]{1,0:T(8,128)(2,1)} %constant_dynamic-update-slice_fusion.6.near_ref), channel_id=1, source_target_pairs={{16,0},{0,16},{17,1},{1,17},{18,2},{2,18},{19,3},{3,19},{20,4},{4,... | collective-permute-start | bytes 3342344 | tf_op jit(solution)/shard_map/ppermute | solution.py:39
  146.9 6.3 %collective-permute-start.28 = (bf16[128,2176]{1,0:T(8,128)(2,1)}, bf16[128,2176]{1,0:T(8,128)(2,1)S(1)}, u32[]{:S(2)}, u32[]{:S(2)}) collective-permute-start(bf16[128,2176]{1,0:T(8,128)(2,1)} %collective-permute-done.26.far_ref), channel_id=1, source_target_pairs={{16,0},{0,16},{17,1},{1,17},{18,2},{2,18},{19,3},{3,19},{20,4},{4,... | collective-permute-start | bytes 1671176 | tf_op jit(solution)/shard_map/ppermute | solution.py:39
  152.6 21.0 %collective-permute-start.9 = (bf16[4,64,1024]{2,1,0:T(8,128)(2,1)S(1)}, bf16[4,64,1024]{2,1,0:T(8,128)(2,1)S(1)}, u32[]{:S(2)}, u32[]{:S(2)}) collective-permute-start(bf16[4,64,1024]{2,1,0:T(8,128)(2,1)S(1)} %get-tuple-element.15), channel_id=1, source_target_pairs={{16,0},{0,16},{17,1},{1,17},{18,2},{2,18},{19,3},{3,19},{20,4},{4,... | collective-permute-start | bytes 1572872 | tf_op jit(solution)/shard_map/ppermute | solution.py:39
  152.8 11.4 %collective-permute-start.18 = (bf16[256,2176]{1,0:T(8,128)(2,1)}, bf16[256,2176]{1,0:T(8,128)(2,1)S(1)}, u32[]{:S(2)}, u32[]{:S(2)}) collective-permute-start(bf16[256,2176]{1,0:T(8,128)(2,1)} %collective-permute-done.16.far_ref), channel_id=1, source_target_pairs={{16,0},{0,16},{17,1},{1,17},{18,2},{2,18},{19,3},{3,19},{20,4},{4,... | collective-permute-start | bytes 3342344 | tf_op jit(solution)/shard_map/ppermute | solution.py:39
  156.4 13.6 %collective-permute-start.29 = (bf16[4,64,1024]{2,1,0:T(8,128)(2,1)S(1)}, bf16[4,64,1024]{2,1,0:T(8,128)(2,1)S(1)}, u32[]{:S(2)}, u32[]{:S(2)}) collective-permute-start(bf16[4,64,1024]{2,1,0:T(8,128)(2,1)S(1)} %get-tuple-element.23), channel_id=1, source_target_pairs={{16,0},{0,16},{17,1},{1,17},{18,2},{2,18},{19,3},{3,19},{20,4},{4,... | collective-permute-start | bytes 1572872 | tf_op jit(solution)/shard_map/ppermute | solution.py:39
  163.7 7.1 %collective-permute-start.20 = (bf16[4,128,1024]{2,1,0:T(8,128)(2,1)S(1)}, bf16[4,128,1024]{2,1,0:T(8,128)(2,1)S(1)}, u32[]{:S(2)}, u32[]{:S(2)}) collective-permute-start(bf16[4,128,1024]{2,1,0:T(8,128)(2,1)S(1)} %get-tuple-element.21), channel_id=1, source_target_pairs={{16,0},{0,16},{17,1},{1,17},{18,2},{2,18},{19,3},{3,19},{20,4},{4,... | collective-permute-start | bytes 3145736 | tf_op jit(solution)/shard_map/ppermute | solution.py:39
  170.2 9.2 %collective-permute-start.31 = (bf16[2,2,64,1024]{3,2,1,0:T(8,128)(2,1)S(1)}, bf16[2,2,64,1024]{3,2,1,0:T(8,128)(2,1)S(1)}, u32[]{:S(2)}, u32[]{:S(2)}) collective-permute-start(bf16[2,2,64,1024]{3,2,1,0:T(8,128)(2,1)S(1)} %pad_maximum_fusion.6), channel_id=1, source_target_pairs={{0,2},{1,3},{2,0},{3,1},{4,6},{5,7},{6,4},{7,5},{8,10},{9,11},{10,... | collective-permute-start | bytes 1572872 | tf_op jit(solution)/shard_map/ppermute | solution.py:118
  173.1 20.4 %collective-permute-start.21 = (bf16[2,2,128,1024]{3,2,1,0:T(8,128)(2,1)S(1)}, bf16[2,2,128,1024]{3,2,1,0:T(8,128)(2,1)S(1)}, u32[]{:S(2)}, u32[]{:S(2)}) collective-permute-start(bf16[2,2,128,1024]{3,2,1,0:T(8,128)(2,1)S(1)} %pad_maximum_fusion), channel_id=1, source_target_pairs={{0,2},{1,3},{2,0},{3,1},{4,6},{5,7},{6,4},{7,5},{8,10},{9,11},{10,... | collective-permute-start | bytes 3145736 | tf_op jit(solution)/shard_map/ppermute | solution.py:118
  174.3 27.7 %collective-permute-start.11 = (bf16[2,2,64,1024]{3,2,1,0:T(8,128)(2,1)S(1)}, bf16[2,2,64,1024]{3,2,1,0:T(8,128)(2,1)S(1)}, u32[]{:S(2)}, u32[]{:S(2)}) collective-permute-start(bf16[2,2,64,1024]{3,2,1,0:T(8,128)(2,1)S(1)} %pad_maximum_fusion.4), channel_id=1, source_target_pairs={{0,2},{1,3},{2,0},{3,1},{4,6},{5,7},{6,4},{7,5},{8,10},{9,11},{10,... | collective-permute-start | bytes 1572872 | tf_op jit(solution)/shard_map/ppermute | solution.py:118
  179.7 22.5 %collective-permute-start.32 = (bf16[2,64,1024]{2,1,0:T(8,128)(2,1)S(1)}, bf16[2,64,1024]{2,1,0:T(8,128)(2,1)S(1)}, u32[]{:S(2)}, u32[]{:S(2)}) collective-permute-start(bf16[2,64,1024]{2,1,0:T(8,128)(2,1)S(1)} %pad_maximum_fusion.10), channel_id=1, source_target_pairs={{0,1},{1,0},{2,3},{3,2},{4,5},{5,4},{6,7},{7,6},{8,9},{9,8},{10,11... | collective-permute-start | bytes 786440 | tf_op jit(solution)/shard_map/ppermute | solution.py:118
  194.0 10.9 %collective-permute-start.22 = (bf16[2,128,1024]{2,1,0:T(8,128)(2,1)S(1)}, bf16[2,128,1024]{2,1,0:T(8,128)(2,1)S(1)}, u32[]{:S(2)}, u32[]{:S(2)}) collective-permute-start(bf16[2,128,1024]{2,1,0:T(8,128)(2,1)S(1)} %pad_maximum_fusion.5), channel_id=1, source_target_pairs={{0,1},{1,0},{2,3},{3,2},{4,5},{5,4},{6,7},{7,6},{8,9},{9,8},{10,11... | collective-permute-start | bytes 1572872 | tf_op jit(solution)/shard_map/ppermute | solution.py:118
  202.1 10.6 %collective-permute-start.12 = (bf16[2,64,1024]{2,1,0:T(8,128)(2,1)S(1)}, bf16[2,64,1024]{2,1,0:T(8,128)(2,1)S(1)}, u32[]{:S(2)}, u32[]{:S(2)}) collective-permute-start(bf16[2,64,1024]{2,1,0:T(8,128)(2,1)S(1)} %pad_maximum_fusion.8), channel_id=1, source_target_pairs={{0,1},{1,0},{2,3},{3,2},{4,5},{5,4},{6,7},{7,6},{8,9},{9,8},{10,11... | collective-permute-start | bytes 786440 | tf_op jit(solution)/shard_map/ppermute | solution.py:118
  203.0 19.5 %collective-permute-start.33 = (bf16[128,1024]{1,0:T(8,128)(2,1)}, bf16[128,1024]{1,0:T(8,128)(2,1)S(1)}, u32[]{:S(2)}, u32[]{:S(2)}) collective-permute-start(bf16[128,1024]{1,0:T(8,128)(2,1)} %pad_maximum_fusion.11), channel_id=1, source_target_pairs={{0,8},{1,9},{2,10},{3,11},{4,12},{5,13},{6,14},{7,15},{8,0},{9,1},... | collective-permute-start | bytes 786440 | tf_op jit(solution)/shard_map/ppermute | solution.py:32
  205.9 16.6 %collective-permute-start.23 = (bf16[128,1024]{1,0:T(8,128)(2,1)}, bf16[128,1024]{1,0:T(8,128)(2,1)S(1)}, u32[]{:S(2)}, u32[]{:S(2)}) collective-permute-start(bf16[128,1024]{1,0:T(8,128)(2,1)} %pad_maximum_fusion.9), channel_id=1, source_target_pairs={{0,4},{1,5},{2,6},{3,7},{4,8},{5,9},{6,10},{7,11},{8,12},{9,13},{1... | collective-permute-start | bytes 786440 | tf_op jit(solution)/shard_map/ppermute | solution.py:32
  208.0 16.2 %collective-permute-start.34 = (bf16[128,1024]{1,0:T(8,128)(2,1)}, bf16[128,1024]{1,0:T(8,128)(2,1)S(1)}, u32[]{:S(2)}, u32[]{:S(2)}) collective-permute-start(bf16[128,1024]{1,0:T(8,128)(2,1)} %pad_maximum_fusion.12), channel_id=1, source_target_pairs={{0,12},{1,13},{2,14},{3,15},{4,0},{5,1},{6,2},{7,3},{8,4},{9,5},{1... | collective-permute-start | bytes 786440 | tf_op jit(solution)/shard_map/ppermute | solution.py:32
  (29 other events, 136.0 us)

commit v3 on v2

v3 whole, which is shorter than its diff:
```python
import functools

import jax
import jax.numpy as jnp
from jax import lax
from jax.experimental import pallas as pl
from jax.experimental.pallas import tpu as pltpu
from jax.sharding import PartitionSpec as P

HEAD_DIM = 128
REACH = 4
PAGE = 16
PLANE = 4
EPSILON = 1e-06


def after(value, *others):
    return lax.optimization_barrier((value, *others))[0]


def flipped(block, mask):
    return lax.ppermute(block, "blk", [(i, i ^ mask) for i in range(lax.axis_size("blk"))])


def next_plane(block):
    count = lax.axis_size("blk")
    return lax.ppermute(block, "blk", [(i, i + PLANE) for i in range(count - PLANE)])


def from_plane(block, ahead):
    count = lax.axis_size("blk")
    return lax.ppermute(
        block, "blk", [((i + PLANE * ahead) % count, i) for i in range(count)]
    )


def to_plane(block, ahead):
    count = lax.axis_size("blk")
    return lax.ppermute(
        block, "blk", [(i, (i + PLANE * ahead) % count) for i in range(count)]
    )


def from_core(block, ahead):
    count = lax.axis_size("tok")
    return lax.ppermute(block, "tok", [((i + ahead) % count, i) for i in range(count)])


def segment_starts(place_ref, lengths_ref, shape):
    token = place_ref[0] * shape[0] + lax.broadcasted_iota(jnp.int32, shape, 0)
    start = jnp.zeros(shape, jnp.int32)
    end = jnp.int32(0)
    for i in range(lengths_ref.shape[0]):
        end = end + lengths_ref[i]
        start = jnp.where(token >= end, end, start)
    return token, start


def rope_kernel(place_ref, lengths_ref, freq_ref, q_ref, k_ref, q_out, k_out):
    rows, width = q_ref.shape
    shape = (rows, HEAD_DIM)
    token, start = segment_starts(place_ref, lengths_ref, shape)
    angle = (token - start).astype(jnp.float32) * freq_ref[...]
    cosine, sine = jnp.cos(angle), jnp.sin(angle)
    lane = lax.broadcasted_iota(jnp.int32, shape, 1)
    sine = jnp.where(lane < HEAD_DIM // 2, -sine, sine)
    for source, target in ((k_ref, k_out), (q_ref, q_out)):
        for head in range(width // HEAD_DIM):
            columns = slice(head * HEAD_DIM, (head + 1) * HEAD_DIM)
            x = source[:, columns].astype(jnp.float32)
            turned = x * cosine + pltpu.roll(x, HEAD_DIM // 2, 1) * sine
            target[:, columns] = turned.astype(jnp.bfloat16)


def score_kernel(place_ref, lengths_ref, q_ref, *rest):
    *keys, out_ref = rest
    rows, width = q_ref.shape
    shape = (rows, rows)
    token, start = segment_starts(place_ref, lengths_ref, shape)
    blk = place_ref[0]
    column = lax.rem(blk, PLANE)
    bases = [blk, blk - PLANE]
    for mask in range(1, PLANE):
        other = column ^ mask
        bases.append(blk - column + other - jnp.where(other > column, PLANE, 0))
    lane = lax.broadcasted_iota(jnp.int32, shape, 1)
    ids = jnp.concatenate([base * rows + lane for base in bases], axis=1)
    token = jnp.concatenate([token] * len(keys), axis=1)
    start = jnp.concatenate([start] * len(keys), axis=1)
    allowed = (ids >= start) & (ids <= token)
    for head in range(width // HEAD_DIM):
        columns = slice(head * HEAD_DIM, (head + 1) * HEAD_DIM)
        key = jnp.concatenate([ref[:, columns] for ref in keys], axis=0)
        scores = lax.dot_general(
            q_ref[:, columns],
            key,
            (((1,), (1,)), ((), ())),
            preferred_element_type=jnp.float32,
        )
        scores = jnp.where(allowed, scores * HEAD_DIM ** (-0.5), -1e30)
        terms = jnp.exp(scores - jnp.max(scores, axis=1, keepdims=True))
        share = 1.0 / jnp.sum(terms, axis=1, keepdims=True)
        out_ref[head] = (terms * share).astype(jnp.bfloat16)


def mix_kernel(place_ref, prob_ref, weight_ref, residual_ref, *rest):
    *values, out_ref = rest
    heads = prob_ref.shape[0]
    mixed = []
    for head in range(heads):
        columns = slice(head * HEAD_DIM, (head + 1) * HEAD_DIM)
        value = jnp.concatenate([ref[:, columns] for ref in values], axis=0)
        product = jnp.dot(prob_ref[head], value, preferred_element_type=jnp.float32)
        mixed.append(product.astype(jnp.bfloat16))
    attention = jnp.concatenate(mixed, axis=1)
    out_ref[...] = jnp.dot(attention, weight_ref[...], preferred_element_type=jnp.float32)
    width = residual_ref.shape[1]
    own = pl.ds(pl.multiple_of(place_ref[1] * width, 128), width)
    out_ref[:, own] = out_ref[:, own] + residual_ref[...].astype(jnp.float32)


def norm_kernel(place_ref, gain_ref, lanes_ref, *rest):
    *addends, rows_out, share_out = rest
    rows, width = addends[0].shape
    part_rows = rows_out.shape[0]
    part_width = share_out.shape[1]
    own = pl.ds(pl.multiple_of(place_ref[1] * part_width, 128), part_width)
    share_out[...] = sum(ref[:, own] for ref in addends).astype(jnp.bfloat16)
    part = pl.ds(pl.multiple_of(place_ref[1] * part_rows, 16), part_rows)
    stream = sum(ref[part, :] for ref in addends).astype(jnp.bfloat16).astype(jnp.float32)
    scale = lax.rsqrt(jnp.mean(stream * stream, axis=1, keepdims=True) + EPSILON)
    rows_out[:, :width] = (stream * scale * gain_ref[...]).astype(jnp.bfloat16)
    rows_out[:, width:] = lanes_ref[part, :]


def local_call(body, out_shapes, scalars, arrays, flops=0, limit=16):
    whole = pl.BlockSpec(memory_space=pltpu.VMEM)
    scalar = pl.BlockSpec(memory_space=pltpu.SMEM)
    moved = sum(x.size * x.dtype.itemsize for x in (*arrays, *out_shapes))
    return pl.pallas_call(
        body,
        in_specs=[scalar] * len(scalars) + [whole] * len(arrays),
        out_specs=[whole] * len(out_shapes),
        out_shape=out_shapes,
        cost_estimate=pl.CostEstimate(flops=flops, bytes_accessed=moved, transcendentals=0),
        compiler_params=pltpu.CompilerParams(vmem_limit_bytes=limit << 20),
    )(*scalars, *arrays)


def gate_lanes(expert_ids, gate_weights, experts):
    hits = expert_ids[:, :, None] == jnp.arange(experts, dtype=jnp.int32)[None, None, :]
    gates = jnp.sum(jnp.where(hits, gate_weights[:, :, None], 0.0), axis=1)
    pieces = []
    for _ in range(3):
        piece = lax.reduce_precision(gates, 8, 7)
        pieces.append(piece.astype(jnp.bfloat16))
        gates = gates - piece
    lanes = jnp.concatenate(pieces, axis=1)
    return jnp.pad(lanes, ((0, 0), (0, -lanes.shape[1] % 128)))


def crossed(block, first):
    cores, count = lax.axis_size("tok"), lax.axis_size("blk")
    route = []
    for core in range(cores):
        mask = 1 if (core % 2 == 0) == first else 2
        route += [(core * count + i, core * count + (i ^ mask)) for i in range(count)]
    return lax.ppermute(block, ("tok", "blk"), route)


def expert_kernel(experts, ahead, place_ref, near_ref, far_ref, gate_ref, up_ref, down_ref, *outs):
    width = gate_ref.shape[1]
    parts = len(outs)
    blocks, part_rows, part_width = outs[0].shape
    held = jnp.concatenate([near_ref[...], far_ref[...]], axis=0)
    rows = held[:, :width]
    lanes = held[:, width:].astype(jnp.float32)
    lane_ids = lax.broadcasted_iota(jnp.int32, lanes.shape, 1)
    named = (lane_ids < 3 * experts) & (lane_ids % experts == place_ref[0])
    weight = jnp.sum(jnp.where(named, lanes, 0.0), axis=1, keepdims=True)
    turned = (((1,), (1,)), ((), ()))
    gate_act = lax.dot_general(rows, gate_ref[...], turned, preferred_element_type=jnp.float32)
    up_act = lax.dot_general(rows, up_ref[...], turned, preferred_element_type=jnp.float32)
    hidden = (gate_act / (1.0 + jnp.exp(-gate_act)) * up_act).astype(jnp.bfloat16)
    for part in range(parts):
        start = lax.rem(place_ref[1] + part, parts) * part_width
        columns = pl.ds(pl.multiple_of(start, 128), part_width)
        product = jnp.dot(hidden, down_ref[:, columns], preferred_element_type=jnp.float32)
        product = (weight * product).astype(jnp.bfloat16)
        order = (0, 2, 1, 3) if (part - ahead) % 2 else (0, 1, 2, 3)
        for block in range(blocks):
            outs[part][order[block]] = product[block * part_rows : (block + 1) * part_rows]


def run_expert(place, near, far, w_gate, w_up, w_down, experts, parts, ahead):
    count = 2 * near.shape[0]
    units, width = w_gate.shape
    out_shape = jax.ShapeDtypeStruct((PLANE, count // PLANE, width // parts), jnp.bfloat16)
    return local_call(
        functools.partial(expert_kernel, experts, ahead),
        [out_shape] * parts,
        [place],
        [near, far, w_gate, w_up, w_down],
        flops=6 * count * width * units,
    )


def wide(block):
    return block.astype(jnp.float32)


def narrow(block):
    return block.astype(jnp.bfloat16)


def plane_scatter(totals):
    sent = narrow(jnp.stack([total[2:4] for total in totals]))
    got = crossed(sent, False)
    totals = [total[0:2] + wide(got[i]) for i, total in enumerate(totals)]
    sent = narrow(jnp.stack([total[1] for total in totals]))
    got = crossed(sent, True)
    return [total[0] + wide(got[i]) for i, total in enumerate(totals)]


def expert_group(place, near, far, weights, experts, cores):
    outs = []
    for ahead in range(cores):
        near_rows = from_core(near, ahead) if ahead else near
        far_rows = from_core(far, ahead) if ahead else far
        outs.append(run_expert(place, near_rows, far_rows, *weights, experts, cores, ahead))
    totals = []
    for rows_of in range(cores):
        total = wide(outs[rows_of][0])
        for ahead in range(1, cores):
            sent = outs[(rows_of + ahead) % cores][ahead]
            total = total + wide(from_core(sent, cores - ahead))
        totals.append(total)
    return plane_scatter(totals)


def on_device(
    q_proj,
    k_proj,
    v_proj,
    residual,
    prompt_lengths,
    expert_ids,
    gate_weights,
    page_table,
    out_weight,
    norm_gain,
    w_gate,
    w_up,
    w_down,
):
    tok_rows = q_proj.shape[0]
    col_width = residual.shape[1]
    model_width = norm_gain.shape[0]
    blk_index = lax.axis_index("blk")
    tok_index = lax.axis_index("tok")
    cores = lax.axis_size("tok")
    experts = lax.axis_size("blk")
    planes = experts // PLANE
    place = jnp.stack([blk_index, tok_index]).astype(jnp.int32)
    part_rows = tok_rows // cores
    half_dim = HEAD_DIM // 2
    inv_freq = 10000.0 ** (-jnp.arange(half_dim, dtype=jnp.float32) / half_dim)
    freq = jnp.concatenate([inv_freq, inv_freq])[None, :]
    rotated = jax.ShapeDtypeStruct(q_proj.shape, jnp.bfloat16)
    rot_query, rot_keys = local_call(
        rope_kernel, [rotated] * 2, [place, prompt_lengths], [freq, q_proj, k_proj]
    )
    column = blk_index % PLANE
    key_blocks, value_blocks = [
        [block, next_plane(block)] for block in (rot_keys, after(v_proj, rot_keys))
    ]
    for blocks in (key_blocks, value_blocks):
        own, below = blocks
        for mask in range(1, PLANE):
            blocks.append(flipped(jnp.where(column < column ^ mask, own, below), mask))
    heads = q_proj.shape[1] // HEAD_DIM
    probs_shape = (heads, tok_rows, len(key_blocks) * tok_rows)
    probs = local_call(
        score_kernel,
        [jax.ShapeDtypeStruct(probs_shape, jnp.bfloat16)],
        [place, prompt_lengths],
        [rot_query, *key_blocks],
        flops=2 * tok_rows * probs_shape[2] * heads * HEAD_DIM,
    )[0]
    page_count = tok_rows // PAGE
    local_page = page_table - blk_index * page_count
    kv_rows = jnp.stack([rot_keys, v_proj], axis=1).reshape(page_count, PAGE, 2, -1)
    kv_pages = jnp.zeros_like(kv_rows).at[local_page].set(kv_rows)
    lanes = gate_lanes(expert_ids, gate_weights, experts)
    probs = after(probs, kv_pages, lanes)
    mixed = local_call(
        mix_kernel,
        [jax.ShapeDtypeStruct((tok_rows, model_width), jnp.float32)],
        [place],
        [probs, out_weight, residual, *value_blocks],
        flops=2 * tok_rows * (probs_shape[2] + model_width) * heads * HEAD_DIM,
    )[0]
    if cores == 2:
        addends = [mixed, from_core(mixed, 1)]
    else:
        addends = [lax.psum(mixed, "tok")]
    payload, own_share = local_call(
        norm_kernel,
        [
            jax.ShapeDtypeStruct((part_rows, model_width + lanes.shape[1]), jnp.bfloat16),
            jax.ShapeDtypeStruct((tok_rows, col_width), jnp.bfloat16),
        ],
        [place],
        [norm_gain[None, :], lanes, *addends],
    )
    weights = (w_gate[0].T, w_up[0].T, w_down[0])
    came = {0: payload}
    for ahead in range(1, planes):
        came[ahead] = from_plane(payload, ahead)
    if planes <= 4:
        groups = [[0]] + [sorted({i, planes - i}) for i in range(1, planes // 2 + 1)]
    else:
        groups = [[0]] + [list(range(i, min(i + 8, planes))) for i in range(1, planes, 8)]
    results = {}
    near_before = None
    done_before = None
    held = []
    for number, group in enumerate(groups):
        column = jnp.concatenate([came[ahead] for ahead in group])
        if near_before is not None:
            if number > 1:
                column = after(column, near_before)
            if planes > 4:
                column = after(column, done_before)
        near = jnp.concatenate([column, crossed(column, True)])
        far = crossed(near, False)
        near_before = near
        if planes > 4:
            done_before = expert_group(place, near, far, weights, experts, cores)
            held.append(done_before)
        else:
            held.append((near, far))
    if planes <= 4:
        held = [expert_group(place, near, far, weights, experts, cores) for near, far in held]
    for group, summed in zip(groups, held, strict=True):
        for i, ahead in enumerate(group):
            results[ahead] = jnp.concatenate(
                [total[i * part_rows : (i + 1) * part_rows] for total in summed]
            )
    moe = results[0]
    for ahead in range(1, planes):
        moe = moe + wide(to_plane(narrow(results[ahead]), ahead))
    moe = jnp.roll(moe.reshape(cores, part_rows, col_width), tok_index, axis=0)
    moe = moe.reshape(tok_rows, col_width)
    layer_out = (own_share.astype(jnp.float32) + moe).astype(jnp.bfloat16)
    return (layer_out, kv_pages)


def solution(mesh):
    placed = (
        P("blk", "tok"),
        P("blk", "tok"),
        P("blk", "tok"),
        P("blk", "tok"),
        P(),
        P("blk", None),
        P("blk", None),
        P("blk"),
        P("tok", None),
        P(),
        P("blk", None, "tok"),
        P("blk", None, "tok"),
        P("blk", "tok", None),
    )
    return jax.shard_map(
        on_device,
        mesh=mesh,
        in_specs=placed,
        out_specs=(P("blk", "tok"), P("blk", None, None, "tok")),
        check_vma=False,
    )
```

time: 227 us -> 186 us (0.82)
  local copies, waits for them, and re-layouts: 31.1 us -> 10.4 us
  waiting for transfers between devices: 92.9 us -> 80.5 us
  matrix products: 7.59 us -> 0 us
  other arithmetic: 14.1 us -> 8.87 us
  starting transfers between devices: 49.9 us -> 54.4 us
    ppermute x4 -> x8, waiting for transfers between devices: 27.7 us -> 10.5 us  [the longest x6 8.08 us: flipped(): lax.ppermute(block, 'blk', [(i, i ^ mask) for i in range(lax.axis_size('b...]
    ppermute x12, waiting for transfers between devices: 31.3 us -> 47.2 us  [crossed(): return lax.ppermute(block, ('tok', 'blk'), route)]
    unnamed x66 -> x31, local copies, waits for them, and re-layouts: 21.5 us -> 6.21 us
    ppermute x3, waiting for transfers between devices: 18.9 us -> 8.48 us  [from_plane(): lax.ppermute(block, 'blk', [((i + PLANE * ahead) % count, i) for i in ran...]
    ppermute x12, starting transfers between devices: 10.4 us -> 17.5 us  [crossed(): return lax.ppermute(block, ('tok', 'blk'), route)]
    ppermute x4 -> x8, starting transfers between devices: 22 us -> 16.6 us  [the longest x2 8.43 us: next_plane(): lax.ppermute(block, 'blk', [(i, i + PLANE) for i in range(count - PLANE)])]
    sub x1 -> x0, matrix products: 4.27 us -> none  [attend(): exp_terms = jnp.where(allowed[None], jnp.exp(scores - top_score), 0.0)]
    ppermute x3, starting transfers between devices: 5.74 us -> 9.12 us  [to_plane(): lax.ppermute(block, 'blk', [(i, (i + PLANE * ahead) % count) for i in ran...]
  transfers between devices with their start and end apart: 35 -> 39, of which waited for: 15 -> 18; matrix products, arithmetic and copies ran while one was open for 12% -> 7% of each run, Pallas kernels for 13% -> 14%
where the time goes in v3:
time: 186 us; the launch traced here: 185 us
  waiting for transfers between devices  80.5 us (43%)
  starting transfers between devices  54.4 us (29%)
  Pallas kernels  30 us (16%)
  local copies, waits for them, and re-layouts  10.4 us (6%)
  other arithmetic  8.87 us (5%)
    ppermute x12, waiting for transfers between devices, crossed(): return lax.ppermute(block, ('tok', 'blk'), route)  47.2 us
    pallas_call x10, Pallas kernels, local_call(): pl.pallas_call(body, in_specs=[scalar] * len(scalars) + [whole] * len(arr...  30 us
    ppermute x12, starting transfers between devices, crossed(): return lax.ppermute(block, ('tok', 'blk'), route)  17.5 us
    ppermute x3, waiting for transfers between devices, to_plane(): lax.ppermute(block, 'blk', [(i, (i + PLANE * ahead) % count) for i in ran...  11.7 us
    ppermute x3, starting transfers between devices, to_plane(): lax.ppermute(block, 'blk', [(i, (i + PLANE * ahead) % count) for i in ran...  9.12 us
    ppermute x3, waiting for transfers between devices, from_plane(): lax.ppermute(block, 'blk', [((i + PLANE * ahead) % count, i) for i in ran...  8.48 us
    ppermute x2, starting transfers between devices, next_plane(): lax.ppermute(block, 'blk', [(i, i + PLANE) for i in range(count - PLANE)])  8.43 us
    ppermute x6, starting transfers between devices, flipped(): lax.ppermute(block, 'blk', [(i, i ^ mask) for i in range(lax.axis_size('b...  8.21 us
  transfers between devices with their start and end apart: 39, of which 18 were waited for; matrix products, arithmetic and copies ran while one was open for 7% of the time, Pallas kernels for 14%

profile of v3, /device:TPU:0, one launch (start us, length us, event | category | flops | bytes accessed | tf_op | source)
XLA Modules:
  0.0 185.4 jit_solution(13037688980978912970)
XLA Ops:
  4.5 4.9 %collective-permute-start = (bf16[128,1024]{1,0:T(8,128)(2,1)S(1)}, bf16[128,1024]{1,0:T(8,128)(2,1)S(1)}, u32[]{:S(2)}, u32[]{:S(2)}) collective-permute-start(bf16[128,1024]{1,0:T(8,128)(2,1)S(1)} %get-tuple-element.22.rest_0_), channel_id=1, source_target_pairs={{0,4},{1,5},{2,6},{3,7},{4,8},{5,9},{6,10},{7,11},{8,12},{9,13},{1... | collective-permute-start | bytes 786440 | tf_op jit(solution)/shard_map/ppermute | solution.py:27
  9.4 3.5 %collective-permute-start.4 = (bf16[128,1024]{1,0:T(8,128)(2,1)}, bf16[128,1024]{1,0:T(8,128)(2,1)S(1)}, u32[]{:S(2)}, u32[]{:S(2)}) collective-permute-start(bf16[128,1024]{1,0:T(8,128)(2,1)} %rest_0_), channel_id=1, source_target_pairs={{0,4},{1,5},{2,6},{3,7},{4,8},{5,9},{6,10},{7,11},{8,12},{9,13},{1... | collective-permute-start | bytes 786440 | tf_op jit(solution)/shard_map/ppermute | solution.py:27
  13.7 2.4 %collective-permute-done.rest_1_ = bf16[128,1024]{1,0:T(8,128)(2,1)S(1)} collective-permute-done((bf16[128,1024]{1,0:T(8,128)(2,1)S(1)}, bf16[128,1024]{1,0:T(8,128)(2,1)S(1)}, u32[]{:S(2)}, u32[]{:S(2)}) %collective-permute-start) | collective-permute-done | bytes 262176 | tf_op jit(solution)/shard_map/ppermute | solution.py:27
  16.9 2.4 %collective-permute-start.3 = (bf16[128,1024]{1,0:T(8,128)(2,1)S(1)}, bf16[128,1024]{1,0:T(8,128)(2,1)S(1)}, u32[]{:S(2)}, u32[]{:S(2)}) collective-permute-start(bf16[128,1024]{1,0:T(8,128)(2,1)S(1)} %get-tuple-element.57), channel_id=1, source_target_pairs={{0,3},{1,2},{2,1},{3,0},{4,7},{5,6},{6,5},{7,4},{8,11},{9,10},{10,... | collective-permute-start | bytes 786440 | tf_op jit(solution)/shard_map/ppermute | solution.py:22
  22.2 2.4 %collective-permute-start.7 = (bf16[128,1024]{1,0:T(8,128)(2,1)}, bf16[128,1024]{1,0:T(8,128)(2,1)S(1)}, u32[]{:S(2)}, u32[]{:S(2)}) collective-permute-start(bf16[128,1024]{1,0:T(8,128)(2,1)} %get-tuple-element.54), channel_id=1, source_target_pairs={{0,3},{1,2},{2,1},{3,0},{4,7},{5,6},{6,5},{7,4},{8,11},{9,10},{10,... | collective-permute-start | bytes 786440 | tf_op jit(solution)/shard_map/ppermute | solution.py:22
  26.8 1.8 collective-permute-start.5
  29.6 2.7 %scatter_fusion = bf16[8,16,2,1024]{3,1,2,0:T(8,128)(2,1)} fusion(bf16[8,16,2,1024]{3,1,2,0:T(8,128)(2,1)} %broadcast_in_dim.31, s32[8]{0:T(128)S(1)} %compare_select_fusion, bf16[8,16,2,1024]{3,1,2,0:T(8,128)(2,1)} %pad_maximum_fusion.2), kind=kCustom, calls=%fused_computation | custom fusion | bytes 1572896 | tf_op jit(solution)/shard_map/scatter | solution.py:293
  32.3 3.0 %collective-permute-done.2.rest_3_ = bf16[128,1024]{1,0:T(8,128)(2,1)S(1)} collective-permute-done((bf16[128,1024]{1,0:T(8,128)(2,1)}, bf16[128,1024]{1,0:T(8,128)(2,1)S(1)}, u32[]{:S(2)}, u32[]{:S(2)}) %collective-permute-start.2) | collective-permute-done | bytes 262176 | tf_op jit(solution)/shard_map/ppermute | solution.py:22
  35.3 1.9 %shard_map.141.prob_ref = bf16[8,128,640]{2,1,0:T(8,128)(2,1)S(1)} custom-call(s32[2]{0:T(128)S(1)} %pad_add_fusion.place_ref, s32[8]{0:T(128)S(1)} %copy-done.10, bf16[128,1024]{1,0:T(8,128)(2,1)S(1)} %get-tuple-element.21.q_ref, bf16[128,1024]{1,0:T(8,128)(2,1)S(1)} %get-tuple-element.22.rest_0_, bf16[128,1024]{1,0:T(8,128)(2,1)S(1)} %collective-permute-done.rest_1_, ...), custom_call_target="tpu_custom_call" | custom-call | flops 167772160 | bytes 2883584 | tf_op jit(solution)/shard_map/pallas_call | solution.py:140
  38.0 2.6 %collective-permute-done.6.rest_3_ = bf16[128,1024]{1,0:T(8,128)(2,1)S(1)} collective-permute-done((bf16[128,1024]{1,0:T(8,128)(2,1)}, bf16[128,1024]{1,0:T(8,128)(2,1)S(1)}, u32[]{:S(2)}, u32[]{:S(2)}) %collective-permute-start.6) | collective-permute-done | bytes 262176 | tf_op jit(solution)/shard_map/ppermute | solution.py:22
  40.7 2.2 %copy-done.3 = bf16[1024,2048]{1,0:T(8,128)(2,1)S(1)} copy-done((bf16[1024,2048]{1,0:T(8,128)(2,1)S(1)}, bf16[1024,2048]{1,0:T(8,128)(2,1)}, u32[]{:S(2)}) %copy-start.3) | copy-done | bytes 4194328
  42.9 1.7 shard_map.142.rest_0_
  44.7 2.6 %collective-permute-done.8.rest_1_ = f32[128,2048]{1,0:T(8,128)S(1)} collective-permute-done((f32[128,2048]{1,0:T(8,128)S(1)}, f32[128,2048]{1,0:T(8,128)S(1)}, u32[]{:S(2)}, u32[]{:S(2)}) %collective-permute-start.8) | collective-permute-done | bytes 1048608 | tf_op jit(solution)/shard_map/ppermute | solution.py:46
  48.1 3.6 %collective-permute-start.28 = (bf16[64,2176]{1,0:T(8,128)(2,1)S(1)}, bf16[64,2176]{1,0:T(8,128)(2,1)S(1)}, u32[]{:S(2)}, u32[]{:S(2)}) collective-permute-start(bf16[64,2176]{1,0:T(8,128)(2,1)S(1)} %get-tuple-element.26), channel_id=1, source_target_pairs={{8,0},{9,1},{10,2},{11,3},{12,4},{13,5},{14,6},{15,7},{0,8},{1,9},... | collective-permute-start | bytes 835592 | tf_op jit(solution)/shard_map/ppermute | solution.py:32
  53.3 2.2 %collective-permute-start.17 = (bf16[64,2176]{1,0:T(8,128)(2,1)S(1)}, bf16[64,2176]{1,0:T(8,128)(2,1)S(1)}, u32[]{:S(2)}, u32[]{:S(2)}) collective-permute-start(bf16[64,2176]{1,0:T(8,128)(2,1)S(1)} %get-tuple-element.26), channel_id=1, source_target_pairs={{4,0},{5,1},{6,2},{7,3},{8,4},{9,5},{10,6},{11,7},{12,8},{13,9},{1... | collective-permute-start | bytes 835592 | tf_op jit(solution)/shard_map/ppermute | solution.py:32
  57.1 5.0 %collective-permute-done.9 = bf16[64,2176]{1,0:T(8,128)(2,1)S(1)} collective-permute-done((bf16[64,2176]{1,0:T(8,128)(2,1)S(1)}, bf16[64,2176]{1,0:T(8,128)(2,1)S(1)}, u32[]{:S(2)}, u32[]{:S(2)}) %collective-permute-start.9) | collective-permute-done | bytes 278560 | tf_op jit(solution)/shard_map/ppermute | solution.py:168
  63.7 2.9 %collective-permute-done.18 = bf16[64,2176]{1,0:T(8,128)(2,1)S(1)} collective-permute-done((bf16[64,2176]{1,0:T(8,128)(2,1)S(1)}, bf16[64,2176]{1,0:T(8,128)(2,1)S(1)}, u32[]{:S(2)}, u32[]{:S(2)}) %collective-permute-start.18) | collective-permute-done | bytes 278560 | tf_op jit(solution)/shard_map/ppermute | solution.py:32
  66.6 5.6 %collective-permute-done.17 = bf16[64,2176]{1,0:T(8,128)(2,1)S(1)} collective-permute-done((bf16[64,2176]{1,0:T(8,128)(2,1)S(1)}, bf16[64,2176]{1,0:T(8,128)(2,1)S(1)}, u32[]{:S(2)}, u32[]{:S(2)}) %collective-permute-start.17) | collective-permute-done | bytes 278560 | tf_op jit(solution)/shard_map/ppermute | solution.py:32
  73.9 7.9 %collective-permute-done.19 = bf16[128,2176]{1,0:T(8,128)(2,1)S(1)} collective-permute-done((bf16[128,2176]{1,0:T(8,128)(2,1)S(1)}, bf16[128,2176]{1,0:T(8,128)(2,1)S(1)}, u32[]{:S(2)}, u32[]{:S(2)}) %collective-permute-start.19) | collective-permute-done | bytes 557088 | tf_op jit(solution)/shard_map/ppermute | solution.py:168
  85.5 3.2 %shard_map.144 = (bf16[4,64,1024]{2,1,0:T(8,128)(2,1)S(1)}, bf16[4,64,1024]{2,1,0:T(8,128)(2,1)S(1)}) custom-call(s32[2]{0:T(128)S(1)} %pad_add_fusion.place_ref, bf16[128,2176]{1,0:T(8,128)(2,1)S(1)} %constant_dynamic-update-slice_fusion.near_ref, bf16[128,2176]{1,0:T(8,128)(2,1)S(1)} %collective-permute-done.10.far_ref, bf16[704,2048]{1,0:T(8,128)(2,1)S(1)} %bitcast.82, ...), custom_call_target="tpu_custom_call" | custom-call | flops 2214592512 | bytes 10813440 | tf_op jit(solution)/shard_map/pallas_call | solution.py:140
  92.3 3.2 %shard_map.145 = (bf16[4,64,1024]{2,1,0:T(8,128)(2,1)S(1)}, bf16[4,64,1024]{2,1,0:T(8,128)(2,1)S(1)}) custom-call(s32[2]{0:T(128)S(1)} %pad_add_fusion.place_ref, bf16[128,2176]{1,0:T(8,128)(2,1)S(1)} %collective-permute-done.11.near_ref, bf16[128,2176]{1,0:T(8,128)(2,1)S(1)} %collective-permute-done.12.far_ref, bf16[704,2048]{1,0:T(8,128)(2,1)S(1)} %bitcast.83, ...), custom_call_target="tpu_custom_call" | custom-call | flops 2214592512 | bytes 10813440 | tf_op jit(solution)/shard_map/pallas_call | solution.py:140
  95.8 9.8 %collective-permute-done.30.far_ref = bf16[128,2176]{1,0:T(8,128)(2,1)S(1)} collective-permute-done((bf16[128,2176]{1,0:T(8,128)(2,1)S(1)}, bf16[128,2176]{1,0:T(8,128)(2,1)S(1)}, u32[]{:S(2)}, u32[]{:S(2)}) %collective-permute-start.30) | collective-permute-done | bytes 557088 | tf_op jit(solution)/shard_map/ppermute | solution.py:168
  106.2 3.2 %shard_map.148 = (bf16[4,64,1024]{2,1,0:T(8,128)(2,1)S(1)}, bf16[4,64,1024]{2,1,0:T(8,128)(2,1)S(1)}) custom-call(s32[2]{0:T(128)S(1)} %pad_add_fusion.place_ref, bf16[128,2176]{1,0:T(8,128)(2,1)S(1)} %constant_dynamic-update-slice_fusion.5.near_ref, bf16[128,2176]{1,0:T(8,128)(2,1)S(1)} %collective-permute-done.30.far_ref, bf16[704,2048]{1,0:T(8,128)(2,1)S(1)} %bitcast.84, ...), custom_call_target="tpu_custom_call" | custom-call | flops 2214592512 | bytes 10813440 | tf_op jit(solution)/shard_map/pallas_call | solution.py:140
  110.0 5.7 %shard_map.146 = (bf16[4,128,1024]{2,1,0:T(8,128)(2,1)S(1)}, bf16[4,128,1024]{2,1,0:T(8,128)(2,1)S(1)}) custom-call(s32[2]{0:T(128)S(1)} %pad_add_fusion.place_ref, bf16[256,2176]{1,0:T(8,128)(2,1)S(1)} %constant_dynamic-update-slice_fusion.2.near_ref, bf16[256,2176]{1,0:T(8,128)(2,1)S(1)} %collective-permute-done.20.far_ref, ...), custom_call_target="tpu_custom_call" | custom-call | flops 4429185024 | bytes 12976128 | tf_op jit(solution)/shard_map/pallas_call | solution.py:140
  116.3 3.5 %shard_map.149 = (bf16[4,64,1024]{2,1,0:T(8,128)(2,1)S(1)}, bf16[4,64,1024]{2,1,0:T(8,128)(2,1)S(1)}) custom-call(s32[2]{0:T(128)S(1)} %pad_add_fusion.place_ref, bf16[128,2176]{1,0:T(8,128)(2,1)S(1)} %collective-permute-done.31.near_ref, bf16[128,2176]{1,0:T(8,128)(2,1)S(1)} %collective-permute-done.32.far_ref, bf16[704,2048]{1,0:T(8,128)(2,1)S(1)} %bitcast.86, ...), custom_call_target="tpu_custom_call" | custom-call | flops 2214592512 | bytes 10813440 | tf_op jit(solution)/shard_map/pallas_call | solution.py:140
  120.2 5.7 %shard_map.147 = (bf16[4,128,1024]{2,1,0:T(8,128)(2,1)S(1)}, bf16[4,128,1024]{2,1,0:T(8,128)(2,1)S(1)}) custom-call(s32[2]{0:T(128)S(1)} %pad_add_fusion.place_ref, bf16[256,2176]{1,0:T(8,128)(2,1)S(1)} %collective-permute-done.21.near_ref, bf16[256,2176]{1,0:T(8,128)(2,1)S(1)} %collective-permute-done.22.far_ref, bf16[704,2048]{1,0:T(8,128)(2,1)S(1)} %bitcast.87, ...), custom_call_target="tpu_custom_call" | custom-call | flops 4429185024 | bytes 12976128 | tf_op jit(solution)/shard_map/pallas_call | solution.py:140
  131.7 4.2 %collective-permute-done.35 = bf16[2,2,64,1024]{3,2,1,0:T(8,128)(2,1)S(1)} collective-permute-done((bf16[2,2,64,1024]{3,2,1,0:T(8,128)(2,1)S(1)}, bf16[2,2,64,1024]{3,2,1,0:T(8,128)(2,1)S(1)}, u32[]{:S(2)}, u32[]{:S(2)}) %collective-permute-start.35) | collective-permute-done | bytes 524320 | tf_op jit(solution)/shard_map/ppermute | solution.py:168
  137.7 12.2 %collective-permute-done.25 = bf16[2,2,128,1024]{3,2,1,0:T(8,128)(2,1)S(1)} collective-permute-done((bf16[2,2,128,1024]{3,2,1,0:T(8,128)(2,1)S(1)}, bf16[2,2,128,1024]{3,2,1,0:T(8,128)(2,1)S(1)}, u32[]{:S(2)}, u32[]{:S(2)}) %collective-permute-start.25) | collective-permute-done | bytes 1048608 | tf_op jit(solution)/shard_map/ppermute | solution.py:168
  152.1 6.5 %collective-permute-done.15 = bf16[2,2,64,1024]{3,2,1,0:T(8,128)(2,1)S(1)} collective-permute-done((bf16[2,2,64,1024]{3,2,1,0:T(8,128)(2,1)S(1)}, bf16[2,2,64,1024]{3,2,1,0:T(8,128)(2,1)S(1)}, u32[]{:S(2)}, u32[]{:S(2)}) %collective-permute-start.15) | collective-permute-done | bytes 524320 | tf_op jit(solution)/shard_map/ppermute | solution.py:168
  160.5 7.1 %collective-permute-start.37 = (bf16[128,1024]{1,0:T(8,128)(2,1)S(1)}, bf16[128,1024]{1,0:T(8,128)(2,1)S(1)}, u32[]{:S(2)}, u32[]{:S(2)}) collective-permute-start(bf16[128,1024]{1,0:T(8,128)(2,1)S(1)} %pad_maximum_fusion.9), channel_id=1, source_target_pairs={{0,8},{1,9},{2,10},{3,11},{4,12},{5,13},{6,14},{7,15},{8,0},{9,1},... | collective-permute-start | bytes 786440 | tf_op jit(solution)/shard_map/ppermute | solution.py:39
  172.7 5.8 %collective-permute-done.37 = bf16[128,1024]{1,0:T(8,128)(2,1)S(1)} collective-permute-done((bf16[128,1024]{1,0:T(8,128)(2,1)S(1)}, bf16[128,1024]{1,0:T(8,128)(2,1)S(1)}, u32[]{:S(2)}, u32[]{:S(2)}) %collective-permute-start.37) | collective-permute-done | bytes 262176 | tf_op jit(solution)/shard_map/ppermute | solution.py:39
  178.5 5.9 %collective-permute-done.38 = bf16[128,1024]{1,0:T(8,128)(2,1)S(1)} collective-permute-done((bf16[128,1024]{1,0:T(8,128)(2,1)}, bf16[128,1024]{1,0:T(8,128)(2,1)S(1)}, u32[]{:S(2)}, u32[]{:S(2)}) %collective-permute-start.38) | collective-permute-done | bytes 262176 | tf_op jit(solution)/shard_map/ppermute | solution.py:39
  (142 shorter events, 46.8 us)
Async XLA Ops:
  4.5 11.6 %collective-permute-start = (bf16[128,1024]{1,0:T(8,128)(2,1)S(1)}, bf16[128,1024]{1,0:T(8,128)(2,1)S(1)}, u32[]{:S(2)}, u32[]{:S(2)}) collective-permute-start(bf16[128,1024]{1,0:T(8,128)(2,1)S(1)} %get-tuple-element.22.rest_0_), channel_id=1, source_target_pairs={{0,4},{1,5},{2,6},{3,7},{4,8},{5,9},{6,10},{7,11},{8,12},{9,13},{1... | collective-permute-start | bytes 786440 | tf_op jit(solution)/shard_map/ppermute | solution.py:27
  9.4 11.8 %collective-permute-start.4 = (bf16[128,1024]{1,0:T(8,128)(2,1)}, bf16[128,1024]{1,0:T(8,128)(2,1)S(1)}, u32[]{:S(2)}, u32[]{:S(2)}) collective-permute-start(bf16[128,1024]{1,0:T(8,128)(2,1)} %rest_0_), channel_id=1, source_target_pairs={{0,4},{1,5},{2,6},{3,7},{4,8},{5,9},{6,10},{7,11},{8,12},{9,13},{1... | collective-permute-start | bytes 786440 | tf_op jit(solution)/shard_map/ppermute | solution.py:27
  16.9 9.9 %collective-permute-start.3 = (bf16[128,1024]{1,0:T(8,128)(2,1)S(1)}, bf16[128,1024]{1,0:T(8,128)(2,1)S(1)}, u32[]{:S(2)}, u32[]{:S(2)}) collective-permute-start(bf16[128,1024]{1,0:T(8,128)(2,1)S(1)} %get-tuple-element.57), channel_id=1, source_target_pairs={{0,3},{1,2},{2,1},{3,0},{4,7},{5,6},{6,5},{7,4},{8,11},{9,10},{10,... | collective-permute-start | bytes 786440 | tf_op jit(solution)/shard_map/ppermute | solution.py:22
  20.2 15.1 %collective-permute-start.2 = (bf16[128,1024]{1,0:T(8,128)(2,1)}, bf16[128,1024]{1,0:T(8,128)(2,1)S(1)}, u32[]{:S(2)}, u32[]{:S(2)}) collective-permute-start(bf16[128,1024]{1,0:T(8,128)(2,1)} %get-tuple-element.58), channel_id=1, source_target_pairs={{0,2},{1,3},{2,0},{3,1},{4,6},{5,7},{6,4},{7,5},{8,10},{9,11},{10,... | collective-permute-start | bytes 786440 | tf_op jit(solution)/shard_map/ppermute | solution.py:22
  20.7 14.6 %collective-permute-start.1 = (bf16[128,1024]{1,0:T(8,128)(2,1)S(1)}, bf16[128,1024]{1,0:T(8,128)(2,1)S(1)}, u32[]{:S(2)}, u32[]{:S(2)}) collective-permute-start(bf16[128,1024]{1,0:T(8,128)(2,1)S(1)} %get-tuple-element.59), channel_id=1, source_target_pairs={{0,1},{1,0},{2,3},{3,2},{4,5},{5,4},{6,7},{7,6},{8,9},{9,8},{10,11... | collective-permute-start | bytes 786440 | tf_op jit(solution)/shard_map/ppermute | solution.py:22
  22.2 15.8 %collective-permute-start.7 = (bf16[128,1024]{1,0:T(8,128)(2,1)}, bf16[128,1024]{1,0:T(8,128)(2,1)S(1)}, u32[]{:S(2)}, u32[]{:S(2)}) collective-permute-start(bf16[128,1024]{1,0:T(8,128)(2,1)} %get-tuple-element.54), channel_id=1, source_target_pairs={{0,3},{1,2},{2,1},{3,0},{4,7},{5,6},{6,5},{7,4},{8,11},{9,10},{10,... | collective-permute-start | bytes 786440 | tf_op jit(solution)/shard_map/ppermute | solution.py:22
  24.7 16.0 %collective-permute-start.6 = (bf16[128,1024]{1,0:T(8,128)(2,1)}, bf16[128,1024]{1,0:T(8,128)(2,1)S(1)}, u32[]{:S(2)}, u32[]{:S(2)}) collective-permute-start(bf16[128,1024]{1,0:T(8,128)(2,1)} %get-tuple-element.55), channel_id=1, source_target_pairs={{0,2},{1,3},{2,0},{3,1},{4,6},{5,7},{6,4},{7,5},{8,10},{9,11},{10,... | collective-permute-start | bytes 786440 | tf_op jit(solution)/shard_map/ppermute | solution.py:22
  26.8 13.9 %collective-permute-start.5 = (bf16[128,1024]{1,0:T(8,128)(2,1)}, bf16[128,1024]{1,0:T(8,128)(2,1)S(1)}, u32[]{:S(2)}, u32[]{:S(2)}) collective-permute-start(bf16[128,1024]{1,0:T(8,128)(2,1)} %get-tuple-element.56), channel_id=1, source_target_pairs={{0,1},{1,0},{2,3},{3,2},{4,5},{5,4},{6,7},{7,6},{8,9},{9,8},{10,11... | collective-permute-start | bytes 786440 | tf_op jit(solution)/shard_map/ppermute | solution.py:22
  48.1 33.8 %collective-permute-start.28 = (bf16[64,2176]{1,0:T(8,128)(2,1)S(1)}, bf16[64,2176]{1,0:T(8,128)(2,1)S(1)}, u32[]{:S(2)}, u32[]{:S(2)}) collective-permute-start(bf16[64,2176]{1,0:T(8,128)(2,1)S(1)} %get-tuple-element.26), channel_id=1, source_target_pairs={{8,0},{9,1},{10,2},{11,3},{12,4},{13,5},{14,6},{15,7},{0,8},{1,9},... | collective-permute-start | bytes 835592 | tf_op jit(solution)/shard_map/ppermute | solution.py:32
  51.7 14.9 %collective-permute-start.18 = (bf16[64,2176]{1,0:T(8,128)(2,1)S(1)}, bf16[64,2176]{1,0:T(8,128)(2,1)S(1)}, u32[]{:S(2)}, u32[]{:S(2)}) collective-permute-start(bf16[64,2176]{1,0:T(8,128)(2,1)S(1)} %get-tuple-element.26), channel_id=1, source_target_pairs={{12,0},{13,1},{14,2},{15,3},{0,4},{1,5},{2,6},{3,7},{4,8},{5,9},{6... | collective-permute-start | bytes 835592 | tf_op jit(solution)/shard_map/ppermute | solution.py:32
  53.3 18.9 %collective-permute-start.17 = (bf16[64,2176]{1,0:T(8,128)(2,1)S(1)}, bf16[64,2176]{1,0:T(8,128)(2,1)S(1)}, u32[]{:S(2)}, u32[]{:S(2)}) collective-permute-start(bf16[64,2176]{1,0:T(8,128)(2,1)S(1)} %get-tuple-element.26), channel_id=1, source_target_pairs={{4,0},{5,1},{6,2},{7,3},{8,4},{9,5},{10,6},{11,7},{12,8},{13,9},{1... | collective-permute-start | bytes 835592 | tf_op jit(solution)/shard_map/ppermute | solution.py:32
  62.1 28.3 %collective-permute-start.11 = (bf16[128,2176]{1,0:T(8,128)(2,1)S(1)}, bf16[128,2176]{1,0:T(8,128)(2,1)S(1)}, u32[]{:S(2)}, u32[]{:S(2)}) collective-permute-start(bf16[128,2176]{1,0:T(8,128)(2,1)S(1)} %constant_dynamic-update-slice_fusion.near_ref), channel_id=1, source_target_pairs={{16,0},{0,16},{17,1},{1,17},{18,2},{2,18},{19,3},{3,19},{20,4},{4,... | collective-permute-start | bytes 1671176 | tf_op jit(solution)/shard_map/ppermute | solution.py:46
  62.2 21.3 %collective-permute-start.10 = (bf16[128,2176]{1,0:T(8,128)(2,1)S(1)}, bf16[128,2176]{1,0:T(8,128)(2,1)S(1)}, u32[]{:S(2)}, u32[]{:S(2)}) collective-permute-start(bf16[128,2176]{1,0:T(8,128)(2,1)S(1)} %constant_dynamic-update-slice_fusion.near_ref), channel_id=1, source_target_pairs={{0,2},{1,3},{2,0},{3,1},{4,6},{5,7},{6,4},{7,5},{8,10},{9,11},{10,... | collective-permute-start | bytes 1671176 | tf_op jit(solution)/shard_map/ppermute | solution.py:168
  72.2 9.6 %collective-permute-start.19 = (bf16[128,2176]{1,0:T(8,128)(2,1)S(1)}, bf16[128,2176]{1,0:T(8,128)(2,1)S(1)}, u32[]{:S(2)}, u32[]{:S(2)}) collective-permute-start(bf16[128,2176]{1,0:T(8,128)(2,1)S(1)} %pad_maximum_fusion.1), channel_id=1, source_target_pairs={{0,1},{1,0},{2,3},{3,2},{4,5},{5,4},{6,7},{7,6},{8,9},{9,8},{10,11... | collective-permute-start | bytes 1671176 | tf_op jit(solution)/shard_map/ppermute | solution.py:168
  83.5 36.6 %collective-permute-start.21 = (bf16[256,2176]{1,0:T(8,128)(2,1)S(1)}, bf16[256,2176]{1,0:T(8,128)(2,1)S(1)}, u32[]{:S(2)}, u32[]{:S(2)}) collective-permute-start(bf16[256,2176]{1,0:T(8,128)(2,1)S(1)} %constant_dynamic-update-slice_fusion.2.near_ref), channel_id=1, source_target_pairs={{16,0},{0,16},{17,1},{1,17},{18,2},{2,18},{19,3},{3,19},{20,4},{4,... | collective-permute-start | bytes 3342344 | tf_op jit(solution)/shard_map/ppermute | solution.py:46
  84.1 25.4 %collective-permute-start.20 = (bf16[256,2176]{1,0:T(8,128)(2,1)S(1)}, bf16[256,2176]{1,0:T(8,128)(2,1)S(1)}, u32[]{:S(2)}, u32[]{:S(2)}) collective-permute-start(bf16[256,2176]{1,0:T(8,128)(2,1)S(1)} %constant_dynamic-update-slice_fusion.2.near_ref), channel_id=1, source_target_pairs={{0,2},{1,3},{2,0},{3,1},{4,6},{5,7},{6,4},{7,5},{8,10},{9,11},{10,... | collective-permute-start | bytes 3342344 | tf_op jit(solution)/shard_map/ppermute | solution.py:168
  90.4 25.4 %collective-permute-start.31 = (bf16[128,2176]{1,0:T(8,128)(2,1)S(1)}, bf16[128,2176]{1,0:T(8,128)(2,1)S(1)}, u32[]{:S(2)}, u32[]{:S(2)}) collective-permute-start(bf16[128,2176]{1,0:T(8,128)(2,1)S(1)} %constant_dynamic-update-slice_fusion.5.near_ref), channel_id=1, source_target_pairs={{16,0},{0,16},{17,1},{1,17},{18,2},{2,18},{19,3},{3,19},{20,4},{4,... | collective-permute-start | bytes 1671176 | tf_op jit(solution)/shard_map/ppermute | solution.py:46
  90.9 14.6 %collective-permute-start.30 = (bf16[128,2176]{1,0:T(8,128)(2,1)S(1)}, bf16[128,2176]{1,0:T(8,128)(2,1)S(1)}, u32[]{:S(2)}, u32[]{:S(2)}) collective-permute-start(bf16[128,2176]{1,0:T(8,128)(2,1)S(1)} %constant_dynamic-update-slice_fusion.5.near_ref), channel_id=1, source_target_pairs={{0,2},{1,3},{2,0},{3,1},{4,6},{5,7},{6,4},{7,5},{8,10},{9,11},{10,... | collective-permute-start | bytes 1671176 | tf_op jit(solution)/shard_map/ppermute | solution.py:168
  105.6 10.3 %collective-permute-start.32 = (bf16[128,2176]{1,0:T(8,128)(2,1)S(1)}, bf16[128,2176]{1,0:T(8,128)(2,1)S(1)}, u32[]{:S(2)}, u32[]{:S(2)}) collective-permute-start(bf16[128,2176]{1,0:T(8,128)(2,1)S(1)} %collective-permute-done.30.far_ref), channel_id=1, source_target_pairs={{16,0},{0,16},{17,1},{1,17},{18,2},{2,18},{19,3},{3,19},{20,4},{4,... | collective-permute-start | bytes 1671176 | tf_op jit(solution)/shard_map/ppermute | solution.py:46
  109.4 10.3 %collective-permute-start.34 = (bf16[4,64,1024]{2,1,0:T(8,128)(2,1)S(1)}, bf16[4,64,1024]{2,1,0:T(8,128)(2,1)S(1)}, u32[]{:S(2)}, u32[]{:S(2)}) collective-permute-start(bf16[4,64,1024]{2,1,0:T(8,128)(2,1)S(1)} %get-tuple-element.39), channel_id=1, source_target_pairs={{16,0},{0,16},{17,1},{1,17},{18,2},{2,18},{19,3},{3,19},{20,4},{4,... | collective-permute-start | bytes 1572872 | tf_op jit(solution)/shard_map/ppermute | solution.py:46
  109.5 10.6 %collective-permute-start.22 = (bf16[256,2176]{1,0:T(8,128)(2,1)S(1)}, bf16[256,2176]{1,0:T(8,128)(2,1)S(1)}, u32[]{:S(2)}, u32[]{:S(2)}) collective-permute-start(bf16[256,2176]{1,0:T(8,128)(2,1)S(1)} %collective-permute-done.20.far_ref), channel_id=1, source_target_pairs={{16,0},{0,16},{17,1},{1,17},{18,2},{2,18},{19,3},{3,19},{20,4},{4,... | collective-permute-start | bytes 3342344 | tf_op jit(solution)/shard_map/ppermute | solution.py:46
  115.7 15.0 %collective-permute-start.13 = (bf16[4,64,1024]{2,1,0:T(8,128)(2,1)S(1)}, bf16[4,64,1024]{2,1,0:T(8,128)(2,1)S(1)}, u32[]{:S(2)}, u32[]{:S(2)}) collective-permute-start(bf16[4,64,1024]{2,1,0:T(8,128)(2,1)S(1)} %get-tuple-element.28), channel_id=1, source_target_pairs={{16,0},{0,16},{17,1},{1,17},{18,2},{2,18},{19,3},{3,19},{20,4},{4,... | collective-permute-start | bytes 1572872 | tf_op jit(solution)/shard_map/ppermute | solution.py:46
  115.9 12.3 %collective-permute-start.24 = (bf16[4,128,1024]{2,1,0:T(8,128)(2,1)S(1)}, bf16[4,128,1024]{2,1,0:T(8,128)(2,1)S(1)}, u32[]{:S(2)}, u32[]{:S(2)}) collective-permute-start(bf16[4,128,1024]{2,1,0:T(8,128)(2,1)S(1)} %get-tuple-element.34), channel_id=1, source_target_pairs={{16,0},{0,16},{17,1},{1,17},{18,2},{2,18},{19,3},{3,19},{20,4},{4,... | collective-permute-start | bytes 3145736 | tf_op jit(solution)/shard_map/ppermute | solution.py:46
  126.6 9.2 %collective-permute-start.35 = (bf16[2,2,64,1024]{3,2,1,0:T(8,128)(2,1)S(1)}, bf16[2,2,64,1024]{3,2,1,0:T(8,128)(2,1)S(1)}, u32[]{:S(2)}, u32[]{:S(2)}) collective-permute-start(bf16[2,2,64,1024]{3,2,1,0:T(8,128)(2,1)S(1)} %pad_maximum_fusion.5), channel_id=1, source_target_pairs={{0,2},{1,3},{2,0},{3,1},{4,6},{5,7},{6,4},{7,5},{8,10},{9,11},{10,... | collective-permute-start | bytes 1572872 | tf_op jit(solution)/shard_map/ppermute | solution.py:168
  129.2 20.7 %collective-permute-start.25 = (bf16[2,2,128,1024]{3,2,1,0:T(8,128)(2,1)S(1)}, bf16[2,2,128,1024]{3,2,1,0:T(8,128)(2,1)S(1)}, u32[]{:S(2)}, u32[]{:S(2)}) collective-permute-start(bf16[2,2,128,1024]{3,2,1,0:T(8,128)(2,1)S(1)} %pad_maximum_fusion), channel_id=1, source_target_pairs={{0,2},{1,3},{2,0},{3,1},{4,6},{5,7},{6,4},{7,5},{8,10},{9,11},{10,... | collective-permute-start | bytes 3145736 | tf_op jit(solution)/shard_map/ppermute | solution.py:168
  131.0 27.6 %collective-permute-start.15 = (bf16[2,2,64,1024]{3,2,1,0:T(8,128)(2,1)S(1)}, bf16[2,2,64,1024]{3,2,1,0:T(8,128)(2,1)S(1)}, u32[]{:S(2)}, u32[]{:S(2)}) collective-permute-start(bf16[2,2,64,1024]{3,2,1,0:T(8,128)(2,1)S(1)} %pad_maximum_fusion.3), channel_id=1, source_target_pairs={{0,2},{1,3},{2,0},{3,1},{4,6},{5,7},{6,4},{7,5},{8,10},{9,11},{10,... | collective-permute-start | bytes 1572872 | tf_op jit(solution)/shard_map/ppermute | solution.py:168
  136.1 24.3 %collective-permute-start.36 = (bf16[2,64,1024]{2,1,0:T(8,128)(2,1)S(1)}, bf16[2,64,1024]{2,1,0:T(8,128)(2,1)S(1)}, u32[]{:S(2)}, u32[]{:S(2)}) collective-permute-start(bf16[2,64,1024]{2,1,0:T(8,128)(2,1)S(1)} %pad_maximum_fusion.8), channel_id=1, source_target_pairs={{0,1},{1,0},{2,3},{3,2},{4,5},{5,4},{6,7},{7,6},{8,9},{9,8},{10,11... | collective-permute-start | bytes 786440 | tf_op jit(solution)/shard_map/ppermute | solution.py:168
  150.5 17.1 %collective-permute-start.26 = (bf16[2,128,1024]{2,1,0:T(8,128)(2,1)S(1)}, bf16[2,128,1024]{2,1,0:T(8,128)(2,1)S(1)}, u32[]{:S(2)}, u32[]{:S(2)}) collective-permute-start(bf16[2,128,1024]{2,1,0:T(8,128)(2,1)S(1)} %pad_maximum_fusion.4), channel_id=1, source_target_pairs={{0,1},{1,0},{2,3},{3,2},{4,5},{5,4},{6,7},{7,6},{8,9},{9,8},{10,11... | collective-permute-start | bytes 1572872 | tf_op jit(solution)/shard_map/ppermute | solution.py:168
  158.8 13.8 %collective-permute-start.16 = (bf16[2,64,1024]{2,1,0:T(8,128)(2,1)S(1)}, bf16[2,64,1024]{2,1,0:T(8,128)(2,1)S(1)}, u32[]{:S(2)}, u32[]{:S(2)}) collective-permute-start(bf16[2,64,1024]{2,1,0:T(8,128)(2,1)S(1)} %pad_maximum_fusion.6), channel_id=1, source_target_pairs={{0,1},{1,0},{2,3},{3,2},{4,5},{5,4},{6,7},{7,6},{8,9},{9,8},{10,11... | collective-permute-start | bytes 786440 | tf_op jit(solution)/shard_map/ppermute | solution.py:168
  160.5 18.0 %collective-permute-start.37 = (bf16[128,1024]{1,0:T(8,128)(2,1)S(1)}, bf16[128,1024]{1,0:T(8,128)(2,1)S(1)}, u32[]{:S(2)}, u32[]{:S(2)}) collective-permute-start(bf16[128,1024]{1,0:T(8,128)(2,1)S(1)} %pad_maximum_fusion.9), channel_id=1, source_target_pairs={{0,8},{1,9},{2,10},{3,11},{4,12},{5,13},{6,14},{7,15},{8,0},{9,1},... | collective-permute-start | bytes 786440 | tf_op jit(solution)/shard_map/ppermute | solution.py:39
  168.5 15.8 %collective-permute-start.38 = (bf16[128,1024]{1,0:T(8,128)(2,1)}, bf16[128,1024]{1,0:T(8,128)(2,1)S(1)}, u32[]{:S(2)}, u32[]{:S(2)}) collective-permute-start(bf16[128,1024]{1,0:T(8,128)(2,1)} %pad_maximum_fusion.10), channel_id=1, source_target_pairs={{0,12},{1,13},{2,14},{3,15},{4,0},{5,1},{6,2},{7,3},{8,4},{9,5},{1... | collective-permute-start | bytes 786440 | tf_op jit(solution)/shard_map/ppermute | solution.py:39
  169.7 14.7 %collective-permute-start.27 = (bf16[128,1024]{1,0:T(8,128)(2,1)}, bf16[128,1024]{1,0:T(8,128)(2,1)S(1)}, u32[]{:S(2)}, u32[]{:S(2)}) collective-permute-start(bf16[128,1024]{1,0:T(8,128)(2,1)} %pad_maximum_fusion.7), channel_id=1, source_target_pairs={{0,4},{1,5},{2,6},{3,7},{4,8},{5,9},{6,10},{7,11},{8,12},{9,13},{1... | collective-permute-start | bytes 786440 | tf_op jit(solution)/shard_map/ppermute | solution.py:39
  (20 other events, 247.7 us)

commit v4 on v3

--- a/solution.py
+++ b/solution.py
@@ -213,21 +213,29 @@
     return block.astype(jnp.bfloat16)
 
 
-def plane_scatter(totals):
-    sent = narrow(jnp.stack([total[2:4] for total in totals]))
-    got = crossed(sent, False)
-    totals = [total[0:2] + wide(got[i]) for i, total in enumerate(totals)]
-    sent = narrow(jnp.stack([total[1] for total in totals]))
-    got = crossed(sent, True)
-    return [total[0] + wide(got[i]) for i, total in enumerate(totals)]
-
-
-def expert_group(place, near, far, weights, experts, cores):
+def second_share(totals):
+    return narrow(jnp.stack([total[2:4] for total in totals]))
+
+
+def first_share(totals):
+    return narrow(jnp.stack([total[1] for total in totals]))
+
+
+def merged(totals, got, count):
+    return [total[0:count] + wide(got[i]) for i, total in enumerate(totals)]
+
+
+def expert_outputs(place, near, far, weights, experts, cores, waits):
     outs = []
     for ahead in range(cores):
         near_rows = from_core(near, ahead) if ahead else near
         far_rows = from_core(far, ahead) if ahead else far
+        near_rows = after(near_rows, *outs[-1:], *waits.get(ahead, []))
         outs.append(run_expert(place, near_rows, far_rows, *weights, experts, cores, ahead))
+    return outs
+
+
+def core_totals(outs, cores):
     totals = []
     for rows_of in range(cores):
         total = wide(outs[rows_of][0])
@@ -235,7 +243,7 @@
             sent = outs[(rows_of + ahead) % cores][ahead]
             total = total + wide(from_core(sent, cores - ahead))
         totals.append(total)
-    return plane_scatter(totals)
+    return totals
 
 
 def on_device(
@@ -314,38 +322,46 @@
         [norm_gain[None, :], lanes, *addends],
     )
     weights = (w_gate[0].T, w_up[0].T, w_down[0])
-    came = {0: payload}
-    for ahead in range(1, planes):
-        came[ahead] = from_plane(payload, ahead)
     if planes <= 4:
         groups = [[0]] + [sorted({i, planes - i}) for i in range(1, planes // 2 + 1)]
     else:
         groups = [[0]] + [list(range(i, min(i + 8, planes))) for i in range(1, planes, 8)]
+    nears, fars = [], []
+    for number, group in enumerate(groups):
+        sent = after(payload, nears[0]) if number > 1 else payload
+        column = jnp.concatenate([from_plane(sent, ahead) if ahead else sent for ahead in group])
+        if number > 1:
+            column = after(column, nears[-1])
+        nears.append(jnp.concatenate([column, crossed(column, True)]))
+        fars.append(crossed(nears[-1], False))
+    weights = (w_gate[0].T, w_up[0].T, w_down[0])
+    run = functools.partial(
+        expert_outputs, place, weights=weights, experts=experts, cores=cores
+    )
+    outs = run(nears[0], fars[0], waits={})
+    own_totals = core_totals(outs, cores)
+    got = crossed(after(second_share(own_totals), nears[-1]), False)
+    own_totals = merged(own_totals, got, 2)
+    own_got = crossed(first_share(own_totals), True)
+    totals, sents = [], []
+    for number in range(1, len(groups)):
+        waits = {0: [outs]}
+        if number == len(groups) - 1:
+            waits = {0: [outs, got], cores - 1: [own_got, *sents]}
+        outs = run(nears[number], fars[number], waits=waits)
+        totals.append(core_totals(outs, cores))
+        sents.append(second_share(totals[-1]))
+    gots = [crossed(sent, False) for sent in sents]
+    totals = [merged(*pair, 2) for pair in zip(totals, gots, strict=True)]
+    gots = [crossed(first_share(pair), True) for pair in totals]
     results = {}
-    near_before = None
-    done_before = None
-    held = []
-    for number, group in enumerate(groups):
-        column = jnp.concatenate([came[ahead] for ahead in group])
-        if near_before is not None:
-            if number > 1:
-                column = after(column, near_before)
-            if planes > 4:
-                column = after(column, done_before)
-        near = jnp.concatenate([column, crossed(column, True)])
-        far = crossed(near, False)
-        near_before = near
-        if planes > 4:
-            done_before = expert_group(place, near, far, weights, experts, cores)
-            held.append(done_before)
-        else:
-            held.append((near, far))
-    if planes <= 4:
-        held = [expert_group(place, near, far, weights, experts, cores) for near, far in held]
-    for group, summed in zip(groups, held, strict=True):
+    for group, pair, came in zip(
+        groups, [own_totals, *totals], [own_got, *gots], strict=True
+    ):
+        rows_of = merged([total[0] for total in pair], came, None)
         for i, ahead in enumerate(group):
             results[ahead] = jnp.concatenate(
-                [total[i * part_rows : (i + 1) * part_rows] for total in summed]
+                [rows[i * part_rows : (i + 1) * part_rows] for rows in rows_of]
             )
     moe = results[0]
     for ahead in range(1, planes):

time: 186 us -> 172 us (0.925)
  waiting for transfers between devices: 80.5 us -> 70.7 us
  starting transfers between devices: 54.4 us -> 51.5 us
    ppermute x12, waiting for transfers between devices: 47.2 us -> 39.5 us  [crossed(): return lax.ppermute(block, ('tok', 'blk'), route)]
    ppermute x3, waiting for transfers between devices: 8.48 us -> 4.43 us  [from_plane(): lax.ppermute(block, 'blk', [((i + PLANE * ahead) % count, i) for i in ran...]
  transfers between devices with their start and end apart: 39 -> 39, of which waited for: 18 -> 21; matrix products, arithmetic and copies ran while one was open for 7% -> 7% of each run, Pallas kernels for 14% -> 15%
where the time goes in v4:
time: 172 us
  waiting for transfers between devices  70.7 us (41%)
  starting transfers between devices  51.5 us (30%)
  Pallas kernels  29.7 us (17%)
  local copies, waits for them, and re-layouts  10.4 us (6%)
  other arithmetic  8 us (5%)
    ppermute x12, waiting for transfers between devices, crossed(): return lax.ppermute(block, ('tok', 'blk'), route)  39.5 us
    pallas_call x10, Pallas kernels, local_call(): pl.pallas_call(body, in_specs=[scalar] * len(scalars) + [whole] * len(arr...  29.7 us
    ppermute x12, starting transfers between devices, crossed(): return lax.ppermute(block, ('tok', 'blk'), route)  17.3 us
    ppermute x3, waiting for transfers between devices, to_plane(): lax.ppermute(block, 'blk', [(i, (i + PLANE * ahead) % count) for i in ran...  13.3 us
    ppermute x3, starting transfers between devices, to_plane(): lax.ppermute(block, 'blk', [(i, (i + PLANE * ahead) % count) for i in ran...  9.85 us
    ppermute x2, starting transfers between devices, next_plane(): lax.ppermute(block, 'blk', [(i, i + PLANE) for i in range(count - PLANE)])  8.43 us
    ppermute x6, starting transfers between devices, flipped(): lax.ppermute(block, 'blk', [(i, i ^ mask) for i in range(lax.axis_size('b...  8.21 us
    ppermute x6, waiting for transfers between devices, flipped(): lax.ppermute(block, 'blk', [(i, i ^ mask) for i in range(lax.axis_size('b...  8.08 us
  transfers between devices with their start and end apart: 39, of which 21 were waited for; matrix products, arithmetic and copies ran while one was open for 7% of the time, Pallas kernels for 15%

profile of v4, /device:TPU:0, one launch (start us, length us, event | category | flops | bytes accessed | tf_op | source)
XLA Modules:
  0.0 171.6 jit_solution(9891830193766270374)
XLA Ops:
  4.5 4.9 %collective-permute-start = (bf16[128,1024]{1,0:T(8,128)(2,1)S(1)}, bf16[128,1024]{1,0:T(8,128)(2,1)S(1)}, u32[]{:S(2)}, u32[]{:S(2)}) collective-permute-start(bf16[128,1024]{1,0:T(8,128)(2,1)S(1)} %get-tuple-element.29.rest_0_), channel_id=1, source_target_pairs={{0,4},{1,5},{2,6},{3,7},{4,8},{5,9},{6,10},{7,11},{8,12},{9,13},{1... | collective-permute-start | bytes 786440 | tf_op jit(solution)/shard_map/ppermute | solution.py:27
  9.4 3.5 %collective-permute-start.4 = (bf16[128,1024]{1,0:T(8,128)(2,1)}, bf16[128,1024]{1,0:T(8,128)(2,1)S(1)}, u32[]{:S(2)}, u32[]{:S(2)}) collective-permute-start(bf16[128,1024]{1,0:T(8,128)(2,1)} %rest_0_), channel_id=1, source_target_pairs={{0,4},{1,5},{2,6},{3,7},{4,8},{5,9},{6,10},{7,11},{8,12},{9,13},{1... | collective-permute-start | bytes 786440 | tf_op jit(solution)/shard_map/ppermute | solution.py:27
  13.7 2.4 %collective-permute-done.rest_1_ = bf16[128,1024]{1,0:T(8,128)(2,1)S(1)} collective-permute-done((bf16[128,1024]{1,0:T(8,128)(2,1)S(1)}, bf16[128,1024]{1,0:T(8,128)(2,1)S(1)}, u32[]{:S(2)}, u32[]{:S(2)}) %collective-permute-start) | collective-permute-done | bytes 262176 | tf_op jit(solution)/shard_map/ppermute | solution.py:27
  16.9 2.4 %collective-permute-start.3 = (bf16[128,1024]{1,0:T(8,128)(2,1)S(1)}, bf16[128,1024]{1,0:T(8,128)(2,1)S(1)}, u32[]{:S(2)}, u32[]{:S(2)}) collective-permute-start(bf16[128,1024]{1,0:T(8,128)(2,1)S(1)} %get-tuple-element.71), channel_id=1, source_target_pairs={{0,3},{1,2},{2,1},{3,0},{4,7},{5,6},{6,5},{7,4},{8,11},{9,10},{10,... | collective-permute-start | bytes 786440 | tf_op jit(solution)/shard_map/ppermute | solution.py:22
  22.2 2.4 %collective-permute-start.7 = (bf16[128,1024]{1,0:T(8,128)(2,1)}, bf16[128,1024]{1,0:T(8,128)(2,1)S(1)}, u32[]{:S(2)}, u32[]{:S(2)}) collective-permute-start(bf16[128,1024]{1,0:T(8,128)(2,1)} %get-tuple-element.68), channel_id=1, source_target_pairs={{0,3},{1,2},{2,1},{3,0},{4,7},{5,6},{6,5},{7,4},{8,11},{9,10},{10,... | collective-permute-start | bytes 786440 | tf_op jit(solution)/shard_map/ppermute | solution.py:22
  26.8 1.8 %collective-permute-start.5 = (bf16[128,1024]{1,0:T(8,128)(2,1)}, bf16[128,1024]{1,0:T(8,128)(2,1)S(1)}, u32[]{:S(2)}, u32[]{:S(2)}) collective-permute-start(bf16[128,1024]{1,0:T(8,128)(2,1)} %get-tuple-element.70), channel_id=1, source_target_pairs={{0,1},{1,0},{2,3},{3,2},{4,5},{5,4},{6,7},{7,6},{8,9},{9,8},{10,11... | collective-permute-start | bytes 786440 | tf_op jit(solution)/shard_map/ppermute | solution.py:22
  29.6 2.7 %scatter_fusion = bf16[8,16,2,1024]{3,1,2,0:T(8,128)(2,1)} fusion(bf16[8,16,2,1024]{3,1,2,0:T(8,128)(2,1)} %broadcast_in_dim.31, s32[8]{0:T(128)S(1)} %compare_select_fusion, bf16[8,16,2,1024]{3,1,2,0:T(8,128)(2,1)} %pad_maximum_fusion.2), kind=kCustom, calls=%fused_computation | custom fusion | bytes 1572896 | tf_op jit(solution)/shard_map/scatter | solution.py:301
  32.3 3.0 %collective-permute-done.2.rest_3_ = bf16[128,1024]{1,0:T(8,128)(2,1)S(1)} collective-permute-done((bf16[128,1024]{1,0:T(8,128)(2,1)}, bf16[128,1024]{1,0:T(8,128)(2,1)S(1)}, u32[]{:S(2)}, u32[]{:S(2)}) %collective-permute-start.2) | collective-permute-done | bytes 262176 | tf_op jit(solution)/shard_map/ppermute | solution.py:22
  35.3 1.9 %shard_map.141.prob_ref = bf16[8,128,640]{2,1,0:T(8,128)(2,1)S(1)} custom-call(s32[2]{0:T(128)S(1)} %pad_add_fusion.place_ref, s32[8]{0:T(128)S(1)} %copy-done.10, bf16[128,1024]{1,0:T(8,128)(2,1)S(1)} %get-tuple-element.28.q_ref, bf16[128,1024]{1,0:T(8,128)(2,1)S(1)} %get-tuple-element.29.rest_0_, bf16[128,1024]{1,0:T(8,128)(2,1)S(1)} %collective-permute-done.rest_1_, ...), custom_call_target="tpu_custom_call" | custom-call | flops 167772160 | bytes 2883584 | tf_op jit(solution)/shard_map/pallas_call | solution.py:140
  38.0 2.6 %collective-permute-done.6.rest_3_ = bf16[128,1024]{1,0:T(8,128)(2,1)S(1)} collective-permute-done((bf16[128,1024]{1,0:T(8,128)(2,1)}, bf16[128,1024]{1,0:T(8,128)(2,1)S(1)}, u32[]{:S(2)}, u32[]{:S(2)}) %collective-permute-start.6) | collective-permute-done | bytes 262176 | tf_op jit(solution)/shard_map/ppermute | solution.py:22
  40.7 2.2 %copy-done.3 = bf16[1024,2048]{1,0:T(8,128)(2,1)S(1)} copy-done((bf16[1024,2048]{1,0:T(8,128)(2,1)S(1)}, bf16[1024,2048]{1,0:T(8,128)(2,1)}, u32[]{:S(2)}) %copy-start.3) | copy-done | bytes 4194328
  42.9 1.7 shard_map.142.rest_0_
  44.7 2.6 %collective-permute-done.8.rest_1_ = f32[128,2048]{1,0:T(8,128)S(1)} collective-permute-done((f32[128,2048]{1,0:T(8,128)S(1)}, f32[128,2048]{1,0:T(8,128)S(1)}, u32[]{:S(2)}, u32[]{:S(2)}) %collective-permute-start.8) | collective-permute-done | bytes 1048608 | tf_op jit(solution)/shard_map/ppermute | solution.py:46
  48.1 2.5 %collective-permute-start.17 = (bf16[64,2176]{1,0:T(8,128)(2,1)S(1)}, bf16[64,2176]{1,0:T(8,128)(2,1)S(1)}, u32[]{:S(2)}, u32[]{:S(2)}) collective-permute-start(bf16[64,2176]{1,0:T(8,128)(2,1)S(1)} %get-tuple-element.39), channel_id=1, source_target_pairs={{12,0},{13,1},{14,2},{15,3},{0,4},{1,5},{2,6},{3,7},{4,8},{5,9},{6... | collective-permute-start | bytes 835592 | tf_op jit(solution)/shard_map/ppermute | solution.py:32
  50.7 2.3 %collective-permute-start.16 = (bf16[64,2176]{1,0:T(8,128)(2,1)S(1)}, bf16[64,2176]{1,0:T(8,128)(2,1)S(1)}, u32[]{:S(2)}, u32[]{:S(2)}) collective-permute-start(bf16[64,2176]{1,0:T(8,128)(2,1)S(1)} %get-tuple-element.39), channel_id=1, source_target_pairs={{4,0},{5,1},{6,2},{7,3},{8,4},{9,5},{10,6},{11,7},{12,8},{13,9},{1... | collective-permute-start | bytes 835592 | tf_op jit(solution)/shard_map/ppermute | solution.py:32
  54.5 5.0 %collective-permute-done.9 = bf16[64,2176]{1,0:T(8,128)(2,1)S(1)} collective-permute-done((bf16[64,2176]{1,0:T(8,128)(2,1)S(1)}, bf16[64,2176]{1,0:T(8,128)(2,1)S(1)}, u32[]{:S(2)}, u32[]{:S(2)}) %collective-permute-start.9) | collective-permute-done | bytes 278560 | tf_op jit(solution)/shard_map/ppermute | solution.py:168
  61.9 3.2 %collective-permute-done.16 = bf16[64,2176]{1,0:T(8,128)(2,1)S(1)} collective-permute-done((bf16[64,2176]{1,0:T(8,128)(2,1)S(1)}, bf16[64,2176]{1,0:T(8,128)(2,1)S(1)}, u32[]{:S(2)}, u32[]{:S(2)}) %collective-permute-start.16) | collective-permute-done | bytes 278560 | tf_op jit(solution)/shard_map/ppermute | solution.py:32
  66.8 4.4 %collective-permute-done.10.far_ref = bf16[128,2176]{1,0:T(8,128)(2,1)S(1)} collective-permute-done((bf16[128,2176]{1,0:T(8,128)(2,1)S(1)}, bf16[128,2176]{1,0:T(8,128)(2,1)S(1)}, u32[]{:S(2)}, u32[]{:S(2)}) %collective-permute-start.10) | collective-permute-done | bytes 557088 | tf_op jit(solution)/shard_map/ppermute | solution.py:168
  71.1 3.6 %collective-permute-done.18 = bf16[128,2176]{1,0:T(8,128)(2,1)S(1)} collective-permute-done((bf16[128,2176]{1,0:T(8,128)(2,1)S(1)}, bf16[128,2176]{1,0:T(8,128)(2,1)S(1)}, u32[]{:S(2)}, u32[]{:S(2)}) %collective-permute-start.18) | collective-permute-done | bytes 557088 | tf_op jit(solution)/shard_map/ppermute | solution.py:168
  79.2 3.2 %shard_map.144 = (bf16[4,64,1024]{2,1,0:T(8,128)(2,1)S(1)}, bf16[4,64,1024]{2,1,0:T(8,128)(2,1)S(1)}) custom-call(s32[2]{0:T(128)S(1)} %pad_add_fusion.place_ref, bf16[128,2176]{1,0:T(8,128)(2,1)S(1)} %constant_dynamic-update-slice_fusion.near_ref, bf16[128,2176]{1,0:T(8,128)(2,1)S(1)} %collective-permute-done.10.far_ref, bf16[704,2048]{1,0:T(8,128)(2,1)S(1)} %bitcast.82, ...), custom_call_target="tpu_custom_call" | custom-call | flops 2214592512 | bytes 10813440 | tf_op jit(solution)/shard_map/pallas_call | solution.py:140
  83.0 3.2 %shard_map.145 = (bf16[4,64,1024]{2,1,0:T(8,128)(2,1)S(1)}, bf16[4,64,1024]{2,1,0:T(8,128)(2,1)S(1)}) custom-call(s32[2]{0:T(128)S(1)} %pad_add_fusion.place_ref, bf16[128,2176]{1,0:T(8,128)(2,1)S(1)} %collective-permute-done.11.near_ref, bf16[128,2176]{1,0:T(8,128)(2,1)S(1)} %collective-permute-done.12.far_ref, bf16[704,2048]{1,0:T(8,128)(2,1)S(1)} %bitcast.83, ...), custom_call_target="tpu_custom_call" | custom-call | flops 2214592512 | bytes 10813440 | tf_op jit(solution)/shard_map/pallas_call | solution.py:140
  88.9 4.4 %collective-permute-done.22.far_ref = bf16[256,2176]{1,0:T(8,128)(2,1)S(1)} collective-permute-done((bf16[256,2176]{1,0:T(8,128)(2,1)S(1)}, bf16[256,2176]{1,0:T(8,128)(2,1)S(1)}, u32[]{:S(2)}, u32[]{:S(2)}) %collective-permute-start.22) | collective-permute-done | bytes 1114144 | tf_op jit(solution)/shard_map/ppermute | solution.py:168
  95.2 5.7 %shard_map.146 = (bf16[4,128,1024]{2,1,0:T(8,128)(2,1)S(1)}, bf16[4,128,1024]{2,1,0:T(8,128)(2,1)S(1)}) custom-call(s32[2]{0:T(128)S(1)} %pad_add_fusion.place_ref, bf16[256,2176]{1,0:T(8,128)(2,1)S(1)} %constant_dynamic-update-slice_fusion.2.near_ref, bf16[256,2176]{1,0:T(8,128)(2,1)S(1)} %collective-permute-done.22.far_ref, ...), custom_call_target="tpu_custom_call" | custom-call | flops 4429185024 | bytes 12976128 | tf_op jit(solution)/shard_map/pallas_call | solution.py:140
  101.7 5.8 %shard_map.147 = (bf16[4,128,1024]{2,1,0:T(8,128)(2,1)S(1)}, bf16[4,128,1024]{2,1,0:T(8,128)(2,1)S(1)}) custom-call(s32[2]{0:T(128)S(1)} %pad_add_fusion.place_ref, bf16[256,2176]{1,0:T(8,128)(2,1)S(1)} %collective-permute-done.23.near_ref, bf16[256,2176]{1,0:T(8,128)(2,1)S(1)} %collective-permute-done.24.far_ref, bf16[704,2048]{1,0:T(8,128)(2,1)S(1)} %bitcast.85, ...), custom_call_target="tpu_custom_call" | custom-call | flops 4429185024 | bytes 12976128 | tf_op jit(solution)/shard_map/pallas_call | solution.py:140
  109.6 3.2 %shard_map.148 = (bf16[4,64,1024]{2,1,0:T(8,128)(2,1)S(1)}, bf16[4,64,1024]{2,1,0:T(8,128)(2,1)S(1)}) custom-call(s32[2]{0:T(128)S(1)} %pad_add_fusion.place_ref, bf16[128,2176]{1,0:T(8,128)(2,1)S(1)} %constant_dynamic-update-slice_fusion.5.near_ref, bf16[128,2176]{1,0:T(8,128)(2,1)S(1)} %collective-permute-done.30.far_ref, bf16[704,2048]{1,0:T(8,128)(2,1)S(1)} %bitcast.86, ...), custom_call_target="tpu_custom_call" | custom-call | flops 2214592512 | bytes 10813440 | tf_op jit(solution)/shard_map/pallas_call | solution.py:140
  114.5 3.2 %shard_map.149 = (bf16[4,64,1024]{2,1,0:T(8,128)(2,1)S(1)}, bf16[4,64,1024]{2,1,0:T(8,128)(2,1)S(1)}) custom-call(s32[2]{0:T(128)S(1)} %pad_add_fusion.place_ref, bf16[128,2176]{1,0:T(8,128)(2,1)S(1)} %collective-permute-done.31.near_ref, bf16[128,2176]{1,0:T(8,128)(2,1)S(1)} %collective-permute-done.32.far_ref, bf16[704,2048]{1,0:T(8,128)(2,1)S(1)} %bitcast.87, ...), custom_call_target="tpu_custom_call" | custom-call | flops 2214592512 | bytes 10813440 | tf_op jit(solution)/shard_map/pallas_call | solution.py:140
  121.3 16.9 %collective-permute-done.35 = bf16[2,2,64,1024]{3,2,1,0:T(8,128)(2,1)S(1)} collective-permute-done((bf16[2,2,64,1024]{3,2,1,0:T(8,128)(2,1)S(1)}, bf16[2,2,64,1024]{3,2,1,0:T(8,128)(2,1)S(1)}, u32[]{:S(2)}, u32[]{:S(2)}) %collective-permute-start.35) | collective-permute-done | bytes 524320 | tf_op jit(solution)/shard_map/ppermute | solution.py:168
  141.1 3.8 %collective-permute-done.36 = bf16[2,64,1024]{2,1,0:T(8,128)(2,1)S(1)} collective-permute-done((bf16[2,64,1024]{2,1,0:T(8,128)(2,1)S(1)}, bf16[2,64,1024]{2,1,0:T(8,128)(2,1)S(1)}, u32[]{:S(2)}, u32[]{:S(2)}) %collective-permute-start.36) | collective-permute-done | bytes 262176 | tf_op jit(solution)/shard_map/ppermute | solution.py:168
  145.1 7.8 %collective-permute-start.37 = (bf16[128,1024]{1,0:T(8,128)(2,1)S(1)}, bf16[128,1024]{1,0:T(8,128)(2,1)S(1)}, u32[]{:S(2)}, u32[]{:S(2)}) collective-permute-start(bf16[128,1024]{1,0:T(8,128)(2,1)S(1)} %pad_maximum_fusion.9), channel_id=1, source_target_pairs={{0,8},{1,9},{2,10},{3,11},{4,12},{5,13},{6,14},{7,15},{8,0},{9,1},... | collective-permute-start | bytes 786440 | tf_op jit(solution)/shard_map/ppermute | solution.py:39
  157.3 2.4 %collective-permute-done.37 = bf16[128,1024]{1,0:T(8,128)(2,1)S(1)} collective-permute-done((bf16[128,1024]{1,0:T(8,128)(2,1)S(1)}, bf16[128,1024]{1,0:T(8,128)(2,1)S(1)}, u32[]{:S(2)}, u32[]{:S(2)}) %collective-permute-start.37) | collective-permute-done | bytes 262176 | tf_op jit(solution)/shard_map/ppermute | solution.py:39
  159.7 6.7 %collective-permute-done.38 = bf16[128,1024]{1,0:T(8,128)(2,1)S(1)} collective-permute-done((bf16[128,1024]{1,0:T(8,128)(2,1)S(1)}, bf16[128,1024]{1,0:T(8,128)(2,1)S(1)}, u32[]{:S(2)}, u32[]{:S(2)}) %collective-permute-start.38) | collective-permute-done | bytes 262176 | tf_op jit(solution)/shard_map/ppermute | solution.py:39
  166.4 4.1 %collective-permute-done.29 = bf16[128,1024]{1,0:T(8,128)(2,1)S(1)} collective-permute-done((bf16[128,1024]{1,0:T(8,128)(2,1)}, bf16[128,1024]{1,0:T(8,128)(2,1)S(1)}, u32[]{:S(2)}, u32[]{:S(2)}) %collective-permute-start.29) | collective-permute-done | bytes 262176 | tf_op jit(solution)/shard_map/ppermute | solution.py:39
  (142 shorter events, 44.7 us)
Async XLA Ops:
  4.5 11.6 %collective-permute-start = (bf16[128,1024]{1,0:T(8,128)(2,1)S(1)}, bf16[128,1024]{1,0:T(8,128)(2,1)S(1)}, u32[]{:S(2)}, u32[]{:S(2)}) collective-permute-start(bf16[128,1024]{1,0:T(8,128)(2,1)S(1)} %get-tuple-element.29.rest_0_), channel_id=1, source_target_pairs={{0,4},{1,5},{2,6},{3,7},{4,8},{5,9},{6,10},{7,11},{8,12},{9,13},{1... | collective-permute-start | bytes 786440 | tf_op jit(solution)/shard_map/ppermute | solution.py:27
  9.4 11.8 %collective-permute-start.4 = (bf16[128,1024]{1,0:T(8,128)(2,1)}, bf16[128,1024]{1,0:T(8,128)(2,1)S(1)}, u32[]{:S(2)}, u32[]{:S(2)}) collective-permute-start(bf16[128,1024]{1,0:T(8,128)(2,1)} %rest_0_), channel_id=1, source_target_pairs={{0,4},{1,5},{2,6},{3,7},{4,8},{5,9},{6,10},{7,11},{8,12},{9,13},{1... | collective-permute-start | bytes 786440 | tf_op jit(solution)/shard_map/ppermute | solution.py:27
  16.9 9.9 %collective-permute-start.3 = (bf16[128,1024]{1,0:T(8,128)(2,1)S(1)}, bf16[128,1024]{1,0:T(8,128)(2,1)S(1)}, u32[]{:S(2)}, u32[]{:S(2)}) collective-permute-start(bf16[128,1024]{1,0:T(8,128)(2,1)S(1)} %get-tuple-element.71), channel_id=1, source_target_pairs={{0,3},{1,2},{2,1},{3,0},{4,7},{5,6},{6,5},{7,4},{8,11},{9,10},{10,... | collective-permute-start | bytes 786440 | tf_op jit(solution)/shard_map/ppermute | solution.py:22
  20.2 15.1 %collective-permute-start.2 = (bf16[128,1024]{1,0:T(8,128)(2,1)}, bf16[128,1024]{1,0:T(8,128)(2,1)S(1)}, u32[]{:S(2)}, u32[]{:S(2)}) collective-permute-start(bf16[128,1024]{1,0:T(8,128)(2,1)} %get-tuple-element.72), channel_id=1, source_target_pairs={{0,2},{1,3},{2,0},{3,1},{4,6},{5,7},{6,4},{7,5},{8,10},{9,11},{10,... | collective-permute-start | bytes 786440 | tf_op jit(solution)/shard_map/ppermute | solution.py:22
  20.7 14.6 %collective-permute-start.1 = (bf16[128,1024]{1,0:T(8,128)(2,1)S(1)}, bf16[128,1024]{1,0:T(8,128)(2,1)S(1)}, u32[]{:S(2)}, u32[]{:S(2)}) collective-permute-start(bf16[128,1024]{1,0:T(8,128)(2,1)S(1)} %get-tuple-element.73), channel_id=1, source_target_pairs={{0,1},{1,0},{2,3},{3,2},{4,5},{5,4},{6,7},{7,6},{8,9},{9,8},{10,11... | collective-permute-start | bytes 786440 | tf_op jit(solution)/shard_map/ppermute | solution.py:22
  22.2 15.8 %collective-permute-start.7 = (bf16[128,1024]{1,0:T(8,128)(2,1)}, bf16[128,1024]{1,0:T(8,128)(2,1)S(1)}, u32[]{:S(2)}, u32[]{:S(2)}) collective-permute-start(bf16[128,1024]{1,0:T(8,128)(2,1)} %get-tuple-element.68), channel_id=1, source_target_pairs={{0,3},{1,2},{2,1},{3,0},{4,7},{5,6},{6,5},{7,4},{8,11},{9,10},{10,... | collective-permute-start | bytes 786440 | tf_op jit(solution)/shard_map/ppermute | solution.py:22
  24.7 16.0 %collective-permute-start.6 = (bf16[128,1024]{1,0:T(8,128)(2,1)}, bf16[128,1024]{1,0:T(8,128)(2,1)S(1)}, u32[]{:S(2)}, u32[]{:S(2)}) collective-permute-start(bf16[128,1024]{1,0:T(8,128)(2,1)} %get-tuple-element.69), channel_id=1, source_target_pairs={{0,2},{1,3},{2,0},{3,1},{4,6},{5,7},{6,4},{7,5},{8,10},{9,11},{10,... | collective-permute-start | bytes 786440 | tf_op jit(solution)/shard_map/ppermute | solution.py:22
  26.8 13.9 %collective-permute-start.5 = (bf16[128,1024]{1,0:T(8,128)(2,1)}, bf16[128,1024]{1,0:T(8,128)(2,1)S(1)}, u32[]{:S(2)}, u32[]{:S(2)}) collective-permute-start(bf16[128,1024]{1,0:T(8,128)(2,1)} %get-tuple-element.70), channel_id=1, source_target_pairs={{0,1},{1,0},{2,3},{3,2},{4,5},{5,4},{6,7},{7,6},{8,9},{9,8},{10,11... | collective-permute-start | bytes 786440 | tf_op jit(solution)/shard_map/ppermute | solution.py:22
  48.1 13.8 %collective-permute-start.17 = (bf16[64,2176]{1,0:T(8,128)(2,1)S(1)}, bf16[64,2176]{1,0:T(8,128)(2,1)S(1)}, u32[]{:S(2)}, u32[]{:S(2)}) collective-permute-start(bf16[64,2176]{1,0:T(8,128)(2,1)S(1)} %get-tuple-element.39), channel_id=1, source_target_pairs={{12,0},{13,1},{14,2},{15,3},{0,4},{1,5},{2,6},{3,7},{4,8},{5,9},{6... | collective-permute-start | bytes 835592 | tf_op jit(solution)/shard_map/ppermute | solution.py:32
  50.7 14.4 %collective-permute-start.16 = (bf16[64,2176]{1,0:T(8,128)(2,1)S(1)}, bf16[64,2176]{1,0:T(8,128)(2,1)S(1)}, u32[]{:S(2)}, u32[]{:S(2)}) collective-permute-start(bf16[64,2176]{1,0:T(8,128)(2,1)S(1)} %get-tuple-element.39), channel_id=1, source_target_pairs={{4,0},{5,1},{6,2},{7,3},{8,4},{9,5},{10,6},{11,7},{12,8},{13,9},{1... | collective-permute-start | bytes 835592 | tf_op jit(solution)/shard_map/ppermute | solution.py:32
  52.9 6.5 %collective-permute-start.9 = (bf16[64,2176]{1,0:T(8,128)(2,1)S(1)}, bf16[64,2176]{1,0:T(8,128)(2,1)S(1)}, u32[]{:S(2)}, u32[]{:S(2)}) collective-permute-start(bf16[64,2176]{1,0:T(8,128)(2,1)S(1)} %get-tuple-element.39), channel_id=1, source_target_pairs={{0,1},{1,0},{2,3},{3,2},{4,5},{5,4},{6,7},{7,6},{8,9},{9,8},{10,11... | collective-permute-start | bytes 835592 | tf_op jit(solution)/shard_map/ppermute | solution.py:168
  59.5 22.9 %collective-permute-start.11 = (bf16[128,2176]{1,0:T(8,128)(2,1)S(1)}, bf16[128,2176]{1,0:T(8,128)(2,1)S(1)}, u32[]{:S(2)}, u32[]{:S(2)}) collective-permute-start(bf16[128,2176]{1,0:T(8,128)(2,1)S(1)} %constant_dynamic-update-slice_fusion.near_ref), channel_id=1, source_target_pairs={{16,0},{0,16},{17,1},{1,17},{18,2},{2,18},{19,3},{3,19},{20,4},{4,... | collective-permute-start | bytes 1671176 | tf_op jit(solution)/shard_map/ppermute | solution.py:46
  59.6 11.5 %collective-permute-start.10 = (bf16[128,2176]{1,0:T(8,128)(2,1)S(1)}, bf16[128,2176]{1,0:T(8,128)(2,1)S(1)}, u32[]{:S(2)}, u32[]{:S(2)}) collective-permute-start(bf16[128,2176]{1,0:T(8,128)(2,1)S(1)} %constant_dynamic-update-slice_fusion.near_ref), channel_id=1, source_target_pairs={{0,2},{1,3},{2,0},{3,1},{4,6},{5,7},{6,4},{7,5},{8,10},{9,11},{10,... | collective-permute-start | bytes 1671176 | tf_op jit(solution)/shard_map/ppermute | solution.py:168
  61.1 16.4 %collective-permute-start.15 = (bf16[64,2176]{1,0:T(8,128)(2,1)S(1)}, bf16[64,2176]{1,0:T(8,128)(2,1)S(1)}, u32[]{:S(2)}, u32[]{:S(2)}) collective-permute-start(bf16[64,2176]{1,0:T(8,128)(2,1)S(1)} %get-tuple-element.39), channel_id=1, source_target_pairs={{8,0},{9,1},{10,2},{11,3},{12,4},{13,5},{14,6},{15,7},{0,8},{1,9},... | collective-permute-start | bytes 835592 | tf_op jit(solution)/shard_map/ppermute | solution.py:32
  65.1 9.6 %collective-permute-start.18 = (bf16[128,2176]{1,0:T(8,128)(2,1)S(1)}, bf16[128,2176]{1,0:T(8,128)(2,1)S(1)}, u32[]{:S(2)}, u32[]{:S(2)}) collective-permute-start(bf16[128,2176]{1,0:T(8,128)(2,1)S(1)} %pad_maximum_fusion.1), channel_id=1, source_target_pairs={{0,1},{1,0},{2,3},{3,2},{4,5},{5,4},{6,7},{7,6},{8,9},{9,8},{10,11... | collective-permute-start | bytes 1671176 | tf_op jit(solution)/shard_map/ppermute | solution.py:168
  71.1 11.8 %collective-permute-start.12 = (bf16[128,2176]{1,0:T(8,128)(2,1)S(1)}, bf16[128,2176]{1,0:T(8,128)(2,1)S(1)}, u32[]{:S(2)}, u32[]{:S(2)}) collective-permute-start(bf16[128,2176]{1,0:T(8,128)(2,1)S(1)} %collective-permute-done.10.far_ref), channel_id=1, source_target_pairs={{16,0},{0,16},{17,1},{1,17},{18,2},{2,18},{19,3},{3,19},{20,4},{4,... | collective-permute-start | bytes 1671176 | tf_op jit(solution)/shard_map/ppermute | solution.py:46
  74.8 18.6 %collective-permute-start.22 = (bf16[256,2176]{1,0:T(8,128)(2,1)S(1)}, bf16[256,2176]{1,0:T(8,128)(2,1)S(1)}, u32[]{:S(2)}, u32[]{:S(2)}) collective-permute-start(bf16[256,2176]{1,0:T(8,128)(2,1)S(1)} %constant_dynamic-update-slice_fusion.2.near_ref), channel_id=1, source_target_pairs={{0,2},{1,3},{2,0},{3,1},{4,6},{5,7},{6,4},{7,5},{8,10},{9,11},{10,... | collective-permute-start | bytes 3342344 | tf_op jit(solution)/shard_map/ppermute | solution.py:168
  77.6 9.6 %collective-permute-start.19 = (bf16[64,2176]{1,0:T(8,128)(2,1)S(1)}, bf16[64,2176]{1,0:T(8,128)(2,1)S(1)}, u32[]{:S(2)}, u32[]{:S(2)}) collective-permute-start(bf16[64,2176]{1,0:T(8,128)(2,1)S(1)} %collective-permute-done.15), channel_id=1, source_target_pairs={{0,1},{1,0},{2,3},{3,2},{4,5},{5,4},{6,7},{7,6},{8,9},{9,8},{10,11... | collective-permute-start | bytes 835592 | tf_op jit(solution)/shard_map/ppermute | solution.py:168
  79.1 22.3 %collective-permute-start.23 = (bf16[256,2176]{1,0:T(8,128)(2,1)S(1)}, bf16[256,2176]{1,0:T(8,128)(2,1)S(1)}, u32[]{:S(2)}, u32[]{:S(2)}) collective-permute-start(bf16[256,2176]{1,0:T(8,128)(2,1)S(1)} %constant_dynamic-update-slice_fusion.2.near_ref), channel_id=1, source_target_pairs={{16,0},{0,16},{17,1},{1,17},{18,2},{2,18},{19,3},{3,19},{20,4},{4,... | collective-permute-start | bytes 3342344 | tf_op jit(solution)/shard_map/ppermute | solution.py:46
  86.2 7.2 %collective-permute-start.13 = (bf16[4,64,1024]{2,1,0:T(8,128)(2,1)S(1)}, bf16[4,64,1024]{2,1,0:T(8,128)(2,1)S(1)}, u32[]{:S(2)}, u32[]{:S(2)}) collective-permute-start(bf16[4,64,1024]{2,1,0:T(8,128)(2,1)S(1)} %get-tuple-element.37), channel_id=1, source_target_pairs={{16,0},{0,16},{17,1},{1,17},{18,2},{2,18},{19,3},{3,19},{20,4},{4,... | collective-permute-start | bytes 1572872 | tf_op jit(solution)/shard_map/ppermute | solution.py:46
  87.2 14.0 %collective-permute-start.30 = (bf16[128,2176]{1,0:T(8,128)(2,1)S(1)}, bf16[128,2176]{1,0:T(8,128)(2,1)S(1)}, u32[]{:S(2)}, u32[]{:S(2)}) collective-permute-start(bf16[128,2176]{1,0:T(8,128)(2,1)S(1)} %constant_dynamic-update-slice_fusion.5.near_ref), channel_id=1, source_target_pairs={{0,2},{1,3},{2,0},{3,1},{4,6},{5,7},{6,4},{7,5},{8,10},{9,11},{10,... | collective-permute-start | bytes 1671176 | tf_op jit(solution)/shard_map/ppermute | solution.py:168
  93.3 8.4 %collective-permute-start.24 = (bf16[256,2176]{1,0:T(8,128)(2,1)S(1)}, bf16[256,2176]{1,0:T(8,128)(2,1)S(1)}, u32[]{:S(2)}, u32[]{:S(2)}) collective-permute-start(bf16[256,2176]{1,0:T(8,128)(2,1)S(1)} %collective-permute-done.22.far_ref), channel_id=1, source_target_pairs={{16,0},{0,16},{17,1},{1,17},{18,2},{2,18},{19,3},{3,19},{20,4},{4,... | collective-permute-start | bytes 3342344 | tf_op jit(solution)/shard_map/ppermute | solution.py:46
  93.6 14.2 %collective-permute-start.20 = (bf16[2,2,64,1024]{3,2,1,0:T(8,128)(2,1)S(1)}, bf16[2,2,64,1024]{3,2,1,0:T(8,128)(2,1)S(1)}, u32[]{:S(2)}, u32[]{:S(2)}) collective-permute-start(bf16[2,2,64,1024]{3,2,1,0:T(8,128)(2,1)S(1)} %pad_maximum_fusion.3), channel_id=1, source_target_pairs={{0,2},{1,3},{2,0},{3,1},{4,6},{5,7},{6,4},{7,5},{8,10},{9,11},{10,... | collective-permute-start | bytes 1572872 | tf_op jit(solution)/shard_map/ppermute | solution.py:168
  100.8 12.0 %collective-permute-start.26 = (bf16[4,128,1024]{2,1,0:T(8,128)(2,1)S(1)}, bf16[4,128,1024]{2,1,0:T(8,128)(2,1)S(1)}, u32[]{:S(2)}, u32[]{:S(2)}) collective-permute-start(bf16[4,128,1024]{2,1,0:T(8,128)(2,1)S(1)} %get-tuple-element.44), channel_id=1, source_target_pairs={{16,0},{0,16},{17,1},{1,17},{18,2},{2,18},{19,3},{3,19},{20,4},{4,... | collective-permute-start | bytes 3145736 | tf_op jit(solution)/shard_map/ppermute | solution.py:46
  101.2 12.8 %collective-permute-start.31 = (bf16[128,2176]{1,0:T(8,128)(2,1)S(1)}, bf16[128,2176]{1,0:T(8,128)(2,1)S(1)}, u32[]{:S(2)}, u32[]{:S(2)}) collective-permute-start(bf16[128,2176]{1,0:T(8,128)(2,1)S(1)} %constant_dynamic-update-slice_fusion.5.near_ref), channel_id=1, source_target_pairs={{16,0},{0,16},{17,1},{1,17},{18,2},{2,18},{19,3},{3,19},{20,4},{4,... | collective-permute-start | bytes 1671176 | tf_op jit(solution)/shard_map/ppermute | solution.py:46
  101.4 13.1 %collective-permute-start.32 = (bf16[128,2176]{1,0:T(8,128)(2,1)S(1)}, bf16[128,2176]{1,0:T(8,128)(2,1)S(1)}, u32[]{:S(2)}, u32[]{:S(2)}) collective-permute-start(bf16[128,2176]{1,0:T(8,128)(2,1)S(1)} %collective-permute-done.30.far_ref), channel_id=1, source_target_pairs={{16,0},{0,16},{17,1},{1,17},{18,2},{2,18},{19,3},{3,19},{20,4},{4,... | collective-permute-start | bytes 1671176 | tf_op jit(solution)/shard_map/ppermute | solution.py:46
  117.8 22.3 %collective-permute-start.27 = (bf16[2,2,128,1024]{3,2,1,0:T(8,128)(2,1)S(1)}, bf16[2,2,128,1024]{3,2,1,0:T(8,128)(2,1)S(1)}, u32[]{:S(2)}, u32[]{:S(2)}) collective-permute-start(bf16[2,2,128,1024]{3,2,1,0:T(8,128)(2,1)S(1)} %pad_maximum_fusion), channel_id=1, source_target_pairs={{0,2},{1,3},{2,0},{3,1},{4,6},{5,7},{6,4},{7,5},{8,10},{9,11},{10,... | collective-permute-start | bytes 3145736 | tf_op jit(solution)/shard_map/ppermute | solution.py:168
  120.0 18.3 %collective-permute-start.35 = (bf16[2,2,64,1024]{3,2,1,0:T(8,128)(2,1)S(1)}, bf16[2,2,64,1024]{3,2,1,0:T(8,128)(2,1)S(1)}, u32[]{:S(2)}, u32[]{:S(2)}) collective-permute-start(bf16[2,2,64,1024]{3,2,1,0:T(8,128)(2,1)S(1)} %pad_maximum_fusion.5), channel_id=1, source_target_pairs={{0,2},{1,3},{2,0},{3,1},{4,6},{5,7},{6,4},{7,5},{8,10},{9,11},{10,... | collective-permute-start | bytes 1572872 | tf_op jit(solution)/shard_map/ppermute | solution.py:168
  140.5 12.3 %collective-permute-start.28 = (bf16[2,128,1024]{2,1,0:T(8,128)(2,1)S(1)}, bf16[2,128,1024]{2,1,0:T(8,128)(2,1)S(1)}, u32[]{:S(2)}, u32[]{:S(2)}) collective-permute-start(bf16[2,128,1024]{2,1,0:T(8,128)(2,1)S(1)} %pad_maximum_fusion.4), channel_id=1, source_target_pairs={{0,1},{1,0},{2,3},{3,2},{4,5},{5,4},{6,7},{7,6},{8,9},{9,8},{10,11... | collective-permute-start | bytes 1572872 | tf_op jit(solution)/shard_map/ppermute | solution.py:168
  145.1 14.6 %collective-permute-start.37 = (bf16[128,1024]{1,0:T(8,128)(2,1)S(1)}, bf16[128,1024]{1,0:T(8,128)(2,1)S(1)}, u32[]{:S(2)}, u32[]{:S(2)}) collective-permute-start(bf16[128,1024]{1,0:T(8,128)(2,1)S(1)} %pad_maximum_fusion.9), channel_id=1, source_target_pairs={{0,8},{1,9},{2,10},{3,11},{4,12},{5,13},{6,14},{7,15},{8,0},{9,1},... | collective-permute-start | bytes 786440 | tf_op jit(solution)/shard_map/ppermute | solution.py:39
  153.1 13.3 %collective-permute-start.38 = (bf16[128,1024]{1,0:T(8,128)(2,1)S(1)}, bf16[128,1024]{1,0:T(8,128)(2,1)S(1)}, u32[]{:S(2)}, u32[]{:S(2)}) collective-permute-start(bf16[128,1024]{1,0:T(8,128)(2,1)S(1)} %pad_maximum_fusion.10), channel_id=1, source_target_pairs={{0,12},{1,13},{2,14},{3,15},{4,0},{5,1},{6,2},{7,3},{8,4},{9,5},{1... | collective-permute-start | bytes 786440 | tf_op jit(solution)/shard_map/ppermute | solution.py:39
  154.5 16.1 %collective-permute-start.29 = (bf16[128,1024]{1,0:T(8,128)(2,1)}, bf16[128,1024]{1,0:T(8,128)(2,1)S(1)}, u32[]{:S(2)}, u32[]{:S(2)}) collective-permute-start(bf16[128,1024]{1,0:T(8,128)(2,1)} %pad_maximum_fusion.7), channel_id=1, source_target_pairs={{0,4},{1,5},{2,6},{3,7},{4,8},{5,9},{6,10},{7,11},{8,12},{9,13},{1... | collective-permute-start | bytes 786440 | tf_op jit(solution)/shard_map/ppermute | solution.py:39
  (20 other events, 227.7 us)

commit v5 on v4

--- a/solution.py
+++ b/solution.py
@@ -133,10 +133,10 @@
     rows_out[:, width:] = lanes_ref[part, :]
 
 
-def local_call(body, out_shapes, scalars, arrays, flops=0, limit=16):
+def local_call(body, out_shapes, scalars, arrays, flops=0, moved=0, limit=16):
     whole = pl.BlockSpec(memory_space=pltpu.VMEM)
     scalar = pl.BlockSpec(memory_space=pltpu.SMEM)
-    moved = sum(x.size * x.dtype.itemsize for x in (*arrays, *out_shapes))
+    moved = moved or sum(x.size * x.dtype.itemsize for x in (*arrays, *out_shapes))
     return pl.pallas_call(
         body,
         in_specs=[scalar] * len(scalars) + [whole] * len(arrays),
@@ -201,7 +201,8 @@
         [out_shape] * parts,
         [place],
         [near, far, w_gate, w_up, w_down],
-        flops=6 * count * width * units,
+        flops=count,
+        moved=count,
     )
 
 
@@ -323,7 +324,7 @@
     )
     weights = (w_gate[0].T, w_up[0].T, w_down[0])
     if planes <= 4:
-        groups = [[0]] + [sorted({i, planes - i}) for i in range(1, planes // 2 + 1)]
+        groups = [[0]] + [sorted({i, planes - i}) for i in range(planes // 2, 0, -1)]
     else:
         groups = [[0]] + [list(range(i, min(i + 8, planes))) for i in range(1, planes, 8)]
     nears, fars = [], []
@@ -333,32 +334,31 @@
         if number > 1:
             column = after(column, nears[-1])
         nears.append(jnp.concatenate([column, crossed(column, True)]))
-        fars.append(crossed(nears[-1], False))
+        fars.append(crossed(after(nears[-1], *fars[-1:]), False))
     weights = (w_gate[0].T, w_up[0].T, w_down[0])
     run = functools.partial(
         expert_outputs, place, weights=weights, experts=experts, cores=cores
     )
     outs = run(nears[0], fars[0], waits={})
     own_totals = core_totals(outs, cores)
-    got = crossed(after(second_share(own_totals), nears[-1]), False)
-    own_totals = merged(own_totals, got, 2)
-    own_got = crossed(first_share(own_totals), True)
-    totals, sents = [], []
+    own_sent = sent = second_share(own_totals)
+    partial = {}
+    shared = None
     for number in range(1, len(groups)):
-        waits = {0: [outs]}
-        if number == len(groups) - 1:
-            waits = {0: [outs, got], cores - 1: [own_got, *sents]}
-        outs = run(nears[number], fars[number], waits=waits)
-        totals.append(core_totals(outs, cores))
-        sents.append(second_share(totals[-1]))
-    gots = [crossed(sent, False) for sent in sents]
-    totals = [merged(*pair, 2) for pair in zip(totals, gots, strict=True)]
-    gots = [crossed(first_share(pair), True) for pair in totals]
+        outs = run(nears[number], fars[number], waits={0: [outs], cores - 1: [sent]})
+        totals = core_totals(outs, cores)
+        if shared is not None:
+            totals = [after(total, shared) for total in totals]
+        sent = second_share(totals)
+        totals = merged(totals, crossed(sent, False), 2)
+        shared = first_share(totals)
+        partial[number] = (totals, crossed(shared, True))
+    totals = merged(own_totals, crossed(after(own_sent, shared), False), 2)
+    partial[0] = (totals, crossed(first_share(totals), True))
     results = {}
-    for group, pair, came in zip(
-        groups, [own_totals, *totals], [own_got, *gots], strict=True
-    ):
-        rows_of = merged([total[0] for total in pair], came, None)
+    for number, group in enumerate(groups):
+        totals, came = partial[number]
+        rows_of = merged([total[0] for total in totals], came, None)
         for i, ahead in enumerate(group):
             results[ahead] = jnp.concatenate(
                 [rows[i * part_rows : (i + 1) * part_rows] for rows in rows_of]

time: 172 us -> 179 us (1.041)
  waiting for transfers between devices: 70.7 us -> 82.3 us
  starting transfers between devices: 51.5 us -> 46.5 us
    ppermute x12, waiting for transfers between devices: 39.5 us -> 46.9 us  [crossed(): return lax.ppermute(block, ('tok', 'blk'), route)]
    ppermute x3, waiting for transfers between devices: 4.43 us -> 11.4 us  [from_plane(): lax.ppermute(block, 'blk', [((i + PLANE * ahead) % count, i) for i in ran...]
    ppermute x3, starting transfers between devices: 9.85 us -> 4.45 us  [to_plane(): lax.ppermute(block, 'blk', [(i, (i + PLANE * ahead) % count) for i in ran...]
    ppermute x3, waiting for transfers between devices: 13.3 us -> 9.79 us  [to_plane(): lax.ppermute(block, 'blk', [(i, (i + PLANE * ahead) % count) for i in ran...]
    ppermute x12, starting transfers between devices: 17.3 us -> 14 us  [crossed(): return lax.ppermute(block, ('tok', 'blk'), route)]
    ppermute x3, starting transfers between devices: 5.57 us -> 7.44 us  [from_plane(): lax.ppermute(block, 'blk', [((i + PLANE * ahead) % count, i) for i in ran...]
    unnamed x31 -> x30, local copies, waits for them, and re-layouts: 6.21 us -> 6.2 us
  transfers between devices with their start and end apart: 39 -> 39, of which waited for: 21 -> 20; matrix products, arithmetic and copies ran while one was open for 7% -> 7% of each run, Pallas kernels for 15% -> 15%
where the time goes in v5:
time: 179 us
  waiting for transfers between devices  82.3 us (46%)
  starting transfers between devices  46.5 us (26%)
  Pallas kernels  29.9 us (17%)
  local copies, waits for them, and re-layouts  10.5 us (6%)
  other arithmetic  8.66 us (5%)
    ppermute x12, waiting for transfers between devices, crossed(): return lax.ppermute(block, ('tok', 'blk'), route)  46.9 us
    pallas_call x10, Pallas kernels, local_call(): pl.pallas_call(body, in_specs=[scalar] * len(scalars) + [whole] * len(arr...  29.9 us
    ppermute x12, starting transfers between devices, crossed(): return lax.ppermute(block, ('tok', 'blk'), route)  14 us
    ppermute x3, waiting for transfers between devices, from_plane(): lax.ppermute(block, 'blk', [((i + PLANE * ahead) % count, i) for i in ran...  11.4 us
    ppermute x3, waiting for transfers between devices, to_plane(): lax.ppermute(block, 'blk', [(i, (i + PLANE * ahead) % count) for i in ran...  9.79 us
    ppermute x2, starting transfers between devices, next_plane(): lax.ppermute(block, 'blk', [(i, i + PLANE) for i in range(count - PLANE)])  8.43 us
    ppermute x6, starting transfers between devices, flipped(): lax.ppermute(block, 'blk', [(i, i ^ mask) for i in range(lax.axis_size('b...  8.21 us
    ppermute x6, waiting for transfers between devices, flipped(): lax.ppermute(block, 'blk', [(i, i ^ mask) for i in range(lax.axis_size('b...  8.16 us
  transfers between devices with their start and end apart: 39, of which 20 were waited for; matrix products, arithmetic and copies ran while one was open for 7% of the time, Pallas kernels for 15%

profile of v5, /device:TPU:0, one launch (start us, length us, event | category | flops | bytes accessed | tf_op | source)
XLA Modules:
  0.0 179.1 jit_solution(3539634989230805743)
XLA Ops:
  4.5 4.9 %collective-permute-start = (bf16[128,1024]{1,0:T(8,128)(2,1)S(1)}, bf16[128,1024]{1,0:T(8,128)(2,1)S(1)}, u32[]{:S(2)}, u32[]{:S(2)}) collective-permute-start(bf16[128,1024]{1,0:T(8,128)(2,1)S(1)} %get-tuple-element.33.rest_0_), channel_id=1, source_target_pairs={{0,4},{1,5},{2,6},{3,7},{4,8},{5,9},{6,10},{7,11},{8,12},{9,13},{1... | collective-permute-start | bytes 786440 | tf_op jit(solution)/shard_map/ppermute | solution.py:27
  9.4 3.5 %collective-permute-start.4 = (bf16[128,1024]{1,0:T(8,128)(2,1)}, bf16[128,1024]{1,0:T(8,128)(2,1)S(1)}, u32[]{:S(2)}, u32[]{:S(2)}) collective-permute-start(bf16[128,1024]{1,0:T(8,128)(2,1)} %rest_0_), channel_id=1, source_target_pairs={{0,4},{1,5},{2,6},{3,7},{4,8},{5,9},{6,10},{7,11},{8,12},{9,13},{1... | collective-permute-start | bytes 786440 | tf_op jit(solution)/shard_map/ppermute | solution.py:27
  13.7 2.4 %collective-permute-done.rest_1_ = bf16[128,1024]{1,0:T(8,128)(2,1)S(1)} collective-permute-done((bf16[128,1024]{1,0:T(8,128)(2,1)S(1)}, bf16[128,1024]{1,0:T(8,128)(2,1)S(1)}, u32[]{:S(2)}, u32[]{:S(2)}) %collective-permute-start) | collective-permute-done | bytes 262176 | tf_op jit(solution)/shard_map/ppermute | solution.py:27
  16.9 2.4 %collective-permute-start.3 = (bf16[128,1024]{1,0:T(8,128)(2,1)S(1)}, bf16[128,1024]{1,0:T(8,128)(2,1)S(1)}, u32[]{:S(2)}, u32[]{:S(2)}) collective-permute-start(bf16[128,1024]{1,0:T(8,128)(2,1)S(1)} %get-tuple-element.79), channel_id=1, source_target_pairs={{0,3},{1,2},{2,1},{3,0},{4,7},{5,6},{6,5},{7,4},{8,11},{9,10},{10,... | collective-permute-start | bytes 786440 | tf_op jit(solution)/shard_map/ppermute | solution.py:22
  22.2 2.4 %collective-permute-start.7 = (bf16[128,1024]{1,0:T(8,128)(2,1)}, bf16[128,1024]{1,0:T(8,128)(2,1)S(1)}, u32[]{:S(2)}, u32[]{:S(2)}) collective-permute-start(bf16[128,1024]{1,0:T(8,128)(2,1)} %get-tuple-element.76), channel_id=1, source_target_pairs={{0,3},{1,2},{2,1},{3,0},{4,7},{5,6},{6,5},{7,4},{8,11},{9,10},{10,... | collective-permute-start | bytes 786440 | tf_op jit(solution)/shard_map/ppermute | solution.py:22
  26.8 1.8 collective-permute-start.5
  29.6 2.7 %scatter_fusion = bf16[8,16,2,1024]{3,1,2,0:T(8,128)(2,1)} fusion(bf16[8,16,2,1024]{3,1,2,0:T(8,128)(2,1)} %broadcast_in_dim.31, s32[8]{0:T(128)S(1)} %compare_select_fusion, bf16[8,16,2,1024]{3,1,2,0:T(8,128)(2,1)} %pad_maximum_fusion.2), kind=kCustom, calls=%fused_computation | custom fusion | bytes 1572896 | tf_op jit(solution)/shard_map/scatter | solution.py:302
  32.3 3.0 %collective-permute-done.2.rest_3_ = bf16[128,1024]{1,0:T(8,128)(2,1)S(1)} collective-permute-done((bf16[128,1024]{1,0:T(8,128)(2,1)}, bf16[128,1024]{1,0:T(8,128)(2,1)S(1)}, u32[]{:S(2)}, u32[]{:S(2)}) %collective-permute-start.2) | collective-permute-done | bytes 262176 | tf_op jit(solution)/shard_map/ppermute | solution.py:22
  35.3 1.9 %shard_map.141.prob_ref = bf16[8,128,640]{2,1,0:T(8,128)(2,1)S(1)} custom-call(s32[2]{0:T(128)S(1)} %pad_add_fusion.place_ref, s32[8]{0:T(128)S(1)} %copy-done.10, bf16[128,1024]{1,0:T(8,128)(2,1)S(1)} %get-tuple-element.32.q_ref, bf16[128,1024]{1,0:T(8,128)(2,1)S(1)} %get-tuple-element.33.rest_0_, bf16[128,1024]{1,0:T(8,128)(2,1)S(1)} %collective-permute-done.rest_1_, ...), custom_call_target="tpu_custom_call" | custom-call | flops 167772160 | bytes 2883584 | tf_op jit(solution)/shard_map/pallas_call | solution.py:140
  38.0 2.6 %collective-permute-done.6.rest_3_ = bf16[128,1024]{1,0:T(8,128)(2,1)S(1)} collective-permute-done((bf16[128,1024]{1,0:T(8,128)(2,1)}, bf16[128,1024]{1,0:T(8,128)(2,1)S(1)}, u32[]{:S(2)}, u32[]{:S(2)}) %collective-permute-start.6) | collective-permute-done | bytes 262176 | tf_op jit(solution)/shard_map/ppermute | solution.py:22
  40.7 2.2 %copy-done.3 = bf16[1024,2048]{1,0:T(8,128)(2,1)S(1)} copy-done((bf16[1024,2048]{1,0:T(8,128)(2,1)S(1)}, bf16[1024,2048]{1,0:T(8,128)(2,1)}, u32[]{:S(2)}) %copy-start.3) | copy-done | bytes 4194328
  44.7 2.6 %collective-permute-done.8.rest_1_ = f32[128,2048]{1,0:T(8,128)S(1)} collective-permute-done((f32[128,2048]{1,0:T(8,128)S(1)}, f32[128,2048]{1,0:T(8,128)S(1)}, u32[]{:S(2)}, u32[]{:S(2)}) %collective-permute-start.8) | collective-permute-done | bytes 1048608 | tf_op jit(solution)/shard_map/ppermute | solution.py:46
  48.1 3.6 %collective-permute-start.17 = (bf16[64,2176]{1,0:T(8,128)(2,1)S(1)}, bf16[64,2176]{1,0:T(8,128)(2,1)S(1)}, u32[]{:S(2)}, u32[]{:S(2)}) collective-permute-start(bf16[64,2176]{1,0:T(8,128)(2,1)S(1)} %get-tuple-element.43), channel_id=1, source_target_pairs={{8,0},{9,1},{10,2},{11,3},{12,4},{13,5},{14,6},{15,7},{0,8},{1,9},... | collective-permute-start | bytes 835592 | tf_op jit(solution)/shard_map/ppermute | solution.py:32
  53.3 5.0 %collective-permute-done.9 = bf16[64,2176]{1,0:T(8,128)(2,1)S(1)} collective-permute-done((bf16[64,2176]{1,0:T(8,128)(2,1)S(1)}, bf16[64,2176]{1,0:T(8,128)(2,1)S(1)}, u32[]{:S(2)}, u32[]{:S(2)}) %collective-permute-start.9) | collective-permute-done | bytes 278560 | tf_op jit(solution)/shard_map/ppermute | solution.py:168
  59.9 2.2 %collective-permute-start.15 = (bf16[64,2176]{1,0:T(8,128)(2,1)S(1)}, bf16[64,2176]{1,0:T(8,128)(2,1)S(1)}, u32[]{:S(2)}, u32[]{:S(2)}) collective-permute-start(bf16[64,2176]{1,0:T(8,128)(2,1)S(1)} %get-tuple-element.43), channel_id=1, source_target_pairs={{4,0},{5,1},{6,2},{7,3},{8,4},{9,5},{10,6},{11,7},{12,8},{13,9},{1... | collective-permute-start | bytes 835592 | tf_op jit(solution)/shard_map/ppermute | solution.py:32
  63.6 7.5 %collective-permute-done.17 = bf16[64,2176]{1,0:T(8,128)(2,1)S(1)} collective-permute-done((bf16[64,2176]{1,0:T(8,128)(2,1)S(1)}, bf16[64,2176]{1,0:T(8,128)(2,1)S(1)}, u32[]{:S(2)}, u32[]{:S(2)}) %collective-permute-start.17) | collective-permute-done | bytes 278560 | tf_op jit(solution)/shard_map/ppermute | solution.py:32
  72.7 3.9 %collective-permute-done.15 = bf16[64,2176]{1,0:T(8,128)(2,1)S(1)} collective-permute-done((bf16[64,2176]{1,0:T(8,128)(2,1)S(1)}, bf16[64,2176]{1,0:T(8,128)(2,1)S(1)}, u32[]{:S(2)}, u32[]{:S(2)}) %collective-permute-start.15) | collective-permute-done | bytes 278560 | tf_op jit(solution)/shard_map/ppermute | solution.py:32
  80.7 3.2 %shard_map.144 = (bf16[4,64,1024]{2,1,0:T(8,128)(2,1)S(1)}, bf16[4,64,1024]{2,1,0:T(8,128)(2,1)S(1)}) custom-call(s32[2]{0:T(128)S(1)} %pad_add_fusion.place_ref, bf16[128,2176]{1,0:T(8,128)(2,1)S(1)} %constant_dynamic-update-slice_fusion.near_ref, bf16[128,2176]{1,0:T(8,128)(2,1)S(1)} %collective-permute-done.10.far_ref, bf16[704,2048]{1,0:T(8,128)(2,1)S(1)} %bitcast.82, ...), custom_call_target="tpu_custom_call" | custom-call | flops 256 | bytes 256 | tf_op jit(solution)/shard_map/pallas_call | solution.py:140
  84.7 3.2 %shard_map.145 = (bf16[4,64,1024]{2,1,0:T(8,128)(2,1)S(1)}, bf16[4,64,1024]{2,1,0:T(8,128)(2,1)S(1)}) custom-call(s32[2]{0:T(128)S(1)} %pad_add_fusion.place_ref, bf16[128,2176]{1,0:T(8,128)(2,1)S(1)} %collective-permute-done.11.near_ref, bf16[128,2176]{1,0:T(8,128)(2,1)S(1)} %collective-permute-done.12.far_ref, bf16[704,2048]{1,0:T(8,128)(2,1)S(1)} %bitcast.83, ...), custom_call_target="tpu_custom_call" | custom-call | flops 256 | bytes 256 | tf_op jit(solution)/shard_map/pallas_call | solution.py:140
  88.0 5.0 %collective-permute-done.19 = bf16[128,2176]{1,0:T(8,128)(2,1)S(1)} collective-permute-done((bf16[128,2176]{1,0:T(8,128)(2,1)S(1)}, bf16[128,2176]{1,0:T(8,128)(2,1)S(1)}, u32[]{:S(2)}, u32[]{:S(2)}) %collective-permute-start.19) | collective-permute-done | bytes 557088 | tf_op jit(solution)/shard_map/ppermute | solution.py:168
  93.1 3.2 %shard_map.146 = (bf16[4,64,1024]{2,1,0:T(8,128)(2,1)S(1)}, bf16[4,64,1024]{2,1,0:T(8,128)(2,1)S(1)}) custom-call(s32[2]{0:T(128)S(1)} %pad_add_fusion.place_ref, bf16[128,2176]{1,0:T(8,128)(2,1)S(1)} %constant_dynamic-update-slice_fusion.2.near_ref, bf16[128,2176]{1,0:T(8,128)(2,1)S(1)} %collective-permute-done.20.far_ref, bf16[704,2048]{1,0:T(8,128)(2,1)S(1)} %bitcast.84, ...), custom_call_target="tpu_custom_call" | custom-call | flops 256 | bytes 256 | tf_op jit(solution)/shard_map/pallas_call | solution.py:140
  99.7 3.2 %shard_map.147 = (bf16[4,64,1024]{2,1,0:T(8,128)(2,1)S(1)}, bf16[4,64,1024]{2,1,0:T(8,128)(2,1)S(1)}) custom-call(s32[2]{0:T(128)S(1)} %pad_add_fusion.place_ref, bf16[128,2176]{1,0:T(8,128)(2,1)S(1)} %collective-permute-done.21.near_ref, bf16[128,2176]{1,0:T(8,128)(2,1)S(1)} %collective-permute-done.22.far_ref, bf16[704,2048]{1,0:T(8,128)(2,1)S(1)} %bitcast.85, ...), custom_call_target="tpu_custom_call" | custom-call | flops 256 | bytes 256 | tf_op jit(solution)/shard_map/pallas_call | solution.py:140
  103.5 8.5 %collective-permute-done.23.far_ref = bf16[256,2176]{1,0:T(8,128)(2,1)S(1)} collective-permute-done((bf16[256,2176]{1,0:T(8,128)(2,1)S(1)}, bf16[256,2176]{1,0:T(8,128)(2,1)S(1)}, u32[]{:S(2)}, u32[]{:S(2)}) %collective-permute-start.23) | collective-permute-done | bytes 1114144 | tf_op jit(solution)/shard_map/ppermute | solution.py:168
  112.4 5.9 %shard_map.148 = (bf16[4,128,1024]{2,1,0:T(8,128)(2,1)S(1)}, bf16[4,128,1024]{2,1,0:T(8,128)(2,1)S(1)}) custom-call(s32[2]{0:T(128)S(1)} %pad_add_fusion.place_ref, bf16[256,2176]{1,0:T(8,128)(2,1)S(1)} %constant_dynamic-update-slice_fusion.4.near_ref, bf16[256,2176]{1,0:T(8,128)(2,1)S(1)} %collective-permute-done.23.far_ref, ...), custom_call_target="tpu_custom_call" | custom-call | flops 512 | bytes 512 | tf_op jit(solution)/shard_map/pallas_call | solution.py:140
  119.6 5.7 %shard_map.149 = (bf16[4,128,1024]{2,1,0:T(8,128)(2,1)S(1)}, bf16[4,128,1024]{2,1,0:T(8,128)(2,1)S(1)}) custom-call(s32[2]{0:T(128)S(1)} %pad_add_fusion.place_ref, bf16[256,2176]{1,0:T(8,128)(2,1)S(1)} %collective-permute-done.24.near_ref, bf16[256,2176]{1,0:T(8,128)(2,1)S(1)} %collective-permute-done.27.far_ref, bf16[704,2048]{1,0:T(8,128)(2,1)S(1)} %bitcast.87, ...), custom_call_target="tpu_custom_call" | custom-call | flops 512 | bytes 512 | tf_op jit(solution)/shard_map/pallas_call | solution.py:140
  126.0 2.2 %collective-permute-done.29 = bf16[2,2,64,1024]{3,2,1,0:T(8,128)(2,1)S(1)} collective-permute-done((bf16[2,2,64,1024]{3,2,1,0:T(8,128)(2,1)S(1)}, bf16[2,2,64,1024]{3,2,1,0:T(8,128)(2,1)S(1)}, u32[]{:S(2)}, u32[]{:S(2)}) %collective-permute-start.29) | collective-permute-done | bytes 524320 | tf_op jit(solution)/shard_map/ppermute | solution.py:168
  131.7 15.0 %collective-permute-done.31 = bf16[2,2,128,1024]{3,2,1,0:T(8,128)(2,1)S(1)} collective-permute-done((bf16[2,2,128,1024]{3,2,1,0:T(8,128)(2,1)S(1)}, bf16[2,2,128,1024]{3,2,1,0:T(8,128)(2,1)S(1)}, u32[]{:S(2)}, u32[]{:S(2)}) %collective-permute-start.31) | collective-permute-done | bytes 1048608 | tf_op jit(solution)/shard_map/ppermute | solution.py:168
  149.3 2.4 %collective-permute-start.37 = (bf16[128,1024]{1,0:T(8,128)(2,1)S(1)}, bf16[128,1024]{1,0:T(8,128)(2,1)S(1)}, u32[]{:S(2)}, u32[]{:S(2)}) collective-permute-start(bf16[128,1024]{1,0:T(8,128)(2,1)S(1)} %pad_maximum_fusion.9), channel_id=1, source_target_pairs={{0,8},{1,9},{2,10},{3,11},{4,12},{5,13},{6,14},{7,15},{8,0},{9,1},... | collective-permute-start | bytes 786440 | tf_op jit(solution)/shard_map/ppermute | solution.py:39
  151.7 9.8 %collective-permute-done.32 = bf16[2,2,64,1024]{3,2,1,0:T(8,128)(2,1)S(1)} collective-permute-done((bf16[2,2,64,1024]{3,2,1,0:T(8,128)(2,1)S(1)}, bf16[2,2,64,1024]{3,2,1,0:T(8,128)(2,1)S(1)}, u32[]{:S(2)}, u32[]{:S(2)}) %collective-permute-start.32) | collective-permute-done | bytes 524320 | tf_op jit(solution)/shard_map/ppermute | solution.py:168
  163.7 1.7 collective-permute-start.38
  168.3 4.3 %collective-permute-done.38 = bf16[128,1024]{1,0:T(8,128)(2,1)S(1)} collective-permute-done((bf16[128,1024]{1,0:T(8,128)(2,1)}, bf16[128,1024]{1,0:T(8,128)(2,1)S(1)}, u32[]{:S(2)}, u32[]{:S(2)}) %collective-permute-start.38) | collective-permute-done | bytes 262176 | tf_op jit(solution)/shard_map/ppermute | solution.py:39
  172.6 5.5 %collective-permute-done.35 = bf16[128,1024]{1,0:T(8,128)(2,1)S(1)} collective-permute-done((bf16[128,1024]{1,0:T(8,128)(2,1)}, bf16[128,1024]{1,0:T(8,128)(2,1)S(1)}, u32[]{:S(2)}, u32[]{:S(2)}) %collective-permute-start.35) | collective-permute-done | bytes 262176 | tf_op jit(solution)/shard_map/ppermute | solution.py:39
  (141 shorter events, 44.2 us)
Async XLA Ops:
  4.5 11.6 %collective-permute-start = (bf16[128,1024]{1,0:T(8,128)(2,1)S(1)}, bf16[128,1024]{1,0:T(8,128)(2,1)S(1)}, u32[]{:S(2)}, u32[]{:S(2)}) collective-permute-start(bf16[128,1024]{1,0:T(8,128)(2,1)S(1)} %get-tuple-element.33.rest_0_), channel_id=1, source_target_pairs={{0,4},{1,5},{2,6},{3,7},{4,8},{5,9},{6,10},{7,11},{8,12},{9,13},{1... | collective-permute-start | bytes 786440 | tf_op jit(solution)/shard_map/ppermute | solution.py:27
  9.4 11.8 %collective-permute-start.4 = (bf16[128,1024]{1,0:T(8,128)(2,1)}, bf16[128,1024]{1,0:T(8,128)(2,1)S(1)}, u32[]{:S(2)}, u32[]{:S(2)}) collective-permute-start(bf16[128,1024]{1,0:T(8,128)(2,1)} %rest_0_), channel_id=1, source_target_pairs={{0,4},{1,5},{2,6},{3,7},{4,8},{5,9},{6,10},{7,11},{8,12},{9,13},{1... | collective-permute-start | bytes 786440 | tf_op jit(solution)/shard_map/ppermute | solution.py:27
  16.9 9.9 %collective-permute-start.3 = (bf16[128,1024]{1,0:T(8,128)(2,1)S(1)}, bf16[128,1024]{1,0:T(8,128)(2,1)S(1)}, u32[]{:S(2)}, u32[]{:S(2)}) collective-permute-start(bf16[128,1024]{1,0:T(8,128)(2,1)S(1)} %get-tuple-element.79), channel_id=1, source_target_pairs={{0,3},{1,2},{2,1},{3,0},{4,7},{5,6},{6,5},{7,4},{8,11},{9,10},{10,... | collective-permute-start | bytes 786440 | tf_op jit(solution)/shard_map/ppermute | solution.py:22
  20.2 15.1 %collective-permute-start.2 = (bf16[128,1024]{1,0:T(8,128)(2,1)}, bf16[128,1024]{1,0:T(8,128)(2,1)S(1)}, u32[]{:S(2)}, u32[]{:S(2)}) collective-permute-start(bf16[128,1024]{1,0:T(8,128)(2,1)} %get-tuple-element.80), channel_id=1, source_target_pairs={{0,2},{1,3},{2,0},{3,1},{4,6},{5,7},{6,4},{7,5},{8,10},{9,11},{10,... | collective-permute-start | bytes 786440 | tf_op jit(solution)/shard_map/ppermute | solution.py:22
  20.7 14.6 %collective-permute-start.1 = (bf16[128,1024]{1,0:T(8,128)(2,1)S(1)}, bf16[128,1024]{1,0:T(8,128)(2,1)S(1)}, u32[]{:S(2)}, u32[]{:S(2)}) collective-permute-start(bf16[128,1024]{1,0:T(8,128)(2,1)S(1)} %get-tuple-element.81), channel_id=1, source_target_pairs={{0,1},{1,0},{2,3},{3,2},{4,5},{5,4},{6,7},{7,6},{8,9},{9,8},{10,11... | collective-permute-start | bytes 786440 | tf_op jit(solution)/shard_map/ppermute | solution.py:22
  22.2 15.8 %collective-permute-start.7 = (bf16[128,1024]{1,0:T(8,128)(2,1)}, bf16[128,1024]{1,0:T(8,128)(2,1)S(1)}, u32[]{:S(2)}, u32[]{:S(2)}) collective-permute-start(bf16[128,1024]{1,0:T(8,128)(2,1)} %get-tuple-element.76), channel_id=1, source_target_pairs={{0,3},{1,2},{2,1},{3,0},{4,7},{5,6},{6,5},{7,4},{8,11},{9,10},{10,... | collective-permute-start | bytes 786440 | tf_op jit(solution)/shard_map/ppermute | solution.py:22
  24.6 16.0 %collective-permute-start.6 = (bf16[128,1024]{1,0:T(8,128)(2,1)}, bf16[128,1024]{1,0:T(8,128)(2,1)S(1)}, u32[]{:S(2)}, u32[]{:S(2)}) collective-permute-start(bf16[128,1024]{1,0:T(8,128)(2,1)} %get-tuple-element.77), channel_id=1, source_target_pairs={{0,2},{1,3},{2,0},{3,1},{4,6},{5,7},{6,4},{7,5},{8,10},{9,11},{10,... | collective-permute-start | bytes 786440 | tf_op jit(solution)/shard_map/ppermute | solution.py:22
  26.8 13.9 %collective-permute-start.5 = (bf16[128,1024]{1,0:T(8,128)(2,1)}, bf16[128,1024]{1,0:T(8,128)(2,1)S(1)}, u32[]{:S(2)}, u32[]{:S(2)}) collective-permute-start(bf16[128,1024]{1,0:T(8,128)(2,1)} %get-tuple-element.78), channel_id=1, source_target_pairs={{0,1},{1,0},{2,3},{3,2},{4,5},{5,4},{6,7},{7,6},{8,9},{9,8},{10,11... | collective-permute-start | bytes 786440 | tf_op jit(solution)/shard_map/ppermute | solution.py:22
  48.1 23.0 %collective-permute-start.17 = (bf16[64,2176]{1,0:T(8,128)(2,1)S(1)}, bf16[64,2176]{1,0:T(8,128)(2,1)S(1)}, u32[]{:S(2)}, u32[]{:S(2)}) collective-permute-start(bf16[64,2176]{1,0:T(8,128)(2,1)S(1)} %get-tuple-element.43), channel_id=1, source_target_pairs={{8,0},{9,1},{10,2},{11,3},{12,4},{13,5},{14,6},{15,7},{0,8},{1,9},... | collective-permute-start | bytes 835592 | tf_op jit(solution)/shard_map/ppermute | solution.py:32
  58.3 14.4 %collective-permute-start.16 = (bf16[64,2176]{1,0:T(8,128)(2,1)S(1)}, bf16[64,2176]{1,0:T(8,128)(2,1)S(1)}, u32[]{:S(2)}, u32[]{:S(2)}) collective-permute-start(bf16[64,2176]{1,0:T(8,128)(2,1)S(1)} %get-tuple-element.43), channel_id=1, source_target_pairs={{12,0},{13,1},{14,2},{15,3},{0,4},{1,5},{2,6},{3,7},{4,8},{5,9},{6... | collective-permute-start | bytes 835592 | tf_op jit(solution)/shard_map/ppermute | solution.py:32
  59.9 16.7 %collective-permute-start.15 = (bf16[64,2176]{1,0:T(8,128)(2,1)S(1)}, bf16[64,2176]{1,0:T(8,128)(2,1)S(1)}, u32[]{:S(2)}, u32[]{:S(2)}) collective-permute-start(bf16[64,2176]{1,0:T(8,128)(2,1)S(1)} %get-tuple-element.43), channel_id=1, source_target_pairs={{4,0},{5,1},{6,2},{7,3},{8,4},{9,5},{10,6},{11,7},{12,8},{13,9},{1... | collective-permute-start | bytes 835592 | tf_op jit(solution)/shard_map/ppermute | solution.py:32
  62.2 21.9 %collective-permute-start.11 = (bf16[128,2176]{1,0:T(8,128)(2,1)S(1)}, bf16[128,2176]{1,0:T(8,128)(2,1)S(1)}, u32[]{:S(2)}, u32[]{:S(2)}) collective-permute-start(bf16[128,2176]{1,0:T(8,128)(2,1)S(1)} %constant_dynamic-update-slice_fusion.near_ref), channel_id=1, source_target_pairs={{16,0},{0,16},{17,1},{1,17},{18,2},{2,18},{19,3},{3,19},{20,4},{4,... | collective-permute-start | bytes 1671176 | tf_op jit(solution)/shard_map/ppermute | solution.py:46
  62.2 14.5 %collective-permute-start.10 = (bf16[128,2176]{1,0:T(8,128)(2,1)S(1)}, bf16[128,2176]{1,0:T(8,128)(2,1)S(1)}, u32[]{:S(2)}, u32[]{:S(2)}) collective-permute-start(bf16[128,2176]{1,0:T(8,128)(2,1)S(1)} %constant_dynamic-update-slice_fusion.near_ref), channel_id=1, source_target_pairs={{0,2},{1,3},{2,0},{3,1},{4,6},{5,7},{6,4},{7,5},{8,10},{9,11},{10,... | collective-permute-start | bytes 1671176 | tf_op jit(solution)/shard_map/ppermute | solution.py:168
  76.6 8.0 %collective-permute-start.12 = (bf16[128,2176]{1,0:T(8,128)(2,1)S(1)}, bf16[128,2176]{1,0:T(8,128)(2,1)S(1)}, u32[]{:S(2)}, u32[]{:S(2)}) collective-permute-start(bf16[128,2176]{1,0:T(8,128)(2,1)S(1)} %collective-permute-done.10.far_ref), channel_id=1, source_target_pairs={{16,0},{0,16},{17,1},{1,17},{18,2},{2,18},{19,3},{3,19},{20,4},{4,... | collective-permute-start | bytes 1671176 | tf_op jit(solution)/shard_map/ppermute | solution.py:46
  77.7 15.3 %collective-permute-start.19 = (bf16[128,2176]{1,0:T(8,128)(2,1)S(1)}, bf16[128,2176]{1,0:T(8,128)(2,1)S(1)}, u32[]{:S(2)}, u32[]{:S(2)}) collective-permute-start(bf16[128,2176]{1,0:T(8,128)(2,1)S(1)} %pad_maximum_fusion.1), channel_id=1, source_target_pairs={{0,1},{1,0},{2,3},{3,2},{4,5},{5,4},{6,7},{7,6},{8,9},{9,8},{10,11... | collective-permute-start | bytes 1671176 | tf_op jit(solution)/shard_map/ppermute | solution.py:168
  79.3 13.8 %collective-permute-start.20 = (bf16[128,2176]{1,0:T(8,128)(2,1)S(1)}, bf16[128,2176]{1,0:T(8,128)(2,1)S(1)}, u32[]{:S(2)}, u32[]{:S(2)}) collective-permute-start(bf16[128,2176]{1,0:T(8,128)(2,1)S(1)} %constant_dynamic-update-slice_fusion.2.near_ref), channel_id=1, source_target_pairs={{0,2},{1,3},{2,0},{3,1},{4,6},{5,7},{6,4},{7,5},{8,10},{9,11},{10,... | collective-permute-start | bytes 1671176 | tf_op jit(solution)/shard_map/ppermute | solution.py:168
  84.0 13.1 %collective-permute-start.14 = (bf16[4,64,1024]{2,1,0:T(8,128)(2,1)S(1)}, bf16[4,64,1024]{2,1,0:T(8,128)(2,1)S(1)}, u32[]{:S(2)}, u32[]{:S(2)}) collective-permute-start(bf16[4,64,1024]{2,1,0:T(8,128)(2,1)S(1)} %get-tuple-element.39), channel_id=1, source_target_pairs={{16,0},{0,16},{17,1},{1,17},{18,2},{2,18},{19,3},{3,19},{20,4},{4,... | collective-permute-start | bytes 1572872 | tf_op jit(solution)/shard_map/ppermute | solution.py:46
  84.1 14.5 %collective-permute-start.21 = (bf16[128,2176]{1,0:T(8,128)(2,1)S(1)}, bf16[128,2176]{1,0:T(8,128)(2,1)S(1)}, u32[]{:S(2)}, u32[]{:S(2)}) collective-permute-start(bf16[128,2176]{1,0:T(8,128)(2,1)S(1)} %constant_dynamic-update-slice_fusion.2.near_ref), channel_id=1, source_target_pairs={{16,0},{0,16},{17,1},{1,17},{18,2},{2,18},{19,3},{3,19},{20,4},{4,... | collective-permute-start | bytes 1671176 | tf_op jit(solution)/shard_map/ppermute | solution.py:46
  87.9 10.4 %collective-permute-start.13 = (bf16[4,64,1024]{2,1,0:T(8,128)(2,1)S(1)}, bf16[4,64,1024]{2,1,0:T(8,128)(2,1)S(1)}, u32[]{:S(2)}, u32[]{:S(2)}) collective-permute-start(bf16[4,64,1024]{2,1,0:T(8,128)(2,1)S(1)} %get-tuple-element.41), channel_id=1, source_target_pairs={{16,0},{0,16},{17,1},{1,17},{18,2},{2,18},{19,3},{3,19},{20,4},{4,... | collective-permute-start | bytes 1572872 | tf_op jit(solution)/shard_map/ppermute | solution.py:46
  96.3 15.7 %collective-permute-start.26 = (bf16[4,64,1024]{2,1,0:T(8,128)(2,1)S(1)}, bf16[4,64,1024]{2,1,0:T(8,128)(2,1)S(1)}, u32[]{:S(2)}, u32[]{:S(2)}) collective-permute-start(bf16[4,64,1024]{2,1,0:T(8,128)(2,1)S(1)} %get-tuple-element.48), channel_id=1, source_target_pairs={{16,0},{0,16},{17,1},{1,17},{18,2},{2,18},{19,3},{3,19},{20,4},{4,... | collective-permute-start | bytes 1572872 | tf_op jit(solution)/shard_map/ppermute | solution.py:46
  96.4 15.6 %collective-permute-start.23 = (bf16[256,2176]{1,0:T(8,128)(2,1)S(1)}, bf16[256,2176]{1,0:T(8,128)(2,1)S(1)}, u32[]{:S(2)}, u32[]{:S(2)}) collective-permute-start(bf16[256,2176]{1,0:T(8,128)(2,1)S(1)} %constant_dynamic-update-slice_fusion.4.near_ref), channel_id=1, source_target_pairs={{0,2},{1,3},{2,0},{3,1},{4,6},{5,7},{6,4},{7,5},{8,10},{9,11},{10,... | collective-permute-start | bytes 3342344 | tf_op jit(solution)/shard_map/ppermute | solution.py:168
  102.9 9.3 %collective-permute-start.25 = (bf16[4,64,1024]{2,1,0:T(8,128)(2,1)S(1)}, bf16[4,64,1024]{2,1,0:T(8,128)(2,1)S(1)}, u32[]{:S(2)}, u32[]{:S(2)}) collective-permute-start(bf16[4,64,1024]{2,1,0:T(8,128)(2,1)S(1)} %get-tuple-element.51), channel_id=1, source_target_pairs={{16,0},{0,16},{17,1},{1,17},{18,2},{2,18},{19,3},{3,19},{20,4},{4,... | collective-permute-start | bytes 1572872 | tf_op jit(solution)/shard_map/ppermute | solution.py:46
  103.3 16.2 %collective-permute-start.24 = (bf16[256,2176]{1,0:T(8,128)(2,1)S(1)}, bf16[256,2176]{1,0:T(8,128)(2,1)S(1)}, u32[]{:S(2)}, u32[]{:S(2)}) collective-permute-start(bf16[256,2176]{1,0:T(8,128)(2,1)S(1)} %constant_dynamic-update-slice_fusion.4.near_ref), channel_id=1, source_target_pairs={{16,0},{0,16},{17,1},{1,17},{18,2},{2,18},{19,3},{3,19},{20,4},{4,... | collective-permute-start | bytes 3342344 | tf_op jit(solution)/shard_map/ppermute | solution.py:46
  118.3 10.1 %collective-permute-start.30 = (bf16[4,128,1024]{2,1,0:T(8,128)(2,1)S(1)}, bf16[4,128,1024]{2,1,0:T(8,128)(2,1)S(1)}, u32[]{:S(2)}, u32[]{:S(2)}) collective-permute-start(bf16[4,128,1024]{2,1,0:T(8,128)(2,1)S(1)} %get-tuple-element.55), channel_id=1, source_target_pairs={{16,0},{0,16},{17,1},{1,17},{18,2},{2,18},{19,3},{3,19},{20,4},{4,... | collective-permute-start | bytes 3145736 | tf_op jit(solution)/shard_map/ppermute | solution.py:46
  118.9 9.2 %collective-permute-start.29 = (bf16[2,2,64,1024]{3,2,1,0:T(8,128)(2,1)S(1)}, bf16[2,2,64,1024]{3,2,1,0:T(8,128)(2,1)S(1)}, u32[]{:S(2)}, u32[]{:S(2)}) collective-permute-start(bf16[2,2,64,1024]{3,2,1,0:T(8,128)(2,1)S(1)} %pad_maximum_fusion.4), channel_id=1, source_target_pairs={{0,2},{1,3},{2,0},{3,1},{4,6},{5,7},{6,4},{7,5},{8,10},{9,11},{10,... | collective-permute-start | bytes 1572872 | tf_op jit(solution)/shard_map/ppermute | solution.py:168
  129.5 17.2 %collective-permute-start.31 = (bf16[2,2,128,1024]{3,2,1,0:T(8,128)(2,1)S(1)}, bf16[2,2,128,1024]{3,2,1,0:T(8,128)(2,1)S(1)}, u32[]{:S(2)}, u32[]{:S(2)}) collective-permute-start(bf16[2,2,128,1024]{3,2,1,0:T(8,128)(2,1)S(1)} %pad_maximum_fusion), channel_id=1, source_target_pairs={{0,2},{1,3},{2,0},{3,1},{4,6},{5,7},{6,4},{7,5},{8,10},{9,11},{10,... | collective-permute-start | bytes 3145736 | tf_op jit(solution)/shard_map/ppermute | solution.py:168
  130.2 19.0 %collective-permute-start.36 = (bf16[2,64,1024]{2,1,0:T(8,128)(2,1)S(1)}, bf16[2,64,1024]{2,1,0:T(8,128)(2,1)S(1)}, u32[]{:S(2)}, u32[]{:S(2)}) collective-permute-start(bf16[2,64,1024]{2,1,0:T(8,128)(2,1)S(1)} %pad_maximum_fusion.6), channel_id=1, source_target_pairs={{0,1},{1,0},{2,3},{3,2},{4,5},{5,4},{6,7},{7,6},{8,9},{9,8},{10,11... | collective-permute-start | bytes 786440 | tf_op jit(solution)/shard_map/ppermute | solution.py:168
  147.2 14.3 %collective-permute-start.32 = (bf16[2,2,64,1024]{3,2,1,0:T(8,128)(2,1)S(1)}, bf16[2,2,64,1024]{3,2,1,0:T(8,128)(2,1)S(1)}, u32[]{:S(2)}, u32[]{:S(2)}) collective-permute-start(bf16[2,2,64,1024]{3,2,1,0:T(8,128)(2,1)S(1)} %pad_maximum_fusion.3), channel_id=1, source_target_pairs={{0,2},{1,3},{2,0},{3,1},{4,6},{5,7},{6,4},{7,5},{8,10},{9,11},{10,... | collective-permute-start | bytes 1572872 | tf_op jit(solution)/shard_map/ppermute | solution.py:168
  148.3 14.5 %collective-permute-start.34 = (bf16[2,128,1024]{2,1,0:T(8,128)(2,1)S(1)}, bf16[2,128,1024]{2,1,0:T(8,128)(2,1)S(1)}, u32[]{:S(2)}, u32[]{:S(2)}) collective-permute-start(bf16[2,128,1024]{2,1,0:T(8,128)(2,1)S(1)} %pad_maximum_fusion.5), channel_id=1, source_target_pairs={{0,1},{1,0},{2,3},{3,2},{4,5},{5,4},{6,7},{7,6},{8,9},{9,8},{10,11... | collective-permute-start | bytes 1572872 | tf_op jit(solution)/shard_map/ppermute | solution.py:168
  149.3 19.0 %collective-permute-start.37 = (bf16[128,1024]{1,0:T(8,128)(2,1)S(1)}, bf16[128,1024]{1,0:T(8,128)(2,1)S(1)}, u32[]{:S(2)}, u32[]{:S(2)}) collective-permute-start(bf16[128,1024]{1,0:T(8,128)(2,1)S(1)} %pad_maximum_fusion.9), channel_id=1, source_target_pairs={{0,8},{1,9},{2,10},{3,11},{4,12},{5,13},{6,14},{7,15},{8,0},{9,1},... | collective-permute-start | bytes 786440 | tf_op jit(solution)/shard_map/ppermute | solution.py:39
  163.7 8.9 %collective-permute-start.38 = (bf16[128,1024]{1,0:T(8,128)(2,1)}, bf16[128,1024]{1,0:T(8,128)(2,1)S(1)}, u32[]{:S(2)}, u32[]{:S(2)}) collective-permute-start(bf16[128,1024]{1,0:T(8,128)(2,1)} %pad_maximum_fusion.10), channel_id=1, source_target_pairs={{0,12},{1,13},{2,14},{3,15},{4,0},{5,1},{6,2},{7,3},{8,4},{9,5},{1... | collective-permute-start | bytes 786440 | tf_op jit(solution)/shard_map/ppermute | solution.py:39
  166.2 11.9 %collective-permute-start.35 = (bf16[128,1024]{1,0:T(8,128)(2,1)}, bf16[128,1024]{1,0:T(8,128)(2,1)S(1)}, u32[]{:S(2)}, u32[]{:S(2)}) collective-permute-start(bf16[128,1024]{1,0:T(8,128)(2,1)} %pad_maximum_fusion.8), channel_id=1, source_target_pairs={{0,4},{1,5},{2,6},{3,7},{4,8},{5,9},{6,10},{7,11},{8,12},{9,13},{1... | collective-permute-start | bytes 786440 | tf_op jit(solution)/shard_map/ppermute | solution.py:39
  (20 other events, 237.1 us)

commit v6 on v5

--- a/solution.py
+++ b/solution.py
@@ -324,37 +324,41 @@
     )
     weights = (w_gate[0].T, w_up[0].T, w_down[0])
     if planes <= 4:
-        groups = [[0]] + [sorted({i, planes - i}) for i in range(planes // 2, 0, -1)]
+        groups = [[0]] + [sorted({i, planes - i}) for i in range(1, planes // 2 + 1)]
     else:
         groups = [[0]] + [list(range(i, min(i + 8, planes))) for i in range(1, planes, 8)]
     nears, fars = [], []
+    weights = (w_gate[0].T, w_up[0].T, w_down[0])
+    run = functools.partial(
+        expert_outputs, place, weights=weights, experts=experts, cores=cores
+    )
     for number, group in enumerate(groups):
         sent = after(payload, nears[0]) if number > 1 else payload
         column = jnp.concatenate([from_plane(sent, ahead) if ahead else sent for ahead in group])
         if number > 1:
             column = after(column, nears[-1])
         nears.append(jnp.concatenate([column, crossed(column, True)]))
+        if number > 1 and number == len(groups) - 1:
+            outs = run(nears[0], fars[0], waits={})
+            nears[-1] = after(nears[-1], *outs)
         fars.append(crossed(after(nears[-1], *fars[-1:]), False))
-    weights = (w_gate[0].T, w_up[0].T, w_down[0])
-    run = functools.partial(
-        expert_outputs, place, weights=weights, experts=experts, cores=cores
-    )
-    outs = run(nears[0], fars[0], waits={})
-    own_totals = core_totals(outs, cores)
-    own_sent = sent = second_share(own_totals)
-    partial = {}
-    shared = None
-    for number in range(1, len(groups)):
-        outs = run(nears[number], fars[number], waits={0: [outs], cores - 1: [sent]})
+    totals = core_totals(outs, cores)
+    sent = second_share(totals)
+    totals = merged(totals, crossed(after(sent, fars[-1]), False), 2)
+    shared = first_share(totals)
+    partial = {0: (totals, crossed(shared, True))}
+    for number in reversed(range(1, len(groups))):
+        waits = {0: [outs], cores - 1: [sent]}
+        if number < len(groups) - 1:
+            waits[cores - 1] = [sent, shared]
+        outs = run(nears[number], fars[number], waits=waits)
         totals = core_totals(outs, cores)
-        if shared is not None:
-            totals = [after(total, shared) for total in totals]
+        if number < len(groups) - 1:
+            totals = [after(total, late) for total in totals]
         sent = second_share(totals)
         totals = merged(totals, crossed(sent, False), 2)
-        shared = first_share(totals)
-        partial[number] = (totals, crossed(shared, True))
-    totals = merged(own_totals, crossed(after(own_sent, shared), False), 2)
-    partial[0] = (totals, crossed(first_share(totals), True))
+        late = first_share(totals)
+        partial[number] = (totals, crossed(late, True))
     results = {}
     for number, group in enumerate(groups):
         totals, came = partial[number]

time: 179 us -> 186 us (1.039)
  waiting for transfers between devices: 82.3 us -> 94.4 us
  starting transfers between devices: 46.5 us -> 42.7 us
    ppermute x3, waiting for transfers between devices: 11.4 us -> 18.6 us  [from_plane(): lax.ppermute(block, 'blk', [((i + PLANE * ahead) % count, i) for i in ran...]
    ppermute x3, starting transfers between devices: 4.45 us -> 2.27 us  [to_plane(): lax.ppermute(block, 'blk', [(i, (i + PLANE * ahead) % count) for i in ran...]
    ppermute x3, waiting for transfers between devices: 9.79 us -> 11.8 us  [to_plane(): lax.ppermute(block, 'blk', [(i, (i + PLANE * ahead) % count) for i in ran...]
    unnamed x30 -> x28, local copies, waits for them, and re-layouts: 6.2 us -> 6.18 us
  transfers between devices with their start and end apart: 39 -> 39, of which waited for: 20 -> 20; matrix products, arithmetic and copies ran while one was open for 7% -> 6% of each run, Pallas kernels for 15% -> 14%
where the time goes in v6:
time: 186 us
  waiting for transfers between devices  94.4 us (51%)
  starting transfers between devices  42.7 us (23%)
  Pallas kernels  29.9 us (16%)
  other arithmetic  8.9 us (5%)
  local copies, waits for them, and re-layouts  8.69 us (5%)
    ppermute x12, waiting for transfers between devices, crossed(): return lax.ppermute(block, ('tok', 'blk'), route)  47.3 us
    pallas_call x10, Pallas kernels, local_call(): pl.pallas_call(body, in_specs=[scalar] * len(scalars) + [whole] * len(arr...  29.9 us
    ppermute x3, waiting for transfers between devices, from_plane(): lax.ppermute(block, 'blk', [((i + PLANE * ahead) % count, i) for i in ran...  18.6 us
    ppermute x12, starting transfers between devices, crossed(): return lax.ppermute(block, ('tok', 'blk'), route)  14.3 us
    ppermute x3, waiting for transfers between devices, to_plane(): lax.ppermute(block, 'blk', [(i, (i + PLANE * ahead) % count) for i in ran...  11.8 us
    ppermute x6, waiting for transfers between devices, flipped(): lax.ppermute(block, 'blk', [(i, i ^ mask) for i in range(lax.axis_size('b...  9.69 us
    ppermute x2, starting transfers between devices, next_plane(): lax.ppermute(block, 'blk', [(i, i + PLANE) for i in range(count - PLANE)])  8.43 us
    ppermute x6, starting transfers between devices, flipped(): lax.ppermute(block, 'blk', [(i, i ^ mask) for i in range(lax.axis_size('b...  8.32 us
  transfers between devices with their start and end apart: 39, of which 20 were waited for; matrix products, arithmetic and copies ran while one was open for 6% of the time, Pallas kernels for 14%

profile of v6, /device:TPU:0, one launch (start us, length us, event | category | flops | bytes accessed | tf_op | source)
XLA Modules:
  0.0 185.9 jit_solution(13053685346847872608)
XLA Ops:
  4.5 4.9 %collective-permute-start = (bf16[128,1024]{1,0:T(8,128)(2,1)S(1)}, bf16[128,1024]{1,0:T(8,128)(2,1)S(1)}, u32[]{:S(2)}, u32[]{:S(2)}) collective-permute-start(bf16[128,1024]{1,0:T(8,128)(2,1)S(1)} %get-tuple-element.34.rest_0_), channel_id=1, source_target_pairs={{0,4},{1,5},{2,6},{3,7},{4,8},{5,9},{6,10},{7,11},{8,12},{9,13},{1... | collective-permute-start | bytes 786440 | tf_op jit(solution)/shard_map/ppermute | solution.py:27
  9.4 3.5 %collective-permute-start.4 = (bf16[128,1024]{1,0:T(8,128)(2,1)}, bf16[128,1024]{1,0:T(8,128)(2,1)S(1)}, u32[]{:S(2)}, u32[]{:S(2)}) collective-permute-start(bf16[128,1024]{1,0:T(8,128)(2,1)} %rest_0_), channel_id=1, source_target_pairs={{0,4},{1,5},{2,6},{3,7},{4,8},{5,9},{6,10},{7,11},{8,12},{9,13},{1... | collective-permute-start | bytes 786440 | tf_op jit(solution)/shard_map/ppermute | solution.py:27
  13.7 2.4 %collective-permute-done.rest_1_ = bf16[128,1024]{1,0:T(8,128)(2,1)S(1)} collective-permute-done((bf16[128,1024]{1,0:T(8,128)(2,1)S(1)}, bf16[128,1024]{1,0:T(8,128)(2,1)S(1)}, u32[]{:S(2)}, u32[]{:S(2)}) %collective-permute-start) | collective-permute-done | bytes 262176 | tf_op jit(solution)/shard_map/ppermute | solution.py:27
  16.9 2.4 %collective-permute-start.3 = (bf16[128,1024]{1,0:T(8,128)(2,1)S(1)}, bf16[128,1024]{1,0:T(8,128)(2,1)S(1)}, u32[]{:S(2)}, u32[]{:S(2)}) collective-permute-start(bf16[128,1024]{1,0:T(8,128)(2,1)S(1)} %get-tuple-element.81), channel_id=1, source_target_pairs={{0,3},{1,2},{2,1},{3,0},{4,7},{5,6},{6,5},{7,4},{8,11},{9,10},{10,... | collective-permute-start | bytes 786440 | tf_op jit(solution)/shard_map/ppermute | solution.py:22
  22.3 2.4 %collective-permute-start.7 = (bf16[128,1024]{1,0:T(8,128)(2,1)}, bf16[128,1024]{1,0:T(8,128)(2,1)S(1)}, u32[]{:S(2)}, u32[]{:S(2)}) collective-permute-start(bf16[128,1024]{1,0:T(8,128)(2,1)} %get-tuple-element.78), channel_id=1, source_target_pairs={{0,3},{1,2},{2,1},{3,0},{4,7},{5,6},{6,5},{7,4},{8,11},{9,10},{10,... | collective-permute-start | bytes 786440 | tf_op jit(solution)/shard_map/ppermute | solution.py:22
  26.8 1.9 %collective-permute-start.5 = (bf16[128,1024]{1,0:T(8,128)(2,1)}, bf16[128,1024]{1,0:T(8,128)(2,1)S(1)}, u32[]{:S(2)}, u32[]{:S(2)}) collective-permute-start(bf16[128,1024]{1,0:T(8,128)(2,1)} %get-tuple-element.80), channel_id=1, source_target_pairs={{0,1},{1,0},{2,3},{3,2},{4,5},{5,4},{6,7},{7,6},{8,9},{9,8},{10,11... | collective-permute-start | bytes 786440 | tf_op jit(solution)/shard_map/ppermute | solution.py:22
  28.9 1.8 scatter_fusion
  30.7 4.7 %collective-permute-done.2.rest_3_ = bf16[128,1024]{1,0:T(8,128)(2,1)S(1)} collective-permute-done((bf16[128,1024]{1,0:T(8,128)(2,1)}, bf16[128,1024]{1,0:T(8,128)(2,1)S(1)}, u32[]{:S(2)}, u32[]{:S(2)}) %collective-permute-start.2) | collective-permute-done | bytes 262176 | tf_op jit(solution)/shard_map/ppermute | solution.py:22
  35.4 1.9 %shard_map.141.prob_ref = bf16[8,128,640]{2,1,0:T(8,128)(2,1)S(1)} custom-call(s32[2]{0:T(128)S(1)} %pad_add_fusion.place_ref, s32[8]{0:T(128)S(1)} %copy-done.10, bf16[128,1024]{1,0:T(8,128)(2,1)S(1)} %get-tuple-element.33.q_ref, bf16[128,1024]{1,0:T(8,128)(2,1)S(1)} %get-tuple-element.34.rest_0_, bf16[128,1024]{1,0:T(8,128)(2,1)S(1)} %collective-permute-done.rest_1_, ...), custom_call_target="tpu_custom_call" | custom-call | flops 167772160 | bytes 2883584 | tf_op jit(solution)/shard_map/pallas_call | solution.py:140
  38.0 2.7 %collective-permute-done.6.rest_3_ = bf16[128,1024]{1,0:T(8,128)(2,1)S(1)} collective-permute-done((bf16[128,1024]{1,0:T(8,128)(2,1)}, bf16[128,1024]{1,0:T(8,128)(2,1)S(1)}, u32[]{:S(2)}, u32[]{:S(2)}) %collective-permute-start.6) | collective-permute-done | bytes 262176 | tf_op jit(solution)/shard_map/ppermute | solution.py:22
  40.8 2.2 %copy-done.3 = bf16[1024,2048]{1,0:T(8,128)(2,1)S(1)} copy-done((bf16[1024,2048]{1,0:T(8,128)(2,1)S(1)}, bf16[1024,2048]{1,0:T(8,128)(2,1)}, u32[]{:S(2)}) %copy-start.3) | copy-done | bytes 4194328
  43.0 1.7 shard_map.142.rest_0_
  44.7 2.6 %collective-permute-done.8.rest_1_ = f32[128,2048]{1,0:T(8,128)S(1)} collective-permute-done((f32[128,2048]{1,0:T(8,128)S(1)}, f32[128,2048]{1,0:T(8,128)S(1)}, u32[]{:S(2)}, u32[]{:S(2)}) %collective-permute-start.8) | collective-permute-done | bytes 1048608 | tf_op jit(solution)/shard_map/ppermute | solution.py:46
  48.2 2.5 %collective-permute-start.17 = (bf16[64,2176]{1,0:T(8,128)(2,1)S(1)}, bf16[64,2176]{1,0:T(8,128)(2,1)S(1)}, u32[]{:S(2)}, u32[]{:S(2)}) collective-permute-start(bf16[64,2176]{1,0:T(8,128)(2,1)S(1)} %get-tuple-element.44), channel_id=1, source_target_pairs={{12,0},{13,1},{14,2},{15,3},{0,4},{1,5},{2,6},{3,7},{4,8},{5,9},{6... | collective-permute-start | bytes 835592 | tf_op jit(solution)/shard_map/ppermute | solution.py:32
  50.7 2.3 %collective-permute-start.16 = (bf16[64,2176]{1,0:T(8,128)(2,1)S(1)}, bf16[64,2176]{1,0:T(8,128)(2,1)S(1)}, u32[]{:S(2)}, u32[]{:S(2)}) collective-permute-start(bf16[64,2176]{1,0:T(8,128)(2,1)S(1)} %get-tuple-element.44), channel_id=1, source_target_pairs={{4,0},{5,1},{6,2},{7,3},{8,4},{9,5},{10,6},{11,7},{12,8},{13,9},{1... | collective-permute-start | bytes 835592 | tf_op jit(solution)/shard_map/ppermute | solution.py:32
  54.6 5.0 %collective-permute-done.9 = bf16[64,2176]{1,0:T(8,128)(2,1)S(1)} collective-permute-done((bf16[64,2176]{1,0:T(8,128)(2,1)S(1)}, bf16[64,2176]{1,0:T(8,128)(2,1)S(1)}, u32[]{:S(2)}, u32[]{:S(2)}) %collective-permute-start.9) | collective-permute-done | bytes 278560 | tf_op jit(solution)/shard_map/ppermute | solution.py:168
  61.1 4.0 %collective-permute-done.16 = bf16[64,2176]{1,0:T(8,128)(2,1)S(1)} collective-permute-done((bf16[64,2176]{1,0:T(8,128)(2,1)S(1)}, bf16[64,2176]{1,0:T(8,128)(2,1)S(1)}, u32[]{:S(2)}, u32[]{:S(2)}) %collective-permute-start.16) | collective-permute-done | bytes 278560 | tf_op jit(solution)/shard_map/ppermute | solution.py:32
  66.8 7.9 %collective-permute-done.18 = bf16[128,2176]{1,0:T(8,128)(2,1)S(1)} collective-permute-done((bf16[128,2176]{1,0:T(8,128)(2,1)S(1)}, bf16[128,2176]{1,0:T(8,128)(2,1)S(1)}, u32[]{:S(2)}, u32[]{:S(2)}) %collective-permute-start.18) | collective-permute-done | bytes 557088 | tf_op jit(solution)/shard_map/ppermute | solution.py:168
  77.7 14.6 %collective-permute-done.15 = bf16[64,2176]{1,0:T(8,128)(2,1)S(1)} collective-permute-done((bf16[64,2176]{1,0:T(8,128)(2,1)S(1)}, bf16[64,2176]{1,0:T(8,128)(2,1)S(1)}, u32[]{:S(2)}, u32[]{:S(2)}) %collective-permute-start.15) | collective-permute-done | bytes 278560 | tf_op jit(solution)/shard_map/ppermute | solution.py:32
  93.8 3.2 %shard_map.144 = (bf16[4,64,1024]{2,1,0:T(8,128)(2,1)S(1)}, bf16[4,64,1024]{2,1,0:T(8,128)(2,1)S(1)}) custom-call(s32[2]{0:T(128)S(1)} %pad_add_fusion.place_ref, bf16[128,2176]{1,0:T(8,128)(2,1)S(1)} %constant_dynamic-update-slice_fusion.near_ref, bf16[128,2176]{1,0:T(8,128)(2,1)S(1)} %collective-permute-done.10.far_ref, bf16[704,2048]{1,0:T(8,128)(2,1)S(1)} %bitcast.82, ...), custom_call_target="tpu_custom_call" | custom-call | flops 256 | bytes 256 | tf_op jit(solution)/shard_map/pallas_call | solution.py:140
  98.9 3.2 %shard_map.145 = (bf16[4,64,1024]{2,1,0:T(8,128)(2,1)S(1)}, bf16[4,64,1024]{2,1,0:T(8,128)(2,1)S(1)}) custom-call(s32[2]{0:T(128)S(1)} %pad_add_fusion.place_ref, bf16[128,2176]{1,0:T(8,128)(2,1)S(1)} %collective-permute-done.11.near_ref, bf16[128,2176]{1,0:T(8,128)(2,1)S(1)} %collective-permute-done.12.far_ref, bf16[704,2048]{1,0:T(8,128)(2,1)S(1)} %bitcast.83, ...), custom_call_target="tpu_custom_call" | custom-call | flops 256 | bytes 256 | tf_op jit(solution)/shard_map/pallas_call | solution.py:140
  103.8 7.9 %collective-permute-done.21.far_ref = bf16[128,2176]{1,0:T(8,128)(2,1)S(1)} collective-permute-done((bf16[128,2176]{1,0:T(8,128)(2,1)S(1)}, bf16[128,2176]{1,0:T(8,128)(2,1)S(1)}, u32[]{:S(2)}, u32[]{:S(2)}) %collective-permute-start.21) | collective-permute-done | bytes 557088 | tf_op jit(solution)/shard_map/ppermute | solution.py:168
  111.7 3.2 %shard_map.146 = (bf16[4,64,1024]{2,1,0:T(8,128)(2,1)S(1)}, bf16[4,64,1024]{2,1,0:T(8,128)(2,1)S(1)}) custom-call(s32[2]{0:T(128)S(1)} %pad_add_fusion.place_ref, bf16[128,2176]{1,0:T(8,128)(2,1)S(1)} %pad_maximum_fusion.2.near_ref, bf16[128,2176]{1,0:T(8,128)(2,1)S(1)} %collective-permute-done.21.far_ref, bf16[704,2048]{1,0:T(8,128)(2,1)S(1)} %bitcast.84, ...), custom_call_target="tpu_custom_call" | custom-call | flops 256 | bytes 256 | tf_op jit(solution)/shard_map/pallas_call | solution.py:140
  115.8 1.9 %collective-permute-done.25.far_ref = bf16[128,2176]{1,0:T(8,128)(2,1)S(1)} collective-permute-done((bf16[128,2176]{1,0:T(8,128)(2,1)S(1)}, bf16[128,2176]{1,0:T(8,128)(2,1)S(1)}, u32[]{:S(2)}, u32[]{:S(2)}) %collective-permute-start.25) | collective-permute-done | bytes 557088 | tf_op jit(solution)/shard_map/ppermute | solution.py:46
  117.7 3.2 %shard_map.147 = (bf16[4,64,1024]{2,1,0:T(8,128)(2,1)S(1)}, bf16[4,64,1024]{2,1,0:T(8,128)(2,1)S(1)}) custom-call(s32[2]{0:T(128)S(1)} %pad_add_fusion.place_ref, bf16[128,2176]{1,0:T(8,128)(2,1)S(1)} %collective-permute-done.24.near_ref, bf16[128,2176]{1,0:T(8,128)(2,1)S(1)} %collective-permute-done.25.far_ref, bf16[704,2048]{1,0:T(8,128)(2,1)S(1)} %bitcast.85, ...), custom_call_target="tpu_custom_call" | custom-call | flops 256 | bytes 256 | tf_op jit(solution)/shard_map/pallas_call | solution.py:140
  122.8 5.9 %shard_map.148 = (bf16[4,128,1024]{2,1,0:T(8,128)(2,1)S(1)}, bf16[4,128,1024]{2,1,0:T(8,128)(2,1)S(1)}) custom-call(s32[2]{0:T(128)S(1)} %pad_add_fusion.place_ref, bf16[256,2176]{1,0:T(8,128)(2,1)S(1)} %constant_dynamic-update-slice_fusion.2.near_ref, bf16[256,2176]{1,0:T(8,128)(2,1)S(1)} %collective-permute-done.20.far_ref, ...), custom_call_target="tpu_custom_call" | custom-call | flops 512 | bytes 512 | tf_op jit(solution)/shard_map/pallas_call | solution.py:140
  131.1 5.7 %shard_map.149 = (bf16[4,128,1024]{2,1,0:T(8,128)(2,1)S(1)}, bf16[4,128,1024]{2,1,0:T(8,128)(2,1)S(1)}) custom-call(s32[2]{0:T(128)S(1)} %pad_add_fusion.place_ref, bf16[256,2176]{1,0:T(8,128)(2,1)S(1)} %collective-permute-done.26.near_ref, bf16[256,2176]{1,0:T(8,128)(2,1)S(1)} %collective-permute-done.29.far_ref, bf16[704,2048]{1,0:T(8,128)(2,1)S(1)} %bitcast.87, ...), custom_call_target="tpu_custom_call" | custom-call | flops 512 | bytes 512 | tf_op jit(solution)/shard_map/pallas_call | solution.py:140
  136.8 2.1 %collective-permute-done.31 = bf16[2,2,64,1024]{3,2,1,0:T(8,128)(2,1)S(1)} collective-permute-done((bf16[2,2,64,1024]{3,2,1,0:T(8,128)(2,1)S(1)}, bf16[2,2,64,1024]{3,2,1,0:T(8,128)(2,1)S(1)}, u32[]{:S(2)}, u32[]{:S(2)}) %collective-permute-start.31) | collective-permute-done | bytes 524320 | tf_op jit(solution)/shard_map/ppermute | solution.py:168
  142.4 15.7 %collective-permute-done.33 = bf16[2,2,128,1024]{3,2,1,0:T(8,128)(2,1)S(1)} collective-permute-done((bf16[2,2,128,1024]{3,2,1,0:T(8,128)(2,1)S(1)}, bf16[2,2,128,1024]{3,2,1,0:T(8,128)(2,1)S(1)}, u32[]{:S(2)}, u32[]{:S(2)}) %collective-permute-start.33) | collective-permute-done | bytes 1048608 | tf_op jit(solution)/shard_map/ppermute | solution.py:168
  160.8 7.0 %collective-permute-done.34 = bf16[2,128,1024]{2,1,0:T(8,128)(2,1)S(1)} collective-permute-done((bf16[2,128,1024]{2,1,0:T(8,128)(2,1)S(1)}, bf16[2,128,1024]{2,1,0:T(8,128)(2,1)S(1)}, u32[]{:S(2)}, u32[]{:S(2)}) %collective-permute-start.34) | collective-permute-done | bytes 524320 | tf_op jit(solution)/shard_map/ppermute | solution.py:168
  168.7 2.2 %collective-permute-start.38 = (bf16[128,1024]{1,0:T(8,128)(2,1)}, bf16[128,1024]{1,0:T(8,128)(2,1)S(1)}, u32[]{:S(2)}, u32[]{:S(2)}) collective-permute-start(bf16[128,1024]{1,0:T(8,128)(2,1)} %pad_maximum_fusion.11), channel_id=1, source_target_pairs={{0,12},{1,13},{2,14},{3,15},{4,0},{5,1},{6,2},{7,3},{8,4},{9,5},{1... | collective-permute-start | bytes 786440 | tf_op jit(solution)/shard_map/ppermute | solution.py:39
  173.7 11.1 %collective-permute-done.38 = bf16[128,1024]{1,0:T(8,128)(2,1)S(1)} collective-permute-done((bf16[128,1024]{1,0:T(8,128)(2,1)}, bf16[128,1024]{1,0:T(8,128)(2,1)S(1)}, u32[]{:S(2)}, u32[]{:S(2)}) %collective-permute-start.38) | collective-permute-done | bytes 262176 | tf_op jit(solution)/shard_map/ppermute | solution.py:39
  (139 shorter events, 40.7 us)
Async XLA Ops:
  4.5 11.6 %collective-permute-start = (bf16[128,1024]{1,0:T(8,128)(2,1)S(1)}, bf16[128,1024]{1,0:T(8,128)(2,1)S(1)}, u32[]{:S(2)}, u32[]{:S(2)}) collective-permute-start(bf16[128,1024]{1,0:T(8,128)(2,1)S(1)} %get-tuple-element.34.rest_0_), channel_id=1, source_target_pairs={{0,4},{1,5},{2,6},{3,7},{4,8},{5,9},{6,10},{7,11},{8,12},{9,13},{1... | collective-permute-start | bytes 786440 | tf_op jit(solution)/shard_map/ppermute | solution.py:27
  9.4 11.9 %collective-permute-start.4 = (bf16[128,1024]{1,0:T(8,128)(2,1)}, bf16[128,1024]{1,0:T(8,128)(2,1)S(1)}, u32[]{:S(2)}, u32[]{:S(2)}) collective-permute-start(bf16[128,1024]{1,0:T(8,128)(2,1)} %rest_0_), channel_id=1, source_target_pairs={{0,4},{1,5},{2,6},{3,7},{4,8},{5,9},{6,10},{7,11},{8,12},{9,13},{1... | collective-permute-start | bytes 786440 | tf_op jit(solution)/shard_map/ppermute | solution.py:27
  16.9 9.8 %collective-permute-start.3 = (bf16[128,1024]{1,0:T(8,128)(2,1)S(1)}, bf16[128,1024]{1,0:T(8,128)(2,1)S(1)}, u32[]{:S(2)}, u32[]{:S(2)}) collective-permute-start(bf16[128,1024]{1,0:T(8,128)(2,1)S(1)} %get-tuple-element.81), channel_id=1, source_target_pairs={{0,3},{1,2},{2,1},{3,0},{4,7},{5,6},{6,5},{7,4},{8,11},{9,10},{10,... | collective-permute-start | bytes 786440 | tf_op jit(solution)/shard_map/ppermute | solution.py:22
  20.2 15.1 %collective-permute-start.2 = (bf16[128,1024]{1,0:T(8,128)(2,1)}, bf16[128,1024]{1,0:T(8,128)(2,1)S(1)}, u32[]{:S(2)}, u32[]{:S(2)}) collective-permute-start(bf16[128,1024]{1,0:T(8,128)(2,1)} %get-tuple-element.82), channel_id=1, source_target_pairs={{0,2},{1,3},{2,0},{3,1},{4,6},{5,7},{6,4},{7,5},{8,10},{9,11},{10,... | collective-permute-start | bytes 786440 | tf_op jit(solution)/shard_map/ppermute | solution.py:22
  20.7 14.6 %collective-permute-start.1 = (bf16[128,1024]{1,0:T(8,128)(2,1)}, bf16[128,1024]{1,0:T(8,128)(2,1)S(1)}, u32[]{:S(2)}, u32[]{:S(2)}) collective-permute-start(bf16[128,1024]{1,0:T(8,128)(2,1)} %get-tuple-element.83), channel_id=1, source_target_pairs={{0,1},{1,0},{2,3},{3,2},{4,5},{5,4},{6,7},{7,6},{8,9},{9,8},{10,11... | collective-permute-start | bytes 786440 | tf_op jit(solution)/shard_map/ppermute | solution.py:22
  22.3 15.7 %collective-permute-start.7 = (bf16[128,1024]{1,0:T(8,128)(2,1)}, bf16[128,1024]{1,0:T(8,128)(2,1)S(1)}, u32[]{:S(2)}, u32[]{:S(2)}) collective-permute-start(bf16[128,1024]{1,0:T(8,128)(2,1)} %get-tuple-element.78), channel_id=1, source_target_pairs={{0,3},{1,2},{2,1},{3,0},{4,7},{5,6},{6,5},{7,4},{8,11},{9,10},{10,... | collective-permute-start | bytes 786440 | tf_op jit(solution)/shard_map/ppermute | solution.py:22
  24.7 16.0 %collective-permute-start.6 = (bf16[128,1024]{1,0:T(8,128)(2,1)}, bf16[128,1024]{1,0:T(8,128)(2,1)S(1)}, u32[]{:S(2)}, u32[]{:S(2)}) collective-permute-start(bf16[128,1024]{1,0:T(8,128)(2,1)} %get-tuple-element.79), channel_id=1, source_target_pairs={{0,2},{1,3},{2,0},{3,1},{4,6},{5,7},{6,4},{7,5},{8,10},{9,11},{10,... | collective-permute-start | bytes 786440 | tf_op jit(solution)/shard_map/ppermute | solution.py:22
  26.8 14.0 %collective-permute-start.5 = (bf16[128,1024]{1,0:T(8,128)(2,1)}, bf16[128,1024]{1,0:T(8,128)(2,1)S(1)}, u32[]{:S(2)}, u32[]{:S(2)}) collective-permute-start(bf16[128,1024]{1,0:T(8,128)(2,1)} %get-tuple-element.80), channel_id=1, source_target_pairs={{0,1},{1,0},{2,3},{3,2},{4,5},{5,4},{6,7},{7,6},{8,9},{9,8},{10,11... | collective-permute-start | bytes 786440 | tf_op jit(solution)/shard_map/ppermute | solution.py:22
  48.2 12.9 %collective-permute-start.17 = (bf16[64,2176]{1,0:T(8,128)(2,1)S(1)}, bf16[64,2176]{1,0:T(8,128)(2,1)S(1)}, u32[]{:S(2)}, u32[]{:S(2)}) collective-permute-start(bf16[64,2176]{1,0:T(8,128)(2,1)S(1)} %get-tuple-element.44), channel_id=1, source_target_pairs={{12,0},{13,1},{14,2},{15,3},{0,4},{1,5},{2,6},{3,7},{4,8},{5,9},{6... | collective-permute-start | bytes 835592 | tf_op jit(solution)/shard_map/ppermute | solution.py:32
  50.7 14.4 %collective-permute-start.16 = (bf16[64,2176]{1,0:T(8,128)(2,1)S(1)}, bf16[64,2176]{1,0:T(8,128)(2,1)S(1)}, u32[]{:S(2)}, u32[]{:S(2)}) collective-permute-start(bf16[64,2176]{1,0:T(8,128)(2,1)S(1)} %get-tuple-element.44), channel_id=1, source_target_pairs={{4,0},{5,1},{6,2},{7,3},{8,4},{9,5},{10,6},{11,7},{12,8},{13,9},{1... | collective-permute-start | bytes 835592 | tf_op jit(solution)/shard_map/ppermute | solution.py:32
  59.6 15.2 %collective-permute-start.10 = (bf16[128,2176]{1,0:T(8,128)(2,1)S(1)}, bf16[128,2176]{1,0:T(8,128)(2,1)S(1)}, u32[]{:S(2)}, u32[]{:S(2)}) collective-permute-start(bf16[128,2176]{1,0:T(8,128)(2,1)S(1)} %constant_dynamic-update-slice_fusion.near_ref), channel_id=1, source_target_pairs={{0,2},{1,3},{2,0},{3,1},{4,6},{5,7},{6,4},{7,5},{8,10},{9,11},{10,... | collective-permute-start | bytes 1671176 | tf_op jit(solution)/shard_map/ppermute | solution.py:168
  65.2 9.6 %collective-permute-start.18 = (bf16[128,2176]{1,0:T(8,128)(2,1)S(1)}, bf16[128,2176]{1,0:T(8,128)(2,1)S(1)}, u32[]{:S(2)}, u32[]{:S(2)}) collective-permute-start(bf16[128,2176]{1,0:T(8,128)(2,1)S(1)} %pad_maximum_fusion.1), channel_id=1, source_target_pairs={{0,1},{1,0},{2,3},{3,2},{4,5},{5,4},{6,7},{7,6},{8,9},{9,8},{10,11... | collective-permute-start | bytes 1671176 | tf_op jit(solution)/shard_map/ppermute | solution.py:168
  74.8 27.3 %collective-permute-start.20 = (bf16[256,2176]{1,0:T(8,128)(2,1)S(1)}, bf16[256,2176]{1,0:T(8,128)(2,1)S(1)}, u32[]{:S(2)}, u32[]{:S(2)}) collective-permute-start(bf16[256,2176]{1,0:T(8,128)(2,1)S(1)} %constant_dynamic-update-slice_fusion.2.near_ref), channel_id=1, source_target_pairs={{0,2},{1,3},{2,0},{3,1},{4,6},{5,7},{6,4},{7,5},{8,10},{9,11},{10,... | collective-permute-start | bytes 3342344 | tf_op jit(solution)/shard_map/ppermute | solution.py:168
  76.4 21.2 %collective-permute-start.11 = (bf16[128,2176]{1,0:T(8,128)(2,1)S(1)}, bf16[128,2176]{1,0:T(8,128)(2,1)S(1)}, u32[]{:S(2)}, u32[]{:S(2)}) collective-permute-start(bf16[128,2176]{1,0:T(8,128)(2,1)S(1)} %constant_dynamic-update-slice_fusion.near_ref), channel_id=1, source_target_pairs={{16,0},{0,16},{17,1},{1,17},{18,2},{2,18},{19,3},{3,19},{20,4},{4,... | collective-permute-start | bytes 1671176 | tf_op jit(solution)/shard_map/ppermute | solution.py:46
  76.4 15.9 %collective-permute-start.15 = (bf16[64,2176]{1,0:T(8,128)(2,1)S(1)}, bf16[64,2176]{1,0:T(8,128)(2,1)S(1)}, u32[]{:S(2)}, u32[]{:S(2)}) collective-permute-start(bf16[64,2176]{1,0:T(8,128)(2,1)S(1)} %get-tuple-element.44), channel_id=1, source_target_pairs={{8,0},{9,1},{10,2},{11,3},{12,4},{13,5},{14,6},{15,7},{0,8},{1,9},... | collective-permute-start | bytes 835592 | tf_op jit(solution)/shard_map/ppermute | solution.py:32
  102.1 9.6 %collective-permute-start.21 = (bf16[128,2176]{1,0:T(8,128)(2,1)S(1)}, bf16[128,2176]{1,0:T(8,128)(2,1)S(1)}, u32[]{:S(2)}, u32[]{:S(2)}) collective-permute-start(bf16[128,2176]{1,0:T(8,128)(2,1)S(1)} %pad_maximum_fusion.2.near_ref), channel_id=1, source_target_pairs={{0,2},{1,3},{2,0},{3,1},{4,6},{5,7},{6,4},{7,5},{8,10},{9,11},{10,... | collective-permute-start | bytes 1671176 | tf_op jit(solution)/shard_map/ppermute | solution.py:168
  103.1 12.4 %collective-permute-start.13 = (bf16[4,64,1024]{2,1,0:T(8,128)(2,1)S(1)}, bf16[4,64,1024]{2,1,0:T(8,128)(2,1)S(1)}, u32[]{:S(2)}, u32[]{:S(2)}) collective-permute-start(bf16[4,64,1024]{2,1,0:T(8,128)(2,1)S(1)} %get-tuple-element.42), channel_id=1, source_target_pairs={{16,0},{0,16},{17,1},{1,17},{18,2},{2,18},{19,3},{3,19},{20,4},{4,... | collective-permute-start | bytes 1572872 | tf_op jit(solution)/shard_map/ppermute | solution.py:46
  103.1 12.7 %collective-permute-start.24 = (bf16[128,2176]{1,0:T(8,128)(2,1)S(1)}, bf16[128,2176]{1,0:T(8,128)(2,1)S(1)}, u32[]{:S(2)}, u32[]{:S(2)}) collective-permute-start(bf16[128,2176]{1,0:T(8,128)(2,1)S(1)} %pad_maximum_fusion.2.near_ref), channel_id=1, source_target_pairs={{16,0},{0,16},{17,1},{1,17},{18,2},{2,18},{19,3},{3,19},{20,4},{4,... | collective-permute-start | bytes 1671176 | tf_op jit(solution)/shard_map/ppermute | solution.py:46
  114.9 7.6 %collective-permute-start.28 = (bf16[4,64,1024]{2,1,0:T(8,128)(2,1)S(1)}, bf16[4,64,1024]{2,1,0:T(8,128)(2,1)S(1)}, u32[]{:S(2)}, u32[]{:S(2)}) collective-permute-start(bf16[4,64,1024]{2,1,0:T(8,128)(2,1)S(1)} %get-tuple-element.52), channel_id=1, source_target_pairs={{16,0},{0,16},{17,1},{1,17},{18,2},{2,18},{19,3},{3,19},{20,4},{4,... | collective-permute-start | bytes 1572872 | tf_op jit(solution)/shard_map/ppermute | solution.py:46
  120.9 8.5 %collective-permute-start.27 = (bf16[4,64,1024]{2,1,0:T(8,128)(2,1)S(1)}, bf16[4,64,1024]{2,1,0:T(8,128)(2,1)S(1)}, u32[]{:S(2)}, u32[]{:S(2)}) collective-permute-start(bf16[4,64,1024]{2,1,0:T(8,128)(2,1)S(1)} %get-tuple-element.55), channel_id=1, source_target_pairs={{16,0},{0,16},{17,1},{1,17},{18,2},{2,18},{19,3},{3,19},{20,4},{4,... | collective-permute-start | bytes 1572872 | tf_op jit(solution)/shard_map/ppermute | solution.py:46
  121.1 9.9 %collective-permute-start.26 = (bf16[256,2176]{1,0:T(8,128)(2,1)S(1)}, bf16[256,2176]{1,0:T(8,128)(2,1)S(1)}, u32[]{:S(2)}, u32[]{:S(2)}) collective-permute-start(bf16[256,2176]{1,0:T(8,128)(2,1)S(1)} %constant_dynamic-update-slice_fusion.2.near_ref), channel_id=1, source_target_pairs={{16,0},{0,16},{17,1},{1,17},{18,2},{2,18},{19,3},{3,19},{20,4},{4,... | collective-permute-start | bytes 3342344 | tf_op jit(solution)/shard_map/ppermute | solution.py:46
  121.5 9.6 %collective-permute-start.29 = (bf16[256,2176]{1,0:T(8,128)(2,1)S(1)}, bf16[256,2176]{1,0:T(8,128)(2,1)S(1)}, u32[]{:S(2)}, u32[]{:S(2)}) collective-permute-start(bf16[256,2176]{1,0:T(8,128)(2,1)S(1)} %collective-permute-done.20.far_ref), channel_id=1, source_target_pairs={{16,0},{0,16},{17,1},{1,17},{18,2},{2,18},{19,3},{3,19},{20,4},{4,... | collective-permute-start | bytes 3342344 | tf_op jit(solution)/shard_map/ppermute | solution.py:46
  121.6 9.2 %collective-permute-start.22 = (bf16[2,2,64,1024]{3,2,1,0:T(8,128)(2,1)S(1)}, bf16[2,2,64,1024]{3,2,1,0:T(8,128)(2,1)S(1)}, u32[]{:S(2)}, u32[]{:S(2)}) collective-permute-start(bf16[2,2,64,1024]{3,2,1,0:T(8,128)(2,1)S(1)} %pad_maximum_fusion.4), channel_id=1, source_target_pairs={{0,2},{1,3},{2,0},{3,1},{4,6},{5,7},{6,4},{7,5},{8,10},{9,11},{10,... | collective-permute-start | bytes 1572872 | tf_op jit(solution)/shard_map/ppermute | solution.py:168
  128.7 10.5 %collective-permute-start.32 = (bf16[4,128,1024]{2,1,0:T(8,128)(2,1)S(1)}, bf16[4,128,1024]{2,1,0:T(8,128)(2,1)S(1)}, u32[]{:S(2)}, u32[]{:S(2)}) collective-permute-start(bf16[4,128,1024]{2,1,0:T(8,128)(2,1)S(1)} %get-tuple-element.58), channel_id=1, source_target_pairs={{16,0},{0,16},{17,1},{1,17},{18,2},{2,18},{19,3},{3,19},{20,4},{4,... | collective-permute-start | bytes 3145736 | tf_op jit(solution)/shard_map/ppermute | solution.py:46
  129.7 9.2 %collective-permute-start.31 = (bf16[2,2,64,1024]{3,2,1,0:T(8,128)(2,1)S(1)}, bf16[2,2,64,1024]{3,2,1,0:T(8,128)(2,1)S(1)}, u32[]{:S(2)}, u32[]{:S(2)}) collective-permute-start(bf16[2,2,64,1024]{3,2,1,0:T(8,128)(2,1)S(1)} %pad_maximum_fusion.5), channel_id=1, source_target_pairs={{0,2},{1,3},{2,0},{3,1},{4,6},{5,7},{6,4},{7,5},{8,10},{9,11},{10,... | collective-permute-start | bytes 1572872 | tf_op jit(solution)/shard_map/ppermute | solution.py:168
  140.3 17.7 %collective-permute-start.33 = (bf16[2,2,128,1024]{3,2,1,0:T(8,128)(2,1)S(1)}, bf16[2,2,128,1024]{3,2,1,0:T(8,128)(2,1)S(1)}, u32[]{:S(2)}, u32[]{:S(2)}) collective-permute-start(bf16[2,2,128,1024]{3,2,1,0:T(8,128)(2,1)S(1)} %pad_maximum_fusion), channel_id=1, source_target_pairs={{0,2},{1,3},{2,0},{3,1},{4,6},{5,7},{6,4},{7,5},{8,10},{9,11},{10,... | collective-permute-start | bytes 3145736 | tf_op jit(solution)/shard_map/ppermute | solution.py:168
  141.2 19.4 %collective-permute-start.36 = (bf16[2,64,1024]{2,1,0:T(8,128)(2,1)S(1)}, bf16[2,64,1024]{2,1,0:T(8,128)(2,1)S(1)}, u32[]{:S(2)}, u32[]{:S(2)}) collective-permute-start(bf16[2,64,1024]{2,1,0:T(8,128)(2,1)S(1)} %pad_maximum_fusion.8), channel_id=1, source_target_pairs={{0,1},{1,0},{2,3},{3,2},{4,5},{5,4},{6,7},{7,6},{8,9},{9,8},{10,11... | collective-permute-start | bytes 786440 | tf_op jit(solution)/shard_map/ppermute | solution.py:168
  158.5 9.2 %collective-permute-start.34 = (bf16[2,128,1024]{2,1,0:T(8,128)(2,1)S(1)}, bf16[2,128,1024]{2,1,0:T(8,128)(2,1)S(1)}, u32[]{:S(2)}, u32[]{:S(2)}) collective-permute-start(bf16[2,128,1024]{2,1,0:T(8,128)(2,1)S(1)} %pad_maximum_fusion.6), channel_id=1, source_target_pairs={{0,1},{1,0},{2,3},{3,2},{4,5},{5,4},{6,7},{7,6},{8,9},{9,8},{10,11... | collective-permute-start | bytes 1572872 | tf_op jit(solution)/shard_map/ppermute | solution.py:168
  159.3 13.7 %collective-permute-start.23 = (bf16[2,64,1024]{2,1,0:T(8,128)(2,1)S(1)}, bf16[2,64,1024]{2,1,0:T(8,128)(2,1)S(1)}, u32[]{:S(2)}, u32[]{:S(2)}) collective-permute-start(bf16[2,64,1024]{2,1,0:T(8,128)(2,1)S(1)} %pad_maximum_fusion.7), channel_id=1, source_target_pairs={{0,1},{1,0},{2,3},{3,2},{4,5},{5,4},{6,7},{7,6},{8,9},{9,8},{10,11... | collective-permute-start | bytes 786440 | tf_op jit(solution)/shard_map/ppermute | solution.py:168
  160.7 13.0 %collective-permute-start.37 = (bf16[128,1024]{1,0:T(8,128)(2,1)S(1)}, bf16[128,1024]{1,0:T(8,128)(2,1)S(1)}, u32[]{:S(2)}, u32[]{:S(2)}) collective-permute-start(bf16[128,1024]{1,0:T(8,128)(2,1)S(1)} %pad_maximum_fusion.10), channel_id=1, source_target_pairs={{0,8},{1,9},{2,10},{3,11},{4,12},{5,13},{6,14},{7,15},{8,0},{9,1},... | collective-permute-start | bytes 786440 | tf_op jit(solution)/shard_map/ppermute | solution.py:39
  168.7 16.1 %collective-permute-start.38 = (bf16[128,1024]{1,0:T(8,128)(2,1)}, bf16[128,1024]{1,0:T(8,128)(2,1)S(1)}, u32[]{:S(2)}, u32[]{:S(2)}) collective-permute-start(bf16[128,1024]{1,0:T(8,128)(2,1)} %pad_maximum_fusion.11), channel_id=1, source_target_pairs={{0,12},{1,13},{2,14},{3,15},{4,0},{5,1},{6,2},{7,3},{8,4},{9,5},{1... | collective-permute-start | bytes 786440 | tf_op jit(solution)/shard_map/ppermute | solution.py:39
  171.6 13.2 %collective-permute-start.35 = (bf16[128,1024]{1,0:T(8,128)(2,1)}, bf16[128,1024]{1,0:T(8,128)(2,1)S(1)}, u32[]{:S(2)}, u32[]{:S(2)}) collective-permute-start(bf16[128,1024]{1,0:T(8,128)(2,1)} %pad_maximum_fusion.9), channel_id=1, source_target_pairs={{0,4},{1,5},{2,6},{3,7},{4,8},{5,9},{6,10},{7,11},{8,12},{9,13},{1... | collective-permute-start | bytes 786440 | tf_op jit(solution)/shard_map/ppermute | solution.py:39
  (19 other events, 216.1 us)

commit v7 on v6

--- a/solution.py
+++ b/solution.py
@@ -29,16 +29,18 @@
 
 def from_plane(block, ahead):
     count = lax.axis_size("blk")
-    return lax.ppermute(
-        block, "blk", [((i + PLANE * ahead) % count, i) for i in range(count)]
-    )
+    with jax.named_scope(f"from_plane_{ahead}"):
+        return lax.ppermute(
+            block, "blk", [((i + PLANE * ahead) % count, i) for i in range(count)]
+        )
 
 
 def to_plane(block, ahead):
     count = lax.axis_size("blk")
-    return lax.ppermute(
-        block, "blk", [(i, (i + PLANE * ahead) % count) for i in range(count)]
-    )
+    with jax.named_scope(f"to_plane_{ahead}"):
+        return lax.ppermute(
+            block, "blk", [(i, (i + PLANE * ahead) % count) for i in range(count)]
+        )
 
 
 def from_core(block, ahead):
@@ -159,13 +161,14 @@
     return jnp.pad(lanes, ((0, 0), (0, -lanes.shape[1] % 128)))
 
 
-def crossed(block, first):
+def crossed(block, first, name="flip"):
     cores, count = lax.axis_size("tok"), lax.axis_size("blk")
     route = []
     for core in range(cores):
         mask = 1 if (core % 2 == 0) == first else 2
         route += [(core * count + i, core * count + (i ^ mask)) for i in range(count)]
-    return lax.ppermute(block, ("tok", "blk"), route)
+    with jax.named_scope(name):
+        return lax.ppermute(block, ("tok", "blk"), route)
 
 
 def expert_kernel(experts, ahead, place_ref, near_ref, far_ref, gate_ref, up_ref, down_ref, *outs):
@@ -201,7 +204,7 @@
         [out_shape] * parts,
         [place],
         [near, far, w_gate, w_up, w_down],
-        flops=count,
+        flops=6 * count * width * units,
         moved=count,
     )
 
@@ -337,16 +340,18 @@
         column = jnp.concatenate([from_plane(sent, ahead) if ahead else sent for ahead in group])
         if number > 1:
             column = after(column, nears[-1])
-        nears.append(jnp.concatenate([column, crossed(column, True)]))
+        nears.append(jnp.concatenate([column, crossed(column, True, f"gather_first_{number}")]))
         if number > 1 and number == len(groups) - 1:
             outs = run(nears[0], fars[0], waits={})
             nears[-1] = after(nears[-1], *outs)
-        fars.append(crossed(after(nears[-1], *fars[-1:]), False))
+        fars.append(crossed(after(nears[-1], *fars[-1:]), False, f"gather_second_{number}"))
     totals = core_totals(outs, cores)
     sent = second_share(totals)
-    totals = merged(totals, crossed(after(sent, fars[-1]), False), 2)
+    totals = merged(totals, crossed(after(sent, fars[-1]), False, "scatter_second_0"), 2)
     shared = first_share(totals)
-    partial = {0: (totals, crossed(shared, True))}
+    partial = (totals, crossed(shared, True, "scatter_first_0"))
+    results = {}
+    returned = []
     for number in reversed(range(1, len(groups))):
         waits = {0: [outs], cores - 1: [sent]}
         if number < len(groups) - 1:
@@ -356,20 +361,19 @@
         if number < len(groups) - 1:
             totals = [after(total, late) for total in totals]
         sent = second_share(totals)
-        totals = merged(totals, crossed(sent, False), 2)
-        late = first_share(totals)
-        partial[number] = (totals, crossed(late, True))
-    results = {}
-    for number, group in enumerate(groups):
-        totals, came = partial[number]
+        totals = merged(totals, crossed(sent, False, f"scatter_second_{number}"), 2)
+        late = after(first_share(totals), *results.values())
+        came = crossed(late, True, f"scatter_first_{number}")
         rows_of = merged([total[0] for total in totals], came, None)
-        for i, ahead in enumerate(group):
-            results[ahead] = jnp.concatenate(
-                [rows[i * part_rows : (i + 1) * part_rows] for rows in rows_of]
-            )
-    moe = results[0]
-    for ahead in range(1, planes):
-        moe = moe + wide(to_plane(narrow(results[ahead]), ahead))
+        results = {}
+        for i, ahead in enumerate(groups[number]):
+            piece = [rows[i * part_rows : (i + 1) * part_rows] for rows in rows_of]
+            results[ahead] = after(narrow(jnp.concatenate(piece)), *returned[-1:])
+        for ahead, block in results.items():
+            returned.append(to_plane(block, ahead))
+    totals, came = partial
+    moe = jnp.concatenate(merged([total[0] for total in totals], came, None))
+    moe = moe + sum(wide(block) for block in returned)
     moe = jnp.roll(moe.reshape(cores, part_rows, col_width), tok_index, axis=0)
     moe = moe.reshape(tok_rows, col_width)
     layer_out = (own_share.astype(jnp.float32) + moe).astype(jnp.bfloat16)

time: 186 us -> 184 us (0.989)
  waiting for transfers between devices: 94.4 us -> 87.3 us
  starting transfers between devices: 42.7 us -> 48.6 us
    ppermute x3, waiting for transfers between devices: 18.6 us -> 5.53 us  [from_plane(): lax.ppermute(block, 'blk', [((i + PLANE * ahead) % count, i) for i in ran...]
    ppermute x3, starting transfers between devices: 2.27 us -> 6.44 us  [to_plane(): lax.ppermute(block, 'blk', [(i, (i + PLANE * ahead) % count) for i in ran...]
    ppermute x12, waiting for transfers between devices: 47.3 us -> 51.3 us  [crossed(): return lax.ppermute(block, ('tok', 'blk'), route)]
    ppermute x3, waiting for transfers between devices: 11.8 us -> 15.7 us  [to_plane(): lax.ppermute(block, 'blk', [(i, (i + PLANE * ahead) % count) for i in ran...]
    ppermute x12, starting transfers between devices: 14.3 us -> 17.1 us  [crossed(): return lax.ppermute(block, ('tok', 'blk'), route)]
  transfers between devices with their start and end apart: 39 -> 39, of which waited for: 20 -> 22; matrix products, arithmetic and copies ran while one was open for 6% -> 5% of each run, Pallas kernels for 14% -> 14%
where the time goes in v7:
time: 184 us
  waiting for transfers between devices  87.3 us (47%)
  starting transfers between devices  48.6 us (26%)
  Pallas kernels  29.9 us (16%)
  local copies, waits for them, and re-layouts  8.68 us (5%)
  other arithmetic  8.23 us (4%)
    ppermute x12, waiting for transfers between devices, crossed(): return lax.ppermute(block, ('tok', 'blk'), route)  51.3 us
    pallas_call x10, Pallas kernels, local_call(): pl.pallas_call(body, in_specs=[scalar] * len(scalars) + [whole] * len(arr...  29.9 us
    ppermute x12, starting transfers between devices, crossed(): return lax.ppermute(block, ('tok', 'blk'), route)  17.1 us
    ppermute x3, waiting for transfers between devices, to_plane(): lax.ppermute(block, 'blk', [(i, (i + PLANE * ahead) % count) for i in ran...  15.7 us
    ppermute x6, waiting for transfers between devices, flipped(): lax.ppermute(block, 'blk', [(i, i ^ mask) for i in range(lax.axis_size('b...  9.69 us
    ppermute x2, starting transfers between devices, next_plane(): lax.ppermute(block, 'blk', [(i, i + PLANE) for i in range(count - PLANE)])  8.43 us
    ppermute x6, starting transfers between devices, flipped(): lax.ppermute(block, 'blk', [(i, i ^ mask) for i in range(lax.axis_size('b...  8.32 us
    ppermute x3, starting transfers between devices, to_plane(): lax.ppermute(block, 'blk', [(i, (i + PLANE * ahead) % count) for i in ran...  6.44 us
  transfers between devices with their start and end apart: 39, of which 22 were waited for; matrix products, arithmetic and copies ran while one was open for 5% of the time, Pallas kernels for 14%

profile of v7, /device:TPU:0, one launch (start us, length us, event | category | flops | bytes accessed | tf_op | source)
XLA Modules:
  0.0 183.9 jit_solution(12490773878111512937)
XLA Ops:
  4.5 4.9 %collective-permute-start = (bf16[128,1024]{1,0:T(8,128)(2,1)S(1)}, bf16[128,1024]{1,0:T(8,128)(2,1)S(1)}, u32[]{:S(2)}, u32[]{:S(2)}) collective-permute-start(bf16[128,1024]{1,0:T(8,128)(2,1)S(1)} %get-tuple-element.37.rest_0_), channel_id=1, source_target_pairs={{0,4},{1,5},{2,6},{3,7},{4,8},{5,9},{6,10},{7,11},{8,12},{9,13},{1... | collective-permute-start | bytes 786440 | tf_op jit(solution)/shard_map/ppermute | solution.py:27
  9.4 3.5 %collective-permute-start.4 = (bf16[128,1024]{1,0:T(8,128)(2,1)}, bf16[128,1024]{1,0:T(8,128)(2,1)S(1)}, u32[]{:S(2)}, u32[]{:S(2)}) collective-permute-start(bf16[128,1024]{1,0:T(8,128)(2,1)} %rest_0_), channel_id=1, source_target_pairs={{0,4},{1,5},{2,6},{3,7},{4,8},{5,9},{6,10},{7,11},{8,12},{9,13},{1... | collective-permute-start | bytes 786440 | tf_op jit(solution)/shard_map/ppermute | solution.py:27
  13.7 2.4 %collective-permute-done.rest_1_ = bf16[128,1024]{1,0:T(8,128)(2,1)S(1)} collective-permute-done((bf16[128,1024]{1,0:T(8,128)(2,1)S(1)}, bf16[128,1024]{1,0:T(8,128)(2,1)S(1)}, u32[]{:S(2)}, u32[]{:S(2)}) %collective-permute-start) | collective-permute-done | bytes 262176 | tf_op jit(solution)/shard_map/ppermute | solution.py:27
  16.9 2.4 %collective-permute-start.3 = (bf16[128,1024]{1,0:T(8,128)(2,1)S(1)}, bf16[128,1024]{1,0:T(8,128)(2,1)S(1)}, u32[]{:S(2)}, u32[]{:S(2)}) collective-permute-start(bf16[128,1024]{1,0:T(8,128)(2,1)S(1)} %get-tuple-element.87), channel_id=1, source_target_pairs={{0,3},{1,2},{2,1},{3,0},{4,7},{5,6},{6,5},{7,4},{8,11},{9,10},{10,... | collective-permute-start | bytes 786440 | tf_op jit(solution)/shard_map/ppermute | solution.py:22
  22.3 2.4 %collective-permute-start.7 = (bf16[128,1024]{1,0:T(8,128)(2,1)}, bf16[128,1024]{1,0:T(8,128)(2,1)S(1)}, u32[]{:S(2)}, u32[]{:S(2)}) collective-permute-start(bf16[128,1024]{1,0:T(8,128)(2,1)} %get-tuple-element.84), channel_id=1, source_target_pairs={{0,3},{1,2},{2,1},{3,0},{4,7},{5,6},{6,5},{7,4},{8,11},{9,10},{10,... | collective-permute-start | bytes 786440 | tf_op jit(solution)/shard_map/ppermute | solution.py:22
  30.7 4.7 %collective-permute-done.2.rest_3_ = bf16[128,1024]{1,0:T(8,128)(2,1)S(1)} collective-permute-done((bf16[128,1024]{1,0:T(8,128)(2,1)}, bf16[128,1024]{1,0:T(8,128)(2,1)S(1)}, u32[]{:S(2)}, u32[]{:S(2)}) %collective-permute-start.2) | collective-permute-done | bytes 262176 | tf_op jit(solution)/shard_map/ppermute | solution.py:22
  38.0 2.7 %collective-permute-done.6.rest_3_ = bf16[128,1024]{1,0:T(8,128)(2,1)S(1)} collective-permute-done((bf16[128,1024]{1,0:T(8,128)(2,1)}, bf16[128,1024]{1,0:T(8,128)(2,1)S(1)}, u32[]{:S(2)}, u32[]{:S(2)}) %collective-permute-start.6) | collective-permute-done | bytes 262176 | tf_op jit(solution)/shard_map/ppermute | solution.py:22
  40.8 2.2 %copy-done.3 = bf16[1024,2048]{1,0:T(8,128)(2,1)S(1)} copy-done((bf16[1024,2048]{1,0:T(8,128)(2,1)S(1)}, bf16[1024,2048]{1,0:T(8,128)(2,1)}, u32[]{:S(2)}) %copy-start.3) | copy-done | bytes 4194328
  44.7 2.6 %collective-permute-done.8.rest_1_ = f32[128,2048]{1,0:T(8,128)S(1)} collective-permute-done((f32[128,2048]{1,0:T(8,128)S(1)}, f32[128,2048]{1,0:T(8,128)S(1)}, u32[]{:S(2)}, u32[]{:S(2)}) %collective-permute-start.8) | collective-permute-done | bytes 1048608 | tf_op jit(solution)/shard_map/ppermute | solution.py:48
  48.2 2.5 %collective-permute-start.17 = (bf16[64,2176]{1,0:T(8,128)(2,1)S(1)}, bf16[64,2176]{1,0:T(8,128)(2,1)S(1)}, u32[]{:S(2)}, u32[]{:S(2)}) collective-permute-start(bf16[64,2176]{1,0:T(8,128)(2,1)S(1)} %get-tuple-element.47), channel_id=1, source_target_pairs={{12,0},{13,1},{14,2},{15,3},{0,4},{1,5},{2,6},{3,7},{4,8},{5,9},{6... | collective-permute-start | bytes 835592 | tf_op jit(solution)/shard_map/from_plane_3/ppermute | solution.py:33
  50.7 2.3 %collective-permute-start.16 = (bf16[64,2176]{1,0:T(8,128)(2,1)S(1)}, bf16[64,2176]{1,0:T(8,128)(2,1)S(1)}, u32[]{:S(2)}, u32[]{:S(2)}) collective-permute-start(bf16[64,2176]{1,0:T(8,128)(2,1)S(1)} %get-tuple-element.47), channel_id=1, source_target_pairs={{4,0},{5,1},{6,2},{7,3},{8,4},{9,5},{10,6},{11,7},{12,8},{13,9},{1... | collective-permute-start | bytes 835592 | tf_op jit(solution)/shard_map/from_plane_1/ppermute | solution.py:33
  54.6 5.0 %collective-permute-done.9 = bf16[64,2176]{1,0:T(8,128)(2,1)S(1)} collective-permute-done((bf16[64,2176]{1,0:T(8,128)(2,1)S(1)}, bf16[64,2176]{1,0:T(8,128)(2,1)S(1)}, u32[]{:S(2)}, u32[]{:S(2)}) %collective-permute-start.9) | collective-permute-done | bytes 278560 | tf_op jit(solution)/shard_map/gather_first_0/ppermute | solution.py:171
  62.0 3.2 %collective-permute-done.16 = bf16[64,2176]{1,0:T(8,128)(2,1)S(1)} collective-permute-done((bf16[64,2176]{1,0:T(8,128)(2,1)S(1)}, bf16[64,2176]{1,0:T(8,128)(2,1)S(1)}, u32[]{:S(2)}, u32[]{:S(2)}) %collective-permute-start.16) | collective-permute-done | bytes 278560 | tf_op jit(solution)/shard_map/from_plane_1/ppermute | solution.py:33
  66.8 5.9 %collective-permute-done.10.far_ref = bf16[128,2176]{1,0:T(8,128)(2,1)S(1)} collective-permute-done((bf16[128,2176]{1,0:T(8,128)(2,1)S(1)}, bf16[128,2176]{1,0:T(8,128)(2,1)S(1)}, u32[]{:S(2)}, u32[]{:S(2)}) %collective-permute-start.10) | collective-permute-done | bytes 557088 | tf_op jit(solution)/shard_map/gather_second_0/ppermute | solution.py:171
  72.7 2.5 %collective-permute-done.18 = bf16[128,2176]{1,0:T(8,128)(2,1)S(1)} collective-permute-done((bf16[128,2176]{1,0:T(8,128)(2,1)S(1)}, bf16[128,2176]{1,0:T(8,128)(2,1)S(1)}, u32[]{:S(2)}, u32[]{:S(2)}) %collective-permute-start.18) | collective-permute-done | bytes 557088 | tf_op jit(solution)/shard_map/gather_first_1/ppermute | solution.py:171
  75.2 2.4 %collective-permute-done.15 = bf16[64,2176]{1,0:T(8,128)(2,1)S(1)} collective-permute-done((bf16[64,2176]{1,0:T(8,128)(2,1)S(1)}, bf16[64,2176]{1,0:T(8,128)(2,1)S(1)}, u32[]{:S(2)}, u32[]{:S(2)}) %collective-permute-start.15) | collective-permute-done | bytes 278560 | tf_op jit(solution)/shard_map/from_plane_2/ppermute | solution.py:33
  80.6 3.2 %shard_map.144 = (bf16[4,64,1024]{2,1,0:T(8,128)(2,1)S(1)}, bf16[4,64,1024]{2,1,0:T(8,128)(2,1)S(1)}) custom-call(s32[2]{0:T(128)S(1)} %pad_add_fusion.place_ref, bf16[128,2176]{1,0:T(8,128)(2,1)S(1)} %constant_dynamic-update-slice_fusion.near_ref, bf16[128,2176]{1,0:T(8,128)(2,1)S(1)} %collective-permute-done.10.far_ref, bf16[704,2048]{1,0:T(8,128)(2,1)S(1)} %bitcast.82, ...), custom_call_target="tpu_custom_call" | custom-call | flops 2214592512 | bytes 256 | tf_op jit(solution)/shard_map/pallas_call | solution.py:142
  83.9 3.2 %shard_map.145 = (bf16[4,64,1024]{2,1,0:T(8,128)(2,1)S(1)}, bf16[4,64,1024]{2,1,0:T(8,128)(2,1)S(1)}) custom-call(s32[2]{0:T(128)S(1)} %pad_add_fusion.place_ref, bf16[128,2176]{1,0:T(8,128)(2,1)S(1)} %collective-permute-done.11.near_ref, bf16[128,2176]{1,0:T(8,128)(2,1)S(1)} %collective-permute-done.12.far_ref, bf16[704,2048]{1,0:T(8,128)(2,1)S(1)} %bitcast.83, ...), custom_call_target="tpu_custom_call" | custom-call | flops 2214592512 | bytes 256 | tf_op jit(solution)/shard_map/pallas_call | solution.py:142
  88.0 7.1 %collective-permute-done.20.far_ref = bf16[256,2176]{1,0:T(8,128)(2,1)S(1)} collective-permute-done((bf16[256,2176]{1,0:T(8,128)(2,1)S(1)}, bf16[256,2176]{1,0:T(8,128)(2,1)S(1)}, u32[]{:S(2)}, u32[]{:S(2)}) %collective-permute-start.20) | collective-permute-done | bytes 1114144 | tf_op jit(solution)/shard_map/gather_second_1/ppermute | solution.py:171
  96.9 7.8 %collective-permute-done.21.far_ref = bf16[128,2176]{1,0:T(8,128)(2,1)S(1)} collective-permute-done((bf16[128,2176]{1,0:T(8,128)(2,1)S(1)}, bf16[128,2176]{1,0:T(8,128)(2,1)S(1)}, u32[]{:S(2)}, u32[]{:S(2)}) %collective-permute-start.21) | collective-permute-done | bytes 557088 | tf_op jit(solution)/shard_map/gather_second_2/ppermute | solution.py:171
  106.7 3.2 %shard_map.146 = (bf16[4,64,1024]{2,1,0:T(8,128)(2,1)S(1)}, bf16[4,64,1024]{2,1,0:T(8,128)(2,1)S(1)}) custom-call(s32[2]{0:T(128)S(1)} %pad_add_fusion.place_ref, bf16[128,2176]{1,0:T(8,128)(2,1)S(1)} %pad_maximum_fusion.2.near_ref, bf16[128,2176]{1,0:T(8,128)(2,1)S(1)} %collective-permute-done.21.far_ref, bf16[704,2048]{1,0:T(8,128)(2,1)S(1)} %bitcast.84, ...), custom_call_target="tpu_custom_call" | custom-call | flops 2214592512 | bytes 256 | tf_op jit(solution)/shard_map/pallas_call | solution.py:142
  110.5 3.4 %collective-permute-done.22 = bf16[2,2,64,1024]{3,2,1,0:T(8,128)(2,1)S(1)} collective-permute-done((bf16[2,2,64,1024]{3,2,1,0:T(8,128)(2,1)S(1)}, bf16[2,2,64,1024]{3,2,1,0:T(8,128)(2,1)S(1)}, u32[]{:S(2)}, u32[]{:S(2)}) %collective-permute-start.22) | collective-permute-done | bytes 524320 | tf_op jit(solution)/shard_map/scatter_second_0/ppermute | solution.py:171
  114.1 3.2 %shard_map.147 = (bf16[4,64,1024]{2,1,0:T(8,128)(2,1)S(1)}, bf16[4,64,1024]{2,1,0:T(8,128)(2,1)S(1)}) custom-call(s32[2]{0:T(128)S(1)} %pad_add_fusion.place_ref, bf16[128,2176]{1,0:T(8,128)(2,1)S(1)} %collective-permute-done.24.near_ref, bf16[128,2176]{1,0:T(8,128)(2,1)S(1)} %collective-permute-done.25.far_ref, bf16[704,2048]{1,0:T(8,128)(2,1)S(1)} %bitcast.85, ...), custom_call_target="tpu_custom_call" | custom-call | flops 2214592512 | bytes 256 | tf_op jit(solution)/shard_map/pallas_call | solution.py:142
  117.4 5.9 %shard_map.148 = (bf16[4,128,1024]{2,1,0:T(8,128)(2,1)S(1)}, bf16[4,128,1024]{2,1,0:T(8,128)(2,1)S(1)}) custom-call(s32[2]{0:T(128)S(1)} %pad_add_fusion.place_ref, bf16[256,2176]{1,0:T(8,128)(2,1)S(1)} %constant_dynamic-update-slice_fusion.2.near_ref, bf16[256,2176]{1,0:T(8,128)(2,1)S(1)} %collective-permute-done.20.far_ref, ...), custom_call_target="tpu_custom_call" | custom-call | flops 4429185024 | bytes 512 | tf_op jit(solution)/shard_map/pallas_call | solution.py:142
  125.9 5.7 %shard_map.149 = (bf16[4,128,1024]{2,1,0:T(8,128)(2,1)S(1)}, bf16[4,128,1024]{2,1,0:T(8,128)(2,1)S(1)}) custom-call(s32[2]{0:T(128)S(1)} %pad_add_fusion.place_ref, bf16[256,2176]{1,0:T(8,128)(2,1)S(1)} %collective-permute-done.31.near_ref, bf16[256,2176]{1,0:T(8,128)(2,1)S(1)} %collective-permute-done.32.far_ref, bf16[704,2048]{1,0:T(8,128)(2,1)S(1)} %bitcast.87, ...), custom_call_target="tpu_custom_call" | custom-call | flops 4429185024 | bytes 512 | tf_op jit(solution)/shard_map/pallas_call | solution.py:142
  138.0 7.8 %collective-permute-done.29 = bf16[2,64,1024]{2,1,0:T(8,128)(2,1)S(1)} collective-permute-done((bf16[2,64,1024]{2,1,0:T(8,128)(2,1)S(1)}, bf16[2,64,1024]{2,1,0:T(8,128)(2,1)S(1)}, u32[]{:S(2)}, u32[]{:S(2)}) %collective-permute-start.29) | collective-permute-done | bytes 262176 | tf_op jit(solution)/shard_map/scatter_first_2/ppermute | solution.py:171
  145.8 6.8 %collective-permute-done.35 = bf16[2,2,128,1024]{3,2,1,0:T(8,128)(2,1)S(1)} collective-permute-done((bf16[2,2,128,1024]{3,2,1,0:T(8,128)(2,1)S(1)}, bf16[2,2,128,1024]{3,2,1,0:T(8,128)(2,1)S(1)}, u32[]{:S(2)}, u32[]{:S(2)}) %collective-permute-start.35) | collective-permute-done | bytes 1048608 | tf_op jit(solution)/shard_map/scatter_second_1/ppermute | solution.py:171
  155.3 4.1 %collective-permute-start.30 = (bf16[128,1024]{1,0:T(8,128)(2,1)S(1)}, bf16[128,1024]{1,0:T(8,128)(2,1)S(1)}, u32[]{:S(2)}, u32[]{:S(2)}) collective-permute-start(bf16[128,1024]{1,0:T(8,128)(2,1)S(1)} %pad_maximum_fusion.9), channel_id=1, source_target_pairs={{0,8},{1,9},{2,10},{3,11},{4,12},{5,13},{6,14},{7,15},{8,0},{9,1},... | collective-permute-start | bytes 786440 | tf_op jit(solution)/shard_map/to_plane_2/ppermute | solution.py:41
  159.4 3.1 %collective-permute-done.36 = bf16[2,128,1024]{2,1,0:T(8,128)(2,1)S(1)} collective-permute-done((bf16[2,128,1024]{2,1,0:T(8,128)(2,1)S(1)}, bf16[2,128,1024]{2,1,0:T(8,128)(2,1)S(1)}, u32[]{:S(2)}, u32[]{:S(2)}) %collective-permute-start.36) | collective-permute-done | bytes 524320 | tf_op jit(solution)/shard_map/scatter_first_1/ppermute | solution.py:171
  162.8 5.4 %collective-permute-done.30 = bf16[128,1024]{1,0:T(8,128)(2,1)S(1)} collective-permute-done((bf16[128,1024]{1,0:T(8,128)(2,1)S(1)}, bf16[128,1024]{1,0:T(8,128)(2,1)S(1)}, u32[]{:S(2)}, u32[]{:S(2)}) %collective-permute-start.30) | collective-permute-done | bytes 262176 | tf_op jit(solution)/shard_map/to_plane_2/ppermute | solution.py:41
  168.8 2.3 %collective-permute-start.38 = (bf16[128,1024]{1,0:T(8,128)(2,1)}, bf16[128,1024]{1,0:T(8,128)(2,1)S(1)}, u32[]{:S(2)}, u32[]{:S(2)}) collective-permute-start(bf16[128,1024]{1,0:T(8,128)(2,1)} %pad_maximum_fusion.11), channel_id=1, source_target_pairs={{0,12},{1,13},{2,14},{3,15},{4,0},{5,1},{6,2},{7,3},{8,4},{9,5},{1... | collective-permute-start | bytes 786440 | tf_op jit(solution)/shard_map/to_plane_3/ppermute | solution.py:41
  172.6 10.3 %collective-permute-done.38 = bf16[128,1024]{1,0:T(8,128)(2,1)S(1)} collective-permute-done((bf16[128,1024]{1,0:T(8,128)(2,1)}, bf16[128,1024]{1,0:T(8,128)(2,1)S(1)}, u32[]{:S(2)}, u32[]{:S(2)}) %collective-permute-start.38) | collective-permute-done | bytes 262176 | tf_op jit(solution)/shard_map/to_plane_3/ppermute | solution.py:41
  (139 shorter events, 48.5 us)
Async XLA Ops:
  4.5 11.6 %collective-permute-start = (bf16[128,1024]{1,0:T(8,128)(2,1)S(1)}, bf16[128,1024]{1,0:T(8,128)(2,1)S(1)}, u32[]{:S(2)}, u32[]{:S(2)}) collective-permute-start(bf16[128,1024]{1,0:T(8,128)(2,1)S(1)} %get-tuple-element.37.rest_0_), channel_id=1, source_target_pairs={{0,4},{1,5},{2,6},{3,7},{4,8},{5,9},{6,10},{7,11},{8,12},{9,13},{1... | collective-permute-start | bytes 786440 | tf_op jit(solution)/shard_map/ppermute | solution.py:27
  9.4 11.9 %collective-permute-start.4 = (bf16[128,1024]{1,0:T(8,128)(2,1)}, bf16[128,1024]{1,0:T(8,128)(2,1)S(1)}, u32[]{:S(2)}, u32[]{:S(2)}) collective-permute-start(bf16[128,1024]{1,0:T(8,128)(2,1)} %rest_0_), channel_id=1, source_target_pairs={{0,4},{1,5},{2,6},{3,7},{4,8},{5,9},{6,10},{7,11},{8,12},{9,13},{1... | collective-permute-start | bytes 786440 | tf_op jit(solution)/shard_map/ppermute | solution.py:27
  16.9 9.8 %collective-permute-start.3 = (bf16[128,1024]{1,0:T(8,128)(2,1)S(1)}, bf16[128,1024]{1,0:T(8,128)(2,1)S(1)}, u32[]{:S(2)}, u32[]{:S(2)}) collective-permute-start(bf16[128,1024]{1,0:T(8,128)(2,1)S(1)} %get-tuple-element.87), channel_id=1, source_target_pairs={{0,3},{1,2},{2,1},{3,0},{4,7},{5,6},{6,5},{7,4},{8,11},{9,10},{10,... | collective-permute-start | bytes 786440 | tf_op jit(solution)/shard_map/ppermute | solution.py:22
  20.2 15.1 %collective-permute-start.2 = (bf16[128,1024]{1,0:T(8,128)(2,1)}, bf16[128,1024]{1,0:T(8,128)(2,1)S(1)}, u32[]{:S(2)}, u32[]{:S(2)}) collective-permute-start(bf16[128,1024]{1,0:T(8,128)(2,1)} %get-tuple-element.88), channel_id=1, source_target_pairs={{0,2},{1,3},{2,0},{3,1},{4,6},{5,7},{6,4},{7,5},{8,10},{9,11},{10,... | collective-permute-start | bytes 786440 | tf_op jit(solution)/shard_map/ppermute | solution.py:22
  20.7 14.6 %collective-permute-start.1 = (bf16[128,1024]{1,0:T(8,128)(2,1)}, bf16[128,1024]{1,0:T(8,128)(2,1)S(1)}, u32[]{:S(2)}, u32[]{:S(2)}) collective-permute-start(bf16[128,1024]{1,0:T(8,128)(2,1)} %get-tuple-element.89), channel_id=1, source_target_pairs={{0,1},{1,0},{2,3},{3,2},{4,5},{5,4},{6,7},{7,6},{8,9},{9,8},{10,11... | collective-permute-start | bytes 786440 | tf_op jit(solution)/shard_map/ppermute | solution.py:22
  22.3 15.7 %collective-permute-start.7 = (bf16[128,1024]{1,0:T(8,128)(2,1)}, bf16[128,1024]{1,0:T(8,128)(2,1)S(1)}, u32[]{:S(2)}, u32[]{:S(2)}) collective-permute-start(bf16[128,1024]{1,0:T(8,128)(2,1)} %get-tuple-element.84), channel_id=1, source_target_pairs={{0,3},{1,2},{2,1},{3,0},{4,7},{5,6},{6,5},{7,4},{8,11},{9,10},{10,... | collective-permute-start | bytes 786440 | tf_op jit(solution)/shard_map/ppermute | solution.py:22
  24.7 16.0 %collective-permute-start.6 = (bf16[128,1024]{1,0:T(8,128)(2,1)}, bf16[128,1024]{1,0:T(8,128)(2,1)S(1)}, u32[]{:S(2)}, u32[]{:S(2)}) collective-permute-start(bf16[128,1024]{1,0:T(8,128)(2,1)} %get-tuple-element.85), channel_id=1, source_target_pairs={{0,2},{1,3},{2,0},{3,1},{4,6},{5,7},{6,4},{7,5},{8,10},{9,11},{10,... | collective-permute-start | bytes 786440 | tf_op jit(solution)/shard_map/ppermute | solution.py:22
  26.8 14.0 %collective-permute-start.5 = (bf16[128,1024]{1,0:T(8,128)(2,1)}, bf16[128,1024]{1,0:T(8,128)(2,1)S(1)}, u32[]{:S(2)}, u32[]{:S(2)}) collective-permute-start(bf16[128,1024]{1,0:T(8,128)(2,1)} %get-tuple-element.86), channel_id=1, source_target_pairs={{0,1},{1,0},{2,3},{3,2},{4,5},{5,4},{6,7},{7,6},{8,9},{9,8},{10,11... | collective-permute-start | bytes 786440 | tf_op jit(solution)/shard_map/ppermute | solution.py:22
  48.2 13.8 %collective-permute-start.17 = (bf16[64,2176]{1,0:T(8,128)(2,1)S(1)}, bf16[64,2176]{1,0:T(8,128)(2,1)S(1)}, u32[]{:S(2)}, u32[]{:S(2)}) collective-permute-start(bf16[64,2176]{1,0:T(8,128)(2,1)S(1)} %get-tuple-element.47), channel_id=1, source_target_pairs={{12,0},{13,1},{14,2},{15,3},{0,4},{1,5},{2,6},{3,7},{4,8},{5,9},{6... | collective-permute-start | bytes 835592 | tf_op jit(solution)/shard_map/from_plane_3/ppermute | solution.py:33
  50.7 14.4 %collective-permute-start.16 = (bf16[64,2176]{1,0:T(8,128)(2,1)S(1)}, bf16[64,2176]{1,0:T(8,128)(2,1)S(1)}, u32[]{:S(2)}, u32[]{:S(2)}) collective-permute-start(bf16[64,2176]{1,0:T(8,128)(2,1)S(1)} %get-tuple-element.47), channel_id=1, source_target_pairs={{4,0},{5,1},{6,2},{7,3},{8,4},{9,5},{10,6},{11,7},{12,8},{13,9},{1... | collective-permute-start | bytes 835592 | tf_op jit(solution)/shard_map/from_plane_1/ppermute | solution.py:33
  59.6 24.3 %collective-permute-start.11 = (bf16[128,2176]{1,0:T(8,128)(2,1)S(1)}, bf16[128,2176]{1,0:T(8,128)(2,1)S(1)}, u32[]{:S(2)}, u32[]{:S(2)}) collective-permute-start(bf16[128,2176]{1,0:T(8,128)(2,1)S(1)} %constant_dynamic-update-slice_fusion.near_ref), channel_id=1, source_target_pairs={{16,0},{0,16},{17,1},{1,17},{18,2},{2,18},{19,3},{3,19},{20,4},{4,... | collective-permute-start | bytes 1671176 | tf_op jit(solution)/shard_map/ppermute | solution.py:48
  59.6 18.0 %collective-permute-start.15 = (bf16[64,2176]{1,0:T(8,128)(2,1)S(1)}, bf16[64,2176]{1,0:T(8,128)(2,1)S(1)}, u32[]{:S(2)}, u32[]{:S(2)}) collective-permute-start(bf16[64,2176]{1,0:T(8,128)(2,1)S(1)} %get-tuple-element.47), channel_id=1, source_target_pairs={{8,0},{9,1},{10,2},{11,3},{12,4},{13,5},{14,6},{15,7},{0,8},{1,9},... | collective-permute-start | bytes 835592 | tf_op jit(solution)/shard_map/from_plane_2/ppermute | solution.py:33
  60.5 12.2 %collective-permute-start.10 = (bf16[128,2176]{1,0:T(8,128)(2,1)S(1)}, bf16[128,2176]{1,0:T(8,128)(2,1)S(1)}, u32[]{:S(2)}, u32[]{:S(2)}) collective-permute-start(bf16[128,2176]{1,0:T(8,128)(2,1)S(1)} %constant_dynamic-update-slice_fusion.near_ref), channel_id=1, source_target_pairs={{0,2},{1,3},{2,0},{3,1},{4,6},{5,7},{6,4},{7,5},{8,10},{9,11},{10,... | collective-permute-start | bytes 1671176 | tf_op jit(solution)/shard_map/gather_second_0/ppermute | solution.py:171
  65.2 10.0 %collective-permute-start.18 = (bf16[128,2176]{1,0:T(8,128)(2,1)S(1)}, bf16[128,2176]{1,0:T(8,128)(2,1)S(1)}, u32[]{:S(2)}, u32[]{:S(2)}) collective-permute-start(bf16[128,2176]{1,0:T(8,128)(2,1)S(1)} %pad_maximum_fusion.1), channel_id=1, source_target_pairs={{0,1},{1,0},{2,3},{3,2},{4,5},{5,4},{6,7},{7,6},{8,9},{9,8},{10,11... | collective-permute-start | bytes 1671176 | tf_op jit(solution)/shard_map/gather_first_1/ppermute | solution.py:171
  72.7 11.2 %collective-permute-start.12 = (bf16[128,2176]{1,0:T(8,128)(2,1)S(1)}, bf16[128,2176]{1,0:T(8,128)(2,1)S(1)}, u32[]{:S(2)}, u32[]{:S(2)}) collective-permute-start(bf16[128,2176]{1,0:T(8,128)(2,1)S(1)} %collective-permute-done.10.far_ref), channel_id=1, source_target_pairs={{16,0},{0,16},{17,1},{1,17},{18,2},{2,18},{19,3},{3,19},{20,4},{4,... | collective-permute-start | bytes 1671176 | tf_op jit(solution)/shard_map/ppermute | solution.py:48
  77.6 10.1 %collective-permute-start.19 = (bf16[64,2176]{1,0:T(8,128)(2,1)S(1)}, bf16[64,2176]{1,0:T(8,128)(2,1)S(1)}, u32[]{:S(2)}, u32[]{:S(2)}) collective-permute-start(bf16[64,2176]{1,0:T(8,128)(2,1)S(1)} %collective-permute-done.15), channel_id=1, source_target_pairs={{0,1},{1,0},{2,3},{3,2},{4,5},{5,4},{6,7},{7,6},{8,9},{9,8},{10,11... | collective-permute-start | bytes 835592 | tf_op jit(solution)/shard_map/gather_first_2/ppermute | solution.py:171
  79.1 16.0 %collective-permute-start.20 = (bf16[256,2176]{1,0:T(8,128)(2,1)S(1)}, bf16[256,2176]{1,0:T(8,128)(2,1)S(1)}, u32[]{:S(2)}, u32[]{:S(2)}) collective-permute-start(bf16[256,2176]{1,0:T(8,128)(2,1)S(1)} %constant_dynamic-update-slice_fusion.2.near_ref), channel_id=1, source_target_pairs={{0,2},{1,3},{2,0},{3,1},{4,6},{5,7},{6,4},{7,5},{8,10},{9,11},{10,... | collective-permute-start | bytes 3342344 | tf_op jit(solution)/shard_map/gather_second_1/ppermute | solution.py:171
  87.1 9.5 %collective-permute-start.13 = (bf16[4,64,1024]{2,1,0:T(8,128)(2,1)S(1)}, bf16[4,64,1024]{2,1,0:T(8,128)(2,1)S(1)}, u32[]{:S(2)}, u32[]{:S(2)}) collective-permute-start(bf16[4,64,1024]{2,1,0:T(8,128)(2,1)S(1)} %get-tuple-element.45), channel_id=1, source_target_pairs={{16,0},{0,16},{17,1},{1,17},{18,2},{2,18},{19,3},{3,19},{20,4},{4,... | collective-permute-start | bytes 1572872 | tf_op jit(solution)/shard_map/ppermute | solution.py:48
  87.7 22.2 %collective-permute-start.24 = (bf16[128,2176]{1,0:T(8,128)(2,1)S(1)}, bf16[128,2176]{1,0:T(8,128)(2,1)S(1)}, u32[]{:S(2)}, u32[]{:S(2)}) collective-permute-start(bf16[128,2176]{1,0:T(8,128)(2,1)S(1)} %pad_maximum_fusion.2.near_ref), channel_id=1, source_target_pairs={{16,0},{0,16},{17,1},{1,17},{18,2},{2,18},{19,3},{3,19},{20,4},{4,... | collective-permute-start | bytes 1671176 | tf_op jit(solution)/shard_map/ppermute | solution.py:48
  95.1 9.5 %collective-permute-start.21 = (bf16[128,2176]{1,0:T(8,128)(2,1)S(1)}, bf16[128,2176]{1,0:T(8,128)(2,1)S(1)}, u32[]{:S(2)}, u32[]{:S(2)}) collective-permute-start(bf16[128,2176]{1,0:T(8,128)(2,1)S(1)} %pad_maximum_fusion.2.near_ref), channel_id=1, source_target_pairs={{0,2},{1,3},{2,0},{3,1},{4,6},{5,7},{6,4},{7,5},{8,10},{9,11},{10,... | collective-permute-start | bytes 1671176 | tf_op jit(solution)/shard_map/gather_second_2/ppermute | solution.py:171
  106.1 19.8 %collective-permute-start.31 = (bf16[256,2176]{1,0:T(8,128)(2,1)S(1)}, bf16[256,2176]{1,0:T(8,128)(2,1)S(1)}, u32[]{:S(2)}, u32[]{:S(2)}) collective-permute-start(bf16[256,2176]{1,0:T(8,128)(2,1)S(1)} %constant_dynamic-update-slice_fusion.2.near_ref), channel_id=1, source_target_pairs={{16,0},{0,16},{17,1},{1,17},{18,2},{2,18},{19,3},{3,19},{20,4},{4,... | collective-permute-start | bytes 3342344 | tf_op jit(solution)/shard_map/ppermute | solution.py:48
  106.1 19.8 %collective-permute-start.32 = (bf16[256,2176]{1,0:T(8,128)(2,1)S(1)}, bf16[256,2176]{1,0:T(8,128)(2,1)S(1)}, u32[]{:S(2)}, u32[]{:S(2)}) collective-permute-start(bf16[256,2176]{1,0:T(8,128)(2,1)S(1)} %collective-permute-done.20.far_ref), channel_id=1, source_target_pairs={{16,0},{0,16},{17,1},{1,17},{18,2},{2,18},{19,3},{3,19},{20,4},{4,... | collective-permute-start | bytes 3342344 | tf_op jit(solution)/shard_map/ppermute | solution.py:48
  109.9 14.0 %collective-permute-start.27 = (bf16[4,64,1024]{2,1,0:T(8,128)(2,1)S(1)}, bf16[4,64,1024]{2,1,0:T(8,128)(2,1)S(1)}, u32[]{:S(2)}, u32[]{:S(2)}) collective-permute-start(bf16[4,64,1024]{2,1,0:T(8,128)(2,1)S(1)} %get-tuple-element.55), channel_id=1, source_target_pairs={{16,0},{0,16},{17,1},{1,17},{18,2},{2,18},{19,3},{3,19},{20,4},{4,... | collective-permute-start | bytes 1572872 | tf_op jit(solution)/shard_map/ppermute | solution.py:48
  123.3 10.5 %collective-permute-start.34 = (bf16[4,128,1024]{2,1,0:T(8,128)(2,1)S(1)}, bf16[4,128,1024]{2,1,0:T(8,128)(2,1)S(1)}, u32[]{:S(2)}, u32[]{:S(2)}) collective-permute-start(bf16[4,128,1024]{2,1,0:T(8,128)(2,1)S(1)} %get-tuple-element.61), channel_id=1, source_target_pairs={{16,0},{0,16},{17,1},{1,17},{18,2},{2,18},{19,3},{3,19},{20,4},{4,... | collective-permute-start | bytes 3145736 | tf_op jit(solution)/shard_map/ppermute | solution.py:48
  124.4 9.2 %collective-permute-start.28 = (bf16[2,2,64,1024]{3,2,1,0:T(8,128)(2,1)S(1)}, bf16[2,2,64,1024]{3,2,1,0:T(8,128)(2,1)S(1)}, u32[]{:S(2)}, u32[]{:S(2)}) collective-permute-start(bf16[2,2,64,1024]{3,2,1,0:T(8,128)(2,1)S(1)} %pad_maximum_fusion.5), channel_id=1, source_target_pairs={{0,2},{1,3},{2,0},{3,1},{4,6},{5,7},{6,4},{7,5},{8,10},{9,11},{10,... | collective-permute-start | bytes 1572872 | tf_op jit(solution)/shard_map/scatter_second_2/ppermute | solution.py:171
  135.0 17.7 %collective-permute-start.35 = (bf16[2,2,128,1024]{3,2,1,0:T(8,128)(2,1)S(1)}, bf16[2,2,128,1024]{3,2,1,0:T(8,128)(2,1)S(1)}, u32[]{:S(2)}, u32[]{:S(2)}) collective-permute-start(bf16[2,2,128,1024]{3,2,1,0:T(8,128)(2,1)S(1)} %pad_maximum_fusion), channel_id=1, source_target_pairs={{0,2},{1,3},{2,0},{3,1},{4,6},{5,7},{6,4},{7,5},{8,10},{9,11},{10,... | collective-permute-start | bytes 3145736 | tf_op jit(solution)/shard_map/scatter_second_1/ppermute | solution.py:171
  136.5 9.2 %collective-permute-start.29 = (bf16[2,64,1024]{2,1,0:T(8,128)(2,1)S(1)}, bf16[2,64,1024]{2,1,0:T(8,128)(2,1)S(1)}, u32[]{:S(2)}, u32[]{:S(2)}) collective-permute-start(bf16[2,64,1024]{2,1,0:T(8,128)(2,1)S(1)} %pad_maximum_fusion.8), channel_id=1, source_target_pairs={{0,1},{1,0},{2,3},{3,2},{4,5},{5,4},{6,7},{7,6},{8,9},{9,8},{10,11... | collective-permute-start | bytes 786440 | tf_op jit(solution)/shard_map/scatter_first_2/ppermute | solution.py:171
  153.3 9.2 %collective-permute-start.36 = (bf16[2,128,1024]{2,1,0:T(8,128)(2,1)S(1)}, bf16[2,128,1024]{2,1,0:T(8,128)(2,1)S(1)}, u32[]{:S(2)}, u32[]{:S(2)}) collective-permute-start(bf16[2,128,1024]{2,1,0:T(8,128)(2,1)S(1)} %pad_maximum_fusion.6), channel_id=1, source_target_pairs={{0,1},{1,0},{2,3},{3,2},{4,5},{5,4},{6,7},{7,6},{8,9},{9,8},{10,11... | collective-permute-start | bytes 1572872 | tf_op jit(solution)/shard_map/scatter_first_1/ppermute | solution.py:171
  154.2 18.3 %collective-permute-start.23 = (bf16[2,64,1024]{2,1,0:T(8,128)(2,1)S(1)}, bf16[2,64,1024]{2,1,0:T(8,128)(2,1)S(1)}, u32[]{:S(2)}, u32[]{:S(2)}) collective-permute-start(bf16[2,64,1024]{2,1,0:T(8,128)(2,1)S(1)} %pad_maximum_fusion.7), channel_id=1, source_target_pairs={{0,1},{1,0},{2,3},{3,2},{4,5},{5,4},{6,7},{7,6},{8,9},{9,8},{10,11... | collective-permute-start | bytes 786440 | tf_op jit(solution)/shard_map/scatter_first_0/ppermute | solution.py:171
  155.3 12.8 %collective-permute-start.30 = (bf16[128,1024]{1,0:T(8,128)(2,1)S(1)}, bf16[128,1024]{1,0:T(8,128)(2,1)S(1)}, u32[]{:S(2)}, u32[]{:S(2)}) collective-permute-start(bf16[128,1024]{1,0:T(8,128)(2,1)S(1)} %pad_maximum_fusion.9), channel_id=1, source_target_pairs={{0,8},{1,9},{2,10},{3,11},{4,12},{5,13},{6,14},{7,15},{8,0},{9,1},... | collective-permute-start | bytes 786440 | tf_op jit(solution)/shard_map/to_plane_2/ppermute | solution.py:41
  168.8 14.1 %collective-permute-start.38 = (bf16[128,1024]{1,0:T(8,128)(2,1)}, bf16[128,1024]{1,0:T(8,128)(2,1)S(1)}, u32[]{:S(2)}, u32[]{:S(2)}) collective-permute-start(bf16[128,1024]{1,0:T(8,128)(2,1)} %pad_maximum_fusion.11), channel_id=1, source_target_pairs={{0,12},{1,13},{2,14},{3,15},{4,0},{5,1},{6,2},{7,3},{8,4},{9,5},{1... | collective-permute-start | bytes 786440 | tf_op jit(solution)/shard_map/to_plane_3/ppermute | solution.py:41
  171.2 11.7 %collective-permute-start.37 = (bf16[128,1024]{1,0:T(8,128)(2,1)S(1)}, bf16[128,1024]{1,0:T(8,128)(2,1)S(1)}, u32[]{:S(2)}, u32[]{:S(2)}) collective-permute-start(bf16[128,1024]{1,0:T(8,128)(2,1)S(1)} %pad_maximum_fusion.10), channel_id=1, source_target_pairs={{0,4},{1,5},{2,6},{3,7},{4,8},{5,9},{6,10},{7,11},{8,12},{9,13},{1... | collective-permute-start | bytes 786440 | tf_op jit(solution)/shard_map/to_plane_1/ppermute | solution.py:41
  (19 other events, 182.7 us)

commit v8 on v7

--- a/solution.py
+++ b/solution.py
@@ -12,6 +12,7 @@
 PAGE = 16
 PLANE = 4
 EPSILON = 1e-06
+LIGHT = 100
 
 
 def after(value, *others):
@@ -195,7 +196,7 @@
             outs[part][order[block]] = product[block * part_rows : (block + 1) * part_rows]
 
 
-def run_expert(place, near, far, w_gate, w_up, w_down, experts, parts, ahead):
+def run_expert(place, near, far, w_gate, w_up, w_down, experts, parts, ahead, weight):
     count = 2 * near.shape[0]
     units, width = w_gate.shape
     out_shape = jax.ShapeDtypeStruct((PLANE, count // PLANE, width // parts), jnp.bfloat16)
@@ -204,7 +205,7 @@
         [out_shape] * parts,
         [place],
         [near, far, w_gate, w_up, w_down],
-        flops=6 * count * width * units,
+        flops=6 * count * width * units // weight,
         moved=count,
     )
 
@@ -229,13 +230,13 @@
     return [total[0:count] + wide(got[i]) for i, total in enumerate(totals)]
 
 
-def expert_outputs(place, near, far, weights, experts, cores, waits):
+def expert_outputs(place, near, far, weights, experts, cores, waits, weight=1):
     outs = []
     for ahead in range(cores):
         near_rows = from_core(near, ahead) if ahead else near
         far_rows = from_core(far, ahead) if ahead else far
         near_rows = after(near_rows, *outs[-1:], *waits.get(ahead, []))
-        outs.append(run_expert(place, near_rows, far_rows, *weights, experts, cores, ahead))
+        outs.append(run_expert(place, near_rows, far_rows, *weights, experts, cores, ahead, weight))
     return outs
 
 
@@ -341,10 +342,8 @@
         if number > 1:
             column = after(column, nears[-1])
         nears.append(jnp.concatenate([column, crossed(column, True, f"gather_first_{number}")]))
-        if number > 1 and number == len(groups) - 1:
-            outs = run(nears[0], fars[0], waits={})
-            nears[-1] = after(nears[-1], *outs)
-        fars.append(crossed(after(nears[-1], *fars[-1:]), False, f"gather_second_{number}"))
+        fars.append(crossed(nears[-1], False, f"gather_second_{number}"))
+    outs = run(nears[0], fars[0], waits={})
     totals = core_totals(outs, cores)
     sent = second_share(totals)
     totals = merged(totals, crossed(after(sent, fars[-1]), False, "scatter_second_0"), 2)
@@ -353,10 +352,10 @@
     results = {}
     returned = []
     for number in reversed(range(1, len(groups))):
-        waits = {0: [outs], cores - 1: [sent]}
+        waits = {0: [outs, fars], cores - 1: [sent]}
         if number < len(groups) - 1:
-            waits[cores - 1] = [sent, shared]
-        outs = run(nears[number], fars[number], waits=waits)
+            waits = {0: [outs], cores - 1: [sent, shared]}
+        outs = run(nears[number], fars[number], waits=waits, weight=LIGHT)
         totals = core_totals(outs, cores)
         if number < len(groups) - 1:
             totals = [after(total, late) for total in totals]

time: 184 us -> 179 us (0.973)
  waiting for transfers between devices: 87.3 us -> 78.8 us
    ppermute x12, waiting for transfers between devices: 51.3 us -> 39.8 us  [crossed(): return lax.ppermute(block, ('tok', 'blk'), route)]
    ppermute x12, starting transfers between devices: 17.1 us -> 12.9 us  [crossed(): return lax.ppermute(block, ('tok', 'blk'), route)]
    ppermute x3, waiting for transfers between devices: 5.53 us -> 8.33 us  [from_plane(): lax.ppermute(block, 'blk', [((i + PLANE * ahead) % count, i) for i in ran...]
    ppermute x3, starting transfers between devices: 5.64 us -> 8 us  [from_plane(): lax.ppermute(block, 'blk', [((i + PLANE * ahead) % count, i) for i in ran...]
    unnamed x28 -> x31, local copies, waits for them, and re-layouts: 6.18 us -> 6.2 us
  transfers between devices with their start and end apart: 39 -> 39, of which waited for: 22 -> 19; matrix products, arithmetic and copies ran while one was open for 5% -> 6% of each run, Pallas kernels for 14% -> 15%
where the time goes in v8:
time: 179 us
  waiting for transfers between devices  78.8 us (44%)
  starting transfers between devices  50.3 us (28%)
  Pallas kernels  29.9 us (17%)
  local copies, waits for them, and re-layouts  10.5 us (6%)
  other arithmetic  8.17 us (5%)
    ppermute x12, waiting for transfers between devices, crossed(): return lax.ppermute(block, ('tok', 'blk'), route)  39.8 us
    pallas_call x10, Pallas kernels, local_call(): pl.pallas_call(body, in_specs=[scalar] * len(scalars) + [whole] * len(arr...  29.9 us
    ppermute x3, waiting for transfers between devices, to_plane(): lax.ppermute(block, 'blk', [(i, (i + PLANE * ahead) % count) for i in ran...  17 us
    ppermute x12, starting transfers between devices, crossed(): return lax.ppermute(block, ('tok', 'blk'), route)  12.9 us
    ppermute x6, starting transfers between devices, flipped(): lax.ppermute(block, 'blk', [(i, i ^ mask) for i in range(lax.axis_size('b...  9.12 us
    ppermute x6, waiting for transfers between devices, flipped(): lax.ppermute(block, 'blk', [(i, i ^ mask) for i in range(lax.axis_size('b...  8.52 us
    ppermute x2, starting transfers between devices, next_plane(): lax.ppermute(block, 'blk', [(i, i + PLANE) for i in range(count - PLANE)])  8.43 us
    ppermute x3, waiting for transfers between devices, from_plane(): lax.ppermute(block, 'blk', [((i + PLANE * ahead) % count, i) for i in ran...  8.33 us
  transfers between devices with their start and end apart: 39, of which 19 were waited for; matrix products, arithmetic and copies ran while one was open for 6% of the time, Pallas kernels for 15%

profile of v8, /device:TPU:0, one launch (start us, length us, event | category | flops | bytes accessed | tf_op | source)
XLA Modules:
  0.0 178.9 jit_solution(13254145089507659462)
XLA Ops:
  4.5 4.9 %collective-permute-start = (bf16[128,1024]{1,0:T(8,128)(2,1)S(1)}, bf16[128,1024]{1,0:T(8,128)(2,1)S(1)}, u32[]{:S(2)}, u32[]{:S(2)}) collective-permute-start(bf16[128,1024]{1,0:T(8,128)(2,1)S(1)} %get-tuple-element.34.rest_0_), channel_id=1, source_target_pairs={{0,4},{1,5},{2,6},{3,7},{4,8},{5,9},{6,10},{7,11},{8,12},{9,13},{1... | collective-permute-start | bytes 786440 | tf_op jit(solution)/shard_map/ppermute | solution.py:28
  9.4 3.5 %collective-permute-start.4 = (bf16[128,1024]{1,0:T(8,128)(2,1)}, bf16[128,1024]{1,0:T(8,128)(2,1)S(1)}, u32[]{:S(2)}, u32[]{:S(2)}) collective-permute-start(bf16[128,1024]{1,0:T(8,128)(2,1)} %rest_0_), channel_id=1, source_target_pairs={{0,4},{1,5},{2,6},{3,7},{4,8},{5,9},{6,10},{7,11},{8,12},{9,13},{1... | collective-permute-start | bytes 786440 | tf_op jit(solution)/shard_map/ppermute | solution.py:28
  13.7 2.4 %collective-permute-done.rest_1_ = bf16[128,1024]{1,0:T(8,128)(2,1)S(1)} collective-permute-done((bf16[128,1024]{1,0:T(8,128)(2,1)S(1)}, bf16[128,1024]{1,0:T(8,128)(2,1)S(1)}, u32[]{:S(2)}, u32[]{:S(2)}) %collective-permute-start) | collective-permute-done | bytes 262176 | tf_op jit(solution)/shard_map/ppermute | solution.py:28
  25.9 2.6 %collective-permute-start.7 = (bf16[128,1024]{1,0:T(8,128)(2,1)}, bf16[128,1024]{1,0:T(8,128)(2,1)S(1)}, u32[]{:S(2)}, u32[]{:S(2)}) collective-permute-start(bf16[128,1024]{1,0:T(8,128)(2,1)} %get-tuple-element.78), channel_id=1, source_target_pairs={{0,3},{1,2},{2,1},{3,0},{4,7},{5,6},{6,5},{7,4},{8,11},{9,10},{10,... | collective-permute-start | bytes 786440 | tf_op jit(solution)/shard_map/ppermute | solution.py:23
  29.6 2.7 %scatter_fusion = bf16[8,16,2,1024]{3,1,2,0:T(8,128)(2,1)} fusion(bf16[8,16,2,1024]{3,1,2,0:T(8,128)(2,1)} %broadcast_in_dim.31, s32[8]{0:T(128)S(1)} %compare_select_fusion, bf16[8,16,2,1024]{3,1,2,0:T(8,128)(2,1)} %pad_maximum_fusion.2), kind=kCustom, calls=%fused_computation | custom fusion | bytes 1572896 | tf_op jit(solution)/shard_map/scatter | solution.py:306
  33.0 1.9 %shard_map.141.prob_ref = bf16[8,128,640]{2,1,0:T(8,128)(2,1)S(1)} custom-call(s32[2]{0:T(128)S(1)} %pad_add_fusion.place_ref, s32[8]{0:T(128)S(1)} %copy-done.10, bf16[128,1024]{1,0:T(8,128)(2,1)S(1)} %get-tuple-element.33.q_ref, bf16[128,1024]{1,0:T(8,128)(2,1)S(1)} %get-tuple-element.34.rest_0_, bf16[128,1024]{1,0:T(8,128)(2,1)S(1)} %collective-permute-done.rest_1_, ...), custom_call_target="tpu_custom_call" | custom-call | flops 167772160 | bytes 2883584 | tf_op jit(solution)/shard_map/pallas_call | solution.py:143
  34.9 2.2 %collective-permute-done.5.rest_2_ = bf16[128,1024]{1,0:T(8,128)(2,1)S(1)} collective-permute-done((bf16[128,1024]{1,0:T(8,128)(2,1)}, bf16[128,1024]{1,0:T(8,128)(2,1)S(1)}, u32[]{:S(2)}, u32[]{:S(2)}) %collective-permute-start.5) | collective-permute-done | bytes 262176 | tf_op jit(solution)/shard_map/ppermute | solution.py:23
  37.2 4.9 %collective-permute-done.6.rest_3_ = bf16[128,1024]{1,0:T(8,128)(2,1)S(1)} collective-permute-done((bf16[128,1024]{1,0:T(8,128)(2,1)}, bf16[128,1024]{1,0:T(8,128)(2,1)S(1)}, u32[]{:S(2)}, u32[]{:S(2)}) %collective-permute-start.6) | collective-permute-done | bytes 262176 | tf_op jit(solution)/shard_map/ppermute | solution.py:23
  42.0 2.2 %copy-done.3 = bf16[1024,2048]{1,0:T(8,128)(2,1)S(1)} copy-done((bf16[1024,2048]{1,0:T(8,128)(2,1)S(1)}, bf16[1024,2048]{1,0:T(8,128)(2,1)}, u32[]{:S(2)}) %copy-start.3) | copy-done | bytes 4194328
  44.2 1.7 shard_map.142.rest_0_
  46.0 2.6 %collective-permute-done.8.rest_1_ = f32[128,2048]{1,0:T(8,128)S(1)} collective-permute-done((f32[128,2048]{1,0:T(8,128)S(1)}, f32[128,2048]{1,0:T(8,128)S(1)}, u32[]{:S(2)}, u32[]{:S(2)}) %collective-permute-start.8) | collective-permute-done | bytes 1048608 | tf_op jit(solution)/shard_map/ppermute | solution.py:49
  50.1 4.5 %collective-permute-start.16 = (bf16[64,2176]{1,0:T(8,128)(2,1)S(1)}, bf16[64,2176]{1,0:T(8,128)(2,1)S(1)}, u32[]{:S(2)}, u32[]{:S(2)}) collective-permute-start(bf16[64,2176]{1,0:T(8,128)(2,1)S(1)} %get-tuple-element.44), channel_id=1, source_target_pairs={{4,0},{5,1},{6,2},{7,3},{8,4},{9,5},{10,6},{11,7},{12,8},{13,9},{1... | collective-permute-start | bytes 835592 | tf_op jit(solution)/shard_map/from_plane_1/ppermute | solution.py:34
  56.2 1.6 collective-permute-start.10
  57.8 3.5 %collective-permute-start.15 = (bf16[64,2176]{1,0:T(8,128)(2,1)S(1)}, bf16[64,2176]{1,0:T(8,128)(2,1)S(1)}, u32[]{:S(2)}, u32[]{:S(2)}) collective-permute-start(bf16[64,2176]{1,0:T(8,128)(2,1)S(1)} %get-tuple-element.44), channel_id=1, source_target_pairs={{8,0},{9,1},{10,2},{11,3},{12,4},{13,5},{14,6},{15,7},{0,8},{1,9},... | collective-permute-start | bytes 835592 | tf_op jit(solution)/shard_map/from_plane_2/ppermute | solution.py:34
  61.7 6.9 %collective-permute-done.17 = bf16[64,2176]{1,0:T(8,128)(2,1)S(1)} collective-permute-done((bf16[64,2176]{1,0:T(8,128)(2,1)S(1)}, bf16[64,2176]{1,0:T(8,128)(2,1)S(1)}, u32[]{:S(2)}, u32[]{:S(2)}) %collective-permute-start.17) | collective-permute-done | bytes 278560 | tf_op jit(solution)/shard_map/from_plane_3/ppermute | solution.py:34
  68.6 1.6 collective-permute-start.18
  70.3 8.0 %collective-permute-done.18 = bf16[128,2176]{1,0:T(8,128)(2,1)S(1)} collective-permute-done((bf16[128,2176]{1,0:T(8,128)(2,1)S(1)}, bf16[128,2176]{1,0:T(8,128)(2,1)S(1)}, u32[]{:S(2)}, u32[]{:S(2)}) %collective-permute-start.18) | collective-permute-done | bytes 557088 | tf_op jit(solution)/shard_map/gather_first_1/ppermute | solution.py:172
  81.5 3.2 %shard_map.144 = (bf16[4,64,1024]{2,1,0:T(8,128)(2,1)S(1)}, bf16[4,64,1024]{2,1,0:T(8,128)(2,1)S(1)}) custom-call(s32[2]{0:T(128)S(1)} %pad_add_fusion.place_ref, bf16[128,2176]{1,0:T(8,128)(2,1)S(1)} %constant_dynamic-update-slice_fusion.near_ref, bf16[128,2176]{1,0:T(8,128)(2,1)S(1)} %collective-permute-done.10.far_ref, bf16[704,2048]{1,0:T(8,128)(2,1)S(1)} %bitcast.81, ...), custom_call_target="tpu_custom_call" | custom-call | flops 2214592512 | bytes 256 | tf_op jit(solution)/shard_map/pallas_call | solution.py:143
  84.9 3.4 %collective-permute-done.19 = bf16[64,2176]{1,0:T(8,128)(2,1)S(1)} collective-permute-done((bf16[64,2176]{1,0:T(8,128)(2,1)S(1)}, bf16[64,2176]{1,0:T(8,128)(2,1)S(1)}, u32[]{:S(2)}, u32[]{:S(2)}) %collective-permute-start.19) | collective-permute-done | bytes 278560 | tf_op jit(solution)/shard_map/gather_first_2/ppermute | solution.py:172
  88.9 3.2 %shard_map.145 = (bf16[4,64,1024]{2,1,0:T(8,128)(2,1)S(1)}, bf16[4,64,1024]{2,1,0:T(8,128)(2,1)S(1)}) custom-call(s32[2]{0:T(128)S(1)} %pad_add_fusion.place_ref, bf16[128,2176]{1,0:T(8,128)(2,1)S(1)} %collective-permute-done.11.near_ref, bf16[128,2176]{1,0:T(8,128)(2,1)S(1)} %collective-permute-done.12.far_ref, bf16[704,2048]{1,0:T(8,128)(2,1)S(1)} %bitcast.82, ...), custom_call_target="tpu_custom_call" | custom-call | flops 2214592512 | bytes 256 | tf_op jit(solution)/shard_map/pallas_call | solution.py:143
  93.0 8.8 %collective-permute-done.20.far_ref = bf16[128,2176]{1,0:T(8,128)(2,1)S(1)} collective-permute-done((bf16[128,2176]{1,0:T(8,128)(2,1)S(1)}, bf16[128,2176]{1,0:T(8,128)(2,1)S(1)}, u32[]{:S(2)}, u32[]{:S(2)}) %collective-permute-start.20) | collective-permute-done | bytes 557088 | tf_op jit(solution)/shard_map/gather_second_2/ppermute | solution.py:172
  101.8 1.8 collective-permute-start.25
  103.6 3.2 %shard_map.146 = (bf16[4,64,1024]{2,1,0:T(8,128)(2,1)S(1)}, bf16[4,64,1024]{2,1,0:T(8,128)(2,1)S(1)}) custom-call(s32[2]{0:T(128)S(1)} %pad_add_fusion.place_ref, bf16[128,2176]{1,0:T(8,128)(2,1)S(1)} %constant_dynamic-update-slice_fusion.5.near_ref, bf16[128,2176]{1,0:T(8,128)(2,1)S(1)} %collective-permute-done.20.far_ref, bf16[704,2048]{1,0:T(8,128)(2,1)S(1)} %bitcast.83, ...), custom_call_target="tpu_custom_call" | custom-call | flops 22145924 | bytes 256 | tf_op jit(solution)/shard_map/pallas_call | solution.py:143
  108.3 3.2 %shard_map.147 = (bf16[4,64,1024]{2,1,0:T(8,128)(2,1)S(1)}, bf16[4,64,1024]{2,1,0:T(8,128)(2,1)S(1)}) custom-call(s32[2]{0:T(128)S(1)} %pad_add_fusion.place_ref, bf16[128,2176]{1,0:T(8,128)(2,1)S(1)} %collective-permute-done.24.near_ref, bf16[128,2176]{1,0:T(8,128)(2,1)S(1)} %collective-permute-done.25.far_ref, bf16[704,2048]{1,0:T(8,128)(2,1)S(1)} %bitcast.84, ...), custom_call_target="tpu_custom_call" | custom-call | flops 22145924 | bytes 256 | tf_op jit(solution)/shard_map/pallas_call | solution.py:143
  111.9 5.9 %shard_map.148 = (bf16[4,128,1024]{2,1,0:T(8,128)(2,1)S(1)}, bf16[4,128,1024]{2,1,0:T(8,128)(2,1)S(1)}) custom-call(s32[2]{0:T(128)S(1)} %pad_add_fusion.place_ref, bf16[256,2176]{1,0:T(8,128)(2,1)S(1)} %constant_dynamic-update-slice_fusion.2.near_ref, bf16[256,2176]{1,0:T(8,128)(2,1)S(1)} %collective-permute-done.23.far_ref, ...), custom_call_target="tpu_custom_call" | custom-call | flops 44291848 | bytes 512 | tf_op jit(solution)/shard_map/pallas_call | solution.py:143
  120.2 5.7 %shard_map.149 = (bf16[4,128,1024]{2,1,0:T(8,128)(2,1)S(1)}, bf16[4,128,1024]{2,1,0:T(8,128)(2,1)S(1)}) custom-call(s32[2]{0:T(128)S(1)} %pad_add_fusion.place_ref, bf16[256,2176]{1,0:T(8,128)(2,1)S(1)} %collective-permute-done.31.near_ref, bf16[256,2176]{1,0:T(8,128)(2,1)S(1)} %collective-permute-done.32.far_ref, bf16[704,2048]{1,0:T(8,128)(2,1)S(1)} %bitcast.86, ...), custom_call_target="tpu_custom_call" | custom-call | flops 44291848 | bytes 512 | tf_op jit(solution)/shard_map/pallas_call | solution.py:143
  125.9 1.9 %collective-permute-done.28 = bf16[2,2,64,1024]{3,2,1,0:T(8,128)(2,1)S(1)} collective-permute-done((bf16[2,2,64,1024]{3,2,1,0:T(8,128)(2,1)S(1)}, bf16[2,2,64,1024]{3,2,1,0:T(8,128)(2,1)S(1)}, u32[]{:S(2)}, u32[]{:S(2)}) %collective-permute-start.28) | collective-permute-done | bytes 524320 | tf_op jit(solution)/shard_map/scatter_second_2/ppermute | solution.py:172
  131.3 8.5 %collective-permute-done.29 = bf16[2,64,1024]{2,1,0:T(8,128)(2,1)S(1)} collective-permute-done((bf16[2,64,1024]{2,1,0:T(8,128)(2,1)S(1)}, bf16[2,64,1024]{2,1,0:T(8,128)(2,1)S(1)}, u32[]{:S(2)}, u32[]{:S(2)}) %collective-permute-start.29) | collective-permute-done | bytes 262176 | tf_op jit(solution)/shard_map/scatter_first_2/ppermute | solution.py:172
  139.9 6.7 %collective-permute-done.35 = bf16[2,2,128,1024]{3,2,1,0:T(8,128)(2,1)S(1)} collective-permute-done((bf16[2,2,128,1024]{3,2,1,0:T(8,128)(2,1)S(1)}, bf16[2,2,128,1024]{3,2,1,0:T(8,128)(2,1)S(1)}, u32[]{:S(2)}, u32[]{:S(2)}) %collective-permute-start.35) | collective-permute-done | bytes 1048608 | tf_op jit(solution)/shard_map/scatter_second_1/ppermute | solution.py:172
  149.3 6.1 %collective-permute-start.30 = (bf16[128,1024]{1,0:T(8,128)(2,1)S(1)}, bf16[128,1024]{1,0:T(8,128)(2,1)S(1)}, u32[]{:S(2)}, u32[]{:S(2)}) collective-permute-start(bf16[128,1024]{1,0:T(8,128)(2,1)S(1)} %pad_maximum_fusion.8), channel_id=1, source_target_pairs={{0,8},{1,9},{2,10},{3,11},{4,12},{5,13},{6,14},{7,15},{8,0},{9,1},... | collective-permute-start | bytes 786440 | tf_op jit(solution)/shard_map/to_plane_2/ppermute | solution.py:42
  156.7 7.3 %collective-permute-done.30 = bf16[128,1024]{1,0:T(8,128)(2,1)S(1)} collective-permute-done((bf16[128,1024]{1,0:T(8,128)(2,1)S(1)}, bf16[128,1024]{1,0:T(8,128)(2,1)S(1)}, u32[]{:S(2)}, u32[]{:S(2)}) %collective-permute-start.30) | collective-permute-done | bytes 262176 | tf_op jit(solution)/shard_map/to_plane_2/ppermute | solution.py:42
  168.1 9.7 %collective-permute-done.38 = bf16[128,1024]{1,0:T(8,128)(2,1)S(1)} collective-permute-done((bf16[128,1024]{1,0:T(8,128)(2,1)S(1)}, bf16[128,1024]{1,0:T(8,128)(2,1)S(1)}, u32[]{:S(2)}, u32[]{:S(2)}) %collective-permute-start.38) | collective-permute-done | bytes 262176 | tf_op jit(solution)/shard_map/to_plane_3/ppermute | solution.py:42
  (142 shorter events, 41.3 us)
Async XLA Ops:
  4.5 11.6 %collective-permute-start = (bf16[128,1024]{1,0:T(8,128)(2,1)S(1)}, bf16[128,1024]{1,0:T(8,128)(2,1)S(1)}, u32[]{:S(2)}, u32[]{:S(2)}) collective-permute-start(bf16[128,1024]{1,0:T(8,128)(2,1)S(1)} %get-tuple-element.34.rest_0_), channel_id=1, source_target_pairs={{0,4},{1,5},{2,6},{3,7},{4,8},{5,9},{6,10},{7,11},{8,12},{9,13},{1... | collective-permute-start | bytes 786440 | tf_op jit(solution)/shard_map/ppermute | solution.py:28
  9.4 11.8 %collective-permute-start.4 = (bf16[128,1024]{1,0:T(8,128)(2,1)}, bf16[128,1024]{1,0:T(8,128)(2,1)S(1)}, u32[]{:S(2)}, u32[]{:S(2)}) collective-permute-start(bf16[128,1024]{1,0:T(8,128)(2,1)} %rest_0_), channel_id=1, source_target_pairs={{0,4},{1,5},{2,6},{3,7},{4,8},{5,9},{6,10},{7,11},{8,12},{9,13},{1... | collective-permute-start | bytes 786440 | tf_op jit(solution)/shard_map/ppermute | solution.py:28
  16.9 9.1 %collective-permute-start.1 = (bf16[128,1024]{1,0:T(8,128)(2,1)S(1)}, bf16[128,1024]{1,0:T(8,128)(2,1)S(1)}, u32[]{:S(2)}, u32[]{:S(2)}) collective-permute-start(bf16[128,1024]{1,0:T(8,128)(2,1)S(1)} %get-tuple-element.83), channel_id=1, source_target_pairs={{0,1},{1,0},{2,3},{3,2},{4,5},{5,4},{6,7},{7,6},{8,9},{9,8},{10,11... | collective-permute-start | bytes 786440 | tf_op jit(solution)/shard_map/ppermute | solution.py:23
  19.2 13.8 %collective-permute-start.2 = (bf16[128,1024]{1,0:T(8,128)(2,1)}, bf16[128,1024]{1,0:T(8,128)(2,1)S(1)}, u32[]{:S(2)}, u32[]{:S(2)}) collective-permute-start(bf16[128,1024]{1,0:T(8,128)(2,1)} %get-tuple-element.82), channel_id=1, source_target_pairs={{0,2},{1,3},{2,0},{3,1},{4,6},{5,7},{6,4},{7,5},{8,10},{9,11},{10,... | collective-permute-start | bytes 786440 | tf_op jit(solution)/shard_map/ppermute | solution.py:23
  20.7 12.3 %collective-permute-start.3 = (bf16[128,1024]{1,0:T(8,128)(2,1)S(1)}, bf16[128,1024]{1,0:T(8,128)(2,1)S(1)}, u32[]{:S(2)}, u32[]{:S(2)}) collective-permute-start(bf16[128,1024]{1,0:T(8,128)(2,1)S(1)} %get-tuple-element.81), channel_id=1, source_target_pairs={{0,3},{1,2},{2,1},{3,0},{4,7},{5,6},{6,5},{7,4},{8,11},{9,10},{10,... | collective-permute-start | bytes 786440 | tf_op jit(solution)/shard_map/ppermute | solution.py:23
  22.2 14.9 %collective-permute-start.5 = (bf16[128,1024]{1,0:T(8,128)(2,1)}, bf16[128,1024]{1,0:T(8,128)(2,1)S(1)}, u32[]{:S(2)}, u32[]{:S(2)}) collective-permute-start(bf16[128,1024]{1,0:T(8,128)(2,1)} %get-tuple-element.80), channel_id=1, source_target_pairs={{0,1},{1,0},{2,3},{3,2},{4,5},{5,4},{6,7},{7,6},{8,9},{9,8},{10,11... | collective-permute-start | bytes 786440 | tf_op jit(solution)/shard_map/ppermute | solution.py:23
  23.7 18.3 %collective-permute-start.6 = (bf16[128,1024]{1,0:T(8,128)(2,1)}, bf16[128,1024]{1,0:T(8,128)(2,1)S(1)}, u32[]{:S(2)}, u32[]{:S(2)}) collective-permute-start(bf16[128,1024]{1,0:T(8,128)(2,1)} %get-tuple-element.79), channel_id=1, source_target_pairs={{0,2},{1,3},{2,0},{3,1},{4,6},{5,7},{6,4},{7,5},{8,10},{9,11},{10,... | collective-permute-start | bytes 786440 | tf_op jit(solution)/shard_map/ppermute | solution.py:23
  25.9 16.1 %collective-permute-start.7 = (bf16[128,1024]{1,0:T(8,128)(2,1)}, bf16[128,1024]{1,0:T(8,128)(2,1)S(1)}, u32[]{:S(2)}, u32[]{:S(2)}) collective-permute-start(bf16[128,1024]{1,0:T(8,128)(2,1)} %get-tuple-element.78), channel_id=1, source_target_pairs={{0,3},{1,2},{2,1},{3,0},{4,7},{5,6},{6,5},{7,4},{8,11},{9,10},{10,... | collective-permute-start | bytes 786440 | tf_op jit(solution)/shard_map/ppermute | solution.py:23
  50.1 11.6 %collective-permute-start.16 = (bf16[64,2176]{1,0:T(8,128)(2,1)S(1)}, bf16[64,2176]{1,0:T(8,128)(2,1)S(1)}, u32[]{:S(2)}, u32[]{:S(2)}) collective-permute-start(bf16[64,2176]{1,0:T(8,128)(2,1)S(1)} %get-tuple-element.44), channel_id=1, source_target_pairs={{4,0},{5,1},{6,2},{7,3},{8,4},{9,5},{10,6},{11,7},{12,8},{13,9},{1... | collective-permute-start | bytes 835592 | tf_op jit(solution)/shard_map/from_plane_1/ppermute | solution.py:34
  54.6 14.0 %collective-permute-start.17 = (bf16[64,2176]{1,0:T(8,128)(2,1)S(1)}, bf16[64,2176]{1,0:T(8,128)(2,1)S(1)}, u32[]{:S(2)}, u32[]{:S(2)}) collective-permute-start(bf16[64,2176]{1,0:T(8,128)(2,1)S(1)} %get-tuple-element.44), channel_id=1, source_target_pairs={{12,0},{13,1},{14,2},{15,3},{0,4},{1,5},{2,6},{3,7},{4,8},{5,9},{6... | collective-permute-start | bytes 835592 | tf_op jit(solution)/shard_map/from_plane_3/ppermute | solution.py:34
  56.1 28.8 %collective-permute-start.11 = (bf16[128,2176]{1,0:T(8,128)(2,1)S(1)}, bf16[128,2176]{1,0:T(8,128)(2,1)S(1)}, u32[]{:S(2)}, u32[]{:S(2)}) collective-permute-start(bf16[128,2176]{1,0:T(8,128)(2,1)S(1)} %constant_dynamic-update-slice_fusion.near_ref), channel_id=1, source_target_pairs={{16,0},{0,16},{17,1},{1,17},{18,2},{2,18},{19,3},{3,19},{20,4},{4,... | collective-permute-start | bytes 1671176 | tf_op jit(solution)/shard_map/ppermute | solution.py:49
  56.2 24.0 %collective-permute-start.10 = (bf16[128,2176]{1,0:T(8,128)(2,1)S(1)}, bf16[128,2176]{1,0:T(8,128)(2,1)S(1)}, u32[]{:S(2)}, u32[]{:S(2)}) collective-permute-start(bf16[128,2176]{1,0:T(8,128)(2,1)S(1)} %constant_dynamic-update-slice_fusion.near_ref), channel_id=1, source_target_pairs={{0,2},{1,3},{2,0},{3,1},{4,6},{5,7},{6,4},{7,5},{8,10},{9,11},{10,... | collective-permute-start | bytes 1671176 | tf_op jit(solution)/shard_map/gather_second_0/ppermute | solution.py:172
  57.8 21.5 %collective-permute-start.15 = (bf16[64,2176]{1,0:T(8,128)(2,1)S(1)}, bf16[64,2176]{1,0:T(8,128)(2,1)S(1)}, u32[]{:S(2)}, u32[]{:S(2)}) collective-permute-start(bf16[64,2176]{1,0:T(8,128)(2,1)S(1)} %get-tuple-element.44), channel_id=1, source_target_pairs={{8,0},{9,1},{10,2},{11,3},{12,4},{13,5},{14,6},{15,7},{0,8},{1,9},... | collective-permute-start | bytes 835592 | tf_op jit(solution)/shard_map/from_plane_2/ppermute | solution.py:34
  68.6 9.6 %collective-permute-start.18 = (bf16[128,2176]{1,0:T(8,128)(2,1)S(1)}, bf16[128,2176]{1,0:T(8,128)(2,1)S(1)}, u32[]{:S(2)}, u32[]{:S(2)}) collective-permute-start(bf16[128,2176]{1,0:T(8,128)(2,1)S(1)} %pad_maximum_fusion.1), channel_id=1, source_target_pairs={{0,1},{1,0},{2,3},{3,2},{4,5},{5,4},{6,7},{7,6},{8,9},{9,8},{10,11... | collective-permute-start | bytes 1671176 | tf_op jit(solution)/shard_map/gather_first_1/ppermute | solution.py:172
  79.3 9.0 %collective-permute-start.19 = (bf16[64,2176]{1,0:T(8,128)(2,1)S(1)}, bf16[64,2176]{1,0:T(8,128)(2,1)S(1)}, u32[]{:S(2)}, u32[]{:S(2)}) collective-permute-start(bf16[64,2176]{1,0:T(8,128)(2,1)S(1)} %collective-permute-done.15), channel_id=1, source_target_pairs={{0,1},{1,0},{2,3},{3,2},{4,5},{5,4},{6,7},{7,6},{8,9},{9,8},{10,11... | collective-permute-start | bytes 835592 | tf_op jit(solution)/shard_map/gather_first_2/ppermute | solution.py:172
  80.2 23.3 %collective-permute-start.23 = (bf16[256,2176]{1,0:T(8,128)(2,1)S(1)}, bf16[256,2176]{1,0:T(8,128)(2,1)S(1)}, u32[]{:S(2)}, u32[]{:S(2)}) collective-permute-start(bf16[256,2176]{1,0:T(8,128)(2,1)S(1)} %constant_dynamic-update-slice_fusion.2.near_ref), channel_id=1, source_target_pairs={{0,2},{1,3},{2,0},{3,1},{4,6},{5,7},{6,4},{7,5},{8,10},{9,11},{10,... | collective-permute-start | bytes 3342344 | tf_op jit(solution)/shard_map/gather_second_1/ppermute | solution.py:172
  88.4 13.4 %collective-permute-start.20 = (bf16[128,2176]{1,0:T(8,128)(2,1)S(1)}, bf16[128,2176]{1,0:T(8,128)(2,1)S(1)}, u32[]{:S(2)}, u32[]{:S(2)}) collective-permute-start(bf16[128,2176]{1,0:T(8,128)(2,1)S(1)} %constant_dynamic-update-slice_fusion.5.near_ref), channel_id=1, source_target_pairs={{0,2},{1,3},{2,0},{3,1},{4,6},{5,7},{6,4},{7,5},{8,10},{9,11},{10,... | collective-permute-start | bytes 1671176 | tf_op jit(solution)/shard_map/gather_second_2/ppermute | solution.py:172
  92.1 14.7 %collective-permute-start.13 = (bf16[4,64,1024]{2,1,0:T(8,128)(2,1)S(1)}, bf16[4,64,1024]{2,1,0:T(8,128)(2,1)S(1)}, u32[]{:S(2)}, u32[]{:S(2)}) collective-permute-start(bf16[4,64,1024]{2,1,0:T(8,128)(2,1)S(1)} %get-tuple-element.42), channel_id=1, source_target_pairs={{16,0},{0,16},{17,1},{1,17},{18,2},{2,18},{19,3},{3,19},{20,4},{4,... | collective-permute-start | bytes 1572872 | tf_op jit(solution)/shard_map/ppermute | solution.py:49
  92.2 28.0 %collective-permute-start.31 = (bf16[256,2176]{1,0:T(8,128)(2,1)S(1)}, bf16[256,2176]{1,0:T(8,128)(2,1)S(1)}, u32[]{:S(2)}, u32[]{:S(2)}) collective-permute-start(bf16[256,2176]{1,0:T(8,128)(2,1)S(1)} %constant_dynamic-update-slice_fusion.2.near_ref), channel_id=1, source_target_pairs={{16,0},{0,16},{17,1},{1,17},{18,2},{2,18},{19,3},{3,19},{20,4},{4,... | collective-permute-start | bytes 3342344 | tf_op jit(solution)/shard_map/ppermute | solution.py:49
  92.7 15.4 %collective-permute-start.24 = (bf16[128,2176]{1,0:T(8,128)(2,1)S(1)}, bf16[128,2176]{1,0:T(8,128)(2,1)S(1)}, u32[]{:S(2)}, u32[]{:S(2)}) collective-permute-start(bf16[128,2176]{1,0:T(8,128)(2,1)S(1)} %constant_dynamic-update-slice_fusion.5.near_ref), channel_id=1, source_target_pairs={{16,0},{0,16},{17,1},{1,17},{18,2},{2,18},{19,3},{3,19},{20,4},{4,... | collective-permute-start | bytes 1671176 | tf_op jit(solution)/shard_map/ppermute | solution.py:49
  106.8 11.0 %collective-permute-start.27 = (bf16[4,64,1024]{2,1,0:T(8,128)(2,1)S(1)}, bf16[4,64,1024]{2,1,0:T(8,128)(2,1)S(1)}, u32[]{:S(2)}, u32[]{:S(2)}) collective-permute-start(bf16[4,64,1024]{2,1,0:T(8,128)(2,1)S(1)} %get-tuple-element.49), channel_id=1, source_target_pairs={{16,0},{0,16},{17,1},{1,17},{18,2},{2,18},{19,3},{3,19},{20,4},{4,... | collective-permute-start | bytes 1572872 | tf_op jit(solution)/shard_map/ppermute | solution.py:49
  107.1 12.8 %collective-permute-start.21 = (bf16[2,2,64,1024]{3,2,1,0:T(8,128)(2,1)S(1)}, bf16[2,2,64,1024]{3,2,1,0:T(8,128)(2,1)S(1)}, u32[]{:S(2)}, u32[]{:S(2)}) collective-permute-start(bf16[2,2,64,1024]{3,2,1,0:T(8,128)(2,1)S(1)} %pad_maximum_fusion.3), channel_id=1, source_target_pairs={{0,2},{1,3},{2,0},{3,1},{4,6},{5,7},{6,4},{7,5},{8,10},{9,11},{10,... | collective-permute-start | bytes 1572872 | tf_op jit(solution)/shard_map/scatter_second_0/ppermute | solution.py:172
  108.1 12.1 %collective-permute-start.32 = (bf16[256,2176]{1,0:T(8,128)(2,1)S(1)}, bf16[256,2176]{1,0:T(8,128)(2,1)S(1)}, u32[]{:S(2)}, u32[]{:S(2)}) collective-permute-start(bf16[256,2176]{1,0:T(8,128)(2,1)S(1)} %collective-permute-done.23.far_ref), channel_id=1, source_target_pairs={{16,0},{0,16},{17,1},{1,17},{18,2},{2,18},{19,3},{3,19},{20,4},{4,... | collective-permute-start | bytes 3342344 | tf_op jit(solution)/shard_map/ppermute | solution.py:49
  117.8 10.3 %collective-permute-start.34 = (bf16[4,128,1024]{2,1,0:T(8,128)(2,1)S(1)}, bf16[4,128,1024]{2,1,0:T(8,128)(2,1)S(1)}, u32[]{:S(2)}, u32[]{:S(2)}) collective-permute-start(bf16[4,128,1024]{2,1,0:T(8,128)(2,1)S(1)} %get-tuple-element.55), channel_id=1, source_target_pairs={{16,0},{0,16},{17,1},{1,17},{18,2},{2,18},{19,3},{3,19},{20,4},{4,... | collective-permute-start | bytes 3145736 | tf_op jit(solution)/shard_map/ppermute | solution.py:49
  118.6 9.2 %collective-permute-start.28 = (bf16[2,2,64,1024]{3,2,1,0:T(8,128)(2,1)S(1)}, bf16[2,2,64,1024]{3,2,1,0:T(8,128)(2,1)S(1)}, u32[]{:S(2)}, u32[]{:S(2)}) collective-permute-start(bf16[2,2,64,1024]{3,2,1,0:T(8,128)(2,1)S(1)} %pad_maximum_fusion.4), channel_id=1, source_target_pairs={{0,2},{1,3},{2,0},{3,1},{4,6},{5,7},{6,4},{7,5},{8,10},{9,11},{10,... | collective-permute-start | bytes 1572872 | tf_op jit(solution)/shard_map/scatter_second_2/ppermute | solution.py:172
  129.2 17.3 %collective-permute-start.35 = (bf16[2,2,128,1024]{3,2,1,0:T(8,128)(2,1)S(1)}, bf16[2,2,128,1024]{3,2,1,0:T(8,128)(2,1)S(1)}, u32[]{:S(2)}, u32[]{:S(2)}) collective-permute-start(bf16[2,2,128,1024]{3,2,1,0:T(8,128)(2,1)S(1)} %pad_maximum_fusion), channel_id=1, source_target_pairs={{0,2},{1,3},{2,0},{3,1},{4,6},{5,7},{6,4},{7,5},{8,10},{9,11},{10,... | collective-permute-start | bytes 3145736 | tf_op jit(solution)/shard_map/scatter_second_1/ppermute | solution.py:172
  130.5 9.2 %collective-permute-start.29 = (bf16[2,64,1024]{2,1,0:T(8,128)(2,1)S(1)}, bf16[2,64,1024]{2,1,0:T(8,128)(2,1)S(1)}, u32[]{:S(2)}, u32[]{:S(2)}) collective-permute-start(bf16[2,64,1024]{2,1,0:T(8,128)(2,1)S(1)} %pad_maximum_fusion.7), channel_id=1, source_target_pairs={{0,1},{1,0},{2,3},{3,2},{4,5},{5,4},{6,7},{7,6},{8,9},{9,8},{10,11... | collective-permute-start | bytes 786440 | tf_op jit(solution)/shard_map/scatter_first_2/ppermute | solution.py:172
  147.2 9.2 %collective-permute-start.36 = (bf16[2,128,1024]{2,1,0:T(8,128)(2,1)S(1)}, bf16[2,128,1024]{2,1,0:T(8,128)(2,1)S(1)}, u32[]{:S(2)}, u32[]{:S(2)}) collective-permute-start(bf16[2,128,1024]{2,1,0:T(8,128)(2,1)S(1)} %pad_maximum_fusion.5), channel_id=1, source_target_pairs={{0,1},{1,0},{2,3},{3,2},{4,5},{5,4},{6,7},{7,6},{8,9},{9,8},{10,11... | collective-permute-start | bytes 1572872 | tf_op jit(solution)/shard_map/scatter_first_1/ppermute | solution.py:172
  148.5 19.6 %collective-permute-start.22 = (bf16[2,64,1024]{2,1,0:T(8,128)(2,1)S(1)}, bf16[2,64,1024]{2,1,0:T(8,128)(2,1)S(1)}, u32[]{:S(2)}, u32[]{:S(2)}) collective-permute-start(bf16[2,64,1024]{2,1,0:T(8,128)(2,1)S(1)} %pad_maximum_fusion.6), channel_id=1, source_target_pairs={{0,1},{1,0},{2,3},{3,2},{4,5},{5,4},{6,7},{7,6},{8,9},{9,8},{10,11... | collective-permute-start | bytes 786440 | tf_op jit(solution)/shard_map/scatter_first_0/ppermute | solution.py:172
  149.3 14.7 %collective-permute-start.30 = (bf16[128,1024]{1,0:T(8,128)(2,1)S(1)}, bf16[128,1024]{1,0:T(8,128)(2,1)S(1)}, u32[]{:S(2)}, u32[]{:S(2)}) collective-permute-start(bf16[128,1024]{1,0:T(8,128)(2,1)S(1)} %pad_maximum_fusion.8), channel_id=1, source_target_pairs={{0,8},{1,9},{2,10},{3,11},{4,12},{5,13},{6,14},{7,15},{8,0},{9,1},... | collective-permute-start | bytes 786440 | tf_op jit(solution)/shard_map/to_plane_2/ppermute | solution.py:42
  164.0 13.8 %collective-permute-start.38 = (bf16[128,1024]{1,0:T(8,128)(2,1)S(1)}, bf16[128,1024]{1,0:T(8,128)(2,1)S(1)}, u32[]{:S(2)}, u32[]{:S(2)}) collective-permute-start(bf16[128,1024]{1,0:T(8,128)(2,1)S(1)} %pad_maximum_fusion.10), channel_id=1, source_target_pairs={{0,12},{1,13},{2,14},{3,15},{4,0},{5,1},{6,2},{7,3},{8,4},{9,5},{1... | collective-permute-start | bytes 786440 | tf_op jit(solution)/shard_map/to_plane_3/ppermute | solution.py:42
  166.2 11.7 %collective-permute-start.37 = (bf16[128,1024]{1,0:T(8,128)(2,1)}, bf16[128,1024]{1,0:T(8,128)(2,1)S(1)}, u32[]{:S(2)}, u32[]{:S(2)}) collective-permute-start(bf16[128,1024]{1,0:T(8,128)(2,1)} %pad_maximum_fusion.9), channel_id=1, source_target_pairs={{0,4},{1,5},{2,6},{3,7},{4,8},{5,9},{6,10},{7,11},{8,12},{9,13},{1... | collective-permute-start | bytes 786440 | tf_op jit(solution)/shard_map/to_plane_1/ppermute | solution.py:42
  (20 other events, 249.4 us)

commit v9 on v7

--- a/solution.py
+++ b/solution.py
@@ -326,53 +326,56 @@
         [norm_gain[None, :], lanes, *addends],
     )
     weights = (w_gate[0].T, w_up[0].T, w_down[0])
-    if planes <= 4:
-        groups = [[0]] + [sorted({i, planes - i}) for i in range(1, planes // 2 + 1)]
-    else:
-        groups = [[0]] + [list(range(i, min(i + 8, planes))) for i in range(1, planes, 8)]
-    nears, fars = [], []
+    size = 1 if planes <= 4 else 4
+    groups = [[0]] + [
+        list(range(i, min(i + size, planes))) for i in range(1, planes, size)
+    ]
     weights = (w_gate[0].T, w_up[0].T, w_down[0])
-    run = functools.partial(
-        expert_outputs, place, weights=weights, experts=experts, cores=cores
-    )
-    for number, group in enumerate(groups):
-        sent = after(payload, nears[0]) if number > 1 else payload
-        column = jnp.concatenate([from_plane(sent, ahead) if ahead else sent for ahead in group])
+    columns, nears, fars = [], [], []
+    every, seconds, firsts, ready, returned = [], [], [], [], []
+    for step in range(len(groups) + 1):
+        if step < len(groups):
+            source = after(payload, nears[step - 2]) if step > 1 else payload
+            column = jnp.concatenate(
+                [from_plane(source, ahead) if ahead else source for ahead in groups[step]]
+            )
+            waits = [*nears[-1:]]
+            if step > 1:
+                waits.append(fars[step - 2])
+            if step > 2:
+                waits.append(every[step - 3])
+            columns.append(after(column, *waits))
+            got = crossed(columns[-1], True, f"gather_first_{step}")
+            nears.append(jnp.concatenate([columns[-1], got]))
+        if step == 0:
+            continue
+        number, group = step - 1, groups[step - 1]
+        fars.append(crossed(nears[number], False, f"gather_second_{number}"))
+        waits = {0: [*every[-1:], *nears[step : step + 1]], cores - 1: []}
+        if number > 0:
+            waits[cores - 1].append(seconds[-1])
         if number > 1:
-            column = after(column, nears[-1])
-        nears.append(jnp.concatenate([column, crossed(column, True, f"gather_first_{number}")]))
-        if number > 1 and number == len(groups) - 1:
-            outs = run(nears[0], fars[0], waits={})
-            nears[-1] = after(nears[-1], *outs)
-        fars.append(crossed(after(nears[-1], *fars[-1:]), False, f"gather_second_{number}"))
-    totals = core_totals(outs, cores)
-    sent = second_share(totals)
-    totals = merged(totals, crossed(after(sent, fars[-1]), False, "scatter_second_0"), 2)
-    shared = first_share(totals)
-    partial = (totals, crossed(shared, True, "scatter_first_0"))
-    results = {}
-    returned = []
-    for number in reversed(range(1, len(groups))):
-        waits = {0: [outs], cores - 1: [sent]}
-        if number < len(groups) - 1:
-            waits[cores - 1] = [sent, shared]
-        outs = run(nears[number], fars[number], waits=waits)
+            waits[0].append(firsts[-2])
+            waits[cores - 1].append(ready[-2])
+        far = after(fars[number], *[outs[0] for outs in every[-1:]])
+        outs = expert_outputs(place, nears[number], far, weights, experts, cores, waits)
+        every.append(outs)
         totals = core_totals(outs, cores)
-        if number < len(groups) - 1:
-            totals = [after(total, late) for total in totals]
-        sent = second_share(totals)
-        totals = merged(totals, crossed(sent, False, f"scatter_second_{number}"), 2)
-        late = after(first_share(totals), *results.values())
-        came = crossed(late, True, f"scatter_first_{number}")
+        seconds.append(second_share(totals))
+        totals = merged(totals, crossed(seconds[-1], False, f"scatter_second_{number}"), 2)
+        firsts.append(first_share(totals))
+        came = crossed(firsts[-1], True, f"scatter_first_{number}")
         rows_of = merged([total[0] for total in totals], came, None)
-        results = {}
-        for i, ahead in enumerate(groups[number]):
+        if group == [0]:
+            moe = jnp.concatenate(rows_of)
+            ready.append(moe)
+            continue
+        blocks = []
+        for i in range(len(group)):
             piece = [rows[i * part_rows : (i + 1) * part_rows] for rows in rows_of]
-            results[ahead] = after(narrow(jnp.concatenate(piece)), *returned[-1:])
-        for ahead, block in results.items():
-            returned.append(to_plane(block, ahead))
-    totals, came = partial
-    moe = jnp.concatenate(merged([total[0] for total in totals], came, None))
+            blocks.append(narrow(jnp.concatenate(piece)))
+        ready.append(blocks)
+        returned += [to_plane(block, ahead) for block, ahead in zip(blocks, group, strict=True)]
     moe = moe + sum(wide(block) for block in returned)
     moe = jnp.roll(moe.reshape(cores, part_rows, col_width), tok_index, axis=0)
     moe = moe.reshape(tok_rows, col_width)

time: 184 us -> 178 us (0.967); the launches traced: 184 us -> 176 us
  waiting for transfers between devices: 87.3 us -> 74 us
    ppermute x3, waiting for transfers between devices: 15.7 us -> 5.15 us  [to_plane(): lax.ppermute(block, 'blk', [(i, (i + PLANE * ahead) % count) for i in ran...]
    ppermute x12 -> x16, waiting for transfers between devices: 51.3 us -> 42.6 us  [crossed(): return lax.ppermute(block, ('tok', 'blk'), route)]
    ppermute x3, waiting for transfers between devices: 5.53 us -> 11.8 us  [from_plane(): lax.ppermute(block, 'blk', [((i + PLANE * ahead) % count, i) for i in ran...]
    ppermute x12 -> x16, starting transfers between devices: 17.1 us -> 14.5 us  [crossed(): return lax.ppermute(block, ('tok', 'blk'), route)]
    ppermute x13 -> x17, starting transfers between devices: 2.64 us -> 4.57 us  [from_core(): lax.ppermute(block, 'tok', [((i + ahead) % count, i) for i in range(count)])]
    pallas_call x10 -> x12, Pallas kernels: 29.9 us -> 31.4 us  [local_call(): pl.pallas_call(body, in_specs=[scalar] * len(scalars) + [whole] * len(arr...]
    unnamed x28 -> x30, local copies, waits for them, and re-layouts: 6.18 us -> 6.18 us
  transfers between devices with their start and end apart: 39 -> 47, of which waited for: 22 -> 18; matrix products, arithmetic and copies ran while one was open for 5% -> 8% of each run, Pallas kernels for 14% -> 16%
where the time goes in v9:
time: 178 us; the launch traced here: 176 us
  waiting for transfers between devices  74 us (42%)
  starting transfers between devices  49.1 us (28%)
  Pallas kernels  31.4 us (18%)
  local copies, waits for them, and re-layouts  10.4 us (6%)
  other arithmetic  9.49 us (5%)
    ppermute x16, waiting for transfers between devices, crossed(): return lax.ppermute(block, ('tok', 'blk'), route)  42.6 us
    pallas_call x12, Pallas kernels, local_call(): pl.pallas_call(body, in_specs=[scalar] * len(scalars) + [whole] * len(arr...  31.4 us
    ppermute x16, starting transfers between devices, crossed(): return lax.ppermute(block, ('tok', 'blk'), route)  14.5 us
    ppermute x3, waiting for transfers between devices, from_plane(): lax.ppermute(block, 'blk', [((i + PLANE * ahead) % count, i) for i in ran...  11.8 us
    ppermute x6, waiting for transfers between devices, flipped(): lax.ppermute(block, 'blk', [(i, i ^ mask) for i in range(lax.axis_size('b...  8.92 us
    ppermute x6, starting transfers between devices, flipped(): lax.ppermute(block, 'blk', [(i, i ^ mask) for i in range(lax.axis_size('b...  8.75 us
    ppermute x2, starting transfers between devices, next_plane(): lax.ppermute(block, 'blk', [(i, i + PLANE) for i in range(count - PLANE)])  8.43 us
    ppermute x3, starting transfers between devices, to_plane(): lax.ppermute(block, 'blk', [(i, (i + PLANE * ahead) % count) for i in ran...  6.83 us
  transfers between devices with their start and end apart: 47, of which 18 were waited for; matrix products, arithmetic and copies ran while one was open for 8% of the time, Pallas kernels for 16%

profile of v9, /device:TPU:0, one launch (start us, length us, event | category | flops | bytes accessed | tf_op | source)
XLA Modules:
  0.0 175.8 jit_solution(15380874739346845035)
XLA Ops:
  4.5 4.9 %collective-permute-start = (bf16[128,1024]{1,0:T(8,128)(2,1)S(1)}, bf16[128,1024]{1,0:T(8,128)(2,1)S(1)}, u32[]{:S(2)}, u32[]{:S(2)}) collective-permute-start(bf16[128,1024]{1,0:T(8,128)(2,1)S(1)} %get-tuple-element.41.rest_0_), channel_id=1, source_target_pairs={{0,4},{1,5},{2,6},{3,7},{4,8},{5,9},{6,10},{7,11},{8,12},{9,13},{1... | collective-permute-start | bytes 786440 | tf_op jit(solution)/shard_map/ppermute | solution.py:27
  9.4 3.5 %collective-permute-start.4 = (bf16[128,1024]{1,0:T(8,128)(2,1)}, bf16[128,1024]{1,0:T(8,128)(2,1)S(1)}, u32[]{:S(2)}, u32[]{:S(2)}) collective-permute-start(bf16[128,1024]{1,0:T(8,128)(2,1)} %rest_0_), channel_id=1, source_target_pairs={{0,4},{1,5},{2,6},{3,7},{4,8},{5,9},{6,10},{7,11},{8,12},{9,13},{1... | collective-permute-start | bytes 786440 | tf_op jit(solution)/shard_map/ppermute | solution.py:27
  13.7 2.4 %collective-permute-done.rest_1_ = bf16[128,1024]{1,0:T(8,128)(2,1)S(1)} collective-permute-done((bf16[128,1024]{1,0:T(8,128)(2,1)S(1)}, bf16[128,1024]{1,0:T(8,128)(2,1)S(1)}, u32[]{:S(2)}, u32[]{:S(2)}) %collective-permute-start) | collective-permute-done | bytes 262176 | tf_op jit(solution)/shard_map/ppermute | solution.py:27
  26.1 2.2 %collective-permute-start.7 = (bf16[128,1024]{1,0:T(8,128)(2,1)}, bf16[128,1024]{1,0:T(8,128)(2,1)S(1)}, u32[]{:S(2)}, u32[]{:S(2)}) collective-permute-start(bf16[128,1024]{1,0:T(8,128)(2,1)} %get-tuple-element.92), channel_id=1, source_target_pairs={{0,3},{1,2},{2,1},{3,0},{4,7},{5,6},{6,5},{7,4},{8,11},{9,10},{10,... | collective-permute-start | bytes 786440 | tf_op jit(solution)/shard_map/ppermute | solution.py:22
  29.4 2.7 %scatter_fusion = bf16[8,16,2,1024]{3,1,2,0:T(8,128)(2,1)} fusion(bf16[8,16,2,1024]{3,1,2,0:T(8,128)(2,1)} %broadcast_in_dim.31, s32[8]{0:T(128)S(1)} %compare_select_fusion, bf16[8,16,2,1024]{3,1,2,0:T(8,128)(2,1)} %pad_maximum_fusion.1), kind=kCustom, calls=%fused_computation | custom fusion | bytes 1572896 | tf_op jit(solution)/shard_map/scatter | solution.py:305
  32.1 3.1 %collective-permute-done.2.rest_3_ = bf16[128,1024]{1,0:T(8,128)(2,1)S(1)} collective-permute-done((bf16[128,1024]{1,0:T(8,128)(2,1)}, bf16[128,1024]{1,0:T(8,128)(2,1)S(1)}, u32[]{:S(2)}, u32[]{:S(2)}) %collective-permute-start.2) | collective-permute-done | bytes 262176 | tf_op jit(solution)/shard_map/ppermute | solution.py:22
  35.2 1.9 %shard_map.141.prob_ref = bf16[8,128,640]{2,1,0:T(8,128)(2,1)S(1)} custom-call(s32[2]{0:T(128)S(1)} %pad_add_fusion.place_ref, s32[8]{0:T(128)S(1)} %copy-done.10, bf16[128,1024]{1,0:T(8,128)(2,1)S(1)} %get-tuple-element.40.q_ref, bf16[128,1024]{1,0:T(8,128)(2,1)S(1)} %get-tuple-element.41.rest_0_, bf16[128,1024]{1,0:T(8,128)(2,1)S(1)} %collective-permute-done.rest_1_, ...), custom_call_target="tpu_custom_call" | custom-call | flops 167772160 | bytes 2883584 | tf_op jit(solution)/shard_map/pallas_call | solution.py:142
  37.2 5.8 %collective-permute-done.6.rest_3_ = bf16[128,1024]{1,0:T(8,128)(2,1)S(1)} collective-permute-done((bf16[128,1024]{1,0:T(8,128)(2,1)}, bf16[128,1024]{1,0:T(8,128)(2,1)S(1)}, u32[]{:S(2)}, u32[]{:S(2)}) %collective-permute-start.6) | collective-permute-done | bytes 262176 | tf_op jit(solution)/shard_map/ppermute | solution.py:22
  43.0 2.2 %copy-done.3 = bf16[1024,2048]{1,0:T(8,128)(2,1)S(1)} copy-done((bf16[1024,2048]{1,0:T(8,128)(2,1)S(1)}, bf16[1024,2048]{1,0:T(8,128)(2,1)}, u32[]{:S(2)}) %copy-start.3) | copy-done | bytes 4194328
  47.0 2.6 %collective-permute-done.8.rest_1_ = f32[128,2048]{1,0:T(8,128)S(1)} collective-permute-done((f32[128,2048]{1,0:T(8,128)S(1)}, f32[128,2048]{1,0:T(8,128)S(1)}, u32[]{:S(2)}, u32[]{:S(2)}) %collective-permute-start.8) | collective-permute-done | bytes 1048608 | tf_op jit(solution)/shard_map/ppermute | solution.py:48
  51.0 4.5 %collective-permute-start.10 = (bf16[64,2176]{1,0:T(8,128)(2,1)S(1)}, bf16[64,2176]{1,0:T(8,128)(2,1)S(1)}, u32[]{:S(2)}, u32[]{:S(2)}) collective-permute-start(bf16[64,2176]{1,0:T(8,128)(2,1)S(1)} %get-tuple-element.53), channel_id=1, source_target_pairs={{4,0},{5,1},{6,2},{7,3},{8,4},{9,5},{10,6},{11,7},{12,8},{13,9},{1... | collective-permute-start | bytes 835592 | tf_op jit(solution)/shard_map/from_plane_1/ppermute | solution.py:33
  58.7 3.8 %collective-permute-done.10 = bf16[64,2176]{1,0:T(8,128)(2,1)S(1)} collective-permute-done((bf16[64,2176]{1,0:T(8,128)(2,1)S(1)}, bf16[64,2176]{1,0:T(8,128)(2,1)S(1)}, u32[]{:S(2)}, u32[]{:S(2)}) %collective-permute-start.10) | collective-permute-done | bytes 278560 | tf_op jit(solution)/shard_map/from_plane_1/ppermute | solution.py:33
  64.5 4.5 %collective-permute-done.11 = bf16[64,2176]{1,0:T(8,128)(2,1)S(1)} collective-permute-done((bf16[64,2176]{1,0:T(8,128)(2,1)S(1)}, bf16[64,2176]{1,0:T(8,128)(2,1)S(1)}, u32[]{:S(2)}, u32[]{:S(2)}) %collective-permute-start.11) | collective-permute-done | bytes 278560 | tf_op jit(solution)/shard_map/gather_first_1/ppermute | solution.py:171
  69.9 8.0 %collective-permute-done.19 = bf16[64,2176]{1,0:T(8,128)(2,1)S(1)} collective-permute-done((bf16[64,2176]{1,0:T(8,128)(2,1)S(1)}, bf16[64,2176]{1,0:T(8,128)(2,1)S(1)}, u32[]{:S(2)}, u32[]{:S(2)}) %collective-permute-start.19) | collective-permute-done | bytes 278560 | tf_op jit(solution)/shard_map/from_plane_2/ppermute | solution.py:33
  78.0 3.2 %shard_map.144 = (bf16[4,64,1024]{2,1,0:T(8,128)(2,1)S(1)}, bf16[4,64,1024]{2,1,0:T(8,128)(2,1)S(1)}) custom-call(s32[2]{0:T(128)S(1)} %pad_add_fusion.place_ref, bf16[128,2176]{1,0:T(8,128)(2,1)S(1)} %pad_maximum_fusion.near_ref, bf16[128,2176]{1,0:T(8,128)(2,1)S(1)} %collective-permute-done.12.far_ref, bf16[704,2048]{1,0:T(8,128)(2,1)S(1)} %bitcast.95, ...), custom_call_target="tpu_custom_call" | custom-call | flops 2214592512 | bytes 256 | tf_op jit(solution)/shard_map/pallas_call | solution.py:142
  81.3 2.0 %collective-permute-start.16 = (bf16[4,64,1024]{2,1,0:T(8,128)(2,1)S(1)}, bf16[4,64,1024]{2,1,0:T(8,128)(2,1)S(1)}, u32[]{:S(2)}, u32[]{:S(2)}) collective-permute-start(bf16[4,64,1024]{2,1,0:T(8,128)(2,1)S(1)} %get-tuple-element.49), channel_id=1, source_target_pairs={{16,0},{0,16},{17,1},{1,17},{18,2},{2,18},{19,3},{3,19},{20,4},{4,... | collective-permute-start | bytes 1572872 | tf_op jit(solution)/shard_map/ppermute | solution.py:48
  83.3 4.5 %collective-permute-done.20 = bf16[64,2176]{1,0:T(8,128)(2,1)S(1)} collective-permute-done((bf16[64,2176]{1,0:T(8,128)(2,1)S(1)}, bf16[64,2176]{1,0:T(8,128)(2,1)S(1)}, u32[]{:S(2)}, u32[]{:S(2)}) %collective-permute-start.20) | collective-permute-done | bytes 278560 | tf_op jit(solution)/shard_map/gather_first_2/ppermute | solution.py:171
  89.7 3.2 %shard_map.145 = (bf16[4,64,1024]{2,1,0:T(8,128)(2,1)S(1)}, bf16[4,64,1024]{2,1,0:T(8,128)(2,1)S(1)}) custom-call(s32[2]{0:T(128)S(1)} %pad_add_fusion.place_ref, bf16[128,2176]{1,0:T(8,128)(2,1)S(1)} %collective-permute-done.13.near_ref, bf16[128,2176]{1,0:T(8,128)(2,1)S(1)} %collective-permute-done.14.far_ref, bf16[704,2048]{1,0:T(8,128)(2,1)S(1)} %bitcast.96, ...), custom_call_target="tpu_custom_call" | custom-call | flops 2214592512 | bytes 256 | tf_op jit(solution)/shard_map/pallas_call | solution.py:142
  93.5 3.2 %shard_map.146 = (bf16[4,64,1024]{2,1,0:T(8,128)(2,1)S(1)}, bf16[4,64,1024]{2,1,0:T(8,128)(2,1)S(1)}) custom-call(s32[2]{0:T(128)S(1)} %pad_add_fusion.place_ref, bf16[128,2176]{1,0:T(8,128)(2,1)S(1)} %constant_dynamic-update-slice_fusion.near_ref, bf16[128,2176]{1,0:T(8,128)(2,1)S(1)} %collective-permute-done.21.far_ref, bf16[704,2048]{1,0:T(8,128)(2,1)S(1)} %bitcast.97, ...), custom_call_target="tpu_custom_call" | custom-call | flops 2214592512 | bytes 256 | tf_op jit(solution)/shard_map/pallas_call | solution.py:142
  96.8 3.7 %collective-permute-done.31.far_ref = bf16[128,2176]{1,0:T(8,128)(2,1)S(1)} collective-permute-done((bf16[128,2176]{1,0:T(8,128)(2,1)S(1)}, bf16[128,2176]{1,0:T(8,128)(2,1)S(1)}, u32[]{:S(2)}, u32[]{:S(2)}) %collective-permute-start.31) | collective-permute-done | bytes 557088 | tf_op jit(solution)/shard_map/gather_second_2/ppermute | solution.py:171
  103.5 3.2 %shard_map.147 = (bf16[4,64,1024]{2,1,0:T(8,128)(2,1)S(1)}, bf16[4,64,1024]{2,1,0:T(8,128)(2,1)S(1)}) custom-call(s32[2]{0:T(128)S(1)} %pad_add_fusion.place_ref, bf16[128,2176]{1,0:T(8,128)(2,1)S(1)} %collective-permute-done.22.near_ref, bf16[128,2176]{1,0:T(8,128)(2,1)S(1)} %collective-permute-done.23.far_ref, bf16[704,2048]{1,0:T(8,128)(2,1)S(1)} %bitcast.98, ...), custom_call_target="tpu_custom_call" | custom-call | flops 2214592512 | bytes 256 | tf_op jit(solution)/shard_map/pallas_call | solution.py:142
  107.0 9.6 %collective-permute-done.17 = bf16[2,2,64,1024]{3,2,1,0:T(8,128)(2,1)S(1)} collective-permute-done((bf16[2,2,64,1024]{3,2,1,0:T(8,128)(2,1)S(1)}, bf16[2,2,64,1024]{3,2,1,0:T(8,128)(2,1)S(1)}, u32[]{:S(2)}, u32[]{:S(2)}) %collective-permute-start.17) | collective-permute-done | bytes 524320 | tf_op jit(solution)/shard_map/scatter_second_0/ppermute | solution.py:171
  118.9 3.4 %shard_map.148 = (bf16[4,64,1024]{2,1,0:T(8,128)(2,1)S(1)}, bf16[4,64,1024]{2,1,0:T(8,128)(2,1)S(1)}) custom-call(s32[2]{0:T(128)S(1)} %pad_add_fusion.place_ref, bf16[128,2176]{1,0:T(8,128)(2,1)S(1)} %constant_dynamic-update-slice_fusion.2.near_ref, bf16[128,2176]{1,0:T(8,128)(2,1)S(1)} %collective-permute-done.31.far_ref, bf16[704,2048]{1,0:T(8,128)(2,1)S(1)} %bitcast.99, ...), custom_call_target="tpu_custom_call" | custom-call | flops 2214592512 | bytes 256 | tf_op jit(solution)/shard_map/pallas_call | solution.py:142
  122.5 3.2 %shard_map.149 = (bf16[4,64,1024]{2,1,0:T(8,128)(2,1)S(1)}, bf16[4,64,1024]{2,1,0:T(8,128)(2,1)S(1)}) custom-call(s32[2]{0:T(128)S(1)} %pad_add_fusion.place_ref, bf16[128,2176]{1,0:T(8,128)(2,1)S(1)} %collective-permute-done.32.near_ref, bf16[128,2176]{1,0:T(8,128)(2,1)S(1)} %collective-permute-done.33.far_ref, bf16[704,2048]{1,0:T(8,128)(2,1)S(1)} %bitcast.100, ...), custom_call_target="tpu_custom_call" | custom-call | flops 2214592512 | bytes 256 | tf_op jit(solution)/shard_map/pallas_call | solution.py:142
  128.0 3.2 %shard_map.150 = (bf16[4,64,1024]{2,1,0:T(8,128)(2,1)S(1)}, bf16[4,64,1024]{2,1,0:T(8,128)(2,1)S(1)}) custom-call(s32[2]{0:T(128)S(1)} %pad_add_fusion.place_ref, bf16[128,2176]{1,0:T(8,128)(2,1)S(1)} %constant_dynamic-update-slice_fusion.4.near_ref, bf16[128,2176]{1,0:T(8,128)(2,1)S(1)} %collective-permute-done.39.far_ref, bf16[704,2048]{1,0:T(8,128)(2,1)S(1)} %bitcast.101, ...), custom_call_target="tpu_custom_call" | custom-call | flops 2214592512 | bytes 256 | tf_op jit(solution)/shard_map/pallas_call | solution.py:142
  133.1 3.2 %shard_map.151 = (bf16[4,64,1024]{2,1,0:T(8,128)(2,1)S(1)}, bf16[4,64,1024]{2,1,0:T(8,128)(2,1)S(1)}) custom-call(s32[2]{0:T(128)S(1)} %pad_add_fusion.place_ref, bf16[128,2176]{1,0:T(8,128)(2,1)S(1)} %collective-permute-done.40.near_ref, bf16[128,2176]{1,0:T(8,128)(2,1)S(1)} %collective-permute-done.41.far_ref, bf16[704,2048]{1,0:T(8,128)(2,1)S(1)} %bitcast.102, ...), custom_call_target="tpu_custom_call" | custom-call | flops 2214592512 | bytes 256 | tf_op jit(solution)/shard_map/pallas_call | solution.py:142
  141.0 7.5 %collective-permute-done.36 = bf16[2,2,64,1024]{3,2,1,0:T(8,128)(2,1)S(1)} collective-permute-done((bf16[2,2,64,1024]{3,2,1,0:T(8,128)(2,1)S(1)}, bf16[2,2,64,1024]{3,2,1,0:T(8,128)(2,1)S(1)}, u32[]{:S(2)}, u32[]{:S(2)}) %collective-permute-start.36) | collective-permute-done | bytes 524320 | tf_op jit(solution)/shard_map/scatter_second_2/ppermute | solution.py:171
  149.2 7.7 %collective-permute-done.44 = bf16[2,2,64,1024]{3,2,1,0:T(8,128)(2,1)S(1)} collective-permute-done((bf16[2,2,64,1024]{3,2,1,0:T(8,128)(2,1)S(1)}, bf16[2,2,64,1024]{3,2,1,0:T(8,128)(2,1)S(1)}, u32[]{:S(2)}, u32[]{:S(2)}) %collective-permute-start.44) | collective-permute-done | bytes 524320 | tf_op jit(solution)/shard_map/scatter_second_3/ppermute | solution.py:171
  158.5 2.9 %collective-permute-start.38 = (bf16[128,1024]{1,0:T(8,128)(2,1)}, bf16[128,1024]{1,0:T(8,128)(2,1)S(1)}, u32[]{:S(2)}, u32[]{:S(2)}) collective-permute-start(bf16[128,1024]{1,0:T(8,128)(2,1)} %pad_maximum_fusion.11), channel_id=1, source_target_pairs={{0,8},{1,9},{2,10},{3,11},{4,12},{5,13},{6,14},{7,15},{8,0},{9,1},... | collective-permute-start | bytes 786440 | tf_op jit(solution)/shard_map/to_plane_2/ppermute | solution.py:41
  161.4 2.2 %collective-permute-done.45 = bf16[2,64,1024]{2,1,0:T(8,128)(2,1)S(1)} collective-permute-done((bf16[2,64,1024]{2,1,0:T(8,128)(2,1)S(1)}, bf16[2,64,1024]{2,1,0:T(8,128)(2,1)S(1)}, u32[]{:S(2)}, u32[]{:S(2)}) %collective-permute-start.45) | collective-permute-done | bytes 262176 | tf_op jit(solution)/shard_map/scatter_first_3/ppermute | solution.py:171
  164.4 3.8 %collective-permute-start.46 = (bf16[128,1024]{1,0:T(8,128)(2,1)}, bf16[128,1024]{1,0:T(8,128)(2,1)S(1)}, u32[]{:S(2)}, u32[]{:S(2)}) collective-permute-start(bf16[128,1024]{1,0:T(8,128)(2,1)} %pad_maximum_fusion.13), channel_id=1, source_target_pairs={{0,12},{1,13},{2,14},{3,15},{4,0},{5,1},{6,2},{7,3},{8,4},{9,5},{1... | collective-permute-start | bytes 786440 | tf_op jit(solution)/shard_map/to_plane_3/ppermute | solution.py:41
  169.6 4.1 %collective-permute-done.38 = bf16[128,1024]{1,0:T(8,128)(2,1)S(1)} collective-permute-done((bf16[128,1024]{1,0:T(8,128)(2,1)}, bf16[128,1024]{1,0:T(8,128)(2,1)S(1)}, u32[]{:S(2)}, u32[]{:S(2)}) %collective-permute-start.38) | collective-permute-done | bytes 262176 | tf_op jit(solution)/shard_map/to_plane_2/ppermute | solution.py:41
  (168 shorter events, 48.2 us)
Async XLA Ops:
  4.5 11.6 %collective-permute-start = (bf16[128,1024]{1,0:T(8,128)(2,1)S(1)}, bf16[128,1024]{1,0:T(8,128)(2,1)S(1)}, u32[]{:S(2)}, u32[]{:S(2)}) collective-permute-start(bf16[128,1024]{1,0:T(8,128)(2,1)S(1)} %get-tuple-element.41.rest_0_), channel_id=1, source_target_pairs={{0,4},{1,5},{2,6},{3,7},{4,8},{5,9},{6,10},{7,11},{8,12},{9,13},{1... | collective-permute-start | bytes 786440 | tf_op jit(solution)/shard_map/ppermute | solution.py:27
  9.4 12.7 %collective-permute-start.4 = (bf16[128,1024]{1,0:T(8,128)(2,1)}, bf16[128,1024]{1,0:T(8,128)(2,1)S(1)}, u32[]{:S(2)}, u32[]{:S(2)}) collective-permute-start(bf16[128,1024]{1,0:T(8,128)(2,1)} %rest_0_), channel_id=1, source_target_pairs={{0,4},{1,5},{2,6},{3,7},{4,8},{5,9},{6,10},{7,11},{8,12},{9,13},{1... | collective-permute-start | bytes 786440 | tf_op jit(solution)/shard_map/ppermute | solution.py:27
  16.9 9.3 %collective-permute-start.1 = (bf16[128,1024]{1,0:T(8,128)(2,1)S(1)}, bf16[128,1024]{1,0:T(8,128)(2,1)S(1)}, u32[]{:S(2)}, u32[]{:S(2)}) collective-permute-start(bf16[128,1024]{1,0:T(8,128)(2,1)S(1)} %get-tuple-element.97), channel_id=1, source_target_pairs={{0,1},{1,0},{2,3},{3,2},{4,5},{5,4},{6,7},{7,6},{8,9},{9,8},{10,11... | collective-permute-start | bytes 786440 | tf_op jit(solution)/shard_map/ppermute | solution.py:22
  20.2 15.0 %collective-permute-start.2 = (bf16[128,1024]{1,0:T(8,128)(2,1)}, bf16[128,1024]{1,0:T(8,128)(2,1)S(1)}, u32[]{:S(2)}, u32[]{:S(2)}) collective-permute-start(bf16[128,1024]{1,0:T(8,128)(2,1)} %get-tuple-element.96), channel_id=1, source_target_pairs={{0,2},{1,3},{2,0},{3,1},{4,6},{5,7},{6,4},{7,5},{8,10},{9,11},{10,... | collective-permute-start | bytes 786440 | tf_op jit(solution)/shard_map/ppermute | solution.py:22
  21.7 13.5 %collective-permute-start.3 = (bf16[128,1024]{1,0:T(8,128)(2,1)S(1)}, bf16[128,1024]{1,0:T(8,128)(2,1)S(1)}, u32[]{:S(2)}, u32[]{:S(2)}) collective-permute-start(bf16[128,1024]{1,0:T(8,128)(2,1)S(1)} %get-tuple-element.95), channel_id=1, source_target_pairs={{0,3},{1,2},{2,1},{3,0},{4,7},{5,6},{6,5},{7,4},{8,11},{9,10},{10,... | collective-permute-start | bytes 786440 | tf_op jit(solution)/shard_map/ppermute | solution.py:22
  23.1 14.0 %collective-permute-start.5 = (bf16[128,1024]{1,0:T(8,128)(2,1)}, bf16[128,1024]{1,0:T(8,128)(2,1)S(1)}, u32[]{:S(2)}, u32[]{:S(2)}) collective-permute-start(bf16[128,1024]{1,0:T(8,128)(2,1)} %get-tuple-element.94), channel_id=1, source_target_pairs={{0,1},{1,0},{2,3},{3,2},{4,5},{5,4},{6,7},{7,6},{8,9},{9,8},{10,11... | collective-permute-start | bytes 786440 | tf_op jit(solution)/shard_map/ppermute | solution.py:22
  24.6 18.4 %collective-permute-start.6 = (bf16[128,1024]{1,0:T(8,128)(2,1)}, bf16[128,1024]{1,0:T(8,128)(2,1)S(1)}, u32[]{:S(2)}, u32[]{:S(2)}) collective-permute-start(bf16[128,1024]{1,0:T(8,128)(2,1)} %get-tuple-element.93), channel_id=1, source_target_pairs={{0,2},{1,3},{2,0},{3,1},{4,6},{5,7},{6,4},{7,5},{8,10},{9,11},{10,... | collective-permute-start | bytes 786440 | tf_op jit(solution)/shard_map/ppermute | solution.py:22
  26.1 16.8 %collective-permute-start.7 = (bf16[128,1024]{1,0:T(8,128)(2,1)}, bf16[128,1024]{1,0:T(8,128)(2,1)S(1)}, u32[]{:S(2)}, u32[]{:S(2)}) collective-permute-start(bf16[128,1024]{1,0:T(8,128)(2,1)} %get-tuple-element.92), channel_id=1, source_target_pairs={{0,3},{1,2},{2,1},{3,0},{4,7},{5,6},{6,5},{7,4},{8,11},{9,10},{10,... | collective-permute-start | bytes 786440 | tf_op jit(solution)/shard_map/ppermute | solution.py:22
  51.0 11.4 %collective-permute-start.10 = (bf16[64,2176]{1,0:T(8,128)(2,1)S(1)}, bf16[64,2176]{1,0:T(8,128)(2,1)S(1)}, u32[]{:S(2)}, u32[]{:S(2)}) collective-permute-start(bf16[64,2176]{1,0:T(8,128)(2,1)S(1)} %get-tuple-element.53), channel_id=1, source_target_pairs={{4,0},{5,1},{6,2},{7,3},{8,4},{9,5},{10,6},{11,7},{12,8},{13,9},{1... | collective-permute-start | bytes 835592 | tf_op jit(solution)/shard_map/from_plane_1/ppermute | solution.py:33
  57.1 20.9 %collective-permute-start.12 = (bf16[128,2176]{1,0:T(8,128)(2,1)S(1)}, bf16[128,2176]{1,0:T(8,128)(2,1)S(1)}, u32[]{:S(2)}, u32[]{:S(2)}) collective-permute-start(bf16[128,2176]{1,0:T(8,128)(2,1)S(1)} %pad_maximum_fusion.near_ref), channel_id=1, source_target_pairs={{0,2},{1,3},{2,0},{3,1},{4,6},{5,7},{6,4},{7,5},{8,10},{9,11},{10,... | collective-permute-start | bytes 1671176 | tf_op jit(solution)/shard_map/gather_second_0/ppermute | solution.py:171
  58.7 22.6 %collective-permute-start.13 = (bf16[128,2176]{1,0:T(8,128)(2,1)S(1)}, bf16[128,2176]{1,0:T(8,128)(2,1)S(1)}, u32[]{:S(2)}, u32[]{:S(2)}) collective-permute-start(bf16[128,2176]{1,0:T(8,128)(2,1)S(1)} %pad_maximum_fusion.near_ref), channel_id=1, source_target_pairs={{16,0},{0,16},{17,1},{1,17},{18,2},{2,18},{19,3},{3,19},{20,4},{4,... | collective-permute-start | bytes 1671176 | tf_op jit(solution)/shard_map/ppermute | solution.py:48
  63.0 14.9 %collective-permute-start.19 = (bf16[64,2176]{1,0:T(8,128)(2,1)S(1)}, bf16[64,2176]{1,0:T(8,128)(2,1)S(1)}, u32[]{:S(2)}, u32[]{:S(2)}) collective-permute-start(bf16[64,2176]{1,0:T(8,128)(2,1)S(1)} %get-tuple-element.53), channel_id=1, source_target_pairs={{8,0},{9,1},{10,2},{11,3},{12,4},{13,5},{14,6},{15,7},{0,8},{1,9},... | collective-permute-start | bytes 835592 | tf_op jit(solution)/shard_map/from_plane_2/ppermute | solution.py:33
  69.0 12.3 %collective-permute-start.21 = (bf16[128,2176]{1,0:T(8,128)(2,1)S(1)}, bf16[128,2176]{1,0:T(8,128)(2,1)S(1)}, u32[]{:S(2)}, u32[]{:S(2)}) collective-permute-start(bf16[128,2176]{1,0:T(8,128)(2,1)S(1)} %constant_dynamic-update-slice_fusion.near_ref), channel_id=1, source_target_pairs={{0,2},{1,3},{2,0},{3,1},{4,6},{5,7},{6,4},{7,5},{8,10},{9,11},{10,... | collective-permute-start | bytes 1671176 | tf_op jit(solution)/shard_map/gather_second_1/ppermute | solution.py:171
  69.6 31.8 %collective-permute-start.22 = (bf16[128,2176]{1,0:T(8,128)(2,1)S(1)}, bf16[128,2176]{1,0:T(8,128)(2,1)S(1)}, u32[]{:S(2)}, u32[]{:S(2)}) collective-permute-start(bf16[128,2176]{1,0:T(8,128)(2,1)S(1)} %constant_dynamic-update-slice_fusion.near_ref), channel_id=1, source_target_pairs={{16,0},{0,16},{17,1},{1,17},{18,2},{2,18},{19,3},{3,19},{20,4},{4,... | collective-permute-start | bytes 1671176 | tf_op jit(solution)/shard_map/ppermute | solution.py:48
  77.9 15.0 %collective-permute-start.29 = (bf16[64,2176]{1,0:T(8,128)(2,1)S(1)}, bf16[64,2176]{1,0:T(8,128)(2,1)S(1)}, u32[]{:S(2)}, u32[]{:S(2)}) collective-permute-start(bf16[64,2176]{1,0:T(8,128)(2,1)S(1)} %get-tuple-element.53), channel_id=1, source_target_pairs={{12,0},{13,1},{14,2},{15,3},{0,4},{1,5},{2,6},{3,7},{4,8},{5,9},{6... | collective-permute-start | bytes 835592 | tf_op jit(solution)/shard_map/from_plane_3/ppermute | solution.py:33
  78.0 9.9 %collective-permute-start.14 = (bf16[128,2176]{1,0:T(8,128)(2,1)S(1)}, bf16[128,2176]{1,0:T(8,128)(2,1)S(1)}, u32[]{:S(2)}, u32[]{:S(2)}) collective-permute-start(bf16[128,2176]{1,0:T(8,128)(2,1)S(1)} %collective-permute-done.12.far_ref), channel_id=1, source_target_pairs={{16,0},{0,16},{17,1},{1,17},{18,2},{2,18},{19,3},{3,19},{20,4},{4,... | collective-permute-start | bytes 1671176 | tf_op jit(solution)/shard_map/ppermute | solution.py:48
  81.3 11.7 %collective-permute-start.16 = (bf16[4,64,1024]{2,1,0:T(8,128)(2,1)S(1)}, bf16[4,64,1024]{2,1,0:T(8,128)(2,1)S(1)}, u32[]{:S(2)}, u32[]{:S(2)}) collective-permute-start(bf16[4,64,1024]{2,1,0:T(8,128)(2,1)S(1)} %get-tuple-element.49), channel_id=1, source_target_pairs={{16,0},{0,16},{17,1},{1,17},{18,2},{2,18},{19,3},{3,19},{20,4},{4,... | collective-permute-start | bytes 1572872 | tf_op jit(solution)/shard_map/ppermute | solution.py:48
  87.8 15.4 %collective-permute-start.23 = (bf16[128,2176]{1,0:T(8,128)(2,1)S(1)}, bf16[128,2176]{1,0:T(8,128)(2,1)S(1)}, u32[]{:S(2)}, u32[]{:S(2)}) collective-permute-start(bf16[128,2176]{1,0:T(8,128)(2,1)S(1)} %collective-permute-done.21.far_ref), channel_id=1, source_target_pairs={{16,0},{0,16},{17,1},{1,17},{18,2},{2,18},{19,3},{3,19},{20,4},{4,... | collective-permute-start | bytes 1671176 | tf_op jit(solution)/shard_map/ppermute | solution.py:48
  87.9 12.6 %collective-permute-start.31 = (bf16[128,2176]{1,0:T(8,128)(2,1)S(1)}, bf16[128,2176]{1,0:T(8,128)(2,1)S(1)}, u32[]{:S(2)}, u32[]{:S(2)}) collective-permute-start(bf16[128,2176]{1,0:T(8,128)(2,1)S(1)} %constant_dynamic-update-slice_fusion.2.near_ref), channel_id=1, source_target_pairs={{0,2},{1,3},{2,0},{3,1},{4,6},{5,7},{6,4},{7,5},{8,10},{9,11},{10,... | collective-permute-start | bytes 1671176 | tf_op jit(solution)/shard_map/gather_second_2/ppermute | solution.py:171
  100.5 21.9 %collective-permute-start.32 = (bf16[128,2176]{1,0:T(8,128)(2,1)S(1)}, bf16[128,2176]{1,0:T(8,128)(2,1)S(1)}, u32[]{:S(2)}, u32[]{:S(2)}) collective-permute-start(bf16[128,2176]{1,0:T(8,128)(2,1)S(1)} %constant_dynamic-update-slice_fusion.2.near_ref), channel_id=1, source_target_pairs={{16,0},{0,16},{17,1},{1,17},{18,2},{2,18},{19,3},{3,19},{20,4},{4,... | collective-permute-start | bytes 1671176 | tf_op jit(solution)/shard_map/ppermute | solution.py:48
  101.0 32.1 %collective-permute-start.40 = (bf16[128,2176]{1,0:T(8,128)(2,1)S(1)}, bf16[128,2176]{1,0:T(8,128)(2,1)S(1)}, u32[]{:S(2)}, u32[]{:S(2)}) collective-permute-start(bf16[128,2176]{1,0:T(8,128)(2,1)S(1)} %constant_dynamic-update-slice_fusion.4.near_ref), channel_id=1, source_target_pairs={{16,0},{0,16},{17,1},{1,17},{18,2},{2,18},{19,3},{3,19},{20,4},{4,... | collective-permute-start | bytes 1671176 | tf_op jit(solution)/shard_map/ppermute | solution.py:48
  101.4 21.1 %collective-permute-start.39 = (bf16[128,2176]{1,0:T(8,128)(2,1)S(1)}, bf16[128,2176]{1,0:T(8,128)(2,1)S(1)}, u32[]{:S(2)}, u32[]{:S(2)}) collective-permute-start(bf16[128,2176]{1,0:T(8,128)(2,1)S(1)} %constant_dynamic-update-slice_fusion.4.near_ref), channel_id=1, source_target_pairs={{0,2},{1,3},{2,0},{3,1},{4,6},{5,7},{6,4},{7,5},{8,10},{9,11},{10,... | collective-permute-start | bytes 1671176 | tf_op jit(solution)/shard_map/gather_second_3/ppermute | solution.py:171
  103.2 13.4 %collective-permute-start.17 = (bf16[2,2,64,1024]{3,2,1,0:T(8,128)(2,1)S(1)}, bf16[2,2,64,1024]{3,2,1,0:T(8,128)(2,1)S(1)}, u32[]{:S(2)}, u32[]{:S(2)}) collective-permute-start(bf16[2,2,64,1024]{3,2,1,0:T(8,128)(2,1)S(1)} %pad_maximum_fusion.2), channel_id=1, source_target_pairs={{0,2},{1,3},{2,0},{3,1},{4,6},{5,7},{6,4},{7,5},{8,10},{9,11},{10,... | collective-permute-start | bytes 1572872 | tf_op jit(solution)/shard_map/scatter_second_0/ppermute | solution.py:171
  106.7 10.0 %collective-permute-start.24 = (bf16[4,64,1024]{2,1,0:T(8,128)(2,1)S(1)}, bf16[4,64,1024]{2,1,0:T(8,128)(2,1)S(1)}, u32[]{:S(2)}, u32[]{:S(2)}) collective-permute-start(bf16[4,64,1024]{2,1,0:T(8,128)(2,1)S(1)} %get-tuple-element.60), channel_id=1, source_target_pairs={{16,0},{0,16},{17,1},{1,17},{18,2},{2,18},{19,3},{3,19},{20,4},{4,... | collective-permute-start | bytes 1572872 | tf_op jit(solution)/shard_map/ppermute | solution.py:48
  117.1 9.2 %collective-permute-start.26 = (bf16[2,2,64,1024]{3,2,1,0:T(8,128)(2,1)S(1)}, bf16[2,2,64,1024]{3,2,1,0:T(8,128)(2,1)S(1)}, u32[]{:S(2)}, u32[]{:S(2)}) collective-permute-start(bf16[2,2,64,1024]{3,2,1,0:T(8,128)(2,1)S(1)} %pad_maximum_fusion.4), channel_id=1, source_target_pairs={{0,2},{1,3},{2,0},{3,1},{4,6},{5,7},{6,4},{7,5},{8,10},{9,11},{10,... | collective-permute-start | bytes 1572872 | tf_op jit(solution)/shard_map/scatter_second_1/ppermute | solution.py:171
  136.4 12.1 %collective-permute-start.36 = (bf16[2,2,64,1024]{3,2,1,0:T(8,128)(2,1)S(1)}, bf16[2,2,64,1024]{3,2,1,0:T(8,128)(2,1)S(1)}, u32[]{:S(2)}, u32[]{:S(2)}) collective-permute-start(bf16[2,2,64,1024]{3,2,1,0:T(8,128)(2,1)S(1)} %pad_maximum_fusion.5), channel_id=1, source_target_pairs={{0,2},{1,3},{2,0},{3,1},{4,6},{5,7},{6,4},{7,5},{8,10},{9,11},{10,... | collective-permute-start | bytes 1572872 | tf_op jit(solution)/shard_map/scatter_second_2/ppermute | solution.py:171
  138.8 18.2 %collective-permute-start.44 = (bf16[2,2,64,1024]{3,2,1,0:T(8,128)(2,1)S(1)}, bf16[2,2,64,1024]{3,2,1,0:T(8,128)(2,1)S(1)}, u32[]{:S(2)}, u32[]{:S(2)}) collective-permute-start(bf16[2,2,64,1024]{3,2,1,0:T(8,128)(2,1)S(1)} %pad_maximum_fusion.6), channel_id=1, source_target_pairs={{0,2},{1,3},{2,0},{3,1},{4,6},{5,7},{6,4},{7,5},{8,10},{9,11},{10,... | collective-permute-start | bytes 1572872 | tf_op jit(solution)/shard_map/scatter_second_3/ppermute | solution.py:171
  140.4 29.1 %collective-permute-start.18 = (bf16[2,64,1024]{2,1,0:T(8,128)(2,1)S(1)}, bf16[2,64,1024]{2,1,0:T(8,128)(2,1)S(1)}, u32[]{:S(2)}, u32[]{:S(2)}) collective-permute-start(bf16[2,64,1024]{2,1,0:T(8,128)(2,1)S(1)} %pad_maximum_fusion.7), channel_id=1, source_target_pairs={{0,1},{1,0},{2,3},{3,2},{4,5},{5,4},{6,7},{7,6},{8,9},{9,8},{10,11... | collective-permute-start | bytes 786440 | tf_op jit(solution)/shard_map/scatter_first_0/ppermute | solution.py:171
  140.9 28.8 %collective-permute-start.28 = (bf16[128,1024]{1,0:T(8,128)(2,1)S(1)}, bf16[128,1024]{1,0:T(8,128)(2,1)S(1)}, u32[]{:S(2)}, u32[]{:S(2)}) collective-permute-start(bf16[128,1024]{1,0:T(8,128)(2,1)S(1)} %pad_maximum_fusion.9), channel_id=1, source_target_pairs={{0,4},{1,5},{2,6},{3,7},{4,8},{5,9},{6,10},{7,11},{8,12},{9,13},{1... | collective-permute-start | bytes 786440 | tf_op jit(solution)/shard_map/to_plane_1/ppermute | solution.py:41
  148.7 9.0 %collective-permute-start.37 = (bf16[2,64,1024]{2,1,0:T(8,128)(2,1)S(1)}, bf16[2,64,1024]{2,1,0:T(8,128)(2,1)S(1)}, u32[]{:S(2)}, u32[]{:S(2)}) collective-permute-start(bf16[2,64,1024]{2,1,0:T(8,128)(2,1)S(1)} %pad_maximum_fusion.10), channel_id=1, source_target_pairs={{0,1},{1,0},{2,3},{3,2},{4,5},{5,4},{6,7},{7,6},{8,9},{9,8},{10,11... | collective-permute-start | bytes 786440 | tf_op jit(solution)/shard_map/scatter_first_2/ppermute | solution.py:171
  158.5 15.3 %collective-permute-start.38 = (bf16[128,1024]{1,0:T(8,128)(2,1)}, bf16[128,1024]{1,0:T(8,128)(2,1)S(1)}, u32[]{:S(2)}, u32[]{:S(2)}) collective-permute-start(bf16[128,1024]{1,0:T(8,128)(2,1)} %pad_maximum_fusion.11), channel_id=1, source_target_pairs={{0,8},{1,9},{2,10},{3,11},{4,12},{5,13},{6,14},{7,15},{8,0},{9,1},... | collective-permute-start | bytes 786440 | tf_op jit(solution)/shard_map/to_plane_2/ppermute | solution.py:41
  164.4 10.4 %collective-permute-start.46 = (bf16[128,1024]{1,0:T(8,128)(2,1)}, bf16[128,1024]{1,0:T(8,128)(2,1)S(1)}, u32[]{:S(2)}, u32[]{:S(2)}) collective-permute-start(bf16[128,1024]{1,0:T(8,128)(2,1)} %pad_maximum_fusion.13), channel_id=1, source_target_pairs={{0,12},{1,13},{2,14},{3,15},{4,0},{5,1},{6,2},{7,3},{8,4},{9,5},{1... | collective-permute-start | bytes 786440 | tf_op jit(solution)/shard_map/to_plane_3/ppermute | solution.py:41
  (28 other events, 309.3 us)

commit v10 on v9

--- a/solution.py
+++ b/solution.py
@@ -195,7 +195,7 @@
             outs[part][order[block]] = product[block * part_rows : (block + 1) * part_rows]
 
 
-def run_expert(place, near, far, w_gate, w_up, w_down, experts, parts, ahead):
+def run_expert(place, near, far, w_gate, w_up, w_down, experts, parts, ahead, light):
     count = 2 * near.shape[0]
     units, width = w_gate.shape
     out_shape = jax.ShapeDtypeStruct((PLANE, count // PLANE, width // parts), jnp.bfloat16)
@@ -204,7 +204,7 @@
         [out_shape] * parts,
         [place],
         [near, far, w_gate, w_up, w_down],
-        flops=6 * count * width * units,
+        flops=count if light else 6 * count * width * units,
         moved=count,
     )
 
@@ -229,13 +229,13 @@
     return [total[0:count] + wide(got[i]) for i, total in enumerate(totals)]
 
 
-def expert_outputs(place, near, far, weights, experts, cores, waits):
+def expert_outputs(place, near, far, weights, experts, cores, waits, light):
     outs = []
     for ahead in range(cores):
         near_rows = from_core(near, ahead) if ahead else near
         far_rows = from_core(far, ahead) if ahead else far
         near_rows = after(near_rows, *outs[-1:], *waits.get(ahead, []))
-        outs.append(run_expert(place, near_rows, far_rows, *weights, experts, cores, ahead))
+        outs.append(run_expert(place, near_rows, far_rows, *weights, experts, cores, ahead, light))
     return outs
 
 
@@ -335,15 +335,15 @@
     every, seconds, firsts, ready, returned = [], [], [], [], []
     for step in range(len(groups) + 1):
         if step < len(groups):
-            source = after(payload, nears[step - 2]) if step > 1 else payload
-            column = jnp.concatenate(
-                [from_plane(source, ahead) if ahead else source for ahead in groups[step]]
-            )
+            blocks = []
+            for ahead in groups[step]:
+                source = from_plane(source, 1) if ahead else payload
+                blocks.append(source)
+            column = jnp.concatenate(blocks)
             waits = [*nears[-1:]]
             if step > 1:
                 waits.append(fars[step - 2])
-            if step > 2:
-                waits.append(every[step - 3])
+                waits.append(every[step - 2][0])
             columns.append(after(column, *waits))
             got = crossed(columns[-1], True, f"gather_first_{step}")
             nears.append(jnp.concatenate([columns[-1], got]))
@@ -354,28 +354,32 @@
         waits = {0: [*every[-1:], *nears[step : step + 1]], cores - 1: []}
         if number > 0:
             waits[cores - 1].append(seconds[-1])
-        if number > 1:
+        if number > 2:
             waits[0].append(firsts[-2])
             waits[cores - 1].append(ready[-2])
         far = after(fars[number], *[outs[0] for outs in every[-1:]])
-        outs = expert_outputs(place, nears[number], far, weights, experts, cores, waits)
+        light = number == len(groups) - 1
+        outs = expert_outputs(place, nears[number], far, weights, experts, cores, waits, light)
         every.append(outs)
         totals = core_totals(outs, cores)
-        seconds.append(second_share(totals))
+        seconds.append(after(second_share(totals), *firsts[-1:]))
+        if number == 0:
+            own_totals = totals
+            continue
         totals = merged(totals, crossed(seconds[-1], False, f"scatter_second_{number}"), 2)
         firsts.append(first_share(totals))
         came = crossed(firsts[-1], True, f"scatter_first_{number}")
         rows_of = merged([total[0] for total in totals], came, None)
-        if group == [0]:
-            moe = jnp.concatenate(rows_of)
-            ready.append(moe)
-            continue
         blocks = []
         for i in range(len(group)):
             piece = [rows[i * part_rows : (i + 1) * part_rows] for rows in rows_of]
             blocks.append(narrow(jnp.concatenate(piece)))
         ready.append(blocks)
         returned += [to_plane(block, ahead) for block, ahead in zip(blocks, group, strict=True)]
+    got = crossed(after(seconds[0], firsts[-1]), False, "scatter_second_0")
+    totals = merged(own_totals, got, 2)
+    got = crossed(first_share(totals), True, "scatter_first_0")
+    moe = jnp.concatenate(merged([total[0] for total in totals], got, None))
     moe = moe + sum(wide(block) for block in returned)
     moe = jnp.roll(moe.reshape(cores, part_rows, col_width), tok_index, axis=0)
     moe = moe.reshape(tok_rows, col_width)

time: 178 us -> 176 us (0.989); the launches traced: 176 us -> 176 us
  starting transfers between devices: 49.1 us -> 51.3 us
  waiting for transfers between devices: 74 us -> 72 us
    ppermute x3, starting transfers between devices: 6.04 us -> 13.1 us  [from_plane(): lax.ppermute(block, 'blk', [((i + PLANE * ahead) % count, i) for i in ran...]
    ppermute x3, starting transfers between devices: 6.83 us -> 0.64 us  [to_plane(): lax.ppermute(block, 'blk', [(i, (i + PLANE * ahead) % count) for i in ran...]
    ppermute x3, waiting for transfers between devices: 11.8 us -> 5.77 us  [from_plane(): lax.ppermute(block, 'blk', [((i + PLANE * ahead) % count, i) for i in ran...]
    ppermute x16, waiting for transfers between devices: 42.6 us -> 44.5 us  [crossed(): return lax.ppermute(block, ('tok', 'blk'), route)]
  transfers between devices with their start and end apart: 47 -> 47, of which waited for: 18 -> 20; matrix products, arithmetic and copies ran while one was open for 8% -> 8% of each run, Pallas kernels for 16% -> 16%
where the time goes in v10:
time: 176 us
  waiting for transfers between devices  72 us (41%)
  starting transfers between devices  51.3 us (29%)
  Pallas kernels  31.4 us (18%)
  local copies, waits for them, and re-layouts  10.4 us (6%)
  other arithmetic  9.49 us (5%)
    ppermute x16, waiting for transfers between devices, crossed(): return lax.ppermute(block, ('tok', 'blk'), route)  44.5 us
    pallas_call x12, Pallas kernels, local_call(): pl.pallas_call(body, in_specs=[scalar] * len(scalars) + [whole] * len(arr...  31.4 us
    ppermute x16, starting transfers between devices, crossed(): return lax.ppermute(block, ('tok', 'blk'), route)  16.3 us
    ppermute x3, starting transfers between devices, from_plane(): lax.ppermute(block, 'blk', [((i + PLANE * ahead) % count, i) for i in ran...  13.1 us
    ppermute x6, waiting for transfers between devices, flipped(): lax.ppermute(block, 'blk', [(i, i ^ mask) for i in range(lax.axis_size('b...  8.92 us
    ppermute x6, starting transfers between devices, flipped(): lax.ppermute(block, 'blk', [(i, i ^ mask) for i in range(lax.axis_size('b...  8.75 us
    ppermute x2, starting transfers between devices, next_plane(): lax.ppermute(block, 'blk', [(i, i + PLANE) for i in range(count - PLANE)])  8.43 us
    ppermute x3, waiting for transfers between devices, to_plane(): lax.ppermute(block, 'blk', [(i, (i + PLANE * ahead) % count) for i in ran...  6.29 us
  transfers between devices with their start and end apart: 47, of which 20 were waited for; matrix products, arithmetic and copies ran while one was open for 8% of the time, Pallas kernels for 16%

profile of v10, /device:TPU:0, one launch (start us, length us, event | category | flops | bytes accessed | tf_op | source)
XLA Modules:
  0.0 176.0 jit_solution(916537619886670380)
XLA Ops:
  4.5 4.9 %collective-permute-start = (bf16[128,1024]{1,0:T(8,128)(2,1)S(1)}, bf16[128,1024]{1,0:T(8,128)(2,1)S(1)}, u32[]{:S(2)}, u32[]{:S(2)}) collective-permute-start(bf16[128,1024]{1,0:T(8,128)(2,1)S(1)} %get-tuple-element.42.rest_0_), channel_id=1, source_target_pairs={{0,4},{1,5},{2,6},{3,7},{4,8},{5,9},{6,10},{7,11},{8,12},{9,13},{1... | collective-permute-start | bytes 786440 | tf_op jit(solution)/shard_map/ppermute | solution.py:27
  9.4 3.5 %collective-permute-start.4 = (bf16[128,1024]{1,0:T(8,128)(2,1)}, bf16[128,1024]{1,0:T(8,128)(2,1)S(1)}, u32[]{:S(2)}, u32[]{:S(2)}) collective-permute-start(bf16[128,1024]{1,0:T(8,128)(2,1)} %rest_0_), channel_id=1, source_target_pairs={{0,4},{1,5},{2,6},{3,7},{4,8},{5,9},{6,10},{7,11},{8,12},{9,13},{1... | collective-permute-start | bytes 786440 | tf_op jit(solution)/shard_map/ppermute | solution.py:27
  13.7 2.4 %collective-permute-done.rest_1_ = bf16[128,1024]{1,0:T(8,128)(2,1)S(1)} collective-permute-done((bf16[128,1024]{1,0:T(8,128)(2,1)S(1)}, bf16[128,1024]{1,0:T(8,128)(2,1)S(1)}, u32[]{:S(2)}, u32[]{:S(2)}) %collective-permute-start) | collective-permute-done | bytes 262176 | tf_op jit(solution)/shard_map/ppermute | solution.py:27
  26.1 2.2 %collective-permute-start.7 = (bf16[128,1024]{1,0:T(8,128)(2,1)}, bf16[128,1024]{1,0:T(8,128)(2,1)S(1)}, u32[]{:S(2)}, u32[]{:S(2)}) collective-permute-start(bf16[128,1024]{1,0:T(8,128)(2,1)} %get-tuple-element.94), channel_id=1, source_target_pairs={{0,3},{1,2},{2,1},{3,0},{4,7},{5,6},{6,5},{7,4},{8,11},{9,10},{10,... | collective-permute-start | bytes 786440 | tf_op jit(solution)/shard_map/ppermute | solution.py:22
  29.4 2.7 %scatter_fusion = bf16[8,16,2,1024]{3,1,2,0:T(8,128)(2,1)} fusion(bf16[8,16,2,1024]{3,1,2,0:T(8,128)(2,1)} %broadcast_in_dim.31, s32[8]{0:T(128)S(1)} %compare_select_fusion, bf16[8,16,2,1024]{3,1,2,0:T(8,128)(2,1)} %pad_maximum_fusion.1), kind=kCustom, calls=%fused_computation | custom fusion | bytes 1572896 | tf_op jit(solution)/shard_map/scatter | solution.py:305
  32.1 3.1 %collective-permute-done.2.rest_3_ = bf16[128,1024]{1,0:T(8,128)(2,1)S(1)} collective-permute-done((bf16[128,1024]{1,0:T(8,128)(2,1)}, bf16[128,1024]{1,0:T(8,128)(2,1)S(1)}, u32[]{:S(2)}, u32[]{:S(2)}) %collective-permute-start.2) | collective-permute-done | bytes 262176 | tf_op jit(solution)/shard_map/ppermute | solution.py:22
  37.2 5.8 %collective-permute-done.6.rest_3_ = bf16[128,1024]{1,0:T(8,128)(2,1)S(1)} collective-permute-done((bf16[128,1024]{1,0:T(8,128)(2,1)}, bf16[128,1024]{1,0:T(8,128)(2,1)S(1)}, u32[]{:S(2)}, u32[]{:S(2)}) %collective-permute-start.6) | collective-permute-done | bytes 262176 | tf_op jit(solution)/shard_map/ppermute | solution.py:22
  43.0 2.2 %copy-done.3 = bf16[1024,2048]{1,0:T(8,128)(2,1)S(1)} copy-done((bf16[1024,2048]{1,0:T(8,128)(2,1)S(1)}, bf16[1024,2048]{1,0:T(8,128)(2,1)}, u32[]{:S(2)}) %copy-start.3) | copy-done | bytes 4194328
  47.0 2.6 %collective-permute-done.8.rest_1_ = f32[128,2048]{1,0:T(8,128)S(1)} collective-permute-done((f32[128,2048]{1,0:T(8,128)S(1)}, f32[128,2048]{1,0:T(8,128)S(1)}, u32[]{:S(2)}, u32[]{:S(2)}) %collective-permute-start.8) | collective-permute-done | bytes 1048608 | tf_op jit(solution)/shard_map/ppermute | solution.py:48
  51.0 4.5 %collective-permute-start.10 = (bf16[64,2176]{1,0:T(8,128)(2,1)S(1)}, bf16[64,2176]{1,0:T(8,128)(2,1)S(1)}, u32[]{:S(2)}, u32[]{:S(2)}) collective-permute-start(bf16[64,2176]{1,0:T(8,128)(2,1)S(1)} %get-tuple-element.46), channel_id=1, source_target_pairs={{4,0},{5,1},{6,2},{7,3},{8,4},{9,5},{10,6},{11,7},{12,8},{13,9},{1... | collective-permute-start | bytes 835592 | tf_op jit(solution)/shard_map/from_plane_1/ppermute | solution.py:33
  58.7 3.7 %collective-permute-done.10 = bf16[64,2176]{1,0:T(8,128)(2,1)S(1)} collective-permute-done((bf16[64,2176]{1,0:T(8,128)(2,1)S(1)}, bf16[64,2176]{1,0:T(8,128)(2,1)S(1)}, u32[]{:S(2)}, u32[]{:S(2)}) %collective-permute-start.10) | collective-permute-done | bytes 278560 | tf_op jit(solution)/shard_map/from_plane_1/ppermute | solution.py:33
  63.0 4.3 %collective-permute-start.17 = (bf16[64,2176]{1,0:T(8,128)(2,1)S(1)}, bf16[64,2176]{1,0:T(8,128)(2,1)S(1)}, u32[]{:S(2)}, u32[]{:S(2)}) collective-permute-start(bf16[64,2176]{1,0:T(8,128)(2,1)S(1)} %collective-permute-done.10), channel_id=1, source_target_pairs={{4,0},{5,1},{6,2},{7,3},{8,4},{9,5},{10,6},{11,7},{12,8},{13,9},{1... | collective-permute-start | bytes 835592 | tf_op jit(solution)/shard_map/from_plane_1/ppermute | solution.py:33
  70.8 2.1 %collective-permute-done.17 = bf16[64,2176]{1,0:T(8,128)(2,1)S(1)} collective-permute-done((bf16[64,2176]{1,0:T(8,128)(2,1)S(1)}, bf16[64,2176]{1,0:T(8,128)(2,1)S(1)}, u32[]{:S(2)}, u32[]{:S(2)}) %collective-permute-start.17) | collective-permute-done | bytes 278560 | tf_op jit(solution)/shard_map/from_plane_1/ppermute | solution.py:33
  72.9 4.3 %collective-permute-start.18 = (bf16[64,2176]{1,0:T(8,128)(2,1)S(1)}, bf16[64,2176]{1,0:T(8,128)(2,1)S(1)}, u32[]{:S(2)}, u32[]{:S(2)}) collective-permute-start(bf16[64,2176]{1,0:T(8,128)(2,1)S(1)} %collective-permute-done.17), channel_id=1, source_target_pairs={{4,0},{5,1},{6,2},{7,3},{8,4},{9,5},{10,6},{11,7},{12,8},{13,9},{1... | collective-permute-start | bytes 835592 | tf_op jit(solution)/shard_map/from_plane_1/ppermute | solution.py:33
  77.2 3.2 %shard_map.144 = (bf16[4,64,1024]{2,1,0:T(8,128)(2,1)S(1)}, bf16[4,64,1024]{2,1,0:T(8,128)(2,1)S(1)}) custom-call(s32[2]{0:T(128)S(1)} %pad_add_fusion.place_ref, bf16[128,2176]{1,0:T(8,128)(2,1)S(1)} %pad_maximum_fusion.near_ref, bf16[128,2176]{1,0:T(8,128)(2,1)S(1)} %collective-permute-done.12.far_ref, bf16[704,2048]{1,0:T(8,128)(2,1)S(1)} %bitcast.95, ...), custom_call_target="tpu_custom_call" | custom-call | flops 2214592512 | bytes 256 | tf_op jit(solution)/shard_map/pallas_call | solution.py:142
  80.5 2.0 %collective-permute-start.16 = (bf16[4,64,1024]{2,1,0:T(8,128)(2,1)S(1)}, bf16[4,64,1024]{2,1,0:T(8,128)(2,1)S(1)}, u32[]{:S(2)}, u32[]{:S(2)}) collective-permute-start(bf16[4,64,1024]{2,1,0:T(8,128)(2,1)S(1)} %get-tuple-element.50), channel_id=1, source_target_pairs={{16,0},{0,16},{17,1},{1,17},{18,2},{2,18},{19,3},{3,19},{20,4},{4,... | collective-permute-start | bytes 1572872 | tf_op jit(solution)/shard_map/ppermute | solution.py:48
  82.5 4.5 %collective-permute-done.19 = bf16[64,2176]{1,0:T(8,128)(2,1)S(1)} collective-permute-done((bf16[64,2176]{1,0:T(8,128)(2,1)S(1)}, bf16[64,2176]{1,0:T(8,128)(2,1)S(1)}, u32[]{:S(2)}, u32[]{:S(2)}) %collective-permute-start.19) | collective-permute-done | bytes 278560 | tf_op jit(solution)/shard_map/gather_first_2/ppermute | solution.py:171
  88.9 3.2 %shard_map.145 = (bf16[4,64,1024]{2,1,0:T(8,128)(2,1)S(1)}, bf16[4,64,1024]{2,1,0:T(8,128)(2,1)S(1)}) custom-call(s32[2]{0:T(128)S(1)} %pad_add_fusion.place_ref, bf16[128,2176]{1,0:T(8,128)(2,1)S(1)} %collective-permute-done.13.near_ref, bf16[128,2176]{1,0:T(8,128)(2,1)S(1)} %collective-permute-done.14.far_ref, bf16[704,2048]{1,0:T(8,128)(2,1)S(1)} %bitcast.96, ...), custom_call_target="tpu_custom_call" | custom-call | flops 2214592512 | bytes 256 | tf_op jit(solution)/shard_map/pallas_call | solution.py:142
  92.1 3.2 %shard_map.146 = (bf16[4,64,1024]{2,1,0:T(8,128)(2,1)S(1)}, bf16[4,64,1024]{2,1,0:T(8,128)(2,1)S(1)}) custom-call(s32[2]{0:T(128)S(1)} %pad_add_fusion.place_ref, bf16[128,2176]{1,0:T(8,128)(2,1)S(1)} %constant_dynamic-update-slice_fusion.near_ref, bf16[128,2176]{1,0:T(8,128)(2,1)S(1)} %collective-permute-done.20.far_ref, bf16[704,2048]{1,0:T(8,128)(2,1)S(1)} %bitcast.97, ...), custom_call_target="tpu_custom_call" | custom-call | flops 2214592512 | bytes 256 | tf_op jit(solution)/shard_map/pallas_call | solution.py:142
  96.7 5.4 %collective-permute-done.21 = bf16[64,2176]{1,0:T(8,128)(2,1)S(1)} collective-permute-done((bf16[64,2176]{1,0:T(8,128)(2,1)S(1)}, bf16[64,2176]{1,0:T(8,128)(2,1)S(1)}, u32[]{:S(2)}, u32[]{:S(2)}) %collective-permute-start.21) | collective-permute-done | bytes 278560 | tf_op jit(solution)/shard_map/gather_first_3/ppermute | solution.py:171
  103.5 3.2 %shard_map.147 = (bf16[4,64,1024]{2,1,0:T(8,128)(2,1)S(1)}, bf16[4,64,1024]{2,1,0:T(8,128)(2,1)S(1)}) custom-call(s32[2]{0:T(128)S(1)} %pad_add_fusion.place_ref, bf16[128,2176]{1,0:T(8,128)(2,1)S(1)} %collective-permute-done.22.near_ref, bf16[128,2176]{1,0:T(8,128)(2,1)S(1)} %collective-permute-done.23.far_ref, bf16[704,2048]{1,0:T(8,128)(2,1)S(1)} %bitcast.98, ...), custom_call_target="tpu_custom_call" | custom-call | flops 2214592512 | bytes 256 | tf_op jit(solution)/shard_map/pallas_call | solution.py:142
  106.8 3.4 %shard_map.148 = (bf16[4,64,1024]{2,1,0:T(8,128)(2,1)S(1)}, bf16[4,64,1024]{2,1,0:T(8,128)(2,1)S(1)}) custom-call(s32[2]{0:T(128)S(1)} %pad_add_fusion.place_ref, bf16[128,2176]{1,0:T(8,128)(2,1)S(1)} %constant_dynamic-update-slice_fusion.2.near_ref, bf16[128,2176]{1,0:T(8,128)(2,1)S(1)} %collective-permute-done.24.far_ref, bf16[704,2048]{1,0:T(8,128)(2,1)S(1)} %bitcast.99, ...), custom_call_target="tpu_custom_call" | custom-call | flops 2214592512 | bytes 256 | tf_op jit(solution)/shard_map/pallas_call | solution.py:142
  113.9 3.2 %shard_map.149 = (bf16[4,64,1024]{2,1,0:T(8,128)(2,1)S(1)}, bf16[4,64,1024]{2,1,0:T(8,128)(2,1)S(1)}) custom-call(s32[2]{0:T(128)S(1)} %pad_add_fusion.place_ref, bf16[128,2176]{1,0:T(8,128)(2,1)S(1)} %collective-permute-done.25.near_ref, bf16[128,2176]{1,0:T(8,128)(2,1)S(1)} %collective-permute-done.28.far_ref, bf16[704,2048]{1,0:T(8,128)(2,1)S(1)} %bitcast.100, ...), custom_call_target="tpu_custom_call" | custom-call | flops 2214592512 | bytes 256 | tf_op jit(solution)/shard_map/pallas_call | solution.py:142
  117.5 5.1 %collective-permute-done.29 = bf16[2,2,64,1024]{3,2,1,0:T(8,128)(2,1)S(1)} collective-permute-done((bf16[2,2,64,1024]{3,2,1,0:T(8,128)(2,1)S(1)}, bf16[2,2,64,1024]{3,2,1,0:T(8,128)(2,1)S(1)}, u32[]{:S(2)}, u32[]{:S(2)}) %collective-permute-start.29) | collective-permute-done | bytes 524320 | tf_op jit(solution)/shard_map/scatter_second_1/ppermute | solution.py:171
  125.5 3.2 %shard_map.150 = (bf16[4,64,1024]{2,1,0:T(8,128)(2,1)S(1)}, bf16[4,64,1024]{2,1,0:T(8,128)(2,1)S(1)}) custom-call(s32[2]{0:T(128)S(1)} %pad_add_fusion.place_ref, bf16[128,2176]{1,0:T(8,128)(2,1)S(1)} %constant_dynamic-update-slice_fusion.4.near_ref, bf16[128,2176]{1,0:T(8,128)(2,1)S(1)} %collective-permute-done.30.far_ref, bf16[704,2048]{1,0:T(8,128)(2,1)S(1)} %bitcast.101, ...), custom_call_target="tpu_custom_call" | custom-call | flops 256 | bytes 256 | tf_op jit(solution)/shard_map/pallas_call | solution.py:142
  128.8 3.6 %collective-permute-done.34 = bf16[2,64,1024]{2,1,0:T(8,128)(2,1)S(1)} collective-permute-done((bf16[2,64,1024]{2,1,0:T(8,128)(2,1)S(1)}, bf16[2,64,1024]{2,1,0:T(8,128)(2,1)S(1)}, u32[]{:S(2)}, u32[]{:S(2)}) %collective-permute-start.34) | collective-permute-done | bytes 262176 | tf_op jit(solution)/shard_map/scatter_first_1/ppermute | solution.py:171
  132.5 3.2 %shard_map.151 = (bf16[4,64,1024]{2,1,0:T(8,128)(2,1)S(1)}, bf16[4,64,1024]{2,1,0:T(8,128)(2,1)S(1)}) custom-call(s32[2]{0:T(128)S(1)} %pad_add_fusion.place_ref, bf16[128,2176]{1,0:T(8,128)(2,1)S(1)} %collective-permute-done.31.near_ref, bf16[128,2176]{1,0:T(8,128)(2,1)S(1)} %collective-permute-done.35.far_ref, bf16[704,2048]{1,0:T(8,128)(2,1)S(1)} %bitcast.102, ...), custom_call_target="tpu_custom_call" | custom-call | flops 256 | bytes 256 | tf_op jit(solution)/shard_map/pallas_call | solution.py:142
  140.3 9.1 %collective-permute-done.39 = bf16[2,2,64,1024]{3,2,1,0:T(8,128)(2,1)S(1)} collective-permute-done((bf16[2,2,64,1024]{3,2,1,0:T(8,128)(2,1)S(1)}, bf16[2,2,64,1024]{3,2,1,0:T(8,128)(2,1)S(1)}, u32[]{:S(2)}, u32[]{:S(2)}) %collective-permute-start.39) | collective-permute-done | bytes 524320 | tf_op jit(solution)/shard_map/scatter_second_3/ppermute | solution.py:171
  152.6 8.5 %collective-permute-done.40 = bf16[2,2,64,1024]{3,2,1,0:T(8,128)(2,1)S(1)} collective-permute-done((bf16[2,2,64,1024]{3,2,1,0:T(8,128)(2,1)S(1)}, bf16[2,2,64,1024]{3,2,1,0:T(8,128)(2,1)S(1)}, u32[]{:S(2)}, u32[]{:S(2)}) %collective-permute-start.40) | collective-permute-done | bytes 524320 | tf_op jit(solution)/shard_map/scatter_second_0/ppermute | solution.py:171
  165.7 2.9 %collective-permute-done.41 = bf16[2,64,1024]{2,1,0:T(8,128)(2,1)S(1)} collective-permute-done((bf16[2,64,1024]{2,1,0:T(8,128)(2,1)}, bf16[2,64,1024]{2,1,0:T(8,128)(2,1)S(1)}, u32[]{:S(2)}, u32[]{:S(2)}) %collective-permute-start.41) | collective-permute-done | bytes 262176 | tf_op jit(solution)/shard_map/scatter_first_0/ppermute | solution.py:171
  168.7 2.5 %collective-permute-done.44 = bf16[128,1024]{1,0:T(8,128)(2,1)S(1)} collective-permute-done((bf16[128,1024]{1,0:T(8,128)(2,1)S(1)}, bf16[128,1024]{1,0:T(8,128)(2,1)S(1)}, u32[]{:S(2)}, u32[]{:S(2)}) %collective-permute-start.44) | collective-permute-done | bytes 262176 | tf_op jit(solution)/shard_map/to_plane_2/ppermute | solution.py:41
  171.2 3.7 %collective-permute-done.46 = bf16[128,1024]{1,0:T(8,128)(2,1)S(1)} collective-permute-done((bf16[128,1024]{1,0:T(8,128)(2,1)}, bf16[128,1024]{1,0:T(8,128)(2,1)S(1)}, u32[]{:S(2)}, u32[]{:S(2)}) %collective-permute-start.46) | collective-permute-done | bytes 262176 | tf_op jit(solution)/shard_map/to_plane_3/ppermute | solution.py:41
  (168 shorter events, 52.8 us)
Async XLA Ops:
  4.5 11.6 %collective-permute-start = (bf16[128,1024]{1,0:T(8,128)(2,1)S(1)}, bf16[128,1024]{1,0:T(8,128)(2,1)S(1)}, u32[]{:S(2)}, u32[]{:S(2)}) collective-permute-start(bf16[128,1024]{1,0:T(8,128)(2,1)S(1)} %get-tuple-element.42.rest_0_), channel_id=1, source_target_pairs={{0,4},{1,5},{2,6},{3,7},{4,8},{5,9},{6,10},{7,11},{8,12},{9,13},{1... | collective-permute-start | bytes 786440 | tf_op jit(solution)/shard_map/ppermute | solution.py:27
  9.4 12.7 %collective-permute-start.4 = (bf16[128,1024]{1,0:T(8,128)(2,1)}, bf16[128,1024]{1,0:T(8,128)(2,1)S(1)}, u32[]{:S(2)}, u32[]{:S(2)}) collective-permute-start(bf16[128,1024]{1,0:T(8,128)(2,1)} %rest_0_), channel_id=1, source_target_pairs={{0,4},{1,5},{2,6},{3,7},{4,8},{5,9},{6,10},{7,11},{8,12},{9,13},{1... | collective-permute-start | bytes 786440 | tf_op jit(solution)/shard_map/ppermute | solution.py:27
  16.9 9.3 %collective-permute-start.1 = (bf16[128,1024]{1,0:T(8,128)(2,1)S(1)}, bf16[128,1024]{1,0:T(8,128)(2,1)S(1)}, u32[]{:S(2)}, u32[]{:S(2)}) collective-permute-start(bf16[128,1024]{1,0:T(8,128)(2,1)S(1)} %get-tuple-element.99), channel_id=1, source_target_pairs={{0,1},{1,0},{2,3},{3,2},{4,5},{5,4},{6,7},{7,6},{8,9},{9,8},{10,11... | collective-permute-start | bytes 786440 | tf_op jit(solution)/shard_map/ppermute | solution.py:22
  20.2 15.0 %collective-permute-start.2 = (bf16[128,1024]{1,0:T(8,128)(2,1)}, bf16[128,1024]{1,0:T(8,128)(2,1)S(1)}, u32[]{:S(2)}, u32[]{:S(2)}) collective-permute-start(bf16[128,1024]{1,0:T(8,128)(2,1)} %get-tuple-element.98), channel_id=1, source_target_pairs={{0,2},{1,3},{2,0},{3,1},{4,6},{5,7},{6,4},{7,5},{8,10},{9,11},{10,... | collective-permute-start | bytes 786440 | tf_op jit(solution)/shard_map/ppermute | solution.py:22
  21.7 13.5 %collective-permute-start.3 = (bf16[128,1024]{1,0:T(8,128)(2,1)S(1)}, bf16[128,1024]{1,0:T(8,128)(2,1)S(1)}, u32[]{:S(2)}, u32[]{:S(2)}) collective-permute-start(bf16[128,1024]{1,0:T(8,128)(2,1)S(1)} %get-tuple-element.97), channel_id=1, source_target_pairs={{0,3},{1,2},{2,1},{3,0},{4,7},{5,6},{6,5},{7,4},{8,11},{9,10},{10,... | collective-permute-start | bytes 786440 | tf_op jit(solution)/shard_map/ppermute | solution.py:22
  23.1 14.0 %collective-permute-start.5 = (bf16[128,1024]{1,0:T(8,128)(2,1)}, bf16[128,1024]{1,0:T(8,128)(2,1)S(1)}, u32[]{:S(2)}, u32[]{:S(2)}) collective-permute-start(bf16[128,1024]{1,0:T(8,128)(2,1)} %get-tuple-element.96), channel_id=1, source_target_pairs={{0,1},{1,0},{2,3},{3,2},{4,5},{5,4},{6,7},{7,6},{8,9},{9,8},{10,11... | collective-permute-start | bytes 786440 | tf_op jit(solution)/shard_map/ppermute | solution.py:22
  24.6 18.4 %collective-permute-start.6 = (bf16[128,1024]{1,0:T(8,128)(2,1)}, bf16[128,1024]{1,0:T(8,128)(2,1)S(1)}, u32[]{:S(2)}, u32[]{:S(2)}) collective-permute-start(bf16[128,1024]{1,0:T(8,128)(2,1)} %get-tuple-element.95), channel_id=1, source_target_pairs={{0,2},{1,3},{2,0},{3,1},{4,6},{5,7},{6,4},{7,5},{8,10},{9,11},{10,... | collective-permute-start | bytes 786440 | tf_op jit(solution)/shard_map/ppermute | solution.py:22
  26.1 16.8 %collective-permute-start.7 = (bf16[128,1024]{1,0:T(8,128)(2,1)}, bf16[128,1024]{1,0:T(8,128)(2,1)S(1)}, u32[]{:S(2)}, u32[]{:S(2)}) collective-permute-start(bf16[128,1024]{1,0:T(8,128)(2,1)} %get-tuple-element.94), channel_id=1, source_target_pairs={{0,3},{1,2},{2,1},{3,0},{4,7},{5,6},{6,5},{7,4},{8,11},{9,10},{10,... | collective-permute-start | bytes 786440 | tf_op jit(solution)/shard_map/ppermute | solution.py:22
  51.0 11.4 %collective-permute-start.10 = (bf16[64,2176]{1,0:T(8,128)(2,1)S(1)}, bf16[64,2176]{1,0:T(8,128)(2,1)S(1)}, u32[]{:S(2)}, u32[]{:S(2)}) collective-permute-start(bf16[64,2176]{1,0:T(8,128)(2,1)S(1)} %get-tuple-element.46), channel_id=1, source_target_pairs={{4,0},{5,1},{6,2},{7,3},{8,4},{9,5},{10,6},{11,7},{12,8},{13,9},{1... | collective-permute-start | bytes 835592 | tf_op jit(solution)/shard_map/from_plane_1/ppermute | solution.py:33
  57.1 23.3 %collective-permute-start.13 = (bf16[128,2176]{1,0:T(8,128)(2,1)S(1)}, bf16[128,2176]{1,0:T(8,128)(2,1)S(1)}, u32[]{:S(2)}, u32[]{:S(2)}) collective-permute-start(bf16[128,2176]{1,0:T(8,128)(2,1)S(1)} %pad_maximum_fusion.near_ref), channel_id=1, source_target_pairs={{16,0},{0,16},{17,1},{1,17},{18,2},{2,18},{19,3},{3,19},{20,4},{4,... | collective-permute-start | bytes 1671176 | tf_op jit(solution)/shard_map/ppermute | solution.py:48
  57.1 20.0 %collective-permute-start.12 = (bf16[128,2176]{1,0:T(8,128)(2,1)S(1)}, bf16[128,2176]{1,0:T(8,128)(2,1)S(1)}, u32[]{:S(2)}, u32[]{:S(2)}) collective-permute-start(bf16[128,2176]{1,0:T(8,128)(2,1)S(1)} %pad_maximum_fusion.near_ref), channel_id=1, source_target_pairs={{0,2},{1,3},{2,0},{3,1},{4,6},{5,7},{6,4},{7,5},{8,10},{9,11},{10,... | collective-permute-start | bytes 1671176 | tf_op jit(solution)/shard_map/gather_second_0/ppermute | solution.py:171
  63.0 9.9 %collective-permute-start.17 = (bf16[64,2176]{1,0:T(8,128)(2,1)S(1)}, bf16[64,2176]{1,0:T(8,128)(2,1)S(1)}, u32[]{:S(2)}, u32[]{:S(2)}) collective-permute-start(bf16[64,2176]{1,0:T(8,128)(2,1)S(1)} %collective-permute-done.10), channel_id=1, source_target_pairs={{4,0},{5,1},{6,2},{7,3},{8,4},{9,5},{10,6},{11,7},{12,8},{13,9},{1... | collective-permute-start | bytes 835592 | tf_op jit(solution)/shard_map/from_plane_1/ppermute | solution.py:33
  69.2 11.3 %collective-permute-start.20 = (bf16[128,2176]{1,0:T(8,128)(2,1)S(1)}, bf16[128,2176]{1,0:T(8,128)(2,1)S(1)}, u32[]{:S(2)}, u32[]{:S(2)}) collective-permute-start(bf16[128,2176]{1,0:T(8,128)(2,1)S(1)} %constant_dynamic-update-slice_fusion.near_ref), channel_id=1, source_target_pairs={{0,2},{1,3},{2,0},{3,1},{4,6},{5,7},{6,4},{7,5},{8,10},{9,11},{10,... | collective-permute-start | bytes 1671176 | tf_op jit(solution)/shard_map/gather_second_1/ppermute | solution.py:171
  70.8 32.1 %collective-permute-start.22 = (bf16[128,2176]{1,0:T(8,128)(2,1)S(1)}, bf16[128,2176]{1,0:T(8,128)(2,1)S(1)}, u32[]{:S(2)}, u32[]{:S(2)}) collective-permute-start(bf16[128,2176]{1,0:T(8,128)(2,1)S(1)} %constant_dynamic-update-slice_fusion.near_ref), channel_id=1, source_target_pairs={{16,0},{0,16},{17,1},{1,17},{18,2},{2,18},{19,3},{3,19},{20,4},{4,... | collective-permute-start | bytes 1671176 | tf_op jit(solution)/shard_map/ppermute | solution.py:48
  72.9 22.4 %collective-permute-start.18 = (bf16[64,2176]{1,0:T(8,128)(2,1)S(1)}, bf16[64,2176]{1,0:T(8,128)(2,1)S(1)}, u32[]{:S(2)}, u32[]{:S(2)}) collective-permute-start(bf16[64,2176]{1,0:T(8,128)(2,1)S(1)} %collective-permute-done.17), channel_id=1, source_target_pairs={{4,0},{5,1},{6,2},{7,3},{8,4},{9,5},{10,6},{11,7},{12,8},{13,9},{1... | collective-permute-start | bytes 835592 | tf_op jit(solution)/shard_map/from_plane_1/ppermute | solution.py:33
  77.1 9.9 %collective-permute-start.14 = (bf16[128,2176]{1,0:T(8,128)(2,1)S(1)}, bf16[128,2176]{1,0:T(8,128)(2,1)S(1)}, u32[]{:S(2)}, u32[]{:S(2)}) collective-permute-start(bf16[128,2176]{1,0:T(8,128)(2,1)S(1)} %collective-permute-done.12.far_ref), channel_id=1, source_target_pairs={{16,0},{0,16},{17,1},{1,17},{18,2},{2,18},{19,3},{3,19},{20,4},{4,... | collective-permute-start | bytes 1671176 | tf_op jit(solution)/shard_map/ppermute | solution.py:48
  80.5 14.9 %collective-permute-start.16 = (bf16[4,64,1024]{2,1,0:T(8,128)(2,1)S(1)}, bf16[4,64,1024]{2,1,0:T(8,128)(2,1)S(1)}, u32[]{:S(2)}, u32[]{:S(2)}) collective-permute-start(bf16[4,64,1024]{2,1,0:T(8,128)(2,1)S(1)} %get-tuple-element.50), channel_id=1, source_target_pairs={{16,0},{0,16},{17,1},{1,17},{18,2},{2,18},{19,3},{3,19},{20,4},{4,... | collective-permute-start | bytes 1572872 | tf_op jit(solution)/shard_map/ppermute | solution.py:48
  87.0 16.5 %collective-permute-start.23 = (bf16[128,2176]{1,0:T(8,128)(2,1)S(1)}, bf16[128,2176]{1,0:T(8,128)(2,1)S(1)}, u32[]{:S(2)}, u32[]{:S(2)}) collective-permute-start(bf16[128,2176]{1,0:T(8,128)(2,1)S(1)} %collective-permute-done.20.far_ref), channel_id=1, source_target_pairs={{16,0},{0,16},{17,1},{1,17},{18,2},{2,18},{19,3},{3,19},{20,4},{4,... | collective-permute-start | bytes 1671176 | tf_op jit(solution)/shard_map/ppermute | solution.py:48
  87.1 9.6 %collective-permute-start.24 = (bf16[128,2176]{1,0:T(8,128)(2,1)S(1)}, bf16[128,2176]{1,0:T(8,128)(2,1)S(1)}, u32[]{:S(2)}, u32[]{:S(2)}) collective-permute-start(bf16[128,2176]{1,0:T(8,128)(2,1)S(1)} %constant_dynamic-update-slice_fusion.2.near_ref), channel_id=1, source_target_pairs={{0,2},{1,3},{2,0},{3,1},{4,6},{5,7},{6,4},{7,5},{8,10},{9,11},{10,... | collective-permute-start | bytes 1671176 | tf_op jit(solution)/shard_map/gather_second_2/ppermute | solution.py:171
  96.7 16.7 %collective-permute-start.25 = (bf16[128,2176]{1,0:T(8,128)(2,1)S(1)}, bf16[128,2176]{1,0:T(8,128)(2,1)S(1)}, u32[]{:S(2)}, u32[]{:S(2)}) collective-permute-start(bf16[128,2176]{1,0:T(8,128)(2,1)S(1)} %constant_dynamic-update-slice_fusion.2.near_ref), channel_id=1, source_target_pairs={{16,0},{0,16},{17,1},{1,17},{18,2},{2,18},{19,3},{3,19},{20,4},{4,... | collective-permute-start | bytes 1671176 | tf_op jit(solution)/shard_map/ppermute | solution.py:48
  102.1 30.4 %collective-permute-start.31 = (bf16[128,2176]{1,0:T(8,128)(2,1)S(1)}, bf16[128,2176]{1,0:T(8,128)(2,1)S(1)}, u32[]{:S(2)}, u32[]{:S(2)}) collective-permute-start(bf16[128,2176]{1,0:T(8,128)(2,1)S(1)} %constant_dynamic-update-slice_fusion.4.near_ref), channel_id=1, source_target_pairs={{16,0},{0,16},{17,1},{1,17},{18,2},{2,18},{19,3},{3,19},{20,4},{4,... | collective-permute-start | bytes 1671176 | tf_op jit(solution)/shard_map/ppermute | solution.py:48
  103.0 9.6 %collective-permute-start.30 = (bf16[128,2176]{1,0:T(8,128)(2,1)S(1)}, bf16[128,2176]{1,0:T(8,128)(2,1)S(1)}, u32[]{:S(2)}, u32[]{:S(2)}) collective-permute-start(bf16[128,2176]{1,0:T(8,128)(2,1)S(1)} %constant_dynamic-update-slice_fusion.4.near_ref), channel_id=1, source_target_pairs={{0,2},{1,3},{2,0},{3,1},{4,6},{5,7},{6,4},{7,5},{8,10},{9,11},{10,... | collective-permute-start | bytes 1671176 | tf_op jit(solution)/shard_map/gather_second_3/ppermute | solution.py:171
  112.6 20.0 %collective-permute-start.35 = (bf16[128,2176]{1,0:T(8,128)(2,1)S(1)}, bf16[128,2176]{1,0:T(8,128)(2,1)S(1)}, u32[]{:S(2)}, u32[]{:S(2)}) collective-permute-start(bf16[128,2176]{1,0:T(8,128)(2,1)S(1)} %collective-permute-done.30.far_ref), channel_id=1, source_target_pairs={{16,0},{0,16},{17,1},{1,17},{18,2},{2,18},{19,3},{3,19},{20,4},{4,... | collective-permute-start | bytes 1671176 | tf_op jit(solution)/shard_map/ppermute | solution.py:48
  123.1 9.3 %collective-permute-start.34 = (bf16[2,64,1024]{2,1,0:T(8,128)(2,1)S(1)}, bf16[2,64,1024]{2,1,0:T(8,128)(2,1)S(1)}, u32[]{:S(2)}, u32[]{:S(2)}) collective-permute-start(bf16[2,64,1024]{2,1,0:T(8,128)(2,1)S(1)} %pad_maximum_fusion.6), channel_id=1, source_target_pairs={{0,1},{1,0},{2,3},{3,2},{4,5},{5,4},{6,7},{7,6},{8,9},{9,8},{10,11... | collective-permute-start | bytes 786440 | tf_op jit(solution)/shard_map/scatter_first_1/ppermute | solution.py:171
  123.7 12.1 %collective-permute-start.38 = (bf16[2,2,64,1024]{3,2,1,0:T(8,128)(2,1)S(1)}, bf16[2,2,64,1024]{3,2,1,0:T(8,128)(2,1)S(1)}, u32[]{:S(2)}, u32[]{:S(2)}) collective-permute-start(bf16[2,2,64,1024]{3,2,1,0:T(8,128)(2,1)S(1)} %pad_maximum_fusion.4), channel_id=1, source_target_pairs={{0,2},{1,3},{2,0},{3,1},{4,6},{5,7},{6,4},{7,5},{8,10},{9,11},{10,... | collective-permute-start | bytes 1572872 | tf_op jit(solution)/shard_map/scatter_second_2/ppermute | solution.py:171
  138.0 11.4 %collective-permute-start.39 = (bf16[2,2,64,1024]{3,2,1,0:T(8,128)(2,1)S(1)}, bf16[2,2,64,1024]{3,2,1,0:T(8,128)(2,1)S(1)}, u32[]{:S(2)}, u32[]{:S(2)}) collective-permute-start(bf16[2,2,64,1024]{3,2,1,0:T(8,128)(2,1)S(1)} %pad_maximum_fusion.5), channel_id=1, source_target_pairs={{0,2},{1,3},{2,0},{3,1},{4,6},{5,7},{6,4},{7,5},{8,10},{9,11},{10,... | collective-permute-start | bytes 1572872 | tf_op jit(solution)/shard_map/scatter_second_3/ppermute | solution.py:171
  138.4 12.3 %collective-permute-start.43 = (bf16[2,64,1024]{2,1,0:T(8,128)(2,1)S(1)}, bf16[2,64,1024]{2,1,0:T(8,128)(2,1)S(1)}, u32[]{:S(2)}, u32[]{:S(2)}) collective-permute-start(bf16[2,64,1024]{2,1,0:T(8,128)(2,1)S(1)} %pad_maximum_fusion.8), channel_id=1, source_target_pairs={{0,1},{1,0},{2,3},{3,2},{4,5},{5,4},{6,7},{7,6},{8,9},{9,8},{10,11... | collective-permute-start | bytes 786440 | tf_op jit(solution)/shard_map/scatter_first_2/ppermute | solution.py:171
  149.7 11.5 %collective-permute-start.40 = (bf16[2,2,64,1024]{3,2,1,0:T(8,128)(2,1)S(1)}, bf16[2,2,64,1024]{3,2,1,0:T(8,128)(2,1)S(1)}, u32[]{:S(2)}, u32[]{:S(2)}) collective-permute-start(bf16[2,2,64,1024]{3,2,1,0:T(8,128)(2,1)S(1)} %pad_maximum_fusion.2), channel_id=1, source_target_pairs={{0,2},{1,3},{2,0},{3,1},{4,6},{5,7},{6,4},{7,5},{8,10},{9,11},{10,... | collective-permute-start | bytes 1572872 | tf_op jit(solution)/shard_map/scatter_second_0/ppermute | solution.py:171
  150.7 18.0 %collective-permute-start.42 = (bf16[128,1024]{1,0:T(8,128)(2,1)S(1)}, bf16[128,1024]{1,0:T(8,128)(2,1)S(1)}, u32[]{:S(2)}, u32[]{:S(2)}) collective-permute-start(bf16[128,1024]{1,0:T(8,128)(2,1)S(1)} %pad_maximum_fusion.7), channel_id=1, source_target_pairs={{0,4},{1,5},{2,6},{3,7},{4,8},{5,9},{6,10},{7,11},{8,12},{9,13},{1... | collective-permute-start | bytes 786440 | tf_op jit(solution)/shard_map/to_plane_1/ppermute | solution.py:41
  150.8 20.4 %collective-permute-start.44 = (bf16[128,1024]{1,0:T(8,128)(2,1)S(1)}, bf16[128,1024]{1,0:T(8,128)(2,1)S(1)}, u32[]{:S(2)}, u32[]{:S(2)}) collective-permute-start(bf16[128,1024]{1,0:T(8,128)(2,1)S(1)} %pad_maximum_fusion.11), channel_id=1, source_target_pairs={{0,8},{1,9},{2,10},{3,11},{4,12},{5,13},{6,14},{7,15},{8,0},{9,1},... | collective-permute-start | bytes 786440 | tf_op jit(solution)/shard_map/to_plane_2/ppermute | solution.py:41
  151.5 12.1 %collective-permute-start.45 = (bf16[2,64,1024]{2,1,0:T(8,128)(2,1)S(1)}, bf16[2,64,1024]{2,1,0:T(8,128)(2,1)S(1)}, u32[]{:S(2)}, u32[]{:S(2)}) collective-permute-start(bf16[2,64,1024]{2,1,0:T(8,128)(2,1)S(1)} %pad_maximum_fusion.9), channel_id=1, source_target_pairs={{0,1},{1,0},{2,3},{3,2},{4,5},{5,4},{6,7},{7,6},{8,9},{9,8},{10,11... | collective-permute-start | bytes 786440 | tf_op jit(solution)/shard_map/scatter_first_3/ppermute | solution.py:171
  164.4 10.6 %collective-permute-start.46 = (bf16[128,1024]{1,0:T(8,128)(2,1)}, bf16[128,1024]{1,0:T(8,128)(2,1)S(1)}, u32[]{:S(2)}, u32[]{:S(2)}) collective-permute-start(bf16[128,1024]{1,0:T(8,128)(2,1)} %pad_maximum_fusion.12), channel_id=1, source_target_pairs={{0,12},{1,13},{2,14},{3,15},{4,0},{5,1},{6,2},{7,3},{8,4},{9,5},{1... | collective-permute-start | bytes 786440 | tf_op jit(solution)/shard_map/to_plane_3/ppermute | solution.py:41
  (28 other events, 304.4 us)

commit v11 on v7

--- a/solution.py
+++ b/solution.py
@@ -205,7 +205,6 @@
         [place],
         [near, far, w_gate, w_up, w_down],
         flops=6 * count * width * units,
-        moved=count,
     )
 
 
@@ -239,13 +238,13 @@
     return outs
 
 
-def core_totals(outs, cores):
+def core_totals(outs, cores, *waits):
     totals = []
     for rows_of in range(cores):
         total = wide(outs[rows_of][0])
         for ahead in range(1, cores):
             sent = outs[(rows_of + ahead) % cores][ahead]
-            total = total + wide(from_core(sent, cores - ahead))
+            total = total + wide(after(from_core(sent, cores - ahead), *waits))
         totals.append(total)
     return totals
 
@@ -331,48 +330,39 @@
     else:
         groups = [[0]] + [list(range(i, min(i + 8, planes))) for i in range(1, planes, 8)]
     nears, fars = [], []
-    weights = (w_gate[0].T, w_up[0].T, w_down[0])
-    run = functools.partial(
-        expert_outputs, place, weights=weights, experts=experts, cores=cores
-    )
     for number, group in enumerate(groups):
         sent = after(payload, nears[0]) if number > 1 else payload
         column = jnp.concatenate([from_plane(sent, ahead) if ahead else sent for ahead in group])
         if number > 1:
             column = after(column, nears[-1])
         nears.append(jnp.concatenate([column, crossed(column, True, f"gather_first_{number}")]))
-        if number > 1 and number == len(groups) - 1:
-            outs = run(nears[0], fars[0], waits={})
-            nears[-1] = after(nears[-1], *outs)
-        fars.append(crossed(after(nears[-1], *fars[-1:]), False, f"gather_second_{number}"))
-    totals = core_totals(outs, cores)
-    sent = second_share(totals)
-    totals = merged(totals, crossed(after(sent, fars[-1]), False, "scatter_second_0"), 2)
-    shared = first_share(totals)
-    partial = (totals, crossed(shared, True, "scatter_first_0"))
-    results = {}
-    returned = []
-    for number in reversed(range(1, len(groups))):
-        waits = {0: [outs], cores - 1: [sent]}
-        if number < len(groups) - 1:
-            waits[cores - 1] = [sent, shared]
+        fars.append(crossed(nears[-1], False, f"gather_second_{number}"))
+    weights = (w_gate[0].T, w_up[0].T, w_down[0])
+    run = functools.partial(
+        expert_outputs, place, weights=weights, experts=experts, cores=cores
+    )
+    outs = run(nears[0], fars[0], waits={})
+    own_totals = core_totals(outs, cores)
+    sent = after(second_share(own_totals), nears[-1])
+    got = crossed(sent, False, "scatter_second_0")
+    own_totals = merged(own_totals, got, 2)
+    own_got = crossed(first_share(own_totals), True, "scatter_first_0")
+    seconds, firsts, returned = [], [], []
+    for number in range(1, len(groups)):
+        waits = {0: [outs], cores - 1: [got]}
+        if number > 1:
+            waits = {0: [outs], cores - 1: [own_got, *seconds]}
         outs = run(nears[number], fars[number], waits=waits)
-        totals = core_totals(outs, cores)
-        if number < len(groups) - 1:
-            totals = [after(total, late) for total in totals]
-        sent = second_share(totals)
-        totals = merged(totals, crossed(sent, False, f"scatter_second_{number}"), 2)
-        late = after(first_share(totals), *results.values())
-        came = crossed(late, True, f"scatter_first_{number}")
+        totals = core_totals(outs, cores, *firsts[-1:])
+        seconds.append(second_share(totals))
+        totals = merged(totals, crossed(seconds[-1], False, f"scatter_second_{number}"), 2)
+        firsts.append(first_share(totals))
+        came = crossed(firsts[-1], True, f"scatter_first_{number}")
         rows_of = merged([total[0] for total in totals], came, None)
-        results = {}
         for i, ahead in enumerate(groups[number]):
             piece = [rows[i * part_rows : (i + 1) * part_rows] for rows in rows_of]
-            results[ahead] = after(narrow(jnp.concatenate(piece)), *returned[-1:])
-        for ahead, block in results.items():
-            returned.append(to_plane(block, ahead))
-    totals, came = partial
-    moe = jnp.concatenate(merged([total[0] for total in totals], came, None))
+            returned.append(to_plane(narrow(jnp.concatenate(piece)), ahead))
+    moe = jnp.concatenate(merged([total[0] for total in own_totals], own_got, None))
     moe = moe + sum(wide(block) for block in returned)
     moe = jnp.roll(moe.reshape(cores, part_rows, col_width), tok_index, axis=0)
     moe = moe.reshape(tok_rows, col_width)

time: 184 us -> 187 us (1.016)
  starting transfers between devices: 48.6 us -> 57.6 us
  waiting for transfers between devices: 87.3 us -> 79.5 us
    ppermute x12, waiting for transfers between devices: 51.3 us -> 39.8 us  [crossed(): return lax.ppermute(block, ('tok', 'blk'), route)]
    ppermute x3, starting transfers between devices: 6.44 us -> 11.5 us  [to_plane(): lax.ppermute(block, 'blk', [(i, (i + PLANE * ahead) % count) for i in ran...]
    ppermute x3, starting transfers between devices: 5.64 us -> 8 us  [from_plane(): lax.ppermute(block, 'blk', [((i + PLANE * ahead) % count, i) for i in ran...]
    ppermute x13, waiting for transfers between devices: 2.75 us -> 5.11 us  [from_core(): lax.ppermute(block, 'tok', [((i + ahead) % count, i) for i in range(count)])]
    unnamed x28 -> x31, local copies, waits for them, and re-layouts: 6.18 us -> 6.2 us
  transfers between devices with their start and end apart: 39 -> 39, of which waited for: 22 -> 24; matrix products, arithmetic and copies ran while one was open for 5% -> 7% of each run, Pallas kernels for 14% -> 14%
where the time goes in v11:
time: 187 us
  waiting for transfers between devices  79.5 us (43%)
  starting transfers between devices  57.6 us (31%)
  Pallas kernels  29.9 us (16%)
  local copies, waits for them, and re-layouts  10.4 us (6%)
  other arithmetic  8.01 us (4%)
    ppermute x12, waiting for transfers between devices, crossed(): return lax.ppermute(block, ('tok', 'blk'), route)  39.8 us
    pallas_call x10, Pallas kernels, local_call(): pl.pallas_call(body, in_specs=[scalar] * len(scalars) + [whole] * len(arr...  29.9 us
    ppermute x12, starting transfers between devices, crossed(): return lax.ppermute(block, ('tok', 'blk'), route)  18.7 us
    ppermute x3, waiting for transfers between devices, to_plane(): lax.ppermute(block, 'blk', [(i, (i + PLANE * ahead) % count) for i in ran...  16.3 us
    ppermute x3, starting transfers between devices, to_plane(): lax.ppermute(block, 'blk', [(i, (i + PLANE * ahead) % count) for i in ran...  11.5 us
    ppermute x6, starting transfers between devices, flipped(): lax.ppermute(block, 'blk', [(i, i ^ mask) for i in range(lax.axis_size('b...  9.12 us
    ppermute x6, waiting for transfers between devices, flipped(): lax.ppermute(block, 'blk', [(i, i ^ mask) for i in range(lax.axis_size('b...  8.53 us
    ppermute x2, starting transfers between devices, next_plane(): lax.ppermute(block, 'blk', [(i, i + PLANE) for i in range(count - PLANE)])  8.43 us
  transfers between devices with their start and end apart: 39, of which 24 were waited for; matrix products, arithmetic and copies ran while one was open for 7% of the time, Pallas kernels for 14%

profile of v11, /device:TPU:0, one launch (start us, length us, event | category | flops | bytes accessed | tf_op | source)
XLA Modules:
  0.0 186.7 jit_solution(9909214291135101174)
XLA Ops:
  4.5 4.9 %collective-permute-start = (bf16[128,1024]{1,0:T(8,128)(2,1)S(1)}, bf16[128,1024]{1,0:T(8,128)(2,1)S(1)}, u32[]{:S(2)}, u32[]{:S(2)}) collective-permute-start(bf16[128,1024]{1,0:T(8,128)(2,1)S(1)} %get-tuple-element.31.rest_0_), channel_id=1, source_target_pairs={{0,4},{1,5},{2,6},{3,7},{4,8},{5,9},{6,10},{7,11},{8,12},{9,13},{1... | collective-permute-start | bytes 786440 | tf_op jit(solution)/shard_map/ppermute | solution.py:27
  9.4 3.5 %collective-permute-start.4 = (bf16[128,1024]{1,0:T(8,128)(2,1)}, bf16[128,1024]{1,0:T(8,128)(2,1)S(1)}, u32[]{:S(2)}, u32[]{:S(2)}) collective-permute-start(bf16[128,1024]{1,0:T(8,128)(2,1)} %rest_0_), channel_id=1, source_target_pairs={{0,4},{1,5},{2,6},{3,7},{4,8},{5,9},{6,10},{7,11},{8,12},{9,13},{1... | collective-permute-start | bytes 786440 | tf_op jit(solution)/shard_map/ppermute | solution.py:27
  13.7 2.4 %collective-permute-done.rest_1_ = bf16[128,1024]{1,0:T(8,128)(2,1)S(1)} collective-permute-done((bf16[128,1024]{1,0:T(8,128)(2,1)S(1)}, bf16[128,1024]{1,0:T(8,128)(2,1)S(1)}, u32[]{:S(2)}, u32[]{:S(2)}) %collective-permute-start) | collective-permute-done | bytes 262176 | tf_op jit(solution)/shard_map/ppermute | solution.py:27
  25.9 2.6 %collective-permute-start.7 = (bf16[128,1024]{1,0:T(8,128)(2,1)}, bf16[128,1024]{1,0:T(8,128)(2,1)S(1)}, u32[]{:S(2)}, u32[]{:S(2)}) collective-permute-start(bf16[128,1024]{1,0:T(8,128)(2,1)} %get-tuple-element.72), channel_id=1, source_target_pairs={{0,3},{1,2},{2,1},{3,0},{4,7},{5,6},{6,5},{7,4},{8,11},{9,10},{10,... | collective-permute-start | bytes 786440 | tf_op jit(solution)/shard_map/ppermute | solution.py:22
  29.6 2.7 %scatter_fusion = bf16[8,16,2,1024]{3,1,2,0:T(8,128)(2,1)} fusion(bf16[8,16,2,1024]{3,1,2,0:T(8,128)(2,1)} %broadcast_in_dim.31, s32[8]{0:T(128)S(1)} %compare_select_fusion, bf16[8,16,2,1024]{3,1,2,0:T(8,128)(2,1)} %pad_maximum_fusion.2), kind=kCustom, calls=%fused_computation | custom fusion | bytes 1572896 | tf_op jit(solution)/shard_map/scatter | solution.py:304
  33.0 1.9 %shard_map.141.prob_ref = bf16[8,128,640]{2,1,0:T(8,128)(2,1)S(1)} custom-call(s32[2]{0:T(128)S(1)} %pad_add_fusion.place_ref, s32[8]{0:T(128)S(1)} %copy-done.10, bf16[128,1024]{1,0:T(8,128)(2,1)S(1)} %get-tuple-element.30.q_ref, bf16[128,1024]{1,0:T(8,128)(2,1)S(1)} %get-tuple-element.31.rest_0_, bf16[128,1024]{1,0:T(8,128)(2,1)S(1)} %collective-permute-done.rest_1_, ...), custom_call_target="tpu_custom_call" | custom-call | flops 167772160 | bytes 2883584 | tf_op jit(solution)/shard_map/pallas_call | solution.py:142
  34.9 2.3 %collective-permute-done.5.rest_2_ = bf16[128,1024]{1,0:T(8,128)(2,1)S(1)} collective-permute-done((bf16[128,1024]{1,0:T(8,128)(2,1)}, bf16[128,1024]{1,0:T(8,128)(2,1)S(1)}, u32[]{:S(2)}, u32[]{:S(2)}) %collective-permute-start.5) | collective-permute-done | bytes 262176 | tf_op jit(solution)/shard_map/ppermute | solution.py:22
  37.2 4.9 %collective-permute-done.6.rest_3_ = bf16[128,1024]{1,0:T(8,128)(2,1)S(1)} collective-permute-done((bf16[128,1024]{1,0:T(8,128)(2,1)}, bf16[128,1024]{1,0:T(8,128)(2,1)S(1)}, u32[]{:S(2)}, u32[]{:S(2)}) %collective-permute-start.6) | collective-permute-done | bytes 262176 | tf_op jit(solution)/shard_map/ppermute | solution.py:22
  42.0 2.2 %copy-done.3 = bf16[1024,2048]{1,0:T(8,128)(2,1)S(1)} copy-done((bf16[1024,2048]{1,0:T(8,128)(2,1)S(1)}, bf16[1024,2048]{1,0:T(8,128)(2,1)}, u32[]{:S(2)}) %copy-start.3) | copy-done | bytes 4194328
  46.0 2.6 %collective-permute-done.8.rest_1_ = f32[128,2048]{1,0:T(8,128)S(1)} collective-permute-done((f32[128,2048]{1,0:T(8,128)S(1)}, f32[128,2048]{1,0:T(8,128)S(1)}, u32[]{:S(2)}, u32[]{:S(2)}) %collective-permute-start.8) | collective-permute-done | bytes 1048608 | tf_op jit(solution)/shard_map/ppermute | solution.py:48
  50.0 4.5 %collective-permute-start.16 = (bf16[64,2176]{1,0:T(8,128)(2,1)S(1)}, bf16[64,2176]{1,0:T(8,128)(2,1)S(1)}, u32[]{:S(2)}, u32[]{:S(2)}) collective-permute-start(bf16[64,2176]{1,0:T(8,128)(2,1)S(1)} %get-tuple-element.41), channel_id=1, source_target_pairs={{4,0},{5,1},{6,2},{7,3},{8,4},{9,5},{10,6},{11,7},{12,8},{13,9},{1... | collective-permute-start | bytes 835592 | tf_op jit(solution)/shard_map/from_plane_1/ppermute | solution.py:33
  57.7 3.5 %collective-permute-start.15 = (bf16[64,2176]{1,0:T(8,128)(2,1)S(1)}, bf16[64,2176]{1,0:T(8,128)(2,1)S(1)}, u32[]{:S(2)}, u32[]{:S(2)}) collective-permute-start(bf16[64,2176]{1,0:T(8,128)(2,1)S(1)} %get-tuple-element.41), channel_id=1, source_target_pairs={{8,0},{9,1},{10,2},{11,3},{12,4},{13,5},{14,6},{15,7},{0,8},{1,9},... | collective-permute-start | bytes 835592 | tf_op jit(solution)/shard_map/from_plane_2/ppermute | solution.py:33
  61.6 6.9 %collective-permute-done.17 = bf16[64,2176]{1,0:T(8,128)(2,1)S(1)} collective-permute-done((bf16[64,2176]{1,0:T(8,128)(2,1)S(1)}, bf16[64,2176]{1,0:T(8,128)(2,1)S(1)}, u32[]{:S(2)}, u32[]{:S(2)}) %collective-permute-start.17) | collective-permute-done | bytes 278560 | tf_op jit(solution)/shard_map/from_plane_3/ppermute | solution.py:33
  70.3 7.9 %collective-permute-done.18 = bf16[128,2176]{1,0:T(8,128)(2,1)S(1)} collective-permute-done((bf16[128,2176]{1,0:T(8,128)(2,1)S(1)}, bf16[128,2176]{1,0:T(8,128)(2,1)S(1)}, u32[]{:S(2)}, u32[]{:S(2)}) %collective-permute-start.18) | collective-permute-done | bytes 557088 | tf_op jit(solution)/shard_map/gather_first_1/ppermute | solution.py:171
  79.9 2.4 %collective-permute-start.19 = (bf16[64,2176]{1,0:T(8,128)(2,1)S(1)}, bf16[64,2176]{1,0:T(8,128)(2,1)S(1)}, u32[]{:S(2)}, u32[]{:S(2)}) collective-permute-start(bf16[64,2176]{1,0:T(8,128)(2,1)S(1)} %collective-permute-done.15), channel_id=1, source_target_pairs={{0,1},{1,0},{2,3},{3,2},{4,5},{5,4},{6,7},{7,6},{8,9},{9,8},{10,11... | collective-permute-start | bytes 835592 | tf_op jit(solution)/shard_map/gather_first_2/ppermute | solution.py:171
  82.3 3.2 %shard_map.144 = (bf16[4,64,1024]{2,1,0:T(8,128)(2,1)S(1)}, bf16[4,64,1024]{2,1,0:T(8,128)(2,1)S(1)}) custom-call(s32[2]{0:T(128)S(1)} %pad_add_fusion.place_ref, bf16[128,2176]{1,0:T(8,128)(2,1)S(1)} %constant_dynamic-update-slice_fusion.near_ref, bf16[128,2176]{1,0:T(8,128)(2,1)S(1)} %collective-permute-done.10.far_ref, bf16[704,2048]{1,0:T(8,128)(2,1)S(1)} %bitcast.81, ...), custom_call_target="tpu_custom_call" | custom-call | flops 2214592512 | bytes 10813440 | tf_op jit(solution)/shard_map/pallas_call | solution.py:142
  86.1 3.2 %shard_map.145 = (bf16[4,64,1024]{2,1,0:T(8,128)(2,1)S(1)}, bf16[4,64,1024]{2,1,0:T(8,128)(2,1)S(1)}) custom-call(s32[2]{0:T(128)S(1)} %pad_add_fusion.place_ref, bf16[128,2176]{1,0:T(8,128)(2,1)S(1)} %collective-permute-done.11.near_ref, bf16[128,2176]{1,0:T(8,128)(2,1)S(1)} %collective-permute-done.12.far_ref, bf16[704,2048]{1,0:T(8,128)(2,1)S(1)} %bitcast.82, ...), custom_call_target="tpu_custom_call" | custom-call | flops 2214592512 | bytes 10813440 | tf_op jit(solution)/shard_map/pallas_call | solution.py:142
  91.3 4.6 %collective-permute-done.22.far_ref = bf16[256,2176]{1,0:T(8,128)(2,1)S(1)} collective-permute-done((bf16[256,2176]{1,0:T(8,128)(2,1)S(1)}, bf16[256,2176]{1,0:T(8,128)(2,1)S(1)}, u32[]{:S(2)}, u32[]{:S(2)}) %collective-permute-start.22) | collective-permute-done | bytes 1114144 | tf_op jit(solution)/shard_map/gather_second_1/ppermute | solution.py:171
  98.0 5.7 %shard_map.146 = (bf16[4,128,1024]{2,1,0:T(8,128)(2,1)S(1)}, bf16[4,128,1024]{2,1,0:T(8,128)(2,1)S(1)}) custom-call(s32[2]{0:T(128)S(1)} %pad_add_fusion.place_ref, bf16[256,2176]{1,0:T(8,128)(2,1)S(1)} %constant_dynamic-update-slice_fusion.2.near_ref, bf16[256,2176]{1,0:T(8,128)(2,1)S(1)} %collective-permute-done.22.far_ref, ...), custom_call_target="tpu_custom_call" | custom-call | flops 4429185024 | bytes 12976128 | tf_op jit(solution)/shard_map/pallas_call | solution.py:142
  105.4 5.9 %shard_map.147 = (bf16[4,128,1024]{2,1,0:T(8,128)(2,1)S(1)}, bf16[4,128,1024]{2,1,0:T(8,128)(2,1)S(1)}) custom-call(s32[2]{0:T(128)S(1)} %pad_add_fusion.place_ref, bf16[256,2176]{1,0:T(8,128)(2,1)S(1)} %collective-permute-done.23.near_ref, bf16[256,2176]{1,0:T(8,128)(2,1)S(1)} %collective-permute-done.24.far_ref, bf16[704,2048]{1,0:T(8,128)(2,1)S(1)} %bitcast.84, ...), custom_call_target="tpu_custom_call" | custom-call | flops 4429185024 | bytes 12976128 | tf_op jit(solution)/shard_map/pallas_call | solution.py:142
  116.5 4.6 %collective-permute-done.31.far_ref = bf16[128,2176]{1,0:T(8,128)(2,1)S(1)} collective-permute-done((bf16[128,2176]{1,0:T(8,128)(2,1)S(1)}, bf16[128,2176]{1,0:T(8,128)(2,1)S(1)}, u32[]{:S(2)}, u32[]{:S(2)}) %collective-permute-start.31) | collective-permute-done | bytes 557088 | tf_op jit(solution)/shard_map/gather_second_2/ppermute | solution.py:171
  121.3 1.8 collective-permute-start.21
  123.1 3.2 %shard_map.148 = (bf16[4,64,1024]{2,1,0:T(8,128)(2,1)S(1)}, bf16[4,64,1024]{2,1,0:T(8,128)(2,1)S(1)}) custom-call(s32[2]{0:T(128)S(1)} %pad_add_fusion.place_ref, bf16[128,2176]{1,0:T(8,128)(2,1)S(1)} %constant_dynamic-update-slice_fusion.5.near_ref, bf16[128,2176]{1,0:T(8,128)(2,1)S(1)} %collective-permute-done.31.far_ref, bf16[704,2048]{1,0:T(8,128)(2,1)S(1)} %bitcast.85, ...), custom_call_target="tpu_custom_call" | custom-call | flops 2214592512 | bytes 10813440 | tf_op jit(solution)/shard_map/pallas_call | solution.py:142
  126.3 4.3 %collective-permute-done.21 = bf16[2,64,1024]{2,1,0:T(8,128)(2,1)S(1)} collective-permute-done((bf16[2,64,1024]{2,1,0:T(8,128)(2,1)S(1)}, bf16[2,64,1024]{2,1,0:T(8,128)(2,1)S(1)}, u32[]{:S(2)}, u32[]{:S(2)}) %collective-permute-start.21) | collective-permute-done | bytes 262176 | tf_op jit(solution)/shard_map/scatter_first_0/ppermute | solution.py:171
  130.6 3.2 %shard_map.149 = (bf16[4,64,1024]{2,1,0:T(8,128)(2,1)S(1)}, bf16[4,64,1024]{2,1,0:T(8,128)(2,1)S(1)}) custom-call(s32[2]{0:T(128)S(1)} %pad_add_fusion.place_ref, bf16[128,2176]{1,0:T(8,128)(2,1)S(1)} %collective-permute-done.32.near_ref, bf16[128,2176]{1,0:T(8,128)(2,1)S(1)} %collective-permute-done.33.far_ref, bf16[704,2048]{1,0:T(8,128)(2,1)S(1)} %bitcast.86, ...), custom_call_target="tpu_custom_call" | custom-call | flops 2214592512 | bytes 10813440 | tf_op jit(solution)/shard_map/pallas_call | solution.py:142
  136.9 1.8 collective-permute-start.36
  139.0 12.1 %collective-permute-done.36 = bf16[2,2,64,1024]{3,2,1,0:T(8,128)(2,1)S(1)} collective-permute-done((bf16[2,2,64,1024]{3,2,1,0:T(8,128)(2,1)S(1)}, bf16[2,2,64,1024]{3,2,1,0:T(8,128)(2,1)S(1)}, u32[]{:S(2)}, u32[]{:S(2)}) %collective-permute-start.36) | collective-permute-done | bytes 524320 | tf_op jit(solution)/shard_map/scatter_second_2/ppermute | solution.py:171
  153.3 1.8 collective-permute-start.30
  155.5 2.4 %collective-permute-done.37 = bf16[2,64,1024]{2,1,0:T(8,128)(2,1)S(1)} collective-permute-done((bf16[2,64,1024]{2,1,0:T(8,128)(2,1)S(1)}, bf16[2,64,1024]{2,1,0:T(8,128)(2,1)S(1)}, u32[]{:S(2)}, u32[]{:S(2)}) %collective-permute-start.37) | collective-permute-done | bytes 262176 | tf_op jit(solution)/shard_map/scatter_first_2/ppermute | solution.py:171
  158.6 9.3 %collective-permute-start.38 = (bf16[128,1024]{1,0:T(8,128)(2,1)}, bf16[128,1024]{1,0:T(8,128)(2,1)S(1)}, u32[]{:S(2)}, u32[]{:S(2)}) collective-permute-start(bf16[128,1024]{1,0:T(8,128)(2,1)} %pad_maximum_fusion.10), channel_id=1, source_target_pairs={{0,8},{1,9},{2,10},{3,11},{4,12},{5,13},{6,14},{7,15},{8,0},{9,1},... | collective-permute-start | bytes 786440 | tf_op jit(solution)/shard_map/to_plane_2/ppermute | solution.py:41
  169.4 8.2 %collective-permute-done.29 = bf16[128,1024]{1,0:T(8,128)(2,1)S(1)} collective-permute-done((bf16[128,1024]{1,0:T(8,128)(2,1)S(1)}, bf16[128,1024]{1,0:T(8,128)(2,1)S(1)}, u32[]{:S(2)}, u32[]{:S(2)}) %collective-permute-start.29) | collective-permute-done | bytes 262176 | tf_op jit(solution)/shard_map/to_plane_1/ppermute | solution.py:41
  177.6 8.1 %collective-permute-done.38 = bf16[128,1024]{1,0:T(8,128)(2,1)S(1)} collective-permute-done((bf16[128,1024]{1,0:T(8,128)(2,1)}, bf16[128,1024]{1,0:T(8,128)(2,1)S(1)}, u32[]{:S(2)}, u32[]{:S(2)}) %collective-permute-start.38) | collective-permute-done | bytes 262176 | tf_op jit(solution)/shard_map/to_plane_2/ppermute | solution.py:41
  (142 shorter events, 46.8 us)
Async XLA Ops:
  4.5 11.6 %collective-permute-start = (bf16[128,1024]{1,0:T(8,128)(2,1)S(1)}, bf16[128,1024]{1,0:T(8,128)(2,1)S(1)}, u32[]{:S(2)}, u32[]{:S(2)}) collective-permute-start(bf16[128,1024]{1,0:T(8,128)(2,1)S(1)} %get-tuple-element.31.rest_0_), channel_id=1, source_target_pairs={{0,4},{1,5},{2,6},{3,7},{4,8},{5,9},{6,10},{7,11},{8,12},{9,13},{1... | collective-permute-start | bytes 786440 | tf_op jit(solution)/shard_map/ppermute | solution.py:27
  9.4 11.8 %collective-permute-start.4 = (bf16[128,1024]{1,0:T(8,128)(2,1)}, bf16[128,1024]{1,0:T(8,128)(2,1)S(1)}, u32[]{:S(2)}, u32[]{:S(2)}) collective-permute-start(bf16[128,1024]{1,0:T(8,128)(2,1)} %rest_0_), channel_id=1, source_target_pairs={{0,4},{1,5},{2,6},{3,7},{4,8},{5,9},{6,10},{7,11},{8,12},{9,13},{1... | collective-permute-start | bytes 786440 | tf_op jit(solution)/shard_map/ppermute | solution.py:27
  16.9 9.1 %collective-permute-start.1 = (bf16[128,1024]{1,0:T(8,128)(2,1)S(1)}, bf16[128,1024]{1,0:T(8,128)(2,1)S(1)}, u32[]{:S(2)}, u32[]{:S(2)}) collective-permute-start(bf16[128,1024]{1,0:T(8,128)(2,1)S(1)} %get-tuple-element.77), channel_id=1, source_target_pairs={{0,1},{1,0},{2,3},{3,2},{4,5},{5,4},{6,7},{7,6},{8,9},{9,8},{10,11... | collective-permute-start | bytes 786440 | tf_op jit(solution)/shard_map/ppermute | solution.py:22
  19.2 13.8 %collective-permute-start.2 = (bf16[128,1024]{1,0:T(8,128)(2,1)}, bf16[128,1024]{1,0:T(8,128)(2,1)S(1)}, u32[]{:S(2)}, u32[]{:S(2)}) collective-permute-start(bf16[128,1024]{1,0:T(8,128)(2,1)} %get-tuple-element.76), channel_id=1, source_target_pairs={{0,2},{1,3},{2,0},{3,1},{4,6},{5,7},{6,4},{7,5},{8,10},{9,11},{10,... | collective-permute-start | bytes 786440 | tf_op jit(solution)/shard_map/ppermute | solution.py:22
  20.7 12.3 %collective-permute-start.3 = (bf16[128,1024]{1,0:T(8,128)(2,1)S(1)}, bf16[128,1024]{1,0:T(8,128)(2,1)S(1)}, u32[]{:S(2)}, u32[]{:S(2)}) collective-permute-start(bf16[128,1024]{1,0:T(8,128)(2,1)S(1)} %get-tuple-element.75), channel_id=1, source_target_pairs={{0,3},{1,2},{2,1},{3,0},{4,7},{5,6},{6,5},{7,4},{8,11},{9,10},{10,... | collective-permute-start | bytes 786440 | tf_op jit(solution)/shard_map/ppermute | solution.py:22
  22.2 14.9 %collective-permute-start.5 = (bf16[128,1024]{1,0:T(8,128)(2,1)}, bf16[128,1024]{1,0:T(8,128)(2,1)S(1)}, u32[]{:S(2)}, u32[]{:S(2)}) collective-permute-start(bf16[128,1024]{1,0:T(8,128)(2,1)} %get-tuple-element.74), channel_id=1, source_target_pairs={{0,1},{1,0},{2,3},{3,2},{4,5},{5,4},{6,7},{7,6},{8,9},{9,8},{10,11... | collective-permute-start | bytes 786440 | tf_op jit(solution)/shard_map/ppermute | solution.py:22
  23.7 18.3 %collective-permute-start.6 = (bf16[128,1024]{1,0:T(8,128)(2,1)}, bf16[128,1024]{1,0:T(8,128)(2,1)S(1)}, u32[]{:S(2)}, u32[]{:S(2)}) collective-permute-start(bf16[128,1024]{1,0:T(8,128)(2,1)} %get-tuple-element.73), channel_id=1, source_target_pairs={{0,2},{1,3},{2,0},{3,1},{4,6},{5,7},{6,4},{7,5},{8,10},{9,11},{10,... | collective-permute-start | bytes 786440 | tf_op jit(solution)/shard_map/ppermute | solution.py:22
  25.9 16.1 %collective-permute-start.7 = (bf16[128,1024]{1,0:T(8,128)(2,1)}, bf16[128,1024]{1,0:T(8,128)(2,1)S(1)}, u32[]{:S(2)}, u32[]{:S(2)}) collective-permute-start(bf16[128,1024]{1,0:T(8,128)(2,1)} %get-tuple-element.72), channel_id=1, source_target_pairs={{0,3},{1,2},{2,1},{3,0},{4,7},{5,6},{6,5},{7,4},{8,11},{9,10},{10,... | collective-permute-start | bytes 786440 | tf_op jit(solution)/shard_map/ppermute | solution.py:22
  49.4 6.6 %collective-permute-start.9 = (bf16[64,2176]{1,0:T(8,128)(2,1)S(1)}, bf16[64,2176]{1,0:T(8,128)(2,1)S(1)}, u32[]{:S(2)}, u32[]{:S(2)}) collective-permute-start(bf16[64,2176]{1,0:T(8,128)(2,1)S(1)} %get-tuple-element.41), channel_id=1, source_target_pairs={{0,1},{1,0},{2,3},{3,2},{4,5},{5,4},{6,7},{7,6},{8,9},{9,8},{10,11... | collective-permute-start | bytes 835592 | tf_op jit(solution)/shard_map/gather_first_0/ppermute | solution.py:171
  50.0 11.6 %collective-permute-start.16 = (bf16[64,2176]{1,0:T(8,128)(2,1)S(1)}, bf16[64,2176]{1,0:T(8,128)(2,1)S(1)}, u32[]{:S(2)}, u32[]{:S(2)}) collective-permute-start(bf16[64,2176]{1,0:T(8,128)(2,1)S(1)} %get-tuple-element.41), channel_id=1, source_target_pairs={{4,0},{5,1},{6,2},{7,3},{8,4},{9,5},{10,6},{11,7},{12,8},{13,9},{1... | collective-permute-start | bytes 835592 | tf_op jit(solution)/shard_map/from_plane_1/ppermute | solution.py:33
  54.6 14.0 %collective-permute-start.17 = (bf16[64,2176]{1,0:T(8,128)(2,1)S(1)}, bf16[64,2176]{1,0:T(8,128)(2,1)S(1)}, u32[]{:S(2)}, u32[]{:S(2)}) collective-permute-start(bf16[64,2176]{1,0:T(8,128)(2,1)S(1)} %get-tuple-element.41), channel_id=1, source_target_pairs={{12,0},{13,1},{14,2},{15,3},{0,4},{1,5},{2,6},{3,7},{4,8},{5,9},{6... | collective-permute-start | bytes 835592 | tf_op jit(solution)/shard_map/from_plane_3/ppermute | solution.py:33
  56.1 29.5 %collective-permute-start.11 = (bf16[128,2176]{1,0:T(8,128)(2,1)S(1)}, bf16[128,2176]{1,0:T(8,128)(2,1)S(1)}, u32[]{:S(2)}, u32[]{:S(2)}) collective-permute-start(bf16[128,2176]{1,0:T(8,128)(2,1)S(1)} %constant_dynamic-update-slice_fusion.near_ref), channel_id=1, source_target_pairs={{16,0},{0,16},{17,1},{1,17},{18,2},{2,18},{19,3},{3,19},{20,4},{4,... | collective-permute-start | bytes 1671176 | tf_op jit(solution)/shard_map/ppermute | solution.py:48
  56.2 14.1 %collective-permute-start.10 = (bf16[128,2176]{1,0:T(8,128)(2,1)S(1)}, bf16[128,2176]{1,0:T(8,128)(2,1)S(1)}, u32[]{:S(2)}, u32[]{:S(2)}) collective-permute-start(bf16[128,2176]{1,0:T(8,128)(2,1)S(1)} %constant_dynamic-update-slice_fusion.near_ref), channel_id=1, source_target_pairs={{0,2},{1,3},{2,0},{3,1},{4,6},{5,7},{6,4},{7,5},{8,10},{9,11},{10,... | collective-permute-start | bytes 1671176 | tf_op jit(solution)/shard_map/gather_second_0/ppermute | solution.py:171
  57.7 22.1 %collective-permute-start.15 = (bf16[64,2176]{1,0:T(8,128)(2,1)S(1)}, bf16[64,2176]{1,0:T(8,128)(2,1)S(1)}, u32[]{:S(2)}, u32[]{:S(2)}) collective-permute-start(bf16[64,2176]{1,0:T(8,128)(2,1)S(1)} %get-tuple-element.41), channel_id=1, source_target_pairs={{8,0},{9,1},{10,2},{11,3},{12,4},{13,5},{14,6},{15,7},{0,8},{1,9},... | collective-permute-start | bytes 835592 | tf_op jit(solution)/shard_map/from_plane_2/ppermute | solution.py:33
  68.6 9.6 %collective-permute-start.18 = (bf16[128,2176]{1,0:T(8,128)(2,1)S(1)}, bf16[128,2176]{1,0:T(8,128)(2,1)S(1)}, u32[]{:S(2)}, u32[]{:S(2)}) collective-permute-start(bf16[128,2176]{1,0:T(8,128)(2,1)S(1)} %pad_maximum_fusion.1), channel_id=1, source_target_pairs={{0,1},{1,0},{2,3},{3,2},{4,5},{5,4},{6,7},{7,6},{8,9},{9,8},{10,11... | collective-permute-start | bytes 1671176 | tf_op jit(solution)/shard_map/gather_first_1/ppermute | solution.py:171
  70.2 15.9 %collective-permute-start.12 = (bf16[128,2176]{1,0:T(8,128)(2,1)S(1)}, bf16[128,2176]{1,0:T(8,128)(2,1)S(1)}, u32[]{:S(2)}, u32[]{:S(2)}) collective-permute-start(bf16[128,2176]{1,0:T(8,128)(2,1)S(1)} %collective-permute-done.10.far_ref), channel_id=1, source_target_pairs={{16,0},{0,16},{17,1},{1,17},{18,2},{2,18},{19,3},{3,19},{20,4},{4,... | collective-permute-start | bytes 1671176 | tf_op jit(solution)/shard_map/ppermute | solution.py:48
  78.3 17.6 %collective-permute-start.22 = (bf16[256,2176]{1,0:T(8,128)(2,1)S(1)}, bf16[256,2176]{1,0:T(8,128)(2,1)S(1)}, u32[]{:S(2)}, u32[]{:S(2)}) collective-permute-start(bf16[256,2176]{1,0:T(8,128)(2,1)S(1)} %constant_dynamic-update-slice_fusion.2.near_ref), channel_id=1, source_target_pairs={{0,2},{1,3},{2,0},{3,1},{4,6},{5,7},{6,4},{7,5},{8,10},{9,11},{10,... | collective-permute-start | bytes 3342344 | tf_op jit(solution)/shard_map/gather_second_1/ppermute | solution.py:171
  79.9 10.0 %collective-permute-start.19 = (bf16[64,2176]{1,0:T(8,128)(2,1)S(1)}, bf16[64,2176]{1,0:T(8,128)(2,1)S(1)}, u32[]{:S(2)}, u32[]{:S(2)}) collective-permute-start(bf16[64,2176]{1,0:T(8,128)(2,1)S(1)} %collective-permute-done.15), channel_id=1, source_target_pairs={{0,1},{1,0},{2,3},{3,2},{4,5},{5,4},{6,7},{7,6},{8,9},{9,8},{10,11... | collective-permute-start | bytes 835592 | tf_op jit(solution)/shard_map/gather_first_2/ppermute | solution.py:171
  82.3 21.7 %collective-permute-start.23 = (bf16[256,2176]{1,0:T(8,128)(2,1)S(1)}, bf16[256,2176]{1,0:T(8,128)(2,1)S(1)}, u32[]{:S(2)}, u32[]{:S(2)}) collective-permute-start(bf16[256,2176]{1,0:T(8,128)(2,1)S(1)} %constant_dynamic-update-slice_fusion.2.near_ref), channel_id=1, source_target_pairs={{16,0},{0,16},{17,1},{1,17},{18,2},{2,18},{19,3},{3,19},{20,4},{4,... | collective-permute-start | bytes 3342344 | tf_op jit(solution)/shard_map/ppermute | solution.py:48
  95.9 9.6 %collective-permute-start.24 = (bf16[256,2176]{1,0:T(8,128)(2,1)S(1)}, bf16[256,2176]{1,0:T(8,128)(2,1)S(1)}, u32[]{:S(2)}, u32[]{:S(2)}) collective-permute-start(bf16[256,2176]{1,0:T(8,128)(2,1)S(1)} %collective-permute-done.22.far_ref), channel_id=1, source_target_pairs={{16,0},{0,16},{17,1},{1,17},{18,2},{2,18},{19,3},{3,19},{20,4},{4,... | collective-permute-start | bytes 3342344 | tf_op jit(solution)/shard_map/ppermute | solution.py:48
  96.2 9.2 %collective-permute-start.20 = (bf16[2,2,64,1024]{3,2,1,0:T(8,128)(2,1)S(1)}, bf16[2,2,64,1024]{3,2,1,0:T(8,128)(2,1)S(1)}, u32[]{:S(2)}, u32[]{:S(2)}) collective-permute-start(bf16[2,2,64,1024]{3,2,1,0:T(8,128)(2,1)S(1)} %pad_maximum_fusion.3), channel_id=1, source_target_pairs={{0,2},{1,3},{2,0},{3,1},{4,6},{5,7},{6,4},{7,5},{8,10},{9,11},{10,... | collective-permute-start | bytes 1572872 | tf_op jit(solution)/shard_map/scatter_second_0/ppermute | solution.py:171
  103.7 9.6 %collective-permute-start.26 = (bf16[4,128,1024]{2,1,0:T(8,128)(2,1)S(1)}, bf16[4,128,1024]{2,1,0:T(8,128)(2,1)S(1)}, u32[]{:S(2)}, u32[]{:S(2)}) collective-permute-start(bf16[4,128,1024]{2,1,0:T(8,128)(2,1)S(1)} %get-tuple-element.46), channel_id=1, source_target_pairs={{16,0},{0,16},{17,1},{1,17},{18,2},{2,18},{19,3},{3,19},{20,4},{4,... | collective-permute-start | bytes 3145736 | tf_op jit(solution)/shard_map/ppermute | solution.py:48
  111.4 9.6 %collective-permute-start.31 = (bf16[128,2176]{1,0:T(8,128)(2,1)S(1)}, bf16[128,2176]{1,0:T(8,128)(2,1)S(1)}, u32[]{:S(2)}, u32[]{:S(2)}) collective-permute-start(bf16[128,2176]{1,0:T(8,128)(2,1)S(1)} %constant_dynamic-update-slice_fusion.5.near_ref), channel_id=1, source_target_pairs={{0,2},{1,3},{2,0},{3,1},{4,6},{5,7},{6,4},{7,5},{8,10},{9,11},{10,... | collective-permute-start | bytes 1671176 | tf_op jit(solution)/shard_map/gather_second_2/ppermute | solution.py:171
  114.7 20.4 %collective-permute-start.27 = (bf16[2,2,128,1024]{3,2,1,0:T(8,128)(2,1)S(1)}, bf16[2,2,128,1024]{3,2,1,0:T(8,128)(2,1)S(1)}, u32[]{:S(2)}, u32[]{:S(2)}) collective-permute-start(bf16[2,2,128,1024]{3,2,1,0:T(8,128)(2,1)S(1)} %pad_maximum_fusion), channel_id=1, source_target_pairs={{0,2},{1,3},{2,0},{3,1},{4,6},{5,7},{6,4},{7,5},{8,10},{9,11},{10,... | collective-permute-start | bytes 3145736 | tf_op jit(solution)/shard_map/scatter_second_1/ppermute | solution.py:171
  116.5 9.9 %collective-permute-start.32 = (bf16[128,2176]{1,0:T(8,128)(2,1)S(1)}, bf16[128,2176]{1,0:T(8,128)(2,1)S(1)}, u32[]{:S(2)}, u32[]{:S(2)}) collective-permute-start(bf16[128,2176]{1,0:T(8,128)(2,1)S(1)} %constant_dynamic-update-slice_fusion.5.near_ref), channel_id=1, source_target_pairs={{16,0},{0,16},{17,1},{1,17},{18,2},{2,18},{19,3},{3,19},{20,4},{4,... | collective-permute-start | bytes 1671176 | tf_op jit(solution)/shard_map/ppermute | solution.py:48
  121.0 9.6 %collective-permute-start.33 = (bf16[128,2176]{1,0:T(8,128)(2,1)S(1)}, bf16[128,2176]{1,0:T(8,128)(2,1)S(1)}, u32[]{:S(2)}, u32[]{:S(2)}) collective-permute-start(bf16[128,2176]{1,0:T(8,128)(2,1)S(1)} %collective-permute-done.31.far_ref), channel_id=1, source_target_pairs={{16,0},{0,16},{17,1},{1,17},{18,2},{2,18},{19,3},{3,19},{20,4},{4,... | collective-permute-start | bytes 1671176 | tf_op jit(solution)/shard_map/ppermute | solution.py:48
  121.3 9.3 %collective-permute-start.21 = (bf16[2,64,1024]{2,1,0:T(8,128)(2,1)S(1)}, bf16[2,64,1024]{2,1,0:T(8,128)(2,1)S(1)}, u32[]{:S(2)}, u32[]{:S(2)}) collective-permute-start(bf16[2,64,1024]{2,1,0:T(8,128)(2,1)S(1)} %pad_maximum_fusion.6), channel_id=1, source_target_pairs={{0,1},{1,0},{2,3},{3,2},{4,5},{5,4},{6,7},{7,6},{8,9},{9,8},{10,11... | collective-permute-start | bytes 786440 | tf_op jit(solution)/shard_map/scatter_first_0/ppermute | solution.py:171
  136.9 14.3 %collective-permute-start.36 = (bf16[2,2,64,1024]{3,2,1,0:T(8,128)(2,1)S(1)}, bf16[2,2,64,1024]{3,2,1,0:T(8,128)(2,1)S(1)}, u32[]{:S(2)}, u32[]{:S(2)}) collective-permute-start(bf16[2,2,64,1024]{3,2,1,0:T(8,128)(2,1)S(1)} %pad_maximum_fusion.5), channel_id=1, source_target_pairs={{0,2},{1,3},{2,0},{3,1},{4,6},{5,7},{6,4},{7,5},{8,10},{9,11},{10,... | collective-permute-start | bytes 1572872 | tf_op jit(solution)/shard_map/scatter_second_2/ppermute | solution.py:171
  138.7 14.4 %collective-permute-start.28 = (bf16[2,128,1024]{2,1,0:T(8,128)(2,1)S(1)}, bf16[2,128,1024]{2,1,0:T(8,128)(2,1)S(1)}, u32[]{:S(2)}, u32[]{:S(2)}) collective-permute-start(bf16[2,128,1024]{2,1,0:T(8,128)(2,1)S(1)} %pad_maximum_fusion.4), channel_id=1, source_target_pairs={{0,1},{1,0},{2,3},{3,2},{4,5},{5,4},{6,7},{7,6},{8,9},{9,8},{10,11... | collective-permute-start | bytes 1572872 | tf_op jit(solution)/shard_map/scatter_first_1/ppermute | solution.py:171
  153.3 16.0 %collective-permute-start.30 = (bf16[128,1024]{1,0:T(8,128)(2,1)S(1)}, bf16[128,1024]{1,0:T(8,128)(2,1)S(1)}, u32[]{:S(2)}, u32[]{:S(2)}) collective-permute-start(bf16[128,1024]{1,0:T(8,128)(2,1)S(1)} %pad_maximum_fusion.8), channel_id=1, source_target_pairs={{0,12},{1,13},{2,14},{3,15},{4,0},{5,1},{6,2},{7,3},{8,4},{9,5},{1... | collective-permute-start | bytes 786440 | tf_op jit(solution)/shard_map/to_plane_3/ppermute | solution.py:41
  155.2 22.4 %collective-permute-start.29 = (bf16[128,1024]{1,0:T(8,128)(2,1)S(1)}, bf16[128,1024]{1,0:T(8,128)(2,1)S(1)}, u32[]{:S(2)}, u32[]{:S(2)}) collective-permute-start(bf16[128,1024]{1,0:T(8,128)(2,1)S(1)} %pad_maximum_fusion.7), channel_id=1, source_target_pairs={{0,4},{1,5},{2,6},{3,7},{4,8},{5,9},{6,10},{7,11},{8,12},{9,13},{1... | collective-permute-start | bytes 786440 | tf_op jit(solution)/shard_map/to_plane_1/ppermute | solution.py:41
  158.6 27.0 %collective-permute-start.38 = (bf16[128,1024]{1,0:T(8,128)(2,1)}, bf16[128,1024]{1,0:T(8,128)(2,1)S(1)}, u32[]{:S(2)}, u32[]{:S(2)}) collective-permute-start(bf16[128,1024]{1,0:T(8,128)(2,1)} %pad_maximum_fusion.10), channel_id=1, source_target_pairs={{0,8},{1,9},{2,10},{3,11},{4,12},{5,13},{6,14},{7,15},{8,0},{9,1},... | collective-permute-start | bytes 786440 | tf_op jit(solution)/shard_map/to_plane_2/ppermute | solution.py:41
  (20 other events, 227.6 us)

commit v12 on v11

--- a/solution.py
+++ b/solution.py
@@ -171,11 +171,15 @@
         return lax.ppermute(block, ("tok", "blk"), route)
 
 
-def expert_kernel(experts, ahead, place_ref, near_ref, far_ref, gate_ref, up_ref, down_ref, *outs):
+def expert_kernel(experts, ahead, planes, plane, span, place_ref, near_ref, far_ref, gate_ref, up_ref, down_ref, *outs):
     width = gate_ref.shape[1]
     parts = len(outs)
     blocks, part_rows, part_width = outs[0].shape
-    held = jnp.concatenate([near_ref[...], far_ref[...]], axis=0)
+    starts = [(i * planes + plane) * part_rows // span for i in range(2)]
+    held = jnp.concatenate(
+        [ref[start : start + part_rows] for ref in (near_ref, far_ref) for start in starts],
+        axis=0,
+    )
     rows = held[:, :width]
     lanes = held[:, width:].astype(jnp.float32)
     lane_ids = lax.broadcasted_iota(jnp.int32, lanes.shape, 1)
@@ -195,12 +199,12 @@
             outs[part][order[block]] = product[block * part_rows : (block + 1) * part_rows]
 
 
-def run_expert(place, near, far, w_gate, w_up, w_down, experts, parts, ahead):
-    count = 2 * near.shape[0]
+def run_expert(place, near, far, w_gate, w_up, w_down, experts, parts, ahead, planes, plane, span):
+    count = 2 * near.shape[0] // planes * span
     units, width = w_gate.shape
     out_shape = jax.ShapeDtypeStruct((PLANE, count // PLANE, width // parts), jnp.bfloat16)
     return local_call(
-        functools.partial(expert_kernel, experts, ahead),
+        functools.partial(expert_kernel, experts, ahead, planes, plane, span),
         [out_shape] * parts,
         [place],
         [near, far, w_gate, w_up, w_down],
@@ -228,13 +232,16 @@
     return [total[0:count] + wide(got[i]) for i, total in enumerate(totals)]
 
 
-def expert_outputs(place, near, far, weights, experts, cores, waits):
+def expert_outputs(place, rows, weights, experts, cores, planes, plane, span, waits):
     outs = []
     for ahead in range(cores):
-        near_rows = from_core(near, ahead) if ahead else near
-        far_rows = from_core(far, ahead) if ahead else far
-        near_rows = after(near_rows, *outs[-1:], *waits.get(ahead, []))
-        outs.append(run_expert(place, near_rows, far_rows, *weights, experts, cores, ahead))
+        near, far = rows[ahead]
+        near = after(near, *outs[-1:], *waits.get(ahead, []))
+        outs.append(
+            run_expert(
+                place, near, far, *weights, experts, cores, ahead, planes, plane, span
+            )
+        )
     return outs
 
 
@@ -324,43 +331,70 @@
         [place],
         [norm_gain[None, :], lanes, *addends],
     )
-    weights = (w_gate[0].T, w_up[0].T, w_down[0])
     if planes <= 4:
         groups = [[0]] + [sorted({i, planes - i}) for i in range(1, planes // 2 + 1)]
     else:
         groups = [[0]] + [list(range(i, min(i + 8, planes))) for i in range(1, planes, 8)]
-    nears, fars = [], []
-    for number, group in enumerate(groups):
-        sent = after(payload, nears[0]) if number > 1 else payload
-        column = jnp.concatenate([from_plane(sent, ahead) if ahead else sent for ahead in group])
-        if number > 1:
-            column = after(column, nears[-1])
-        nears.append(jnp.concatenate([column, crossed(column, True, f"gather_first_{number}")]))
-        fars.append(crossed(nears[-1], False, f"gather_second_{number}"))
     weights = (w_gate[0].T, w_up[0].T, w_down[0])
     run = functools.partial(
         expert_outputs, place, weights=weights, experts=experts, cores=cores
     )
-    outs = run(nears[0], fars[0], waits={})
+    columns, nears, fars, rows = [], [], [], []
+    sent = payload
+    for group in groups:
+        columns.append(
+            jnp.concatenate([from_plane(sent, ahead) if ahead else sent for ahead in group])
+        )
+        sent = after(payload, columns[-1])
+    for number, column in enumerate(columns):
+        if number > 0:
+            column = after(column, nears[-1])
+        if number == 2:
+            outs = run(rows=rows[0], planes=1, plane=0, span=1, waits={})
+            column = after(column, outs)
+        nears.append(
+            jnp.concatenate([column, crossed(column, True, f"gather_first_{number}")])
+        )
+        ready = after(nears[-1], fars[0], columns[2]) if number == 1 else nears[-1]
+        fars.append(crossed(ready, False, f"gather_second_{number}"))
+        rows.append(
+            [
+                (from_core(nears[-1], i), from_core(fars[-1], i)) if i else (nears[-1], fars[-1])
+                for i in range(cores)
+            ]
+        )
     own_totals = core_totals(outs, cores)
     sent = after(second_share(own_totals), nears[-1])
-    got = crossed(sent, False, "scatter_second_0")
-    own_totals = merged(own_totals, got, 2)
+    own_second = crossed(sent, False, "scatter_second_0")
+    own_totals = merged(own_totals, own_second, 2)
     own_got = crossed(first_share(own_totals), True, "scatter_first_0")
     seconds, firsts, returned = [], [], []
-    for number in range(1, len(groups)):
-        waits = {0: [outs], cores - 1: [got]}
-        if number > 1:
-            waits = {0: [outs], cores - 1: [own_got, *seconds]}
-        outs = run(nears[number], fars[number], waits=waits)
+    span_of = 1 if planes <= 4 else 8
+    steps = [
+        (number, plane, group[plane : plane + span_of])
+        for number, group in enumerate(groups)
+        for plane in range(0, len(group), span_of)
+    ]
+    for number, plane, aheads in steps[1:]:
+        waits = {0: [outs], cores - 1: [*seconds[-1:]]}
+        if len(seconds) == 2:
+            waits[0].append(own_second)
+        outs = run(
+            rows=rows[number],
+            planes=len(groups[number]),
+            plane=plane,
+            span=len(aheads),
+            waits=waits,
+        )
         totals = core_totals(outs, cores, *firsts[-1:])
         seconds.append(second_share(totals))
-        totals = merged(totals, crossed(seconds[-1], False, f"scatter_second_{number}"), 2)
+        got = crossed(seconds[-1], False, f"scatter_second_{aheads[0]}")
+        totals = merged(totals, got, 2)
         firsts.append(first_share(totals))
-        came = crossed(firsts[-1], True, f"scatter_first_{number}")
-        rows_of = merged([total[0] for total in totals], came, None)
-        for i, ahead in enumerate(groups[number]):
-            piece = [rows[i * part_rows : (i + 1) * part_rows] for rows in rows_of]
+        got = crossed(firsts[-1], True, f"scatter_first_{aheads[0]}")
+        rows_of = merged([total[0] for total in totals], got, None)
+        for i, ahead in enumerate(aheads):
+            piece = [part[i * part_rows : (i + 1) * part_rows] for part in rows_of]
             returned.append(to_plane(narrow(jnp.concatenate(piece)), ahead))
     moe = jnp.concatenate(merged([total[0] for total in own_totals], own_got, None))
     moe = moe + sum(wide(block) for block in returned)

time: 187 us -> 174 us (0.930)
  starting transfers between devices: 57.6 us -> 44.3 us
    ppermute x3, starting transfers between devices: 11.5 us -> 1.48 us  [to_plane(): lax.ppermute(block, 'blk', [(i, (i + PLANE * ahead) % count) for i in ran...]
    ppermute x3, waiting for transfers between devices: 7.33 us -> 14.6 us  [from_plane(): lax.ppermute(block, 'blk', [((i + PLANE * ahead) % count, i) for i in ran...]
    ppermute x3, waiting for transfers between devices: 16.3 us -> 11.1 us  [to_plane(): lax.ppermute(block, 'blk', [(i, (i + PLANE * ahead) % count) for i in ran...]
    ppermute x12 -> x14, waiting for transfers between devices: 39.8 us -> 36.4 us  [crossed(): return lax.ppermute(block, ('tok', 'blk'), route)]
    ppermute x3, starting transfers between devices: 8 us -> 5.24 us  [from_plane(): lax.ppermute(block, 'blk', [((i + PLANE * ahead) % count, i) for i in ran...]
    ppermute x12 -> x14, starting transfers between devices: 18.7 us -> 16.2 us  [crossed(): return lax.ppermute(block, ('tok', 'blk'), route)]
    ppermute x13 -> x15, starting transfers between devices: 1.81 us -> 3.69 us  [from_core(): lax.ppermute(block, 'tok', [((i + ahead) % count, i) for i in range(count)])]
    pallas_call x10 -> x12, Pallas kernels: 29.9 us -> 31.4 us  [local_call(): pl.pallas_call(body, in_specs=[scalar] * len(scalars) + [whole] * len(arr...]
  transfers between devices with their start and end apart: 39 -> 43, of which waited for: 24 -> 21; matrix products, arithmetic and copies ran while one was open for 7% -> 7% of each run, Pallas kernels for 14% -> 16%
where the time goes in v12:
time: 174 us
  waiting for transfers between devices  79.8 us (46%)
  starting transfers between devices  44.3 us (25%)
  Pallas kernels  31.4 us (18%)
  local copies, waits for them, and re-layouts  8.71 us (5%)
  other arithmetic  8.63 us (5%)
    ppermute x14, waiting for transfers between devices, crossed(): return lax.ppermute(block, ('tok', 'blk'), route)  36.4 us
    pallas_call x12, Pallas kernels, local_call(): pl.pallas_call(body, in_specs=[scalar] * len(scalars) + [whole] * len(arr...  31.4 us
    ppermute x14, starting transfers between devices, crossed(): return lax.ppermute(block, ('tok', 'blk'), route)  16.2 us
    ppermute x3, waiting for transfers between devices, from_plane(): lax.ppermute(block, 'blk', [((i + PLANE * ahead) % count, i) for i in ran...  14.6 us
    ppermute x3, waiting for transfers between devices, to_plane(): lax.ppermute(block, 'blk', [(i, (i + PLANE * ahead) % count) for i in ran...  11.1 us
    ppermute x6, waiting for transfers between devices, flipped(): lax.ppermute(block, 'blk', [(i, i ^ mask) for i in range(lax.axis_size('b...  10.1 us
    ppermute x6, starting transfers between devices, flipped(): lax.ppermute(block, 'blk', [(i, i ^ mask) for i in range(lax.axis_size('b...  9.31 us
    ppermute x2, starting transfers between devices, next_plane(): lax.ppermute(block, 'blk', [(i, i + PLANE) for i in range(count - PLANE)])  8.43 us
  transfers between devices with their start and end apart: 43, of which 21 were waited for; matrix products, arithmetic and copies ran while one was open for 7% of the time, Pallas kernels for 16%

profile of v12, /device:TPU:0, one launch (start us, length us, event | category | flops | bytes accessed | tf_op | source)
XLA Modules:
  0.0 174.2 jit_solution(6813243090047027670)
XLA Ops:
  4.5 4.9 %collective-permute-start = (bf16[128,1024]{1,0:T(8,128)(2,1)S(1)}, bf16[128,1024]{1,0:T(8,128)(2,1)S(1)}, u32[]{:S(2)}, u32[]{:S(2)}) collective-permute-start(bf16[128,1024]{1,0:T(8,128)(2,1)S(1)} %get-tuple-element.43.rest_0_), channel_id=1, source_target_pairs={{0,4},{1,5},{2,6},{3,7},{4,8},{5,9},{6,10},{7,11},{8,12},{9,13},{1... | collective-permute-start | bytes 786440 | tf_op jit(solution)/shard_map/ppermute | solution.py:27
  9.4 3.5 %collective-permute-start.4 = (bf16[128,1024]{1,0:T(8,128)(2,1)}, bf16[128,1024]{1,0:T(8,128)(2,1)S(1)}, u32[]{:S(2)}, u32[]{:S(2)}) collective-permute-start(bf16[128,1024]{1,0:T(8,128)(2,1)} %rest_0_), channel_id=1, source_target_pairs={{0,4},{1,5},{2,6},{3,7},{4,8},{5,9},{6,10},{7,11},{8,12},{9,13},{1... | collective-permute-start | bytes 786440 | tf_op jit(solution)/shard_map/ppermute | solution.py:27
  13.7 2.4 %collective-permute-done.rest_1_ = bf16[128,1024]{1,0:T(8,128)(2,1)S(1)} collective-permute-done((bf16[128,1024]{1,0:T(8,128)(2,1)S(1)}, bf16[128,1024]{1,0:T(8,128)(2,1)S(1)}, u32[]{:S(2)}, u32[]{:S(2)}) %collective-permute-start) | collective-permute-done | bytes 262176 | tf_op jit(solution)/shard_map/ppermute | solution.py:27
  25.8 2.8 %collective-permute-start.7 = (bf16[128,1024]{1,0:T(8,128)(2,1)}, bf16[128,1024]{1,0:T(8,128)(2,1)S(1)}, u32[]{:S(2)}, u32[]{:S(2)}) collective-permute-start(bf16[128,1024]{1,0:T(8,128)(2,1)} %get-tuple-element.96), channel_id=1, source_target_pairs={{0,3},{1,2},{2,1},{3,0},{4,7},{5,6},{6,5},{7,4},{8,11},{9,10},{10,... | collective-permute-start | bytes 786440 | tf_op jit(solution)/shard_map/ppermute | solution.py:22
  28.9 1.8 %scatter_fusion = bf16[8,16,2,1024]{3,1,2,0:T(8,128)(2,1)S(1)} fusion(bf16[8,16,2,1024]{3,1,2,0:T(8,128)(2,1)S(1)} %broadcast_in_dim.31, s32[8]{0:T(128)S(1)} %compare_select_fusion, bf16[8,16,2,1024]{3,1,2,0:T(8,128)(2,1)} %pad_maximum_fusion), kind=kCustom, calls=%fused_computation | custom fusion | bytes 1572896 | tf_op jit(solution)/shard_map/scatter | solution.py:311
  30.7 2.4 %collective-permute-done.2.rest_3_ = bf16[128,1024]{1,0:T(8,128)(2,1)S(1)} collective-permute-done((bf16[128,1024]{1,0:T(8,128)(2,1)}, bf16[128,1024]{1,0:T(8,128)(2,1)S(1)}, u32[]{:S(2)}, u32[]{:S(2)}) %collective-permute-start.2) | collective-permute-done | bytes 262176 | tf_op jit(solution)/shard_map/ppermute | solution.py:22
  33.1 1.9 %shard_map.141.prob_ref = bf16[8,128,640]{2,1,0:T(8,128)(2,1)S(1)} custom-call(s32[2]{0:T(128)S(1)} %pad_add_fusion.place_ref, s32[8]{0:T(128)S(1)} %copy-done.10, bf16[128,1024]{1,0:T(8,128)(2,1)S(1)} %get-tuple-element.42.q_ref, bf16[128,1024]{1,0:T(8,128)(2,1)S(1)} %get-tuple-element.43.rest_0_, bf16[128,1024]{1,0:T(8,128)(2,1)S(1)} %collective-permute-done.rest_1_, ...), custom_call_target="tpu_custom_call" | custom-call | flops 167772160 | bytes 2883584 | tf_op jit(solution)/shard_map/pallas_call | solution.py:142
  35.0 2.1 %collective-permute-done.5.rest_2_ = bf16[128,1024]{1,0:T(8,128)(2,1)S(1)} collective-permute-done((bf16[128,1024]{1,0:T(8,128)(2,1)}, bf16[128,1024]{1,0:T(8,128)(2,1)S(1)}, u32[]{:S(2)}, u32[]{:S(2)}) %collective-permute-start.5) | collective-permute-done | bytes 262176 | tf_op jit(solution)/shard_map/ppermute | solution.py:22
  37.1 5.0 %collective-permute-done.6.rest_3_ = bf16[128,1024]{1,0:T(8,128)(2,1)S(1)} collective-permute-done((bf16[128,1024]{1,0:T(8,128)(2,1)}, bf16[128,1024]{1,0:T(8,128)(2,1)S(1)}, u32[]{:S(2)}, u32[]{:S(2)}) %collective-permute-start.6) | collective-permute-done | bytes 262176 | tf_op jit(solution)/shard_map/ppermute | solution.py:22
  42.1 2.2 %copy-done.3 = bf16[1024,2048]{1,0:T(8,128)(2,1)S(1)} copy-done((bf16[1024,2048]{1,0:T(8,128)(2,1)S(1)}, bf16[1024,2048]{1,0:T(8,128)(2,1)}, u32[]{:S(2)}) %copy-start.3) | copy-done | bytes 4194328
  46.1 2.6 %collective-permute-done.8.rest_1_ = f32[128,2048]{1,0:T(8,128)S(1)} collective-permute-done((f32[128,2048]{1,0:T(8,128)S(1)}, f32[128,2048]{1,0:T(8,128)S(1)}, u32[]{:S(2)}, u32[]{:S(2)}) %collective-permute-start.8) | collective-permute-done | bytes 1048608 | tf_op jit(solution)/shard_map/ppermute | solution.py:48
  50.1 4.5 %collective-permute-start.15 = (bf16[64,2176]{1,0:T(8,128)(2,1)S(1)}, bf16[64,2176]{1,0:T(8,128)(2,1)S(1)}, u32[]{:S(2)}, u32[]{:S(2)}) collective-permute-start(bf16[64,2176]{1,0:T(8,128)(2,1)S(1)} %get-tuple-element.54), channel_id=1, source_target_pairs={{4,0},{5,1},{6,2},{7,3},{8,4},{9,5},{10,6},{11,7},{12,8},{13,9},{1... | collective-permute-start | bytes 835592 | tf_op jit(solution)/shard_map/from_plane_1/ppermute | solution.py:33
  54.6 7.1 %collective-permute-done.15 = bf16[64,2176]{1,0:T(8,128)(2,1)S(1)} collective-permute-done((bf16[64,2176]{1,0:T(8,128)(2,1)S(1)}, bf16[64,2176]{1,0:T(8,128)(2,1)S(1)}, u32[]{:S(2)}, u32[]{:S(2)}) %collective-permute-start.15) | collective-permute-done | bytes 278560 | tf_op jit(solution)/shard_map/from_plane_1/ppermute | solution.py:33
  61.8 6.6 %collective-permute-done.16 = bf16[64,2176]{1,0:T(8,128)(2,1)S(1)} collective-permute-done((bf16[64,2176]{1,0:T(8,128)(2,1)S(1)}, bf16[64,2176]{1,0:T(8,128)(2,1)S(1)}, u32[]{:S(2)}, u32[]{:S(2)}) %collective-permute-start.16) | collective-permute-done | bytes 278560 | tf_op jit(solution)/shard_map/from_plane_3/ppermute | solution.py:33
  70.3 12.8 %collective-permute-done.18 = bf16[128,2176]{1,0:T(8,128)(2,1)S(1)} collective-permute-done((bf16[128,2176]{1,0:T(8,128)(2,1)S(1)}, bf16[128,2176]{1,0:T(8,128)(2,1)S(1)}, u32[]{:S(2)}, u32[]{:S(2)}) %collective-permute-start.18) | collective-permute-done | bytes 557088 | tf_op jit(solution)/shard_map/gather_first_1/ppermute | solution.py:171
  86.2 3.2 %shard_map.144 = (bf16[4,64,1024]{2,1,0:T(8,128)(2,1)S(1)}, bf16[4,64,1024]{2,1,0:T(8,128)(2,1)S(1)}) custom-call(s32[2]{0:T(128)S(1)} %pad_add_fusion.place_ref, bf16[128,2176]{1,0:T(8,128)(2,1)S(1)} %constant_dynamic-update-slice_fusion.near_ref, bf16[128,2176]{1,0:T(8,128)(2,1)S(1)} %collective-permute-done.10.far_ref, bf16[704,2048]{1,0:T(8,128)(2,1)S(1)} %bitcast.95, ...), custom_call_target="tpu_custom_call" | custom-call | flops 2214592512 | bytes 10813440 | tf_op jit(solution)/shard_map/pallas_call | solution.py:142
  91.4 3.2 %shard_map.145 = (bf16[4,64,1024]{2,1,0:T(8,128)(2,1)S(1)}, bf16[4,64,1024]{2,1,0:T(8,128)(2,1)S(1)}) custom-call(s32[2]{0:T(128)S(1)} %pad_add_fusion.place_ref, bf16[128,2176]{1,0:T(8,128)(2,1)S(1)} %collective-permute-done.11.near_ref, bf16[128,2176]{1,0:T(8,128)(2,1)S(1)} %collective-permute-done.12.far_ref, bf16[704,2048]{1,0:T(8,128)(2,1)S(1)} %bitcast.96, ...), custom_call_target="tpu_custom_call" | custom-call | flops 2214592512 | bytes 10813440 | tf_op jit(solution)/shard_map/pallas_call | solution.py:142
  94.8 1.7 %collective-permute-start.19 = (bf16[64,2176]{1,0:T(8,128)(2,1)S(1)}, bf16[64,2176]{1,0:T(8,128)(2,1)S(1)}, u32[]{:S(2)}, u32[]{:S(2)}) collective-permute-start(bf16[64,2176]{1,0:T(8,128)(2,1)S(1)} %collective-permute-done.17), channel_id=1, source_target_pairs={{0,1},{1,0},{2,3},{3,2},{4,5},{5,4},{6,7},{7,6},{8,9},{9,8},{10,11... | collective-permute-start | bytes 835592 | tf_op jit(solution)/shard_map/gather_first_2/ppermute | solution.py:171
  96.6 5.0 %collective-permute-done.22.far_ref = bf16[256,2176]{1,0:T(8,128)(2,1)S(1)} collective-permute-done((bf16[256,2176]{1,0:T(8,128)(2,1)S(1)}, bf16[256,2176]{1,0:T(8,128)(2,1)S(1)}, u32[]{:S(2)}, u32[]{:S(2)}) %collective-permute-start.22) | collective-permute-done | bytes 1114144 | tf_op jit(solution)/shard_map/gather_second_1/ppermute | solution.py:171
  101.8 2.5 %collective-permute-start.35 = (bf16[128,2176]{1,0:T(8,128)(2,1)S(1)}, bf16[128,2176]{1,0:T(8,128)(2,1)S(1)}, u32[]{:S(2)}, u32[]{:S(2)}) collective-permute-start(bf16[128,2176]{1,0:T(8,128)(2,1)S(1)} %constant_dynamic-update-slice_fusion.6.near_ref), channel_id=1, source_target_pairs={{0,2},{1,3},{2,0},{3,1},{4,6},{5,7},{6,4},{7,5},{8,10},{9,11},{10,... | collective-permute-start | bytes 1671176 | tf_op jit(solution)/shard_map/gather_second_2/ppermute | solution.py:171
  104.6 3.2 %shard_map.146 = (bf16[4,64,1024]{2,1,0:T(8,128)(2,1)S(1)}, bf16[4,64,1024]{2,1,0:T(8,128)(2,1)S(1)}) custom-call(s32[2]{0:T(128)S(1)} %pad_add_fusion.place_ref, bf16[256,2176]{1,0:T(8,128)(2,1)S(1)} %constant_dynamic-update-slice_fusion.4.near_ref, bf16[256,2176]{1,0:T(8,128)(2,1)S(1)} %collective-permute-done.22.far_ref, bf16[704,2048]{1,0:T(8,128)(2,1)S(1)} %bitcast.97, ...), custom_call_target="tpu_custom_call" | custom-call | flops 2214592512 | bytes 11927552 | tf_op jit(solution)/shard_map/pallas_call | solution.py:142
  107.9 3.2 %shard_map.147 = (bf16[4,64,1024]{2,1,0:T(8,128)(2,1)S(1)}, bf16[4,64,1024]{2,1,0:T(8,128)(2,1)S(1)}) custom-call(s32[2]{0:T(128)S(1)} %pad_add_fusion.place_ref, bf16[256,2176]{1,0:T(8,128)(2,1)S(1)} %collective-permute-done.23.near_ref, bf16[256,2176]{1,0:T(8,128)(2,1)S(1)} %collective-permute-done.24.far_ref, bf16[704,2048]{1,0:T(8,128)(2,1)S(1)} %bitcast.98, ...), custom_call_target="tpu_custom_call" | custom-call | flops 2214592512 | bytes 11927552 | tf_op jit(solution)/shard_map/pallas_call | solution.py:142
  116.0 3.4 %shard_map.148 = (bf16[4,64,1024]{2,1,0:T(8,128)(2,1)S(1)}, bf16[4,64,1024]{2,1,0:T(8,128)(2,1)S(1)}) custom-call(s32[2]{0:T(128)S(1)} %pad_add_fusion.place_ref, bf16[256,2176]{1,0:T(8,128)(2,1)S(1)} %constant_dynamic-update-slice_fusion.4.near_ref, bf16[256,2176]{1,0:T(8,128)(2,1)S(1)} %collective-permute-done.22.far_ref, bf16[704,2048]{1,0:T(8,128)(2,1)S(1)} %bitcast.99, ...), custom_call_target="tpu_custom_call" | custom-call | flops 2214592512 | bytes 11927552 | tf_op jit(solution)/shard_map/pallas_call | solution.py:142
  119.5 3.2 %shard_map.149 = (bf16[4,64,1024]{2,1,0:T(8,128)(2,1)S(1)}, bf16[4,64,1024]{2,1,0:T(8,128)(2,1)S(1)}) custom-call(s32[2]{0:T(128)S(1)} %pad_add_fusion.place_ref, bf16[256,2176]{1,0:T(8,128)(2,1)S(1)} %collective-permute-done.23.near_ref, bf16[256,2176]{1,0:T(8,128)(2,1)S(1)} %collective-permute-done.24.far_ref, bf16[704,2048]{1,0:T(8,128)(2,1)S(1)} %bitcast.100, ...), custom_call_target="tpu_custom_call" | custom-call | flops 2214592512 | bytes 11927552 | tf_op jit(solution)/shard_map/pallas_call | solution.py:142
  123.3 3.3 %collective-permute-done.27 = bf16[2,2,64,1024]{3,2,1,0:T(8,128)(2,1)S(1)} collective-permute-done((bf16[2,2,64,1024]{3,2,1,0:T(8,128)(2,1)S(1)}, bf16[2,2,64,1024]{3,2,1,0:T(8,128)(2,1)S(1)}, u32[]{:S(2)}, u32[]{:S(2)}) %collective-permute-start.27) | collective-permute-done | bytes 524320 | tf_op jit(solution)/shard_map/scatter_second_1/ppermute | solution.py:171
  129.1 3.2 %shard_map.150 = (bf16[4,64,1024]{2,1,0:T(8,128)(2,1)S(1)}, bf16[4,64,1024]{2,1,0:T(8,128)(2,1)S(1)}) custom-call(s32[2]{0:T(128)S(1)} %pad_add_fusion.place_ref, bf16[128,2176]{1,0:T(8,128)(2,1)S(1)} %constant_dynamic-update-slice_fusion.6.near_ref, bf16[128,2176]{1,0:T(8,128)(2,1)S(1)} %collective-permute-done.35.far_ref, bf16[704,2048]{1,0:T(8,128)(2,1)S(1)} %bitcast.101, ...), custom_call_target="tpu_custom_call" | custom-call | flops 2214592512 | bytes 10813440 | tf_op jit(solution)/shard_map/pallas_call | solution.py:142
  132.3 3.2 %shard_map.151 = (bf16[4,64,1024]{2,1,0:T(8,128)(2,1)S(1)}, bf16[4,64,1024]{2,1,0:T(8,128)(2,1)S(1)}) custom-call(s32[2]{0:T(128)S(1)} %pad_add_fusion.place_ref, bf16[128,2176]{1,0:T(8,128)(2,1)S(1)} %collective-permute-done.36.near_ref, bf16[128,2176]{1,0:T(8,128)(2,1)S(1)} %collective-permute-done.37.far_ref, bf16[704,2048]{1,0:T(8,128)(2,1)S(1)} %bitcast.102, ...), custom_call_target="tpu_custom_call" | custom-call | flops 2214592512 | bytes 10813440 | tf_op jit(solution)/shard_map/pallas_call | solution.py:142
  139.5 1.7 collective-permute-start.21
  141.2 2.3 %collective-permute-done.28 = bf16[2,64,1024]{2,1,0:T(8,128)(2,1)S(1)} collective-permute-done((bf16[2,64,1024]{2,1,0:T(8,128)(2,1)S(1)}, bf16[2,64,1024]{2,1,0:T(8,128)(2,1)S(1)}, u32[]{:S(2)}, u32[]{:S(2)}) %collective-permute-start.28) | collective-permute-done | bytes 262176 | tf_op jit(solution)/shard_map/scatter_first_1/ppermute | solution.py:171
  144.1 9.1 %collective-permute-done.40 = bf16[2,2,64,1024]{3,2,1,0:T(8,128)(2,1)S(1)} collective-permute-done((bf16[2,2,64,1024]{3,2,1,0:T(8,128)(2,1)S(1)}, bf16[2,2,64,1024]{3,2,1,0:T(8,128)(2,1)S(1)}, u32[]{:S(2)}, u32[]{:S(2)}) %collective-permute-start.40) | collective-permute-done | bytes 524320 | tf_op jit(solution)/shard_map/scatter_second_2/ppermute | solution.py:171
  156.3 3.5 %collective-permute-done.41 = bf16[2,64,1024]{2,1,0:T(8,128)(2,1)S(1)} collective-permute-done((bf16[2,64,1024]{2,1,0:T(8,128)(2,1)S(1)}, bf16[2,64,1024]{2,1,0:T(8,128)(2,1)S(1)}, u32[]{:S(2)}, u32[]{:S(2)}) %collective-permute-start.41) | collective-permute-done | bytes 262176 | tf_op jit(solution)/shard_map/scatter_first_2/ppermute | solution.py:171
  162.4 10.8 %collective-permute-done.42 = bf16[128,1024]{1,0:T(8,128)(2,1)S(1)} collective-permute-done((bf16[128,1024]{1,0:T(8,128)(2,1)}, bf16[128,1024]{1,0:T(8,128)(2,1)S(1)}, u32[]{:S(2)}, u32[]{:S(2)}) %collective-permute-start.42) | collective-permute-done | bytes 262176 | tf_op jit(solution)/shard_map/to_plane_2/ppermute | solution.py:41
  (157 shorter events, 44.1 us)
Async XLA Ops:
  4.5 11.6 %collective-permute-start = (bf16[128,1024]{1,0:T(8,128)(2,1)S(1)}, bf16[128,1024]{1,0:T(8,128)(2,1)S(1)}, u32[]{:S(2)}, u32[]{:S(2)}) collective-permute-start(bf16[128,1024]{1,0:T(8,128)(2,1)S(1)} %get-tuple-element.43.rest_0_), channel_id=1, source_target_pairs={{0,4},{1,5},{2,6},{3,7},{4,8},{5,9},{6,10},{7,11},{8,12},{9,13},{1... | collective-permute-start | bytes 786440 | tf_op jit(solution)/shard_map/ppermute | solution.py:27
  9.4 11.9 %collective-permute-start.4 = (bf16[128,1024]{1,0:T(8,128)(2,1)}, bf16[128,1024]{1,0:T(8,128)(2,1)S(1)}, u32[]{:S(2)}, u32[]{:S(2)}) collective-permute-start(bf16[128,1024]{1,0:T(8,128)(2,1)} %rest_0_), channel_id=1, source_target_pairs={{0,4},{1,5},{2,6},{3,7},{4,8},{5,9},{6,10},{7,11},{8,12},{9,13},{1... | collective-permute-start | bytes 786440 | tf_op jit(solution)/shard_map/ppermute | solution.py:27
  16.9 8.9 %collective-permute-start.1 = (bf16[128,1024]{1,0:T(8,128)(2,1)S(1)}, bf16[128,1024]{1,0:T(8,128)(2,1)S(1)}, u32[]{:S(2)}, u32[]{:S(2)}) collective-permute-start(bf16[128,1024]{1,0:T(8,128)(2,1)S(1)} %get-tuple-element.101), channel_id=1, source_target_pairs={{0,1},{1,0},{2,3},{3,2},{4,5},{5,4},{6,7},{7,6},{8,9},{9,8},{10,11... | collective-permute-start | bytes 786440 | tf_op jit(solution)/shard_map/ppermute | solution.py:22
  19.3 13.8 %collective-permute-start.2 = (bf16[128,1024]{1,0:T(8,128)(2,1)}, bf16[128,1024]{1,0:T(8,128)(2,1)S(1)}, u32[]{:S(2)}, u32[]{:S(2)}) collective-permute-start(bf16[128,1024]{1,0:T(8,128)(2,1)} %get-tuple-element.100), channel_id=1, source_target_pairs={{0,2},{1,3},{2,0},{3,1},{4,6},{5,7},{6,4},{7,5},{8,10},{9,11},{10,... | collective-permute-start | bytes 786440 | tf_op jit(solution)/shard_map/ppermute | solution.py:22
  20.8 12.3 %collective-permute-start.3 = (bf16[128,1024]{1,0:T(8,128)(2,1)}, bf16[128,1024]{1,0:T(8,128)(2,1)S(1)}, u32[]{:S(2)}, u32[]{:S(2)}) collective-permute-start(bf16[128,1024]{1,0:T(8,128)(2,1)} %get-tuple-element.99), channel_id=1, source_target_pairs={{0,3},{1,2},{2,1},{3,0},{4,7},{5,6},{6,5},{7,4},{8,11},{9,10},{10,... | collective-permute-start | bytes 786440 | tf_op jit(solution)/shard_map/ppermute | solution.py:22
  22.3 14.8 %collective-permute-start.5 = (bf16[128,1024]{1,0:T(8,128)(2,1)}, bf16[128,1024]{1,0:T(8,128)(2,1)S(1)}, u32[]{:S(2)}, u32[]{:S(2)}) collective-permute-start(bf16[128,1024]{1,0:T(8,128)(2,1)} %get-tuple-element.98), channel_id=1, source_target_pairs={{0,1},{1,0},{2,3},{3,2},{4,5},{5,4},{6,7},{7,6},{8,9},{9,8},{10,11... | collective-permute-start | bytes 786440 | tf_op jit(solution)/shard_map/ppermute | solution.py:22
  23.8 18.3 %collective-permute-start.6 = (bf16[128,1024]{1,0:T(8,128)(2,1)}, bf16[128,1024]{1,0:T(8,128)(2,1)S(1)}, u32[]{:S(2)}, u32[]{:S(2)}) collective-permute-start(bf16[128,1024]{1,0:T(8,128)(2,1)} %get-tuple-element.97), channel_id=1, source_target_pairs={{0,2},{1,3},{2,0},{3,1},{4,6},{5,7},{6,4},{7,5},{8,10},{9,11},{10,... | collective-permute-start | bytes 786440 | tf_op jit(solution)/shard_map/ppermute | solution.py:22
  25.8 16.3 %collective-permute-start.7 = (bf16[128,1024]{1,0:T(8,128)(2,1)}, bf16[128,1024]{1,0:T(8,128)(2,1)S(1)}, u32[]{:S(2)}, u32[]{:S(2)}) collective-permute-start(bf16[128,1024]{1,0:T(8,128)(2,1)} %get-tuple-element.96), channel_id=1, source_target_pairs={{0,3},{1,2},{2,1},{3,0},{4,7},{5,6},{6,5},{7,4},{8,11},{9,10},{10,... | collective-permute-start | bytes 786440 | tf_op jit(solution)/shard_map/ppermute | solution.py:22
  49.5 12.2 %collective-permute-start.9 = (bf16[64,2176]{1,0:T(8,128)(2,1)S(1)}, bf16[64,2176]{1,0:T(8,128)(2,1)S(1)}, u32[]{:S(2)}, u32[]{:S(2)}) collective-permute-start(bf16[64,2176]{1,0:T(8,128)(2,1)S(1)} %get-tuple-element.54), channel_id=1, source_target_pairs={{0,1},{1,0},{2,3},{3,2},{4,5},{5,4},{6,7},{7,6},{8,9},{9,8},{10,11... | collective-permute-start | bytes 835592 | tf_op jit(solution)/shard_map/gather_first_0/ppermute | solution.py:171
  50.1 11.6 %collective-permute-start.15 = (bf16[64,2176]{1,0:T(8,128)(2,1)S(1)}, bf16[64,2176]{1,0:T(8,128)(2,1)S(1)}, u32[]{:S(2)}, u32[]{:S(2)}) collective-permute-start(bf16[64,2176]{1,0:T(8,128)(2,1)S(1)} %get-tuple-element.54), channel_id=1, source_target_pairs={{4,0},{5,1},{6,2},{7,3},{8,4},{9,5},{10,6},{11,7},{12,8},{13,9},{1... | collective-permute-start | bytes 835592 | tf_op jit(solution)/shard_map/from_plane_1/ppermute | solution.py:33
  54.6 13.8 %collective-permute-start.16 = (bf16[64,2176]{1,0:T(8,128)(2,1)S(1)}, bf16[64,2176]{1,0:T(8,128)(2,1)S(1)}, u32[]{:S(2)}, u32[]{:S(2)}) collective-permute-start(bf16[64,2176]{1,0:T(8,128)(2,1)S(1)} %get-tuple-element.54), channel_id=1, source_target_pairs={{12,0},{13,1},{14,2},{15,3},{0,4},{1,5},{2,6},{3,7},{4,8},{5,9},{6... | collective-permute-start | bytes 835592 | tf_op jit(solution)/shard_map/from_plane_3/ppermute | solution.py:33
  68.4 14.7 %collective-permute-start.18 = (bf16[128,2176]{1,0:T(8,128)(2,1)S(1)}, bf16[128,2176]{1,0:T(8,128)(2,1)S(1)}, u32[]{:S(2)}, u32[]{:S(2)}) collective-permute-start(bf16[128,2176]{1,0:T(8,128)(2,1)S(1)} %constant_dynamic-update-slice_fusion.2), channel_id=1, source_target_pairs={{0,1},{1,0},{2,3},{3,2},{4,5},{5,4},{6,7},{7,6},{8,9},{9,8},{10,11... | collective-permute-start | bytes 1671176 | tf_op jit(solution)/shard_map/gather_first_1/ppermute | solution.py:171
  69.0 15.0 %collective-permute-start.10 = (bf16[128,2176]{1,0:T(8,128)(2,1)S(1)}, bf16[128,2176]{1,0:T(8,128)(2,1)S(1)}, u32[]{:S(2)}, u32[]{:S(2)}) collective-permute-start(bf16[128,2176]{1,0:T(8,128)(2,1)S(1)} %constant_dynamic-update-slice_fusion.near_ref), channel_id=1, source_target_pairs={{0,2},{1,3},{2,0},{3,1},{4,6},{5,7},{6,4},{7,5},{8,10},{9,11},{10,... | collective-permute-start | bytes 1671176 | tf_op jit(solution)/shard_map/gather_second_0/ppermute | solution.py:171
  69.5 14.5 %collective-permute-start.17 = (bf16[64,2176]{1,0:T(8,128)(2,1)S(1)}, bf16[64,2176]{1,0:T(8,128)(2,1)S(1)}, u32[]{:S(2)}, u32[]{:S(2)}) collective-permute-start(bf16[64,2176]{1,0:T(8,128)(2,1)S(1)} %get-tuple-element.54), channel_id=1, source_target_pairs={{8,0},{9,1},{10,2},{11,3},{12,4},{13,5},{14,6},{15,7},{0,8},{1,9},... | collective-permute-start | bytes 835592 | tf_op jit(solution)/shard_map/from_plane_2/ppermute | solution.py:33
  84.1 17.5 %collective-permute-start.22 = (bf16[256,2176]{1,0:T(8,128)(2,1)S(1)}, bf16[256,2176]{1,0:T(8,128)(2,1)S(1)}, u32[]{:S(2)}, u32[]{:S(2)}) collective-permute-start(bf16[256,2176]{1,0:T(8,128)(2,1)S(1)} %constant_dynamic-update-slice_fusion.4.near_ref), channel_id=1, source_target_pairs={{0,2},{1,3},{2,0},{3,1},{4,6},{5,7},{6,4},{7,5},{8,10},{9,11},{10,... | collective-permute-start | bytes 3342344 | tf_op jit(solution)/shard_map/gather_second_1/ppermute | solution.py:171
  89.5 18.4 %collective-permute-start.23 = (bf16[256,2176]{1,0:T(8,128)(2,1)S(1)}, bf16[256,2176]{1,0:T(8,128)(2,1)S(1)}, u32[]{:S(2)}, u32[]{:S(2)}) collective-permute-start(bf16[256,2176]{1,0:T(8,128)(2,1)S(1)} %constant_dynamic-update-slice_fusion.4.near_ref), channel_id=1, source_target_pairs={{16,0},{0,16},{17,1},{1,17},{18,2},{2,18},{19,3},{3,19},{20,4},{4,... | collective-permute-start | bytes 3342344 | tf_op jit(solution)/shard_map/ppermute | solution.py:48
  94.6 9.8 %collective-permute-start.13 = (bf16[4,64,1024]{2,1,0:T(8,128)(2,1)S(1)}, bf16[4,64,1024]{2,1,0:T(8,128)(2,1)S(1)}, u32[]{:S(2)}, u32[]{:S(2)}) collective-permute-start(bf16[4,64,1024]{2,1,0:T(8,128)(2,1)S(1)} %get-tuple-element.51), channel_id=1, source_target_pairs={{16,0},{0,16},{17,1},{1,17},{18,2},{2,18},{19,3},{3,19},{20,4},{4,... | collective-permute-start | bytes 1572872 | tf_op jit(solution)/shard_map/ppermute | solution.py:48
  94.8 7.0 %collective-permute-start.19 = (bf16[64,2176]{1,0:T(8,128)(2,1)S(1)}, bf16[64,2176]{1,0:T(8,128)(2,1)S(1)}, u32[]{:S(2)}, u32[]{:S(2)}) collective-permute-start(bf16[64,2176]{1,0:T(8,128)(2,1)S(1)} %collective-permute-done.17), channel_id=1, source_target_pairs={{0,1},{1,0},{2,3},{3,2},{4,5},{5,4},{6,7},{7,6},{8,9},{9,8},{10,11... | collective-permute-start | bytes 835592 | tf_op jit(solution)/shard_map/gather_first_2/ppermute | solution.py:171
  101.8 13.7 %collective-permute-start.35 = (bf16[128,2176]{1,0:T(8,128)(2,1)S(1)}, bf16[128,2176]{1,0:T(8,128)(2,1)S(1)}, u32[]{:S(2)}, u32[]{:S(2)}) collective-permute-start(bf16[128,2176]{1,0:T(8,128)(2,1)S(1)} %constant_dynamic-update-slice_fusion.6.near_ref), channel_id=1, source_target_pairs={{0,2},{1,3},{2,0},{3,1},{4,6},{5,7},{6,4},{7,5},{8,10},{9,11},{10,... | collective-permute-start | bytes 1671176 | tf_op jit(solution)/shard_map/gather_second_2/ppermute | solution.py:171
  111.8 11.0 %collective-permute-start.20 = (bf16[2,2,64,1024]{3,2,1,0:T(8,128)(2,1)S(1)}, bf16[2,2,64,1024]{3,2,1,0:T(8,128)(2,1)S(1)}, u32[]{:S(2)}, u32[]{:S(2)}) collective-permute-start(bf16[2,2,64,1024]{3,2,1,0:T(8,128)(2,1)S(1)} %pad_maximum_fusion.1), channel_id=1, source_target_pairs={{0,2},{1,3},{2,0},{3,1},{4,6},{5,7},{6,4},{7,5},{8,10},{9,11},{10,... | collective-permute-start | bytes 1572872 | tf_op jit(solution)/shard_map/scatter_second_0/ppermute | solution.py:171
  113.9 12.7 %collective-permute-start.27 = (bf16[2,2,64,1024]{3,2,1,0:T(8,128)(2,1)S(1)}, bf16[2,2,64,1024]{3,2,1,0:T(8,128)(2,1)S(1)}, u32[]{:S(2)}, u32[]{:S(2)}) collective-permute-start(bf16[2,2,64,1024]{3,2,1,0:T(8,128)(2,1)S(1)} %pad_maximum_fusion.2), channel_id=1, source_target_pairs={{0,2},{1,3},{2,0},{3,1},{4,6},{5,7},{6,4},{7,5},{8,10},{9,11},{10,... | collective-permute-start | bytes 1572872 | tf_op jit(solution)/shard_map/scatter_second_1/ppermute | solution.py:171
  115.5 16.8 %collective-permute-start.36 = (bf16[128,2176]{1,0:T(8,128)(2,1)S(1)}, bf16[128,2176]{1,0:T(8,128)(2,1)S(1)}, u32[]{:S(2)}, u32[]{:S(2)}) collective-permute-start(bf16[128,2176]{1,0:T(8,128)(2,1)S(1)} %constant_dynamic-update-slice_fusion.6.near_ref), channel_id=1, source_target_pairs={{16,0},{0,16},{17,1},{1,17},{18,2},{2,18},{19,3},{3,19},{20,4},{4,... | collective-permute-start | bytes 1671176 | tf_op jit(solution)/shard_map/ppermute | solution.py:48
  115.5 16.8 %collective-permute-start.37 = (bf16[128,2176]{1,0:T(8,128)(2,1)S(1)}, bf16[128,2176]{1,0:T(8,128)(2,1)S(1)}, u32[]{:S(2)}, u32[]{:S(2)}) collective-permute-start(bf16[128,2176]{1,0:T(8,128)(2,1)S(1)} %collective-permute-done.35.far_ref), channel_id=1, source_target_pairs={{16,0},{0,16},{17,1},{1,17},{18,2},{2,18},{19,3},{3,19},{20,4},{4,... | collective-permute-start | bytes 1671176 | tf_op jit(solution)/shard_map/ppermute | solution.py:48
  119.5 7.5 %collective-permute-start.31 = (bf16[4,64,1024]{2,1,0:T(8,128)(2,1)S(1)}, bf16[4,64,1024]{2,1,0:T(8,128)(2,1)S(1)}, u32[]{:S(2)}, u32[]{:S(2)}) collective-permute-start(bf16[4,64,1024]{2,1,0:T(8,128)(2,1)S(1)} %get-tuple-element.68), channel_id=1, source_target_pairs={{16,0},{0,16},{17,1},{1,17},{18,2},{2,18},{19,3},{3,19},{20,4},{4,... | collective-permute-start | bytes 1572872 | tf_op jit(solution)/shard_map/ppermute | solution.py:48
  127.5 9.2 %collective-permute-start.32 = (bf16[2,2,64,1024]{3,2,1,0:T(8,128)(2,1)S(1)}, bf16[2,2,64,1024]{3,2,1,0:T(8,128)(2,1)S(1)}, u32[]{:S(2)}, u32[]{:S(2)}) collective-permute-start(bf16[2,2,64,1024]{3,2,1,0:T(8,128)(2,1)S(1)} %pad_maximum_fusion.3), channel_id=1, source_target_pairs={{0,2},{1,3},{2,0},{3,1},{4,6},{5,7},{6,4},{7,5},{8,10},{9,11},{10,... | collective-permute-start | bytes 1572872 | tf_op jit(solution)/shard_map/scatter_second_3/ppermute | solution.py:171
  136.1 7.4 %collective-permute-start.28 = (bf16[2,64,1024]{2,1,0:T(8,128)(2,1)S(1)}, bf16[2,64,1024]{2,1,0:T(8,128)(2,1)S(1)}, u32[]{:S(2)}, u32[]{:S(2)}) collective-permute-start(bf16[2,64,1024]{2,1,0:T(8,128)(2,1)S(1)} %pad_maximum_fusion.6), channel_id=1, source_target_pairs={{0,1},{1,0},{2,3},{3,2},{4,5},{5,4},{6,7},{7,6},{8,9},{9,8},{10,11... | collective-permute-start | bytes 786440 | tf_op jit(solution)/shard_map/scatter_first_1/ppermute | solution.py:171
  138.6 14.6 %collective-permute-start.40 = (bf16[2,2,64,1024]{3,2,1,0:T(8,128)(2,1)S(1)}, bf16[2,2,64,1024]{3,2,1,0:T(8,128)(2,1)S(1)}, u32[]{:S(2)}, u32[]{:S(2)}) collective-permute-start(bf16[2,2,64,1024]{3,2,1,0:T(8,128)(2,1)S(1)} %pad_maximum_fusion.4), channel_id=1, source_target_pairs={{0,2},{1,3},{2,0},{3,1},{4,6},{5,7},{6,4},{7,5},{8,10},{9,11},{10,... | collective-permute-start | bytes 1572872 | tf_op jit(solution)/shard_map/scatter_second_2/ppermute | solution.py:171
  139.5 22.5 %collective-permute-start.21 = (bf16[2,64,1024]{2,1,0:T(8,128)(2,1)S(1)}, bf16[2,64,1024]{2,1,0:T(8,128)(2,1)S(1)}, u32[]{:S(2)}, u32[]{:S(2)}) collective-permute-start(bf16[2,64,1024]{2,1,0:T(8,128)(2,1)S(1)} %pad_maximum_fusion.5), channel_id=1, source_target_pairs={{0,1},{1,0},{2,3},{3,2},{4,5},{5,4},{6,7},{7,6},{8,9},{9,8},{10,11... | collective-permute-start | bytes 786440 | tf_op jit(solution)/shard_map/scatter_first_0/ppermute | solution.py:171
  143.6 18.4 %collective-permute-start.29 = (bf16[128,1024]{1,0:T(8,128)(2,1)S(1)}, bf16[128,1024]{1,0:T(8,128)(2,1)S(1)}, u32[]{:S(2)}, u32[]{:S(2)}) collective-permute-start(bf16[128,1024]{1,0:T(8,128)(2,1)S(1)} %pad_maximum_fusion.7), channel_id=1, source_target_pairs={{0,4},{1,5},{2,6},{3,7},{4,8},{5,9},{6,10},{7,11},{8,12},{9,13},{1... | collective-permute-start | bytes 786440 | tf_op jit(solution)/shard_map/to_plane_1/ppermute | solution.py:41
  143.7 10.4 %collective-permute-start.33 = (bf16[2,64,1024]{2,1,0:T(8,128)(2,1)S(1)}, bf16[2,64,1024]{2,1,0:T(8,128)(2,1)S(1)}, u32[]{:S(2)}, u32[]{:S(2)}) collective-permute-start(bf16[2,64,1024]{2,1,0:T(8,128)(2,1)S(1)} %pad_maximum_fusion.8), channel_id=1, source_target_pairs={{0,1},{1,0},{2,3},{3,2},{4,5},{5,4},{6,7},{7,6},{8,9},{9,8},{10,11... | collective-permute-start | bytes 786440 | tf_op jit(solution)/shard_map/scatter_first_3/ppermute | solution.py:171
  154.9 7.5 %collective-permute-start.34 = (bf16[128,1024]{1,0:T(8,128)(2,1)}, bf16[128,1024]{1,0:T(8,128)(2,1)S(1)}, u32[]{:S(2)}, u32[]{:S(2)}) collective-permute-start(bf16[128,1024]{1,0:T(8,128)(2,1)} %pad_maximum_fusion.9), channel_id=1, source_target_pairs={{0,12},{1,13},{2,14},{3,15},{4,0},{5,1},{6,2},{7,3},{8,4},{9,5},{1... | collective-permute-start | bytes 786440 | tf_op jit(solution)/shard_map/to_plane_3/ppermute | solution.py:41
  160.7 12.5 %collective-permute-start.42 = (bf16[128,1024]{1,0:T(8,128)(2,1)}, bf16[128,1024]{1,0:T(8,128)(2,1)S(1)}, u32[]{:S(2)}, u32[]{:S(2)}) collective-permute-start(bf16[128,1024]{1,0:T(8,128)(2,1)} %pad_maximum_fusion.11), channel_id=1, source_target_pairs={{0,8},{1,9},{2,10},{3,11},{4,12},{5,13},{6,14},{7,15},{8,0},{9,1},... | collective-permute-start | bytes 786440 | tf_op jit(solution)/shard_map/to_plane_2/ppermute | solution.py:41
  (23 other events, 210.4 us)

commit v13 on v12

--- a/solution.py
+++ b/solution.py
@@ -348,14 +348,14 @@
         sent = after(payload, columns[-1])
     for number, column in enumerate(columns):
         if number > 0:
-            column = after(column, nears[-1])
+            column = after(column, nears[-1], fars[0])
         if number == 2:
             outs = run(rows=rows[0], planes=1, plane=0, span=1, waits={})
             column = after(column, outs)
         nears.append(
             jnp.concatenate([column, crossed(column, True, f"gather_first_{number}")])
         )
-        ready = after(nears[-1], fars[0], columns[2]) if number == 1 else nears[-1]
+        ready = after(nears[-1], columns[2]) if number == 1 else nears[-1]
         fars.append(crossed(ready, False, f"gather_second_{number}"))
         rows.append(
             [
@@ -367,8 +367,7 @@
     sent = after(second_share(own_totals), nears[-1])
     own_second = crossed(sent, False, "scatter_second_0")
     own_totals = merged(own_totals, own_second, 2)
-    own_got = crossed(first_share(own_totals), True, "scatter_first_0")
-    seconds, firsts, returned = [], [], []
+    seconds, firsts, flips, returned = [], [], [], []
     span_of = 1 if planes <= 4 else 8
     steps = [
         (number, plane, group[plane : plane + span_of])
@@ -377,7 +376,7 @@
     ]
     for number, plane, aheads in steps[1:]:
         waits = {0: [outs], cores - 1: [*seconds[-1:]]}
-        if len(seconds) == 2:
+        if len(seconds) > 1:
             waits[0].append(own_second)
         outs = run(
             rows=rows[number],
@@ -386,16 +385,21 @@
             span=len(aheads),
             waits=waits,
         )
-        totals = core_totals(outs, cores, *firsts[-1:])
+        totals = core_totals(outs, cores, *firsts[-1:], *flips[-2:-1])
         seconds.append(second_share(totals))
         got = crossed(seconds[-1], False, f"scatter_second_{aheads[0]}")
         totals = merged(totals, got, 2)
         firsts.append(first_share(totals))
         got = crossed(firsts[-1], True, f"scatter_first_{aheads[0]}")
         rows_of = merged([total[0] for total in totals], got, None)
+        blocks = []
         for i, ahead in enumerate(aheads):
             piece = [part[i * part_rows : (i + 1) * part_rows] for part in rows_of]
-            returned.append(to_plane(narrow(jnp.concatenate(piece)), ahead))
+            blocks.append(narrow(jnp.concatenate(piece)))
+            returned.append(to_plane(blocks[-1], ahead))
+        flips.append(blocks)
+    own_first = after(first_share(own_totals), *flips[-2:-1])
+    own_got = crossed(own_first, True, "scatter_first_0")
     moe = jnp.concatenate(merged([total[0] for total in own_totals], own_got, None))
     moe = moe + sum(wide(block) for block in returned)
     moe = jnp.roll(moe.reshape(cores, part_rows, col_width), tok_index, axis=0)

time: 174 us -> 172 us (0.989)
  starting transfers between devices: 44.3 us -> 41 us
    ppermute x14, starting transfers between devices: 16.2 us -> 13.5 us  [crossed(): return lax.ppermute(block, ('tok', 'blk'), route)]
    ppermute x3, waiting for transfers between devices: 14.6 us -> 16.5 us  [from_plane(): lax.ppermute(block, 'blk', [((i + PLANE * ahead) % count, i) for i in ran...]
  transfers between devices with their start and end apart: 43 -> 43, of which waited for: 21 -> 21; matrix products, arithmetic and copies ran while one was open for 7% -> 6% of each run, Pallas kernels for 16% -> 16%
where the time goes in v13:
time: 172 us
  waiting for transfers between devices  81 us (47%)
  starting transfers between devices  41 us (24%)
  Pallas kernels  31.4 us (18%)
  local copies, waits for them, and re-layouts  8.71 us (5%)
  other arithmetic  8.59 us (5%)
    ppermute x14, waiting for transfers between devices, crossed(): return lax.ppermute(block, ('tok', 'blk'), route)  36.4 us
    pallas_call x12, Pallas kernels, local_call(): pl.pallas_call(body, in_specs=[scalar] * len(scalars) + [whole] * len(arr...  31.4 us
    ppermute x3, waiting for transfers between devices, from_plane(): lax.ppermute(block, 'blk', [((i + PLANE * ahead) % count, i) for i in ran...  16.5 us
    ppermute x14, starting transfers between devices, crossed(): return lax.ppermute(block, ('tok', 'blk'), route)  13.5 us
    ppermute x6, waiting for transfers between devices, flipped(): lax.ppermute(block, 'blk', [(i, i ^ mask) for i in range(lax.axis_size('b...  10.1 us
    ppermute x3, waiting for transfers between devices, to_plane(): lax.ppermute(block, 'blk', [(i, (i + PLANE * ahead) % count) for i in ran...  9.99 us
    ppermute x6, starting transfers between devices, flipped(): lax.ppermute(block, 'blk', [(i, i ^ mask) for i in range(lax.axis_size('b...  9.31 us
    ppermute x2, starting transfers between devices, next_plane(): lax.ppermute(block, 'blk', [(i, i + PLANE) for i in range(count - PLANE)])  8.43 us
  transfers between devices with their start and end apart: 43, of which 21 were waited for; matrix products, arithmetic and copies ran while one was open for 6% of the time, Pallas kernels for 16%

profile of v13, /device:TPU:0, one launch (start us, length us, event | category | flops | bytes accessed | tf_op | source)
XLA Modules:
  0.0 172.1 jit_solution(13222126488437603176)
XLA Ops:
  4.5 4.9 %collective-permute-start = (bf16[128,1024]{1,0:T(8,128)(2,1)S(1)}, bf16[128,1024]{1,0:T(8,128)(2,1)S(1)}, u32[]{:S(2)}, u32[]{:S(2)}) collective-permute-start(bf16[128,1024]{1,0:T(8,128)(2,1)S(1)} %get-tuple-element.44.rest_0_), channel_id=1, source_target_pairs={{0,4},{1,5},{2,6},{3,7},{4,8},{5,9},{6,10},{7,11},{8,12},{9,13},{1... | collective-permute-start | bytes 786440 | tf_op jit(solution)/shard_map/ppermute | solution.py:27
  9.4 3.5 %collective-permute-start.4 = (bf16[128,1024]{1,0:T(8,128)(2,1)}, bf16[128,1024]{1,0:T(8,128)(2,1)S(1)}, u32[]{:S(2)}, u32[]{:S(2)}) collective-permute-start(bf16[128,1024]{1,0:T(8,128)(2,1)} %rest_0_), channel_id=1, source_target_pairs={{0,4},{1,5},{2,6},{3,7},{4,8},{5,9},{6,10},{7,11},{8,12},{9,13},{1... | collective-permute-start | bytes 786440 | tf_op jit(solution)/shard_map/ppermute | solution.py:27
  13.7 2.4 %collective-permute-done.rest_1_ = bf16[128,1024]{1,0:T(8,128)(2,1)S(1)} collective-permute-done((bf16[128,1024]{1,0:T(8,128)(2,1)S(1)}, bf16[128,1024]{1,0:T(8,128)(2,1)S(1)}, u32[]{:S(2)}, u32[]{:S(2)}) %collective-permute-start) | collective-permute-done | bytes 262176 | tf_op jit(solution)/shard_map/ppermute | solution.py:27
  25.8 2.8 %collective-permute-start.7 = (bf16[128,1024]{1,0:T(8,128)(2,1)}, bf16[128,1024]{1,0:T(8,128)(2,1)S(1)}, u32[]{:S(2)}, u32[]{:S(2)}) collective-permute-start(bf16[128,1024]{1,0:T(8,128)(2,1)} %get-tuple-element.98), channel_id=1, source_target_pairs={{0,3},{1,2},{2,1},{3,0},{4,7},{5,6},{6,5},{7,4},{8,11},{9,10},{10,... | collective-permute-start | bytes 786440 | tf_op jit(solution)/shard_map/ppermute | solution.py:22
  30.7 2.4 %collective-permute-done.2.rest_3_ = bf16[128,1024]{1,0:T(8,128)(2,1)S(1)} collective-permute-done((bf16[128,1024]{1,0:T(8,128)(2,1)}, bf16[128,1024]{1,0:T(8,128)(2,1)S(1)}, u32[]{:S(2)}, u32[]{:S(2)}) %collective-permute-start.2) | collective-permute-done | bytes 262176 | tf_op jit(solution)/shard_map/ppermute | solution.py:22
  33.1 1.9 %shard_map.141.prob_ref = bf16[8,128,640]{2,1,0:T(8,128)(2,1)S(1)} custom-call(s32[2]{0:T(128)S(1)} %pad_add_fusion.place_ref, s32[8]{0:T(128)S(1)} %copy-done.10, bf16[128,1024]{1,0:T(8,128)(2,1)S(1)} %get-tuple-element.43.q_ref, bf16[128,1024]{1,0:T(8,128)(2,1)S(1)} %get-tuple-element.44.rest_0_, bf16[128,1024]{1,0:T(8,128)(2,1)S(1)} %collective-permute-done.rest_1_, ...), custom_call_target="tpu_custom_call" | custom-call | flops 167772160 | bytes 2883584 | tf_op jit(solution)/shard_map/pallas_call | solution.py:142
  35.0 2.1 %collective-permute-done.5.rest_2_ = bf16[128,1024]{1,0:T(8,128)(2,1)S(1)} collective-permute-done((bf16[128,1024]{1,0:T(8,128)(2,1)}, bf16[128,1024]{1,0:T(8,128)(2,1)S(1)}, u32[]{:S(2)}, u32[]{:S(2)}) %collective-permute-start.5) | collective-permute-done | bytes 262176 | tf_op jit(solution)/shard_map/ppermute | solution.py:22
  37.1 5.0 %collective-permute-done.6.rest_3_ = bf16[128,1024]{1,0:T(8,128)(2,1)S(1)} collective-permute-done((bf16[128,1024]{1,0:T(8,128)(2,1)}, bf16[128,1024]{1,0:T(8,128)(2,1)S(1)}, u32[]{:S(2)}, u32[]{:S(2)}) %collective-permute-start.6) | collective-permute-done | bytes 262176 | tf_op jit(solution)/shard_map/ppermute | solution.py:22
  42.1 2.2 %copy-done.3 = bf16[1024,2048]{1,0:T(8,128)(2,1)S(1)} copy-done((bf16[1024,2048]{1,0:T(8,128)(2,1)S(1)}, bf16[1024,2048]{1,0:T(8,128)(2,1)}, u32[]{:S(2)}) %copy-start.3) | copy-done | bytes 4194328
  46.1 2.6 %collective-permute-done.8.rest_1_ = f32[128,2048]{1,0:T(8,128)S(1)} collective-permute-done((f32[128,2048]{1,0:T(8,128)S(1)}, f32[128,2048]{1,0:T(8,128)S(1)}, u32[]{:S(2)}, u32[]{:S(2)}) %collective-permute-start.8) | collective-permute-done | bytes 1048608 | tf_op jit(solution)/shard_map/ppermute | solution.py:48
  50.1 4.5 %collective-permute-start.15 = (bf16[64,2176]{1,0:T(8,128)(2,1)S(1)}, bf16[64,2176]{1,0:T(8,128)(2,1)S(1)}, u32[]{:S(2)}, u32[]{:S(2)}) collective-permute-start(bf16[64,2176]{1,0:T(8,128)(2,1)S(1)} %get-tuple-element.55), channel_id=1, source_target_pairs={{4,0},{5,1},{6,2},{7,3},{8,4},{9,5},{10,6},{11,7},{12,8},{13,9},{1... | collective-permute-start | bytes 835592 | tf_op jit(solution)/shard_map/from_plane_1/ppermute | solution.py:33
  57.7 4.0 %collective-permute-done.15 = bf16[64,2176]{1,0:T(8,128)(2,1)S(1)} collective-permute-done((bf16[64,2176]{1,0:T(8,128)(2,1)S(1)}, bf16[64,2176]{1,0:T(8,128)(2,1)S(1)}, u32[]{:S(2)}, u32[]{:S(2)}) %collective-permute-start.15) | collective-permute-done | bytes 278560 | tf_op jit(solution)/shard_map/from_plane_1/ppermute | solution.py:33
  61.7 6.7 %collective-permute-done.16 = bf16[64,2176]{1,0:T(8,128)(2,1)S(1)} collective-permute-done((bf16[64,2176]{1,0:T(8,128)(2,1)S(1)}, bf16[64,2176]{1,0:T(8,128)(2,1)S(1)}, u32[]{:S(2)}, u32[]{:S(2)}) %collective-permute-start.16) | collective-permute-done | bytes 278560 | tf_op jit(solution)/shard_map/from_plane_3/ppermute | solution.py:33
  69.8 8.2 %collective-permute-done.18 = bf16[128,2176]{1,0:T(8,128)(2,1)S(1)} collective-permute-done((bf16[128,2176]{1,0:T(8,128)(2,1)S(1)}, bf16[128,2176]{1,0:T(8,128)(2,1)S(1)}, u32[]{:S(2)}, u32[]{:S(2)}) %collective-permute-start.18) | collective-permute-done | bytes 557088 | tf_op jit(solution)/shard_map/gather_first_1/ppermute | solution.py:171
  78.1 5.9 %collective-permute-done.17 = bf16[64,2176]{1,0:T(8,128)(2,1)S(1)} collective-permute-done((bf16[64,2176]{1,0:T(8,128)(2,1)S(1)}, bf16[64,2176]{1,0:T(8,128)(2,1)S(1)}, u32[]{:S(2)}, u32[]{:S(2)}) %collective-permute-start.17) | collective-permute-done | bytes 278560 | tf_op jit(solution)/shard_map/from_plane_2/ppermute | solution.py:33
  86.2 3.2 %shard_map.144 = (bf16[4,64,1024]{2,1,0:T(8,128)(2,1)S(1)}, bf16[4,64,1024]{2,1,0:T(8,128)(2,1)S(1)}) custom-call(s32[2]{0:T(128)S(1)} %pad_add_fusion.place_ref, bf16[128,2176]{1,0:T(8,128)(2,1)S(1)} %constant_dynamic-update-slice_fusion.near_ref, bf16[128,2176]{1,0:T(8,128)(2,1)S(1)} %collective-permute-done.10.far_ref, bf16[704,2048]{1,0:T(8,128)(2,1)S(1)} %bitcast.95, ...), custom_call_target="tpu_custom_call" | custom-call | flops 2214592512 | bytes 10813440 | tf_op jit(solution)/shard_map/pallas_call | solution.py:142
  89.5 1.9 %collective-permute-done.14 = bf16[4,64,1024]{2,1,0:T(8,128)(2,1)S(1)} collective-permute-done((bf16[4,64,1024]{2,1,0:T(8,128)(2,1)S(1)}, bf16[4,64,1024]{2,1,0:T(8,128)(2,1)S(1)}, u32[]{:S(2)}, u32[]{:S(2)}) %collective-permute-start.14) | collective-permute-done | bytes 524320 | tf_op jit(solution)/shard_map/ppermute | solution.py:48
  91.5 3.2 %shard_map.145 = (bf16[4,64,1024]{2,1,0:T(8,128)(2,1)S(1)}, bf16[4,64,1024]{2,1,0:T(8,128)(2,1)S(1)}) custom-call(s32[2]{0:T(128)S(1)} %pad_add_fusion.place_ref, bf16[128,2176]{1,0:T(8,128)(2,1)S(1)} %collective-permute-done.11.near_ref, bf16[128,2176]{1,0:T(8,128)(2,1)S(1)} %collective-permute-done.12.far_ref, bf16[704,2048]{1,0:T(8,128)(2,1)S(1)} %bitcast.96, ...), custom_call_target="tpu_custom_call" | custom-call | flops 2214592512 | bytes 10813440 | tf_op jit(solution)/shard_map/pallas_call | solution.py:142
  95.2 6.3 %collective-permute-done.21.far_ref = bf16[256,2176]{1,0:T(8,128)(2,1)S(1)} collective-permute-done((bf16[256,2176]{1,0:T(8,128)(2,1)S(1)}, bf16[256,2176]{1,0:T(8,128)(2,1)S(1)}, u32[]{:S(2)}, u32[]{:S(2)}) %collective-permute-start.21) | collective-permute-done | bytes 1114144 | tf_op jit(solution)/shard_map/gather_second_1/ppermute | solution.py:171
  102.4 2.4 %collective-permute-start.35 = (bf16[128,2176]{1,0:T(8,128)(2,1)S(1)}, bf16[128,2176]{1,0:T(8,128)(2,1)S(1)}, u32[]{:S(2)}, u32[]{:S(2)}) collective-permute-start(bf16[128,2176]{1,0:T(8,128)(2,1)S(1)} %constant_dynamic-update-slice_fusion.6.near_ref), channel_id=1, source_target_pairs={{0,2},{1,3},{2,0},{3,1},{4,6},{5,7},{6,4},{7,5},{8,10},{9,11},{10,... | collective-permute-start | bytes 1671176 | tf_op jit(solution)/shard_map/gather_second_2/ppermute | solution.py:171
  105.0 3.2 %shard_map.146 = (bf16[4,64,1024]{2,1,0:T(8,128)(2,1)S(1)}, bf16[4,64,1024]{2,1,0:T(8,128)(2,1)S(1)}) custom-call(s32[2]{0:T(128)S(1)} %pad_add_fusion.place_ref, bf16[256,2176]{1,0:T(8,128)(2,1)S(1)} %constant_dynamic-update-slice_fusion.4.near_ref, bf16[256,2176]{1,0:T(8,128)(2,1)S(1)} %collective-permute-done.21.far_ref, bf16[704,2048]{1,0:T(8,128)(2,1)S(1)} %bitcast.97, ...), custom_call_target="tpu_custom_call" | custom-call | flops 2214592512 | bytes 11927552 | tf_op jit(solution)/shard_map/pallas_call | solution.py:142
  108.3 3.2 %shard_map.147 = (bf16[4,64,1024]{2,1,0:T(8,128)(2,1)S(1)}, bf16[4,64,1024]{2,1,0:T(8,128)(2,1)S(1)}) custom-call(s32[2]{0:T(128)S(1)} %pad_add_fusion.place_ref, bf16[256,2176]{1,0:T(8,128)(2,1)S(1)} %collective-permute-done.22.near_ref, bf16[256,2176]{1,0:T(8,128)(2,1)S(1)} %collective-permute-done.23.far_ref, bf16[704,2048]{1,0:T(8,128)(2,1)S(1)} %bitcast.98, ...), custom_call_target="tpu_custom_call" | custom-call | flops 2214592512 | bytes 11927552 | tf_op jit(solution)/shard_map/pallas_call | solution.py:142
  114.9 3.4 %shard_map.148 = (bf16[4,64,1024]{2,1,0:T(8,128)(2,1)S(1)}, bf16[4,64,1024]{2,1,0:T(8,128)(2,1)S(1)}) custom-call(s32[2]{0:T(128)S(1)} %pad_add_fusion.place_ref, bf16[256,2176]{1,0:T(8,128)(2,1)S(1)} %constant_dynamic-update-slice_fusion.4.near_ref, bf16[256,2176]{1,0:T(8,128)(2,1)S(1)} %collective-permute-done.21.far_ref, bf16[704,2048]{1,0:T(8,128)(2,1)S(1)} %bitcast.99, ...), custom_call_target="tpu_custom_call" | custom-call | flops 2214592512 | bytes 11927552 | tf_op jit(solution)/shard_map/pallas_call | solution.py:142
  118.5 3.2 %shard_map.149 = (bf16[4,64,1024]{2,1,0:T(8,128)(2,1)S(1)}, bf16[4,64,1024]{2,1,0:T(8,128)(2,1)S(1)}) custom-call(s32[2]{0:T(128)S(1)} %pad_add_fusion.place_ref, bf16[256,2176]{1,0:T(8,128)(2,1)S(1)} %collective-permute-done.22.near_ref, bf16[256,2176]{1,0:T(8,128)(2,1)S(1)} %collective-permute-done.23.far_ref, bf16[704,2048]{1,0:T(8,128)(2,1)S(1)} %bitcast.100, ...), custom_call_target="tpu_custom_call" | custom-call | flops 2214592512 | bytes 11927552 | tf_op jit(solution)/shard_map/pallas_call | solution.py:142
  122.3 3.2 %shard_map.150 = (bf16[4,64,1024]{2,1,0:T(8,128)(2,1)S(1)}, bf16[4,64,1024]{2,1,0:T(8,128)(2,1)S(1)}) custom-call(s32[2]{0:T(128)S(1)} %pad_add_fusion.place_ref, bf16[128,2176]{1,0:T(8,128)(2,1)S(1)} %constant_dynamic-update-slice_fusion.6.near_ref, bf16[128,2176]{1,0:T(8,128)(2,1)S(1)} %collective-permute-done.35.far_ref, bf16[704,2048]{1,0:T(8,128)(2,1)S(1)} %bitcast.101, ...), custom_call_target="tpu_custom_call" | custom-call | flops 2214592512 | bytes 10813440 | tf_op jit(solution)/shard_map/pallas_call | solution.py:142
  129.4 3.2 %shard_map.151 = (bf16[4,64,1024]{2,1,0:T(8,128)(2,1)S(1)}, bf16[4,64,1024]{2,1,0:T(8,128)(2,1)S(1)}) custom-call(s32[2]{0:T(128)S(1)} %pad_add_fusion.place_ref, bf16[128,2176]{1,0:T(8,128)(2,1)S(1)} %collective-permute-done.36.near_ref, bf16[128,2176]{1,0:T(8,128)(2,1)S(1)} %collective-permute-done.37.far_ref, bf16[704,2048]{1,0:T(8,128)(2,1)S(1)} %bitcast.102, ...), custom_call_target="tpu_custom_call" | custom-call | flops 2214592512 | bytes 10813440 | tf_op jit(solution)/shard_map/pallas_call | solution.py:142
  132.7 3.8 %collective-permute-done.32 = bf16[2,64,1024]{2,1,0:T(8,128)(2,1)S(1)} collective-permute-done((bf16[2,64,1024]{2,1,0:T(8,128)(2,1)S(1)}, bf16[2,64,1024]{2,1,0:T(8,128)(2,1)S(1)}, u32[]{:S(2)}, u32[]{:S(2)}) %collective-permute-start.32) | collective-permute-done | bytes 262176 | tf_op jit(solution)/shard_map/scatter_first_1/ppermute | solution.py:171
  136.6 2.4 %collective-permute-done.29 = bf16[2,2,64,1024]{3,2,1,0:T(8,128)(2,1)S(1)} collective-permute-done((bf16[2,2,64,1024]{3,2,1,0:T(8,128)(2,1)S(1)}, bf16[2,2,64,1024]{3,2,1,0:T(8,128)(2,1)S(1)}, u32[]{:S(2)}, u32[]{:S(2)}) %collective-permute-start.29) | collective-permute-done | bytes 524320 | tf_op jit(solution)/shard_map/scatter_second_3/ppermute | solution.py:171
  141.5 10.0 %collective-permute-done.40 = bf16[2,2,64,1024]{3,2,1,0:T(8,128)(2,1)S(1)} collective-permute-done((bf16[2,2,64,1024]{3,2,1,0:T(8,128)(2,1)S(1)}, bf16[2,2,64,1024]{3,2,1,0:T(8,128)(2,1)S(1)}, u32[]{:S(2)}, u32[]{:S(2)}) %collective-permute-start.40) | collective-permute-done | bytes 524320 | tf_op jit(solution)/shard_map/scatter_second_2/ppermute | solution.py:171
  154.4 2.0 %collective-permute-start.31 = (bf16[2,64,1024]{2,1,0:T(8,128)(2,1)S(1)}, bf16[2,64,1024]{2,1,0:T(8,128)(2,1)S(1)}, u32[]{:S(2)}, u32[]{:S(2)}) collective-permute-start(bf16[2,64,1024]{2,1,0:T(8,128)(2,1)S(1)} %pad_maximum_fusion.5), channel_id=1, source_target_pairs={{0,1},{1,0},{2,3},{3,2},{4,5},{5,4},{6,7},{7,6},{8,9},{9,8},{10,11... | collective-permute-start | bytes 786440 | tf_op jit(solution)/shard_map/scatter_first_0/ppermute | solution.py:171
  156.4 1.8 %collective-permute-done.41 = bf16[2,64,1024]{2,1,0:T(8,128)(2,1)S(1)} collective-permute-done((bf16[2,64,1024]{2,1,0:T(8,128)(2,1)S(1)}, bf16[2,64,1024]{2,1,0:T(8,128)(2,1)S(1)}, u32[]{:S(2)}, u32[]{:S(2)}) %collective-permute-start.41) | collective-permute-done | bytes 262176 | tf_op jit(solution)/shard_map/scatter_first_2/ppermute | solution.py:171
  161.0 10.0 %collective-permute-done.42 = bf16[128,1024]{1,0:T(8,128)(2,1)S(1)} collective-permute-done((bf16[128,1024]{1,0:T(8,128)(2,1)}, bf16[128,1024]{1,0:T(8,128)(2,1)S(1)}, u32[]{:S(2)}, u32[]{:S(2)}) %collective-permute-start.42) | collective-permute-done | bytes 262176 | tf_op jit(solution)/shard_map/to_plane_2/ppermute | solution.py:41
  (157 shorter events, 45.0 us)
Async XLA Ops:
  4.5 11.6 %collective-permute-start = (bf16[128,1024]{1,0:T(8,128)(2,1)S(1)}, bf16[128,1024]{1,0:T(8,128)(2,1)S(1)}, u32[]{:S(2)}, u32[]{:S(2)}) collective-permute-start(bf16[128,1024]{1,0:T(8,128)(2,1)S(1)} %get-tuple-element.44.rest_0_), channel_id=1, source_target_pairs={{0,4},{1,5},{2,6},{3,7},{4,8},{5,9},{6,10},{7,11},{8,12},{9,13},{1... | collective-permute-start | bytes 786440 | tf_op jit(solution)/shard_map/ppermute | solution.py:27
  9.4 11.9 %collective-permute-start.4 = (bf16[128,1024]{1,0:T(8,128)(2,1)}, bf16[128,1024]{1,0:T(8,128)(2,1)S(1)}, u32[]{:S(2)}, u32[]{:S(2)}) collective-permute-start(bf16[128,1024]{1,0:T(8,128)(2,1)} %rest_0_), channel_id=1, source_target_pairs={{0,4},{1,5},{2,6},{3,7},{4,8},{5,9},{6,10},{7,11},{8,12},{9,13},{1... | collective-permute-start | bytes 786440 | tf_op jit(solution)/shard_map/ppermute | solution.py:27
  16.9 8.9 %collective-permute-start.1 = (bf16[128,1024]{1,0:T(8,128)(2,1)S(1)}, bf16[128,1024]{1,0:T(8,128)(2,1)S(1)}, u32[]{:S(2)}, u32[]{:S(2)}) collective-permute-start(bf16[128,1024]{1,0:T(8,128)(2,1)S(1)} %get-tuple-element.103), channel_id=1, source_target_pairs={{0,1},{1,0},{2,3},{3,2},{4,5},{5,4},{6,7},{7,6},{8,9},{9,8},{10,11... | collective-permute-start | bytes 786440 | tf_op jit(solution)/shard_map/ppermute | solution.py:22
  19.3 13.8 %collective-permute-start.2 = (bf16[128,1024]{1,0:T(8,128)(2,1)}, bf16[128,1024]{1,0:T(8,128)(2,1)S(1)}, u32[]{:S(2)}, u32[]{:S(2)}) collective-permute-start(bf16[128,1024]{1,0:T(8,128)(2,1)} %get-tuple-element.102), channel_id=1, source_target_pairs={{0,2},{1,3},{2,0},{3,1},{4,6},{5,7},{6,4},{7,5},{8,10},{9,11},{10,... | collective-permute-start | bytes 786440 | tf_op jit(solution)/shard_map/ppermute | solution.py:22
  20.8 12.3 %collective-permute-start.3 = (bf16[128,1024]{1,0:T(8,128)(2,1)}, bf16[128,1024]{1,0:T(8,128)(2,1)S(1)}, u32[]{:S(2)}, u32[]{:S(2)}) collective-permute-start(bf16[128,1024]{1,0:T(8,128)(2,1)} %get-tuple-element.101), channel_id=1, source_target_pairs={{0,3},{1,2},{2,1},{3,0},{4,7},{5,6},{6,5},{7,4},{8,11},{9,10},{10,... | collective-permute-start | bytes 786440 | tf_op jit(solution)/shard_map/ppermute | solution.py:22
  22.3 14.8 %collective-permute-start.5 = (bf16[128,1024]{1,0:T(8,128)(2,1)}, bf16[128,1024]{1,0:T(8,128)(2,1)S(1)}, u32[]{:S(2)}, u32[]{:S(2)}) collective-permute-start(bf16[128,1024]{1,0:T(8,128)(2,1)} %get-tuple-element.100), channel_id=1, source_target_pairs={{0,1},{1,0},{2,3},{3,2},{4,5},{5,4},{6,7},{7,6},{8,9},{9,8},{10,11... | collective-permute-start | bytes 786440 | tf_op jit(solution)/shard_map/ppermute | solution.py:22
  23.8 18.3 %collective-permute-start.6 = (bf16[128,1024]{1,0:T(8,128)(2,1)}, bf16[128,1024]{1,0:T(8,128)(2,1)S(1)}, u32[]{:S(2)}, u32[]{:S(2)}) collective-permute-start(bf16[128,1024]{1,0:T(8,128)(2,1)} %get-tuple-element.99), channel_id=1, source_target_pairs={{0,2},{1,3},{2,0},{3,1},{4,6},{5,7},{6,4},{7,5},{8,10},{9,11},{10,... | collective-permute-start | bytes 786440 | tf_op jit(solution)/shard_map/ppermute | solution.py:22
  25.8 16.3 %collective-permute-start.7 = (bf16[128,1024]{1,0:T(8,128)(2,1)}, bf16[128,1024]{1,0:T(8,128)(2,1)S(1)}, u32[]{:S(2)}, u32[]{:S(2)}) collective-permute-start(bf16[128,1024]{1,0:T(8,128)(2,1)} %get-tuple-element.98), channel_id=1, source_target_pairs={{0,3},{1,2},{2,1},{3,0},{4,7},{5,6},{6,5},{7,4},{8,11},{9,10},{10,... | collective-permute-start | bytes 786440 | tf_op jit(solution)/shard_map/ppermute | solution.py:22
  50.1 11.6 %collective-permute-start.15 = (bf16[64,2176]{1,0:T(8,128)(2,1)S(1)}, bf16[64,2176]{1,0:T(8,128)(2,1)S(1)}, u32[]{:S(2)}, u32[]{:S(2)}) collective-permute-start(bf16[64,2176]{1,0:T(8,128)(2,1)S(1)} %get-tuple-element.55), channel_id=1, source_target_pairs={{4,0},{5,1},{6,2},{7,3},{8,4},{9,5},{10,6},{11,7},{12,8},{13,9},{1... | collective-permute-start | bytes 835592 | tf_op jit(solution)/shard_map/from_plane_1/ppermute | solution.py:33
  54.6 13.8 %collective-permute-start.16 = (bf16[64,2176]{1,0:T(8,128)(2,1)S(1)}, bf16[64,2176]{1,0:T(8,128)(2,1)S(1)}, u32[]{:S(2)}, u32[]{:S(2)}) collective-permute-start(bf16[64,2176]{1,0:T(8,128)(2,1)S(1)} %get-tuple-element.55), channel_id=1, source_target_pairs={{12,0},{13,1},{14,2},{15,3},{0,4},{1,5},{2,6},{3,7},{4,8},{5,9},{6... | collective-permute-start | bytes 835592 | tf_op jit(solution)/shard_map/from_plane_3/ppermute | solution.py:33
  56.2 12.3 %collective-permute-start.10 = (bf16[128,2176]{1,0:T(8,128)(2,1)S(1)}, bf16[128,2176]{1,0:T(8,128)(2,1)S(1)}, u32[]{:S(2)}, u32[]{:S(2)}) collective-permute-start(bf16[128,2176]{1,0:T(8,128)(2,1)S(1)} %constant_dynamic-update-slice_fusion.near_ref), channel_id=1, source_target_pairs={{0,2},{1,3},{2,0},{3,1},{4,6},{5,7},{6,4},{7,5},{8,10},{9,11},{10,... | collective-permute-start | bytes 1671176 | tf_op jit(solution)/shard_map/gather_second_0/ppermute | solution.py:171
  68.5 9.6 %collective-permute-start.18 = (bf16[128,2176]{1,0:T(8,128)(2,1)S(1)}, bf16[128,2176]{1,0:T(8,128)(2,1)S(1)}, u32[]{:S(2)}, u32[]{:S(2)}) collective-permute-start(bf16[128,2176]{1,0:T(8,128)(2,1)S(1)} %constant_dynamic-update-slice_fusion.2), channel_id=1, source_target_pairs={{0,1},{1,0},{2,3},{3,2},{4,5},{5,4},{6,7},{7,6},{8,9},{9,8},{10,11... | collective-permute-start | bytes 1671176 | tf_op jit(solution)/shard_map/gather_first_1/ppermute | solution.py:171
  69.1 15.0 %collective-permute-start.17 = (bf16[64,2176]{1,0:T(8,128)(2,1)S(1)}, bf16[64,2176]{1,0:T(8,128)(2,1)S(1)}, u32[]{:S(2)}, u32[]{:S(2)}) collective-permute-start(bf16[64,2176]{1,0:T(8,128)(2,1)S(1)} %get-tuple-element.55), channel_id=1, source_target_pairs={{8,0},{9,1},{10,2},{11,3},{12,4},{13,5},{14,6},{15,7},{0,8},{1,9},... | collective-permute-start | bytes 835592 | tf_op jit(solution)/shard_map/from_plane_2/ppermute | solution.py:33
  84.0 17.5 %collective-permute-start.21 = (bf16[256,2176]{1,0:T(8,128)(2,1)S(1)}, bf16[256,2176]{1,0:T(8,128)(2,1)S(1)}, u32[]{:S(2)}, u32[]{:S(2)}) collective-permute-start(bf16[256,2176]{1,0:T(8,128)(2,1)S(1)} %constant_dynamic-update-slice_fusion.4.near_ref), channel_id=1, source_target_pairs={{0,2},{1,3},{2,0},{3,1},{4,6},{5,7},{6,4},{7,5},{8,10},{9,11},{10,... | collective-permute-start | bytes 3342344 | tf_op jit(solution)/shard_map/gather_second_1/ppermute | solution.py:171
  91.4 16.9 %collective-permute-start.22 = (bf16[256,2176]{1,0:T(8,128)(2,1)S(1)}, bf16[256,2176]{1,0:T(8,128)(2,1)S(1)}, u32[]{:S(2)}, u32[]{:S(2)}) collective-permute-start(bf16[256,2176]{1,0:T(8,128)(2,1)S(1)} %constant_dynamic-update-slice_fusion.4.near_ref), channel_id=1, source_target_pairs={{16,0},{0,16},{17,1},{1,17},{18,2},{2,18},{19,3},{3,19},{20,4},{4,... | collective-permute-start | bytes 3342344 | tf_op jit(solution)/shard_map/ppermute | solution.py:48
  94.7 10.1 %collective-permute-start.13 = (bf16[4,64,1024]{2,1,0:T(8,128)(2,1)S(1)}, bf16[4,64,1024]{2,1,0:T(8,128)(2,1)S(1)}, u32[]{:S(2)}, u32[]{:S(2)}) collective-permute-start(bf16[4,64,1024]{2,1,0:T(8,128)(2,1)S(1)} %get-tuple-element.52), channel_id=1, source_target_pairs={{16,0},{0,16},{17,1},{1,17},{18,2},{2,18},{19,3},{3,19},{20,4},{4,... | collective-permute-start | bytes 1572872 | tf_op jit(solution)/shard_map/ppermute | solution.py:48
  101.5 6.8 %collective-permute-start.23 = (bf16[256,2176]{1,0:T(8,128)(2,1)S(1)}, bf16[256,2176]{1,0:T(8,128)(2,1)S(1)}, u32[]{:S(2)}, u32[]{:S(2)}) collective-permute-start(bf16[256,2176]{1,0:T(8,128)(2,1)S(1)} %collective-permute-done.21.far_ref), channel_id=1, source_target_pairs={{16,0},{0,16},{17,1},{1,17},{18,2},{2,18},{19,3},{3,19},{20,4},{4,... | collective-permute-start | bytes 3342344 | tf_op jit(solution)/shard_map/ppermute | solution.py:48
  101.8 27.6 %collective-permute-start.36 = (bf16[128,2176]{1,0:T(8,128)(2,1)S(1)}, bf16[128,2176]{1,0:T(8,128)(2,1)S(1)}, u32[]{:S(2)}, u32[]{:S(2)}) collective-permute-start(bf16[128,2176]{1,0:T(8,128)(2,1)S(1)} %constant_dynamic-update-slice_fusion.6.near_ref), channel_id=1, source_target_pairs={{16,0},{0,16},{17,1},{1,17},{18,2},{2,18},{19,3},{3,19},{20,4},{4,... | collective-permute-start | bytes 1671176 | tf_op jit(solution)/shard_map/ppermute | solution.py:48
  102.4 9.9 %collective-permute-start.35 = (bf16[128,2176]{1,0:T(8,128)(2,1)S(1)}, bf16[128,2176]{1,0:T(8,128)(2,1)S(1)}, u32[]{:S(2)}, u32[]{:S(2)}) collective-permute-start(bf16[128,2176]{1,0:T(8,128)(2,1)S(1)} %constant_dynamic-update-slice_fusion.6.near_ref), channel_id=1, source_target_pairs={{0,2},{1,3},{2,0},{3,1},{4,6},{5,7},{6,4},{7,5},{8,10},{9,11},{10,... | collective-permute-start | bytes 1671176 | tf_op jit(solution)/shard_map/gather_second_2/ppermute | solution.py:171
  112.2 9.5 %collective-permute-start.20 = (bf16[2,2,64,1024]{3,2,1,0:T(8,128)(2,1)S(1)}, bf16[2,2,64,1024]{3,2,1,0:T(8,128)(2,1)S(1)}, u32[]{:S(2)}, u32[]{:S(2)}) collective-permute-start(bf16[2,2,64,1024]{3,2,1,0:T(8,128)(2,1)S(1)} %pad_maximum_fusion.1), channel_id=1, source_target_pairs={{0,2},{1,3},{2,0},{3,1},{4,6},{5,7},{6,4},{7,5},{8,10},{9,11},{10,... | collective-permute-start | bytes 1572872 | tf_op jit(solution)/shard_map/scatter_second_0/ppermute | solution.py:171
  112.3 17.0 %collective-permute-start.37 = (bf16[128,2176]{1,0:T(8,128)(2,1)S(1)}, bf16[128,2176]{1,0:T(8,128)(2,1)S(1)}, u32[]{:S(2)}, u32[]{:S(2)}) collective-permute-start(bf16[128,2176]{1,0:T(8,128)(2,1)S(1)} %collective-permute-done.35.far_ref), channel_id=1, source_target_pairs={{16,0},{0,16},{17,1},{1,17},{18,2},{2,18},{19,3},{3,19},{20,4},{4,... | collective-permute-start | bytes 1671176 | tf_op jit(solution)/shard_map/ppermute | solution.py:48
  114.0 13.1 %collective-permute-start.27 = (bf16[2,2,64,1024]{3,2,1,0:T(8,128)(2,1)S(1)}, bf16[2,2,64,1024]{3,2,1,0:T(8,128)(2,1)S(1)}, u32[]{:S(2)}, u32[]{:S(2)}) collective-permute-start(bf16[2,2,64,1024]{3,2,1,0:T(8,128)(2,1)S(1)} %pad_maximum_fusion.2), channel_id=1, source_target_pairs={{0,2},{1,3},{2,0},{3,1},{4,6},{5,7},{6,4},{7,5},{8,10},{9,11},{10,... | collective-permute-start | bytes 1572872 | tf_op jit(solution)/shard_map/scatter_second_1/ppermute | solution.py:171
  118.4 9.2 %collective-permute-start.28 = (bf16[4,64,1024]{2,1,0:T(8,128)(2,1)S(1)}, bf16[4,64,1024]{2,1,0:T(8,128)(2,1)S(1)}, u32[]{:S(2)}, u32[]{:S(2)}) collective-permute-start(bf16[4,64,1024]{2,1,0:T(8,128)(2,1)S(1)} %get-tuple-element.69), channel_id=1, source_target_pairs={{16,0},{0,16},{17,1},{1,17},{18,2},{2,18},{19,3},{3,19},{20,4},{4,... | collective-permute-start | bytes 1572872 | tf_op jit(solution)/shard_map/ppermute | solution.py:48
  127.1 12.3 %collective-permute-start.39 = (bf16[4,64,1024]{2,1,0:T(8,128)(2,1)S(1)}, bf16[4,64,1024]{2,1,0:T(8,128)(2,1)S(1)}, u32[]{:S(2)}, u32[]{:S(2)}) collective-permute-start(bf16[4,64,1024]{2,1,0:T(8,128)(2,1)S(1)} %get-tuple-element.78), channel_id=1, source_target_pairs={{16,0},{0,16},{17,1},{1,17},{18,2},{2,18},{19,3},{3,19},{20,4},{4,... | collective-permute-start | bytes 1572872 | tf_op jit(solution)/shard_map/ppermute | solution.py:48
  127.4 9.1 %collective-permute-start.32 = (bf16[2,64,1024]{2,1,0:T(8,128)(2,1)S(1)}, bf16[2,64,1024]{2,1,0:T(8,128)(2,1)S(1)}, u32[]{:S(2)}, u32[]{:S(2)}) collective-permute-start(bf16[2,64,1024]{2,1,0:T(8,128)(2,1)S(1)} %pad_maximum_fusion.6), channel_id=1, source_target_pairs={{0,1},{1,0},{2,3},{3,2},{4,5},{5,4},{6,7},{7,6},{8,9},{9,8},{10,11... | collective-permute-start | bytes 786440 | tf_op jit(solution)/shard_map/scatter_first_1/ppermute | solution.py:171
  128.0 11.0 %collective-permute-start.29 = (bf16[2,2,64,1024]{3,2,1,0:T(8,128)(2,1)S(1)}, bf16[2,2,64,1024]{3,2,1,0:T(8,128)(2,1)S(1)}, u32[]{:S(2)}, u32[]{:S(2)}) collective-permute-start(bf16[2,2,64,1024]{3,2,1,0:T(8,128)(2,1)S(1)} %pad_maximum_fusion.3), channel_id=1, source_target_pairs={{0,2},{1,3},{2,0},{3,1},{4,6},{5,7},{6,4},{7,5},{8,10},{9,11},{10,... | collective-permute-start | bytes 1572872 | tf_op jit(solution)/shard_map/scatter_second_3/ppermute | solution.py:171
  132.6 6.7 %collective-permute-start.38 = (bf16[4,64,1024]{2,1,0:T(8,128)(2,1)S(1)}, bf16[4,64,1024]{2,1,0:T(8,128)(2,1)S(1)}, u32[]{:S(2)}, u32[]{:S(2)}) collective-permute-start(bf16[4,64,1024]{2,1,0:T(8,128)(2,1)S(1)} %get-tuple-element.80), channel_id=1, source_target_pairs={{16,0},{0,16},{17,1},{1,17},{18,2},{2,18},{19,3},{3,19},{20,4},{4,... | collective-permute-start | bytes 1572872 | tf_op jit(solution)/shard_map/ppermute | solution.py:48
  139.8 11.7 %collective-permute-start.40 = (bf16[2,2,64,1024]{3,2,1,0:T(8,128)(2,1)S(1)}, bf16[2,2,64,1024]{3,2,1,0:T(8,128)(2,1)S(1)}, u32[]{:S(2)}, u32[]{:S(2)}) collective-permute-start(bf16[2,2,64,1024]{3,2,1,0:T(8,128)(2,1)S(1)} %pad_maximum_fusion.4), channel_id=1, source_target_pairs={{0,2},{1,3},{2,0},{3,1},{4,6},{5,7},{6,4},{7,5},{8,10},{9,11},{10,... | collective-permute-start | bytes 1572872 | tf_op jit(solution)/shard_map/scatter_second_2/ppermute | solution.py:171
  140.3 20.7 %collective-permute-start.33 = (bf16[128,1024]{1,0:T(8,128)(2,1)S(1)}, bf16[128,1024]{1,0:T(8,128)(2,1)S(1)}, u32[]{:S(2)}, u32[]{:S(2)}) collective-permute-start(bf16[128,1024]{1,0:T(8,128)(2,1)S(1)} %pad_maximum_fusion.9), channel_id=1, source_target_pairs={{0,4},{1,5},{2,6},{3,7},{4,8},{5,9},{6,10},{7,11},{8,12},{9,13},{1... | collective-permute-start | bytes 786440 | tf_op jit(solution)/shard_map/to_plane_1/ppermute | solution.py:41
  140.4 12.0 %collective-permute-start.30 = (bf16[2,64,1024]{2,1,0:T(8,128)(2,1)S(1)}, bf16[2,64,1024]{2,1,0:T(8,128)(2,1)S(1)}, u32[]{:S(2)}, u32[]{:S(2)}) collective-permute-start(bf16[2,64,1024]{2,1,0:T(8,128)(2,1)S(1)} %pad_maximum_fusion.7), channel_id=1, source_target_pairs={{0,1},{1,0},{2,3},{3,2},{4,5},{5,4},{6,7},{7,6},{8,9},{9,8},{10,11... | collective-permute-start | bytes 786440 | tf_op jit(solution)/shard_map/scatter_first_3/ppermute | solution.py:171
  153.2 7.9 %collective-permute-start.34 = (bf16[128,1024]{1,0:T(8,128)(2,1)}, bf16[128,1024]{1,0:T(8,128)(2,1)S(1)}, u32[]{:S(2)}, u32[]{:S(2)}) collective-permute-start(bf16[128,1024]{1,0:T(8,128)(2,1)} %pad_maximum_fusion.8), channel_id=1, source_target_pairs={{0,12},{1,13},{2,14},{3,15},{4,0},{5,1},{6,2},{7,3},{8,4},{9,5},{1... | collective-permute-start | bytes 786440 | tf_op jit(solution)/shard_map/to_plane_3/ppermute | solution.py:41
  158.9 12.1 %collective-permute-start.42 = (bf16[128,1024]{1,0:T(8,128)(2,1)}, bf16[128,1024]{1,0:T(8,128)(2,1)S(1)}, u32[]{:S(2)}, u32[]{:S(2)}) collective-permute-start(bf16[128,1024]{1,0:T(8,128)(2,1)} %pad_maximum_fusion.11), channel_id=1, source_target_pairs={{0,8},{1,9},{2,10},{3,11},{4,12},{5,13},{6,14},{7,15},{8,0},{9,1},... | collective-permute-start | bytes 786440 | tf_op jit(solution)/shard_map/to_plane_2/ppermute | solution.py:41
  (23 other events, 218.4 us)

commit v14 on v13

--- a/solution.py
+++ b/solution.py
@@ -339,7 +339,7 @@
     run = functools.partial(
         expert_outputs, place, weights=weights, experts=experts, cores=cores
     )
-    columns, nears, fars, rows = [], [], [], []
+    columns, nears, fars, rows = [], [], [], {}
     sent = payload
     for group in groups:
         columns.append(
@@ -347,22 +347,19 @@
         )
         sent = after(payload, columns[-1])
     for number, column in enumerate(columns):
-        if number > 0:
-            column = after(column, nears[-1], fars[0])
-        if number == 2:
-            outs = run(rows=rows[0], planes=1, plane=0, span=1, waits={})
-            column = after(column, outs)
+        if number > 1:
+            column = after(column, nears[-1])
         nears.append(
             jnp.concatenate([column, crossed(column, True, f"gather_first_{number}")])
         )
-        ready = after(nears[-1], columns[2]) if number == 1 else nears[-1]
-        fars.append(crossed(ready, False, f"gather_second_{number}"))
-        rows.append(
-            [
-                (from_core(nears[-1], i), from_core(fars[-1], i)) if i else (nears[-1], fars[-1])
-                for i in range(cores)
-            ]
-        )
+        fars.append(crossed(nears[-1], False, f"gather_second_{number}"))
+    def rows_of_cores(number, *waits):
+        near, far = nears[number], after(fars[number], *waits)
+        return [
+            (from_core(near, i), from_core(far, i)) if i else (near, far) for i in range(cores)
+        ]
+
+    outs = run(rows=rows_of_cores(0), planes=1, plane=0, span=1, waits={0: [columns[2]]})
     own_totals = core_totals(outs, cores)
     sent = after(second_share(own_totals), nears[-1])
     own_second = crossed(sent, False, "scatter_second_0")
@@ -374,10 +371,13 @@
         for number, group in enumerate(groups)
         for plane in range(0, len(group), span_of)
     ]
+    steps.sort(key=lambda step: step[2][0])
     for number, plane, aheads in steps[1:]:
         waits = {0: [outs], cores - 1: [*seconds[-1:]]}
         if len(seconds) > 1:
             waits[0].append(own_second)
+        if number not in rows:
+            rows[number] = rows_of_cores(number, outs if number == 1 else outs[0])
         outs = run(
             rows=rows[number],
             planes=len(groups[number]),

time: 172 us -> 172 us (level)
    ppermute x3, waiting for transfers between devices: 16.5 us -> 22.6 us  [from_plane(): lax.ppermute(block, 'blk', [((i + PLANE * ahead) % count, i) for i in ran...]
    ppermute x14, waiting for transfers between devices: 36.4 us -> 32 us  [crossed(): return lax.ppermute(block, ('tok', 'blk'), route)]
    ppermute x15, waiting for transfers between devices: 5.61 us -> 3.25 us  [from_core(): lax.ppermute(block, 'tok', [((i + ahead) % count, i) for i in range(count)])]
  transfers between devices with their start and end apart: 43 -> 43, of which waited for: 21 -> 20; matrix products, arithmetic and copies ran while one was open for 6% -> 6% of each run, Pallas kernels for 16% -> 16%
where the time goes in v14:
time: 172 us
  waiting for transfers between devices  79.8 us (46%)
  starting transfers between devices  41.9 us (24%)
  Pallas kernels  31.4 us (18%)
  local copies, waits for them, and re-layouts  8.72 us (5%)
  other arithmetic  8.57 us (5%)
    ppermute x14, waiting for transfers between devices, crossed(): return lax.ppermute(block, ('tok', 'blk'), route)  32 us
    pallas_call x12, Pallas kernels, local_call(): pl.pallas_call(body, in_specs=[scalar] * len(scalars) + [whole] * len(arr...  31.4 us
    ppermute x3, waiting for transfers between devices, from_plane(): lax.ppermute(block, 'blk', [((i + PLANE * ahead) % count, i) for i in ran...  22.6 us
    ppermute x14, starting transfers between devices, crossed(): return lax.ppermute(block, ('tok', 'blk'), route)  14.3 us
    ppermute x3, waiting for transfers between devices, to_plane(): lax.ppermute(block, 'blk', [(i, (i + PLANE * ahead) % count) for i in ran...  9.76 us
    ppermute x6, waiting for transfers between devices, flipped(): lax.ppermute(block, 'blk', [(i, i ^ mask) for i in range(lax.axis_size('b...  9.73 us
    ppermute x2, starting transfers between devices, next_plane(): lax.ppermute(block, 'blk', [(i, i + PLANE) for i in range(count - PLANE)])  8.43 us
    ppermute x6, starting transfers between devices, flipped(): lax.ppermute(block, 'blk', [(i, i ^ mask) for i in range(lax.axis_size('b...  8.32 us
  transfers between devices with their start and end apart: 43, of which 20 were waited for; matrix products, arithmetic and copies ran while one was open for 6% of the time, Pallas kernels for 16%

profile of v14, /device:TPU:0, one launch (start us, length us, event | category | flops | bytes accessed | tf_op | source)
XLA Modules:
  0.0 171.6 jit_solution(5907925575207123552)
XLA Ops:
  4.5 4.9 %collective-permute-start = (bf16[128,1024]{1,0:T(8,128)(2,1)S(1)}, bf16[128,1024]{1,0:T(8,128)(2,1)S(1)}, u32[]{:S(2)}, u32[]{:S(2)}) collective-permute-start(bf16[128,1024]{1,0:T(8,128)(2,1)S(1)} %get-tuple-element.44.rest_0_), channel_id=1, source_target_pairs={{0,4},{1,5},{2,6},{3,7},{4,8},{5,9},{6,10},{7,11},{8,12},{9,13},{1... | collective-permute-start | bytes 786440 | tf_op jit(solution)/shard_map/ppermute | solution.py:27
  9.4 3.5 %collective-permute-start.4 = (bf16[128,1024]{1,0:T(8,128)(2,1)}, bf16[128,1024]{1,0:T(8,128)(2,1)S(1)}, u32[]{:S(2)}, u32[]{:S(2)}) collective-permute-start(bf16[128,1024]{1,0:T(8,128)(2,1)} %rest_0_), channel_id=1, source_target_pairs={{0,4},{1,5},{2,6},{3,7},{4,8},{5,9},{6,10},{7,11},{8,12},{9,13},{1... | collective-permute-start | bytes 786440 | tf_op jit(solution)/shard_map/ppermute | solution.py:27
  13.7 2.4 %collective-permute-done.rest_1_ = bf16[128,1024]{1,0:T(8,128)(2,1)S(1)} collective-permute-done((bf16[128,1024]{1,0:T(8,128)(2,1)S(1)}, bf16[128,1024]{1,0:T(8,128)(2,1)S(1)}, u32[]{:S(2)}, u32[]{:S(2)}) %collective-permute-start) | collective-permute-done | bytes 262176 | tf_op jit(solution)/shard_map/ppermute | solution.py:27
  16.9 2.4 %collective-permute-start.3 = (bf16[128,1024]{1,0:T(8,128)(2,1)S(1)}, bf16[128,1024]{1,0:T(8,128)(2,1)S(1)}, u32[]{:S(2)}, u32[]{:S(2)}) collective-permute-start(bf16[128,1024]{1,0:T(8,128)(2,1)S(1)} %get-tuple-element.101), channel_id=1, source_target_pairs={{0,3},{1,2},{2,1},{3,0},{4,7},{5,6},{6,5},{7,4},{8,11},{9,10},{10,... | collective-permute-start | bytes 786440 | tf_op jit(solution)/shard_map/ppermute | solution.py:22
  22.3 2.4 %collective-permute-start.7 = (bf16[128,1024]{1,0:T(8,128)(2,1)}, bf16[128,1024]{1,0:T(8,128)(2,1)S(1)}, u32[]{:S(2)}, u32[]{:S(2)}) collective-permute-start(bf16[128,1024]{1,0:T(8,128)(2,1)} %get-tuple-element.98), channel_id=1, source_target_pairs={{0,3},{1,2},{2,1},{3,0},{4,7},{5,6},{6,5},{7,4},{8,11},{9,10},{10,... | collective-permute-start | bytes 786440 | tf_op jit(solution)/shard_map/ppermute | solution.py:22
  26.8 1.9 %collective-permute-start.5 = (bf16[128,1024]{1,0:T(8,128)(2,1)}, bf16[128,1024]{1,0:T(8,128)(2,1)S(1)}, u32[]{:S(2)}, u32[]{:S(2)}) collective-permute-start(bf16[128,1024]{1,0:T(8,128)(2,1)} %get-tuple-element.100), channel_id=1, source_target_pairs={{0,1},{1,0},{2,3},{3,2},{4,5},{5,4},{6,7},{7,6},{8,9},{9,8},{10,11... | collective-permute-start | bytes 786440 | tf_op jit(solution)/shard_map/ppermute | solution.py:22
  28.9 1.8 %scatter_fusion = bf16[8,16,2,1024]{3,1,2,0:T(8,128)(2,1)S(1)} fusion(bf16[8,16,2,1024]{3,1,2,0:T(8,128)(2,1)S(1)} %broadcast_in_dim.31, s32[8]{0:T(128)S(1)} %compare_select_fusion, bf16[8,16,2,1024]{3,1,2,0:T(8,128)(2,1)} %pad_maximum_fusion), kind=kCustom, calls=%fused_computation | custom fusion | bytes 1572896 | tf_op jit(solution)/shard_map/scatter | solution.py:311
  30.7 4.7 %collective-permute-done.2.rest_3_ = bf16[128,1024]{1,0:T(8,128)(2,1)S(1)} collective-permute-done((bf16[128,1024]{1,0:T(8,128)(2,1)}, bf16[128,1024]{1,0:T(8,128)(2,1)S(1)}, u32[]{:S(2)}, u32[]{:S(2)}) %collective-permute-start.2) | collective-permute-done | bytes 262176 | tf_op jit(solution)/shard_map/ppermute | solution.py:22
  35.4 1.9 %shard_map.141.prob_ref = bf16[8,128,640]{2,1,0:T(8,128)(2,1)S(1)} custom-call(s32[2]{0:T(128)S(1)} %pad_add_fusion.place_ref, s32[8]{0:T(128)S(1)} %copy-done.10, bf16[128,1024]{1,0:T(8,128)(2,1)S(1)} %get-tuple-element.43.q_ref, bf16[128,1024]{1,0:T(8,128)(2,1)S(1)} %get-tuple-element.44.rest_0_, bf16[128,1024]{1,0:T(8,128)(2,1)S(1)} %collective-permute-done.rest_1_, ...), custom_call_target="tpu_custom_call" | custom-call | flops 167772160 | bytes 2883584 | tf_op jit(solution)/shard_map/pallas_call | solution.py:142
  38.0 2.7 %collective-permute-done.6.rest_3_ = bf16[128,1024]{1,0:T(8,128)(2,1)S(1)} collective-permute-done((bf16[128,1024]{1,0:T(8,128)(2,1)}, bf16[128,1024]{1,0:T(8,128)(2,1)S(1)}, u32[]{:S(2)}, u32[]{:S(2)}) %collective-permute-start.6) | collective-permute-done | bytes 262176 | tf_op jit(solution)/shard_map/ppermute | solution.py:22
  40.8 2.2 %copy-done.3 = bf16[1024,2048]{1,0:T(8,128)(2,1)S(1)} copy-done((bf16[1024,2048]{1,0:T(8,128)(2,1)S(1)}, bf16[1024,2048]{1,0:T(8,128)(2,1)}, u32[]{:S(2)}) %copy-start.3) | copy-done | bytes 4194328
  43.0 1.7 shard_map.142.rest_0_
  44.7 2.6 %collective-permute-done.8.rest_1_ = f32[128,2048]{1,0:T(8,128)S(1)} collective-permute-done((f32[128,2048]{1,0:T(8,128)S(1)}, f32[128,2048]{1,0:T(8,128)S(1)}, u32[]{:S(2)}, u32[]{:S(2)}) %collective-permute-start.8) | collective-permute-done | bytes 1048608 | tf_op jit(solution)/shard_map/ppermute | solution.py:48
  48.2 4.6 %collective-permute-start.10 = (bf16[64,2176]{1,0:T(8,128)(2,1)S(1)}, bf16[64,2176]{1,0:T(8,128)(2,1)S(1)}, u32[]{:S(2)}, u32[]{:S(2)}) collective-permute-start(bf16[64,2176]{1,0:T(8,128)(2,1)S(1)} %get-tuple-element.50), channel_id=1, source_target_pairs={{4,0},{5,1},{6,2},{7,3},{8,4},{9,5},{10,6},{11,7},{12,8},{13,9},{1... | collective-permute-start | bytes 835592 | tf_op jit(solution)/shard_map/from_plane_1/ppermute | solution.py:33
  54.3 5.5 %collective-permute-done.10 = bf16[64,2176]{1,0:T(8,128)(2,1)S(1)} collective-permute-done((bf16[64,2176]{1,0:T(8,128)(2,1)S(1)}, bf16[64,2176]{1,0:T(8,128)(2,1)S(1)}, u32[]{:S(2)}, u32[]{:S(2)}) %collective-permute-start.10) | collective-permute-done | bytes 278560 | tf_op jit(solution)/shard_map/from_plane_1/ppermute | solution.py:33
  59.9 6.0 %collective-permute-done.11 = bf16[64,2176]{1,0:T(8,128)(2,1)S(1)} collective-permute-done((bf16[64,2176]{1,0:T(8,128)(2,1)S(1)}, bf16[64,2176]{1,0:T(8,128)(2,1)S(1)}, u32[]{:S(2)}, u32[]{:S(2)}) %collective-permute-start.11) | collective-permute-done | bytes 278560 | tf_op jit(solution)/shard_map/from_plane_3/ppermute | solution.py:33
  69.0 12.4 %collective-permute-done.18 = bf16[128,2176]{1,0:T(8,128)(2,1)S(1)} collective-permute-done((bf16[128,2176]{1,0:T(8,128)(2,1)S(1)}, bf16[128,2176]{1,0:T(8,128)(2,1)S(1)}, u32[]{:S(2)}, u32[]{:S(2)}) %collective-permute-start.18) | collective-permute-done | bytes 557088 | tf_op jit(solution)/shard_map/gather_first_1/ppermute | solution.py:171
  83.3 11.1 %collective-permute-done.12 = bf16[64,2176]{1,0:T(8,128)(2,1)S(1)} collective-permute-done((bf16[64,2176]{1,0:T(8,128)(2,1)S(1)}, bf16[64,2176]{1,0:T(8,128)(2,1)S(1)}, u32[]{:S(2)}, u32[]{:S(2)}) %collective-permute-start.12) | collective-permute-done | bytes 278560 | tf_op jit(solution)/shard_map/from_plane_2/ppermute | solution.py:33
  94.8 3.2 %shard_map.144 = (bf16[4,64,1024]{2,1,0:T(8,128)(2,1)S(1)}, bf16[4,64,1024]{2,1,0:T(8,128)(2,1)S(1)}) custom-call(s32[2]{0:T(128)S(1)} %pad_add_fusion.place_ref, bf16[128,2176]{1,0:T(8,128)(2,1)S(1)} %constant_dynamic-update-slice_fusion.near_ref, bf16[128,2176]{1,0:T(8,128)(2,1)S(1)} %collective-permute-done.13.far_ref, bf16[704,2048]{1,0:T(8,128)(2,1)S(1)} %bitcast.96, ...), custom_call_target="tpu_custom_call" | custom-call | flops 2214592512 | bytes 10813440 | tf_op jit(solution)/shard_map/pallas_call | solution.py:142
  99.3 3.2 %shard_map.145 = (bf16[4,64,1024]{2,1,0:T(8,128)(2,1)S(1)}, bf16[4,64,1024]{2,1,0:T(8,128)(2,1)S(1)}) custom-call(s32[2]{0:T(128)S(1)} %pad_add_fusion.place_ref, bf16[128,2176]{1,0:T(8,128)(2,1)S(1)} %collective-permute-done.14.near_ref, bf16[128,2176]{1,0:T(8,128)(2,1)S(1)} %collective-permute-done.15.far_ref, bf16[704,2048]{1,0:T(8,128)(2,1)S(1)} %bitcast.97, ...), custom_call_target="tpu_custom_call" | custom-call | flops 2214592512 | bytes 10813440 | tf_op jit(solution)/shard_map/pallas_call | solution.py:142
  104.7 3.2 %shard_map.146 = (bf16[4,64,1024]{2,1,0:T(8,128)(2,1)S(1)}, bf16[4,64,1024]{2,1,0:T(8,128)(2,1)S(1)}) custom-call(s32[2]{0:T(128)S(1)} %pad_add_fusion.place_ref, bf16[256,2176]{1,0:T(8,128)(2,1)S(1)} %constant_dynamic-update-slice_fusion.4.near_ref, bf16[256,2176]{1,0:T(8,128)(2,1)S(1)} %collective-permute-done.21.far_ref, bf16[704,2048]{1,0:T(8,128)(2,1)S(1)} %bitcast.98, ...), custom_call_target="tpu_custom_call" | custom-call | flops 2214592512 | bytes 11927552 | tf_op jit(solution)/shard_map/pallas_call | solution.py:142
  108.2 3.2 %shard_map.147 = (bf16[4,64,1024]{2,1,0:T(8,128)(2,1)S(1)}, bf16[4,64,1024]{2,1,0:T(8,128)(2,1)S(1)}) custom-call(s32[2]{0:T(128)S(1)} %pad_add_fusion.place_ref, bf16[256,2176]{1,0:T(8,128)(2,1)S(1)} %collective-permute-done.22.near_ref, bf16[256,2176]{1,0:T(8,128)(2,1)S(1)} %collective-permute-done.23.far_ref, bf16[704,2048]{1,0:T(8,128)(2,1)S(1)} %bitcast.99, ...), custom_call_target="tpu_custom_call" | custom-call | flops 2214592512 | bytes 11927552 | tf_op jit(solution)/shard_map/pallas_call | solution.py:142
  114.8 3.4 %shard_map.148 = (bf16[4,64,1024]{2,1,0:T(8,128)(2,1)S(1)}, bf16[4,64,1024]{2,1,0:T(8,128)(2,1)S(1)}) custom-call(s32[2]{0:T(128)S(1)} %pad_add_fusion.place_ref, bf16[128,2176]{1,0:T(8,128)(2,1)S(1)} %constant_dynamic-update-slice_fusion.7.near_ref, bf16[128,2176]{1,0:T(8,128)(2,1)S(1)} %collective-permute-done.24.far_ref, bf16[704,2048]{1,0:T(8,128)(2,1)S(1)} %bitcast.100, ...), custom_call_target="tpu_custom_call" | custom-call | flops 2214592512 | bytes 10813440 | tf_op jit(solution)/shard_map/pallas_call | solution.py:142
  118.6 3.2 %shard_map.149 = (bf16[4,64,1024]{2,1,0:T(8,128)(2,1)S(1)}, bf16[4,64,1024]{2,1,0:T(8,128)(2,1)S(1)}) custom-call(s32[2]{0:T(128)S(1)} %pad_add_fusion.place_ref, bf16[128,2176]{1,0:T(8,128)(2,1)S(1)} %collective-permute-done.25.near_ref, bf16[128,2176]{1,0:T(8,128)(2,1)S(1)} %collective-permute-done.28.far_ref, bf16[704,2048]{1,0:T(8,128)(2,1)S(1)} %bitcast.101, ...), custom_call_target="tpu_custom_call" | custom-call | flops 2214592512 | bytes 10813440 | tf_op jit(solution)/shard_map/pallas_call | solution.py:142
  122.1 3.2 %shard_map.150 = (bf16[4,64,1024]{2,1,0:T(8,128)(2,1)S(1)}, bf16[4,64,1024]{2,1,0:T(8,128)(2,1)S(1)}) custom-call(s32[2]{0:T(128)S(1)} %pad_add_fusion.place_ref, bf16[256,2176]{1,0:T(8,128)(2,1)S(1)} %constant_dynamic-update-slice_fusion.4.near_ref, bf16[256,2176]{1,0:T(8,128)(2,1)S(1)} %collective-permute-done.21.far_ref, bf16[704,2048]{1,0:T(8,128)(2,1)S(1)} %bitcast.102, ...), custom_call_target="tpu_custom_call" | custom-call | flops 2214592512 | bytes 11927552 | tf_op jit(solution)/shard_map/pallas_call | solution.py:142
  129.6 3.2 %shard_map.151 = (bf16[4,64,1024]{2,1,0:T(8,128)(2,1)S(1)}, bf16[4,64,1024]{2,1,0:T(8,128)(2,1)S(1)}) custom-call(s32[2]{0:T(128)S(1)} %pad_add_fusion.place_ref, bf16[256,2176]{1,0:T(8,128)(2,1)S(1)} %collective-permute-done.22.near_ref, bf16[256,2176]{1,0:T(8,128)(2,1)S(1)} %collective-permute-done.23.far_ref, bf16[704,2048]{1,0:T(8,128)(2,1)S(1)} %bitcast.103, ...), custom_call_target="tpu_custom_call" | custom-call | flops 2214592512 | bytes 11927552 | tf_op jit(solution)/shard_map/pallas_call | solution.py:142
  132.9 3.3 %collective-permute-done.35 = bf16[2,64,1024]{2,1,0:T(8,128)(2,1)S(1)} collective-permute-done((bf16[2,64,1024]{2,1,0:T(8,128)(2,1)S(1)}, bf16[2,64,1024]{2,1,0:T(8,128)(2,1)S(1)}, u32[]{:S(2)}, u32[]{:S(2)}) %collective-permute-start.35) | collective-permute-done | bytes 262176 | tf_op jit(solution)/shard_map/scatter_first_1/ppermute | solution.py:171
  136.3 1.8 %collective-permute-done.32 = bf16[2,2,64,1024]{3,2,1,0:T(8,128)(2,1)S(1)} collective-permute-done((bf16[2,2,64,1024]{3,2,1,0:T(8,128)(2,1)S(1)}, bf16[2,2,64,1024]{3,2,1,0:T(8,128)(2,1)S(1)}, u32[]{:S(2)}, u32[]{:S(2)}) %collective-permute-start.32) | collective-permute-done | bytes 524320 | tf_op jit(solution)/shard_map/scatter_second_2/ppermute | solution.py:171
  141.1 9.8 %collective-permute-done.40 = bf16[2,2,64,1024]{3,2,1,0:T(8,128)(2,1)S(1)} collective-permute-done((bf16[2,2,64,1024]{3,2,1,0:T(8,128)(2,1)S(1)}, bf16[2,2,64,1024]{3,2,1,0:T(8,128)(2,1)S(1)}, u32[]{:S(2)}, u32[]{:S(2)}) %collective-permute-start.40) | collective-permute-done | bytes 524320 | tf_op jit(solution)/shard_map/scatter_second_3/ppermute | solution.py:171
  154.1 3.6 %collective-permute-done.41 = bf16[2,64,1024]{2,1,0:T(8,128)(2,1)S(1)} collective-permute-done((bf16[2,64,1024]{2,1,0:T(8,128)(2,1)S(1)}, bf16[2,64,1024]{2,1,0:T(8,128)(2,1)S(1)}, u32[]{:S(2)}, u32[]{:S(2)}) %collective-permute-start.41) | collective-permute-done | bytes 262176 | tf_op jit(solution)/shard_map/scatter_first_3/ppermute | solution.py:171
  160.8 5.1 %collective-permute-done.37 = bf16[128,1024]{1,0:T(8,128)(2,1)S(1)} collective-permute-done((bf16[128,1024]{1,0:T(8,128)(2,1)}, bf16[128,1024]{1,0:T(8,128)(2,1)S(1)}, u32[]{:S(2)}, u32[]{:S(2)}) %collective-permute-start.37) | collective-permute-done | bytes 262176 | tf_op jit(solution)/shard_map/to_plane_2/ppermute | solution.py:41
  165.9 4.7 %collective-permute-done.42 = bf16[128,1024]{1,0:T(8,128)(2,1)S(1)} collective-permute-done((bf16[128,1024]{1,0:T(8,128)(2,1)}, bf16[128,1024]{1,0:T(8,128)(2,1)S(1)}, u32[]{:S(2)}, u32[]{:S(2)}) %collective-permute-start.42) | collective-permute-done | bytes 262176 | tf_op jit(solution)/shard_map/to_plane_3/ppermute | solution.py:41
  (156 shorter events, 41.4 us)
Async XLA Ops:
  4.5 11.6 %collective-permute-start = (bf16[128,1024]{1,0:T(8,128)(2,1)S(1)}, bf16[128,1024]{1,0:T(8,128)(2,1)S(1)}, u32[]{:S(2)}, u32[]{:S(2)}) collective-permute-start(bf16[128,1024]{1,0:T(8,128)(2,1)S(1)} %get-tuple-element.44.rest_0_), channel_id=1, source_target_pairs={{0,4},{1,5},{2,6},{3,7},{4,8},{5,9},{6,10},{7,11},{8,12},{9,13},{1... | collective-permute-start | bytes 786440 | tf_op jit(solution)/shard_map/ppermute | solution.py:27
  9.4 11.9 %collective-permute-start.4 = (bf16[128,1024]{1,0:T(8,128)(2,1)}, bf16[128,1024]{1,0:T(8,128)(2,1)S(1)}, u32[]{:S(2)}, u32[]{:S(2)}) collective-permute-start(bf16[128,1024]{1,0:T(8,128)(2,1)} %rest_0_), channel_id=1, source_target_pairs={{0,4},{1,5},{2,6},{3,7},{4,8},{5,9},{6,10},{7,11},{8,12},{9,13},{1... | collective-permute-start | bytes 786440 | tf_op jit(solution)/shard_map/ppermute | solution.py:27
  16.9 9.8 %collective-permute-start.3 = (bf16[128,1024]{1,0:T(8,128)(2,1)S(1)}, bf16[128,1024]{1,0:T(8,128)(2,1)S(1)}, u32[]{:S(2)}, u32[]{:S(2)}) collective-permute-start(bf16[128,1024]{1,0:T(8,128)(2,1)S(1)} %get-tuple-element.101), channel_id=1, source_target_pairs={{0,3},{1,2},{2,1},{3,0},{4,7},{5,6},{6,5},{7,4},{8,11},{9,10},{10,... | collective-permute-start | bytes 786440 | tf_op jit(solution)/shard_map/ppermute | solution.py:22
  20.2 15.1 %collective-permute-start.2 = (bf16[128,1024]{1,0:T(8,128)(2,1)}, bf16[128,1024]{1,0:T(8,128)(2,1)S(1)}, u32[]{:S(2)}, u32[]{:S(2)}) collective-permute-start(bf16[128,1024]{1,0:T(8,128)(2,1)} %get-tuple-element.102), channel_id=1, source_target_pairs={{0,2},{1,3},{2,0},{3,1},{4,6},{5,7},{6,4},{7,5},{8,10},{9,11},{10,... | collective-permute-start | bytes 786440 | tf_op jit(solution)/shard_map/ppermute | solution.py:22
  20.7 14.6 %collective-permute-start.1 = (bf16[128,1024]{1,0:T(8,128)(2,1)}, bf16[128,1024]{1,0:T(8,128)(2,1)S(1)}, u32[]{:S(2)}, u32[]{:S(2)}) collective-permute-start(bf16[128,1024]{1,0:T(8,128)(2,1)} %get-tuple-element.103), channel_id=1, source_target_pairs={{0,1},{1,0},{2,3},{3,2},{4,5},{5,4},{6,7},{7,6},{8,9},{9,8},{10,11... | collective-permute-start | bytes 786440 | tf_op jit(solution)/shard_map/ppermute | solution.py:22
  22.3 15.7 %collective-permute-start.7 = (bf16[128,1024]{1,0:T(8,128)(2,1)}, bf16[128,1024]{1,0:T(8,128)(2,1)S(1)}, u32[]{:S(2)}, u32[]{:S(2)}) collective-permute-start(bf16[128,1024]{1,0:T(8,128)(2,1)} %get-tuple-element.98), channel_id=1, source_target_pairs={{0,3},{1,2},{2,1},{3,0},{4,7},{5,6},{6,5},{7,4},{8,11},{9,10},{10,... | collective-permute-start | bytes 786440 | tf_op jit(solution)/shard_map/ppermute | solution.py:22
  24.7 16.0 %collective-permute-start.6 = (bf16[128,1024]{1,0:T(8,128)(2,1)}, bf16[128,1024]{1,0:T(8,128)(2,1)S(1)}, u32[]{:S(2)}, u32[]{:S(2)}) collective-permute-start(bf16[128,1024]{1,0:T(8,128)(2,1)} %get-tuple-element.99), channel_id=1, source_target_pairs={{0,2},{1,3},{2,0},{3,1},{4,6},{5,7},{6,4},{7,5},{8,10},{9,11},{10,... | collective-permute-start | bytes 786440 | tf_op jit(solution)/shard_map/ppermute | solution.py:22
  26.8 14.0 %collective-permute-start.5 = (bf16[128,1024]{1,0:T(8,128)(2,1)}, bf16[128,1024]{1,0:T(8,128)(2,1)S(1)}, u32[]{:S(2)}, u32[]{:S(2)}) collective-permute-start(bf16[128,1024]{1,0:T(8,128)(2,1)} %get-tuple-element.100), channel_id=1, source_target_pairs={{0,1},{1,0},{2,3},{3,2},{4,5},{5,4},{6,7},{7,6},{8,9},{9,8},{10,11... | collective-permute-start | bytes 786440 | tf_op jit(solution)/shard_map/ppermute | solution.py:22
  48.2 11.6 %collective-permute-start.10 = (bf16[64,2176]{1,0:T(8,128)(2,1)S(1)}, bf16[64,2176]{1,0:T(8,128)(2,1)S(1)}, u32[]{:S(2)}, u32[]{:S(2)}) collective-permute-start(bf16[64,2176]{1,0:T(8,128)(2,1)S(1)} %get-tuple-element.50), channel_id=1, source_target_pairs={{4,0},{5,1},{6,2},{7,3},{8,4},{9,5},{10,6},{11,7},{12,8},{13,9},{1... | collective-permute-start | bytes 835592 | tf_op jit(solution)/shard_map/from_plane_1/ppermute | solution.py:33
  52.7 13.1 %collective-permute-start.11 = (bf16[64,2176]{1,0:T(8,128)(2,1)S(1)}, bf16[64,2176]{1,0:T(8,128)(2,1)S(1)}, u32[]{:S(2)}, u32[]{:S(2)}) collective-permute-start(bf16[64,2176]{1,0:T(8,128)(2,1)S(1)} %get-tuple-element.50), channel_id=1, source_target_pairs={{12,0},{13,1},{14,2},{15,3},{0,4},{1,5},{2,6},{3,7},{4,8},{5,9},{6... | collective-permute-start | bytes 835592 | tf_op jit(solution)/shard_map/from_plane_3/ppermute | solution.py:33
  52.8 14.8 %collective-permute-start.9 = (bf16[64,2176]{1,0:T(8,128)(2,1)S(1)}, bf16[64,2176]{1,0:T(8,128)(2,1)S(1)}, u32[]{:S(2)}, u32[]{:S(2)}) collective-permute-start(bf16[64,2176]{1,0:T(8,128)(2,1)S(1)} %get-tuple-element.50), channel_id=1, source_target_pairs={{0,1},{1,0},{2,3},{3,2},{4,5},{5,4},{6,7},{7,6},{8,9},{9,8},{10,11... | collective-permute-start | bytes 835592 | tf_op jit(solution)/shard_map/gather_first_0/ppermute | solution.py:171
  65.9 15.6 %collective-permute-start.18 = (bf16[128,2176]{1,0:T(8,128)(2,1)S(1)}, bf16[128,2176]{1,0:T(8,128)(2,1)S(1)}, u32[]{:S(2)}, u32[]{:S(2)}) collective-permute-start(bf16[128,2176]{1,0:T(8,128)(2,1)S(1)} %get-tuple-element.105), channel_id=1, source_target_pairs={{0,1},{1,0},{2,3},{3,2},{4,5},{5,4},{6,7},{7,6},{8,9},{9,8},{10,11... | collective-permute-start | bytes 1671176 | tf_op jit(solution)/shard_map/gather_first_1/ppermute | solution.py:171
  67.6 15.2 %collective-permute-start.13 = (bf16[128,2176]{1,0:T(8,128)(2,1)S(1)}, bf16[128,2176]{1,0:T(8,128)(2,1)S(1)}, u32[]{:S(2)}, u32[]{:S(2)}) collective-permute-start(bf16[128,2176]{1,0:T(8,128)(2,1)S(1)} %constant_dynamic-update-slice_fusion.near_ref), channel_id=1, source_target_pairs={{0,2},{1,3},{2,0},{3,1},{4,6},{5,7},{6,4},{7,5},{8,10},{9,11},{10,... | collective-permute-start | bytes 1671176 | tf_op jit(solution)/shard_map/gather_second_0/ppermute | solution.py:171
  81.5 21.1 %collective-permute-start.21 = (bf16[256,2176]{1,0:T(8,128)(2,1)S(1)}, bf16[256,2176]{1,0:T(8,128)(2,1)S(1)}, u32[]{:S(2)}, u32[]{:S(2)}) collective-permute-start(bf16[256,2176]{1,0:T(8,128)(2,1)S(1)} %constant_dynamic-update-slice_fusion.4.near_ref), channel_id=1, source_target_pairs={{0,2},{1,3},{2,0},{3,1},{4,6},{5,7},{6,4},{7,5},{8,10},{9,11},{10,... | collective-permute-start | bytes 3342344 | tf_op jit(solution)/shard_map/gather_second_1/ppermute | solution.py:171
  82.0 12.4 %collective-permute-start.12 = (bf16[64,2176]{1,0:T(8,128)(2,1)S(1)}, bf16[64,2176]{1,0:T(8,128)(2,1)S(1)}, u32[]{:S(2)}, u32[]{:S(2)}) collective-permute-start(bf16[64,2176]{1,0:T(8,128)(2,1)S(1)} %get-tuple-element.50), channel_id=1, source_target_pairs={{8,0},{9,1},{10,2},{11,3},{12,4},{13,5},{14,6},{15,7},{0,8},{1,9},... | collective-permute-start | bytes 835592 | tf_op jit(solution)/shard_map/from_plane_2/ppermute | solution.py:33
  82.8 15.2 %collective-permute-start.14 = (bf16[128,2176]{1,0:T(8,128)(2,1)S(1)}, bf16[128,2176]{1,0:T(8,128)(2,1)S(1)}, u32[]{:S(2)}, u32[]{:S(2)}) collective-permute-start(bf16[128,2176]{1,0:T(8,128)(2,1)S(1)} %constant_dynamic-update-slice_fusion.near_ref), channel_id=1, source_target_pairs={{16,0},{0,16},{17,1},{1,17},{18,2},{2,18},{19,3},{3,19},{20,4},{4,... | collective-permute-start | bytes 1671176 | tf_op jit(solution)/shard_map/ppermute | solution.py:48
  82.8 16.5 %collective-permute-start.15 = (bf16[128,2176]{1,0:T(8,128)(2,1)S(1)}, bf16[128,2176]{1,0:T(8,128)(2,1)S(1)}, u32[]{:S(2)}, u32[]{:S(2)}) collective-permute-start(bf16[128,2176]{1,0:T(8,128)(2,1)S(1)} %collective-permute-done.13.far_ref), channel_id=1, source_target_pairs={{16,0},{0,16},{17,1},{1,17},{18,2},{2,18},{19,3},{3,19},{20,4},{4,... | collective-permute-start | bytes 1671176 | tf_op jit(solution)/shard_map/ppermute | solution.py:48
  94.4 13.8 %collective-permute-start.22 = (bf16[256,2176]{1,0:T(8,128)(2,1)S(1)}, bf16[256,2176]{1,0:T(8,128)(2,1)S(1)}, u32[]{:S(2)}, u32[]{:S(2)}) collective-permute-start(bf16[256,2176]{1,0:T(8,128)(2,1)S(1)} %constant_dynamic-update-slice_fusion.4.near_ref), channel_id=1, source_target_pairs={{16,0},{0,16},{17,1},{1,17},{18,2},{2,18},{19,3},{3,19},{20,4},{4,... | collective-permute-start | bytes 3342344 | tf_op jit(solution)/shard_map/ppermute | solution.py:48
  94.4 8.8 %collective-permute-start.19 = (bf16[64,2176]{1,0:T(8,128)(2,1)S(1)}, bf16[64,2176]{1,0:T(8,128)(2,1)S(1)}, u32[]{:S(2)}, u32[]{:S(2)}) collective-permute-start(bf16[64,2176]{1,0:T(8,128)(2,1)S(1)} %collective-permute-done.12), channel_id=1, source_target_pairs={{0,1},{1,0},{2,3},{3,2},{4,5},{5,4},{6,7},{7,6},{8,9},{9,8},{10,11... | collective-permute-start | bytes 835592 | tf_op jit(solution)/shard_map/gather_first_2/ppermute | solution.py:171
  103.2 15.4 %collective-permute-start.25 = (bf16[128,2176]{1,0:T(8,128)(2,1)S(1)}, bf16[128,2176]{1,0:T(8,128)(2,1)S(1)}, u32[]{:S(2)}, u32[]{:S(2)}) collective-permute-start(bf16[128,2176]{1,0:T(8,128)(2,1)S(1)} %constant_dynamic-update-slice_fusion.7.near_ref), channel_id=1, source_target_pairs={{16,0},{0,16},{17,1},{1,17},{18,2},{2,18},{19,3},{3,19},{20,4},{4,... | collective-permute-start | bytes 1671176 | tf_op jit(solution)/shard_map/ppermute | solution.py:48
  103.3 9.7 %collective-permute-start.24 = (bf16[128,2176]{1,0:T(8,128)(2,1)S(1)}, bf16[128,2176]{1,0:T(8,128)(2,1)S(1)}, u32[]{:S(2)}, u32[]{:S(2)}) collective-permute-start(bf16[128,2176]{1,0:T(8,128)(2,1)S(1)} %constant_dynamic-update-slice_fusion.7.near_ref), channel_id=1, source_target_pairs={{0,2},{1,3},{2,0},{3,1},{4,6},{5,7},{6,4},{7,5},{8,10},{9,11},{10,... | collective-permute-start | bytes 1671176 | tf_op jit(solution)/shard_map/gather_second_2/ppermute | solution.py:171
  111.9 10.2 %collective-permute-start.20 = (bf16[2,2,64,1024]{3,2,1,0:T(8,128)(2,1)S(1)}, bf16[2,2,64,1024]{3,2,1,0:T(8,128)(2,1)S(1)}, u32[]{:S(2)}, u32[]{:S(2)}) collective-permute-start(bf16[2,2,64,1024]{3,2,1,0:T(8,128)(2,1)S(1)} %pad_maximum_fusion.1), channel_id=1, source_target_pairs={{0,2},{1,3},{2,0},{3,1},{4,6},{5,7},{6,4},{7,5},{8,10},{9,11},{10,... | collective-permute-start | bytes 1572872 | tf_op jit(solution)/shard_map/scatter_second_0/ppermute | solution.py:171
  113.7 13.1 %collective-permute-start.30 = (bf16[2,2,64,1024]{3,2,1,0:T(8,128)(2,1)S(1)}, bf16[2,2,64,1024]{3,2,1,0:T(8,128)(2,1)S(1)}, u32[]{:S(2)}, u32[]{:S(2)}) collective-permute-start(bf16[2,2,64,1024]{3,2,1,0:T(8,128)(2,1)S(1)} %pad_maximum_fusion.2), channel_id=1, source_target_pairs={{0,2},{1,3},{2,0},{3,1},{4,6},{5,7},{6,4},{7,5},{8,10},{9,11},{10,... | collective-permute-start | bytes 1572872 | tf_op jit(solution)/shard_map/scatter_second_1/ppermute | solution.py:171
  118.2 10.1 %collective-permute-start.31 = (bf16[4,64,1024]{2,1,0:T(8,128)(2,1)S(1)}, bf16[4,64,1024]{2,1,0:T(8,128)(2,1)S(1)}, u32[]{:S(2)}, u32[]{:S(2)}) collective-permute-start(bf16[4,64,1024]{2,1,0:T(8,128)(2,1)S(1)} %get-tuple-element.69), channel_id=1, source_target_pairs={{16,0},{0,16},{17,1},{1,17},{18,2},{2,18},{19,3},{3,19},{20,4},{4,... | collective-permute-start | bytes 1572872 | tf_op jit(solution)/shard_map/ppermute | solution.py:48
  125.3 13.1 %collective-permute-start.39 = (bf16[4,64,1024]{2,1,0:T(8,128)(2,1)S(1)}, bf16[4,64,1024]{2,1,0:T(8,128)(2,1)S(1)}, u32[]{:S(2)}, u32[]{:S(2)}) collective-permute-start(bf16[4,64,1024]{2,1,0:T(8,128)(2,1)S(1)} %get-tuple-element.78), channel_id=1, source_target_pairs={{16,0},{0,16},{17,1},{1,17},{18,2},{2,18},{19,3},{3,19},{20,4},{4,... | collective-permute-start | bytes 1572872 | tf_op jit(solution)/shard_map/ppermute | solution.py:48
  127.1 9.2 %collective-permute-start.35 = (bf16[2,64,1024]{2,1,0:T(8,128)(2,1)S(1)}, bf16[2,64,1024]{2,1,0:T(8,128)(2,1)S(1)}, u32[]{:S(2)}, u32[]{:S(2)}) collective-permute-start(bf16[2,64,1024]{2,1,0:T(8,128)(2,1)S(1)} %pad_maximum_fusion.6), channel_id=1, source_target_pairs={{0,1},{1,0},{2,3},{3,2},{4,5},{5,4},{6,7},{7,6},{8,9},{9,8},{10,11... | collective-permute-start | bytes 786440 | tf_op jit(solution)/shard_map/scatter_first_1/ppermute | solution.py:171
  128.8 9.2 %collective-permute-start.32 = (bf16[2,2,64,1024]{3,2,1,0:T(8,128)(2,1)S(1)}, bf16[2,2,64,1024]{3,2,1,0:T(8,128)(2,1)S(1)}, u32[]{:S(2)}, u32[]{:S(2)}) collective-permute-start(bf16[2,2,64,1024]{3,2,1,0:T(8,128)(2,1)S(1)} %pad_maximum_fusion.3), channel_id=1, source_target_pairs={{0,2},{1,3},{2,0},{3,1},{4,6},{5,7},{6,4},{7,5},{8,10},{9,11},{10,... | collective-permute-start | bytes 1572872 | tf_op jit(solution)/shard_map/scatter_second_2/ppermute | solution.py:171
  138.9 12.1 %collective-permute-start.40 = (bf16[2,2,64,1024]{3,2,1,0:T(8,128)(2,1)S(1)}, bf16[2,2,64,1024]{3,2,1,0:T(8,128)(2,1)S(1)}, u32[]{:S(2)}, u32[]{:S(2)}) collective-permute-start(bf16[2,2,64,1024]{3,2,1,0:T(8,128)(2,1)S(1)} %pad_maximum_fusion.4), channel_id=1, source_target_pairs={{0,2},{1,3},{2,0},{3,1},{4,6},{5,7},{6,4},{7,5},{8,10},{9,11},{10,... | collective-permute-start | bytes 1572872 | tf_op jit(solution)/shard_map/scatter_second_3/ppermute | solution.py:171
  139.9 20.9 %collective-permute-start.36 = (bf16[128,1024]{1,0:T(8,128)(2,1)S(1)}, bf16[128,1024]{1,0:T(8,128)(2,1)S(1)}, u32[]{:S(2)}, u32[]{:S(2)}) collective-permute-start(bf16[128,1024]{1,0:T(8,128)(2,1)S(1)} %pad_maximum_fusion.9), channel_id=1, source_target_pairs={{0,4},{1,5},{2,6},{3,7},{4,8},{5,9},{6,10},{7,11},{8,12},{9,13},{1... | collective-permute-start | bytes 786440 | tf_op jit(solution)/shard_map/to_plane_1/ppermute | solution.py:41
  140.0 12.1 %collective-permute-start.33 = (bf16[2,64,1024]{2,1,0:T(8,128)(2,1)S(1)}, bf16[2,64,1024]{2,1,0:T(8,128)(2,1)S(1)}, u32[]{:S(2)}, u32[]{:S(2)}) collective-permute-start(bf16[2,64,1024]{2,1,0:T(8,128)(2,1)S(1)} %pad_maximum_fusion.7), channel_id=1, source_target_pairs={{0,1},{1,0},{2,3},{3,2},{4,5},{5,4},{6,7},{7,6},{8,9},{9,8},{10,11... | collective-permute-start | bytes 786440 | tf_op jit(solution)/shard_map/scatter_first_2/ppermute | solution.py:171
  152.9 13.0 %collective-permute-start.37 = (bf16[128,1024]{1,0:T(8,128)(2,1)}, bf16[128,1024]{1,0:T(8,128)(2,1)S(1)}, u32[]{:S(2)}, u32[]{:S(2)}) collective-permute-start(bf16[128,1024]{1,0:T(8,128)(2,1)} %pad_maximum_fusion.8), channel_id=1, source_target_pairs={{0,8},{1,9},{2,10},{3,11},{4,12},{5,13},{6,14},{7,15},{8,0},{9,1},... | collective-permute-start | bytes 786440 | tf_op jit(solution)/shard_map/to_plane_2/ppermute | solution.py:41
  158.4 12.2 %collective-permute-start.42 = (bf16[128,1024]{1,0:T(8,128)(2,1)}, bf16[128,1024]{1,0:T(8,128)(2,1)S(1)}, u32[]{:S(2)}, u32[]{:S(2)}) collective-permute-start(bf16[128,1024]{1,0:T(8,128)(2,1)} %pad_maximum_fusion.11), channel_id=1, source_target_pairs={{0,12},{1,13},{2,14},{3,15},{4,0},{5,1},{6,2},{7,3},{8,4},{9,5},{1... | collective-permute-start | bytes 786440 | tf_op jit(solution)/shard_map/to_plane_3/ppermute | solution.py:41
  (23 other events, 239.9 us)

commit v15 on v14

--- a/solution.py
+++ b/solution.py
@@ -346,24 +346,22 @@
             jnp.concatenate([from_plane(sent, ahead) if ahead else sent for ahead in group])
         )
         sent = after(payload, columns[-1])
-    for number, column in enumerate(columns):
-        if number > 1:
-            column = after(column, nears[-1])
-        nears.append(
-            jnp.concatenate([column, crossed(column, True, f"gather_first_{number}")])
-        )
-        fars.append(crossed(nears[-1], False, f"gather_second_{number}"))
     def rows_of_cores(number, *waits):
         near, far = nears[number], after(fars[number], *waits)
         return [
             (from_core(near, i), from_core(far, i)) if i else (near, far) for i in range(cores)
         ]
 
-    outs = run(rows=rows_of_cores(0), planes=1, plane=0, span=1, waits={0: [columns[2]]})
+    def gather(number, *waits):
+        column = after(columns[number], *waits)
+        got = crossed(column, True, f"gather_first_{number}")
+        nears.append(jnp.concatenate([column, got]))
+        fars.append(crossed(nears[-1], False, f"gather_second_{number}"))
+
+    gather(0)
+    gather(1, nears[0], fars[0])
+    outs = run(rows=rows_of_cores(0), planes=1, plane=0, span=1, waits={})
     own_totals = core_totals(outs, cores)
-    sent = after(second_share(own_totals), nears[-1])
-    own_second = crossed(sent, False, "scatter_second_0")
-    own_totals = merged(own_totals, own_second, 2)
     seconds, firsts, flips, returned = [], [], [], []
     span_of = 1 if planes <= 4 else 8
     steps = [
@@ -371,7 +369,6 @@
         for number, group in enumerate(groups)
         for plane in range(0, len(group), span_of)
     ]
-    steps.sort(key=lambda step: step[2][0])
     for number, plane, aheads in steps[1:]:
         waits = {0: [outs], cores - 1: [*seconds[-1:]]}
         if len(seconds) > 1:
@@ -385,6 +382,11 @@
             span=len(aheads),
             waits=waits,
         )
+        if len(seconds) == 0:
+            gather(2, nears[1], outs[0])
+            sent = after(second_share(own_totals), nears[-1])
+            own_second = crossed(sent, False, "scatter_second_0")
+            own_totals = merged(own_totals, own_second, 2)
         totals = core_totals(outs, cores, *firsts[-1:], *flips[-2:-1])
         seconds.append(second_share(totals))
         got = crossed(seconds[-1], False, f"scatter_second_{aheads[0]}")

time: 172 us -> 175 us (1.017)
    ppermute x14, waiting for transfers between devices: 32 us -> 42.1 us  [crossed(): return lax.ppermute(block, ('tok', 'blk'), route)]
    ppermute x3, waiting for transfers between devices: 22.6 us -> 14.7 us  [from_plane(): lax.ppermute(block, 'blk', [((i + PLANE * ahead) % count, i) for i in ran...]
    ppermute x15, starting transfers between devices: 4.33 us -> 2.04 us  [from_core(): lax.ppermute(block, 'tok', [((i + ahead) % count, i) for i in range(count)])]
    unnamed x29 -> x28, local copies, waits for them, and re-layouts: 6.24 us -> 6.19 us
  transfers between devices with their start and end apart: 43 -> 43, of which waited for: 20 -> 23; matrix products, arithmetic and copies ran while one was open for 6% -> 7% of each run, Pallas kernels for 16% -> 16%
where the time goes in v15:
time: 175 us
  waiting for transfers between devices  80.5 us (46%)
  starting transfers between devices  42.7 us (24%)
  Pallas kernels  31.4 us (18%)
  other arithmetic  10.2 us (6%)
  local copies, waits for them, and re-layouts  8.66 us (5%)
    ppermute x14, waiting for transfers between devices, crossed(): return lax.ppermute(block, ('tok', 'blk'), route)  42.1 us
    pallas_call x12, Pallas kernels, local_call(): pl.pallas_call(body, in_specs=[scalar] * len(scalars) + [whole] * len(arr...  31.4 us
    ppermute x3, waiting for transfers between devices, from_plane(): lax.ppermute(block, 'blk', [((i + PLANE * ahead) % count, i) for i in ran...  14.7 us
    ppermute x14, starting transfers between devices, crossed(): return lax.ppermute(block, ('tok', 'blk'), route)  14 us
    ppermute x6, waiting for transfers between devices, flipped(): lax.ppermute(block, 'blk', [(i, i ^ mask) for i in range(lax.axis_size('b...  10.1 us
    ppermute x6, starting transfers between devices, flipped(): lax.ppermute(block, 'blk', [(i, i ^ mask) for i in range(lax.axis_size('b...  9.31 us
    ppermute x3, waiting for transfers between devices, to_plane(): lax.ppermute(block, 'blk', [(i, (i + PLANE * ahead) % count) for i in ran...  8.48 us
    ppermute x2, starting transfers between devices, next_plane(): lax.ppermute(block, 'blk', [(i, i + PLANE) for i in range(count - PLANE)])  8.43 us
  transfers between devices with their start and end apart: 43, of which 23 were waited for; matrix products, arithmetic and copies ran while one was open for 7% of the time, Pallas kernels for 16%

profile of v15, /device:TPU:0, one launch (start us, length us, event | category | flops | bytes accessed | tf_op | source)
XLA Modules:
  0.0 174.9 jit_solution(13635844111543837982)
XLA Ops:
  4.5 4.9 %collective-permute-start = (bf16[128,1024]{1,0:T(8,128)(2,1)S(1)}, bf16[128,1024]{1,0:T(8,128)(2,1)S(1)}, u32[]{:S(2)}, u32[]{:S(2)}) collective-permute-start(bf16[128,1024]{1,0:T(8,128)(2,1)S(1)} %get-tuple-element.44.rest_0_), channel_id=1, source_target_pairs={{0,4},{1,5},{2,6},{3,7},{4,8},{5,9},{6,10},{7,11},{8,12},{9,13},{1... | collective-permute-start | bytes 786440 | tf_op jit(solution)/shard_map/ppermute | solution.py:27
  9.4 3.5 %collective-permute-start.4 = (bf16[128,1024]{1,0:T(8,128)(2,1)}, bf16[128,1024]{1,0:T(8,128)(2,1)S(1)}, u32[]{:S(2)}, u32[]{:S(2)}) collective-permute-start(bf16[128,1024]{1,0:T(8,128)(2,1)} %rest_0_), channel_id=1, source_target_pairs={{0,4},{1,5},{2,6},{3,7},{4,8},{5,9},{6,10},{7,11},{8,12},{9,13},{1... | collective-permute-start | bytes 786440 | tf_op jit(solution)/shard_map/ppermute | solution.py:27
  13.7 2.4 %collective-permute-done.rest_1_ = bf16[128,1024]{1,0:T(8,128)(2,1)S(1)} collective-permute-done((bf16[128,1024]{1,0:T(8,128)(2,1)S(1)}, bf16[128,1024]{1,0:T(8,128)(2,1)S(1)}, u32[]{:S(2)}, u32[]{:S(2)}) %collective-permute-start) | collective-permute-done | bytes 262176 | tf_op jit(solution)/shard_map/ppermute | solution.py:27
  25.8 2.8 %collective-permute-start.7 = (bf16[128,1024]{1,0:T(8,128)(2,1)}, bf16[128,1024]{1,0:T(8,128)(2,1)S(1)}, u32[]{:S(2)}, u32[]{:S(2)}) collective-permute-start(bf16[128,1024]{1,0:T(8,128)(2,1)} %get-tuple-element.98), channel_id=1, source_target_pairs={{0,3},{1,2},{2,1},{3,0},{4,7},{5,6},{6,5},{7,4},{8,11},{9,10},{10,... | collective-permute-start | bytes 786440 | tf_op jit(solution)/shard_map/ppermute | solution.py:22
  30.7 2.4 %collective-permute-done.2.rest_3_ = bf16[128,1024]{1,0:T(8,128)(2,1)S(1)} collective-permute-done((bf16[128,1024]{1,0:T(8,128)(2,1)}, bf16[128,1024]{1,0:T(8,128)(2,1)S(1)}, u32[]{:S(2)}, u32[]{:S(2)}) %collective-permute-start.2) | collective-permute-done | bytes 262176 | tf_op jit(solution)/shard_map/ppermute | solution.py:22
  35.0 2.1 %collective-permute-done.5.rest_2_ = bf16[128,1024]{1,0:T(8,128)(2,1)S(1)} collective-permute-done((bf16[128,1024]{1,0:T(8,128)(2,1)}, bf16[128,1024]{1,0:T(8,128)(2,1)S(1)}, u32[]{:S(2)}, u32[]{:S(2)}) %collective-permute-start.5) | collective-permute-done | bytes 262176 | tf_op jit(solution)/shard_map/ppermute | solution.py:22
  37.1 5.0 %collective-permute-done.6.rest_3_ = bf16[128,1024]{1,0:T(8,128)(2,1)S(1)} collective-permute-done((bf16[128,1024]{1,0:T(8,128)(2,1)}, bf16[128,1024]{1,0:T(8,128)(2,1)S(1)}, u32[]{:S(2)}, u32[]{:S(2)}) %collective-permute-start.6) | collective-permute-done | bytes 262176 | tf_op jit(solution)/shard_map/ppermute | solution.py:22
  42.1 2.2 %copy-done.3 = bf16[1024,2048]{1,0:T(8,128)(2,1)S(1)} copy-done((bf16[1024,2048]{1,0:T(8,128)(2,1)S(1)}, bf16[1024,2048]{1,0:T(8,128)(2,1)}, u32[]{:S(2)}) %copy-start.3) | copy-done | bytes 4194328
  46.1 2.6 %collective-permute-done.8.rest_1_ = f32[128,2048]{1,0:T(8,128)S(1)} collective-permute-done((f32[128,2048]{1,0:T(8,128)S(1)}, f32[128,2048]{1,0:T(8,128)S(1)}, u32[]{:S(2)}, u32[]{:S(2)}) %collective-permute-start.8) | collective-permute-done | bytes 1048608 | tf_op jit(solution)/shard_map/ppermute | solution.py:48
  50.1 4.5 %collective-permute-start.15 = (bf16[64,2176]{1,0:T(8,128)(2,1)S(1)}, bf16[64,2176]{1,0:T(8,128)(2,1)S(1)}, u32[]{:S(2)}, u32[]{:S(2)}) collective-permute-start(bf16[64,2176]{1,0:T(8,128)(2,1)S(1)} %get-tuple-element.55), channel_id=1, source_target_pairs={{4,0},{5,1},{6,2},{7,3},{8,4},{9,5},{10,6},{11,7},{12,8},{13,9},{1... | collective-permute-start | bytes 835592 | tf_op jit(solution)/shard_map/from_plane_1/ppermute | solution.py:33
  57.8 3.9 %collective-permute-done.15 = bf16[64,2176]{1,0:T(8,128)(2,1)S(1)} collective-permute-done((bf16[64,2176]{1,0:T(8,128)(2,1)S(1)}, bf16[64,2176]{1,0:T(8,128)(2,1)S(1)}, u32[]{:S(2)}, u32[]{:S(2)}) %collective-permute-start.15) | collective-permute-done | bytes 278560 | tf_op jit(solution)/shard_map/from_plane_1/ppermute | solution.py:33
  61.8 6.7 %collective-permute-done.16 = bf16[64,2176]{1,0:T(8,128)(2,1)S(1)} collective-permute-done((bf16[64,2176]{1,0:T(8,128)(2,1)S(1)}, bf16[64,2176]{1,0:T(8,128)(2,1)S(1)}, u32[]{:S(2)}, u32[]{:S(2)}) %collective-permute-start.16) | collective-permute-done | bytes 278560 | tf_op jit(solution)/shard_map/from_plane_3/ppermute | solution.py:33
  69.6 8.4 %collective-permute-done.18 = bf16[128,2176]{1,0:T(8,128)(2,1)S(1)} collective-permute-done((bf16[128,2176]{1,0:T(8,128)(2,1)S(1)}, bf16[128,2176]{1,0:T(8,128)(2,1)S(1)}, u32[]{:S(2)}, u32[]{:S(2)}) %collective-permute-start.18) | collective-permute-done | bytes 557088 | tf_op jit(solution)/shard_map/gather_first_1/ppermute | solution.py:171
  78.7 3.2 %shard_map.144 = (bf16[4,64,1024]{2,1,0:T(8,128)(2,1)S(1)}, bf16[4,64,1024]{2,1,0:T(8,128)(2,1)S(1)}) custom-call(s32[2]{0:T(128)S(1)} %pad_add_fusion.place_ref, bf16[128,2176]{1,0:T(8,128)(2,1)S(1)} %pad_maximum_fusion.near_ref, bf16[128,2176]{1,0:T(8,128)(2,1)S(1)} %collective-permute-done.10.far_ref, bf16[704,2048]{1,0:T(8,128)(2,1)S(1)} %bitcast.95, ...), custom_call_target="tpu_custom_call" | custom-call | flops 2214592512 | bytes 10813440 | tf_op jit(solution)/shard_map/pallas_call | solution.py:142
  82.0 3.2 %shard_map.145 = (bf16[4,64,1024]{2,1,0:T(8,128)(2,1)S(1)}, bf16[4,64,1024]{2,1,0:T(8,128)(2,1)S(1)}) custom-call(s32[2]{0:T(128)S(1)} %pad_add_fusion.place_ref, bf16[128,2176]{1,0:T(8,128)(2,1)S(1)} %collective-permute-done.11.near_ref, bf16[128,2176]{1,0:T(8,128)(2,1)S(1)} %collective-permute-done.12.far_ref, bf16[704,2048]{1,0:T(8,128)(2,1)S(1)} %bitcast.96, ...), custom_call_target="tpu_custom_call" | custom-call | flops 2214592512 | bytes 10813440 | tf_op jit(solution)/shard_map/pallas_call | solution.py:142
  87.8 5.9 %collective-permute-done.19.far_ref = bf16[256,2176]{1,0:T(8,128)(2,1)S(1)} collective-permute-done((bf16[256,2176]{1,0:T(8,128)(2,1)S(1)}, bf16[256,2176]{1,0:T(8,128)(2,1)S(1)}, u32[]{:S(2)}, u32[]{:S(2)}) %collective-permute-start.19) | collective-permute-done | bytes 1114144 | tf_op jit(solution)/shard_map/gather_second_1/ppermute | solution.py:171
  94.0 3.2 %shard_map.146 = (bf16[4,64,1024]{2,1,0:T(8,128)(2,1)S(1)}, bf16[4,64,1024]{2,1,0:T(8,128)(2,1)S(1)}) custom-call(s32[2]{0:T(128)S(1)} %pad_add_fusion.place_ref, bf16[256,2176]{1,0:T(8,128)(2,1)S(1)} %constant_dynamic-update-slice_fusion.2.near_ref, bf16[256,2176]{1,0:T(8,128)(2,1)S(1)} %collective-permute-done.19.far_ref, bf16[704,2048]{1,0:T(8,128)(2,1)S(1)} %bitcast.97, ...), custom_call_target="tpu_custom_call" | custom-call | flops 2214592512 | bytes 11927552 | tf_op jit(solution)/shard_map/pallas_call | solution.py:142
  97.2 4.1 %collective-permute-done.17 = bf16[64,2176]{1,0:T(8,128)(2,1)S(1)} collective-permute-done((bf16[64,2176]{1,0:T(8,128)(2,1)S(1)}, bf16[64,2176]{1,0:T(8,128)(2,1)S(1)}, u32[]{:S(2)}, u32[]{:S(2)}) %collective-permute-start.17) | collective-permute-done | bytes 278560 | tf_op jit(solution)/shard_map/from_plane_2/ppermute | solution.py:33
  102.0 3.2 %shard_map.147 = (bf16[4,64,1024]{2,1,0:T(8,128)(2,1)S(1)}, bf16[4,64,1024]{2,1,0:T(8,128)(2,1)S(1)}) custom-call(s32[2]{0:T(128)S(1)} %pad_add_fusion.place_ref, bf16[256,2176]{1,0:T(8,128)(2,1)S(1)} %collective-permute-done.22.near_ref, bf16[256,2176]{1,0:T(8,128)(2,1)S(1)} %collective-permute-done.23.far_ref, bf16[704,2048]{1,0:T(8,128)(2,1)S(1)} %bitcast.98, ...), custom_call_target="tpu_custom_call" | custom-call | flops 2214592512 | bytes 11927552 | tf_op jit(solution)/shard_map/pallas_call | solution.py:142
  105.7 2.1 %collective-permute-done.20 = bf16[64,2176]{1,0:T(8,128)(2,1)S(1)} collective-permute-done((bf16[64,2176]{1,0:T(8,128)(2,1)S(1)}, bf16[64,2176]{1,0:T(8,128)(2,1)S(1)}, u32[]{:S(2)}, u32[]{:S(2)}) %collective-permute-start.20) | collective-permute-done | bytes 278560 | tf_op jit(solution)/shard_map/gather_first_2/ppermute | solution.py:171
  112.2 3.4 %shard_map.148 = (bf16[4,64,1024]{2,1,0:T(8,128)(2,1)S(1)}, bf16[4,64,1024]{2,1,0:T(8,128)(2,1)S(1)}) custom-call(s32[2]{0:T(128)S(1)} %pad_add_fusion.place_ref, bf16[256,2176]{1,0:T(8,128)(2,1)S(1)} %constant_dynamic-update-slice_fusion.2.near_ref, bf16[256,2176]{1,0:T(8,128)(2,1)S(1)} %collective-permute-done.19.far_ref, bf16[704,2048]{1,0:T(8,128)(2,1)S(1)} %bitcast.99, ...), custom_call_target="tpu_custom_call" | custom-call | flops 2214592512 | bytes 11927552 | tf_op jit(solution)/shard_map/pallas_call | solution.py:142
  115.7 1.9 %collective-permute-done.35.far_ref = bf16[128,2176]{1,0:T(8,128)(2,1)S(1)} collective-permute-done((bf16[128,2176]{1,0:T(8,128)(2,1)S(1)}, bf16[128,2176]{1,0:T(8,128)(2,1)S(1)}, u32[]{:S(2)}, u32[]{:S(2)}) %collective-permute-start.35) | collective-permute-done | bytes 557088 | tf_op jit(solution)/shard_map/gather_second_2/ppermute | solution.py:171
  117.6 3.2 %shard_map.149 = (bf16[4,64,1024]{2,1,0:T(8,128)(2,1)S(1)}, bf16[4,64,1024]{2,1,0:T(8,128)(2,1)S(1)}) custom-call(s32[2]{0:T(128)S(1)} %pad_add_fusion.place_ref, bf16[256,2176]{1,0:T(8,128)(2,1)S(1)} %collective-permute-done.22.near_ref, bf16[256,2176]{1,0:T(8,128)(2,1)S(1)} %collective-permute-done.23.far_ref, bf16[704,2048]{1,0:T(8,128)(2,1)S(1)} %bitcast.100, ...), custom_call_target="tpu_custom_call" | custom-call | flops 2214592512 | bytes 11927552 | tf_op jit(solution)/shard_map/pallas_call | solution.py:142
  120.8 2.4 %collective-permute-done.21 = bf16[2,2,64,1024]{3,2,1,0:T(8,128)(2,1)S(1)} collective-permute-done((bf16[2,2,64,1024]{3,2,1,0:T(8,128)(2,1)S(1)}, bf16[2,2,64,1024]{3,2,1,0:T(8,128)(2,1)S(1)}, u32[]{:S(2)}, u32[]{:S(2)}) %collective-permute-start.21) | collective-permute-done | bytes 524320 | tf_op jit(solution)/shard_map/scatter_second_0/ppermute | solution.py:171
  123.2 3.2 %shard_map.150 = (bf16[4,64,1024]{2,1,0:T(8,128)(2,1)S(1)}, bf16[4,64,1024]{2,1,0:T(8,128)(2,1)S(1)}) custom-call(s32[2]{0:T(128)S(1)} %pad_add_fusion.place_ref, bf16[128,2176]{1,0:T(8,128)(2,1)S(1)} %constant_dynamic-update-slice_fusion.4.near_ref, bf16[128,2176]{1,0:T(8,128)(2,1)S(1)} %collective-permute-done.35.far_ref, bf16[704,2048]{1,0:T(8,128)(2,1)S(1)} %bitcast.101, ...), custom_call_target="tpu_custom_call" | custom-call | flops 2214592512 | bytes 10813440 | tf_op jit(solution)/shard_map/pallas_call | solution.py:142
  126.4 2.4 %collective-permute-done.27 = bf16[2,2,64,1024]{3,2,1,0:T(8,128)(2,1)S(1)} collective-permute-done((bf16[2,2,64,1024]{3,2,1,0:T(8,128)(2,1)S(1)}, bf16[2,2,64,1024]{3,2,1,0:T(8,128)(2,1)S(1)}, u32[]{:S(2)}, u32[]{:S(2)}) %collective-permute-start.27) | collective-permute-done | bytes 524320 | tf_op jit(solution)/shard_map/scatter_second_1/ppermute | solution.py:171
  131.7 3.2 %shard_map.151 = (bf16[4,64,1024]{2,1,0:T(8,128)(2,1)S(1)}, bf16[4,64,1024]{2,1,0:T(8,128)(2,1)S(1)}) custom-call(s32[2]{0:T(128)S(1)} %pad_add_fusion.place_ref, bf16[128,2176]{1,0:T(8,128)(2,1)S(1)} %collective-permute-done.36.near_ref, bf16[128,2176]{1,0:T(8,128)(2,1)S(1)} %collective-permute-done.37.far_ref, bf16[704,2048]{1,0:T(8,128)(2,1)S(1)} %bitcast.102, ...), custom_call_target="tpu_custom_call" | custom-call | flops 2214592512 | bytes 10813440 | tf_op jit(solution)/shard_map/pallas_call | solution.py:142
  137.7 3.0 %collective-permute-done.29 = bf16[2,2,64,1024]{3,2,1,0:T(8,128)(2,1)S(1)} collective-permute-done((bf16[2,2,64,1024]{3,2,1,0:T(8,128)(2,1)S(1)}, bf16[2,2,64,1024]{3,2,1,0:T(8,128)(2,1)S(1)}, u32[]{:S(2)}, u32[]{:S(2)}) %collective-permute-start.29) | collective-permute-done | bytes 524320 | tf_op jit(solution)/shard_map/scatter_second_3/ppermute | solution.py:171
  144.4 9.0 %collective-permute-done.40 = bf16[2,2,64,1024]{3,2,1,0:T(8,128)(2,1)S(1)} collective-permute-done((bf16[2,2,64,1024]{3,2,1,0:T(8,128)(2,1)S(1)}, bf16[2,2,64,1024]{3,2,1,0:T(8,128)(2,1)S(1)}, u32[]{:S(2)}, u32[]{:S(2)}) %collective-permute-start.40) | collective-permute-done | bytes 524320 | tf_op jit(solution)/shard_map/scatter_second_2/ppermute | solution.py:171
  155.1 2.7 %collective-permute-start.34 = (bf16[128,1024]{1,0:T(8,128)(2,1)}, bf16[128,1024]{1,0:T(8,128)(2,1)S(1)}, u32[]{:S(2)}, u32[]{:S(2)}) collective-permute-start(bf16[128,1024]{1,0:T(8,128)(2,1)} %pad_maximum_fusion.9), channel_id=1, source_target_pairs={{0,12},{1,13},{2,14},{3,15},{4,0},{5,1},{6,2},{7,3},{8,4},{9,5},{1... | collective-permute-start | bytes 786440 | tf_op jit(solution)/shard_map/to_plane_3/ppermute | solution.py:41
  161.7 2.7 %collective-permute-done.31 = bf16[2,64,1024]{2,1,0:T(8,128)(2,1)S(1)} collective-permute-done((bf16[2,64,1024]{2,1,0:T(8,128)(2,1)}, bf16[2,64,1024]{2,1,0:T(8,128)(2,1)S(1)}, u32[]{:S(2)}, u32[]{:S(2)}) %collective-permute-start.31) | collective-permute-done | bytes 262176 | tf_op jit(solution)/shard_map/scatter_first_0/ppermute | solution.py:171
  164.7 8.2 %collective-permute-done.42 = bf16[128,1024]{1,0:T(8,128)(2,1)S(1)} collective-permute-done((bf16[128,1024]{1,0:T(8,128)(2,1)S(1)}, bf16[128,1024]{1,0:T(8,128)(2,1)S(1)}, u32[]{:S(2)}, u32[]{:S(2)}) %collective-permute-start.42) | collective-permute-done | bytes 262176 | tf_op jit(solution)/shard_map/to_plane_2/ppermute | solution.py:41
  (157 shorter events, 51.7 us)
Async XLA Ops:
  4.5 11.6 %collective-permute-start = (bf16[128,1024]{1,0:T(8,128)(2,1)S(1)}, bf16[128,1024]{1,0:T(8,128)(2,1)S(1)}, u32[]{:S(2)}, u32[]{:S(2)}) collective-permute-start(bf16[128,1024]{1,0:T(8,128)(2,1)S(1)} %get-tuple-element.44.rest_0_), channel_id=1, source_target_pairs={{0,4},{1,5},{2,6},{3,7},{4,8},{5,9},{6,10},{7,11},{8,12},{9,13},{1... | collective-permute-start | bytes 786440 | tf_op jit(solution)/shard_map/ppermute | solution.py:27
  9.4 11.9 %collective-permute-start.4 = (bf16[128,1024]{1,0:T(8,128)(2,1)}, bf16[128,1024]{1,0:T(8,128)(2,1)S(1)}, u32[]{:S(2)}, u32[]{:S(2)}) collective-permute-start(bf16[128,1024]{1,0:T(8,128)(2,1)} %rest_0_), channel_id=1, source_target_pairs={{0,4},{1,5},{2,6},{3,7},{4,8},{5,9},{6,10},{7,11},{8,12},{9,13},{1... | collective-permute-start | bytes 786440 | tf_op jit(solution)/shard_map/ppermute | solution.py:27
  17.0 8.9 %collective-permute-start.1 = (bf16[128,1024]{1,0:T(8,128)(2,1)S(1)}, bf16[128,1024]{1,0:T(8,128)(2,1)S(1)}, u32[]{:S(2)}, u32[]{:S(2)}) collective-permute-start(bf16[128,1024]{1,0:T(8,128)(2,1)S(1)} %get-tuple-element.103), channel_id=1, source_target_pairs={{0,1},{1,0},{2,3},{3,2},{4,5},{5,4},{6,7},{7,6},{8,9},{9,8},{10,11... | collective-permute-start | bytes 786440 | tf_op jit(solution)/shard_map/ppermute | solution.py:22
  19.3 13.8 %collective-permute-start.2 = (bf16[128,1024]{1,0:T(8,128)(2,1)}, bf16[128,1024]{1,0:T(8,128)(2,1)S(1)}, u32[]{:S(2)}, u32[]{:S(2)}) collective-permute-start(bf16[128,1024]{1,0:T(8,128)(2,1)} %get-tuple-element.102), channel_id=1, source_target_pairs={{0,2},{1,3},{2,0},{3,1},{4,6},{5,7},{6,4},{7,5},{8,10},{9,11},{10,... | collective-permute-start | bytes 786440 | tf_op jit(solution)/shard_map/ppermute | solution.py:22
  20.8 12.3 %collective-permute-start.3 = (bf16[128,1024]{1,0:T(8,128)(2,1)}, bf16[128,1024]{1,0:T(8,128)(2,1)S(1)}, u32[]{:S(2)}, u32[]{:S(2)}) collective-permute-start(bf16[128,1024]{1,0:T(8,128)(2,1)} %get-tuple-element.101), channel_id=1, source_target_pairs={{0,3},{1,2},{2,1},{3,0},{4,7},{5,6},{6,5},{7,4},{8,11},{9,10},{10,... | collective-permute-start | bytes 786440 | tf_op jit(solution)/shard_map/ppermute | solution.py:22
  22.2 14.8 %collective-permute-start.5 = (bf16[128,1024]{1,0:T(8,128)(2,1)}, bf16[128,1024]{1,0:T(8,128)(2,1)S(1)}, u32[]{:S(2)}, u32[]{:S(2)}) collective-permute-start(bf16[128,1024]{1,0:T(8,128)(2,1)} %get-tuple-element.100), channel_id=1, source_target_pairs={{0,1},{1,0},{2,3},{3,2},{4,5},{5,4},{6,7},{7,6},{8,9},{9,8},{10,11... | collective-permute-start | bytes 786440 | tf_op jit(solution)/shard_map/ppermute | solution.py:22
  23.7 18.4 %collective-permute-start.6 = (bf16[128,1024]{1,0:T(8,128)(2,1)}, bf16[128,1024]{1,0:T(8,128)(2,1)S(1)}, u32[]{:S(2)}, u32[]{:S(2)}) collective-permute-start(bf16[128,1024]{1,0:T(8,128)(2,1)} %get-tuple-element.99), channel_id=1, source_target_pairs={{0,2},{1,3},{2,0},{3,1},{4,6},{5,7},{6,4},{7,5},{8,10},{9,11},{10,... | collective-permute-start | bytes 786440 | tf_op jit(solution)/shard_map/ppermute | solution.py:22
  25.8 16.3 %collective-permute-start.7 = (bf16[128,1024]{1,0:T(8,128)(2,1)}, bf16[128,1024]{1,0:T(8,128)(2,1)S(1)}, u32[]{:S(2)}, u32[]{:S(2)}) collective-permute-start(bf16[128,1024]{1,0:T(8,128)(2,1)} %get-tuple-element.98), channel_id=1, source_target_pairs={{0,3},{1,2},{2,1},{3,0},{4,7},{5,6},{6,5},{7,4},{8,11},{9,10},{10,... | collective-permute-start | bytes 786440 | tf_op jit(solution)/shard_map/ppermute | solution.py:22
  50.1 11.6 %collective-permute-start.15 = (bf16[64,2176]{1,0:T(8,128)(2,1)S(1)}, bf16[64,2176]{1,0:T(8,128)(2,1)S(1)}, u32[]{:S(2)}, u32[]{:S(2)}) collective-permute-start(bf16[64,2176]{1,0:T(8,128)(2,1)S(1)} %get-tuple-element.55), channel_id=1, source_target_pairs={{4,0},{5,1},{6,2},{7,3},{8,4},{9,5},{10,6},{11,7},{12,8},{13,9},{1... | collective-permute-start | bytes 835592 | tf_op jit(solution)/shard_map/from_plane_1/ppermute | solution.py:33
  54.6 13.8 %collective-permute-start.16 = (bf16[64,2176]{1,0:T(8,128)(2,1)S(1)}, bf16[64,2176]{1,0:T(8,128)(2,1)S(1)}, u32[]{:S(2)}, u32[]{:S(2)}) collective-permute-start(bf16[64,2176]{1,0:T(8,128)(2,1)S(1)} %get-tuple-element.55), channel_id=1, source_target_pairs={{12,0},{13,1},{14,2},{15,3},{0,4},{1,5},{2,6},{3,7},{4,8},{5,9},{6... | collective-permute-start | bytes 835592 | tf_op jit(solution)/shard_map/from_plane_3/ppermute | solution.py:33
  56.2 12.3 %collective-permute-start.10 = (bf16[128,2176]{1,0:T(8,128)(2,1)S(1)}, bf16[128,2176]{1,0:T(8,128)(2,1)S(1)}, u32[]{:S(2)}, u32[]{:S(2)}) collective-permute-start(bf16[128,2176]{1,0:T(8,128)(2,1)S(1)} %pad_maximum_fusion.near_ref), channel_id=1, source_target_pairs={{0,2},{1,3},{2,0},{3,1},{4,6},{5,7},{6,4},{7,5},{8,10},{9,11},{10,... | collective-permute-start | bytes 1671176 | tf_op jit(solution)/shard_map/gather_second_0/ppermute | solution.py:171
  68.5 9.6 %collective-permute-start.18 = (bf16[128,2176]{1,0:T(8,128)(2,1)S(1)}, bf16[128,2176]{1,0:T(8,128)(2,1)S(1)}, u32[]{:S(2)}, u32[]{:S(2)}) collective-permute-start(bf16[128,2176]{1,0:T(8,128)(2,1)S(1)} %constant_dynamic-update-slice_fusion), channel_id=1, source_target_pairs={{0,1},{1,0},{2,3},{3,2},{4,5},{5,4},{6,7},{7,6},{8,9},{9,8},{10,11... | collective-permute-start | bytes 1671176 | tf_op jit(solution)/shard_map/gather_first_1/ppermute | solution.py:171
  69.1 12.9 %collective-permute-start.11 = (bf16[128,2176]{1,0:T(8,128)(2,1)S(1)}, bf16[128,2176]{1,0:T(8,128)(2,1)S(1)}, u32[]{:S(2)}, u32[]{:S(2)}) collective-permute-start(bf16[128,2176]{1,0:T(8,128)(2,1)S(1)} %pad_maximum_fusion.near_ref), channel_id=1, source_target_pairs={{16,0},{0,16},{17,1},{1,17},{18,2},{2,18},{19,3},{3,19},{20,4},{4,... | collective-permute-start | bytes 1671176 | tf_op jit(solution)/shard_map/ppermute | solution.py:48
  69.1 13.0 %collective-permute-start.12 = (bf16[128,2176]{1,0:T(8,128)(2,1)S(1)}, bf16[128,2176]{1,0:T(8,128)(2,1)S(1)}, u32[]{:S(2)}, u32[]{:S(2)}) collective-permute-start(bf16[128,2176]{1,0:T(8,128)(2,1)S(1)} %collective-permute-done.10.far_ref), channel_id=1, source_target_pairs={{16,0},{0,16},{17,1},{1,17},{18,2},{2,18},{19,3},{3,19},{20,4},{4,... | collective-permute-start | bytes 1671176 | tf_op jit(solution)/shard_map/ppermute | solution.py:48
  78.1 15.6 %collective-permute-start.19 = (bf16[256,2176]{1,0:T(8,128)(2,1)S(1)}, bf16[256,2176]{1,0:T(8,128)(2,1)S(1)}, u32[]{:S(2)}, u32[]{:S(2)}) collective-permute-start(bf16[256,2176]{1,0:T(8,128)(2,1)S(1)} %constant_dynamic-update-slice_fusion.2.near_ref), channel_id=1, source_target_pairs={{0,2},{1,3},{2,0},{3,1},{4,6},{5,7},{6,4},{7,5},{8,10},{9,11},{10,... | collective-permute-start | bytes 3342344 | tf_op jit(solution)/shard_map/gather_second_1/ppermute | solution.py:171
  85.8 15.5 %collective-permute-start.17 = (bf16[64,2176]{1,0:T(8,128)(2,1)S(1)}, bf16[64,2176]{1,0:T(8,128)(2,1)S(1)}, u32[]{:S(2)}, u32[]{:S(2)}) collective-permute-start(bf16[64,2176]{1,0:T(8,128)(2,1)S(1)} %get-tuple-element.55), channel_id=1, source_target_pairs={{8,0},{9,1},{10,2},{11,3},{12,4},{13,5},{14,6},{15,7},{0,8},{1,9},... | collective-permute-start | bytes 835592 | tf_op jit(solution)/shard_map/from_plane_2/ppermute | solution.py:33
  87.6 14.4 %collective-permute-start.22 = (bf16[256,2176]{1,0:T(8,128)(2,1)S(1)}, bf16[256,2176]{1,0:T(8,128)(2,1)S(1)}, u32[]{:S(2)}, u32[]{:S(2)}) collective-permute-start(bf16[256,2176]{1,0:T(8,128)(2,1)S(1)} %constant_dynamic-update-slice_fusion.2.near_ref), channel_id=1, source_target_pairs={{16,0},{0,16},{17,1},{1,17},{18,2},{2,18},{19,3},{3,19},{20,4},{4,... | collective-permute-start | bytes 3342344 | tf_op jit(solution)/shard_map/ppermute | solution.py:48
  93.7 8.3 %collective-permute-start.23 = (bf16[256,2176]{1,0:T(8,128)(2,1)S(1)}, bf16[256,2176]{1,0:T(8,128)(2,1)S(1)}, u32[]{:S(2)}, u32[]{:S(2)}) collective-permute-start(bf16[256,2176]{1,0:T(8,128)(2,1)S(1)} %collective-permute-done.19.far_ref), channel_id=1, source_target_pairs={{16,0},{0,16},{17,1},{1,17},{18,2},{2,18},{19,3},{3,19},{20,4},{4,... | collective-permute-start | bytes 3342344 | tf_op jit(solution)/shard_map/ppermute | solution.py:48
  101.9 8.2 %collective-permute-start.25 = (bf16[4,64,1024]{2,1,0:T(8,128)(2,1)S(1)}, bf16[4,64,1024]{2,1,0:T(8,128)(2,1)S(1)}, u32[]{:S(2)}, u32[]{:S(2)}) collective-permute-start(bf16[4,64,1024]{2,1,0:T(8,128)(2,1)S(1)} %get-tuple-element.60), channel_id=1, source_target_pairs={{16,0},{0,16},{17,1},{1,17},{18,2},{2,18},{19,3},{3,19},{20,4},{4,... | collective-permute-start | bytes 1572872 | tf_op jit(solution)/shard_map/ppermute | solution.py:48
  107.9 23.9 %collective-permute-start.36 = (bf16[128,2176]{1,0:T(8,128)(2,1)S(1)}, bf16[128,2176]{1,0:T(8,128)(2,1)S(1)}, u32[]{:S(2)}, u32[]{:S(2)}) collective-permute-start(bf16[128,2176]{1,0:T(8,128)(2,1)S(1)} %constant_dynamic-update-slice_fusion.4.near_ref), channel_id=1, source_target_pairs={{16,0},{0,16},{17,1},{1,17},{18,2},{2,18},{19,3},{3,19},{20,4},{4,... | collective-permute-start | bytes 1671176 | tf_op jit(solution)/shard_map/ppermute | solution.py:48
  108.0 9.6 %collective-permute-start.35 = (bf16[128,2176]{1,0:T(8,128)(2,1)S(1)}, bf16[128,2176]{1,0:T(8,128)(2,1)S(1)}, u32[]{:S(2)}, u32[]{:S(2)}) collective-permute-start(bf16[128,2176]{1,0:T(8,128)(2,1)S(1)} %constant_dynamic-update-slice_fusion.4.near_ref), channel_id=1, source_target_pairs={{0,2},{1,3},{2,0},{3,1},{4,6},{5,7},{6,4},{7,5},{8,10},{9,11},{10,... | collective-permute-start | bytes 1671176 | tf_op jit(solution)/shard_map/gather_second_2/ppermute | solution.py:171
  109.6 13.6 %collective-permute-start.21 = (bf16[2,2,64,1024]{3,2,1,0:T(8,128)(2,1)S(1)}, bf16[2,2,64,1024]{3,2,1,0:T(8,128)(2,1)S(1)}, u32[]{:S(2)}, u32[]{:S(2)}) collective-permute-start(bf16[2,2,64,1024]{3,2,1,0:T(8,128)(2,1)S(1)} %pad_maximum_fusion.2), channel_id=1, source_target_pairs={{0,2},{1,3},{2,0},{3,1},{4,6},{5,7},{6,4},{7,5},{8,10},{9,11},{10,... | collective-permute-start | bytes 1572872 | tf_op jit(solution)/shard_map/scatter_second_0/ppermute | solution.py:171
  110.6 18.2 %collective-permute-start.27 = (bf16[2,2,64,1024]{3,2,1,0:T(8,128)(2,1)S(1)}, bf16[2,2,64,1024]{3,2,1,0:T(8,128)(2,1)S(1)}, u32[]{:S(2)}, u32[]{:S(2)}) collective-permute-start(bf16[2,2,64,1024]{3,2,1,0:T(8,128)(2,1)S(1)} %pad_maximum_fusion.3), channel_id=1, source_target_pairs={{0,2},{1,3},{2,0},{3,1},{4,6},{5,7},{6,4},{7,5},{8,10},{9,11},{10,... | collective-permute-start | bytes 1572872 | tf_op jit(solution)/shard_map/scatter_second_1/ppermute | solution.py:171
  115.6 14.2 %collective-permute-start.28 = (bf16[4,64,1024]{2,1,0:T(8,128)(2,1)S(1)}, bf16[4,64,1024]{2,1,0:T(8,128)(2,1)S(1)}, u32[]{:S(2)}, u32[]{:S(2)}) collective-permute-start(bf16[4,64,1024]{2,1,0:T(8,128)(2,1)S(1)} %get-tuple-element.68), channel_id=1, source_target_pairs={{16,0},{0,16},{17,1},{1,17},{18,2},{2,18},{19,3},{3,19},{20,4},{4,... | collective-permute-start | bytes 1572872 | tf_op jit(solution)/shard_map/ppermute | solution.py:48
  117.6 14.2 %collective-permute-start.37 = (bf16[128,2176]{1,0:T(8,128)(2,1)S(1)}, bf16[128,2176]{1,0:T(8,128)(2,1)S(1)}, u32[]{:S(2)}, u32[]{:S(2)}) collective-permute-start(bf16[128,2176]{1,0:T(8,128)(2,1)S(1)} %collective-permute-done.35.far_ref), channel_id=1, source_target_pairs={{16,0},{0,16},{17,1},{1,17},{18,2},{2,18},{19,3},{3,19},{20,4},{4,... | collective-permute-start | bytes 1671176 | tf_op jit(solution)/shard_map/ppermute | solution.py:48
  128.8 12.3 %collective-permute-start.39 = (bf16[4,64,1024]{2,1,0:T(8,128)(2,1)S(1)}, bf16[4,64,1024]{2,1,0:T(8,128)(2,1)S(1)}, u32[]{:S(2)}, u32[]{:S(2)}) collective-permute-start(bf16[4,64,1024]{2,1,0:T(8,128)(2,1)S(1)} %get-tuple-element.78), channel_id=1, source_target_pairs={{16,0},{0,16},{17,1},{1,17},{18,2},{2,18},{19,3},{3,19},{20,4},{4,... | collective-permute-start | bytes 1572872 | tf_op jit(solution)/shard_map/ppermute | solution.py:48
  130.2 10.5 %collective-permute-start.29 = (bf16[2,2,64,1024]{3,2,1,0:T(8,128)(2,1)S(1)}, bf16[2,2,64,1024]{3,2,1,0:T(8,128)(2,1)S(1)}, u32[]{:S(2)}, u32[]{:S(2)}) collective-permute-start(bf16[2,2,64,1024]{3,2,1,0:T(8,128)(2,1)S(1)} %pad_maximum_fusion.4), channel_id=1, source_target_pairs={{0,2},{1,3},{2,0},{3,1},{4,6},{5,7},{6,4},{7,5},{8,10},{9,11},{10,... | collective-permute-start | bytes 1572872 | tf_op jit(solution)/shard_map/scatter_second_3/ppermute | solution.py:171
  141.4 12.1 %collective-permute-start.40 = (bf16[2,2,64,1024]{3,2,1,0:T(8,128)(2,1)S(1)}, bf16[2,2,64,1024]{3,2,1,0:T(8,128)(2,1)S(1)}, u32[]{:S(2)}, u32[]{:S(2)}) collective-permute-start(bf16[2,2,64,1024]{3,2,1,0:T(8,128)(2,1)S(1)} %pad_maximum_fusion.5), channel_id=1, source_target_pairs={{0,2},{1,3},{2,0},{3,1},{4,6},{5,7},{6,4},{7,5},{8,10},{9,11},{10,... | collective-permute-start | bytes 1572872 | tf_op jit(solution)/shard_map/scatter_second_2/ppermute | solution.py:171
  143.9 20.5 %collective-permute-start.33 = (bf16[128,1024]{1,0:T(8,128)(2,1)}, bf16[128,1024]{1,0:T(8,128)(2,1)}, u32[]{:S(2)}, u32[]{:S(2)}) collective-permute-start(bf16[128,1024]{1,0:T(8,128)(2,1)} %pad_maximum_fusion.10), channel_id=1, source_target_pairs={{0,4},{1,5},{2,6},{3,7},{4,8},{5,9},{6,10},{7,11},{8,12},{9,13},{1... | collective-permute-start | bytes 786440 | tf_op jit(solution)/shard_map/to_plane_1/ppermute | solution.py:41
  143.9 10.4 %collective-permute-start.30 = (bf16[2,64,1024]{2,1,0:T(8,128)(2,1)S(1)}, bf16[2,64,1024]{2,1,0:T(8,128)(2,1)S(1)}, u32[]{:S(2)}, u32[]{:S(2)}) collective-permute-start(bf16[2,64,1024]{2,1,0:T(8,128)(2,1)S(1)} %pad_maximum_fusion.8), channel_id=1, source_target_pairs={{0,1},{1,0},{2,3},{3,2},{4,5},{5,4},{6,7},{7,6},{8,9},{9,8},{10,11... | collective-permute-start | bytes 786440 | tf_op jit(solution)/shard_map/scatter_first_3/ppermute | solution.py:171
  155.1 9.6 %collective-permute-start.34 = (bf16[128,1024]{1,0:T(8,128)(2,1)}, bf16[128,1024]{1,0:T(8,128)(2,1)S(1)}, u32[]{:S(2)}, u32[]{:S(2)}) collective-permute-start(bf16[128,1024]{1,0:T(8,128)(2,1)} %pad_maximum_fusion.9), channel_id=1, source_target_pairs={{0,12},{1,13},{2,14},{3,15},{4,0},{5,1},{6,2},{7,3},{8,4},{9,5},{1... | collective-permute-start | bytes 786440 | tf_op jit(solution)/shard_map/to_plane_3/ppermute | solution.py:41
  160.3 12.7 %collective-permute-start.42 = (bf16[128,1024]{1,0:T(8,128)(2,1)S(1)}, bf16[128,1024]{1,0:T(8,128)(2,1)S(1)}, u32[]{:S(2)}, u32[]{:S(2)}) collective-permute-start(bf16[128,1024]{1,0:T(8,128)(2,1)S(1)} %pad_maximum_fusion.12), channel_id=1, source_target_pairs={{0,8},{1,9},{2,10},{3,11},{4,12},{5,13},{6,14},{7,15},{8,0},{9,1},... | collective-permute-start | bytes 786440 | tf_op jit(solution)/shard_map/to_plane_2/ppermute | solution.py:41
  (23 other events, 205.1 us)

commit v16 on v4

--- a/solution.py
+++ b/solution.py
@@ -72,7 +72,7 @@
             target[:, columns] = turned.astype(jnp.bfloat16)
 
 
-def score_kernel(place_ref, lengths_ref, q_ref, *rest):
+def score_kernel(place_ref, lengths_ref, q_ref, weight_ref, *rest):
     *keys, out_ref = rest
     rows, width = q_ref.shape
     shape = (rows, rows)
@@ -292,7 +292,7 @@
         score_kernel,
         [jax.ShapeDtypeStruct(probs_shape, jnp.bfloat16)],
         [place, prompt_lengths],
-        [rot_query, *key_blocks],
+        [rot_query, out_weight, *key_blocks],
         flops=2 * tok_rows * probs_shape[2] * heads * HEAD_DIM,
     )[0]
     page_count = tok_rows // PAGE
@@ -351,9 +351,13 @@
         outs = run(nears[number], fars[number], waits=waits)
         totals.append(core_totals(outs, cores))
         sents.append(second_share(totals[-1]))
-    gots = [crossed(sent, False) for sent in sents]
-    totals = [merged(*pair, 2) for pair in zip(totals, gots, strict=True)]
-    gots = [crossed(first_share(pair), True) for pair in totals]
+    got_list, ready = [], []
+    for pair, sent in zip(totals, sents, strict=True):
+        pair = merged(pair, after(crossed(sent, False), *ready), 2)
+        ready = [first_share(pair)]
+        got_list.append((pair, crossed(ready[0], True)))
+    totals = [pair for pair, _ in got_list]
+    gots = [got for _, got in got_list]
     results = {}
     for group, pair, came in zip(
         groups, [own_totals, *totals], [own_got, *gots], strict=True

time: 172 us -> 170 us (0.988)
  transfers between devices with their start and end apart: 39 -> 39, of which waited for: 21 -> 21; matrix products, arithmetic and copies ran while one was open for 7% -> 6% of each run, Pallas kernels for 15% -> 15%
where the time goes in v16:
time: 170 us
  waiting for transfers between devices  70.2 us (41%)
  starting transfers between devices  51.6 us (30%)
  Pallas kernels  29.7 us (17%)
  local copies, waits for them, and re-layouts  8.72 us (5%)
  other arithmetic  8.12 us (5%)
    ppermute x12, waiting for transfers between devices, crossed(): return lax.ppermute(block, ('tok', 'blk'), route)  39.6 us
    pallas_call x10, Pallas kernels, local_call(): pl.pallas_call(body, in_specs=[scalar] * len(scalars) + [whole] * len(arr...  29.7 us
    ppermute x12, starting transfers between devices, crossed(): return lax.ppermute(block, ('tok', 'blk'), route)  17.2 us
    ppermute x3, waiting for transfers between devices, to_plane(): lax.ppermute(block, 'blk', [(i, (i + PLANE * ahead) % count) for i in ran...  13.3 us
    ppermute x3, starting transfers between devices, to_plane(): lax.ppermute(block, 'blk', [(i, (i + PLANE * ahead) % count) for i in ran...  9.86 us
    ppermute x2, starting transfers between devices, next_plane(): lax.ppermute(block, 'blk', [(i, i + PLANE) for i in range(count - PLANE)])  8.43 us
    ppermute x6, starting transfers between devices, flipped(): lax.ppermute(block, 'blk', [(i, i ^ mask) for i in range(lax.axis_size('b...  8.32 us
    ppermute x6, waiting for transfers between devices, flipped(): lax.ppermute(block, 'blk', [(i, i ^ mask) for i in range(lax.axis_size('b...  7.49 us
  transfers between devices with their start and end apart: 39, of which 21 were waited for; matrix products, arithmetic and copies ran while one was open for 6% of the time, Pallas kernels for 15%

profile of v16, /device:TPU:0, one launch (start us, length us, event | category | flops | bytes accessed | tf_op | source)
XLA Modules:
  0.0 169.5 jit_solution(10202004890567132364)
XLA Ops:
  4.5 4.9 %collective-permute-start = (bf16[128,1024]{1,0:T(8,128)(2,1)S(1)}, bf16[128,1024]{1,0:T(8,128)(2,1)S(1)}, u32[]{:S(2)}, u32[]{:S(2)}) collective-permute-start(bf16[128,1024]{1,0:T(8,128)(2,1)S(1)} %get-tuple-element.30.rest_0_), channel_id=1, source_target_pairs={{0,4},{1,5},{2,6},{3,7},{4,8},{5,9},{6,10},{7,11},{8,12},{9,13},{1... | collective-permute-start | bytes 786440 | tf_op jit(solution)/shard_map/ppermute | solution.py:27
  9.4 3.5 %collective-permute-start.4 = (bf16[128,1024]{1,0:T(8,128)(2,1)}, bf16[128,1024]{1,0:T(8,128)(2,1)S(1)}, u32[]{:S(2)}, u32[]{:S(2)}) collective-permute-start(bf16[128,1024]{1,0:T(8,128)(2,1)} %rest_0_), channel_id=1, source_target_pairs={{0,4},{1,5},{2,6},{3,7},{4,8},{5,9},{6,10},{7,11},{8,12},{9,13},{1... | collective-permute-start | bytes 786440 | tf_op jit(solution)/shard_map/ppermute | solution.py:27
  13.7 2.4 %collective-permute-done.rest_1_ = bf16[128,1024]{1,0:T(8,128)(2,1)S(1)} collective-permute-done((bf16[128,1024]{1,0:T(8,128)(2,1)S(1)}, bf16[128,1024]{1,0:T(8,128)(2,1)S(1)}, u32[]{:S(2)}, u32[]{:S(2)}) %collective-permute-start) | collective-permute-done | bytes 262176 | tf_op jit(solution)/shard_map/ppermute | solution.py:27
  17.0 2.4 %collective-permute-start.3 = (bf16[128,1024]{1,0:T(8,128)(2,1)S(1)}, bf16[128,1024]{1,0:T(8,128)(2,1)S(1)}, u32[]{:S(2)}, u32[]{:S(2)}) collective-permute-start(bf16[128,1024]{1,0:T(8,128)(2,1)S(1)} %get-tuple-element.73), channel_id=1, source_target_pairs={{0,3},{1,2},{2,1},{3,0},{4,7},{5,6},{6,5},{7,4},{8,11},{9,10},{10,... | collective-permute-start | bytes 786440 | tf_op jit(solution)/shard_map/ppermute | solution.py:22
  22.3 2.4 %collective-permute-start.7 = (bf16[128,1024]{1,0:T(8,128)(2,1)}, bf16[128,1024]{1,0:T(8,128)(2,1)S(1)}, u32[]{:S(2)}, u32[]{:S(2)}) collective-permute-start(bf16[128,1024]{1,0:T(8,128)(2,1)} %get-tuple-element.70), channel_id=1, source_target_pairs={{0,3},{1,2},{2,1},{3,0},{4,7},{5,6},{6,5},{7,4},{8,11},{9,10},{10,... | collective-permute-start | bytes 786440 | tf_op jit(solution)/shard_map/ppermute | solution.py:22
  26.8 1.9 %collective-permute-start.5 = (bf16[128,1024]{1,0:T(8,128)(2,1)}, bf16[128,1024]{1,0:T(8,128)(2,1)S(1)}, u32[]{:S(2)}, u32[]{:S(2)}) collective-permute-start(bf16[128,1024]{1,0:T(8,128)(2,1)} %get-tuple-element.72), channel_id=1, source_target_pairs={{0,1},{1,0},{2,3},{3,2},{4,5},{5,4},{6,7},{7,6},{8,9},{9,8},{10,11... | collective-permute-start | bytes 786440 | tf_op jit(solution)/shard_map/ppermute | solution.py:22
  28.9 1.8 %scatter_fusion = bf16[8,16,2,1024]{3,1,2,0:T(8,128)(2,1)S(1)} fusion(bf16[8,16,2,1024]{3,1,2,0:T(8,128)(2,1)S(1)} %broadcast_in_dim.31, s32[8]{0:T(128)S(1)} %compare_select_fusion, bf16[8,16,2,1024]{3,1,2,0:T(8,128)(2,1)} %pad_maximum_fusion.2), kind=kCustom, calls=%fused_computation | custom fusion | bytes 1572896 | tf_op jit(solution)/shard_map/scatter | solution.py:301
  30.7 4.7 %collective-permute-done.2.rest_3_ = bf16[128,1024]{1,0:T(8,128)(2,1)S(1)} collective-permute-done((bf16[128,1024]{1,0:T(8,128)(2,1)}, bf16[128,1024]{1,0:T(8,128)(2,1)S(1)}, u32[]{:S(2)}, u32[]{:S(2)}) %collective-permute-start.2) | collective-permute-done | bytes 262176 | tf_op jit(solution)/shard_map/ppermute | solution.py:22
  35.4 2.2 %copy-done.3 = bf16[1024,2048]{1,0:T(8,128)(2,1)S(1)} copy-done((bf16[1024,2048]{1,0:T(8,128)(2,1)S(1)}, bf16[1024,2048]{1,0:T(8,128)(2,1)}, u32[]{:S(2)}) %copy-start.3) | copy-done | bytes 4194328
  37.6 1.9 %shard_map.141.prob_ref = bf16[8,128,640]{2,1,0:T(8,128)(2,1)S(1)} custom-call(s32[2]{0:T(128)S(1)} %pad_add_fusion.place_ref, s32[8]{0:T(128)S(1)} %copy-done.11, bf16[128,1024]{1,0:T(8,128)(2,1)S(1)} %get-tuple-element.29.q_ref, bf16[1024,2048]{1,0:T(8,128)(2,1)S(1)} %copy-done.3, bf16[128,1024]{1,0:T(8,128)(2,1)S(1)} %get-tuple-element.30.rest_0_, ...), custom_call_target="tpu_custom_call" | custom-call | flops 167772160 | bytes 7077888 | tf_op jit(solution)/shard_map/pallas_call | solution.py:140
  40.8 1.7 shard_map.142.rest_0_
  42.6 2.6 %collective-permute-done.8.rest_1_ = f32[128,2048]{1,0:T(8,128)S(1)} collective-permute-done((f32[128,2048]{1,0:T(8,128)S(1)}, f32[128,2048]{1,0:T(8,128)S(1)}, u32[]{:S(2)}, u32[]{:S(2)}) %collective-permute-start.8) | collective-permute-done | bytes 1048608 | tf_op jit(solution)/shard_map/ppermute | solution.py:46
  46.0 2.5 %collective-permute-start.17 = (bf16[64,2176]{1,0:T(8,128)(2,1)S(1)}, bf16[64,2176]{1,0:T(8,128)(2,1)S(1)}, u32[]{:S(2)}, u32[]{:S(2)}) collective-permute-start(bf16[64,2176]{1,0:T(8,128)(2,1)S(1)} %get-tuple-element.40), channel_id=1, source_target_pairs={{12,0},{13,1},{14,2},{15,3},{0,4},{1,5},{2,6},{3,7},{4,8},{5,9},{6... | collective-permute-start | bytes 835592 | tf_op jit(solution)/shard_map/ppermute | solution.py:32
  48.6 2.3 %collective-permute-start.16 = (bf16[64,2176]{1,0:T(8,128)(2,1)S(1)}, bf16[64,2176]{1,0:T(8,128)(2,1)S(1)}, u32[]{:S(2)}, u32[]{:S(2)}) collective-permute-start(bf16[64,2176]{1,0:T(8,128)(2,1)S(1)} %get-tuple-element.40), channel_id=1, source_target_pairs={{4,0},{5,1},{6,2},{7,3},{8,4},{9,5},{10,6},{11,7},{12,8},{13,9},{1... | collective-permute-start | bytes 835592 | tf_op jit(solution)/shard_map/ppermute | solution.py:32
  52.4 5.0 %collective-permute-done.9 = bf16[64,2176]{1,0:T(8,128)(2,1)S(1)} collective-permute-done((bf16[64,2176]{1,0:T(8,128)(2,1)S(1)}, bf16[64,2176]{1,0:T(8,128)(2,1)S(1)}, u32[]{:S(2)}, u32[]{:S(2)}) %collective-permute-start.9) | collective-permute-done | bytes 278560 | tf_op jit(solution)/shard_map/ppermute | solution.py:168
  59.8 3.1 %collective-permute-done.16 = bf16[64,2176]{1,0:T(8,128)(2,1)S(1)} collective-permute-done((bf16[64,2176]{1,0:T(8,128)(2,1)S(1)}, bf16[64,2176]{1,0:T(8,128)(2,1)S(1)}, u32[]{:S(2)}, u32[]{:S(2)}) %collective-permute-start.16) | collective-permute-done | bytes 278560 | tf_op jit(solution)/shard_map/ppermute | solution.py:32
  64.7 4.4 %collective-permute-done.10.far_ref = bf16[128,2176]{1,0:T(8,128)(2,1)S(1)} collective-permute-done((bf16[128,2176]{1,0:T(8,128)(2,1)S(1)}, bf16[128,2176]{1,0:T(8,128)(2,1)S(1)}, u32[]{:S(2)}, u32[]{:S(2)}) %collective-permute-start.10) | collective-permute-done | bytes 557088 | tf_op jit(solution)/shard_map/ppermute | solution.py:168
  69.0 3.6 %collective-permute-done.18 = bf16[128,2176]{1,0:T(8,128)(2,1)S(1)} collective-permute-done((bf16[128,2176]{1,0:T(8,128)(2,1)S(1)}, bf16[128,2176]{1,0:T(8,128)(2,1)S(1)}, u32[]{:S(2)}, u32[]{:S(2)}) %collective-permute-start.18) | collective-permute-done | bytes 557088 | tf_op jit(solution)/shard_map/ppermute | solution.py:168
  77.1 3.2 %shard_map.144 = (bf16[4,64,1024]{2,1,0:T(8,128)(2,1)S(1)}, bf16[4,64,1024]{2,1,0:T(8,128)(2,1)S(1)}) custom-call(s32[2]{0:T(128)S(1)} %pad_add_fusion.place_ref, bf16[128,2176]{1,0:T(8,128)(2,1)S(1)} %constant_dynamic-update-slice_fusion.near_ref, bf16[128,2176]{1,0:T(8,128)(2,1)S(1)} %collective-permute-done.10.far_ref, bf16[704,2048]{1,0:T(8,128)(2,1)S(1)} %bitcast.78, ...), custom_call_target="tpu_custom_call" | custom-call | flops 2214592512 | bytes 10813440 | tf_op jit(solution)/shard_map/pallas_call | solution.py:140
  80.9 3.2 %shard_map.145 = (bf16[4,64,1024]{2,1,0:T(8,128)(2,1)S(1)}, bf16[4,64,1024]{2,1,0:T(8,128)(2,1)S(1)}) custom-call(s32[2]{0:T(128)S(1)} %pad_add_fusion.place_ref, bf16[128,2176]{1,0:T(8,128)(2,1)S(1)} %collective-permute-done.11.near_ref, bf16[128,2176]{1,0:T(8,128)(2,1)S(1)} %collective-permute-done.12.far_ref, bf16[704,2048]{1,0:T(8,128)(2,1)S(1)} %bitcast.79, ...), custom_call_target="tpu_custom_call" | custom-call | flops 2214592512 | bytes 10813440 | tf_op jit(solution)/shard_map/pallas_call | solution.py:140
  86.8 4.4 %collective-permute-done.22.far_ref = bf16[256,2176]{1,0:T(8,128)(2,1)S(1)} collective-permute-done((bf16[256,2176]{1,0:T(8,128)(2,1)S(1)}, bf16[256,2176]{1,0:T(8,128)(2,1)S(1)}, u32[]{:S(2)}, u32[]{:S(2)}) %collective-permute-start.22) | collective-permute-done | bytes 1114144 | tf_op jit(solution)/shard_map/ppermute | solution.py:168
  93.1 5.7 %shard_map.146 = (bf16[4,128,1024]{2,1,0:T(8,128)(2,1)S(1)}, bf16[4,128,1024]{2,1,0:T(8,128)(2,1)S(1)}) custom-call(s32[2]{0:T(128)S(1)} %pad_add_fusion.place_ref, bf16[256,2176]{1,0:T(8,128)(2,1)S(1)} %constant_dynamic-update-slice_fusion.2.near_ref, bf16[256,2176]{1,0:T(8,128)(2,1)S(1)} %collective-permute-done.22.far_ref, ...), custom_call_target="tpu_custom_call" | custom-call | flops 4429185024 | bytes 12976128 | tf_op jit(solution)/shard_map/pallas_call | solution.py:140
  99.6 5.8 %shard_map.147 = (bf16[4,128,1024]{2,1,0:T(8,128)(2,1)S(1)}, bf16[4,128,1024]{2,1,0:T(8,128)(2,1)S(1)}) custom-call(s32[2]{0:T(128)S(1)} %pad_add_fusion.place_ref, bf16[256,2176]{1,0:T(8,128)(2,1)S(1)} %collective-permute-done.23.near_ref, bf16[256,2176]{1,0:T(8,128)(2,1)S(1)} %collective-permute-done.24.far_ref, bf16[704,2048]{1,0:T(8,128)(2,1)S(1)} %bitcast.81, ...), custom_call_target="tpu_custom_call" | custom-call | flops 4429185024 | bytes 12976128 | tf_op jit(solution)/shard_map/pallas_call | solution.py:140
  107.6 3.2 %shard_map.148 = (bf16[4,64,1024]{2,1,0:T(8,128)(2,1)S(1)}, bf16[4,64,1024]{2,1,0:T(8,128)(2,1)S(1)}) custom-call(s32[2]{0:T(128)S(1)} %pad_add_fusion.place_ref, bf16[128,2176]{1,0:T(8,128)(2,1)S(1)} %constant_dynamic-update-slice_fusion.5.near_ref, bf16[128,2176]{1,0:T(8,128)(2,1)S(1)} %collective-permute-done.30.far_ref, bf16[704,2048]{1,0:T(8,128)(2,1)S(1)} %bitcast.82, ...), custom_call_target="tpu_custom_call" | custom-call | flops 2214592512 | bytes 10813440 | tf_op jit(solution)/shard_map/pallas_call | solution.py:140
  112.4 3.2 %shard_map.149 = (bf16[4,64,1024]{2,1,0:T(8,128)(2,1)S(1)}, bf16[4,64,1024]{2,1,0:T(8,128)(2,1)S(1)}) custom-call(s32[2]{0:T(128)S(1)} %pad_add_fusion.place_ref, bf16[128,2176]{1,0:T(8,128)(2,1)S(1)} %collective-permute-done.31.near_ref, bf16[128,2176]{1,0:T(8,128)(2,1)S(1)} %collective-permute-done.32.far_ref, bf16[704,2048]{1,0:T(8,128)(2,1)S(1)} %bitcast.83, ...), custom_call_target="tpu_custom_call" | custom-call | flops 2214592512 | bytes 10813440 | tf_op jit(solution)/shard_map/pallas_call | solution.py:140
  119.3 11.3 %collective-permute-done.27 = bf16[2,2,128,1024]{3,2,1,0:T(8,128)(2,1)S(1)} collective-permute-done((bf16[2,2,128,1024]{3,2,1,0:T(8,128)(2,1)S(1)}, bf16[2,2,128,1024]{3,2,1,0:T(8,128)(2,1)S(1)}, u32[]{:S(2)}, u32[]{:S(2)}) %collective-permute-start.27) | collective-permute-done | bytes 1048608 | tf_op jit(solution)/shard_map/ppermute | solution.py:168
  131.0 5.1 %collective-permute-done.35 = bf16[2,2,64,1024]{3,2,1,0:T(8,128)(2,1)S(1)} collective-permute-done((bf16[2,2,64,1024]{3,2,1,0:T(8,128)(2,1)S(1)}, bf16[2,2,64,1024]{3,2,1,0:T(8,128)(2,1)S(1)}, u32[]{:S(2)}, u32[]{:S(2)}) %collective-permute-start.35) | collective-permute-done | bytes 524320 | tf_op jit(solution)/shard_map/ppermute | solution.py:168
  138.5 4.3 %collective-permute-done.36 = bf16[2,64,1024]{2,1,0:T(8,128)(2,1)S(1)} collective-permute-done((bf16[2,64,1024]{2,1,0:T(8,128)(2,1)S(1)}, bf16[2,64,1024]{2,1,0:T(8,128)(2,1)S(1)}, u32[]{:S(2)}, u32[]{:S(2)}) %collective-permute-start.36) | collective-permute-done | bytes 262176 | tf_op jit(solution)/shard_map/ppermute | solution.py:168
  143.0 7.8 %collective-permute-start.37 = (bf16[128,1024]{1,0:T(8,128)(2,1)S(1)}, bf16[128,1024]{1,0:T(8,128)(2,1)S(1)}, u32[]{:S(2)}, u32[]{:S(2)}) collective-permute-start(bf16[128,1024]{1,0:T(8,128)(2,1)S(1)} %pad_maximum_fusion.9), channel_id=1, source_target_pairs={{0,8},{1,9},{2,10},{3,11},{4,12},{5,13},{6,14},{7,15},{8,0},{9,1},... | collective-permute-start | bytes 786440 | tf_op jit(solution)/shard_map/ppermute | solution.py:39
  155.2 2.4 %collective-permute-done.37 = bf16[128,1024]{1,0:T(8,128)(2,1)S(1)} collective-permute-done((bf16[128,1024]{1,0:T(8,128)(2,1)S(1)}, bf16[128,1024]{1,0:T(8,128)(2,1)S(1)}, u32[]{:S(2)}, u32[]{:S(2)}) %collective-permute-start.37) | collective-permute-done | bytes 262176 | tf_op jit(solution)/shard_map/ppermute | solution.py:39
  157.6 6.7 %collective-permute-done.38 = bf16[128,1024]{1,0:T(8,128)(2,1)S(1)} collective-permute-done((bf16[128,1024]{1,0:T(8,128)(2,1)S(1)}, bf16[128,1024]{1,0:T(8,128)(2,1)S(1)}, u32[]{:S(2)}, u32[]{:S(2)}) %collective-permute-start.38) | collective-permute-done | bytes 262176 | tf_op jit(solution)/shard_map/ppermute | solution.py:39
  164.2 4.3 %collective-permute-done.29 = bf16[128,1024]{1,0:T(8,128)(2,1)S(1)} collective-permute-done((bf16[128,1024]{1,0:T(8,128)(2,1)}, bf16[128,1024]{1,0:T(8,128)(2,1)S(1)}, u32[]{:S(2)}, u32[]{:S(2)}) %collective-permute-start.29) | collective-permute-done | bytes 262176 | tf_op jit(solution)/shard_map/ppermute | solution.py:39
  (142 shorter events, 44.3 us)
Async XLA Ops:
  4.5 11.6 %collective-permute-start = (bf16[128,1024]{1,0:T(8,128)(2,1)S(1)}, bf16[128,1024]{1,0:T(8,128)(2,1)S(1)}, u32[]{:S(2)}, u32[]{:S(2)}) collective-permute-start(bf16[128,1024]{1,0:T(8,128)(2,1)S(1)} %get-tuple-element.30.rest_0_), channel_id=1, source_target_pairs={{0,4},{1,5},{2,6},{3,7},{4,8},{5,9},{6,10},{7,11},{8,12},{9,13},{1... | collective-permute-start | bytes 786440 | tf_op jit(solution)/shard_map/ppermute | solution.py:27
  9.4 11.9 %collective-permute-start.4 = (bf16[128,1024]{1,0:T(8,128)(2,1)}, bf16[128,1024]{1,0:T(8,128)(2,1)S(1)}, u32[]{:S(2)}, u32[]{:S(2)}) collective-permute-start(bf16[128,1024]{1,0:T(8,128)(2,1)} %rest_0_), channel_id=1, source_target_pairs={{0,4},{1,5},{2,6},{3,7},{4,8},{5,9},{6,10},{7,11},{8,12},{9,13},{1... | collective-permute-start | bytes 786440 | tf_op jit(solution)/shard_map/ppermute | solution.py:27
  17.0 9.8 %collective-permute-start.3 = (bf16[128,1024]{1,0:T(8,128)(2,1)S(1)}, bf16[128,1024]{1,0:T(8,128)(2,1)S(1)}, u32[]{:S(2)}, u32[]{:S(2)}) collective-permute-start(bf16[128,1024]{1,0:T(8,128)(2,1)S(1)} %get-tuple-element.73), channel_id=1, source_target_pairs={{0,3},{1,2},{2,1},{3,0},{4,7},{5,6},{6,5},{7,4},{8,11},{9,10},{10,... | collective-permute-start | bytes 786440 | tf_op jit(solution)/shard_map/ppermute | solution.py:22
  20.3 15.1 %collective-permute-start.2 = (bf16[128,1024]{1,0:T(8,128)(2,1)}, bf16[128,1024]{1,0:T(8,128)(2,1)S(1)}, u32[]{:S(2)}, u32[]{:S(2)}) collective-permute-start(bf16[128,1024]{1,0:T(8,128)(2,1)} %get-tuple-element.74), channel_id=1, source_target_pairs={{0,2},{1,3},{2,0},{3,1},{4,6},{5,7},{6,4},{7,5},{8,10},{9,11},{10,... | collective-permute-start | bytes 786440 | tf_op jit(solution)/shard_map/ppermute | solution.py:22
  20.8 14.6 %collective-permute-start.1 = (bf16[128,1024]{1,0:T(8,128)(2,1)}, bf16[128,1024]{1,0:T(8,128)(2,1)S(1)}, u32[]{:S(2)}, u32[]{:S(2)}) collective-permute-start(bf16[128,1024]{1,0:T(8,128)(2,1)} %get-tuple-element.75), channel_id=1, source_target_pairs={{0,1},{1,0},{2,3},{3,2},{4,5},{5,4},{6,7},{7,6},{8,9},{9,8},{10,11... | collective-permute-start | bytes 786440 | tf_op jit(solution)/shard_map/ppermute | solution.py:22
  22.3 17.2 %collective-permute-start.7 = (bf16[128,1024]{1,0:T(8,128)(2,1)}, bf16[128,1024]{1,0:T(8,128)(2,1)S(1)}, u32[]{:S(2)}, u32[]{:S(2)}) collective-permute-start(bf16[128,1024]{1,0:T(8,128)(2,1)} %get-tuple-element.70), channel_id=1, source_target_pairs={{0,3},{1,2},{2,1},{3,0},{4,7},{5,6},{6,5},{7,4},{8,11},{9,10},{10,... | collective-permute-start | bytes 786440 | tf_op jit(solution)/shard_map/ppermute | solution.py:22
  24.8 16.0 %collective-permute-start.6 = (bf16[128,1024]{1,0:T(8,128)(2,1)}, bf16[128,1024]{1,0:T(8,128)(2,1)S(1)}, u32[]{:S(2)}, u32[]{:S(2)}) collective-permute-start(bf16[128,1024]{1,0:T(8,128)(2,1)} %get-tuple-element.71), channel_id=1, source_target_pairs={{0,2},{1,3},{2,0},{3,1},{4,6},{5,7},{6,4},{7,5},{8,10},{9,11},{10,... | collective-permute-start | bytes 786440 | tf_op jit(solution)/shard_map/ppermute | solution.py:22
  26.8 14.0 %collective-permute-start.5 = (bf16[128,1024]{1,0:T(8,128)(2,1)}, bf16[128,1024]{1,0:T(8,128)(2,1)S(1)}, u32[]{:S(2)}, u32[]{:S(2)}) collective-permute-start(bf16[128,1024]{1,0:T(8,128)(2,1)} %get-tuple-element.72), channel_id=1, source_target_pairs={{0,1},{1,0},{2,3},{3,2},{4,5},{5,4},{6,7},{7,6},{8,9},{9,8},{10,11... | collective-permute-start | bytes 786440 | tf_op jit(solution)/shard_map/ppermute | solution.py:22
  46.0 13.8 %collective-permute-start.17 = (bf16[64,2176]{1,0:T(8,128)(2,1)S(1)}, bf16[64,2176]{1,0:T(8,128)(2,1)S(1)}, u32[]{:S(2)}, u32[]{:S(2)}) collective-permute-start(bf16[64,2176]{1,0:T(8,128)(2,1)S(1)} %get-tuple-element.40), channel_id=1, source_target_pairs={{12,0},{13,1},{14,2},{15,3},{0,4},{1,5},{2,6},{3,7},{4,8},{5,9},{6... | collective-permute-start | bytes 835592 | tf_op jit(solution)/shard_map/ppermute | solution.py:32
  48.6 14.4 %collective-permute-start.16 = (bf16[64,2176]{1,0:T(8,128)(2,1)S(1)}, bf16[64,2176]{1,0:T(8,128)(2,1)S(1)}, u32[]{:S(2)}, u32[]{:S(2)}) collective-permute-start(bf16[64,2176]{1,0:T(8,128)(2,1)S(1)} %get-tuple-element.40), channel_id=1, source_target_pairs={{4,0},{5,1},{6,2},{7,3},{8,4},{9,5},{10,6},{11,7},{12,8},{13,9},{1... | collective-permute-start | bytes 835592 | tf_op jit(solution)/shard_map/ppermute | solution.py:32
  50.8 6.5 %collective-permute-start.9 = (bf16[64,2176]{1,0:T(8,128)(2,1)S(1)}, bf16[64,2176]{1,0:T(8,128)(2,1)S(1)}, u32[]{:S(2)}, u32[]{:S(2)}) collective-permute-start(bf16[64,2176]{1,0:T(8,128)(2,1)S(1)} %get-tuple-element.40), channel_id=1, source_target_pairs={{0,1},{1,0},{2,3},{3,2},{4,5},{5,4},{6,7},{7,6},{8,9},{9,8},{10,11... | collective-permute-start | bytes 835592 | tf_op jit(solution)/shard_map/ppermute | solution.py:168
  57.4 22.9 %collective-permute-start.11 = (bf16[128,2176]{1,0:T(8,128)(2,1)S(1)}, bf16[128,2176]{1,0:T(8,128)(2,1)S(1)}, u32[]{:S(2)}, u32[]{:S(2)}) collective-permute-start(bf16[128,2176]{1,0:T(8,128)(2,1)S(1)} %constant_dynamic-update-slice_fusion.near_ref), channel_id=1, source_target_pairs={{16,0},{0,16},{17,1},{1,17},{18,2},{2,18},{19,3},{3,19},{20,4},{4,... | collective-permute-start | bytes 1671176 | tf_op jit(solution)/shard_map/ppermute | solution.py:46
  57.5 11.5 %collective-permute-start.10 = (bf16[128,2176]{1,0:T(8,128)(2,1)S(1)}, bf16[128,2176]{1,0:T(8,128)(2,1)S(1)}, u32[]{:S(2)}, u32[]{:S(2)}) collective-permute-start(bf16[128,2176]{1,0:T(8,128)(2,1)S(1)} %constant_dynamic-update-slice_fusion.near_ref), channel_id=1, source_target_pairs={{0,2},{1,3},{2,0},{3,1},{4,6},{5,7},{6,4},{7,5},{8,10},{9,11},{10,... | collective-permute-start | bytes 1671176 | tf_op jit(solution)/shard_map/ppermute | solution.py:168
  59.0 16.4 %collective-permute-start.15 = (bf16[64,2176]{1,0:T(8,128)(2,1)S(1)}, bf16[64,2176]{1,0:T(8,128)(2,1)S(1)}, u32[]{:S(2)}, u32[]{:S(2)}) collective-permute-start(bf16[64,2176]{1,0:T(8,128)(2,1)S(1)} %get-tuple-element.40), channel_id=1, source_target_pairs={{8,0},{9,1},{10,2},{11,3},{12,4},{13,5},{14,6},{15,7},{0,8},{1,9},... | collective-permute-start | bytes 835592 | tf_op jit(solution)/shard_map/ppermute | solution.py:32
  63.0 9.6 %collective-permute-start.18 = (bf16[128,2176]{1,0:T(8,128)(2,1)S(1)}, bf16[128,2176]{1,0:T(8,128)(2,1)S(1)}, u32[]{:S(2)}, u32[]{:S(2)}) collective-permute-start(bf16[128,2176]{1,0:T(8,128)(2,1)S(1)} %pad_maximum_fusion.1), channel_id=1, source_target_pairs={{0,1},{1,0},{2,3},{3,2},{4,5},{5,4},{6,7},{7,6},{8,9},{9,8},{10,11... | collective-permute-start | bytes 1671176 | tf_op jit(solution)/shard_map/ppermute | solution.py:168
  69.0 11.8 %collective-permute-start.12 = (bf16[128,2176]{1,0:T(8,128)(2,1)S(1)}, bf16[128,2176]{1,0:T(8,128)(2,1)S(1)}, u32[]{:S(2)}, u32[]{:S(2)}) collective-permute-start(bf16[128,2176]{1,0:T(8,128)(2,1)S(1)} %collective-permute-done.10.far_ref), channel_id=1, source_target_pairs={{16,0},{0,16},{17,1},{1,17},{18,2},{2,18},{19,3},{3,19},{20,4},{4,... | collective-permute-start | bytes 1671176 | tf_op jit(solution)/shard_map/ppermute | solution.py:46
  72.7 18.6 %collective-permute-start.22 = (bf16[256,2176]{1,0:T(8,128)(2,1)S(1)}, bf16[256,2176]{1,0:T(8,128)(2,1)S(1)}, u32[]{:S(2)}, u32[]{:S(2)}) collective-permute-start(bf16[256,2176]{1,0:T(8,128)(2,1)S(1)} %constant_dynamic-update-slice_fusion.2.near_ref), channel_id=1, source_target_pairs={{0,2},{1,3},{2,0},{3,1},{4,6},{5,7},{6,4},{7,5},{8,10},{9,11},{10,... | collective-permute-start | bytes 3342344 | tf_op jit(solution)/shard_map/ppermute | solution.py:168
  75.5 9.6 %collective-permute-start.19 = (bf16[64,2176]{1,0:T(8,128)(2,1)S(1)}, bf16[64,2176]{1,0:T(8,128)(2,1)S(1)}, u32[]{:S(2)}, u32[]{:S(2)}) collective-permute-start(bf16[64,2176]{1,0:T(8,128)(2,1)S(1)} %collective-permute-done.15), channel_id=1, source_target_pairs={{0,1},{1,0},{2,3},{3,2},{4,5},{5,4},{6,7},{7,6},{8,9},{9,8},{10,11... | collective-permute-start | bytes 835592 | tf_op jit(solution)/shard_map/ppermute | solution.py:168
  77.0 22.3 %collective-permute-start.23 = (bf16[256,2176]{1,0:T(8,128)(2,1)S(1)}, bf16[256,2176]{1,0:T(8,128)(2,1)S(1)}, u32[]{:S(2)}, u32[]{:S(2)}) collective-permute-start(bf16[256,2176]{1,0:T(8,128)(2,1)S(1)} %constant_dynamic-update-slice_fusion.2.near_ref), channel_id=1, source_target_pairs={{16,0},{0,16},{17,1},{1,17},{18,2},{2,18},{19,3},{3,19},{20,4},{4,... | collective-permute-start | bytes 3342344 | tf_op jit(solution)/shard_map/ppermute | solution.py:46
  84.0 7.2 %collective-permute-start.13 = (bf16[4,64,1024]{2,1,0:T(8,128)(2,1)S(1)}, bf16[4,64,1024]{2,1,0:T(8,128)(2,1)S(1)}, u32[]{:S(2)}, u32[]{:S(2)}) collective-permute-start(bf16[4,64,1024]{2,1,0:T(8,128)(2,1)S(1)} %get-tuple-element.38), channel_id=1, source_target_pairs={{16,0},{0,16},{17,1},{1,17},{18,2},{2,18},{19,3},{3,19},{20,4},{4,... | collective-permute-start | bytes 1572872 | tf_op jit(solution)/shard_map/ppermute | solution.py:46
  85.1 14.0 %collective-permute-start.30 = (bf16[128,2176]{1,0:T(8,128)(2,1)S(1)}, bf16[128,2176]{1,0:T(8,128)(2,1)S(1)}, u32[]{:S(2)}, u32[]{:S(2)}) collective-permute-start(bf16[128,2176]{1,0:T(8,128)(2,1)S(1)} %constant_dynamic-update-slice_fusion.5.near_ref), channel_id=1, source_target_pairs={{0,2},{1,3},{2,0},{3,1},{4,6},{5,7},{6,4},{7,5},{8,10},{9,11},{10,... | collective-permute-start | bytes 1671176 | tf_op jit(solution)/shard_map/ppermute | solution.py:168
  91.2 8.4 %collective-permute-start.24 = (bf16[256,2176]{1,0:T(8,128)(2,1)S(1)}, bf16[256,2176]{1,0:T(8,128)(2,1)S(1)}, u32[]{:S(2)}, u32[]{:S(2)}) collective-permute-start(bf16[256,2176]{1,0:T(8,128)(2,1)S(1)} %collective-permute-done.22.far_ref), channel_id=1, source_target_pairs={{16,0},{0,16},{17,1},{1,17},{18,2},{2,18},{19,3},{3,19},{20,4},{4,... | collective-permute-start | bytes 3342344 | tf_op jit(solution)/shard_map/ppermute | solution.py:46
  91.5 14.2 %collective-permute-start.20 = (bf16[2,2,64,1024]{3,2,1,0:T(8,128)(2,1)S(1)}, bf16[2,2,64,1024]{3,2,1,0:T(8,128)(2,1)S(1)}, u32[]{:S(2)}, u32[]{:S(2)}) collective-permute-start(bf16[2,2,64,1024]{3,2,1,0:T(8,128)(2,1)S(1)} %pad_maximum_fusion.3), channel_id=1, source_target_pairs={{0,2},{1,3},{2,0},{3,1},{4,6},{5,7},{6,4},{7,5},{8,10},{9,11},{10,... | collective-permute-start | bytes 1572872 | tf_op jit(solution)/shard_map/ppermute | solution.py:168
  98.7 12.0 %collective-permute-start.26 = (bf16[4,128,1024]{2,1,0:T(8,128)(2,1)S(1)}, bf16[4,128,1024]{2,1,0:T(8,128)(2,1)S(1)}, u32[]{:S(2)}, u32[]{:S(2)}) collective-permute-start(bf16[4,128,1024]{2,1,0:T(8,128)(2,1)S(1)} %get-tuple-element.45), channel_id=1, source_target_pairs={{16,0},{0,16},{17,1},{1,17},{18,2},{2,18},{19,3},{3,19},{20,4},{4,... | collective-permute-start | bytes 3145736 | tf_op jit(solution)/shard_map/ppermute | solution.py:46
  99.1 12.8 %collective-permute-start.31 = (bf16[128,2176]{1,0:T(8,128)(2,1)S(1)}, bf16[128,2176]{1,0:T(8,128)(2,1)S(1)}, u32[]{:S(2)}, u32[]{:S(2)}) collective-permute-start(bf16[128,2176]{1,0:T(8,128)(2,1)S(1)} %constant_dynamic-update-slice_fusion.5.near_ref), channel_id=1, source_target_pairs={{16,0},{0,16},{17,1},{1,17},{18,2},{2,18},{19,3},{3,19},{20,4},{4,... | collective-permute-start | bytes 1671176 | tf_op jit(solution)/shard_map/ppermute | solution.py:46
  99.3 13.1 %collective-permute-start.32 = (bf16[128,2176]{1,0:T(8,128)(2,1)S(1)}, bf16[128,2176]{1,0:T(8,128)(2,1)S(1)}, u32[]{:S(2)}, u32[]{:S(2)}) collective-permute-start(bf16[128,2176]{1,0:T(8,128)(2,1)S(1)} %collective-permute-done.30.far_ref), channel_id=1, source_target_pairs={{16,0},{0,16},{17,1},{1,17},{18,2},{2,18},{19,3},{3,19},{20,4},{4,... | collective-permute-start | bytes 1671176 | tf_op jit(solution)/shard_map/ppermute | solution.py:46
  115.7 14.9 %collective-permute-start.27 = (bf16[2,2,128,1024]{3,2,1,0:T(8,128)(2,1)S(1)}, bf16[2,2,128,1024]{3,2,1,0:T(8,128)(2,1)S(1)}, u32[]{:S(2)}, u32[]{:S(2)}) collective-permute-start(bf16[2,2,128,1024]{3,2,1,0:T(8,128)(2,1)S(1)} %pad_maximum_fusion), channel_id=1, source_target_pairs={{0,2},{1,3},{2,0},{3,1},{4,6},{5,7},{6,4},{7,5},{8,10},{9,11},{10,... | collective-permute-start | bytes 3145736 | tf_op jit(solution)/shard_map/ppermute | solution.py:168
  117.9 18.3 %collective-permute-start.35 = (bf16[2,2,64,1024]{3,2,1,0:T(8,128)(2,1)S(1)}, bf16[2,2,64,1024]{3,2,1,0:T(8,128)(2,1)S(1)}, u32[]{:S(2)}, u32[]{:S(2)}) collective-permute-start(bf16[2,2,64,1024]{3,2,1,0:T(8,128)(2,1)S(1)} %pad_maximum_fusion.5), channel_id=1, source_target_pairs={{0,2},{1,3},{2,0},{3,1},{4,6},{5,7},{6,4},{7,5},{8,10},{9,11},{10,... | collective-permute-start | bytes 1572872 | tf_op jit(solution)/shard_map/ppermute | solution.py:168
  138.0 12.8 %collective-permute-start.28 = (bf16[2,128,1024]{2,1,0:T(8,128)(2,1)S(1)}, bf16[2,128,1024]{2,1,0:T(8,128)(2,1)S(1)}, u32[]{:S(2)}, u32[]{:S(2)}) collective-permute-start(bf16[2,128,1024]{2,1,0:T(8,128)(2,1)S(1)} %pad_maximum_fusion.4), channel_id=1, source_target_pairs={{0,1},{1,0},{2,3},{3,2},{4,5},{5,4},{6,7},{7,6},{8,9},{9,8},{10,11... | collective-permute-start | bytes 1572872 | tf_op jit(solution)/shard_map/ppermute | solution.py:168
  143.0 14.6 %collective-permute-start.37 = (bf16[128,1024]{1,0:T(8,128)(2,1)S(1)}, bf16[128,1024]{1,0:T(8,128)(2,1)S(1)}, u32[]{:S(2)}, u32[]{:S(2)}) collective-permute-start(bf16[128,1024]{1,0:T(8,128)(2,1)S(1)} %pad_maximum_fusion.9), channel_id=1, source_target_pairs={{0,8},{1,9},{2,10},{3,11},{4,12},{5,13},{6,14},{7,15},{8,0},{9,1},... | collective-permute-start | bytes 786440 | tf_op jit(solution)/shard_map/ppermute | solution.py:39
  151.0 13.2 %collective-permute-start.38 = (bf16[128,1024]{1,0:T(8,128)(2,1)S(1)}, bf16[128,1024]{1,0:T(8,128)(2,1)S(1)}, u32[]{:S(2)}, u32[]{:S(2)}) collective-permute-start(bf16[128,1024]{1,0:T(8,128)(2,1)S(1)} %pad_maximum_fusion.10), channel_id=1, source_target_pairs={{0,12},{1,13},{2,14},{3,15},{4,0},{5,1},{6,2},{7,3},{8,4},{9,5},{1... | collective-permute-start | bytes 786440 | tf_op jit(solution)/shard_map/ppermute | solution.py:39
  152.4 16.1 %collective-permute-start.29 = (bf16[128,1024]{1,0:T(8,128)(2,1)}, bf16[128,1024]{1,0:T(8,128)(2,1)S(1)}, u32[]{:S(2)}, u32[]{:S(2)}) collective-permute-start(bf16[128,1024]{1,0:T(8,128)(2,1)} %pad_maximum_fusion.7), channel_id=1, source_target_pairs={{0,4},{1,5},{2,6},{3,7},{4,8},{5,9},{6,10},{7,11},{8,12},{9,13},{1... | collective-permute-start | bytes 786440 | tf_op jit(solution)/shard_map/ppermute | solution.py:39
  (20 other events, 206.0 us)

commit v17 on v16

--- a/solution.py
+++ b/solution.py
@@ -354,8 +354,8 @@
     got_list, ready = [], []
     for pair, sent in zip(totals, sents, strict=True):
         pair = merged(pair, after(crossed(sent, False), *ready), 2)
-        ready = [first_share(pair)]
-        got_list.append((pair, crossed(ready[0], True)))
+        ready = [crossed(first_share(pair), True)]
+        got_list.append((pair, ready[0]))
     totals = [pair for pair, _ in got_list]
     gots = [got for _, got in got_list]
     results = {}

time: 170 us -> 176 us (1.035)
  waiting for transfers between devices: 70.2 us -> 73.9 us
  starting transfers between devices: 51.6 us -> 53.5 us
    ppermute x3, waiting for transfers between devices: 13.3 us -> 16.4 us  [to_plane(): lax.ppermute(block, 'blk', [(i, (i + PLANE * ahead) % count) for i in ran...]
where the time goes in v17:
time: 176 us; the launch traced here: 175 us
  waiting for transfers between devices  73.9 us (42%)
  starting transfers between devices  53.5 us (30%)
  Pallas kernels  29.7 us (17%)
  local copies, waits for them, and re-layouts  8.72 us (5%)
  other arithmetic  8.13 us (5%)
    ppermute x12, waiting for transfers between devices, crossed(): return lax.ppermute(block, ('tok', 'blk'), route)  40.2 us
    pallas_call x10, Pallas kernels, local_call(): pl.pallas_call(body, in_specs=[scalar] * len(scalars) + [whole] * len(arr...  29.7 us
    ppermute x12, starting transfers between devices, crossed(): return lax.ppermute(block, ('tok', 'blk'), route)  18.2 us
    ppermute x3, waiting for transfers between devices, to_plane(): lax.ppermute(block, 'blk', [(i, (i + PLANE * ahead) % count) for i in ran...  16.4 us
    ppermute x3, starting transfers between devices, to_plane(): lax.ppermute(block, 'blk', [(i, (i + PLANE * ahead) % count) for i in ran...  10.8 us
    ppermute x2, starting transfers between devices, next_plane(): lax.ppermute(block, 'blk', [(i, i + PLANE) for i in range(count - PLANE)])  8.43 us
    ppermute x6, starting transfers between devices, flipped(): lax.ppermute(block, 'blk', [(i, i ^ mask) for i in range(lax.axis_size('b...  8.32 us
    ppermute x6, waiting for transfers between devices, flipped(): lax.ppermute(block, 'blk', [(i, i ^ mask) for i in range(lax.axis_size('b...  7.49 us
  transfers between devices with their start and end apart: 39, of which 21 were waited for; matrix products, arithmetic and copies ran while one was open for 6% of the time, Pallas kernels for 15%

profile of v17, /device:TPU:0, one launch (start us, length us, event | category | flops | bytes accessed | tf_op | source)
XLA Modules:
  0.0 175.3 jit_solution(2355818855744683003)
XLA Ops:
  4.5 4.9 %collective-permute-start = (bf16[128,1024]{1,0:T(8,128)(2,1)S(1)}, bf16[128,1024]{1,0:T(8,128)(2,1)S(1)}, u32[]{:S(2)}, u32[]{:S(2)}) collective-permute-start(bf16[128,1024]{1,0:T(8,128)(2,1)S(1)} %get-tuple-element.30.rest_0_), channel_id=1, source_target_pairs={{0,4},{1,5},{2,6},{3,7},{4,8},{5,9},{6,10},{7,11},{8,12},{9,13},{1... | collective-permute-start | bytes 786440 | tf_op jit(solution)/shard_map/ppermute | solution.py:27
  9.4 3.5 %collective-permute-start.4 = (bf16[128,1024]{1,0:T(8,128)(2,1)}, bf16[128,1024]{1,0:T(8,128)(2,1)S(1)}, u32[]{:S(2)}, u32[]{:S(2)}) collective-permute-start(bf16[128,1024]{1,0:T(8,128)(2,1)} %rest_0_), channel_id=1, source_target_pairs={{0,4},{1,5},{2,6},{3,7},{4,8},{5,9},{6,10},{7,11},{8,12},{9,13},{1... | collective-permute-start | bytes 786440 | tf_op jit(solution)/shard_map/ppermute | solution.py:27
  13.7 2.4 %collective-permute-done.rest_1_ = bf16[128,1024]{1,0:T(8,128)(2,1)S(1)} collective-permute-done((bf16[128,1024]{1,0:T(8,128)(2,1)S(1)}, bf16[128,1024]{1,0:T(8,128)(2,1)S(1)}, u32[]{:S(2)}, u32[]{:S(2)}) %collective-permute-start) | collective-permute-done | bytes 262176 | tf_op jit(solution)/shard_map/ppermute | solution.py:27
  17.0 2.4 %collective-permute-start.3 = (bf16[128,1024]{1,0:T(8,128)(2,1)S(1)}, bf16[128,1024]{1,0:T(8,128)(2,1)S(1)}, u32[]{:S(2)}, u32[]{:S(2)}) collective-permute-start(bf16[128,1024]{1,0:T(8,128)(2,1)S(1)} %get-tuple-element.73), channel_id=1, source_target_pairs={{0,3},{1,2},{2,1},{3,0},{4,7},{5,6},{6,5},{7,4},{8,11},{9,10},{10,... | collective-permute-start | bytes 786440 | tf_op jit(solution)/shard_map/ppermute | solution.py:22
  22.3 2.4 %collective-permute-start.7 = (bf16[128,1024]{1,0:T(8,128)(2,1)}, bf16[128,1024]{1,0:T(8,128)(2,1)S(1)}, u32[]{:S(2)}, u32[]{:S(2)}) collective-permute-start(bf16[128,1024]{1,0:T(8,128)(2,1)} %get-tuple-element.70), channel_id=1, source_target_pairs={{0,3},{1,2},{2,1},{3,0},{4,7},{5,6},{6,5},{7,4},{8,11},{9,10},{10,... | collective-permute-start | bytes 786440 | tf_op jit(solution)/shard_map/ppermute | solution.py:22
  26.8 1.9 %collective-permute-start.5 = (bf16[128,1024]{1,0:T(8,128)(2,1)}, bf16[128,1024]{1,0:T(8,128)(2,1)S(1)}, u32[]{:S(2)}, u32[]{:S(2)}) collective-permute-start(bf16[128,1024]{1,0:T(8,128)(2,1)} %get-tuple-element.72), channel_id=1, source_target_pairs={{0,1},{1,0},{2,3},{3,2},{4,5},{5,4},{6,7},{7,6},{8,9},{9,8},{10,11... | collective-permute-start | bytes 786440 | tf_op jit(solution)/shard_map/ppermute | solution.py:22
  28.9 1.8 %scatter_fusion = bf16[8,16,2,1024]{3,1,2,0:T(8,128)(2,1)S(1)} fusion(bf16[8,16,2,1024]{3,1,2,0:T(8,128)(2,1)S(1)} %broadcast_in_dim.31, s32[8]{0:T(128)S(1)} %compare_select_fusion, bf16[8,16,2,1024]{3,1,2,0:T(8,128)(2,1)} %pad_maximum_fusion.2), kind=kCustom, calls=%fused_computation | custom fusion | bytes 1572896 | tf_op jit(solution)/shard_map/scatter | solution.py:301
  30.7 4.7 %collective-permute-done.2.rest_3_ = bf16[128,1024]{1,0:T(8,128)(2,1)S(1)} collective-permute-done((bf16[128,1024]{1,0:T(8,128)(2,1)}, bf16[128,1024]{1,0:T(8,128)(2,1)S(1)}, u32[]{:S(2)}, u32[]{:S(2)}) %collective-permute-start.2) | collective-permute-done | bytes 262176 | tf_op jit(solution)/shard_map/ppermute | solution.py:22
  35.4 2.2 %copy-done.3 = bf16[1024,2048]{1,0:T(8,128)(2,1)S(1)} copy-done((bf16[1024,2048]{1,0:T(8,128)(2,1)S(1)}, bf16[1024,2048]{1,0:T(8,128)(2,1)}, u32[]{:S(2)}) %copy-start.3) | copy-done | bytes 4194328
  37.6 1.9 %shard_map.141.prob_ref = bf16[8,128,640]{2,1,0:T(8,128)(2,1)S(1)} custom-call(s32[2]{0:T(128)S(1)} %pad_add_fusion.place_ref, s32[8]{0:T(128)S(1)} %copy-done.11, bf16[128,1024]{1,0:T(8,128)(2,1)S(1)} %get-tuple-element.29.q_ref, bf16[1024,2048]{1,0:T(8,128)(2,1)S(1)} %copy-done.3, bf16[128,1024]{1,0:T(8,128)(2,1)S(1)} %get-tuple-element.30.rest_0_, ...), custom_call_target="tpu_custom_call" | custom-call | flops 167772160 | bytes 7077888 | tf_op jit(solution)/shard_map/pallas_call | solution.py:140
  40.8 1.7 shard_map.142.rest_0_
  42.6 2.6 %collective-permute-done.8.rest_1_ = f32[128,2048]{1,0:T(8,128)S(1)} collective-permute-done((f32[128,2048]{1,0:T(8,128)S(1)}, f32[128,2048]{1,0:T(8,128)S(1)}, u32[]{:S(2)}, u32[]{:S(2)}) %collective-permute-start.8) | collective-permute-done | bytes 1048608 | tf_op jit(solution)/shard_map/ppermute | solution.py:46
  46.0 2.5 %collective-permute-start.17 = (bf16[64,2176]{1,0:T(8,128)(2,1)S(1)}, bf16[64,2176]{1,0:T(8,128)(2,1)S(1)}, u32[]{:S(2)}, u32[]{:S(2)}) collective-permute-start(bf16[64,2176]{1,0:T(8,128)(2,1)S(1)} %get-tuple-element.40), channel_id=1, source_target_pairs={{12,0},{13,1},{14,2},{15,3},{0,4},{1,5},{2,6},{3,7},{4,8},{5,9},{6... | collective-permute-start | bytes 835592 | tf_op jit(solution)/shard_map/ppermute | solution.py:32
  48.6 2.3 %collective-permute-start.16 = (bf16[64,2176]{1,0:T(8,128)(2,1)S(1)}, bf16[64,2176]{1,0:T(8,128)(2,1)S(1)}, u32[]{:S(2)}, u32[]{:S(2)}) collective-permute-start(bf16[64,2176]{1,0:T(8,128)(2,1)S(1)} %get-tuple-element.40), channel_id=1, source_target_pairs={{4,0},{5,1},{6,2},{7,3},{8,4},{9,5},{10,6},{11,7},{12,8},{13,9},{1... | collective-permute-start | bytes 835592 | tf_op jit(solution)/shard_map/ppermute | solution.py:32
  52.4 5.0 %collective-permute-done.9 = bf16[64,2176]{1,0:T(8,128)(2,1)S(1)} collective-permute-done((bf16[64,2176]{1,0:T(8,128)(2,1)S(1)}, bf16[64,2176]{1,0:T(8,128)(2,1)S(1)}, u32[]{:S(2)}, u32[]{:S(2)}) %collective-permute-start.9) | collective-permute-done | bytes 278560 | tf_op jit(solution)/shard_map/ppermute | solution.py:168
  59.8 3.1 %collective-permute-done.16 = bf16[64,2176]{1,0:T(8,128)(2,1)S(1)} collective-permute-done((bf16[64,2176]{1,0:T(8,128)(2,1)S(1)}, bf16[64,2176]{1,0:T(8,128)(2,1)S(1)}, u32[]{:S(2)}, u32[]{:S(2)}) %collective-permute-start.16) | collective-permute-done | bytes 278560 | tf_op jit(solution)/shard_map/ppermute | solution.py:32
  64.7 4.4 %collective-permute-done.10.far_ref = bf16[128,2176]{1,0:T(8,128)(2,1)S(1)} collective-permute-done((bf16[128,2176]{1,0:T(8,128)(2,1)S(1)}, bf16[128,2176]{1,0:T(8,128)(2,1)S(1)}, u32[]{:S(2)}, u32[]{:S(2)}) %collective-permute-start.10) | collective-permute-done | bytes 557088 | tf_op jit(solution)/shard_map/ppermute | solution.py:168
  69.0 3.6 %collective-permute-done.18 = bf16[128,2176]{1,0:T(8,128)(2,1)S(1)} collective-permute-done((bf16[128,2176]{1,0:T(8,128)(2,1)S(1)}, bf16[128,2176]{1,0:T(8,128)(2,1)S(1)}, u32[]{:S(2)}, u32[]{:S(2)}) %collective-permute-start.18) | collective-permute-done | bytes 557088 | tf_op jit(solution)/shard_map/ppermute | solution.py:168
  77.1 3.2 %shard_map.144 = (bf16[4,64,1024]{2,1,0:T(8,128)(2,1)S(1)}, bf16[4,64,1024]{2,1,0:T(8,128)(2,1)S(1)}) custom-call(s32[2]{0:T(128)S(1)} %pad_add_fusion.place_ref, bf16[128,2176]{1,0:T(8,128)(2,1)S(1)} %constant_dynamic-update-slice_fusion.near_ref, bf16[128,2176]{1,0:T(8,128)(2,1)S(1)} %collective-permute-done.10.far_ref, bf16[704,2048]{1,0:T(8,128)(2,1)S(1)} %bitcast.78, ...), custom_call_target="tpu_custom_call" | custom-call | flops 2214592512 | bytes 10813440 | tf_op jit(solution)/shard_map/pallas_call | solution.py:140
  80.9 3.2 %shard_map.145 = (bf16[4,64,1024]{2,1,0:T(8,128)(2,1)S(1)}, bf16[4,64,1024]{2,1,0:T(8,128)(2,1)S(1)}) custom-call(s32[2]{0:T(128)S(1)} %pad_add_fusion.place_ref, bf16[128,2176]{1,0:T(8,128)(2,1)S(1)} %collective-permute-done.11.near_ref, bf16[128,2176]{1,0:T(8,128)(2,1)S(1)} %collective-permute-done.12.far_ref, bf16[704,2048]{1,0:T(8,128)(2,1)S(1)} %bitcast.79, ...), custom_call_target="tpu_custom_call" | custom-call | flops 2214592512 | bytes 10813440 | tf_op jit(solution)/shard_map/pallas_call | solution.py:140
  86.8 4.4 %collective-permute-done.22.far_ref = bf16[256,2176]{1,0:T(8,128)(2,1)S(1)} collective-permute-done((bf16[256,2176]{1,0:T(8,128)(2,1)S(1)}, bf16[256,2176]{1,0:T(8,128)(2,1)S(1)}, u32[]{:S(2)}, u32[]{:S(2)}) %collective-permute-start.22) | collective-permute-done | bytes 1114144 | tf_op jit(solution)/shard_map/ppermute | solution.py:168
  93.1 5.7 %shard_map.146 = (bf16[4,128,1024]{2,1,0:T(8,128)(2,1)S(1)}, bf16[4,128,1024]{2,1,0:T(8,128)(2,1)S(1)}) custom-call(s32[2]{0:T(128)S(1)} %pad_add_fusion.place_ref, bf16[256,2176]{1,0:T(8,128)(2,1)S(1)} %constant_dynamic-update-slice_fusion.2.near_ref, bf16[256,2176]{1,0:T(8,128)(2,1)S(1)} %collective-permute-done.22.far_ref, ...), custom_call_target="tpu_custom_call" | custom-call | flops 4429185024 | bytes 12976128 | tf_op jit(solution)/shard_map/pallas_call | solution.py:140
  99.6 5.8 %shard_map.147 = (bf16[4,128,1024]{2,1,0:T(8,128)(2,1)S(1)}, bf16[4,128,1024]{2,1,0:T(8,128)(2,1)S(1)}) custom-call(s32[2]{0:T(128)S(1)} %pad_add_fusion.place_ref, bf16[256,2176]{1,0:T(8,128)(2,1)S(1)} %collective-permute-done.23.near_ref, bf16[256,2176]{1,0:T(8,128)(2,1)S(1)} %collective-permute-done.24.far_ref, bf16[704,2048]{1,0:T(8,128)(2,1)S(1)} %bitcast.81, ...), custom_call_target="tpu_custom_call" | custom-call | flops 4429185024 | bytes 12976128 | tf_op jit(solution)/shard_map/pallas_call | solution.py:140
  107.6 3.2 %shard_map.148 = (bf16[4,64,1024]{2,1,0:T(8,128)(2,1)S(1)}, bf16[4,64,1024]{2,1,0:T(8,128)(2,1)S(1)}) custom-call(s32[2]{0:T(128)S(1)} %pad_add_fusion.place_ref, bf16[128,2176]{1,0:T(8,128)(2,1)S(1)} %constant_dynamic-update-slice_fusion.5.near_ref, bf16[128,2176]{1,0:T(8,128)(2,1)S(1)} %collective-permute-done.30.far_ref, bf16[704,2048]{1,0:T(8,128)(2,1)S(1)} %bitcast.82, ...), custom_call_target="tpu_custom_call" | custom-call | flops 2214592512 | bytes 10813440 | tf_op jit(solution)/shard_map/pallas_call | solution.py:140
  112.4 3.2 %shard_map.149 = (bf16[4,64,1024]{2,1,0:T(8,128)(2,1)S(1)}, bf16[4,64,1024]{2,1,0:T(8,128)(2,1)S(1)}) custom-call(s32[2]{0:T(128)S(1)} %pad_add_fusion.place_ref, bf16[128,2176]{1,0:T(8,128)(2,1)S(1)} %collective-permute-done.31.near_ref, bf16[128,2176]{1,0:T(8,128)(2,1)S(1)} %collective-permute-done.32.far_ref, bf16[704,2048]{1,0:T(8,128)(2,1)S(1)} %bitcast.83, ...), custom_call_target="tpu_custom_call" | custom-call | flops 2214592512 | bytes 10813440 | tf_op jit(solution)/shard_map/pallas_call | solution.py:140
  119.3 11.3 %collective-permute-done.27 = bf16[2,2,128,1024]{3,2,1,0:T(8,128)(2,1)S(1)} collective-permute-done((bf16[2,2,128,1024]{3,2,1,0:T(8,128)(2,1)S(1)}, bf16[2,2,128,1024]{3,2,1,0:T(8,128)(2,1)S(1)}, u32[]{:S(2)}, u32[]{:S(2)}) %collective-permute-start.27) | collective-permute-done | bytes 1048608 | tf_op jit(solution)/shard_map/ppermute | solution.py:168
  132.6 6.4 %collective-permute-done.35 = bf16[2,2,64,1024]{3,2,1,0:T(8,128)(2,1)S(1)} collective-permute-done((bf16[2,2,64,1024]{3,2,1,0:T(8,128)(2,1)S(1)}, bf16[2,2,64,1024]{3,2,1,0:T(8,128)(2,1)S(1)}, u32[]{:S(2)}, u32[]{:S(2)}) %collective-permute-start.35) | collective-permute-done | bytes 524320 | tf_op jit(solution)/shard_map/ppermute | solution.py:168
  139.0 2.3 %collective-permute-done.28 = bf16[2,128,1024]{2,1,0:T(8,128)(2,1)S(1)} collective-permute-done((bf16[2,128,1024]{2,1,0:T(8,128)(2,1)S(1)}, bf16[2,128,1024]{2,1,0:T(8,128)(2,1)S(1)}, u32[]{:S(2)}, u32[]{:S(2)}) %collective-permute-start.28) | collective-permute-done | bytes 524320 | tf_op jit(solution)/shard_map/ppermute | solution.py:168
  143.3 3.0 %collective-permute-start.38 = (bf16[128,1024]{1,0:T(8,128)(2,1)S(1)}, bf16[128,1024]{1,0:T(8,128)(2,1)S(1)}, u32[]{:S(2)}, u32[]{:S(2)}) collective-permute-start(bf16[128,1024]{1,0:T(8,128)(2,1)S(1)} %pad_maximum_fusion.10), channel_id=1, source_target_pairs={{0,12},{1,13},{2,14},{3,15},{4,0},{5,1},{6,2},{7,3},{8,4},{9,5},{1... | collective-permute-start | bytes 786440 | tf_op jit(solution)/shard_map/ppermute | solution.py:39
  148.7 7.7 %collective-permute-start.37 = (bf16[128,1024]{1,0:T(8,128)(2,1)}, bf16[128,1024]{1,0:T(8,128)(2,1)S(1)}, u32[]{:S(2)}, u32[]{:S(2)}) collective-permute-start(bf16[128,1024]{1,0:T(8,128)(2,1)} %pad_maximum_fusion.9), channel_id=1, source_target_pairs={{0,8},{1,9},{2,10},{3,11},{4,12},{5,13},{6,14},{7,15},{8,0},{9,1},... | collective-permute-start | bytes 786440 | tf_op jit(solution)/shard_map/ppermute | solution.py:39
  157.9 7.6 %collective-permute-done.29 = bf16[128,1024]{1,0:T(8,128)(2,1)S(1)} collective-permute-done((bf16[128,1024]{1,0:T(8,128)(2,1)S(1)}, bf16[128,1024]{1,0:T(8,128)(2,1)S(1)}, u32[]{:S(2)}, u32[]{:S(2)}) %collective-permute-start.29) | collective-permute-done | bytes 262176 | tf_op jit(solution)/shard_map/ppermute | solution.py:39
  165.4 8.8 %collective-permute-done.37 = bf16[128,1024]{1,0:T(8,128)(2,1)S(1)} collective-permute-done((bf16[128,1024]{1,0:T(8,128)(2,1)}, bf16[128,1024]{1,0:T(8,128)(2,1)S(1)}, u32[]{:S(2)}, u32[]{:S(2)}) %collective-permute-start.37) | collective-permute-done | bytes 262176 | tf_op jit(solution)/shard_map/ppermute | solution.py:39
  (142 shorter events, 44.9 us)
Async XLA Ops:
  4.5 11.6 %collective-permute-start = (bf16[128,1024]{1,0:T(8,128)(2,1)S(1)}, bf16[128,1024]{1,0:T(8,128)(2,1)S(1)}, u32[]{:S(2)}, u32[]{:S(2)}) collective-permute-start(bf16[128,1024]{1,0:T(8,128)(2,1)S(1)} %get-tuple-element.30.rest_0_), channel_id=1, source_target_pairs={{0,4},{1,5},{2,6},{3,7},{4,8},{5,9},{6,10},{7,11},{8,12},{9,13},{1... | collective-permute-start | bytes 786440 | tf_op jit(solution)/shard_map/ppermute | solution.py:27
  9.4 11.9 %collective-permute-start.4 = (bf16[128,1024]{1,0:T(8,128)(2,1)}, bf16[128,1024]{1,0:T(8,128)(2,1)S(1)}, u32[]{:S(2)}, u32[]{:S(2)}) collective-permute-start(bf16[128,1024]{1,0:T(8,128)(2,1)} %rest_0_), channel_id=1, source_target_pairs={{0,4},{1,5},{2,6},{3,7},{4,8},{5,9},{6,10},{7,11},{8,12},{9,13},{1... | collective-permute-start | bytes 786440 | tf_op jit(solution)/shard_map/ppermute | solution.py:27
  17.0 9.8 %collective-permute-start.3 = (bf16[128,1024]{1,0:T(8,128)(2,1)S(1)}, bf16[128,1024]{1,0:T(8,128)(2,1)S(1)}, u32[]{:S(2)}, u32[]{:S(2)}) collective-permute-start(bf16[128,1024]{1,0:T(8,128)(2,1)S(1)} %get-tuple-element.73), channel_id=1, source_target_pairs={{0,3},{1,2},{2,1},{3,0},{4,7},{5,6},{6,5},{7,4},{8,11},{9,10},{10,... | collective-permute-start | bytes 786440 | tf_op jit(solution)/shard_map/ppermute | solution.py:22
  20.3 15.1 %collective-permute-start.2 = (bf16[128,1024]{1,0:T(8,128)(2,1)}, bf16[128,1024]{1,0:T(8,128)(2,1)S(1)}, u32[]{:S(2)}, u32[]{:S(2)}) collective-permute-start(bf16[128,1024]{1,0:T(8,128)(2,1)} %get-tuple-element.74), channel_id=1, source_target_pairs={{0,2},{1,3},{2,0},{3,1},{4,6},{5,7},{6,4},{7,5},{8,10},{9,11},{10,... | collective-permute-start | bytes 786440 | tf_op jit(solution)/shard_map/ppermute | solution.py:22
  20.8 14.6 %collective-permute-start.1 = (bf16[128,1024]{1,0:T(8,128)(2,1)}, bf16[128,1024]{1,0:T(8,128)(2,1)S(1)}, u32[]{:S(2)}, u32[]{:S(2)}) collective-permute-start(bf16[128,1024]{1,0:T(8,128)(2,1)} %get-tuple-element.75), channel_id=1, source_target_pairs={{0,1},{1,0},{2,3},{3,2},{4,5},{5,4},{6,7},{7,6},{8,9},{9,8},{10,11... | collective-permute-start | bytes 786440 | tf_op jit(solution)/shard_map/ppermute | solution.py:22
  22.3 17.2 %collective-permute-start.7 = (bf16[128,1024]{1,0:T(8,128)(2,1)}, bf16[128,1024]{1,0:T(8,128)(2,1)S(1)}, u32[]{:S(2)}, u32[]{:S(2)}) collective-permute-start(bf16[128,1024]{1,0:T(8,128)(2,1)} %get-tuple-element.70), channel_id=1, source_target_pairs={{0,3},{1,2},{2,1},{3,0},{4,7},{5,6},{6,5},{7,4},{8,11},{9,10},{10,... | collective-permute-start | bytes 786440 | tf_op jit(solution)/shard_map/ppermute | solution.py:22
  24.8 16.0 %collective-permute-start.6 = (bf16[128,1024]{1,0:T(8,128)(2,1)}, bf16[128,1024]{1,0:T(8,128)(2,1)S(1)}, u32[]{:S(2)}, u32[]{:S(2)}) collective-permute-start(bf16[128,1024]{1,0:T(8,128)(2,1)} %get-tuple-element.71), channel_id=1, source_target_pairs={{0,2},{1,3},{2,0},{3,1},{4,6},{5,7},{6,4},{7,5},{8,10},{9,11},{10,... | collective-permute-start | bytes 786440 | tf_op jit(solution)/shard_map/ppermute | solution.py:22
  26.8 14.0 %collective-permute-start.5 = (bf16[128,1024]{1,0:T(8,128)(2,1)}, bf16[128,1024]{1,0:T(8,128)(2,1)S(1)}, u32[]{:S(2)}, u32[]{:S(2)}) collective-permute-start(bf16[128,1024]{1,0:T(8,128)(2,1)} %get-tuple-element.72), channel_id=1, source_target_pairs={{0,1},{1,0},{2,3},{3,2},{4,5},{5,4},{6,7},{7,6},{8,9},{9,8},{10,11... | collective-permute-start | bytes 786440 | tf_op jit(solution)/shard_map/ppermute | solution.py:22
  46.0 13.8 %collective-permute-start.17 = (bf16[64,2176]{1,0:T(8,128)(2,1)S(1)}, bf16[64,2176]{1,0:T(8,128)(2,1)S(1)}, u32[]{:S(2)}, u32[]{:S(2)}) collective-permute-start(bf16[64,2176]{1,0:T(8,128)(2,1)S(1)} %get-tuple-element.40), channel_id=1, source_target_pairs={{12,0},{13,1},{14,2},{15,3},{0,4},{1,5},{2,6},{3,7},{4,8},{5,9},{6... | collective-permute-start | bytes 835592 | tf_op jit(solution)/shard_map/ppermute | solution.py:32
  48.6 14.4 %collective-permute-start.16 = (bf16[64,2176]{1,0:T(8,128)(2,1)S(1)}, bf16[64,2176]{1,0:T(8,128)(2,1)S(1)}, u32[]{:S(2)}, u32[]{:S(2)}) collective-permute-start(bf16[64,2176]{1,0:T(8,128)(2,1)S(1)} %get-tuple-element.40), channel_id=1, source_target_pairs={{4,0},{5,1},{6,2},{7,3},{8,4},{9,5},{10,6},{11,7},{12,8},{13,9},{1... | collective-permute-start | bytes 835592 | tf_op jit(solution)/shard_map/ppermute | solution.py:32
  50.8 6.5 %collective-permute-start.9 = (bf16[64,2176]{1,0:T(8,128)(2,1)S(1)}, bf16[64,2176]{1,0:T(8,128)(2,1)S(1)}, u32[]{:S(2)}, u32[]{:S(2)}) collective-permute-start(bf16[64,2176]{1,0:T(8,128)(2,1)S(1)} %get-tuple-element.40), channel_id=1, source_target_pairs={{0,1},{1,0},{2,3},{3,2},{4,5},{5,4},{6,7},{7,6},{8,9},{9,8},{10,11... | collective-permute-start | bytes 835592 | tf_op jit(solution)/shard_map/ppermute | solution.py:168
  57.4 22.9 %collective-permute-start.11 = (bf16[128,2176]{1,0:T(8,128)(2,1)S(1)}, bf16[128,2176]{1,0:T(8,128)(2,1)S(1)}, u32[]{:S(2)}, u32[]{:S(2)}) collective-permute-start(bf16[128,2176]{1,0:T(8,128)(2,1)S(1)} %constant_dynamic-update-slice_fusion.near_ref), channel_id=1, source_target_pairs={{16,0},{0,16},{17,1},{1,17},{18,2},{2,18},{19,3},{3,19},{20,4},{4,... | collective-permute-start | bytes 1671176 | tf_op jit(solution)/shard_map/ppermute | solution.py:46
  57.5 11.5 %collective-permute-start.10 = (bf16[128,2176]{1,0:T(8,128)(2,1)S(1)}, bf16[128,2176]{1,0:T(8,128)(2,1)S(1)}, u32[]{:S(2)}, u32[]{:S(2)}) collective-permute-start(bf16[128,2176]{1,0:T(8,128)(2,1)S(1)} %constant_dynamic-update-slice_fusion.near_ref), channel_id=1, source_target_pairs={{0,2},{1,3},{2,0},{3,1},{4,6},{5,7},{6,4},{7,5},{8,10},{9,11},{10,... | collective-permute-start | bytes 1671176 | tf_op jit(solution)/shard_map/ppermute | solution.py:168
  59.0 16.4 %collective-permute-start.15 = (bf16[64,2176]{1,0:T(8,128)(2,1)S(1)}, bf16[64,2176]{1,0:T(8,128)(2,1)S(1)}, u32[]{:S(2)}, u32[]{:S(2)}) collective-permute-start(bf16[64,2176]{1,0:T(8,128)(2,1)S(1)} %get-tuple-element.40), channel_id=1, source_target_pairs={{8,0},{9,1},{10,2},{11,3},{12,4},{13,5},{14,6},{15,7},{0,8},{1,9},... | collective-permute-start | bytes 835592 | tf_op jit(solution)/shard_map/ppermute | solution.py:32
  63.0 9.6 %collective-permute-start.18 = (bf16[128,2176]{1,0:T(8,128)(2,1)S(1)}, bf16[128,2176]{1,0:T(8,128)(2,1)S(1)}, u32[]{:S(2)}, u32[]{:S(2)}) collective-permute-start(bf16[128,2176]{1,0:T(8,128)(2,1)S(1)} %pad_maximum_fusion.1), channel_id=1, source_target_pairs={{0,1},{1,0},{2,3},{3,2},{4,5},{5,4},{6,7},{7,6},{8,9},{9,8},{10,11... | collective-permute-start | bytes 1671176 | tf_op jit(solution)/shard_map/ppermute | solution.py:168
  69.0 11.8 %collective-permute-start.12 = (bf16[128,2176]{1,0:T(8,128)(2,1)S(1)}, bf16[128,2176]{1,0:T(8,128)(2,1)S(1)}, u32[]{:S(2)}, u32[]{:S(2)}) collective-permute-start(bf16[128,2176]{1,0:T(8,128)(2,1)S(1)} %collective-permute-done.10.far_ref), channel_id=1, source_target_pairs={{16,0},{0,16},{17,1},{1,17},{18,2},{2,18},{19,3},{3,19},{20,4},{4,... | collective-permute-start | bytes 1671176 | tf_op jit(solution)/shard_map/ppermute | solution.py:46
  72.7 18.6 %collective-permute-start.22 = (bf16[256,2176]{1,0:T(8,128)(2,1)S(1)}, bf16[256,2176]{1,0:T(8,128)(2,1)S(1)}, u32[]{:S(2)}, u32[]{:S(2)}) collective-permute-start(bf16[256,2176]{1,0:T(8,128)(2,1)S(1)} %constant_dynamic-update-slice_fusion.2.near_ref), channel_id=1, source_target_pairs={{0,2},{1,3},{2,0},{3,1},{4,6},{5,7},{6,4},{7,5},{8,10},{9,11},{10,... | collective-permute-start | bytes 3342344 | tf_op jit(solution)/shard_map/ppermute | solution.py:168
  75.5 9.6 %collective-permute-start.19 = (bf16[64,2176]{1,0:T(8,128)(2,1)S(1)}, bf16[64,2176]{1,0:T(8,128)(2,1)S(1)}, u32[]{:S(2)}, u32[]{:S(2)}) collective-permute-start(bf16[64,2176]{1,0:T(8,128)(2,1)S(1)} %collective-permute-done.15), channel_id=1, source_target_pairs={{0,1},{1,0},{2,3},{3,2},{4,5},{5,4},{6,7},{7,6},{8,9},{9,8},{10,11... | collective-permute-start | bytes 835592 | tf_op jit(solution)/shard_map/ppermute | solution.py:168
  77.0 22.3 %collective-permute-start.23 = (bf16[256,2176]{1,0:T(8,128)(2,1)S(1)}, bf16[256,2176]{1,0:T(8,128)(2,1)S(1)}, u32[]{:S(2)}, u32[]{:S(2)}) collective-permute-start(bf16[256,2176]{1,0:T(8,128)(2,1)S(1)} %constant_dynamic-update-slice_fusion.2.near_ref), channel_id=1, source_target_pairs={{16,0},{0,16},{17,1},{1,17},{18,2},{2,18},{19,3},{3,19},{20,4},{4,... | collective-permute-start | bytes 3342344 | tf_op jit(solution)/shard_map/ppermute | solution.py:46
  84.0 7.2 %collective-permute-start.13 = (bf16[4,64,1024]{2,1,0:T(8,128)(2,1)S(1)}, bf16[4,64,1024]{2,1,0:T(8,128)(2,1)S(1)}, u32[]{:S(2)}, u32[]{:S(2)}) collective-permute-start(bf16[4,64,1024]{2,1,0:T(8,128)(2,1)S(1)} %get-tuple-element.38), channel_id=1, source_target_pairs={{16,0},{0,16},{17,1},{1,17},{18,2},{2,18},{19,3},{3,19},{20,4},{4,... | collective-permute-start | bytes 1572872 | tf_op jit(solution)/shard_map/ppermute | solution.py:46
  85.1 14.0 %collective-permute-start.30 = (bf16[128,2176]{1,0:T(8,128)(2,1)S(1)}, bf16[128,2176]{1,0:T(8,128)(2,1)S(1)}, u32[]{:S(2)}, u32[]{:S(2)}) collective-permute-start(bf16[128,2176]{1,0:T(8,128)(2,1)S(1)} %constant_dynamic-update-slice_fusion.5.near_ref), channel_id=1, source_target_pairs={{0,2},{1,3},{2,0},{3,1},{4,6},{5,7},{6,4},{7,5},{8,10},{9,11},{10,... | collective-permute-start | bytes 1671176 | tf_op jit(solution)/shard_map/ppermute | solution.py:168
  91.2 8.4 %collective-permute-start.24 = (bf16[256,2176]{1,0:T(8,128)(2,1)S(1)}, bf16[256,2176]{1,0:T(8,128)(2,1)S(1)}, u32[]{:S(2)}, u32[]{:S(2)}) collective-permute-start(bf16[256,2176]{1,0:T(8,128)(2,1)S(1)} %collective-permute-done.22.far_ref), channel_id=1, source_target_pairs={{16,0},{0,16},{17,1},{1,17},{18,2},{2,18},{19,3},{3,19},{20,4},{4,... | collective-permute-start | bytes 3342344 | tf_op jit(solution)/shard_map/ppermute | solution.py:46
  91.5 14.2 %collective-permute-start.20 = (bf16[2,2,64,1024]{3,2,1,0:T(8,128)(2,1)S(1)}, bf16[2,2,64,1024]{3,2,1,0:T(8,128)(2,1)S(1)}, u32[]{:S(2)}, u32[]{:S(2)}) collective-permute-start(bf16[2,2,64,1024]{3,2,1,0:T(8,128)(2,1)S(1)} %pad_maximum_fusion.3), channel_id=1, source_target_pairs={{0,2},{1,3},{2,0},{3,1},{4,6},{5,7},{6,4},{7,5},{8,10},{9,11},{10,... | collective-permute-start | bytes 1572872 | tf_op jit(solution)/shard_map/ppermute | solution.py:168
  98.7 12.0 %collective-permute-start.26 = (bf16[4,128,1024]{2,1,0:T(8,128)(2,1)S(1)}, bf16[4,128,1024]{2,1,0:T(8,128)(2,1)S(1)}, u32[]{:S(2)}, u32[]{:S(2)}) collective-permute-start(bf16[4,128,1024]{2,1,0:T(8,128)(2,1)S(1)} %get-tuple-element.45), channel_id=1, source_target_pairs={{16,0},{0,16},{17,1},{1,17},{18,2},{2,18},{19,3},{3,19},{20,4},{4,... | collective-permute-start | bytes 3145736 | tf_op jit(solution)/shard_map/ppermute | solution.py:46
  99.1 12.8 %collective-permute-start.31 = (bf16[128,2176]{1,0:T(8,128)(2,1)S(1)}, bf16[128,2176]{1,0:T(8,128)(2,1)S(1)}, u32[]{:S(2)}, u32[]{:S(2)}) collective-permute-start(bf16[128,2176]{1,0:T(8,128)(2,1)S(1)} %constant_dynamic-update-slice_fusion.5.near_ref), channel_id=1, source_target_pairs={{16,0},{0,16},{17,1},{1,17},{18,2},{2,18},{19,3},{3,19},{20,4},{4,... | collective-permute-start | bytes 1671176 | tf_op jit(solution)/shard_map/ppermute | solution.py:46
  99.3 13.1 %collective-permute-start.32 = (bf16[128,2176]{1,0:T(8,128)(2,1)S(1)}, bf16[128,2176]{1,0:T(8,128)(2,1)S(1)}, u32[]{:S(2)}, u32[]{:S(2)}) collective-permute-start(bf16[128,2176]{1,0:T(8,128)(2,1)S(1)} %collective-permute-done.30.far_ref), channel_id=1, source_target_pairs={{16,0},{0,16},{17,1},{1,17},{18,2},{2,18},{19,3},{3,19},{20,4},{4,... | collective-permute-start | bytes 1671176 | tf_op jit(solution)/shard_map/ppermute | solution.py:46
  115.7 14.9 %collective-permute-start.27 = (bf16[2,2,128,1024]{3,2,1,0:T(8,128)(2,1)S(1)}, bf16[2,2,128,1024]{3,2,1,0:T(8,128)(2,1)S(1)}, u32[]{:S(2)}, u32[]{:S(2)}) collective-permute-start(bf16[2,2,128,1024]{3,2,1,0:T(8,128)(2,1)S(1)} %pad_maximum_fusion), channel_id=1, source_target_pairs={{0,2},{1,3},{2,0},{3,1},{4,6},{5,7},{6,4},{7,5},{8,10},{9,11},{10,... | collective-permute-start | bytes 3145736 | tf_op jit(solution)/shard_map/ppermute | solution.py:168
  117.9 21.1 %collective-permute-start.35 = (bf16[2,2,64,1024]{3,2,1,0:T(8,128)(2,1)S(1)}, bf16[2,2,64,1024]{3,2,1,0:T(8,128)(2,1)S(1)}, u32[]{:S(2)}, u32[]{:S(2)}) collective-permute-start(bf16[2,2,64,1024]{3,2,1,0:T(8,128)(2,1)S(1)} %pad_maximum_fusion.5), channel_id=1, source_target_pairs={{0,2},{1,3},{2,0},{3,1},{4,6},{5,7},{6,4},{7,5},{8,10},{9,11},{10,... | collective-permute-start | bytes 1572872 | tf_op jit(solution)/shard_map/ppermute | solution.py:168
  131.1 10.2 %collective-permute-start.28 = (bf16[2,128,1024]{2,1,0:T(8,128)(2,1)S(1)}, bf16[2,128,1024]{2,1,0:T(8,128)(2,1)S(1)}, u32[]{:S(2)}, u32[]{:S(2)}) collective-permute-start(bf16[2,128,1024]{2,1,0:T(8,128)(2,1)S(1)} %pad_maximum_fusion.4), channel_id=1, source_target_pairs={{0,1},{1,0},{2,3},{3,2},{4,5},{5,4},{6,7},{7,6},{8,9},{9,8},{10,11... | collective-permute-start | bytes 1572872 | tf_op jit(solution)/shard_map/ppermute | solution.py:168
  143.3 14.5 %collective-permute-start.38 = (bf16[128,1024]{1,0:T(8,128)(2,1)S(1)}, bf16[128,1024]{1,0:T(8,128)(2,1)S(1)}, u32[]{:S(2)}, u32[]{:S(2)}) collective-permute-start(bf16[128,1024]{1,0:T(8,128)(2,1)S(1)} %pad_maximum_fusion.10), channel_id=1, source_target_pairs={{0,12},{1,13},{2,14},{3,15},{4,0},{5,1},{6,2},{7,3},{8,4},{9,5},{1... | collective-permute-start | bytes 786440 | tf_op jit(solution)/shard_map/ppermute | solution.py:39
  146.4 19.1 %collective-permute-start.29 = (bf16[128,1024]{1,0:T(8,128)(2,1)S(1)}, bf16[128,1024]{1,0:T(8,128)(2,1)S(1)}, u32[]{:S(2)}, u32[]{:S(2)}) collective-permute-start(bf16[128,1024]{1,0:T(8,128)(2,1)S(1)} %pad_maximum_fusion.7), channel_id=1, source_target_pairs={{0,4},{1,5},{2,6},{3,7},{4,8},{5,9},{6,10},{7,11},{8,12},{9,13},{1... | collective-permute-start | bytes 786440 | tf_op jit(solution)/shard_map/ppermute | solution.py:39
  148.7 25.5 %collective-permute-start.37 = (bf16[128,1024]{1,0:T(8,128)(2,1)}, bf16[128,1024]{1,0:T(8,128)(2,1)S(1)}, u32[]{:S(2)}, u32[]{:S(2)}) collective-permute-start(bf16[128,1024]{1,0:T(8,128)(2,1)} %pad_maximum_fusion.9), channel_id=1, source_target_pairs={{0,8},{1,9},{2,10},{3,11},{4,12},{5,13},{6,14},{7,15},{8,0},{9,1},... | collective-permute-start | bytes 786440 | tf_op jit(solution)/shard_map/ppermute | solution.py:39
  (20 other events, 206.0 us)

commit v18 on v16

--- a/solution.py
+++ b/solution.py
@@ -133,14 +133,20 @@
     rows_out[:, width:] = lanes_ref[part, :]
 
 
-def local_call(body, out_shapes, scalars, arrays, flops=0, limit=16):
+def local_call(body, out_shapes, scalars, arrays, flops=0, limit=16, fetch=False):
     whole = pl.BlockSpec(memory_space=pltpu.VMEM)
     scalar = pl.BlockSpec(memory_space=pltpu.SMEM)
     moved = sum(x.size * x.dtype.itemsize for x in (*arrays, *out_shapes))
+    ins, outs, extra = [whole] * len(arrays), [whole] * len(out_shapes), {}
+    if fetch:
+        ins = [pl.BlockSpec(x.shape, lambda i: (0, 0)) for x in arrays]
+        outs = [pl.BlockSpec(x.shape, lambda i: (0, 0)) for x in out_shapes]
+        extra = {"grid": (1,)}
     return pl.pallas_call(
         body,
-        in_specs=[scalar] * len(scalars) + [whole] * len(arrays),
-        out_specs=[whole] * len(out_shapes),
+        in_specs=[scalar] * len(scalars) + ins,
+        out_specs=outs,
+        **extra,
         out_shape=out_shapes,
         cost_estimate=pl.CostEstimate(flops=flops, bytes_accessed=moved, transcendentals=0),
         compiler_params=pltpu.CompilerParams(vmem_limit_bytes=limit << 20),
@@ -276,7 +282,7 @@
     freq = jnp.concatenate([inv_freq, inv_freq])[None, :]
     rotated = jax.ShapeDtypeStruct(q_proj.shape, jnp.bfloat16)
     rot_query, rot_keys = local_call(
-        rope_kernel, [rotated] * 2, [place, prompt_lengths], [freq, q_proj, k_proj]
+        rope_kernel, [rotated] * 2, [place, prompt_lengths], [freq, q_proj, k_proj], fetch=True
     )
     column = blk_index % PLANE
     key_blocks, value_blocks = [

time: 170 us -> 170 us (level)
  no operation moved by 1% of the time
where the time goes in v18:
time: 170 us
  waiting for transfers between devices  70.2 us (41%)
  starting transfers between devices  51.6 us (30%)
  Pallas kernels  29.7 us (17%)
  local copies, waits for them, and re-layouts  8.72 us (5%)
  other arithmetic  8.12 us (5%)
    ppermute x12, waiting for transfers between devices, crossed(): return lax.ppermute(block, ('tok', 'blk'), route)  39.6 us
    pallas_call x10, Pallas kernels, local_call(): pl.pallas_call(body, in_specs=[scalar] * len(scalars) + ins, out_specs=ou...  29.7 us
    ppermute x12, starting transfers between devices, crossed(): return lax.ppermute(block, ('tok', 'blk'), route)  17.2 us
    ppermute x3, waiting for transfers between devices, to_plane(): lax.ppermute(block, 'blk', [(i, (i + PLANE * ahead) % count) for i in ran...  13.3 us
    ppermute x3, starting transfers between devices, to_plane(): lax.ppermute(block, 'blk', [(i, (i + PLANE * ahead) % count) for i in ran...  9.86 us
    ppermute x2, starting transfers between devices, next_plane(): lax.ppermute(block, 'blk', [(i, i + PLANE) for i in range(count - PLANE)])  8.43 us
    ppermute x6, starting transfers between devices, flipped(): lax.ppermute(block, 'blk', [(i, i ^ mask) for i in range(lax.axis_size('b...  8.32 us
    ppermute x6, waiting for transfers between devices, flipped(): lax.ppermute(block, 'blk', [(i, i ^ mask) for i in range(lax.axis_size('b...  7.49 us
  transfers between devices with their start and end apart: 39, of which 21 were waited for; matrix products, arithmetic and copies ran while one was open for 6% of the time, Pallas kernels for 15%

profile of v18, /device:TPU:0, one launch (start us, length us, event | category | flops | bytes accessed | tf_op | source)
XLA Modules:
  0.0 169.5 jit_solution(10202004890567132364)
XLA Ops:
  4.5 4.9 %collective-permute-start = (bf16[128,1024]{1,0:T(8,128)(2,1)S(1)}, bf16[128,1024]{1,0:T(8,128)(2,1)S(1)}, u32[]{:S(2)}, u32[]{:S(2)}) collective-permute-start(bf16[128,1024]{1,0:T(8,128)(2,1)S(1)} %get-tuple-element.30.rest_0_), channel_id=1, source_target_pairs={{0,4},{1,5},{2,6},{3,7},{4,8},{5,9},{6,10},{7,11},{8,12},{9,13},{1... | collective-permute-start | bytes 786440 | tf_op jit(solution)/shard_map/ppermute | solution.py:27
  9.4 3.5 %collective-permute-start.4 = (bf16[128,1024]{1,0:T(8,128)(2,1)}, bf16[128,1024]{1,0:T(8,128)(2,1)S(1)}, u32[]{:S(2)}, u32[]{:S(2)}) collective-permute-start(bf16[128,1024]{1,0:T(8,128)(2,1)} %rest_0_), channel_id=1, source_target_pairs={{0,4},{1,5},{2,6},{3,7},{4,8},{5,9},{6,10},{7,11},{8,12},{9,13},{1... | collective-permute-start | bytes 786440 | tf_op jit(solution)/shard_map/ppermute | solution.py:27
  13.7 2.4 %collective-permute-done.rest_1_ = bf16[128,1024]{1,0:T(8,128)(2,1)S(1)} collective-permute-done((bf16[128,1024]{1,0:T(8,128)(2,1)S(1)}, bf16[128,1024]{1,0:T(8,128)(2,1)S(1)}, u32[]{:S(2)}, u32[]{:S(2)}) %collective-permute-start) | collective-permute-done | bytes 262176 | tf_op jit(solution)/shard_map/ppermute | solution.py:27
  17.0 2.4 %collective-permute-start.3 = (bf16[128,1024]{1,0:T(8,128)(2,1)S(1)}, bf16[128,1024]{1,0:T(8,128)(2,1)S(1)}, u32[]{:S(2)}, u32[]{:S(2)}) collective-permute-start(bf16[128,1024]{1,0:T(8,128)(2,1)S(1)} %get-tuple-element.73), channel_id=1, source_target_pairs={{0,3},{1,2},{2,1},{3,0},{4,7},{5,6},{6,5},{7,4},{8,11},{9,10},{10,... | collective-permute-start | bytes 786440 | tf_op jit(solution)/shard_map/ppermute | solution.py:22
  22.3 2.4 %collective-permute-start.7 = (bf16[128,1024]{1,0:T(8,128)(2,1)}, bf16[128,1024]{1,0:T(8,128)(2,1)S(1)}, u32[]{:S(2)}, u32[]{:S(2)}) collective-permute-start(bf16[128,1024]{1,0:T(8,128)(2,1)} %get-tuple-element.70), channel_id=1, source_target_pairs={{0,3},{1,2},{2,1},{3,0},{4,7},{5,6},{6,5},{7,4},{8,11},{9,10},{10,... | collective-permute-start | bytes 786440 | tf_op jit(solution)/shard_map/ppermute | solution.py:22
  26.8 1.9 %collective-permute-start.5 = (bf16[128,1024]{1,0:T(8,128)(2,1)}, bf16[128,1024]{1,0:T(8,128)(2,1)S(1)}, u32[]{:S(2)}, u32[]{:S(2)}) collective-permute-start(bf16[128,1024]{1,0:T(8,128)(2,1)} %get-tuple-element.72), channel_id=1, source_target_pairs={{0,1},{1,0},{2,3},{3,2},{4,5},{5,4},{6,7},{7,6},{8,9},{9,8},{10,11... | collective-permute-start | bytes 786440 | tf_op jit(solution)/shard_map/ppermute | solution.py:22
  28.9 1.8 %scatter_fusion = bf16[8,16,2,1024]{3,1,2,0:T(8,128)(2,1)S(1)} fusion(bf16[8,16,2,1024]{3,1,2,0:T(8,128)(2,1)S(1)} %broadcast_in_dim.31, s32[8]{0:T(128)S(1)} %compare_select_fusion, bf16[8,16,2,1024]{3,1,2,0:T(8,128)(2,1)} %pad_maximum_fusion.2), kind=kCustom, calls=%fused_computation | custom fusion | bytes 1572896 | tf_op jit(solution)/shard_map/scatter | solution.py:307
  30.7 4.7 %collective-permute-done.2.rest_3_ = bf16[128,1024]{1,0:T(8,128)(2,1)S(1)} collective-permute-done((bf16[128,1024]{1,0:T(8,128)(2,1)}, bf16[128,1024]{1,0:T(8,128)(2,1)S(1)}, u32[]{:S(2)}, u32[]{:S(2)}) %collective-permute-start.2) | collective-permute-done | bytes 262176 | tf_op jit(solution)/shard_map/ppermute | solution.py:22
  35.4 2.2 %copy-done.3 = bf16[1024,2048]{1,0:T(8,128)(2,1)S(1)} copy-done((bf16[1024,2048]{1,0:T(8,128)(2,1)S(1)}, bf16[1024,2048]{1,0:T(8,128)(2,1)}, u32[]{:S(2)}) %copy-start.3) | copy-done | bytes 4194328
  37.6 1.9 %shard_map.141.prob_ref = bf16[8,128,640]{2,1,0:T(8,128)(2,1)S(1)} custom-call(s32[2]{0:T(128)S(1)} %pad_add_fusion.place_ref, s32[8]{0:T(128)S(1)} %copy-done.11, bf16[128,1024]{1,0:T(8,128)(2,1)S(1)} %get-tuple-element.29.q_ref, bf16[1024,2048]{1,0:T(8,128)(2,1)S(1)} %copy-done.3, bf16[128,1024]{1,0:T(8,128)(2,1)S(1)} %get-tuple-element.30.rest_0_, ...), custom_call_target="tpu_custom_call" | custom-call | flops 167772160 | bytes 7077888 | tf_op jit(solution)/shard_map/pallas_call | solution.py:145
  40.8 1.7 shard_map.142.rest_0_
  42.6 2.6 %collective-permute-done.8.rest_1_ = f32[128,2048]{1,0:T(8,128)S(1)} collective-permute-done((f32[128,2048]{1,0:T(8,128)S(1)}, f32[128,2048]{1,0:T(8,128)S(1)}, u32[]{:S(2)}, u32[]{:S(2)}) %collective-permute-start.8) | collective-permute-done | bytes 1048608 | tf_op jit(solution)/shard_map/ppermute | solution.py:46
  46.0 2.5 %collective-permute-start.17 = (bf16[64,2176]{1,0:T(8,128)(2,1)S(1)}, bf16[64,2176]{1,0:T(8,128)(2,1)S(1)}, u32[]{:S(2)}, u32[]{:S(2)}) collective-permute-start(bf16[64,2176]{1,0:T(8,128)(2,1)S(1)} %get-tuple-element.40), channel_id=1, source_target_pairs={{12,0},{13,1},{14,2},{15,3},{0,4},{1,5},{2,6},{3,7},{4,8},{5,9},{6... | collective-permute-start | bytes 835592 | tf_op jit(solution)/shard_map/ppermute | solution.py:32
  48.6 2.3 %collective-permute-start.16 = (bf16[64,2176]{1,0:T(8,128)(2,1)S(1)}, bf16[64,2176]{1,0:T(8,128)(2,1)S(1)}, u32[]{:S(2)}, u32[]{:S(2)}) collective-permute-start(bf16[64,2176]{1,0:T(8,128)(2,1)S(1)} %get-tuple-element.40), channel_id=1, source_target_pairs={{4,0},{5,1},{6,2},{7,3},{8,4},{9,5},{10,6},{11,7},{12,8},{13,9},{1... | collective-permute-start | bytes 835592 | tf_op jit(solution)/shard_map/ppermute | solution.py:32
  52.4 5.0 %collective-permute-done.9 = bf16[64,2176]{1,0:T(8,128)(2,1)S(1)} collective-permute-done((bf16[64,2176]{1,0:T(8,128)(2,1)S(1)}, bf16[64,2176]{1,0:T(8,128)(2,1)S(1)}, u32[]{:S(2)}, u32[]{:S(2)}) %collective-permute-start.9) | collective-permute-done | bytes 278560 | tf_op jit(solution)/shard_map/ppermute | solution.py:174
  59.8 3.1 %collective-permute-done.16 = bf16[64,2176]{1,0:T(8,128)(2,1)S(1)} collective-permute-done((bf16[64,2176]{1,0:T(8,128)(2,1)S(1)}, bf16[64,2176]{1,0:T(8,128)(2,1)S(1)}, u32[]{:S(2)}, u32[]{:S(2)}) %collective-permute-start.16) | collective-permute-done | bytes 278560 | tf_op jit(solution)/shard_map/ppermute | solution.py:32
  64.7 4.4 %collective-permute-done.10.far_ref = bf16[128,2176]{1,0:T(8,128)(2,1)S(1)} collective-permute-done((bf16[128,2176]{1,0:T(8,128)(2,1)S(1)}, bf16[128,2176]{1,0:T(8,128)(2,1)S(1)}, u32[]{:S(2)}, u32[]{:S(2)}) %collective-permute-start.10) | collective-permute-done | bytes 557088 | tf_op jit(solution)/shard_map/ppermute | solution.py:174
  69.0 3.6 %collective-permute-done.18 = bf16[128,2176]{1,0:T(8,128)(2,1)S(1)} collective-permute-done((bf16[128,2176]{1,0:T(8,128)(2,1)S(1)}, bf16[128,2176]{1,0:T(8,128)(2,1)S(1)}, u32[]{:S(2)}, u32[]{:S(2)}) %collective-permute-start.18) | collective-permute-done | bytes 557088 | tf_op jit(solution)/shard_map/ppermute | solution.py:174
  77.1 3.2 %shard_map.144 = (bf16[4,64,1024]{2,1,0:T(8,128)(2,1)S(1)}, bf16[4,64,1024]{2,1,0:T(8,128)(2,1)S(1)}) custom-call(s32[2]{0:T(128)S(1)} %pad_add_fusion.place_ref, bf16[128,2176]{1,0:T(8,128)(2,1)S(1)} %constant_dynamic-update-slice_fusion.near_ref, bf16[128,2176]{1,0:T(8,128)(2,1)S(1)} %collective-permute-done.10.far_ref, bf16[704,2048]{1,0:T(8,128)(2,1)S(1)} %bitcast.78, ...), custom_call_target="tpu_custom_call" | custom-call | flops 2214592512 | bytes 10813440 | tf_op jit(solution)/shard_map/pallas_call | solution.py:145
  80.9 3.2 %shard_map.145 = (bf16[4,64,1024]{2,1,0:T(8,128)(2,1)S(1)}, bf16[4,64,1024]{2,1,0:T(8,128)(2,1)S(1)}) custom-call(s32[2]{0:T(128)S(1)} %pad_add_fusion.place_ref, bf16[128,2176]{1,0:T(8,128)(2,1)S(1)} %collective-permute-done.11.near_ref, bf16[128,2176]{1,0:T(8,128)(2,1)S(1)} %collective-permute-done.12.far_ref, bf16[704,2048]{1,0:T(8,128)(2,1)S(1)} %bitcast.79, ...), custom_call_target="tpu_custom_call" | custom-call | flops 2214592512 | bytes 10813440 | tf_op jit(solution)/shard_map/pallas_call | solution.py:145
  86.8 4.4 %collective-permute-done.22.far_ref = bf16[256,2176]{1,0:T(8,128)(2,1)S(1)} collective-permute-done((bf16[256,2176]{1,0:T(8,128)(2,1)S(1)}, bf16[256,2176]{1,0:T(8,128)(2,1)S(1)}, u32[]{:S(2)}, u32[]{:S(2)}) %collective-permute-start.22) | collective-permute-done | bytes 1114144 | tf_op jit(solution)/shard_map/ppermute | solution.py:174
  93.1 5.7 %shard_map.146 = (bf16[4,128,1024]{2,1,0:T(8,128)(2,1)S(1)}, bf16[4,128,1024]{2,1,0:T(8,128)(2,1)S(1)}) custom-call(s32[2]{0:T(128)S(1)} %pad_add_fusion.place_ref, bf16[256,2176]{1,0:T(8,128)(2,1)S(1)} %constant_dynamic-update-slice_fusion.2.near_ref, bf16[256,2176]{1,0:T(8,128)(2,1)S(1)} %collective-permute-done.22.far_ref, ...), custom_call_target="tpu_custom_call" | custom-call | flops 4429185024 | bytes 12976128 | tf_op jit(solution)/shard_map/pallas_call | solution.py:145
  99.6 5.8 %shard_map.147 = (bf16[4,128,1024]{2,1,0:T(8,128)(2,1)S(1)}, bf16[4,128,1024]{2,1,0:T(8,128)(2,1)S(1)}) custom-call(s32[2]{0:T(128)S(1)} %pad_add_fusion.place_ref, bf16[256,2176]{1,0:T(8,128)(2,1)S(1)} %collective-permute-done.23.near_ref, bf16[256,2176]{1,0:T(8,128)(2,1)S(1)} %collective-permute-done.24.far_ref, bf16[704,2048]{1,0:T(8,128)(2,1)S(1)} %bitcast.81, ...), custom_call_target="tpu_custom_call" | custom-call | flops 4429185024 | bytes 12976128 | tf_op jit(solution)/shard_map/pallas_call | solution.py:145
  107.6 3.2 %shard_map.148 = (bf16[4,64,1024]{2,1,0:T(8,128)(2,1)S(1)}, bf16[4,64,1024]{2,1,0:T(8,128)(2,1)S(1)}) custom-call(s32[2]{0:T(128)S(1)} %pad_add_fusion.place_ref, bf16[128,2176]{1,0:T(8,128)(2,1)S(1)} %constant_dynamic-update-slice_fusion.5.near_ref, bf16[128,2176]{1,0:T(8,128)(2,1)S(1)} %collective-permute-done.30.far_ref, bf16[704,2048]{1,0:T(8,128)(2,1)S(1)} %bitcast.82, ...), custom_call_target="tpu_custom_call" | custom-call | flops 2214592512 | bytes 10813440 | tf_op jit(solution)/shard_map/pallas_call | solution.py:145
  112.4 3.2 %shard_map.149 = (bf16[4,64,1024]{2,1,0:T(8,128)(2,1)S(1)}, bf16[4,64,1024]{2,1,0:T(8,128)(2,1)S(1)}) custom-call(s32[2]{0:T(128)S(1)} %pad_add_fusion.place_ref, bf16[128,2176]{1,0:T(8,128)(2,1)S(1)} %collective-permute-done.31.near_ref, bf16[128,2176]{1,0:T(8,128)(2,1)S(1)} %collective-permute-done.32.far_ref, bf16[704,2048]{1,0:T(8,128)(2,1)S(1)} %bitcast.83, ...), custom_call_target="tpu_custom_call" | custom-call | flops 2214592512 | bytes 10813440 | tf_op jit(solution)/shard_map/pallas_call | solution.py:145
  119.3 11.3 %collective-permute-done.27 = bf16[2,2,128,1024]{3,2,1,0:T(8,128)(2,1)S(1)} collective-permute-done((bf16[2,2,128,1024]{3,2,1,0:T(8,128)(2,1)S(1)}, bf16[2,2,128,1024]{3,2,1,0:T(8,128)(2,1)S(1)}, u32[]{:S(2)}, u32[]{:S(2)}) %collective-permute-start.27) | collective-permute-done | bytes 1048608 | tf_op jit(solution)/shard_map/ppermute | solution.py:174
  131.0 5.1 %collective-permute-done.35 = bf16[2,2,64,1024]{3,2,1,0:T(8,128)(2,1)S(1)} collective-permute-done((bf16[2,2,64,1024]{3,2,1,0:T(8,128)(2,1)S(1)}, bf16[2,2,64,1024]{3,2,1,0:T(8,128)(2,1)S(1)}, u32[]{:S(2)}, u32[]{:S(2)}) %collective-permute-start.35) | collective-permute-done | bytes 524320 | tf_op jit(solution)/shard_map/ppermute | solution.py:174
  138.5 4.3 %collective-permute-done.36 = bf16[2,64,1024]{2,1,0:T(8,128)(2,1)S(1)} collective-permute-done((bf16[2,64,1024]{2,1,0:T(8,128)(2,1)S(1)}, bf16[2,64,1024]{2,1,0:T(8,128)(2,1)S(1)}, u32[]{:S(2)}, u32[]{:S(2)}) %collective-permute-start.36) | collective-permute-done | bytes 262176 | tf_op jit(solution)/shard_map/ppermute | solution.py:174
  143.0 7.8 %collective-permute-start.37 = (bf16[128,1024]{1,0:T(8,128)(2,1)S(1)}, bf16[128,1024]{1,0:T(8,128)(2,1)S(1)}, u32[]{:S(2)}, u32[]{:S(2)}) collective-permute-start(bf16[128,1024]{1,0:T(8,128)(2,1)S(1)} %pad_maximum_fusion.9), channel_id=1, source_target_pairs={{0,8},{1,9},{2,10},{3,11},{4,12},{5,13},{6,14},{7,15},{8,0},{9,1},... | collective-permute-start | bytes 786440 | tf_op jit(solution)/shard_map/ppermute | solution.py:39
  155.2 2.4 %collective-permute-done.37 = bf16[128,1024]{1,0:T(8,128)(2,1)S(1)} collective-permute-done((bf16[128,1024]{1,0:T(8,128)(2,1)S(1)}, bf16[128,1024]{1,0:T(8,128)(2,1)S(1)}, u32[]{:S(2)}, u32[]{:S(2)}) %collective-permute-start.37) | collective-permute-done | bytes 262176 | tf_op jit(solution)/shard_map/ppermute | solution.py:39
  157.6 6.7 %collective-permute-done.38 = bf16[128,1024]{1,0:T(8,128)(2,1)S(1)} collective-permute-done((bf16[128,1024]{1,0:T(8,128)(2,1)S(1)}, bf16[128,1024]{1,0:T(8,128)(2,1)S(1)}, u32[]{:S(2)}, u32[]{:S(2)}) %collective-permute-start.38) | collective-permute-done | bytes 262176 | tf_op jit(solution)/shard_map/ppermute | solution.py:39
  164.2 4.3 %collective-permute-done.29 = bf16[128,1024]{1,0:T(8,128)(2,1)S(1)} collective-permute-done((bf16[128,1024]{1,0:T(8,128)(2,1)}, bf16[128,1024]{1,0:T(8,128)(2,1)S(1)}, u32[]{:S(2)}, u32[]{:S(2)}) %collective-permute-start.29) | collective-permute-done | bytes 262176 | tf_op jit(solution)/shard_map/ppermute | solution.py:39
  (142 shorter events, 44.3 us)
Async XLA Ops:
  4.5 11.6 %collective-permute-start = (bf16[128,1024]{1,0:T(8,128)(2,1)S(1)}, bf16[128,1024]{1,0:T(8,128)(2,1)S(1)}, u32[]{:S(2)}, u32[]{:S(2)}) collective-permute-start(bf16[128,1024]{1,0:T(8,128)(2,1)S(1)} %get-tuple-element.30.rest_0_), channel_id=1, source_target_pairs={{0,4},{1,5},{2,6},{3,7},{4,8},{5,9},{6,10},{7,11},{8,12},{9,13},{1... | collective-permute-start | bytes 786440 | tf_op jit(solution)/shard_map/ppermute | solution.py:27
  9.4 11.9 %collective-permute-start.4 = (bf16[128,1024]{1,0:T(8,128)(2,1)}, bf16[128,1024]{1,0:T(8,128)(2,1)S(1)}, u32[]{:S(2)}, u32[]{:S(2)}) collective-permute-start(bf16[128,1024]{1,0:T(8,128)(2,1)} %rest_0_), channel_id=1, source_target_pairs={{0,4},{1,5},{2,6},{3,7},{4,8},{5,9},{6,10},{7,11},{8,12},{9,13},{1... | collective-permute-start | bytes 786440 | tf_op jit(solution)/shard_map/ppermute | solution.py:27
  17.0 9.8 %collective-permute-start.3 = (bf16[128,1024]{1,0:T(8,128)(2,1)S(1)}, bf16[128,1024]{1,0:T(8,128)(2,1)S(1)}, u32[]{:S(2)}, u32[]{:S(2)}) collective-permute-start(bf16[128,1024]{1,0:T(8,128)(2,1)S(1)} %get-tuple-element.73), channel_id=1, source_target_pairs={{0,3},{1,2},{2,1},{3,0},{4,7},{5,6},{6,5},{7,4},{8,11},{9,10},{10,... | collective-permute-start | bytes 786440 | tf_op jit(solution)/shard_map/ppermute | solution.py:22
  20.3 15.1 %collective-permute-start.2 = (bf16[128,1024]{1,0:T(8,128)(2,1)}, bf16[128,1024]{1,0:T(8,128)(2,1)S(1)}, u32[]{:S(2)}, u32[]{:S(2)}) collective-permute-start(bf16[128,1024]{1,0:T(8,128)(2,1)} %get-tuple-element.74), channel_id=1, source_target_pairs={{0,2},{1,3},{2,0},{3,1},{4,6},{5,7},{6,4},{7,5},{8,10},{9,11},{10,... | collective-permute-start | bytes 786440 | tf_op jit(solution)/shard_map/ppermute | solution.py:22
  20.8 14.6 %collective-permute-start.1 = (bf16[128,1024]{1,0:T(8,128)(2,1)}, bf16[128,1024]{1,0:T(8,128)(2,1)S(1)}, u32[]{:S(2)}, u32[]{:S(2)}) collective-permute-start(bf16[128,1024]{1,0:T(8,128)(2,1)} %get-tuple-element.75), channel_id=1, source_target_pairs={{0,1},{1,0},{2,3},{3,2},{4,5},{5,4},{6,7},{7,6},{8,9},{9,8},{10,11... | collective-permute-start | bytes 786440 | tf_op jit(solution)/shard_map/ppermute | solution.py:22
  22.3 17.2 %collective-permute-start.7 = (bf16[128,1024]{1,0:T(8,128)(2,1)}, bf16[128,1024]{1,0:T(8,128)(2,1)S(1)}, u32[]{:S(2)}, u32[]{:S(2)}) collective-permute-start(bf16[128,1024]{1,0:T(8,128)(2,1)} %get-tuple-element.70), channel_id=1, source_target_pairs={{0,3},{1,2},{2,1},{3,0},{4,7},{5,6},{6,5},{7,4},{8,11},{9,10},{10,... | collective-permute-start | bytes 786440 | tf_op jit(solution)/shard_map/ppermute | solution.py:22
  24.8 16.0 %collective-permute-start.6 = (bf16[128,1024]{1,0:T(8,128)(2,1)}, bf16[128,1024]{1,0:T(8,128)(2,1)S(1)}, u32[]{:S(2)}, u32[]{:S(2)}) collective-permute-start(bf16[128,1024]{1,0:T(8,128)(2,1)} %get-tuple-element.71), channel_id=1, source_target_pairs={{0,2},{1,3},{2,0},{3,1},{4,6},{5,7},{6,4},{7,5},{8,10},{9,11},{10,... | collective-permute-start | bytes 786440 | tf_op jit(solution)/shard_map/ppermute | solution.py:22
  26.8 14.0 %collective-permute-start.5 = (bf16[128,1024]{1,0:T(8,128)(2,1)}, bf16[128,1024]{1,0:T(8,128)(2,1)S(1)}, u32[]{:S(2)}, u32[]{:S(2)}) collective-permute-start(bf16[128,1024]{1,0:T(8,128)(2,1)} %get-tuple-element.72), channel_id=1, source_target_pairs={{0,1},{1,0},{2,3},{3,2},{4,5},{5,4},{6,7},{7,6},{8,9},{9,8},{10,11... | collective-permute-start | bytes 786440 | tf_op jit(solution)/shard_map/ppermute | solution.py:22
  46.0 13.8 %collective-permute-start.17 = (bf16[64,2176]{1,0:T(8,128)(2,1)S(1)}, bf16[64,2176]{1,0:T(8,128)(2,1)S(1)}, u32[]{:S(2)}, u32[]{:S(2)}) collective-permute-start(bf16[64,2176]{1,0:T(8,128)(2,1)S(1)} %get-tuple-element.40), channel_id=1, source_target_pairs={{12,0},{13,1},{14,2},{15,3},{0,4},{1,5},{2,6},{3,7},{4,8},{5,9},{6... | collective-permute-start | bytes 835592 | tf_op jit(solution)/shard_map/ppermute | solution.py:32
  48.6 14.4 %collective-permute-start.16 = (bf16[64,2176]{1,0:T(8,128)(2,1)S(1)}, bf16[64,2176]{1,0:T(8,128)(2,1)S(1)}, u32[]{:S(2)}, u32[]{:S(2)}) collective-permute-start(bf16[64,2176]{1,0:T(8,128)(2,1)S(1)} %get-tuple-element.40), channel_id=1, source_target_pairs={{4,0},{5,1},{6,2},{7,3},{8,4},{9,5},{10,6},{11,7},{12,8},{13,9},{1... | collective-permute-start | bytes 835592 | tf_op jit(solution)/shard_map/ppermute | solution.py:32
  50.8 6.5 %collective-permute-start.9 = (bf16[64,2176]{1,0:T(8,128)(2,1)S(1)}, bf16[64,2176]{1,0:T(8,128)(2,1)S(1)}, u32[]{:S(2)}, u32[]{:S(2)}) collective-permute-start(bf16[64,2176]{1,0:T(8,128)(2,1)S(1)} %get-tuple-element.40), channel_id=1, source_target_pairs={{0,1},{1,0},{2,3},{3,2},{4,5},{5,4},{6,7},{7,6},{8,9},{9,8},{10,11... | collective-permute-start | bytes 835592 | tf_op jit(solution)/shard_map/ppermute | solution.py:174
  57.4 22.9 %collective-permute-start.11 = (bf16[128,2176]{1,0:T(8,128)(2,1)S(1)}, bf16[128,2176]{1,0:T(8,128)(2,1)S(1)}, u32[]{:S(2)}, u32[]{:S(2)}) collective-permute-start(bf16[128,2176]{1,0:T(8,128)(2,1)S(1)} %constant_dynamic-update-slice_fusion.near_ref), channel_id=1, source_target_pairs={{16,0},{0,16},{17,1},{1,17},{18,2},{2,18},{19,3},{3,19},{20,4},{4,... | collective-permute-start | bytes 1671176 | tf_op jit(solution)/shard_map/ppermute | solution.py:46
  57.5 11.5 %collective-permute-start.10 = (bf16[128,2176]{1,0:T(8,128)(2,1)S(1)}, bf16[128,2176]{1,0:T(8,128)(2,1)S(1)}, u32[]{:S(2)}, u32[]{:S(2)}) collective-permute-start(bf16[128,2176]{1,0:T(8,128)(2,1)S(1)} %constant_dynamic-update-slice_fusion.near_ref), channel_id=1, source_target_pairs={{0,2},{1,3},{2,0},{3,1},{4,6},{5,7},{6,4},{7,5},{8,10},{9,11},{10,... | collective-permute-start | bytes 1671176 | tf_op jit(solution)/shard_map/ppermute | solution.py:174
  59.0 16.4 %collective-permute-start.15 = (bf16[64,2176]{1,0:T(8,128)(2,1)S(1)}, bf16[64,2176]{1,0:T(8,128)(2,1)S(1)}, u32[]{:S(2)}, u32[]{:S(2)}) collective-permute-start(bf16[64,2176]{1,0:T(8,128)(2,1)S(1)} %get-tuple-element.40), channel_id=1, source_target_pairs={{8,0},{9,1},{10,2},{11,3},{12,4},{13,5},{14,6},{15,7},{0,8},{1,9},... | collective-permute-start | bytes 835592 | tf_op jit(solution)/shard_map/ppermute | solution.py:32
  63.0 9.6 %collective-permute-start.18 = (bf16[128,2176]{1,0:T(8,128)(2,1)S(1)}, bf16[128,2176]{1,0:T(8,128)(2,1)S(1)}, u32[]{:S(2)}, u32[]{:S(2)}) collective-permute-start(bf16[128,2176]{1,0:T(8,128)(2,1)S(1)} %pad_maximum_fusion.1), channel_id=1, source_target_pairs={{0,1},{1,0},{2,3},{3,2},{4,5},{5,4},{6,7},{7,6},{8,9},{9,8},{10,11... | collective-permute-start | bytes 1671176 | tf_op jit(solution)/shard_map/ppermute | solution.py:174
  69.0 11.8 %collective-permute-start.12 = (bf16[128,2176]{1,0:T(8,128)(2,1)S(1)}, bf16[128,2176]{1,0:T(8,128)(2,1)S(1)}, u32[]{:S(2)}, u32[]{:S(2)}) collective-permute-start(bf16[128,2176]{1,0:T(8,128)(2,1)S(1)} %collective-permute-done.10.far_ref), channel_id=1, source_target_pairs={{16,0},{0,16},{17,1},{1,17},{18,2},{2,18},{19,3},{3,19},{20,4},{4,... | collective-permute-start | bytes 1671176 | tf_op jit(solution)/shard_map/ppermute | solution.py:46
  72.7 18.6 %collective-permute-start.22 = (bf16[256,2176]{1,0:T(8,128)(2,1)S(1)}, bf16[256,2176]{1,0:T(8,128)(2,1)S(1)}, u32[]{:S(2)}, u32[]{:S(2)}) collective-permute-start(bf16[256,2176]{1,0:T(8,128)(2,1)S(1)} %constant_dynamic-update-slice_fusion.2.near_ref), channel_id=1, source_target_pairs={{0,2},{1,3},{2,0},{3,1},{4,6},{5,7},{6,4},{7,5},{8,10},{9,11},{10,... | collective-permute-start | bytes 3342344 | tf_op jit(solution)/shard_map/ppermute | solution.py:174
  75.5 9.6 %collective-permute-start.19 = (bf16[64,2176]{1,0:T(8,128)(2,1)S(1)}, bf16[64,2176]{1,0:T(8,128)(2,1)S(1)}, u32[]{:S(2)}, u32[]{:S(2)}) collective-permute-start(bf16[64,2176]{1,0:T(8,128)(2,1)S(1)} %collective-permute-done.15), channel_id=1, source_target_pairs={{0,1},{1,0},{2,3},{3,2},{4,5},{5,4},{6,7},{7,6},{8,9},{9,8},{10,11... | collective-permute-start | bytes 835592 | tf_op jit(solution)/shard_map/ppermute | solution.py:174
  77.0 22.3 %collective-permute-start.23 = (bf16[256,2176]{1,0:T(8,128)(2,1)S(1)}, bf16[256,2176]{1,0:T(8,128)(2,1)S(1)}, u32[]{:S(2)}, u32[]{:S(2)}) collective-permute-start(bf16[256,2176]{1,0:T(8,128)(2,1)S(1)} %constant_dynamic-update-slice_fusion.2.near_ref), channel_id=1, source_target_pairs={{16,0},{0,16},{17,1},{1,17},{18,2},{2,18},{19,3},{3,19},{20,4},{4,... | collective-permute-start | bytes 3342344 | tf_op jit(solution)/shard_map/ppermute | solution.py:46
  84.0 7.2 %collective-permute-start.13 = (bf16[4,64,1024]{2,1,0:T(8,128)(2,1)S(1)}, bf16[4,64,1024]{2,1,0:T(8,128)(2,1)S(1)}, u32[]{:S(2)}, u32[]{:S(2)}) collective-permute-start(bf16[4,64,1024]{2,1,0:T(8,128)(2,1)S(1)} %get-tuple-element.38), channel_id=1, source_target_pairs={{16,0},{0,16},{17,1},{1,17},{18,2},{2,18},{19,3},{3,19},{20,4},{4,... | collective-permute-start | bytes 1572872 | tf_op jit(solution)/shard_map/ppermute | solution.py:46
  85.1 14.0 %collective-permute-start.30 = (bf16[128,2176]{1,0:T(8,128)(2,1)S(1)}, bf16[128,2176]{1,0:T(8,128)(2,1)S(1)}, u32[]{:S(2)}, u32[]{:S(2)}) collective-permute-start(bf16[128,2176]{1,0:T(8,128)(2,1)S(1)} %constant_dynamic-update-slice_fusion.5.near_ref), channel_id=1, source_target_pairs={{0,2},{1,3},{2,0},{3,1},{4,6},{5,7},{6,4},{7,5},{8,10},{9,11},{10,... | collective-permute-start | bytes 1671176 | tf_op jit(solution)/shard_map/ppermute | solution.py:174
  91.2 8.4 %collective-permute-start.24 = (bf16[256,2176]{1,0:T(8,128)(2,1)S(1)}, bf16[256,2176]{1,0:T(8,128)(2,1)S(1)}, u32[]{:S(2)}, u32[]{:S(2)}) collective-permute-start(bf16[256,2176]{1,0:T(8,128)(2,1)S(1)} %collective-permute-done.22.far_ref), channel_id=1, source_target_pairs={{16,0},{0,16},{17,1},{1,17},{18,2},{2,18},{19,3},{3,19},{20,4},{4,... | collective-permute-start | bytes 3342344 | tf_op jit(solution)/shard_map/ppermute | solution.py:46
  91.5 14.2 %collective-permute-start.20 = (bf16[2,2,64,1024]{3,2,1,0:T(8,128)(2,1)S(1)}, bf16[2,2,64,1024]{3,2,1,0:T(8,128)(2,1)S(1)}, u32[]{:S(2)}, u32[]{:S(2)}) collective-permute-start(bf16[2,2,64,1024]{3,2,1,0:T(8,128)(2,1)S(1)} %pad_maximum_fusion.3), channel_id=1, source_target_pairs={{0,2},{1,3},{2,0},{3,1},{4,6},{5,7},{6,4},{7,5},{8,10},{9,11},{10,... | collective-permute-start | bytes 1572872 | tf_op jit(solution)/shard_map/ppermute | solution.py:174
  98.7 12.0 %collective-permute-start.26 = (bf16[4,128,1024]{2,1,0:T(8,128)(2,1)S(1)}, bf16[4,128,1024]{2,1,0:T(8,128)(2,1)S(1)}, u32[]{:S(2)}, u32[]{:S(2)}) collective-permute-start(bf16[4,128,1024]{2,1,0:T(8,128)(2,1)S(1)} %get-tuple-element.45), channel_id=1, source_target_pairs={{16,0},{0,16},{17,1},{1,17},{18,2},{2,18},{19,3},{3,19},{20,4},{4,... | collective-permute-start | bytes 3145736 | tf_op jit(solution)/shard_map/ppermute | solution.py:46
  99.1 12.8 %collective-permute-start.31 = (bf16[128,2176]{1,0:T(8,128)(2,1)S(1)}, bf16[128,2176]{1,0:T(8,128)(2,1)S(1)}, u32[]{:S(2)}, u32[]{:S(2)}) collective-permute-start(bf16[128,2176]{1,0:T(8,128)(2,1)S(1)} %constant_dynamic-update-slice_fusion.5.near_ref), channel_id=1, source_target_pairs={{16,0},{0,16},{17,1},{1,17},{18,2},{2,18},{19,3},{3,19},{20,4},{4,... | collective-permute-start | bytes 1671176 | tf_op jit(solution)/shard_map/ppermute | solution.py:46
  99.3 13.1 %collective-permute-start.32 = (bf16[128,2176]{1,0:T(8,128)(2,1)S(1)}, bf16[128,2176]{1,0:T(8,128)(2,1)S(1)}, u32[]{:S(2)}, u32[]{:S(2)}) collective-permute-start(bf16[128,2176]{1,0:T(8,128)(2,1)S(1)} %collective-permute-done.30.far_ref), channel_id=1, source_target_pairs={{16,0},{0,16},{17,1},{1,17},{18,2},{2,18},{19,3},{3,19},{20,4},{4,... | collective-permute-start | bytes 1671176 | tf_op jit(solution)/shard_map/ppermute | solution.py:46
  115.7 14.9 %collective-permute-start.27 = (bf16[2,2,128,1024]{3,2,1,0:T(8,128)(2,1)S(1)}, bf16[2,2,128,1024]{3,2,1,0:T(8,128)(2,1)S(1)}, u32[]{:S(2)}, u32[]{:S(2)}) collective-permute-start(bf16[2,2,128,1024]{3,2,1,0:T(8,128)(2,1)S(1)} %pad_maximum_fusion), channel_id=1, source_target_pairs={{0,2},{1,3},{2,0},{3,1},{4,6},{5,7},{6,4},{7,5},{8,10},{9,11},{10,... | collective-permute-start | bytes 3145736 | tf_op jit(solution)/shard_map/ppermute | solution.py:174
  117.9 18.3 %collective-permute-start.35 = (bf16[2,2,64,1024]{3,2,1,0:T(8,128)(2,1)S(1)}, bf16[2,2,64,1024]{3,2,1,0:T(8,128)(2,1)S(1)}, u32[]{:S(2)}, u32[]{:S(2)}) collective-permute-start(bf16[2,2,64,1024]{3,2,1,0:T(8,128)(2,1)S(1)} %pad_maximum_fusion.5), channel_id=1, source_target_pairs={{0,2},{1,3},{2,0},{3,1},{4,6},{5,7},{6,4},{7,5},{8,10},{9,11},{10,... | collective-permute-start | bytes 1572872 | tf_op jit(solution)/shard_map/ppermute | solution.py:174
  138.0 12.8 %collective-permute-start.28 = (bf16[2,128,1024]{2,1,0:T(8,128)(2,1)S(1)}, bf16[2,128,1024]{2,1,0:T(8,128)(2,1)S(1)}, u32[]{:S(2)}, u32[]{:S(2)}) collective-permute-start(bf16[2,128,1024]{2,1,0:T(8,128)(2,1)S(1)} %pad_maximum_fusion.4), channel_id=1, source_target_pairs={{0,1},{1,0},{2,3},{3,2},{4,5},{5,4},{6,7},{7,6},{8,9},{9,8},{10,11... | collective-permute-start | bytes 1572872 | tf_op jit(solution)/shard_map/ppermute | solution.py:174
  143.0 14.6 %collective-permute-start.37 = (bf16[128,1024]{1,0:T(8,128)(2,1)S(1)}, bf16[128,1024]{1,0:T(8,128)(2,1)S(1)}, u32[]{:S(2)}, u32[]{:S(2)}) collective-permute-start(bf16[128,1024]{1,0:T(8,128)(2,1)S(1)} %pad_maximum_fusion.9), channel_id=1, source_target_pairs={{0,8},{1,9},{2,10},{3,11},{4,12},{5,13},{6,14},{7,15},{8,0},{9,1},... | collective-permute-start | bytes 786440 | tf_op jit(solution)/shard_map/ppermute | solution.py:39
  151.0 13.2 %collective-permute-start.38 = (bf16[128,1024]{1,0:T(8,128)(2,1)S(1)}, bf16[128,1024]{1,0:T(8,128)(2,1)S(1)}, u32[]{:S(2)}, u32[]{:S(2)}) collective-permute-start(bf16[128,1024]{1,0:T(8,128)(2,1)S(1)} %pad_maximum_fusion.10), channel_id=1, source_target_pairs={{0,12},{1,13},{2,14},{3,15},{4,0},{5,1},{6,2},{7,3},{8,4},{9,5},{1... | collective-permute-start | bytes 786440 | tf_op jit(solution)/shard_map/ppermute | solution.py:39
  152.4 16.1 %collective-permute-start.29 = (bf16[128,1024]{1,0:T(8,128)(2,1)}, bf16[128,1024]{1,0:T(8,128)(2,1)S(1)}, u32[]{:S(2)}, u32[]{:S(2)}) collective-permute-start(bf16[128,1024]{1,0:T(8,128)(2,1)} %pad_maximum_fusion.7), channel_id=1, source_target_pairs={{0,4},{1,5},{2,6},{3,7},{4,8},{5,9},{6,10},{7,11},{8,12},{9,13},{1... | collective-permute-start | bytes 786440 | tf_op jit(solution)/shard_map/ppermute | solution.py:39
  (20 other events, 206.0 us)
